TPU v7x, 32 devices: a whole 2x2x4 slice. The times are simulated.
32 devices in a mesh: dp: 4 (over z), pipe: 2 (over core), tensor: 4 (over y, x).
Axes of the slice: x: 2, y: 2, z: 4, core: 2. Of those that a mesh axis runs over, the one named last changes fastest.
Arguments:
- heads_out: bfloat16 [2, 512, 4096], P('pipe', 'dp', 'tensor'), may hold values from -6 to 6
- out_proj: bfloat16 [2, 4096, 4096], P('pipe', 'tensor', 'dp'), may hold values from -0.09375 to 0.09375
- encoder: bfloat16 [2, 512, 4096], P('pipe', None, 'dp'), may hold values from -0.09375 to 0.09375
- decoder: bfloat16 [2, 512, 4096], P('pipe', None, 'tensor'), may hold values from -1.767767 to 1.767767
- norm_gain: float32 [2, 4096], P('pipe', 'tensor'), may hold values from 0.25 to 1.75
- send_encoder: bfloat16 [2, 4096, 128], P('pipe', 'tensor'), may hold values from -0.1875 to 0.1875
- recv_decoder: bfloat16 [2, 128, 4096], P('pipe', None, 'tensor'), may hold values from -3.535534 to 3.535534
- input_code: bfloat16 [512, 512], P('dp', 'tensor'), may hold values from -40 to 40
- code_cotangent: bfloat16 [512, 512], P('dp', 'tensor'), may hold values from -4 to 4
Outputs:
- sent_codes: bfloat16 [2, 512, 512], P('pipe', 'dp', 'tensor')
- returned_codes: bfloat16 [2, 512, 512], P('pipe', 'dp', 'tensor')
- heads_grad: bfloat16 [2, 512, 4096], P('pipe', 'dp', 'tensor')
- proj_grad: bfloat16 [2, 4096, 4096], P('pipe', 'tensor', 'dp')
- encoder_grad: bfloat16 [2, 512, 4096], P('pipe', 'tensor', 'dp')
- decoder_grad: bfloat16 [2, 512, 4096], P('pipe', 'dp', 'tensor')
- gain_grad: float32 [2, 4096], P('pipe', 'tensor')
- send_grad: bfloat16 [2, 4096, 128], P('pipe', 'tensor')
- recv_grad: bfloat16 [2, 128, 4096], P('pipe', None, 'tensor')
All inputs are finite; a program needn't handle non-finite values.
Results may differ from a plain program's by a relative error of at most 0.035.
Values may be sent and summed in bfloat16 or wider, within the bound.
No kernel may reach another device: no remote copies, remote signals or barrier semaphores. Data moves between devices by JAX's collectives and lax.ppermute only.
A program may use at most 64 MiB of HBM per device.

v0:
```python
import jax
import jax.numpy as jnp
from jax import lax
from jax.sharding import PartitionSpec as P

D = 4096


epsilon = 1e-05
highest_precision = lax.Precision.HIGHEST


def from_behind(shard, axis, by):
    devices = lax.axis_size(axis)
    pairs = [(i, i + by) for i in range(devices) if 0 <= i + by < devices]
    return lax.ppermute(shard, axis, pairs)


def on_device(
    heads_out,
    out_proj,
    encoder,
    decoder,
    norm_gain,
    send_encoder,
    recv_decoder,
    input_code,
    code_cotangent,
):
    section_index = lax.axis_index("pipe")
    section_count = lax.axis_size("pipe")
    head_row_block = heads_out[0]
    proj_local = out_proj[0]
    enc_local = encoder[0]
    dec_local = decoder[0]
    norm_scale = norm_gain[0]
    send_local = send_encoder[0]
    recv_local = recv_decoder[0]
    tokens_here = head_row_block.shape[0]
    feature_cols = dec_local.shape[1]
    local_fold = lax.dot_general(
        proj_local, enc_local, (((1,), (1,)), ((), ())), preferred_element_type=jnp.float32
    )
    folded = lax.psum(local_fold.astype(jnp.bfloat16), "dp").astype(jnp.float32)
    partial_code = jnp.dot(head_row_block.astype(jnp.float32), folded, precision=highest_precision)
    mix_code = lax.psum(partial_code.astype(jnp.bfloat16), "tensor")
    attention = jnp.dot(mix_code, dec_local, preferred_element_type=jnp.float32)

    def decode_turn(received, previous):
        return jnp.dot(received, recv_local, preferred_element_type=jnp.float32) + attention

    def keep_mixed(received, previous):
        return previous

    def encode_turn(mixed_rows, totals, previous):
        row_scale = lax.rsqrt(totals / D + epsilon)[:, None]
        normed = mixed_rows * row_scale
        out_rows = (normed * norm_scale).astype(jnp.bfloat16)
        sent_code = jnp.dot(out_rows, send_local, preferred_element_type=jnp.float32).astype(
            jnp.bfloat16
        )
        return (row_scale, normed, out_rows, sent_code)

    def keep_state(mixed_rows, totals, previous):
        return previous

    held_code = input_code
    mixed_rows = jnp.zeros((tokens_here, feature_cols), jnp.float32)
    forward_state = (
        jnp.zeros((tokens_here, 1), jnp.float32),
        jnp.zeros((tokens_here, feature_cols), jnp.float32),
        jnp.zeros((tokens_here, feature_cols), jnp.bfloat16),
        jnp.zeros_like(input_code),
    )
    for turn_index in range(section_count):
        is_live = section_index == turn_index
        if turn_index > 0:
            shifted = from_behind(forward_state[3], "pipe", 1)
            held_code = jnp.where(is_live, shifted, held_code)
        mixed_rows = lax.cond(is_live, decode_turn, keep_mixed, held_code, mixed_rows)
        totals = lax.psum(jnp.sum(mixed_rows * mixed_rows, axis=1), "tensor")
        forward_state = lax.cond(
            is_live, encode_turn, keep_state, mixed_rows, totals, forward_state
        )
    row_scale, normed, out_rows, sent_code = forward_state

    def backward_norm(incoming, previous):
        return jnp.dot(incoming, send_local.T, preferred_element_type=jnp.float32)

    def keep_norm(incoming, previous):
        return previous

    def backward_turn(grad_norm, inner_sum, previous):
        scaled = grad_norm * norm_scale
        grad_mixed = (row_scale * (scaled - normed * (inner_sum / D)[:, None])).astype(jnp.bfloat16)
        grad_code = jnp.dot(grad_mixed, recv_local.T, preferred_element_type=jnp.float32).astype(
            jnp.bfloat16
        )
        return (grad_mixed, grad_code)

    def keep_back(grad_norm, inner_sum, previous):
        return previous

    incoming = code_cotangent
    grad_norm = jnp.zeros((tokens_here, feature_cols), jnp.float32)
    back_state = (jnp.zeros((tokens_here, feature_cols), jnp.bfloat16), jnp.zeros_like(input_code))
    for turn_index in range(section_count):
        is_live = section_index == section_count - 1 - turn_index
        if turn_index > 0:
            shifted = from_behind(back_state[1], "pipe", -1)
            incoming = jnp.where(is_live, shifted, incoming)
        grad_norm = lax.cond(is_live, backward_norm, keep_norm, incoming, grad_norm)
        inner_sum = lax.psum(jnp.sum(grad_norm * norm_scale * normed, axis=1), "tensor")
        back_state = lax.cond(is_live, backward_turn, keep_back, grad_norm, inner_sum, back_state)
    grad_mixed, grad_code = back_state
    send_term = jnp.einsum("td,tc->dc", out_rows, incoming, preferred_element_type=jnp.float32)
    recv_term = jnp.einsum("tc,td->cd", held_code, grad_mixed, preferred_element_type=jnp.float32)
    gain_term = jnp.sum(grad_norm * normed, axis=0)
    send_sum, recv_sum, gain_sum = (
        lax.psum(send_term.astype(jnp.bfloat16), "dp").astype(jnp.float32),
        lax.psum(recv_term.astype(jnp.bfloat16), "dp").astype(jnp.float32),
        lax.psum(gain_term.astype(jnp.bfloat16), "dp").astype(jnp.float32),
    )
    code_term = jnp.einsum("td,cd->tc", grad_mixed, dec_local, preferred_element_type=jnp.float32)
    code_grad = lax.psum(code_term.astype(jnp.bfloat16), "tensor")
    dec_term = jnp.einsum("tc,td->cd", mix_code, grad_mixed, preferred_element_type=jnp.float32)
    dec_sum = lax.psum_scatter(dec_term.astype(jnp.bfloat16), "dp", scatter_dimension=0, tiled=True)
    head_term = jnp.einsum(
        "th,tc->hc", head_row_block, code_grad, preferred_element_type=jnp.float32
    )
    head_sum = lax.psum(head_term.astype(jnp.bfloat16), "dp")
    proj_grad = jnp.dot(head_sum, enc_local, preferred_element_type=jnp.float32)
    enc_term = lax.dot_general(
        head_sum, proj_local, (((0,), (0,)), ((), ())), preferred_element_type=jnp.float32
    )
    enc_sum = lax.psum_scatter(
        enc_term.astype(jnp.bfloat16), "tensor", scatter_dimension=0, tiled=True
    )
    heads_grad = lax.dot_general(
        code_grad.astype(jnp.float32), folded, (((1,), (1,)), ((), ())), precision=highest_precision
    )
    return (
        sent_code[None],
        grad_code[None],
        heads_grad.astype(jnp.bfloat16)[None],
        proj_grad.astype(jnp.bfloat16)[None],
        enc_sum[None],
        dec_sum[None],
        gain_sum[None],
        send_sum.astype(jnp.bfloat16)[None],
        recv_sum.astype(jnp.bfloat16)[None],
    )


def solution(mesh):
    return jax.shard_map(
        on_device,
        mesh=mesh,
        in_specs=(
            P("pipe", "dp", "tensor"),
            P("pipe", "tensor", "dp"),
            P("pipe", None, "dp"),
            P("pipe", None, "tensor"),
            P("pipe", "tensor"),
            P("pipe", "tensor", None),
            P("pipe", None, "tensor"),
            P("dp", "tensor"),
            P("dp", "tensor"),
        ),
        out_specs=(
            P("pipe", "dp", "tensor"),
            P("pipe", "dp", "tensor"),
            P("pipe", "dp", "tensor"),
            P("pipe", "tensor", "dp"),
            P("pipe", "tensor", "dp"),
            P("pipe", "dp", "tensor"),
            P("pipe", "tensor"),
            P("pipe", "tensor", None),
            P("pipe", None, "tensor"),
        ),
        check_vma=False,
    )
```

profile of v0, /device:TPU:0, one launch (start us, length us, event | category | flops | bytes accessed | tf_op | source)
XLA Modules:
  0.0 352.1 jit_solution(3017223903138532589)
XLA Ops:
  7.2 1.5 copy-done
  8.8 3.5 fusion.8
  12.3 54.6 %all-reduce.6.cloned.1.call-done = bf16[1024,512]{1,0:T(8,128)(2,1)} async-done(((bf16[1024,512]{1,0:T(8,128)(2,1)}), bf16[1024,512]{1,0:T(8,128)(2,1)}) %all-reduce.6.cloned.1.call-update) | async-done | bytes 1048592 | tf_op jit(solution)/shard_map/psum | solution.py:44
  67.0 2.4 fusion.18
  69.4 42.7 %all-reduce.8.cloned.1.call-done = bf16[128,512]{0,1:T(8,128)(2,1)} async-done(((bf16[128,512]{0,1:T(8,128)(2,1)}), bf16[128,512]{0,1:T(8,128)(2,1)}) %all-reduce.8.cloned.1.call-update) | async-done | bytes 131088 | tf_op jit(solution)/shard_map/psum | solution.py:46
  112.1 2.0 fusion.20
  114.1 1.3 conditional.8
  114.1 1.3 convolution_add_fusion
  115.5 0.1 multiply_reduce_fusion.4
  115.6 8.9 %psum.79 = f32[128]{0:T(128)S(1)} all-reduce(f32[128]{0:T(128)S(1)} %multiply_reduce_fusion.4), channel_id=1, replica_groups=mesh['dp'=4,'pipe'=2,'tensor'=4] {'tensor'}, use_global_device_ids=true, to_apply=%region_5.0 | all-reduce | flops 128 | bytes 1024 | tf_op jit(solution)/shard_map/psum | solution.py:81
  124.5 2.0 conditional.9
  124.6 0.8 multiply_convert_fusion
  125.4 1.2 convolution_convert_fusion
  126.6 1.3 collective-permute-start
  127.9 0.9 conditional.12
  127.9 0.9 broadcast.42
  128.8 0.1 multiply_reduce_fusion.3
  128.9 8.8 %psum.80 = f32[128]{0:T(128)S(1)} all-reduce(f32[128]{0:T(128)S(1)} %multiply_reduce_fusion.3), channel_id=1, replica_groups=mesh['dp'=4,'pipe'=2,'tensor'=4] {'tensor'}, use_global_device_ids=true, to_apply=%region_11.12 | all-reduce | flops 128 | bytes 1024 | tf_op jit(solution)/shard_map/psum | solution.py:81
  137.7 1.2 multiply_reduce_fusion.2
  138.9 9.0 %psum.81 = f32[128]{0:T(128)S(1)} all-reduce(f32[128]{0:T(128)S(1)} %multiply_reduce_fusion.2), channel_id=1, replica_groups=mesh['dp'=4,'pipe'=2,'tensor'=4] {'tensor'}, use_global_device_ids=true, to_apply=%region_17.18 | all-reduce | flops 128 | bytes 1024 | tf_op jit(solution)/shard_map/psum | solution.py:113
  147.9 0.7 conditional.13
  147.9 0.7 broadcast.43
  148.7 1.3 collective-permute-start.1
  149.9 3.3 collective-permute-done.1
  153.3 1.1 conditional.14
  153.3 1.0 fusion.27
  154.3 1.2 multiply_reduce_fusion
  155.5 8.0 %psum.82 = f32[128]{0:T(128)S(1)} all-reduce(f32[128]{0:T(128)S(1)} %get-tuple-element.178), channel_id=1, replica_groups=mesh['dp'=4,'pipe'=2,'tensor'=4] {'tensor'}, use_global_device_ids=true, to_apply=%region_23.24 | all-reduce | flops 128 | bytes 1024 | tf_op jit(solution)/shard_map/psum | solution.py:113
  163.5 3.2 conditional.15
  163.5 1.9 multiply_convert_fusion.3
  165.5 1.3 fusion.3
  166.7 2.5 convolution_convert_fusion.9
  169.2 0.0 all-reduce.12.cloned.1.call-start
  169.3 1.9 fusion.17
  171.2 1.9 fusion.16
  173.1 38.3 %all-reduce.10.cloned.1.call-done = bf16[128,512]{1,0:T(8,128)(2,1)} async-done(((bf16[128,512]{1,0:T(8,128)(2,1)}), bf16[128,512]{1,0:T(8,128)(2,1)}) %all-reduce.10.cloned.1.call-update) | async-done | bytes 131088 | tf_op jit(solution)/shard_map/psum | solution.py:125
  211.4 2.3 fusion.14
  213.9 2.4 convolution_convert_fusion.4
  216.3 68.8 %all-reduce.12.cloned.1.call-done = (bf16[1024,512]{0,1:T(8,128)(2,1)}, bf16[1,1024,128]{2,1,0:T(8,128)(2,1)}, bf16[1,128,1024]{2,1,0:T(8,128)(2,1)}) async-done(((bf16[1024,512]{0,1:T(8,128)(2,1)}, bf16[1,1024,128]{2,1,0:T(8,128)(2,1)}, bf16[1,128,1024]{2,1,0:T(8,128)(2,1)}), (bf16[1024,512]{0,1:T(8,128)(2,1)}, bf16[1,1024,128]{2,1,0:T(8,128)(2,1)}, ...) | async-done | bytes 1572880 | tf_op jit(solution)/shard_map/psum | solution.py:131
  285.1 3.6 %fusion.11 = bf16[512,1024]{1,0:T(8,128)(2,1)} fusion(bf16[1024,512]{0,1:T(8,128)(2,1)} %get-tuple-element.179, bf16[1,1024,1024]{2,1,0:T(8,128)(2,1)S(1)} %copy-done), kind=kOutput, calls=%fused_computation.28 | convolution fusion | flops 1074266112 | bytes 4194304 | tf_op jit(solution)/shard_map/dot_general | solution.py:133
  288.7 9.8 %psum.85 = bf16[1,1024]{1,0:T(2,128)(2,1)S(1)} all-reduce(bf16[1,1024]{1,0:T(2,128)(2,1)S(1)} %broadcast_in_dim.59), channel_id=1, replica_groups=mesh['dp'=4,'pipe'=2,'tensor'=4] {'dp'}, use_global_device_ids=true, to_apply=%region_31.32 | all-reduce | flops 1024 | bytes 4096 | tf_op jit(solution)/shard_map/psum | solution.py:122
  298.5 0.6 broadcast_in_dim.60
  299.1 1.2 fusion.15
  300.3 4.2 %convert_bitcast_fusion = bf16[1,1024,1024]{2,1,0:T(8,128)(2,1)} fusion(bf16[1024,512]{0,1:T(8,128)(2,1)} %get-tuple-element.179, bf16[1,512,1024]{2,1,0:T(8,128)(2,1)} %param.27), kind=kOutput, calls=%fused_computation.24 | convolution fusion | flops 1074790400 | bytes 4194304 | tf_op jit(solution)/shard_map/dot_general | solution.py:132
  304.5 9.6 %reduce-scatter.5.cloned.1.call-done = bf16[128,1024]{1,0:T(8,128)(2,1)} async-done(((bf16[512,1024]{1,0:T(8,128)(2,1)}), bf16[128,1024]{1,0:T(8,128)(2,1)}) %reduce-scatter.5.cloned.1.call-update) | async-done | bytes 262160 | tf_op jit(solution)/shard_map/reduce_scatter | solution.py:127
  314.1 29.7 %reduce-scatter.3.cloned.1.call-done = bf16[128,1024]{1,0:T(8,128)(2,1)} async-done(((bf16[512,1024]{1,0:T(8,128)(2,1)}), bf16[128,1024]{1,0:T(8,128)(2,1)}) %reduce-scatter.3.cloned.1.call-update) | async-done | bytes 262160 | tf_op jit(solution)/shard_map/reduce_scatter | solution.py:136
  343.8 0.7 copy.58
  344.5 0.7 copy.59
  (49 shorter events, 0.4 us)
Async XLA Ops:
  7.2 1.6 copy-start
  7.2 59.8 %copy-start.4 = (bf16[1,128,1024]{2,1,0:T(8,128)(2,1)S(1)}, bf16[1,128,1024]{2,1,0:T(8,128)(2,1)}, u32[]{:S(2)}) copy-start(bf16[1,128,1024]{2,1,0:T(8,128)(2,1)} %param.25) | copy-start | bytes 786436
  7.2 59.8 %all-reduce.6.cloned.1.call-start = ((), (), s32[]{:S(2)}) async-start(), calls=%async_computation.2 | async-start | bytes 2097152 | tf_op jit(solution)/shard_map/psum | solution.py:44
  12.3 99.8 %copy-start.3 = (bf16[1,512,1024]{2,1,0:T(8,128)(2,1)S(1)}, bf16[1,512,1024]{2,1,0:T(8,128)(2,1)}, u32[]{:S(2)}) copy-start(bf16[1,512,1024]{2,1,0:T(8,128)(2,1)} %param.28) | copy-start | bytes 3145732
  12.3 101.9 %copy-start.12 = (bf16[128,128]{1,0:T(8,128)(2,1)S(1)}, bf16[128,128]{1,0:T(8,128)(2,1)}, u32[]{:S(2)}) copy-start(bf16[128,128]{1,0:T(8,128)(2,1)} %param.32) | copy-start | bytes 98308
  12.3 99.8 %all-reduce.8.cloned.1.call-start = ((), (), s32[]{:S(2)}) async-start(), calls=%async_computation.3 | async-start | bytes 262144 | tf_op jit(solution)/shard_map/psum | solution.py:46
  69.3 55.2 %copy-start.1 = (bf16[1,1024,128]{2,1,0:T(8,128)(2,1)S(1)}, bf16[1,1024,128]{2,1,0:T(8,128)(2,1)}, u32[]{:S(2)}) copy-start(bf16[1,1024,128]{2,1,0:T(8,128)(2,1)} %param.30) | copy-start | bytes 786436
  69.4 55.2 %copy-start.10 = (f32[1,1024]{1,0:T(1,128)S(1)}, f32[1,1024]{1,0:T(1,128)}, u32[]{:S(2)}) copy-start(f32[1,1024]{1,0:T(1,128)} %param.29) | copy-start | bytes 12292
  69.4 142.1 %all-reduce.10.cloned.1.call-start = ((), (), s32[]{:S(2)}) async-start(), calls=%async_computation.4 | async-start | bytes 262144 | tf_op jit(solution)/shard_map/psum | solution.py:125
  115.5 12.4 %copy-start.11 = (bf16[128,128]{1,0:T(8,128)(2,1)S(1)}, bf16[128,128]{1,0:T(8,128)(2,1)}, u32[]{:S(2)}) copy-start(bf16[128,128]{1,0:T(8,128)(2,1)} %param.33) | copy-start | bytes 98308
  126.6 2.2 copy-start.13
  126.6 2.2 collective-permute-start
  148.7 4.6 %collective-permute-start.1 = (bf16[128,128]{1,0:T(8,128)(2,1)S(1)}, bf16[128,128]{1,0:T(8,128)(2,1)S(1)}, u32[]{:S(2)}, u32[]{:S(2)}) collective-permute-start(bf16[128,128]{1,0:T(8,128)(2,1)S(1)} %get-tuple-element.219), channel_id=1, source_target_pairs={{4,0},{5,1},{6,2},{7,3},{12,8},{13,9},{14,10},{15,11},{20,16},{21,... | collective-permute-start | bytes 98312 | tf_op jit(solution)/shard_map/ppermute | solution.py:16
  163.5 47.9 %copy-start.5 = (bf16[1,128,1024]{2,1,0:T(8,128)(2,1)S(1)}, bf16[1,128,1024]{2,1,0:T(8,128)(2,1)}, u32[]{:S(2)}) copy-start(bf16[1,128,1024]{2,1,0:T(8,128)(2,1)} %param.25) | copy-start | bytes 786436
  166.7 47.1 %copy-start.14 = (bf16[1,128,128]{2,1,0:T(8,128)(2,1)}, bf16[1,128,128]{2,1,0:T(8,128)(2,1)S(1)}, u32[]{:S(2)}) copy-start(bf16[1,128,128]{2,1,0:T(8,128)(2,1)S(1)} %get-tuple-element.221) | copy-start | bytes 98308
  169.2 44.6 %copy-start.6 = (bf16[128,512]{0,1:T(8,128)(2,1)S(1)}, bf16[128,512]{0,1:T(8,128)(2,1)}, u32[]{:S(2)}) copy-start(bf16[128,512]{0,1:T(8,128)(2,1)} %all-reduce.8.cloned.1.call-done) | copy-start | bytes 393220
  169.2 115.8 %all-reduce.12.cloned.1.call-start = ((), (), s32[]{:S(2)}) async-start(), calls=%async_computation.7 | async-start | bytes 3145728 | tf_op jit(solution)/shard_map/psum | solution.py:131
  213.8 100.3 %reduce-scatter.5.cloned.1.call-start = ((), (), s32[]{:S(2)}) async-start(), calls=%async_computation.6 | async-start | bytes 1310720 | tf_op jit(solution)/shard_map/reduce_scatter | solution.py:127
  216.3 127.5 %reduce-scatter.3.cloned.1.call-start = ((), (), s32[]{:S(2)}) async-start(), calls=%async_computation.5 | async-start | bytes 1310720 | tf_op jit(solution)/shard_map/reduce_scatter | solution.py:136
  285.1 14.0 %copy-start.2 = (bf16[1024,512]{1,0:T(8,128)(2,1)S(1)}, bf16[1024,512]{1,0:T(8,128)(2,1)}, u32[]{:S(2)}) copy-start(bf16[1024,512]{1,0:T(8,128)(2,1)} %all-reduce.6.cloned.1.call-done) | copy-start | bytes 3145732
  285.1 14.0 %copy-start.7 = (bf16[128,512]{1,0:T(8,128)(2,1)S(1)}, bf16[128,512]{1,0:T(8,128)(2,1)}, u32[]{:S(2)}) copy-start(bf16[128,512]{1,0:T(8,128)(2,1)} %all-reduce.10.cloned.1.call-done) | copy-start | bytes 393220
  300.3 43.5 %copy-start.9 = (bf16[1,1024,128]{2,1,0:T(8,128)(2,1)S(1)}, bf16[1,1024,128]{2,1,0:T(8,128)(2,1)}, u32[]{:S(2)}) copy-start(bf16[1,1024,128]{2,1,0:T(8,128)(2,1)} %get-tuple-element.227) | copy-start | bytes 786436
  300.3 44.2 %copy-start.8 = (bf16[1,128,1024]{2,1,0:T(8,128)(2,1)S(1)}, bf16[1,128,1024]{2,1,0:T(8,128)(2,1)}, u32[]{:S(2)}) copy-start(bf16[1,128,1024]{2,1,0:T(8,128)(2,1)} %get-tuple-element.228) | copy-start | bytes 786436
Sparse Core Ops, SparseCore 0:
  12.4 54.5 all-reduce.5
  70.7 41.3 all-reduce.7
  169.3 42.0 all-reduce.9
  215.2 69.8 all-reduce.11
  287.9 26.1 reduce-scatter.4
  317.4 26.3 reduce-scatter.2
where the time goes:
time: 353 us; the launch traced here: 352 us
  waiting for transfers between devices  247 us (70%)
  blocking collectives  44.5 us (13%)
  matrix products  32.6 us (9%)
  between operations  14.3 us (4%)
  other arithmetic  6 us (2%)
  local copies, waits for them, and re-layouts  4.62 us (1%)
    psum x1, waiting for transfers between devices, on_device(): head_sum = lax.psum(head_term.astype(jnp.bfloat16), 'dp')  68.8 us
    psum x1, waiting for transfers between devices, on_device(): folded = lax.psum(local_fold.astype(jnp.bfloat16), 'dp').astype(jnp.float32)  54.6 us
    psum x1, waiting for transfers between devices, on_device(): mix_code = lax.psum(partial_code.astype(jnp.bfloat16), 'tensor')  42.7 us
    psum x1, waiting for transfers between devices, on_device(): code_grad = lax.psum(code_term.astype(jnp.bfloat16), 'tensor')  38.3 us
    reduce_scatter x1, waiting for transfers between devices, on_device(): lax.psum_scatter(enc_term.astype(jnp.bfloat16), 'tensor', scatter_dimensi...  29.7 us
    psum x2, blocking collectives, on_device(): totals = lax.psum(jnp.sum(mixed_rows * mixed_rows, axis=1), 'tensor')  17.7 us
    psum x2, blocking collectives, on_device(): lax.psum(jnp.sum(grad_norm * norm_scale * normed, axis=1), 'tensor')  17 us
    psum x1, blocking collectives, on_device(): lax.psum(gain_term.astype(jnp.bfloat16), 'dp').astype(jnp.float32)  9.78 us
  transfers between devices with their start and end apart: 8, of which 7 were waited for; matrix products, arithmetic and copies ran while one was open for 5% of the time, Pallas kernels for 0%

commit v1 on v0

v1 whole, which is shorter than its diff:
```python
import jax
import jax.numpy as jnp
from jax import lax
from jax.sharding import PartitionSpec as P

epsilon = 1e-05
f32 = jnp.float32
bf16 = jnp.bfloat16


def shift(shard, axis, by):
    devices = lax.axis_size(axis)
    return lax.ppermute(shard, axis, [(i, (i + by) % devices) for i in range(devices)])


def move(shard, axis, by):
    devices = lax.axis_size(axis)
    pairs = [(i, i + by) for i in range(devices) if 0 <= i + by < devices]
    return lax.ppermute(shard, axis, pairs)


def gathered(shard, axis):
    return [shard] + [shift(shard, axis, -k) for k in range(1, lax.axis_size(axis))]


def scatter_sum(blocks, axis):
    total = blocks[0].astype(f32)
    for k in range(1, len(blocks)):
        total = total + shift(blocks[k].astype(bf16), axis, k).astype(f32)
    return total


def small_sum(rows, axis):
    total = rows
    for k in range(1, lax.axis_size(axis)):
        total = total + shift(rows, axis, k)
    return total


def rolled_rows(matrix, index, count):
    size = matrix.shape[0] // count
    doubled = jnp.concatenate([matrix, matrix[:-size]])
    return lax.dynamic_slice_in_dim(doubled, index * size, matrix.shape[0])


def dot(left, right, over):
    return lax.dot_general(left, right, ((over[0], over[1]), ((), ())), preferred_element_type=f32)


def on_device(
    heads_out,
    out_proj,
    encoder,
    decoder,
    norm_gain,
    send_encoder,
    recv_decoder,
    input_code,
    code_cotangent,
):
    sections = lax.axis_size("pipe")
    section = lax.axis_index("pipe")
    groups = lax.axis_size("dp")
    parts = lax.axis_size("tensor")
    part = lax.axis_index("tensor")
    group = lax.axis_index("dp")
    width = norm_gain.shape[1] * parts
    proj = out_proj[0]
    enc = rolled_rows(encoder[0], part, parts)
    dec = rolled_rows(decoder[0], part, parts)
    gain = norm_gain[0]
    send = send_encoder[0]
    recv = recv_decoder[0]
    tokens = input_code.shape[0]
    code_cols = input_code.shape[1]

    head_rows = jnp.concatenate(gathered(heads_out[0], "dp"))
    received = jnp.concatenate(gathered(input_code, "dp"))
    incoming = jnp.concatenate(gathered(code_cotangent, "dp"))

    local_fold = dot(proj, enc, ((1,), (1,)))
    local_fold = local_fold.astype(bf16)
    partial = dot(head_rows, local_fold, ((1,), (0,)))
    over_parts = scatter_sum(
        [partial[:, k * code_cols : (k + 1) * code_cols] for k in range(parts)], "tensor"
    )
    own_code = scatter_sum(
        [over_parts[k * tokens : (k + 1) * tokens] for k in range(groups)], "dp"
    ).astype(bf16)
    code_block = jnp.concatenate(gathered(own_code, "dp"))
    mix_code = jnp.concatenate(gathered(code_block, "tensor"), axis=1)
    fold_in, mix_code = lax.optimization_barrier((local_fold, mix_code))
    fold = lax.psum(fold_in, "dp")
    attention = dot(mix_code, dec, ((1,), (0,)))

    for turn in range(sections):
        if turn > 0:
            received = jnp.where(section == turn, move(sent, "pipe", 1), received)
        mixed = attention + dot(received, recv, ((1,), (0,)))
        totals = small_sum(jnp.sum(mixed * mixed, axis=1), "tensor")
        row_scale = lax.rsqrt(totals / width + epsilon)[:, None]
        scaled_rows = (mixed * gain).astype(bf16)
        sent = (row_scale * dot(scaled_rows, send, ((1,), (0,)))).astype(bf16)
    normed = mixed * row_scale
    out_rows = (normed * gain).astype(bf16)
    for turn in range(sections):
        if turn > 0:
            incoming = jnp.where(
                section == sections - 1 - turn, move(returned, "pipe", -1), incoming
            )
        grad_norm = dot(incoming, send, ((1,), (1,)))
        scaled = grad_norm * gain
        inner = small_sum(jnp.sum(scaled * normed, axis=1), "tensor")[:, None] / width
        grad_mixed = (row_scale * (scaled - normed * inner)).astype(bf16)
        returned = dot(grad_mixed, recv, ((1,), (1,))).astype(bf16)

    code_term = dot(grad_mixed, dec, ((1,), (1,)))
    code_block = scatter_sum(
        [code_term[:, k * code_cols : (k + 1) * code_cols] for k in range(parts)], "tensor"
    ).astype(bf16)
    code_blocks = gathered(code_block, "tensor")
    code_grad = jnp.concatenate(code_blocks, axis=1)
    head_sum = dot(head_rows, code_grad, ((0,), (0,))).astype(bf16)
    enc_term = dot(head_sum, proj, ((0,), (0,)))
    enc_grad = scatter_sum(
        [enc_term[k * code_cols : (k + 1) * code_cols] for k in range(parts)], "tensor"
    ).astype(bf16)
    proj_grad = dot(head_sum, enc, ((1,), (0,))).astype(bf16)
    heads_grad = dot(code_grad[:tokens], fold, ((1,), (1,))).astype(bf16)

    codes = mix_code.shape[1]
    mine = lax.rem(group * (codes // groups) + codes - part * code_cols, codes)
    mix_cols = lax.dynamic_slice_in_dim(mix_code, mine, codes // groups, 1)
    dec_grad = dot(mix_cols, grad_mixed, ((0,), (0,))).astype(bf16)
    gain_grad = jnp.sum(grad_norm * normed, axis=0)
    send_grad = dot(out_rows, incoming, ((0,), (0,))).astype(bf16)
    recv_grad = dot(received, grad_mixed, ((0,), (0,))).astype(bf16)
    return (
        sent[None, :tokens],
        returned[None, :tokens],
        heads_grad[None],
        proj_grad[None],
        enc_grad[None],
        dec_grad[None],
        gain_grad[None],
        send_grad[None],
        recv_grad[None],
    )


def solution(mesh):
    return jax.shard_map(
        on_device,
        mesh=mesh,
        in_specs=(
            P("pipe", "dp", "tensor"),
            P("pipe", "tensor", "dp"),
            P("pipe", None, "dp"),
            P("pipe", None, "tensor"),
            P("pipe", "tensor"),
            P("pipe", "tensor", None),
            P("pipe", None, "tensor"),
            P("dp", "tensor"),
            P("dp", "tensor"),
        ),
        out_specs=(
            P("pipe", "dp", "tensor"),
            P("pipe", "dp", "tensor"),
            P("pipe", "dp", "tensor"),
            P("pipe", "tensor", "dp"),
            P("pipe", "tensor", "dp"),
            P("pipe", "dp", "tensor"),
            P("pipe", "tensor"),
            P("pipe", "tensor", None),
            P("pipe", None, "tensor"),
        ),
        check_vma=False,
    )
```

time: 353 us -> 161 us (0.46)
  waiting for transfers between devices: 247 us -> 41.5 us
  starting transfers between devices: 2.82 us -> 62.7 us
  blocking collectives: 44.5 us -> 0 us
  local copies, waits for them, and re-layouts: 4.62 us -> 8.29 us
    psum x4 -> x1, waiting for transfers between devices: 204 us -> 0.01 us  [on_device(): fold = lax.psum(fold_in, 'dp')]
    ppermute x2 -> x44, starting transfers between devices: 2.57 us -> 62.7 us  [the longest x42 60.1 us: shift(): lax.ppermute(shard, axis, [(i, (i + by) % devices) for i in range(devices)])]
    psum x5 -> x0, blocking collectives: 44.5 us -> none  [the longest x2 17.7 us: on_device(): totals = lax.psum(jnp.sum(mixed_rows * mixed_rows, axis=1), 'tensor')]
    reduce_scatter x2 -> x0, waiting for transfers between devices: 39.3 us -> none  [the longest x1 29.7 us: on_device(): lax.psum_scatter(enc_term.astype(jnp.bfloat16), 'tensor', scatter_dimensi...]
    ppermute x2 -> x44, waiting for transfers between devices: 3.32 us -> 41.5 us  [the longest x42 40.2 us: shift(): lax.ppermute(shard, axis, [(i, (i + by) % devices) for i in range(devices)])]
    dot_general x15 -> x19, matrix products: 32.6 us -> 30.7 us  [dot(): lax.dot_general(left, right, ((over[0], over[1]), ((), ())), preferred_el...]
  transfers between devices with their start and end apart: 8 -> 45, of which waited for: 7 -> 28; matrix products, arithmetic and copies ran while one was open for 5% -> 24% of each run, Pallas kernels for 0% -> 0%
where the time goes in v1:
time: 161 us
  starting transfers between devices  62.7 us (39%)
  waiting for transfers between devices  41.5 us (26%)
  matrix products  30.7 us (19%)
  between operations  14.4 us (9%)
  local copies, waits for them, and re-layouts  8.29 us (5%)
  other arithmetic  3.06 us (2%)
    ppermute x42, starting transfers between devices, shift(): lax.ppermute(shard, axis, [(i, (i + by) % devices) for i in range(devices)])  60.1 us
    ppermute x42, waiting for transfers between devices, shift(): lax.ppermute(shard, axis, [(i, (i + by) % devices) for i in range(devices)])  40.2 us
    dot_general x19, matrix products, dot(): lax.dot_general(left, right, ((over[0], over[1]), ((), ())), preferred_el...  30.7 us
    unnamed x40, local copies, waits for them, and re-layouts  5.35 us
  transfers between devices with their start and end apart: 45, of which 28 were waited for; matrix products, arithmetic and copies ran while one was open for 24% of the time, Pallas kernels for 0%

profile of v1, /device:TPU:0, one launch (start us, length us, event | category | flops | bytes accessed | tf_op | source)
XLA Modules:
  0.0 160.6 jit_solution(17999352601523784534)
XLA Ops:
  7.2 4.1 %collective-permute-start.16 = (bf16[128,128]{1,0:T(8,128)(2,1)}, bf16[128,128]{1,0:T(8,128)(2,1)}, u32[]{:S(2)}, u32[]{:S(2)}) collective-permute-start(bf16[128,128]{1,0:T(8,128)(2,1)} %param.16), channel_id=1, source_target_pairs={{0,16},{8,24},{16,0},{24,8},{1,17},{9,25},{17,1},{25,9},{2,18},{10... | collective-permute-start | bytes 98312 | tf_op jit(solution)/shard_map/ppermute | solution.py:13
  11.3 1.3 collective-permute-start.15
  14.4 2.9 %collective-permute-start = (bf16[128,1024]{1,0:T(8,128)(2,1)}, bf16[128,1024]{1,0:T(8,128)(2,1)}, u32[]{:S(2)}, u32[]{:S(2)}) collective-permute-start(bf16[128,1024]{1,0:T(8,128)(2,1)} %bitcast.89), channel_id=1, source_target_pairs={{0,24},{8,0},{16,8},{24,16},{1,25},{9,1},{17,9},{25,17},{2,26},{10... | collective-permute-start | bytes 786440 | tf_op jit(solution)/shard_map/ppermute | solution.py:13
  19.4 2.6 %fusion.4 = bf16[512,1024]{1,0:T(8,128)(2,1)S(1)} fusion(bf16[1,1024,1024]{2,1,0:T(8,128)(2,1)S(1)} %copy-done, s32[]{:T(128)S(6)} %select_n.21, bf16[512,1024]{1,0:T(8,128)(2,1)} %bitcast.77, bf16[384,1024]{1,0:T(8,128)(2,1)S(1)} %slice_bitcast_fusion.1), kind=kOutput, calls=%fused_computation.21 | convolution fusion | flops 1076363264 | bytes 4980740 | tf_op jit(solution)/shard_map/dot_general | solution.py:47
  22.0 2.1 %collective-permute-done.2 = bf16[128,1024]{1,0:T(8,128)(2,1)} collective-permute-done((bf16[128,1024]{1,0:T(8,128)(2,1)}, bf16[128,1024]{1,0:T(8,128)(2,1)}, u32[]{:S(2)}, u32[]{:S(2)}) %collective-permute-start.2) | collective-permute-done | bytes 262176 | tf_op jit(solution)/shard_map/ppermute | solution.py:13
  24.1 9.7 %collective-permute-done.1 = bf16[128,1024]{1,0:T(8,128)(2,1)} collective-permute-done((bf16[128,1024]{1,0:T(8,128)(2,1)}, bf16[128,1024]{1,0:T(8,128)(2,1)}, u32[]{:S(2)}, u32[]{:S(2)}) %collective-permute-start.1) | collective-permute-done | bytes 262176 | tf_op jit(solution)/shard_map/ppermute | solution.py:13
  33.8 1.9 %fusion.77 = (bf16[512,512]{1,0:T(8,128)(2,1)S(1)}, f32[512,512]{1,0:T(8,128)S(1)}) fusion(bf16[512,1024]{1,0:T(8,128)(2,1)S(1)} %fusion.4, bf16[128,1024]{1,0:T(8,128)(2,1)} %collective-permute-done.2, bf16[128,1024]{1,0:T(8,128)(2,1)} %collective-permute-done.1, bf16[128,1024]{1,0:T(8,128)(2,1)} %collective-permute-done, bf16[128,1024]{1,0:T(8,128)(2,1)S(1)} %bitcast.90), kind=kOutput, calls=%fused_computation.119 | convolution fusion | flops 541327360 | bytes 3670016 | tf_op jit(solution)/shard_map/dot_general | solution.py:47
  35.8 1.5 collective-permute-start.3
  37.3 1.4 collective-permute-start.5
  38.8 1.5 collective-permute-start.4
  41.2 1.7 %collective-permute-done.3 = bf16[512,128]{1,0:T(8,128)(2,1)S(1)} collective-permute-done((bf16[512,128]{1,0:T(8,128)(2,1)S(1)}, bf16[512,128]{1,0:T(8,128)(2,1)S(1)}, u32[]{:S(2)}, u32[]{:S(2)}) %collective-permute-start.3) | collective-permute-done | bytes 131104 | tf_op jit(solution)/shard_map/ppermute | solution.py:13
  42.9 1.4 collective-permute-done.5
  44.4 6.2 %collective-permute-start.6 = (bf16[128,128]{1,0:T(8,128)(2,1)S(1)}, bf16[128,128]{1,0:T(8,128)(2,1)S(1)}, u32[]{:S(2)}, u32[]{:S(2)}) collective-permute-start(bf16[128,128]{1,0:T(8,128)(2,1)S(1)} %get-tuple-element.26), channel_id=1, source_target_pairs={{0,8},{8,16},{16,24},{24,0},{1,9},{9,17},{17,25},{25,1},{2,10},{10... | collective-permute-start | bytes 98312 | tf_op jit(solution)/shard_map/ppermute | solution.py:13
  54.5 1.8 %collective-permute-done.7 = bf16[128,128]{1,0:T(8,128)(2,1)S(1)} collective-permute-done((bf16[128,128]{1,0:T(8,128)(2,1)S(1)}, bf16[128,128]{1,0:T(8,128)(2,1)S(1)}, u32[]{:S(2)}, u32[]{:S(2)}) %collective-permute-start.7) | collective-permute-done | bytes 32800 | tf_op jit(solution)/shard_map/ppermute | solution.py:13
  57.5 1.4 collective-permute-start.10
  61.0 1.4 collective-permute-done.11
  63.6 1.7 %collective-permute-start.14 = (bf16[512,128]{1,0:T(8,128)(2,1)S(1)}, bf16[512,128]{1,0:T(8,128)(2,1)S(1)}, u32[]{:S(2)}, u32[]{:S(2)}) collective-permute-start(bf16[512,128]{1,0:T(8,128)(2,1)S(1)} %pad_maximum_fusion.4), channel_id=1, source_target_pairs={{0,1},{1,2},{2,3},{3,0},{4,5},{5,6},{6,7},{7,4},{8,9},{9,10},{10,1... | collective-permute-start | bytes 393224 | tf_op jit(solution)/shard_map/ppermute | solution.py:13
  65.2 1.9 %collective-permute-start.13 = (bf16[512,128]{1,0:T(8,128)(2,1)S(1)}, bf16[512,128]{1,0:T(8,128)(2,1)S(1)}, u32[]{:S(2)}, u32[]{:S(2)}) collective-permute-start(bf16[512,128]{1,0:T(8,128)(2,1)S(1)} %pad_maximum_fusion.4), channel_id=1, source_target_pairs={{0,2},{1,3},{2,0},{3,1},{4,6},{5,7},{6,4},{7,5},{8,10},{9,11},{10,... | collective-permute-start | bytes 393224 | tf_op jit(solution)/shard_map/ppermute | solution.py:13
  68.8 2.5 %collective-permute-start.25 = (bf16[128,128]{1,0:T(8,128)(2,1)}, bf16[128,128]{1,0:T(8,128)(2,1)}, u32[]{:S(2)}, u32[]{:S(2)}) collective-permute-start(bf16[128,128]{1,0:T(8,128)(2,1)} %param.17), channel_id=1, source_target_pairs={{0,24},{8,0},{16,8},{24,16},{1,25},{9,1},{17,9},{25,17},{2,26},{10... | collective-permute-start | bytes 98312 | tf_op jit(solution)/shard_map/ppermute | solution.py:13
  73.0 1.9 %fusion.67 = f32[512,1024]{1,0:T(8,128)S(1)} fusion(bf16[512,512]{1,0:T(8,128)(2,1)} %pad_maximum_fusion.1, s32[]{:T(128)S(6)} %select_n.21, bf16[512,1024]{1,0:T(8,128)(2,1)S(1)} %bitcast.74, bf16[384,1024]{1,0:T(8,128)(2,1)} %slice_bitcast_fusion), kind=kOutput, calls=%fused_computation.112 | convolution fusion | flops 538968064 | bytes 4456452 | tf_op jit(solution)/shard_map/dot_general | solution.py:47
  74.9 2.0 %multiply_reduce_fusion.4 = (f32[512]{0:T(512)S(1)}, f32[512,1024]{1,0:T(8,128)}) fusion(f32[512,1024]{1,0:T(8,128)S(1)} %fusion.67, bf16[512,128]{1,0:T(8,128)(2,1)S(1)} %constant_dynamic-update-slice_fusion, bf16[1,128,1024]{2,1,0:T(8,128)(2,1)S(1)} %copy-done.4), kind=kOutput, calls=%fused_computation.14 | convolution fusion | flops 135790080 | bytes 4589568 | tf_op jit(solution)/shard_map/dot_general | solution.py:47
  76.9 2.0 %collective-permute-start.20 = (f32[512]{0:T(512)S(1)}, f32[512]{0:T(512)S(1)}, u32[]{:S(2)}, u32[]{:S(2)}) collective-permute-start(f32[512]{0:T(512)S(1)} %get-tuple-element.31), channel_id=1, source_target_pairs={{0,3},{1,0},{2,1},{3,2},{4,7},{5,4},{6,5},{7,6},{8,11},{9,8},{10,9... | collective-permute-start | bytes 6152 | tf_op jit(solution)/shard_map/ppermute | solution.py:13
  80.5 1.3 collective-permute-start.27
  82.5 1.4 collective-permute-done.18
  84.0 2.0 %multiply_convert_fusion.9 = bf16[512,128]{1,0:T(8,128)(2,1)S(1)} fusion(f32[512]{0:T(512)S(1)} %add_rsqrt_fusion.1, bf16[1,1024,128]{2,1,0:T(8,128)(2,1)S(1)} %copy-done.5, f32[512,1024]{1,0:T(8,128)} %get-tuple-element.32, f32[1024]{0:T(1024)S(1)} %bitcast.79), kind=kOutput, calls=%fused_computation.74 | convolution fusion | flops 135397376 | bytes 2496512 | tf_op jit(solution)/shard_map/dot_general | solution.py:47
  86.0 1.3 collective-permute-start.21
  88.9 1.7 %multiply_reduce_fusion.3 = (f32[512]{0:T(512)S(1)}, f32[512,1024]{1,0:T(8,128)}) fusion(f32[512,1024]{1,0:T(8,128)S(1)} %copy-done.3, bf16[1,128,1024]{2,1,0:T(8,128)(2,1)S(1)} %copy-done.4, bf16[512,128]{1,0:T(8,128)(2,1)S(1)} %collective-permute-done.21, bf16[512,128]{1,0:T(8,128)(2,1)S(1)} %constant_dynamic-update-slice_fusion, pred[]{:T(512)S(6)} %eq.6), kind=kOutput, calls=%fused_computation.12 | convolution fusion | flops 135855616 | bytes 4720641 | tf_op jit(solution)/shard_map/dot_general | solution.py:47
  92.6 1.6 collective-permute-start.22
  94.9 2.1 %collective-permute-done.22 = f32[512]{0:T(512)S(1)} collective-permute-done((f32[512]{0:T(512)S(1)}, f32[512]{0:T(512)S(1)}, u32[]{:S(2)}, u32[]{:S(2)}) %collective-permute-start.22) | collective-permute-done | bytes 2080 | tf_op jit(solution)/shard_map/ppermute | solution.py:13
  97.1 2.3 %multiply_reduce_fusion.2 = (f32[512]{0:T(512)S(1)}, f32[512,1024]{1,0:T(8,128)S(1)}) fusion(f32[512,1024]{1,0:T(8,128)} %get-tuple-element.34, f32[512]{0:T(512)S(1)} %add_rsqrt_fusion, f32[1024]{0:T(1024)S(1)} %bitcast.80, bf16[512,128]{1,0:T(8,128)(2,1)S(1)} %constant_dynamic-update-slice_fusion.4, bf16[1,1024,128]{2,1,0:T(8,128)(2,1)S(1)} %copy-done.5), kind=kOutput, calls=%fused_computation.10 | convolution fusion | flops 136314368 | bytes 4595712 | tf_op jit(solution)/shard_map/dot_general | solution.py:47
  100.0 1.5 collective-permute-start.29
  103.6 2.4 %collective-permute-done.28 = f32[512]{0:T(512)S(1)} collective-permute-done((f32[512]{0:T(512)S(1)}, f32[512]{0:T(512)S(1)}, u32[]{:S(2)}, u32[]{:S(2)}) %collective-permute-start.28) | collective-permute-done | bytes 2080 | tf_op jit(solution)/shard_map/ppermute | solution.py:13
  106.7 1.3 collective-permute-start.31
  112.3 1.3 collective-permute-start.32
  113.6 1.3 fusion.9
  115.1 1.7 %collective-permute-done.32 = f32[512]{0:T(512)S(1)} collective-permute-done((f32[512]{0:T(512)S(1)}, f32[512]{0:T(512)S(1)}, u32[]{:S(2)}, u32[]{:S(2)}) %collective-permute-start.32) | collective-permute-done | bytes 2080 | tf_op jit(solution)/shard_map/ppermute | solution.py:13
  120.5 2.5 %collective-permute-start.37 = (bf16[512,128]{0,1:T(8,128)(2,1)S(1)}, bf16[512,128]{0,1:T(8,128)(2,1)S(1)}, u32[]{:S(2)}, u32[]{:S(2)}) collective-permute-start(bf16[512,128]{0,1:T(8,128)(2,1)S(1)} %get-tuple-element.21), channel_id=1, source_target_pairs={{0,3},{1,0},{2,1},{3,2},{4,7},{5,4},{6,5},{7,6},{8,11},{9,8},{10,9... | collective-permute-start | bytes 393224 | tf_op jit(solution)/shard_map/ppermute | solution.py:13
  125.3 1.4 collective-permute-done.35
  128.1 1.7 %collective-permute-start.40 = (bf16[512,128]{0,1:T(8,128)(2,1)S(1)}, bf16[512,128]{0,1:T(8,128)(2,1)S(1)}, u32[]{:S(2)}, u32[]{:S(2)}) collective-permute-start(bf16[512,128]{0,1:T(8,128)(2,1)S(1)} %fusion.32), channel_id=1, source_target_pairs={{0,1},{1,2},{2,3},{3,0},{4,5},{5,6},{6,7},{7,4},{8,9},{9,10},{10,1... | collective-permute-start | bytes 393224 | tf_op jit(solution)/shard_map/ppermute | solution.py:13
  130.9 1.4 collective-permute-start.38
  132.4 1.9 %fusion.8 = bf16[1,128,1024]{2,1,0:T(8,128)(2,1)} fusion(bf16[512,1024]{1,0:T(8,128)(2,1)S(1)} %multiply_convert_fusion.1, bf16[512,512]{1,0:T(8,128)(2,1)} %pad_maximum_fusion.1, s32[]{:T(128)S(6)} %select_n.26), kind=kOutput, calls=%fused_computation.28 | convolution fusion | flops 134348800 | bytes 1441796 | tf_op jit(solution)/shard_map/dot_general | solution.py:47
  135.9 1.9 %convolution_convert_fusion = bf16[1024,512]{1,0:T(8,128)(2,1)S(1)} fusion(bf16[512,128]{0,1:T(8,128)(2,1)S(1)} %collective-permute-done.40, bf16[512,128]{0,1:T(8,128)(2,1)S(1)} %collective-permute-done.39, bf16[512,128]{0,1:T(8,128)(2,1)S(1)} %collective-permute-done.38, bf16[512,128]{0,1:T(8,128)(2,1)S(1)} %fusion.32, ...), kind=kOutput, calls=%fused_computation.22 | convolution fusion | flops 543686656 | bytes 2621440 | tf_op jit(solution)/shard_map/dot_general | solution.py:47
  139.1 1.7 %collective-permute-start.41 = (bf16[128,1024]{1,0:T(8,128)(2,1)S(1)}, bf16[128,1024]{1,0:T(8,128)(2,1)S(1)}, u32[]{:S(2)}, u32[]{:S(2)}) collective-permute-start(bf16[128,1024]{1,0:T(8,128)(2,1)S(1)} %get-tuple-element.17), channel_id=1, source_target_pairs={{0,1},{1,2},{2,3},{3,0},{4,5},{5,6},{6,7},{7,4},{8,9},{9,10},{10,1... | collective-permute-start | bytes 786440 | tf_op jit(solution)/shard_map/ppermute | solution.py:13
  140.8 1.3 collective-permute-start.43
  143.0 2.7 %convert_bitcast_fusion = bf16[1,1024,1024]{2,1,0:T(8,128)(2,1)} fusion(bf16[1024,512]{1,0:T(8,128)(2,1)S(1)} %convolution_convert_fusion, s32[]{:T(128)S(6)} %select_n.21, bf16[512,1024]{1,0:T(8,128)(2,1)S(1)} %bitcast.78, bf16[384,1024]{1,0:T(8,128)(2,1)S(1)} %copy-done.11), kind=kOutput, calls=%fused_computation.6 | convolution fusion | flops 1076887552 | bytes 4980740 | tf_op jit(solution)/shard_map/dot_general | solution.py:47
  145.8 2.2 %collective-permute-done.41 = bf16[128,1024]{1,0:T(8,128)(2,1)S(1)} collective-permute-done((bf16[128,1024]{1,0:T(8,128)(2,1)S(1)}, bf16[128,1024]{1,0:T(8,128)(2,1)S(1)}, u32[]{:S(2)}, u32[]{:S(2)}) %collective-permute-start.41) | collective-permute-done | bytes 262176 | tf_op jit(solution)/shard_map/ppermute | solution.py:13
  148.0 2.6 %collective-permute-done.43 = bf16[128,1024]{1,0:T(8,128)(2,1)S(1)} collective-permute-done((bf16[128,1024]{1,0:T(8,128)(2,1)S(1)}, bf16[128,1024]{1,0:T(8,128)(2,1)S(1)}, u32[]{:S(2)}, u32[]{:S(2)}) %collective-permute-start.43) | collective-permute-done | bytes 262176 | tf_op jit(solution)/shard_map/ppermute | solution.py:13
  151.5 2.3 %fusion.7 = bf16[1,128,1024]{2,1,0:T(8,128)(2,1)} fusion(bf16[1024,512]{0,1:T(8,128)(2,1)} %all-reduce.2.cloned.1.call-done, bf16[512,128]{0,1:T(8,128)(2,1)S(1)} %collective-permute-done.40, bf16[512,128]{0,1:T(8,128)(2,1)S(1)} %collective-permute-done.39, bf16[512,128]{0,1:T(8,128)(2,1)S(1)} %collective-permute-done.38, bf16[512,128]{0,1:T(8,128)(2,1)S(1)} %fusion.32), kind=kOutput, calls=%fused_computation.27 | convolution fusion | flops 134873088 | bytes 1835008 | tf_op jit(solution)/shard_map/dot_general | solution.py:47
  (124 shorter events, 44.3 us)
Async XLA Ops:
  7.2 144.3 %all-reduce.2.cloned.1.call-start = ((), (), s32[]{:S(2)}) async-start(), calls=%async_computation | async-start | bytes 2097152 | tf_op jit(solution)/shard_map/psum | solution.py:93
  7.2 59.9 %collective-permute-start.16 = (bf16[128,128]{1,0:T(8,128)(2,1)}, bf16[128,128]{1,0:T(8,128)(2,1)}, u32[]{:S(2)}, u32[]{:S(2)}) collective-permute-start(bf16[128,128]{1,0:T(8,128)(2,1)} %param.16), channel_id=1, source_target_pairs={{0,16},{8,24},{16,0},{24,8},{1,17},{9,25},{17,1},{25,9},{2,18},{10... | collective-permute-start | bytes 98312 | tf_op jit(solution)/shard_map/ppermute | solution.py:13
  11.3 47.7 %collective-permute-start.15 = (bf16[128,128]{1,0:T(8,128)(2,1)}, bf16[128,128]{1,0:T(8,128)(2,1)}, u32[]{:S(2)}, u32[]{:S(2)}) collective-permute-start(bf16[128,128]{1,0:T(8,128)(2,1)} %param.16), channel_id=1, source_target_pairs={{0,24},{8,0},{16,8},{24,16},{1,25},{9,1},{17,9},{25,17},{2,26},{10... | collective-permute-start | bytes 98312 | tf_op jit(solution)/shard_map/ppermute | solution.py:13
  12.7 11.5 %collective-permute-start.2 = (bf16[128,1024]{1,0:T(8,128)(2,1)}, bf16[128,1024]{1,0:T(8,128)(2,1)}, u32[]{:S(2)}, u32[]{:S(2)}) collective-permute-start(bf16[128,1024]{1,0:T(8,128)(2,1)} %bitcast.87), channel_id=1, source_target_pairs={{0,8},{8,16},{16,24},{24,0},{1,9},{9,17},{17,25},{25,1},{2,10},{10... | collective-permute-start | bytes 786440 | tf_op jit(solution)/shard_map/ppermute | solution.py:13
  13.4 20.5 %collective-permute-start.1 = (bf16[128,1024]{1,0:T(8,128)(2,1)}, bf16[128,1024]{1,0:T(8,128)(2,1)}, u32[]{:S(2)}, u32[]{:S(2)}) collective-permute-start(bf16[128,1024]{1,0:T(8,128)(2,1)} %bitcast.88), channel_id=1, source_target_pairs={{0,16},{8,24},{16,0},{24,8},{1,17},{9,25},{17,1},{25,9},{2,18},{10... | collective-permute-start | bytes 786440 | tf_op jit(solution)/shard_map/ppermute | solution.py:13
  14.4 19.4 %collective-permute-start = (bf16[128,1024]{1,0:T(8,128)(2,1)}, bf16[128,1024]{1,0:T(8,128)(2,1)}, u32[]{:S(2)}, u32[]{:S(2)}) collective-permute-start(bf16[128,1024]{1,0:T(8,128)(2,1)} %bitcast.89), channel_id=1, source_target_pairs={{0,24},{8,0},{16,8},{24,16},{1,25},{9,1},{17,9},{25,17},{2,26},{10... | collective-permute-start | bytes 786440 | tf_op jit(solution)/shard_map/ppermute | solution.py:13
  22.0 18.3 %copy-start.6 = (bf16[1,512,1024]{2,1,0:T(8,128)(2,1)S(1)}, bf16[1,512,1024]{2,1,0:T(8,128)(2,1)}, u32[]{:S(2)}) copy-start(bf16[1,512,1024]{2,1,0:T(8,128)(2,1)} %param.12) | copy-start | bytes 3145732
  35.7 16.5 %copy-start.14 = (bf16[128,128]{1,0:T(8,128)(2,1)S(1)}, bf16[128,128]{1,0:T(8,128)(2,1)}, u32[]{:S(2)}) copy-start(bf16[128,128]{1,0:T(8,128)(2,1)} %param.16) | copy-start | bytes 98308
  35.8 7.2 %collective-permute-start.3 = (bf16[512,128]{1,0:T(8,128)(2,1)S(1)}, bf16[512,128]{1,0:T(8,128)(2,1)S(1)}, u32[]{:S(2)}, u32[]{:S(2)}) collective-permute-start(bf16[512,128]{1,0:T(8,128)(2,1)S(1)} %get-tuple-element.23), channel_id=1, source_target_pairs={{0,1},{1,2},{2,3},{3,0},{4,5},{5,6},{6,7},{7,4},{8,9},{9,10},{10,1... | collective-permute-start | bytes 393224 | tf_op jit(solution)/shard_map/ppermute | solution.py:13
  37.3 7.0 %collective-permute-start.5 = (bf16[512,128]{1,0:T(8,128)(2,1)S(1)}, bf16[512,128]{1,0:T(8,128)(2,1)S(1)}, u32[]{:S(2)}, u32[]{:S(2)}) collective-permute-start(bf16[512,128]{1,0:T(8,128)(2,1)S(1)} %get-tuple-element.24), channel_id=1, source_target_pairs={{0,3},{1,0},{2,1},{3,2},{4,7},{5,4},{6,5},{7,6},{8,11},{9,8},{10,9... | collective-permute-start | bytes 393224 | tf_op jit(solution)/shard_map/ppermute | solution.py:13
  38.8 5.5 %collective-permute-start.4 = (bf16[512,128]{1,0:T(8,128)(2,1)S(1)}, bf16[512,128]{1,0:T(8,128)(2,1)S(1)}, u32[]{:S(2)}, u32[]{:S(2)}) collective-permute-start(bf16[512,128]{1,0:T(8,128)(2,1)S(1)} %get-tuple-element.25), channel_id=1, source_target_pairs={{0,2},{1,3},{2,0},{3,1},{4,6},{5,7},{6,4},{7,5},{8,10},{9,11},{10,... | collective-permute-start | bytes 393224 | tf_op jit(solution)/shard_map/ppermute | solution.py:13
  44.4 8.9 %collective-permute-start.6 = (bf16[128,128]{1,0:T(8,128)(2,1)S(1)}, bf16[128,128]{1,0:T(8,128)(2,1)S(1)}, u32[]{:S(2)}, u32[]{:S(2)}) collective-permute-start(bf16[128,128]{1,0:T(8,128)(2,1)S(1)} %get-tuple-element.26), channel_id=1, source_target_pairs={{0,8},{8,16},{16,24},{24,0},{1,9},{9,17},{17,25},{25,1},{2,10},{10... | collective-permute-start | bytes 98312 | tf_op jit(solution)/shard_map/ppermute | solution.py:13
  50.6 3.9 %collective-permute-start.8 = (bf16[128,128]{1,0:T(8,128)(2,1)S(1)}, bf16[128,128]{1,0:T(8,128)(2,1)S(1)}, u32[]{:S(2)}, u32[]{:S(2)}) collective-permute-start(bf16[128,128]{1,0:T(8,128)(2,1)S(1)} %get-tuple-element.27), channel_id=1, source_target_pairs={{0,24},{8,0},{16,8},{24,16},{1,25},{9,1},{17,9},{25,17},{2,26},{10... | collective-permute-start | bytes 98312 | tf_op jit(solution)/shard_map/ppermute | solution.py:13
  51.5 4.8 %collective-permute-start.7 = (bf16[128,128]{1,0:T(8,128)(2,1)S(1)}, bf16[128,128]{1,0:T(8,128)(2,1)S(1)}, u32[]{:S(2)}, u32[]{:S(2)}) collective-permute-start(bf16[128,128]{1,0:T(8,128)(2,1)S(1)} %get-tuple-element.28), channel_id=1, source_target_pairs={{0,16},{8,24},{16,0},{24,8},{1,17},{9,25},{17,1},{25,9},{2,18},{10... | collective-permute-start | bytes 98312 | tf_op jit(solution)/shard_map/ppermute | solution.py:13
  53.3 15.5 %collective-permute-start.17 = (bf16[128,128]{1,0:T(8,128)(2,1)S(1)}, bf16[128,128]{1,0:T(8,128)(2,1)S(1)}, u32[]{:S(2)}, u32[]{:S(2)}) collective-permute-start(bf16[128,128]{1,0:T(8,128)(2,1)S(1)} %copy-done.14), channel_id=1, source_target_pairs={{0,8},{8,16},{16,24},{24,0},{1,9},{9,17},{17,25},{25,1},{2,10},{10... | collective-permute-start | bytes 98312 | tf_op jit(solution)/shard_map/ppermute | solution.py:13
  56.3 6.1 %collective-permute-start.11 = (bf16[128,128]{1,0:T(8,128)(2,1)S(1)}, bf16[128,128]{1,0:T(8,128)(2,1)S(1)}, u32[]{:S(2)}, u32[]{:S(2)}) collective-permute-start(bf16[128,128]{1,0:T(8,128)(2,1)S(1)} %fusion.58), channel_id=1, source_target_pairs={{0,8},{8,16},{16,24},{24,0},{1,9},{9,17},{17,25},{25,1},{2,10},{10... | collective-permute-start | bytes 98312 | tf_op jit(solution)/shard_map/ppermute | solution.py:13
  57.5 6.0 %collective-permute-start.10 = (bf16[128,128]{1,0:T(8,128)(2,1)S(1)}, bf16[128,128]{1,0:T(8,128)(2,1)S(1)}, u32[]{:S(2)}, u32[]{:S(2)}) collective-permute-start(bf16[128,128]{1,0:T(8,128)(2,1)S(1)} %fusion.58), channel_id=1, source_target_pairs={{0,16},{8,24},{16,0},{24,8},{1,17},{9,25},{17,1},{25,9},{2,18},{10... | collective-permute-start | bytes 98312 | tf_op jit(solution)/shard_map/ppermute | solution.py:13
  59.0 4.6 %collective-permute-start.9 = (bf16[128,128]{1,0:T(8,128)(2,1)S(1)}, bf16[128,128]{1,0:T(8,128)(2,1)S(1)}, u32[]{:S(2)}, u32[]{:S(2)}) collective-permute-start(bf16[128,128]{1,0:T(8,128)(2,1)S(1)} %fusion.58), channel_id=1, source_target_pairs={{0,24},{8,0},{16,8},{24,16},{1,25},{9,1},{17,9},{25,17},{2,26},{10... | collective-permute-start | bytes 98312 | tf_op jit(solution)/shard_map/ppermute | solution.py:13
  62.4 25.7 %collective-permute-start.26 = (bf16[128,128]{1,0:T(8,128)(2,1)}, bf16[128,128]{1,0:T(8,128)(2,1)}, u32[]{:S(2)}, u32[]{:S(2)}) collective-permute-start(bf16[128,128]{1,0:T(8,128)(2,1)} %param.17), channel_id=1, source_target_pairs={{0,16},{8,24},{16,0},{24,8},{1,17},{9,25},{17,1},{25,9},{2,18},{10... | collective-permute-start | bytes 98312 | tf_op jit(solution)/shard_map/ppermute | solution.py:13
  63.6 7.7 %collective-permute-start.14 = (bf16[512,128]{1,0:T(8,128)(2,1)S(1)}, bf16[512,128]{1,0:T(8,128)(2,1)S(1)}, u32[]{:S(2)}, u32[]{:S(2)}) collective-permute-start(bf16[512,128]{1,0:T(8,128)(2,1)S(1)} %pad_maximum_fusion.4), channel_id=1, source_target_pairs={{0,1},{1,2},{2,3},{3,0},{4,5},{5,6},{6,7},{7,4},{8,9},{9,10},{10,1... | collective-permute-start | bytes 393224 | tf_op jit(solution)/shard_map/ppermute | solution.py:13
  65.2 6.1 %collective-permute-start.13 = (bf16[512,128]{1,0:T(8,128)(2,1)S(1)}, bf16[512,128]{1,0:T(8,128)(2,1)S(1)}, u32[]{:S(2)}, u32[]{:S(2)}) collective-permute-start(bf16[512,128]{1,0:T(8,128)(2,1)S(1)} %pad_maximum_fusion.4), channel_id=1, source_target_pairs={{0,2},{1,3},{2,0},{3,1},{4,6},{5,7},{6,4},{7,5},{8,10},{9,11},{10,... | collective-permute-start | bytes 393224 | tf_op jit(solution)/shard_map/ppermute | solution.py:13
  67.2 5.0 %collective-permute-start.12 = (bf16[512,128]{1,0:T(8,128)(2,1)S(1)}, bf16[512,128]{1,0:T(8,128)(2,1)S(1)}, u32[]{:S(2)}, u32[]{:S(2)}) collective-permute-start(bf16[512,128]{1,0:T(8,128)(2,1)S(1)} %pad_maximum_fusion.4), channel_id=1, source_target_pairs={{0,3},{1,0},{2,1},{3,2},{4,7},{5,4},{6,5},{7,6},{8,11},{9,8},{10,9... | collective-permute-start | bytes 393224 | tf_op jit(solution)/shard_map/ppermute | solution.py:13
  68.8 18.5 %collective-permute-start.25 = (bf16[128,128]{1,0:T(8,128)(2,1)}, bf16[128,128]{1,0:T(8,128)(2,1)}, u32[]{:S(2)}, u32[]{:S(2)}) collective-permute-start(bf16[128,128]{1,0:T(8,128)(2,1)} %param.17), channel_id=1, source_target_pairs={{0,24},{8,0},{16,8},{24,16},{1,25},{9,1},{17,9},{25,17},{2,26},{10... | collective-permute-start | bytes 98312 | tf_op jit(solution)/shard_map/ppermute | solution.py:13
  76.9 3.6 %collective-permute-start.20 = (f32[512]{0:T(512)S(1)}, f32[512]{0:T(512)S(1)}, u32[]{:S(2)}, u32[]{:S(2)}) collective-permute-start(f32[512]{0:T(512)S(1)} %get-tuple-element.31), channel_id=1, source_target_pairs={{0,3},{1,0},{2,1},{3,2},{4,7},{5,4},{6,5},{7,6},{8,11},{9,8},{10,9... | collective-permute-start | bytes 6152 | tf_op jit(solution)/shard_map/ppermute | solution.py:13
  79.0 3.6 %collective-permute-start.19 = (f32[512]{0:T(512)S(1)}, f32[512]{0:T(512)S(1)}, u32[]{:S(2)}, u32[]{:S(2)}) collective-permute-start(f32[512]{0:T(512)S(1)} %get-tuple-element.31), channel_id=1, source_target_pairs={{0,2},{1,3},{2,0},{3,1},{4,6},{5,7},{6,4},{7,5},{8,10},{9,11},{10,... | collective-permute-start | bytes 6152 | tf_op jit(solution)/shard_map/ppermute | solution.py:13
  79.4 4.5 %collective-permute-start.18 = (f32[512]{0:T(512)S(1)}, f32[512]{0:T(512)S(1)}, u32[]{:S(2)}, u32[]{:S(2)}) collective-permute-start(f32[512]{0:T(512)S(1)} %get-tuple-element.31), channel_id=1, source_target_pairs={{0,1},{1,2},{2,3},{3,0},{4,5},{5,6},{6,7},{7,4},{8,9},{9,10},{10,1... | collective-permute-start | bytes 6152 | tf_op jit(solution)/shard_map/ppermute | solution.py:13
  80.5 13.6 %collective-permute-start.27 = (bf16[128,128]{1,0:T(8,128)(2,1)}, bf16[128,128]{1,0:T(8,128)(2,1)S(1)}, u32[]{:S(2)}, u32[]{:S(2)}) collective-permute-start(bf16[128,128]{1,0:T(8,128)(2,1)} %param.17), channel_id=1, source_target_pairs={{0,8},{8,16},{16,24},{24,0},{1,9},{9,17},{17,25},{25,1},{2,10},{10... | collective-permute-start | bytes 98312 | tf_op jit(solution)/shard_map/ppermute | solution.py:13
  86.0 2.9 %collective-permute-start.21 = (bf16[512,128]{1,0:T(8,128)(2,1)S(1)}, bf16[512,128]{1,0:T(8,128)(2,1)S(1)}, u32[]{:S(2)}, u32[]{:S(2)}) collective-permute-start(bf16[512,128]{1,0:T(8,128)(2,1)S(1)} %multiply_convert_fusion.9), channel_id=1, source_target_pairs={{0,4},{1,5},{2,6},{3,7},{8,12},{9,13},{10,14},{11,15},{16,20},{17,... | collective-permute-start | bytes 393224 | tf_op jit(solution)/shard_map/ppermute | solution.py:19
  90.6 3.6 %collective-permute-start.24 = (f32[512]{0:T(512)S(1)}, f32[512]{0:T(512)S(1)}, u32[]{:S(2)}, u32[]{:S(2)}) collective-permute-start(f32[512]{0:T(512)S(1)} %get-tuple-element.33), channel_id=1, source_target_pairs={{0,3},{1,0},{2,1},{3,2},{4,7},{5,4},{6,5},{7,6},{8,11},{9,8},{10,9... | collective-permute-start | bytes 6152 | tf_op jit(solution)/shard_map/ppermute | solution.py:13
  91.3 3.6 %collective-permute-start.23 = (f32[512]{0:T(512)S(1)}, f32[512]{0:T(512)S(1)}, u32[]{:S(2)}, u32[]{:S(2)}) collective-permute-start(f32[512]{0:T(512)S(1)} %get-tuple-element.33), channel_id=1, source_target_pairs={{0,2},{1,3},{2,0},{3,1},{4,6},{5,7},{6,4},{7,5},{8,10},{9,11},{10,... | collective-permute-start | bytes 6152 | tf_op jit(solution)/shard_map/ppermute | solution.py:13
  92.6 4.5 %collective-permute-start.22 = (f32[512]{0:T(512)S(1)}, f32[512]{0:T(512)S(1)}, u32[]{:S(2)}, u32[]{:S(2)}) collective-permute-start(f32[512]{0:T(512)S(1)} %get-tuple-element.33), channel_id=1, source_target_pairs={{0,1},{1,2},{2,3},{3,0},{4,5},{5,6},{6,7},{7,4},{8,9},{9,10},{10,1... | collective-permute-start | bytes 6152 | tf_op jit(solution)/shard_map/ppermute | solution.py:13
  99.4 3.6 %collective-permute-start.30 = (f32[512]{0:T(512)S(1)}, f32[512]{0:T(512)S(1)}, u32[]{:S(2)}, u32[]{:S(2)}) collective-permute-start(f32[512]{0:T(512)S(1)} %get-tuple-element.35), channel_id=1, source_target_pairs={{0,3},{1,0},{2,1},{3,2},{4,7},{5,4},{6,5},{7,6},{8,11},{9,8},{10,9... | collective-permute-start | bytes 6152 | tf_op jit(solution)/shard_map/ppermute | solution.py:13
  100.0 3.6 %collective-permute-start.29 = (f32[512]{0:T(512)S(1)}, f32[512]{0:T(512)S(1)}, u32[]{:S(2)}, u32[]{:S(2)}) collective-permute-start(f32[512]{0:T(512)S(1)} %get-tuple-element.35), channel_id=1, source_target_pairs={{0,2},{1,3},{2,0},{3,1},{4,6},{5,7},{6,4},{7,5},{8,10},{9,11},{10,... | collective-permute-start | bytes 6152 | tf_op jit(solution)/shard_map/ppermute | solution.py:13
  101.6 4.5 %collective-permute-start.28 = (f32[512]{0:T(512)S(1)}, f32[512]{0:T(512)S(1)}, u32[]{:S(2)}, u32[]{:S(2)}) collective-permute-start(f32[512]{0:T(512)S(1)} %get-tuple-element.35), channel_id=1, source_target_pairs={{0,1},{1,2},{2,3},{3,0},{4,5},{5,6},{6,7},{7,4},{8,9},{9,10},{10,1... | collective-permute-start | bytes 6152 | tf_op jit(solution)/shard_map/ppermute | solution.py:13
  106.7 3.2 %collective-permute-start.31 = (bf16[512,128]{1,0:T(8,128)(2,1)S(1)}, bf16[512,128]{1,0:T(8,128)(2,1)S(1)}, u32[]{:S(2)}, u32[]{:S(2)}) collective-permute-start(bf16[512,128]{1,0:T(8,128)(2,1)S(1)} %convolution_convert_fusion.5), channel_id=1, source_target_pairs={{4,0},{5,1},{6,2},{7,3},{12,8},{13,9},{14,10},{15,11},{20,16},{21,... | collective-permute-start | bytes 393224 | tf_op jit(solution)/shard_map/ppermute | solution.py:19
  111.1 3.9 %collective-permute-start.34 = (f32[512]{0:T(512)S(1)}, f32[512]{0:T(512)S(1)}, u32[]{:S(2)}, u32[]{:S(2)}) collective-permute-start(f32[512]{0:T(512)S(1)} %get-tuple-element.14), channel_id=1, source_target_pairs={{0,3},{1,0},{2,1},{3,2},{4,7},{5,4},{6,5},{7,6},{8,11},{9,8},{10,9... | collective-permute-start | bytes 6152 | tf_op jit(solution)/shard_map/ppermute | solution.py:13
  111.6 3.6 %collective-permute-start.33 = (f32[512]{0:T(512)S(1)}, f32[512]{0:T(512)S(1)}, u32[]{:S(2)}, u32[]{:S(2)}) collective-permute-start(f32[512]{0:T(512)S(1)} %get-tuple-element.14), channel_id=1, source_target_pairs={{0,2},{1,3},{2,0},{3,1},{4,6},{5,7},{6,4},{7,5},{8,10},{9,11},{10,... | collective-permute-start | bytes 6152 | tf_op jit(solution)/shard_map/ppermute | solution.py:13
  112.3 4.5 %collective-permute-start.32 = (f32[512]{0:T(512)S(1)}, f32[512]{0:T(512)S(1)}, u32[]{:S(2)}, u32[]{:S(2)}) collective-permute-start(f32[512]{0:T(512)S(1)} %get-tuple-element.14), channel_id=1, source_target_pairs={{0,1},{1,2},{2,3},{3,0},{4,5},{5,6},{6,7},{7,4},{8,9},{9,10},{10,1... | collective-permute-start | bytes 6152 | tf_op jit(solution)/shard_map/ppermute | solution.py:13
  120.0 15.9 %copy-start.16 = (bf16[1,128,1024]{2,1,0:T(8,128)(2,1)S(1)}, bf16[1,128,1024]{2,1,0:T(8,128)(2,1)}, u32[]{:S(2)}) copy-start(bf16[1,128,1024]{2,1,0:T(8,128)(2,1)} %param.9) | copy-start | bytes 786436
  120.0 6.7 %collective-permute-start.35 = (bf16[512,128]{0,1:T(8,128)(2,1)S(1)}, bf16[512,128]{0,1:T(8,128)(2,1)S(1)}, u32[]{:S(2)}, u32[]{:S(2)}) collective-permute-start(bf16[512,128]{0,1:T(8,128)(2,1)S(1)} %get-tuple-element.20), channel_id=1, source_target_pairs={{0,1},{1,2},{2,3},{3,0},{4,5},{5,6},{6,7},{7,4},{8,9},{9,10},{10,1... | collective-permute-start | bytes 393224 | tf_op jit(solution)/shard_map/ppermute | solution.py:13
  120.5 7.3 %collective-permute-start.37 = (bf16[512,128]{0,1:T(8,128)(2,1)S(1)}, bf16[512,128]{0,1:T(8,128)(2,1)S(1)}, u32[]{:S(2)}, u32[]{:S(2)}) collective-permute-start(bf16[512,128]{0,1:T(8,128)(2,1)S(1)} %get-tuple-element.21), channel_id=1, source_target_pairs={{0,3},{1,0},{2,1},{3,2},{4,7},{5,4},{6,5},{7,6},{8,11},{9,8},{10,9... | collective-permute-start | bytes 393224 | tf_op jit(solution)/shard_map/ppermute | solution.py:13
  123.0 5.1 %collective-permute-start.36 = (bf16[512,128]{0,1:T(8,128)(2,1)S(1)}, bf16[512,128]{0,1:T(8,128)(2,1)S(1)}, u32[]{:S(2)}, u32[]{:S(2)}) collective-permute-start(bf16[512,128]{0,1:T(8,128)(2,1)S(1)} %get-tuple-element.22), channel_id=1, source_target_pairs={{0,2},{1,3},{2,0},{3,1},{4,6},{5,7},{6,4},{7,5},{8,10},{9,11},{10,... | collective-permute-start | bytes 393224 | tf_op jit(solution)/shard_map/ppermute | solution.py:13
  128.1 6.2 %collective-permute-start.40 = (bf16[512,128]{0,1:T(8,128)(2,1)S(1)}, bf16[512,128]{0,1:T(8,128)(2,1)S(1)}, u32[]{:S(2)}, u32[]{:S(2)}) collective-permute-start(bf16[512,128]{0,1:T(8,128)(2,1)S(1)} %fusion.32), channel_id=1, source_target_pairs={{0,1},{1,2},{2,3},{3,0},{4,5},{5,6},{6,7},{7,4},{8,9},{9,10},{10,1... | collective-permute-start | bytes 393224 | tf_op jit(solution)/shard_map/ppermute | solution.py:13
  129.8 5.6 %collective-permute-start.39 = (bf16[512,128]{0,1:T(8,128)(2,1)S(1)}, bf16[512,128]{0,1:T(8,128)(2,1)S(1)}, u32[]{:S(2)}, u32[]{:S(2)}) collective-permute-start(bf16[512,128]{0,1:T(8,128)(2,1)S(1)} %fusion.32), channel_id=1, source_target_pairs={{0,2},{1,3},{2,0},{3,1},{4,6},{5,7},{6,4},{7,5},{8,10},{9,11},{10,... | collective-permute-start | bytes 393224 | tf_op jit(solution)/shard_map/ppermute | solution.py:13
  130.9 5.0 %collective-permute-start.38 = (bf16[512,128]{0,1:T(8,128)(2,1)S(1)}, bf16[512,128]{0,1:T(8,128)(2,1)S(1)}, u32[]{:S(2)}, u32[]{:S(2)}) collective-permute-start(bf16[512,128]{0,1:T(8,128)(2,1)S(1)} %fusion.32), channel_id=1, source_target_pairs={{0,3},{1,0},{2,1},{3,2},{4,7},{5,4},{6,5},{7,6},{8,11},{9,8},{10,9... | collective-permute-start | bytes 393224 | tf_op jit(solution)/shard_map/ppermute | solution.py:13
  139.1 8.8 %collective-permute-start.41 = (bf16[128,1024]{1,0:T(8,128)(2,1)S(1)}, bf16[128,1024]{1,0:T(8,128)(2,1)S(1)}, u32[]{:S(2)}, u32[]{:S(2)}) collective-permute-start(bf16[128,1024]{1,0:T(8,128)(2,1)S(1)} %get-tuple-element.17), channel_id=1, source_target_pairs={{0,1},{1,2},{2,3},{3,0},{4,5},{5,6},{6,7},{7,4},{8,9},{9,10},{10,1... | collective-permute-start | bytes 786440 | tf_op jit(solution)/shard_map/ppermute | solution.py:13
  140.8 9.7 %collective-permute-start.43 = (bf16[128,1024]{1,0:T(8,128)(2,1)S(1)}, bf16[128,1024]{1,0:T(8,128)(2,1)S(1)}, u32[]{:S(2)}, u32[]{:S(2)}) collective-permute-start(bf16[128,1024]{1,0:T(8,128)(2,1)S(1)} %get-tuple-element.18), channel_id=1, source_target_pairs={{0,3},{1,0},{2,1},{3,2},{4,7},{5,4},{6,5},{7,6},{8,11},{9,8},{10,9... | collective-permute-start | bytes 786440 | tf_op jit(solution)/shard_map/ppermute | solution.py:13
  142.1 8.5 %collective-permute-start.42 = (bf16[128,1024]{1,0:T(8,128)(2,1)S(1)}, bf16[128,1024]{1,0:T(8,128)(2,1)S(1)}, u32[]{:S(2)}, u32[]{:S(2)}) collective-permute-start(bf16[128,1024]{1,0:T(8,128)(2,1)S(1)} %get-tuple-element.19), channel_id=1, source_target_pairs={{0,2},{1,3},{2,0},{3,1},{4,6},{5,7},{6,4},{7,5},{8,10},{9,11},{10,... | collective-permute-start | bytes 786440 | tf_op jit(solution)/shard_map/ppermute | solution.py:13
  (14 other events, 90.1 us)
Sparse Core Ops, SparseCore 0:
  94.3 50.9 all-reduce.1

commit v2 on v1

--- a/solution.py
+++ b/solution.py
@@ -19,6 +19,19 @@
     return lax.ppermute(shard, axis, pairs)
 
 
+def exchanged(blocks, axis):
+    return lax.all_to_all(blocks, axis, 0, 0)
+
+
+def spread(shard, axis):
+    copies = jnp.broadcast_to(shard[None], (lax.axis_size(axis),) + shard.shape)
+    return exchanged(copies, axis)
+
+
+def summed(blocks, axis):
+    return jnp.sum(exchanged(jnp.stack(blocks).astype(bf16), axis).astype(f32), axis=0)
+
+
 def gathered(shard, axis):
     return [shard] + [shift(shard, axis, -k) for k in range(1, lax.axis_size(axis))]
 
@@ -31,16 +44,7 @@
 
 
 def small_sum(rows, axis):
-    total = rows
-    for k in range(1, lax.axis_size(axis)):
-        total = total + shift(rows, axis, k)
-    return total
-
-
-def rolled_rows(matrix, index, count):
-    size = matrix.shape[0] // count
-    doubled = jnp.concatenate([matrix, matrix[:-size]])
-    return lax.dynamic_slice_in_dim(doubled, index * size, matrix.shape[0])
+    return jnp.sum(spread(rows, axis), axis=0)
 
 
 def dot(left, right, over):
@@ -62,12 +66,11 @@
     section = lax.axis_index("pipe")
     groups = lax.axis_size("dp")
     parts = lax.axis_size("tensor")
-    part = lax.axis_index("tensor")
     group = lax.axis_index("dp")
     width = norm_gain.shape[1] * parts
     proj = out_proj[0]
-    enc = rolled_rows(encoder[0], part, parts)
-    dec = rolled_rows(decoder[0], part, parts)
+    enc = encoder[0]
+    dec = decoder[0]
     gain = norm_gain[0]
     send = send_encoder[0]
     recv = recv_decoder[0]
@@ -81,14 +84,14 @@
     local_fold = dot(proj, enc, ((1,), (1,)))
     local_fold = local_fold.astype(bf16)
     partial = dot(head_rows, local_fold, ((1,), (0,)))
-    over_parts = scatter_sum(
+    over_parts = summed(
         [partial[:, k * code_cols : (k + 1) * code_cols] for k in range(parts)], "tensor"
     )
     own_code = scatter_sum(
         [over_parts[k * tokens : (k + 1) * tokens] for k in range(groups)], "dp"
     ).astype(bf16)
     code_block = jnp.concatenate(gathered(own_code, "dp"))
-    mix_code = jnp.concatenate(gathered(code_block, "tensor"), axis=1)
+    mix_code = jnp.concatenate(list(spread(code_block, "tensor")), axis=1)
     fold_in, mix_code = lax.optimization_barrier((local_fold, mix_code))
     fold = lax.psum(fold_in, "dp")
     attention = dot(mix_code, dec, ((1,), (0,)))
@@ -115,22 +118,20 @@
         returned = dot(grad_mixed, recv, ((1,), (1,))).astype(bf16)
 
     code_term = dot(grad_mixed, dec, ((1,), (1,)))
-    code_block = scatter_sum(
+    code_block = summed(
         [code_term[:, k * code_cols : (k + 1) * code_cols] for k in range(parts)], "tensor"
     ).astype(bf16)
-    code_blocks = gathered(code_block, "tensor")
-    code_grad = jnp.concatenate(code_blocks, axis=1)
+    code_grad = jnp.concatenate(list(spread(code_block, "tensor")), axis=1)
     head_sum = dot(head_rows, code_grad, ((0,), (0,))).astype(bf16)
     enc_term = dot(head_sum, proj, ((0,), (0,)))
-    enc_grad = scatter_sum(
+    enc_grad = summed(
         [enc_term[k * code_cols : (k + 1) * code_cols] for k in range(parts)], "tensor"
     ).astype(bf16)
     proj_grad = dot(head_sum, enc, ((1,), (0,))).astype(bf16)
     heads_grad = dot(code_grad[:tokens], fold, ((1,), (1,))).astype(bf16)
 
     codes = mix_code.shape[1]
-    mine = lax.rem(group * (codes // groups) + codes - part * code_cols, codes)
-    mix_cols = lax.dynamic_slice_in_dim(mix_code, mine, codes // groups, 1)
+    mix_cols = lax.dynamic_slice_in_dim(mix_code, group * (codes // groups), codes // groups, 1)
     dec_grad = dot(mix_cols, grad_mixed, ((0,), (0,))).astype(bf16)
     gain_grad = jnp.sum(grad_norm * normed, axis=0)
     send_grad = dot(out_rows, incoming, ((0,), (0,))).astype(bf16)

time: 161 us -> 199 us (1.24)
  blocking collectives: 0 us -> 19.1 us
  matrix products: 30.7 us -> 41.6 us
  starting transfers between devices: 62.7 us -> 55 us
  other arithmetic: 3.06 us -> 10.7 us
  waiting for transfers between devices: 41.5 us -> 47.2 us
    ppermute x42 -> x15, starting transfers between devices: 60.1 us -> 26.4 us  [shift(): lax.ppermute(shard, axis, [(i, (i + by) % devices) for i in range(devices)])]
    all_to_all x0 -> x7, waiting for transfers between devices: none -> 27.5 us  [exchanged(): return lax.all_to_all(blocks, axis, 0, 0)]
    all_to_all x0 -> x7, starting transfers between devices: none -> 25.9 us  [exchanged(): return lax.all_to_all(blocks, axis, 0, 0)]
    ppermute x42 -> x15, waiting for transfers between devices: 40.2 us -> 16.9 us  [shift(): lax.ppermute(shard, axis, [(i, (i + by) % devices) for i in range(devices)])]
    all_to_all x0 -> x2, blocking collectives: none -> 19.1 us  [exchanged(): return lax.all_to_all(blocks, axis, 0, 0)]
    dot_general x19, matrix products: 30.7 us -> 41.6 us  [dot(): lax.dot_general(left, right, ((over[0], over[1]), ((), ())), preferred_el...]
    broadcast_in_dim x0 -> x6, local copies, waits for them, and re-layouts: none -> 4.44 us  [spread(): copies = jnp.broadcast_to(shard[None], (lax.axis_size(axis),) + shard.shape)]
    reduce_sum x0 -> x7, other arithmetic: none -> 4.17 us  [the longest x3 4.08 us: summed(): jnp.sum(exchanged(jnp.stack(blocks).astype(bf16), axis).astype(f32), axis=0)]
  transfers between devices with their start and end apart: 45 -> 25, of which waited for: 28 -> 14; matrix products, arithmetic and copies ran while one was open for 24% -> 25% of each run, Pallas kernels for 0% -> 0%
where the time goes in v2:
time: 199 us; the launch traced here: 198 us
  starting transfers between devices  55 us (28%)
  waiting for transfers between devices  47.2 us (24%)
  matrix products  41.6 us (21%)
  blocking collectives  19.1 us (10%)
  between operations  14.6 us (7%)
  other arithmetic  10.7 us (5%)
  local copies, waits for them, and re-layouts  9.59 us (5%)
    dot_general x19, matrix products, dot(): lax.dot_general(left, right, ((over[0], over[1]), ((), ())), preferred_el...  41.6 us
    all_to_all x7, waiting for transfers between devices, exchanged(): return lax.all_to_all(blocks, axis, 0, 0)  27.5 us
    ppermute x15, starting transfers between devices, shift(): lax.ppermute(shard, axis, [(i, (i + by) % devices) for i in range(devices)])  26.4 us
    all_to_all x7, starting transfers between devices, exchanged(): return lax.all_to_all(blocks, axis, 0, 0)  25.9 us
    all_to_all x2, blocking collectives, exchanged(): return lax.all_to_all(blocks, axis, 0, 0)  19.1 us
    ppermute x15, waiting for transfers between devices, shift(): lax.ppermute(shard, axis, [(i, (i + by) % devices) for i in range(devices)])  16.9 us
    broadcast_in_dim x6, local copies, waits for them, and re-layouts, spread(): copies = jnp.broadcast_to(shard[None], (lax.axis_size(axis),) + shard.shape)  4.44 us
    reduce_sum x3, other arithmetic, summed(): jnp.sum(exchanged(jnp.stack(blocks).astype(bf16), axis).astype(f32), axis=0)  4.08 us
  transfers between devices with their start and end apart: 25, of which 14 were waited for; matrix products, arithmetic and copies ran while one was open for 25% of the time, Pallas kernels for 0%

profile of v2, /device:TPU:0, one launch (start us, length us, event | category | flops | bytes accessed | tf_op | source)
XLA Modules:
  0.0 197.7 jit_solution(17334799850429636263)
XLA Ops:
  7.2 3.1 %collective-permute-start.2 = (bf16[128,1024]{1,0:T(8,128)(2,1)}, bf16[128,1024]{1,0:T(8,128)(2,1)}, u32[]{:S(2)}, u32[]{:S(2)}) collective-permute-start(bf16[128,1024]{1,0:T(8,128)(2,1)} %bitcast.123), channel_id=1, source_target_pairs={{0,8},{8,16},{16,24},{24,0},{1,9},{9,17},{17,25},{25,1},{2,10},{10... | collective-permute-start | bytes 786440 | tf_op jit(solution)/shard_map/ppermute | solution.py:13
  10.3 2.6 %collective-permute-start.1 = (bf16[128,1024]{1,0:T(8,128)(2,1)}, bf16[128,1024]{1,0:T(8,128)(2,1)}, u32[]{:S(2)}, u32[]{:S(2)}) collective-permute-start(bf16[128,1024]{1,0:T(8,128)(2,1)} %bitcast.124), channel_id=1, source_target_pairs={{0,16},{8,24},{16,0},{24,8},{1,17},{9,25},{17,1},{25,9},{2,18},{10... | collective-permute-start | bytes 786440 | tf_op jit(solution)/shard_map/ppermute | solution.py:13
  14.2 2.5 %fusion.4 = bf16[1024,512]{1,0:T(8,128)(2,1)S(1)} fusion(bf16[1,1024,1024]{2,1,0:T(8,128)(2,1)S(1)} %copy-done, bf16[1,512,1024]{2,1,0:T(8,128)(2,1)} %param.11), kind=kOutput, calls=%fused_computation.17 | convolution fusion | flops 1074266112 | bytes 4194304 | tf_op jit(solution)/shard_map/dot_general | solution.py:51
  16.7 3.2 %collective-permute-done.2 = bf16[128,1024]{1,0:T(8,128)(2,1)} collective-permute-done((bf16[128,1024]{1,0:T(8,128)(2,1)}, bf16[128,1024]{1,0:T(8,128)(2,1)}, u32[]{:S(2)}, u32[]{:S(2)}) %collective-permute-start.2) | collective-permute-done | bytes 262176 | tf_op jit(solution)/shard_map/ppermute | solution.py:13
  19.9 10.4 %collective-permute-done.1 = bf16[128,1024]{1,0:T(8,128)(2,1)} collective-permute-done((bf16[128,1024]{1,0:T(8,128)(2,1)}, bf16[128,1024]{1,0:T(8,128)(2,1)}, u32[]{:S(2)}, u32[]{:S(2)}) %collective-permute-start.1) | collective-permute-done | bytes 262176 | tf_op jit(solution)/shard_map/ppermute | solution.py:13
  30.3 1.8 convolution_convert_fusion.2
  32.3 12.1 %all_to_all.49 = bf16[4,512,128]{2,1,0:T(8,128)(2,1)S(1)} all-to-all(bf16[4,512,128]{2,1,0:T(8,128)(2,1)S(1)} %pad_maximum_fusion.2), channel_id=1, replica_groups=mesh['dp'=4,'pipe'=2,'tensor'=4] {'tensor'}, dimensions={0} | all-to-all | bytes 1048576 | tf_op jit(solution)/shard_map/all_to_all | solution.py:23
  44.6 6.2 %collective-permute-start.3 = (bf16[128,128]{1,0:T(8,128)(2,1)S(1)}, bf16[128,128]{1,0:T(8,128)(2,1)S(1)}, u32[]{:S(2)}, u32[]{:S(2)}) collective-permute-start(bf16[128,128]{1,0:T(8,128)(2,1)S(1)} %get-tuple-element.35), channel_id=1, source_target_pairs={{0,8},{8,16},{16,24},{24,0},{1,9},{9,17},{17,25},{25,1},{2,10},{10... | collective-permute-start | bytes 98312 | tf_op jit(solution)/shard_map/ppermute | solution.py:13
  50.8 1.5 collective-permute-start.4
  52.7 2.0 %collective-permute-done.5 = bf16[128,128]{1,0:T(8,128)(2,1)S(1)} collective-permute-done((bf16[128,128]{1,0:T(8,128)(2,1)S(1)}, bf16[128,128]{1,0:T(8,128)(2,1)S(1)}, u32[]{:S(2)}, u32[]{:S(2)}) %collective-permute-start.5) | collective-permute-done | bytes 32800 | tf_op jit(solution)/shard_map/ppermute | solution.py:13
  55.7 2.0 %collective-permute-start.8 = (bf16[128,128]{1,0:T(8,128)(2,1)S(1)}, bf16[128,128]{1,0:T(8,128)(2,1)S(1)}, u32[]{:S(2)}, u32[]{:S(2)}) collective-permute-start(bf16[128,128]{1,0:T(8,128)(2,1)S(1)} %fusion.54), channel_id=1, source_target_pairs={{0,8},{8,16},{16,24},{24,0},{1,9},{9,17},{17,25},{25,1},{2,10},{10... | collective-permute-start | bytes 98312 | tf_op jit(solution)/shard_map/ppermute | solution.py:13
  58.3 1.9 collective-permute-start.6
  63.6 1.6 collective-permute-start.14
  65.2 1.9 collective-permute-start.13
  68.0 3.5 %all-to-all-start.1 = ((bf16[4,512,128]{2,1,0:T(8,128)(2,1)}), bf16[4,512,128]{2,1,0:T(8,128)(2,1)S(1)}, u32[]{:S(2)}, u32[]{:S(2)}) async-start(bf16[4,512,128]{2,1,0:T(8,128)(2,1)} %broadcast_in_dim.30), calls=%async_computation.1 | async-start | bytes 1048576 | tf_op jit(solution)/shard_map/all_to_all | solution.py:23
  71.8 6.2 %all-to-all-done.1 = bf16[4,512,128]{2,1,0:T(8,128)(2,1)S(1)} async-done(((bf16[4,512,128]{2,1,0:T(8,128)(2,1)}), bf16[4,512,128]{2,1,0:T(8,128)(2,1)S(1)}, u32[]{:S(2)}, u32[]{:S(2)}) %all-to-all-start.1) | async-done | bytes 524320 | tf_op jit(solution)/shard_map/all_to_all | solution.py:23
  80.4 2.0 %multiply_reduce_fusion.4 = (f32[512]{0:T(512)S(1)}, f32[512,1024]{1,0:T(8,128)}) fusion(f32[512,1024]{1,0:T(8,128)S(1)} %fusion.17, bf16[512,128]{1,0:T(8,128)(2,1)S(1)} %constant_dynamic-update-slice_fusion, bf16[1,128,1024]{2,1,0:T(8,128)(2,1)S(1)} %copy-done.3), kind=kOutput, calls=%fused_computation.14 | convolution fusion | flops 135790080 | bytes 4589568 | tf_op jit(solution)/shard_map/dot_general | solution.py:51
  83.0 3.2 %all-to-all-start.2 = ((f32[4,1,512]{2,1,0:T(1,128)}), f32[4,1,512]{2,1,0:T(1,128)S(1)}, u32[]{:S(2)}, u32[]{:S(2)}) async-start(f32[4,1,512]{2,1,0:T(1,128)} %broadcast_in_dim.31), calls=%async_computation.2 | async-start | bytes 16384 | tf_op jit(solution)/shard_map/all_to_all | solution.py:23
  86.3 4.6 %all-to-all-done.2 = f32[4,1,512]{2,1,0:T(1,128)S(1)} async-done(((f32[4,1,512]{2,1,0:T(1,128)}), f32[4,1,512]{2,1,0:T(1,128)S(1)}, u32[]{:S(2)}, u32[]{:S(2)}) %all-to-all-start.2) | async-done | bytes 8224 | tf_op jit(solution)/shard_map/all_to_all | solution.py:23
  91.0 2.2 %fusion.14 = bf16[512,128]{1,0:T(8,128)(2,1)S(1)} fusion(f32[512,1024]{1,0:T(8,128)} %get-tuple-element.39, f32[1024]{0:T(1024)S(1)} %bitcast.115, bf16[1,1024,128]{2,1,0:T(8,128)(2,1)S(1)} %copy-done.4, f32[512]{0:T(512)S(1)} %add_rsqrt_fusion.1), kind=kOutput, calls=%fused_computation.32 | convolution fusion | flops 135397376 | bytes 2496512 | tf_op jit(solution)/shard_map/dot_general | solution.py:51
  95.4 1.7 multiply_reduce_fusion.3
  97.8 3.2 %all-to-all-start.3 = ((f32[4,1,512]{2,1,0:T(1,128)}), f32[4,1,512]{2,1,0:T(1,128)S(1)}, u32[]{:S(2)}, u32[]{:S(2)}) async-start(f32[4,1,512]{2,1,0:T(1,128)} %broadcast_in_dim.32), calls=%async_computation.3 | async-start | bytes 16384 | tf_op jit(solution)/shard_map/all_to_all | solution.py:23
  101.1 4.6 %all-to-all-done.3 = f32[4,1,512]{2,1,0:T(1,128)S(1)} async-done(((f32[4,1,512]{2,1,0:T(1,128)}), f32[4,1,512]{2,1,0:T(1,128)S(1)}, u32[]{:S(2)}, u32[]{:S(2)}) %all-to-all-start.3) | async-done | bytes 8224 | tf_op jit(solution)/shard_map/all_to_all | solution.py:23
  105.8 3.4 %multiply_reduce_fusion.2 = (f32[512]{0:T(512)S(1)}, f32[512,1024]{1,0:T(8,128)}) fusion(f32[512,1024]{1,0:T(8,128)} %get-tuple-element.41, f32[512]{0:T(512)S(1)} %add_rsqrt_fusion, f32[1024]{0:T(1024)S(1)} %bitcast.116, bf16[512,128]{1,0:T(8,128)(2,1)S(1)} %constant_dynamic-update-slice_fusion.4, bf16[1,1024,128]{2,1,0:T(8,128)(2,1)S(1)} %copy-done.4), kind=kOutput, calls=%fused_computation.10 | convolution fusion | flops 136314368 | bytes 4595712 | tf_op jit(solution)/shard_map/dot_general | solution.py:51
  109.2 7.0 %all_to_all.50 = f32[4,1,512]{2,1,0:T(1,128)S(1)} all-to-all(f32[4,1,512]{2,1,0:T(1,128)S(1)} %broadcast_in_dim.34), channel_id=1, replica_groups=mesh['dp'=4,'pipe'=2,'tensor'=4] {'tensor'}, dimensions={0} | all-to-all | bytes 16384 | tf_op jit(solution)/shard_map/all_to_all | solution.py:23
  116.2 2.8 %convolution_convert_fusion.7 = bf16[512,128]{1,0:T(8,128)(2,1)S(1)} fusion(f32[512,1024]{1,0:T(8,128)} %get-tuple-element.43, f32[512,1024]{1,0:T(8,128)} %get-tuple-element.41, f32[512]{0:T(512)S(1)} %broadcast_multiply_fusion.1, f32[512]{0:T(512)S(1)} %add_rsqrt_fusion, f32[1024]{0:T(1024)S(1)} %bitcast.117, bf16[1,128,1024]{2,1,0:T(8,128)(2,1)S(1)} %copy-done.3), kind=kOutput, calls=%fused_computation.31 | convolution fusion | flops 137428992 | bytes 4595712 | tf_op jit(solution)/shard_map/dot_general | solution.py:51
  120.3 1.9 collective-permute-done.16
  122.3 4.1 %multiply_reduce_fusion = (f32[1024]{0:T(1024)}, f32[512]{0:T(512)S(1)}, f32[512,1024]{1,0:T(8,128)}) fusion(f32[512,1024]{1,0:T(8,128)} %get-tuple-element.41, f32[512]{0:T(512)S(1)} %add_rsqrt_fusion, f32[1024]{0:T(1024)S(1)} %bitcast.118, bf16[1,1024,128]{2,1,0:T(8,128)(2,1)S(1)} %copy-done.4, bf16[512,128]{1,0:T(8,128)(2,1)S(1)} %collective-permute-done.16, ...), kind=kOutput, calls=%fused_computation.5 | convolution fusion | flops 137427456 | bytes 4730881 | tf_op jit(solution)/shard_map/dot_general | solution.py:51
  127.0 3.2 %all-to-all-start.5 = ((f32[4,1,512]{2,1,0:T(1,128)}), f32[4,1,512]{2,1,0:T(1,128)S(1)}, u32[]{:S(2)}, u32[]{:S(2)}) async-start(f32[4,1,512]{2,1,0:T(1,128)} %broadcast_in_dim.35), calls=%async_computation.5 | async-start | bytes 16384 | tf_op jit(solution)/shard_map/all_to_all | solution.py:23
  130.3 2.7 %fusion.15 = f32[512,128]{1,0:T(8,128)} fusion(f32[512,1024]{1,0:T(8,128)} %get-tuple-element.41, f32[1024]{0:T(1024)S(1)} %bitcast.119, bf16[1,1024,128]{2,1,0:T(8,128)(2,1)S(1)} %copy-done.4), kind=kOutput, calls=%fused_computation.33 | convolution fusion | flops 135266304 | bytes 2625536 | tf_op jit(solution)/shard_map/dot_general | solution.py:51
  133.0 1.9 all-to-all-done.5
  135.0 2.8 %multiply_convert_fusion.1 = bf16[512,1024]{1,0:T(8,128)(2,1)S(1)} fusion(f32[512,1024]{1,0:T(8,128)} %get-tuple-element.44, f32[512,1024]{1,0:T(8,128)} %get-tuple-element.41, f32[512]{0:T(512)S(1)} %broadcast_multiply_fusion, f32[512]{0:T(512)S(1)} %add_rsqrt_fusion, f32[1024]{0:T(1024)S(1)} %bitcast.120), kind=kLoop, calls=%fused_computation.7 | loop fusion | flops 3145728 | bytes 5251072 | tf_op jit(solution)/shard_map/convert_element_type | solution.py:117
  139.5 4.1 %all-to-all-start.6 = ((bf16[4,512,128]{2,1,0:T(8,128)(2,1)}), bf16[4,512,128]{2,1,0:T(8,128)(2,1)}, u32[]{:S(2)}, u32[]{:S(2)}) async-start(bf16[4,512,128]{2,1,0:T(8,128)(2,1)} %pad_maximum_fusion.4), calls=%async_computation.6 | async-start | bytes 1048576 | tf_op jit(solution)/shard_map/all_to_all | solution.py:23
  143.7 1.5 fusion.55
  145.2 2.9 %fusion.12 = bf16[1,1024,128]{2,1,0:T(8,128)(2,1)} fusion(f32[512,1024]{1,0:T(8,128)} %get-tuple-element.41, f32[512]{0:T(512)S(1)} %copy-done.17, f32[1024]{0:T(1024)S(1)} %bitcast.121, bf16[512,128]{1,0:T(8,128)(2,1)} %copy-done.13, bf16[512,128]{1,0:T(8,128)(2,1)S(1)} %constant_dynamic-update-slice_fusion.4, pred[]{:T(512)S(6)} %eq.7), kind=kOutput, calls=%fused_computation.28 | convolution fusion | flops 135987200 | bytes 2627585 | tf_op jit(solution)/shard_map/dot_general | solution.py:51
  148.1 3.4 %all-to-all-done.6 = bf16[4,512,128]{2,1,0:T(8,128)(2,1)} async-done(((bf16[4,512,128]{2,1,0:T(8,128)(2,1)}), bf16[4,512,128]{2,1,0:T(8,128)(2,1)}, u32[]{:S(2)}, u32[]{:S(2)}) %all-to-all-start.6) | async-done | bytes 524320 | tf_op jit(solution)/shard_map/all_to_all | solution.py:23
  151.6 1.8 reduce_sum.123
  153.4 1.8 broadcast_in_dim.74
  155.1 4.3 %all-to-all-start.7 = ((bf16[4,512,128]{2,1,0:T(8,128)(2,1)}), bf16[4,512,128]{2,1,0:T(8,128)(2,1)}, u32[]{:S(2)}, u32[]{:S(2)}) async-start(bf16[4,512,128]{2,1,0:T(8,128)(2,1)} %broadcast_in_dim.74), calls=%async_computation.7 | async-start | bytes 1048576 | tf_op jit(solution)/shard_map/all_to_all | solution.py:23
  161.6 4.8 %all-to-all-done.7 = bf16[4,512,128]{2,1,0:T(8,128)(2,1)} async-done(((bf16[4,512,128]{2,1,0:T(8,128)(2,1)}), bf16[4,512,128]{2,1,0:T(8,128)(2,1)}, u32[]{:S(2)}, u32[]{:S(2)}) %all-to-all-start.7) | async-done | bytes 524320 | tf_op jit(solution)/shard_map/all_to_all | solution.py:23
  168.2 1.9 convolution_convert_fusion
  172.7 4.3 %all-to-all-start.8 = ((bf16[4,128,1024]{2,1,0:T(8,128)(2,1)}), bf16[4,128,1024]{2,1,0:T(8,128)(2,1)}, u32[]{:S(2)}, u32[]{:S(2)}) async-start(bf16[4,128,1024]{2,1,0:T(8,128)(2,1)} %pad_maximum_fusion.1), calls=%async_computation.8 | async-start | bytes 2097152 | tf_op jit(solution)/shard_map/all_to_all | solution.py:23
  176.9 1.9 fusion.11
  178.9 1.4 fusion.56
  180.3 2.4 %fusion.10 = bf16[1,128,1024]{2,1,0:T(8,128)(2,1)} fusion(bf16[1024,512]{1,0:T(8,128)(2,1)} %all-reduce.2.cloned.1.call-done, bf16[512,128]{1,0:T(8,128)(2,1)S(1)} %get-tuple-element.20, bf16[512,128]{1,0:T(8,128)(2,1)S(1)} %get-tuple-element.21, bf16[512,128]{1,0:T(8,128)(2,1)} %copy-done.14, bf16[512,128]{1,0:T(8,128)(2,1)S(1)} %get-tuple-element.19), kind=kOutput, calls=%fused_computation.26 | convolution fusion | flops 134873088 | bytes 1835008 | tf_op jit(solution)/shard_map/dot_general | solution.py:51
  182.7 4.1 %convert_bitcast_fusion = bf16[1,1024,1024]{2,1,0:T(8,128)(2,1)} fusion(bf16[1024,512]{1,0:T(8,128)(2,1)} %copy-done.11, bf16[1,512,1024]{2,1,0:T(8,128)(2,1)} %param.11), kind=kOutput, calls=%fused_computation.6 | convolution fusion | flops 1074790400 | bytes 4194304 | tf_op jit(solution)/shard_map/dot_general | solution.py:51
  186.8 1.9 all-to-all-done.8
  188.7 2.2 %reduce_sum.124 = bf16[128,1024]{1,0:T(8,128)(2,1)} reduce(bf16[4,128,1024]{2,1,0:T(8,128)(2,1)} %all-to-all-done.8, bf16[]{:T(256)} %constant.28.clone.1), dimensions={0}, to_apply=%region_11.12 | reduce | flops 393216 | bytes 1310722 | tf_op jit(solution)/shard_map/reduce_sum | solution.py:32
  (109 shorter events, 24.2 us)
Async XLA Ops:
  7.2 7.0 %copy-start = (bf16[1,1024,1024]{2,1,0:T(8,128)(2,1)S(1)}, bf16[1,1024,1024]{2,1,0:T(8,128)(2,1)}, u32[]{:S(2)}) copy-start(bf16[1,1024,1024]{2,1,0:T(8,128)(2,1)} %param.10) | copy-start | bytes 6291460
  7.2 23.1 %copy-start.20 = (bf16[1,128,1024]{2,1,0:T(8,128)(2,1)S(1)}, bf16[1,128,1024]{2,1,0:T(8,128)(2,1)}, u32[]{:S(2)}) copy-start(bf16[1,128,1024]{2,1,0:T(8,128)(2,1)} %param.9) | copy-start | bytes 786436
  7.2 12.7 %collective-permute-start.2 = (bf16[128,1024]{1,0:T(8,128)(2,1)}, bf16[128,1024]{1,0:T(8,128)(2,1)}, u32[]{:S(2)}, u32[]{:S(2)}) collective-permute-start(bf16[128,1024]{1,0:T(8,128)(2,1)} %bitcast.123), channel_id=1, source_target_pairs={{0,8},{8,16},{16,24},{24,0},{1,9},{9,17},{17,25},{25,1},{2,10},{10... | collective-permute-start | bytes 786440 | tf_op jit(solution)/shard_map/ppermute | solution.py:13
  10.3 20.0 %collective-permute-start.1 = (bf16[128,1024]{1,0:T(8,128)(2,1)}, bf16[128,1024]{1,0:T(8,128)(2,1)}, u32[]{:S(2)}, u32[]{:S(2)}) collective-permute-start(bf16[128,1024]{1,0:T(8,128)(2,1)} %bitcast.124), channel_id=1, source_target_pairs={{0,16},{8,24},{16,0},{24,8},{1,17},{9,25},{17,1},{25,9},{2,18},{10... | collective-permute-start | bytes 786440 | tf_op jit(solution)/shard_map/ppermute | solution.py:13
  12.9 17.4 %collective-permute-start = (bf16[128,1024]{1,0:T(8,128)(2,1)}, bf16[128,1024]{1,0:T(8,128)(2,1)}, u32[]{:S(2)}, u32[]{:S(2)}) collective-permute-start(bf16[128,1024]{1,0:T(8,128)(2,1)} %bitcast.125), channel_id=1, source_target_pairs={{0,24},{8,0},{16,8},{24,16},{1,25},{9,1},{17,9},{25,17},{2,26},{10... | collective-permute-start | bytes 786440 | tf_op jit(solution)/shard_map/ppermute | solution.py:13
  16.7 15.4 %copy-start.10 = (bf16[1024,512]{1,0:T(8,128)(2,1)}, bf16[1024,512]{1,0:T(8,128)(2,1)S(1)}, u32[]{:S(2)}) copy-start(bf16[1024,512]{1,0:T(8,128)(2,1)S(1)} %fusion.4) | copy-start | bytes 3145732
  32.2 28.0 %copy-start.18 = (bf16[128,128]{1,0:T(8,128)(2,1)S(1)}, bf16[128,128]{1,0:T(8,128)(2,1)}, u32[]{:S(2)}) copy-start(bf16[128,128]{1,0:T(8,128)(2,1)} %param.16) | copy-start | bytes 98308
  32.2 31.4 %copy-start.19 = (bf16[128,128]{1,0:T(8,128)(2,1)S(1)}, bf16[128,128]{1,0:T(8,128)(2,1)}, u32[]{:S(2)}) copy-start(bf16[128,128]{1,0:T(8,128)(2,1)} %param.17) | copy-start | bytes 98308
  44.6 8.1 %collective-permute-start.3 = (bf16[128,128]{1,0:T(8,128)(2,1)S(1)}, bf16[128,128]{1,0:T(8,128)(2,1)S(1)}, u32[]{:S(2)}, u32[]{:S(2)}) collective-permute-start(bf16[128,128]{1,0:T(8,128)(2,1)S(1)} %get-tuple-element.35), channel_id=1, source_target_pairs={{0,8},{8,16},{16,24},{24,0},{1,9},{9,17},{17,25},{25,1},{2,10},{10... | collective-permute-start | bytes 98312 | tf_op jit(solution)/shard_map/ppermute | solution.py:13
  50.8 3.9 %collective-permute-start.5 = (bf16[128,128]{1,0:T(8,128)(2,1)S(1)}, bf16[128,128]{1,0:T(8,128)(2,1)S(1)}, u32[]{:S(2)}, u32[]{:S(2)}) collective-permute-start(bf16[128,128]{1,0:T(8,128)(2,1)S(1)} %get-tuple-element.36), channel_id=1, source_target_pairs={{0,24},{8,0},{16,8},{24,16},{1,25},{9,1},{17,9},{25,17},{2,26},{10... | collective-permute-start | bytes 98312 | tf_op jit(solution)/shard_map/ppermute | solution.py:13
  50.8 4.8 %collective-permute-start.4 = (bf16[128,128]{1,0:T(8,128)(2,1)S(1)}, bf16[128,128]{1,0:T(8,128)(2,1)S(1)}, u32[]{:S(2)}, u32[]{:S(2)}) collective-permute-start(bf16[128,128]{1,0:T(8,128)(2,1)S(1)} %get-tuple-element.37), channel_id=1, source_target_pairs={{0,16},{8,24},{16,0},{24,8},{1,17},{9,25},{17,1},{25,9},{2,18},{10... | collective-permute-start | bytes 98312 | tf_op jit(solution)/shard_map/ppermute | solution.py:13
  55.7 7.0 %collective-permute-start.8 = (bf16[128,128]{1,0:T(8,128)(2,1)S(1)}, bf16[128,128]{1,0:T(8,128)(2,1)S(1)}, u32[]{:S(2)}, u32[]{:S(2)}) collective-permute-start(bf16[128,128]{1,0:T(8,128)(2,1)S(1)} %fusion.54), channel_id=1, source_target_pairs={{0,8},{8,16},{16,24},{24,0},{1,9},{9,17},{17,25},{25,1},{2,10},{10... | collective-permute-start | bytes 98312 | tf_op jit(solution)/shard_map/ppermute | solution.py:13
  57.7 5.9 %collective-permute-start.7 = (bf16[128,128]{1,0:T(8,128)(2,1)S(1)}, bf16[128,128]{1,0:T(8,128)(2,1)S(1)}, u32[]{:S(2)}, u32[]{:S(2)}) collective-permute-start(bf16[128,128]{1,0:T(8,128)(2,1)S(1)} %fusion.54), channel_id=1, source_target_pairs={{0,16},{8,24},{16,0},{24,8},{1,17},{9,25},{17,1},{25,9},{2,18},{10... | collective-permute-start | bytes 98312 | tf_op jit(solution)/shard_map/ppermute | solution.py:13
  58.3 6.9 %collective-permute-start.6 = (bf16[128,128]{1,0:T(8,128)(2,1)S(1)}, bf16[128,128]{1,0:T(8,128)(2,1)S(1)}, u32[]{:S(2)}, u32[]{:S(2)}) collective-permute-start(bf16[128,128]{1,0:T(8,128)(2,1)S(1)} %fusion.54), channel_id=1, source_target_pairs={{0,24},{8,0},{16,8},{24,16},{1,25},{9,1},{17,9},{25,17},{2,26},{10... | collective-permute-start | bytes 98312 | tf_op jit(solution)/shard_map/ppermute | solution.py:13
  60.3 11.4 %collective-permute-start.10 = (bf16[128,128]{1,0:T(8,128)(2,1)S(1)}, bf16[128,128]{1,0:T(8,128)(2,1)S(1)}, u32[]{:S(2)}, u32[]{:S(2)}) collective-permute-start(bf16[128,128]{1,0:T(8,128)(2,1)S(1)} %copy-done.18), channel_id=1, source_target_pairs={{0,16},{8,24},{16,0},{24,8},{1,17},{9,25},{17,1},{25,9},{2,18},{10... | collective-permute-start | bytes 98312 | tf_op jit(solution)/shard_map/ppermute | solution.py:13
  61.6 9.9 %collective-permute-start.9 = (bf16[128,128]{1,0:T(8,128)(2,1)S(1)}, bf16[128,128]{1,0:T(8,128)(2,1)S(1)}, u32[]{:S(2)}, u32[]{:S(2)}) collective-permute-start(bf16[128,128]{1,0:T(8,128)(2,1)S(1)} %copy-done.18), channel_id=1, source_target_pairs={{0,24},{8,0},{16,8},{24,16},{1,25},{9,1},{17,9},{25,17},{2,26},{10... | collective-permute-start | bytes 98312 | tf_op jit(solution)/shard_map/ppermute | solution.py:13
  62.7 9.0 %collective-permute-start.11 = (bf16[128,128]{1,0:T(8,128)(2,1)S(1)}, bf16[128,128]{1,0:T(8,128)(2,1)S(1)}, u32[]{:S(2)}, u32[]{:S(2)}) collective-permute-start(bf16[128,128]{1,0:T(8,128)(2,1)S(1)} %copy-done.18), channel_id=1, source_target_pairs={{0,8},{8,16},{16,24},{24,0},{1,9},{9,17},{17,25},{25,1},{2,10},{10... | collective-permute-start | bytes 98312 | tf_op jit(solution)/shard_map/ppermute | solution.py:13
  63.6 30.9 %collective-permute-start.14 = (bf16[128,128]{1,0:T(8,128)(2,1)S(1)}, bf16[128,128]{1,0:T(8,128)(2,1)S(1)}, u32[]{:S(2)}, u32[]{:S(2)}) collective-permute-start(bf16[128,128]{1,0:T(8,128)(2,1)S(1)} %copy-done.19), channel_id=1, source_target_pairs={{0,16},{8,24},{16,0},{24,8},{1,17},{9,25},{17,1},{25,9},{2,18},{10... | collective-permute-start | bytes 98312 | tf_op jit(solution)/shard_map/ppermute | solution.py:13
  65.2 29.2 %collective-permute-start.13 = (bf16[128,128]{1,0:T(8,128)(2,1)S(1)}, bf16[128,128]{1,0:T(8,128)(2,1)S(1)}, u32[]{:S(2)}, u32[]{:S(2)}) collective-permute-start(bf16[128,128]{1,0:T(8,128)(2,1)S(1)} %copy-done.19), channel_id=1, source_target_pairs={{0,24},{8,0},{16,8},{24,16},{1,25},{9,1},{17,9},{25,17},{2,26},{10... | collective-permute-start | bytes 98312 | tf_op jit(solution)/shard_map/ppermute | solution.py:13
  68.0 10.0 %all-to-all-start.1 = ((bf16[4,512,128]{2,1,0:T(8,128)(2,1)}), bf16[4,512,128]{2,1,0:T(8,128)(2,1)S(1)}, u32[]{:S(2)}, u32[]{:S(2)}) async-start(bf16[4,512,128]{2,1,0:T(8,128)(2,1)} %broadcast_in_dim.30), calls=%async_computation.1 | async-start | bytes 1048576 | tf_op jit(solution)/shard_map/all_to_all | solution.py:23
  71.5 29.6 %collective-permute-start.15 = (bf16[128,128]{1,0:T(8,128)(2,1)S(1)}, bf16[128,128]{1,0:T(8,128)(2,1)S(1)}, u32[]{:S(2)}, u32[]{:S(2)}) collective-permute-start(bf16[128,128]{1,0:T(8,128)(2,1)S(1)} %copy-done.19), channel_id=1, source_target_pairs={{0,8},{8,16},{16,24},{24,0},{1,9},{9,17},{17,25},{25,1},{2,10},{10... | collective-permute-start | bytes 98312 | tf_op jit(solution)/shard_map/ppermute | solution.py:13
  71.7 23.7 %copy-start.6 = (bf16[512,128]{1,0:T(8,128)(2,1)}, bf16[512,128]{1,0:T(8,128)(2,1)S(1)}, u32[]{:S(2)}) copy-start(bf16[512,128]{1,0:T(8,128)(2,1)S(1)} %constant_dynamic-update-slice_fusion) | copy-start | bytes 393220
  78.0 1.4 copy-start.8
  78.1 0.8 copy-start.5
  79.4 0.9 copy-start.3
  80.3 2.0 %copy-start.1 = (f32[512,1024]{1,0:T(8,128)}, f32[512,1024]{1,0:T(8,128)S(1)}, u32[]{:S(2)}) copy-start(f32[512,1024]{1,0:T(8,128)S(1)} %fusion.17) | copy-start | bytes 6291460
  80.3 10.6 %copy-start.4 = (bf16[1,1024,128]{2,1,0:T(8,128)(2,1)S(1)}, bf16[1,1024,128]{2,1,0:T(8,128)(2,1)}, u32[]{:S(2)}) copy-start(bf16[1,1024,128]{2,1,0:T(8,128)(2,1)} %param.14) | copy-start | bytes 786436
  80.3 10.6 %copy-start.15 = (f32[1,1024]{1,0:T(1,128)S(1)}, f32[1,1024]{1,0:T(1,128)}, u32[]{:S(2)}) copy-start(f32[1,1024]{1,0:T(1,128)} %param.13) | copy-start | bytes 12292
  83.0 7.9 %all-to-all-start.2 = ((f32[4,1,512]{2,1,0:T(1,128)}), f32[4,1,512]{2,1,0:T(1,128)S(1)}, u32[]{:S(2)}, u32[]{:S(2)}) async-start(f32[4,1,512]{2,1,0:T(1,128)} %broadcast_in_dim.31), calls=%async_computation.2 | async-start | bytes 16384 | tf_op jit(solution)/shard_map/all_to_all | solution.py:23
  90.9 4.5 %copy-start.2 = (f32[512,1024]{1,0:T(8,128)S(1)}, f32[512,1024]{1,0:T(8,128)}, u32[]{:S(2)}) copy-start(f32[512,1024]{1,0:T(8,128)} %copy-done.1) | copy-start | bytes 6291460
  93.1 2.3 %collective-permute-start.12 = (bf16[512,128]{1,0:T(8,128)(2,1)S(1)}, bf16[512,128]{1,0:T(8,128)(2,1)S(1)}, u32[]{:S(2)}, u32[]{:S(2)}) collective-permute-start(bf16[512,128]{1,0:T(8,128)(2,1)S(1)} %fusion.14), channel_id=1, source_target_pairs={{0,4},{1,5},{2,6},{3,7},{8,12},{9,13},{10,14},{11,15},{16,20},{17,... | collective-permute-start | bytes 393224 | tf_op jit(solution)/shard_map/ppermute | solution.py:19
  95.4 1.8 copy-start.12
  97.8 7.9 %all-to-all-start.3 = ((f32[4,1,512]{2,1,0:T(1,128)}), f32[4,1,512]{2,1,0:T(1,128)S(1)}, u32[]{:S(2)}, u32[]{:S(2)}) async-start(f32[4,1,512]{2,1,0:T(1,128)} %broadcast_in_dim.32), calls=%async_computation.3 | async-start | bytes 16384 | tf_op jit(solution)/shard_map/all_to_all | solution.py:23
  101.0 79.2 %all-reduce.2.cloned.1.call-start = ((), (), s32[]{:S(2)}) async-start(), calls=%async_computation.9 | async-start | bytes 2097152 | tf_op jit(solution)/shard_map/psum | solution.py:96
  105.7 29.2 %copy-start.16 = (f32[512]{0:T(512)}, f32[512]{0:T(512)S(1)}, u32[]{:S(2)}) copy-start(f32[512]{0:T(512)S(1)} %add_rsqrt_fusion) | copy-start | bytes 6148
  119.0 3.2 %collective-permute-start.16 = (bf16[512,128]{1,0:T(8,128)(2,1)S(1)}, bf16[512,128]{1,0:T(8,128)(2,1)S(1)}, u32[]{:S(2)}, u32[]{:S(2)}) collective-permute-start(bf16[512,128]{1,0:T(8,128)(2,1)S(1)} %convolution_convert_fusion.7), channel_id=1, source_target_pairs={{4,0},{5,1},{6,2},{7,3},{12,8},{13,9},{14,10},{15,11},{20,16},{21,... | collective-permute-start | bytes 393224 | tf_op jit(solution)/shard_map/ppermute | solution.py:19
  122.3 4.2 %copy-start.13 = (bf16[512,128]{1,0:T(8,128)(2,1)}, bf16[512,128]{1,0:T(8,128)(2,1)S(1)}, u32[]{:S(2)}) copy-start(bf16[512,128]{1,0:T(8,128)(2,1)S(1)} %collective-permute-done.16) | copy-start | bytes 393220
  127.0 7.9 %all-to-all-start.5 = ((f32[4,1,512]{2,1,0:T(1,128)}), f32[4,1,512]{2,1,0:T(1,128)S(1)}, u32[]{:S(2)}, u32[]{:S(2)}) async-start(f32[4,1,512]{2,1,0:T(1,128)} %broadcast_in_dim.35), calls=%async_computation.5 | async-start | bytes 16384 | tf_op jit(solution)/shard_map/all_to_all | solution.py:23
  135.0 2.8 %copy-start.9 = (bf16[1,512,1024]{2,1,0:T(8,128)(2,1)S(1)}, bf16[1,512,1024]{2,1,0:T(8,128)(2,1)}, u32[]{:S(2)}) copy-start(bf16[1,512,1024]{2,1,0:T(8,128)(2,1)} %param.12) | copy-start | bytes 3145732
  138.5 5.1 %slice-start = ((f32[512]{0:T(512)}), f32[128]{0:T(128)S(1)}, s32[]{:S(2)}) async-start(f32[512]{0:T(512)} %copy-done.16), calls=%async_computation.10 | async-start | bytes 1024 | tf_op jit(solution)/shard_map/slice | solution.py:140
  138.5 6.7 %copy-start.17 = (f32[512]{0:T(512)S(1)}, f32[512]{0:T(512)}, u32[]{:S(2)}) copy-start(f32[512]{0:T(512)} %copy-done.16) | copy-start | bytes 6148
  139.5 12.1 %all-to-all-start.6 = ((bf16[4,512,128]{2,1,0:T(8,128)(2,1)}), bf16[4,512,128]{2,1,0:T(8,128)(2,1)}, u32[]{:S(2)}, u32[]{:S(2)}) async-start(bf16[4,512,128]{2,1,0:T(8,128)(2,1)} %pad_maximum_fusion.4), calls=%async_computation.6 | async-start | bytes 1048576 | tf_op jit(solution)/shard_map/all_to_all | solution.py:23
  148.1 11.4 %copy-start.7 = (bf16[512,128]{1,0:T(8,128)(2,1)S(1)}, bf16[512,128]{1,0:T(8,128)(2,1)}, u32[]{:S(2)}) copy-start(bf16[512,128]{1,0:T(8,128)(2,1)} %copy-done.6) | copy-start | bytes 393220
  155.1 11.2 %all-to-all-start.7 = ((bf16[4,512,128]{2,1,0:T(8,128)(2,1)}), bf16[4,512,128]{2,1,0:T(8,128)(2,1)}, u32[]{:S(2)}, u32[]{:S(2)}) async-start(bf16[4,512,128]{2,1,0:T(8,128)(2,1)} %broadcast_in_dim.74), calls=%async_computation.7 | async-start | bytes 1048576 | tf_op jit(solution)/shard_map/all_to_all | solution.py:23
  167.5 0.7 copy-start.14
  170.1 1.3 copy-start.11
  172.7 16.0 %all-to-all-start.8 = ((bf16[4,128,1024]{2,1,0:T(8,128)(2,1)}), bf16[4,128,1024]{2,1,0:T(8,128)(2,1)}, u32[]{:S(2)}, u32[]{:S(2)}) async-start(bf16[4,128,1024]{2,1,0:T(8,128)(2,1)} %pad_maximum_fusion.1), calls=%async_computation.8 | async-start | bytes 2097152 | tf_op jit(solution)/shard_map/all_to_all | solution.py:23
Sparse Core Ops, SparseCore 0:
  120.5 49.8 all-reduce.1

commit v3 on v2

v3 whole, which is shorter than its diff:
```python
import jax
import jax.numpy as jnp
from jax import lax
from jax.sharding import PartitionSpec as P

epsilon = 1e-05
f32 = jnp.float32
bf16 = jnp.bfloat16


def shift(shard, axis, by):
    devices = lax.axis_size(axis)
    return lax.ppermute(shard, axis, [(i, (i + by) % devices) for i in range(devices)])


def move(shard, axis, by):
    devices = lax.axis_size(axis)
    pairs = [(i, i + by) for i in range(devices) if 0 <= i + by < devices]
    return lax.ppermute(shard, axis, pairs)


def gathered(shard, axis):
    return [shard] + [shift(shard, axis, -k) for k in range(1, lax.axis_size(axis))]


def scatter_sum(blocks, axis):
    total = blocks[0].astype(f32)
    for k in range(1, len(blocks)):
        total = total + shift(blocks[k].astype(bf16), axis, k).astype(f32)
    return total


def place(axis, k):
    return lax.rem(lax.axis_index(axis) + k, lax.axis_size(axis))


def block(array, axis, k, dim):
    size = array.shape[dim] // lax.axis_size(axis)
    return lax.dynamic_slice_in_dim(array, place(axis, k) * size, size, dim)


def laid(blocks, axis, dim):
    size = blocks[0].shape[dim]
    shape = list(blocks[0].shape)
    shape[dim] = size * len(blocks)
    whole = jnp.zeros(shape, blocks[0].dtype)
    for k, part in enumerate(blocks):
        whole = lax.dynamic_update_slice_in_dim(whole, part, place(axis, k) * size, dim)
    return whole


def diagonal(blocks, axis):
    rows, cols = blocks[0].shape
    whole = jnp.zeros((rows * len(blocks), cols * len(blocks)), blocks[0].dtype)
    for k, part in enumerate(blocks):
        at = place(axis, k)
        whole = lax.dynamic_update_slice(whole, part, (at * rows, at * cols))
    return whole


def dot(left, right, over):
    return lax.dot_general(left, right, ((over[0], over[1]), ((), ())), preferred_element_type=f32)


def on_device(
    heads_out,
    out_proj,
    encoder,
    decoder,
    norm_gain,
    send_encoder,
    recv_decoder,
    input_code,
    code_cotangent,
):
    sections = lax.axis_size("pipe")
    section = lax.axis_index("pipe")
    groups = lax.axis_size("dp")
    parts = lax.axis_size("tensor")
    group = lax.axis_index("dp")
    width = norm_gain.shape[1] * parts
    proj = out_proj[0]
    enc = encoder[0]
    dec = decoder[0]
    gain = norm_gain[0]
    send = send_encoder[0]
    recv = recv_decoder[0]
    tokens, code_cols = input_code.shape
    codes = dec.shape[0]
    per_part = codes // parts

    head_rows = jnp.concatenate(gathered(heads_out[0], "dp"))
    ends = jnp.concatenate(gathered(jnp.concatenate([input_code, code_cotangent], 1), "dp"))
    end_blocks = gathered(ends, "tensor")
    received = laid([b[:, :code_cols] for b in end_blocks], "tensor", 1)
    incoming = laid([b[:, code_cols:] for b in end_blocks], "tensor", 1)

    send_gain = (send.astype(f32) * gain[:, None]).astype(bf16)
    decoders = jnp.concatenate([dec, recv])
    code_gram = dot(dec, dec, ((1,), (1,)))
    side = jnp.concatenate(
        [
            dot(recv, decoders, ((1,), (1,))),
            dot(send_gain, decoders, ((0,), (1,))),
        ],
        axis=1,
    ).astype(bf16)
    gram_rows = scatter_sum([block(code_gram, "tensor", k, 0) for k in range(parts)], "tensor")
    gram = laid(gathered(gram_rows.astype(bf16), "tensor"), "tensor", 0)
    sides = gathered(side, "tensor")
    both = codes + code_cols
    recv_code = laid([b[:, :codes] for b in sides], "tensor", 0)
    recv_recv = diagonal([b[:, codes:both] for b in sides], "tensor")
    send_code = laid([b[:, both : both + codes] for b in sides], "tensor", 0)
    send_recv = diagonal([b[:, both + codes :] for b in sides], "tensor")

    local_fold = dot(proj, enc, ((1,), (1,))).astype(bf16)
    partial = dot(head_rows, local_fold, ((1,), (0,)))
    code_block = scatter_sum([block(partial, "tensor", k, 1) for k in range(parts)], "tensor")
    code_block = code_block.astype(bf16)
    mix_block = code_block.astype(f32)
    for k in range(1, groups):
        other = shift(code_block, "dp", -k).astype(f32)
        mix_block = mix_block + jnp.concatenate([other[-k * tokens :], other[: -k * tokens]])
    mix_code = laid(gathered(mix_block.astype(bf16), "tensor"), "tensor", 1)

    mix_gram = dot(mix_code, gram, ((1,), (0,)))
    mix_recv = dot(mix_code, recv_code, ((1,), (1,)))
    mix_send = dot(mix_code, send_code, ((1,), (1,)))
    mix_square = jnp.sum(mix_gram * mix_code.astype(f32), axis=1, keepdims=True)

    for turn in range(sections):
        if turn > 0:
            received = jnp.where(section == turn, move(sent, "pipe", 1), received)
        recv_square = dot(received, recv_recv, ((1,), (0,)))
        code_mixed = mix_recv + recv_square
        totals = mix_square + jnp.sum(
            received.astype(f32) * (mix_recv + code_mixed), axis=1, keepdims=True
        )
        row_scale = lax.rsqrt(jnp.maximum(totals, 0.0) / width + epsilon)
        unscaled = mix_send + dot(received, send_recv, ((1,), (1,)))
        sent = (row_scale * unscaled).astype(bf16)
    for turn in range(sections):
        if turn > 0:
            incoming = jnp.where(
                section == sections - 1 - turn, move(returned, "pipe", -1), incoming
            )
        inner = row_scale * jnp.sum(incoming.astype(f32) * unscaled, axis=1, keepdims=True) / width
        back = dot(incoming, send_recv, ((1,), (0,)))
        returned = (row_scale * (back - row_scale * inner * code_mixed)).astype(bf16)
    code_mixed = mix_gram + dot(received, recv_code, ((1,), (0,)))
    back = dot(incoming, send_code, ((1,), (0,)))
    code_grad = (row_scale * (back - row_scale * inner * code_mixed)).astype(bf16)

    heads_term = dot(code_grad, local_fold, ((1,), (1,)))
    heads_grad = scatter_sum(
        [heads_term[k * tokens : (k + 1) * tokens] for k in range(groups)], "dp"
    ).astype(bf16)
    head_sum = dot(head_rows, code_grad, ((0,), (0,))).astype(bf16)
    enc_term = dot(head_sum, proj, ((0,), (0,)))
    enc_grad = scatter_sum([block(enc_term, "tensor", k, 0) for k in range(parts)], "tensor")
    proj_grad = dot(head_sum, enc, ((1,), (0,))).astype(bf16)

    received_here = block(received, "tensor", 0, 1)
    incoming_here = block(incoming, "tensor", 0, 1)
    mixed = dot(mix_code, dec, ((1,), (0,))) + dot(received_here, recv, ((1,), (0,)))
    normed = mixed * row_scale
    out_rows = (normed * gain).astype(bf16)
    grad_norm = dot(incoming_here, send, ((1,), (1,)))
    grad_mixed = (row_scale * (grad_norm * gain - normed * inner)).astype(bf16)
    mix_cols = block(mix_code, "dp", 0, 1)
    dec_grad = dot(mix_cols, grad_mixed, ((0,), (0,))).astype(bf16)
    gain_grad = jnp.sum(grad_norm * normed, axis=0)
    send_grad = dot(out_rows, incoming_here, ((0,), (0,))).astype(bf16)
    recv_grad = dot(received_here, grad_mixed, ((0,), (0,))).astype(bf16)
    return (
        block(sent[:tokens], "tensor", 0, 1)[None],
        block(returned[:tokens], "tensor", 0, 1)[None],
        heads_grad[None],
        proj_grad[None],
        enc_grad.astype(bf16)[None],
        dec_grad[None],
        gain_grad[None],
        send_grad[None],
        recv_grad[None],
    )


def solution(mesh):
    return jax.shard_map(
        on_device,
        mesh=mesh,
        in_specs=(
            P("pipe", "dp", "tensor"),
            P("pipe", "tensor", "dp"),
            P("pipe", None, "dp"),
            P("pipe", None, "tensor"),
            P("pipe", "tensor"),
            P("pipe", "tensor", None),
            P("pipe", None, "tensor"),
            P("dp", "tensor"),
            P("dp", "tensor"),
        ),
        out_specs=(
            P("pipe", "dp", "tensor"),
            P("pipe", "dp", "tensor"),
            P("pipe", "dp", "tensor"),
            P("pipe", "tensor", "dp"),
            P("pipe", "tensor", "dp"),
            P("pipe", "dp", "tensor"),
            P("pipe", "tensor"),
            P("pipe", "tensor", None),
            P("pipe", None, "tensor"),
        ),
        check_vma=False,
    )
```

time: 199 us -> 179 us (0.90)
  local copies, waits for them, and re-layouts: 9.59 us -> 33 us
  blocking collectives: 19.1 us -> 0 us
  between operations: 14.6 us -> 1.26 us
  waiting for transfers between devices: 47.2 us -> 41.1 us
  starting transfers between devices: 55 us -> 51.1 us
  other arithmetic: 10.7 us -> 8.19 us
    all_to_all x7 -> x0, waiting for transfers between devices: 27.5 us -> none  [exchanged(): return lax.all_to_all(blocks, axis, 0, 0)]
    all_to_all x7 -> x0, starting transfers between devices: 25.9 us -> none  [exchanged(): return lax.all_to_all(blocks, axis, 0, 0)]
    ppermute x15 -> x33, waiting for transfers between devices: 16.9 us -> 39 us  [shift(): lax.ppermute(shard, axis, [(i, (i + by) % devices) for i in range(devices)])]
    ppermute x15 -> x33, starting transfers between devices: 26.4 us -> 47.4 us  [shift(): lax.ppermute(shard, axis, [(i, (i + by) % devices) for i in range(devices)])]
    all_to_all x2 -> x0, blocking collectives: 19.1 us -> none  [exchanged(): return lax.all_to_all(blocks, axis, 0, 0)]
    dynamic_update_slice x0 -> x22, local copies, waits for them, and re-layouts: none -> 18.8 us  [the longest x17 14 us: laid(): lax.dynamic_update_slice_in_dim(whole, part, place(axis, k) * size, dim)]
    broadcast_in_dim x7 -> x0, local copies, waits for them, and re-layouts: 5.82 us -> none  [the longest x6 4.44 us: spread(): copies = jnp.broadcast_to(shard[None], (lax.axis_size(axis),) + shard.shape)]
    reduce_sum x7 -> x1, other arithmetic: 4.17 us -> 0.27 us  [on_device(): jnp.sum(incoming.astype(f32) * unscaled, axis=1, keepdims=True)]
  transfers between devices with their start and end apart: 25 -> 35, of which waited for: 14 -> 18; matrix products, arithmetic and copies ran while one was open for 25% -> 28% of each run, Pallas kernels for 0% -> 0%
where the time goes in v3:
time: 179 us; the launch traced here: 178 us
  starting transfers between devices  51.1 us (29%)
  matrix products  43.5 us (24%)
  waiting for transfers between devices  41.1 us (23%)
  local copies, waits for them, and re-layouts  33 us (18%)
  other arithmetic  8.19 us (5%)
    ppermute x33, starting transfers between devices, shift(): lax.ppermute(shard, axis, [(i, (i + by) % devices) for i in range(devices)])  47.4 us
    dot_general x26, matrix products, dot(): lax.dot_general(left, right, ((over[0], over[1]), ((), ())), preferred_el...  43.5 us
    ppermute x33, waiting for transfers between devices, shift(): lax.ppermute(shard, axis, [(i, (i + by) % devices) for i in range(devices)])  39 us
    dynamic_update_slice x17, local copies, waits for them, and re-layouts, laid(): lax.dynamic_update_slice_in_dim(whole, part, place(axis, k) * size, dim)  14 us
    dynamic_update_slice x5, local copies, waits for them, and re-layouts, diagonal(): whole = lax.dynamic_update_slice(whole, part, (at * rows, at * cols))  4.81 us
    another operation x8, local copies, waits for them, and re-layouts  4.35 us
    ppermute x2, starting transfers between devices, move(): return lax.ppermute(shard, axis, pairs)  3.71 us
  transfers between devices with their start and end apart: 35, of which 18 were waited for; matrix products, arithmetic and copies ran while one was open for 28% of the time, Pallas kernels for 0%

profile of v3, /device:TPU:0, one launch (start us, length us, event | category | flops | bytes accessed | tf_op | source)
XLA Modules:
  0.0 178.1 jit_solution(5392663338082186993)
XLA Ops:
  0.7 2.0 %fusion.17 = bf16[128,640]{0,1:T(8,128)(2,1)S(1)} fusion(bf16[128,1024]{1,0:T(8,128)(2,1)} %bitcast.82, bf16[512,1024]{1,0:T(8,128)(2,1)} %bitcast.80), kind=kOutput, calls=%fused_computation.34 | convolution fusion | flops 170475520 | bytes 1474560 | tf_op jit(solution)/shard_map/dot_general | solution.py:62
  4.2 3.9 %collective-permute-start.24 = (bf16[128,1280]{0,1:T(8,128)(2,1)}, bf16[128,1280]{0,1:T(8,128)(2,1)}, u32[]{:S(2)}, u32[]{:S(2)}) collective-permute-start(bf16[128,1280]{0,1:T(8,128)(2,1)} %pad_maximum_fusion.4), channel_id=1, source_target_pairs={{0,3},{1,0},{2,1},{3,2},{4,7},{5,4},{6,5},{7,6},{8,11},{9,8},{10,9... | collective-permute-start | bytes 983048 | tf_op jit(solution)/shard_map/ppermute | solution.py:13
  8.8 1.6 collective-permute-start.20
  10.4 2.6 %collective-permute-start.19 = (bf16[128,256]{0,1:T(8,128)(2,1)S(1)}, bf16[128,256]{0,1:T(8,128)(2,1)S(1)}, u32[]{:S(2)}, u32[]{:S(2)}) collective-permute-start(bf16[128,256]{0,1:T(8,128)(2,1)S(1)} %pad_maximum_fusion.8), channel_id=1, source_target_pairs={{0,16},{8,24},{16,0},{24,8},{1,17},{9,25},{17,1},{25,9},{2,18},{10... | collective-permute-start | bytes 196616 | tf_op jit(solution)/shard_map/ppermute | solution.py:13
  14.4 3.4 %fusion.54 = f32[512,512]{1,0:T(8,128)} fusion(bf16[1,512,1024]{2,1,0:T(8,128)(2,1)} %param.12), kind=kOutput, calls=%fused_computation.136 | convolution fusion | flops 536870912 | bytes 2097152 | tf_op jit(solution)/shard_map/dot_general | solution.py:62
  22.3 3.6 %fusion.4 = bf16[1024,512]{1,0:T(8,128)(2,1)} fusion(bf16[1,1024,1024]{2,1,0:T(8,128)(2,1)S(1)} %copy-done, bf16[1,512,1024]{2,1,0:T(8,128)(2,1)} %param.11), kind=kOutput, calls=%fused_computation.10 | convolution fusion | flops 1074266112 | bytes 4194304 | tf_op jit(solution)/shard_map/dot_general | solution.py:62
  26.6 1.5 collective-permute-start.13
  28.1 1.5 collective-permute-start.12
  38.6 4.2 %collective-permute-done.2 = bf16[128,1024]{1,0:T(8,128)(2,1)} collective-permute-done((bf16[128,1024]{1,0:T(8,128)(2,1)}, bf16[128,1024]{1,0:T(8,128)(2,1)}, u32[]{:S(2)}, u32[]{:S(2)}) %collective-permute-start.2) | collective-permute-done | bytes 262176 | tf_op jit(solution)/shard_map/ppermute | solution.py:13
  42.8 1.6 collective-permute-start.26
  44.3 6.3 %collective-permute-done.1 = bf16[128,1024]{1,0:T(8,128)(2,1)} collective-permute-done((bf16[128,1024]{1,0:T(8,128)(2,1)}, bf16[128,1024]{1,0:T(8,128)(2,1)}, u32[]{:S(2)}, u32[]{:S(2)}) %collective-permute-start.1) | collective-permute-done | bytes 262176 | tf_op jit(solution)/shard_map/ppermute | solution.py:13
  53.0 3.3 %fusion.33 = f32[512,512]{0,1:T(8,128)} fusion(bf16[1024,512]{1,0:T(8,128)(2,1)} %fusion.4, bf16[128,1024]{1,0:T(8,128)(2,1)} %collective-permute-done.2, bf16[128,1024]{1,0:T(8,128)(2,1)} %collective-permute-done.1, bf16[128,1024]{1,0:T(8,128)(2,1)} %collective-permute-done, bf16[128,1024]{1,0:T(8,128)(2,1)} %bitcast), kind=kOutput, calls=%fused_computation.75 | convolution fusion | flops 541065216 | bytes 3145728 | tf_op jit(solution)/shard_map/dot_general | solution.py:62
  57.0 1.7 collective-permute-start.17
  68.3 1.8 %collective-permute-start.23 = (bf16[512,256]{0,1:T(8,128)(2,1)S(1)}, bf16[512,256]{0,1:T(8,128)(2,1)S(1)}, u32[]{:S(2)}, u32[]{:S(2)}) collective-permute-start(bf16[512,256]{0,1:T(8,128)(2,1)S(1)} %pad_maximum_fusion.5), channel_id=1, source_target_pairs={{0,1},{1,2},{2,3},{3,0},{4,5},{5,6},{6,7},{7,4},{8,9},{9,10},{10,1... | collective-permute-start | bytes 786440 | tf_op jit(solution)/shard_map/ppermute | solution.py:13
  70.1 1.7 slice_dynamic-update-slice_fusion.2
  71.8 4.6 %collective-permute-done.22 = bf16[512,256]{0,1:T(8,128)(2,1)} collective-permute-done((bf16[512,256]{0,1:T(8,128)(2,1)S(1)}, bf16[512,256]{0,1:T(8,128)(2,1)}, u32[]{:S(2)}, u32[]{:S(2)}) %collective-permute-start.22) | collective-permute-done | bytes 262176 | tf_op jit(solution)/shard_map/ppermute | solution.py:13
  76.4 1.7 slice_dynamic-update-slice_fusion.1
  80.8 1.7 slice_dynamic-update-slice_fusion.10
  82.5 1.7 slice_dynamic-update-slice_fusion.9
  84.2 1.7 slice_dynamic-update-slice_fusion.8
  88.3 4.7 %collective-permute-start.8 = (bf16[512,128]{0,1:T(8,128)(2,1)S(1)}, bf16[512,128]{0,1:T(8,128)(2,1)S(1)}, u32[]{:S(2)}, u32[]{:S(2)}) collective-permute-start(bf16[512,128]{0,1:T(8,128)(2,1)S(1)} %add_convert_fusion.2), channel_id=1, source_target_pairs={{0,8},{8,16},{16,24},{24,0},{1,9},{9,17},{17,25},{25,1},{2,10},{10... | collective-permute-start | bytes 393224 | tf_op jit(solution)/shard_map/ppermute | solution.py:13
  93.1 1.5 collective-permute-start.7
  94.6 2.8 %collective-permute-start.6 = (bf16[512,128]{0,1:T(8,128)(2,1)S(1)}, bf16[512,128]{0,1:T(8,128)(2,1)S(1)}, u32[]{:S(2)}, u32[]{:S(2)}) collective-permute-start(bf16[512,128]{0,1:T(8,128)(2,1)S(1)} %add_convert_fusion.2), channel_id=1, source_target_pairs={{0,24},{8,0},{16,8},{24,16},{1,25},{9,1},{17,9},{25,17},{2,26},{10... | collective-permute-start | bytes 393224 | tf_op jit(solution)/shard_map/ppermute | solution.py:13
  97.4 1.4 slice_dynamic-update-slice_fusion.21
  100.1 2.1 %collective-permute-done.7 = bf16[512,128]{0,1:T(8,128)(2,1)S(1)} collective-permute-done((bf16[512,128]{0,1:T(8,128)(2,1)S(1)}, bf16[512,128]{0,1:T(8,128)(2,1)S(1)}, u32[]{:S(2)}, u32[]{:S(2)}) %collective-permute-start.7) | collective-permute-done | bytes 131104 | tf_op jit(solution)/shard_map/ppermute | solution.py:13
  102.3 2.0 %collective-permute-start.9 = (bf16[512,128]{0,1:T(8,128)(2,1)S(1)}, bf16[512,128]{0,1:T(8,128)(2,1)S(1)}, u32[]{:S(2)}, u32[]{:S(2)}) collective-permute-start(bf16[512,128]{0,1:T(8,128)(2,1)S(1)} %get-tuple-element.14), channel_id=1, source_target_pairs={{0,3},{1,0},{2,1},{3,2},{4,7},{5,4},{6,5},{7,6},{8,11},{9,8},{10,9... | collective-permute-start | bytes 393224 | tf_op jit(solution)/shard_map/ppermute | solution.py:13
  107.9 2.8 %collective-permute-done.10 = bf16[512,128]{0,1:T(8,128)(2,1)S(1)} collective-permute-done((bf16[512,128]{0,1:T(8,128)(2,1)S(1)}, bf16[512,128]{0,1:T(8,128)(2,1)S(1)}, u32[]{:S(2)}, u32[]{:S(2)}) %collective-permute-start.10) | collective-permute-done | bytes 131104 | tf_op jit(solution)/shard_map/ppermute | solution.py:13
  110.7 1.9 %collective-permute-done.11 = bf16[512,128]{0,1:T(8,128)(2,1)S(1)} collective-permute-done((bf16[512,128]{0,1:T(8,128)(2,1)S(1)}, bf16[512,128]{0,1:T(8,128)(2,1)S(1)}, u32[]{:S(2)}, u32[]{:S(2)}) %collective-permute-start.11) | collective-permute-done | bytes 131104 | tf_op jit(solution)/shard_map/ppermute | solution.py:13
  112.6 1.5 fusion.62
  114.2 2.9 %multiply_reduce_fusion.5 = (f32[512]{0:T(512)S(1)}, f32[512,512]{0,1:T(8,128)}) fusion(bf16[512,512]{0,1:T(8,128)(2,1)S(1)} %constant_dynamic-update-slice_fusion.4, bf16[512,512]{0,1:T(8,128)(2,1)} %constant_dynamic-update-slice_fusion), kind=kOutput, calls=%fused_computation.43 | convolution fusion | flops 269221376 | bytes 2099200 | tf_op jit(solution)/shard_map/dot_general | solution.py:62
  117.0 1.5 fusion.61
  119.5 1.8 %multiply_reduce_fusion.4 = f32[512]{0:T(512)S(1)} fusion(bf16[512,512]{0,1:T(8,128)(2,1)} %get-tuple-element.42, f32[512,512]{0,1:T(8,128)S(1)} %fusion.61, bf16[512,512]{0,1:T(8,128)(2,1)} %get-tuple-element.29), kind=kOutput, calls=%fused_computation.42 | convolution fusion | flops 269745664 | bytes 2099200 | tf_op jit(solution)/shard_map/dot_general | solution.py:62
  121.4 2.3 %fusion.11 = bf16[512,512]{0,1:T(8,128)(2,1)} fusion(f32[512,512]{0,1:T(8,128)S(1)} %fusion.62, bf16[512,512]{0,1:T(8,128)(2,1)} %get-tuple-element.42, bf16[512,512]{0,1:T(8,128)(2,1)S(1)} %get-tuple-element.30, f32[512]{0:T(512)S(1)} %add_rsqrt_fusion.1), kind=kOutput, calls=%fused_computation.23 | convolution fusion | flops 269221888 | bytes 2623488 | tf_op jit(solution)/shard_map/dot_general | solution.py:62
  123.7 2.1 %collective-permute-start.27 = (bf16[512,512]{0,1:T(8,128)(2,1)}, bf16[512,512]{0,1:T(8,128)(2,1)}, u32[]{:S(2)}, u32[]{:S(2)}) collective-permute-start(bf16[512,512]{0,1:T(8,128)(2,1)} %fusion.11), channel_id=1, source_target_pairs={{0,4},{1,5},{2,6},{3,7},{8,12},{9,13},{10,14},{11,15},{16,20},{17,... | collective-permute-start | bytes 1572872 | tf_op jit(solution)/shard_map/ppermute | solution.py:19
  128.0 1.9 %multiply_reduce_fusion.3 = (f32[512]{0:T(512)S(1)}, f32[512,512]{0,1:T(8,128)S(1)}) fusion(f32[512,512]{0,1:T(8,128)} %copy-done.7, bf16[512,512]{0,1:T(8,128)(2,1)S(1)} %broadcast_select_fusion.1, bf16[512,512]{0,1:T(8,128)(2,1)} %get-tuple-element.29), kind=kOutput, calls=%fused_computation.41 | convolution fusion | flops 269745664 | bytes 3147776 | tf_op jit(solution)/shard_map/dot_general | solution.py:62
  130.9 1.6 collective-permute-start.28
  135.6 1.8 %fusion.7 = f32[512,512]{0,1:T(8,128)S(1)} fusion(f32[512,512]{0,1:T(8,128)S(1)} %copy-done.6, bf16[512,512]{0,1:T(8,128)(2,1)} %get-tuple-element.35, bf16[512,512]{0,1:T(8,128)(2,1)S(1)} %broadcast_select_fusion.1, f32[512]{0:T(512)S(1)} %get-tuple-element.50), kind=kOutput, calls=%fused_computation.13 | convolution fusion | flops 268959744 | bytes 3147776 | tf_op jit(solution)/shard_map/dot_general | solution.py:62
  137.5 1.6 fusion.13
  139.1 2.1 %fusion.60 = (bf16[512,1024]{1,0:T(8,128)(2,1)S(1)}, f32[512,1024]{1,0:T(8,128)}) fusion(bf16[512,512]{0,1:T(8,128)(2,1)S(1)} %fusion.13, bf16[1024,512]{1,0:T(8,128)(2,1)S(1)} %copy-done.11), kind=kOutput, calls=%fused_computation.141 | convolution fusion | flops 537395200 | bytes 4718592 | tf_op jit(solution)/shard_map/dot_general | solution.py:62
  141.2 2.0 %convolution_convert_fusion = bf16[1024,512]{1,0:T(8,128)(2,1)S(1)} fusion(bf16[512,512]{0,1:T(8,128)(2,1)S(1)} %fusion.13, bf16[128,1024]{1,0:T(8,128)(2,1)} %collective-permute-done.2, bf16[128,1024]{1,0:T(8,128)(2,1)} %collective-permute-done.1, bf16[128,1024]{1,0:T(8,128)(2,1)} %collective-permute-done, bf16[128,1024]{1,0:T(8,128)(2,1)} %bitcast), kind=kOutput, calls=%fused_computation.11 | convolution fusion | flops 541589504 | bytes 2621440 | tf_op jit(solution)/shard_map/dot_general | solution.py:62
  143.2 2.6 %convert_bitcast_fusion = bf16[1,1024,1024]{2,1,0:T(8,128)(2,1)} fusion(bf16[1024,512]{1,0:T(8,128)(2,1)S(1)} %convolution_convert_fusion, bf16[1,512,1024]{2,1,0:T(8,128)(2,1)S(1)} %copy-done.20), kind=kOutput, calls=%fused_computation.8 | convolution fusion | flops 1074790400 | bytes 4194304 | tf_op jit(solution)/shard_map/dot_general | solution.py:62
  148.1 4.0 %collective-permute-start.31 = (bf16[128,1024]{1,0:T(8,128)(2,1)}, bf16[128,1024]{1,0:T(8,128)(2,1)}, u32[]{:S(2)}, u32[]{:S(2)}) collective-permute-start(bf16[128,1024]{1,0:T(8,128)(2,1)} %get-tuple-element.21), channel_id=1, source_target_pairs={{0,24},{8,0},{16,8},{24,16},{1,25},{9,1},{17,9},{25,17},{2,26},{10... | collective-permute-start | bytes 786440 | tf_op jit(solution)/shard_map/ppermute | solution.py:13
  153.4 1.9 %collective-permute-start.32 = (bf16[128,1024]{1,0:T(8,128)(2,1)S(1)}, bf16[128,1024]{1,0:T(8,128)(2,1)}, u32[]{:S(2)}, u32[]{:S(2)}) collective-permute-start(bf16[128,1024]{1,0:T(8,128)(2,1)S(1)} %get-tuple-element.17), channel_id=1, source_target_pairs={{0,1},{1,2},{2,3},{3,0},{4,5},{5,6},{6,7},{7,4},{8,9},{9,10},{10,1... | collective-permute-start | bytes 786440 | tf_op jit(solution)/shard_map/ppermute | solution.py:13
  159.0 2.9 %collective-permute-done.34 = bf16[128,1024]{1,0:T(8,128)(2,1)S(1)} collective-permute-done((bf16[128,1024]{1,0:T(8,128)(2,1)S(1)}, bf16[128,1024]{1,0:T(8,128)(2,1)S(1)}, u32[]{:S(2)}, u32[]{:S(2)}) %collective-permute-start.34) | collective-permute-done | bytes 262176 | tf_op jit(solution)/shard_map/ppermute | solution.py:13
  164.4 2.0 %collective-permute-done.32 = bf16[128,1024]{1,0:T(8,128)(2,1)} collective-permute-done((bf16[128,1024]{1,0:T(8,128)(2,1)S(1)}, bf16[128,1024]{1,0:T(8,128)(2,1)}, u32[]{:S(2)}, u32[]{:S(2)}) %collective-permute-start.32) | collective-permute-done | bytes 262176 | tf_op jit(solution)/shard_map/ppermute | solution.py:13
  166.4 2.1 %fusion.24 = bf16[1,128,1024]{2,1,0:T(8,128)(2,1)} fusion(bf16[128,1024]{1,0:T(8,128)(2,1)} %copy-done.13, bf16[128,1024]{1,0:T(8,128)(2,1)} %collective-permute-done.33, bf16[128,1024]{1,0:T(8,128)(2,1)} %collective-permute-done.32, f32[512,1024]{1,0:T(8,128)} %copy-done.5, s32[]{:T(128)S(6)} %select_n.22), kind=kLoop, calls=%fused_computation.56 | loop fusion | flops 917504 | bytes 1572868 | tf_op jit(solution)/shard_map/broadcast_in_dim | solution.py:181
  168.5 7.6 %collective-permute-done.30 = bf16[128,1024]{1,0:T(8,128)(2,1)} collective-permute-done((bf16[128,1024]{1,0:T(8,128)(2,1)}, bf16[128,1024]{1,0:T(8,128)(2,1)}, u32[]{:S(2)}, u32[]{:S(2)}) %collective-permute-start.30) | collective-permute-done | bytes 262176 | tf_op jit(solution)/shard_map/ppermute | solution.py:13
  176.1 2.1 %fusion.25 = bf16[1,128,1024]{2,1,0:T(8,128)(2,1)} fusion(bf16[128,1024]{1,0:T(8,128)(2,1)} %collective-permute-done.31, bf16[128,1024]{1,0:T(8,128)(2,1)} %collective-permute-done.30, bf16[128,1024]{1,0:T(8,128)(2,1)S(1)} %collective-permute-done.29, f32[512,1024]{1,0:T(8,128)} %get-tuple-element.60), kind=kLoop, calls=%fused_computation.57 | loop fusion | flops 917504 | bytes 1572864 | tf_op jit(solution)/shard_map/broadcast_in_dim | solution.py:179
  (161 shorter events, 57.2 us)
Async XLA Ops:
  0.6 21.7 %copy-start = (bf16[1,1024,1024]{2,1,0:T(8,128)(2,1)S(1)}, bf16[1,1024,1024]{2,1,0:T(8,128)(2,1)}, u32[]{:S(2)}) copy-start(bf16[1,1024,1024]{2,1,0:T(8,128)(2,1)} %param.10) | copy-start | bytes 6291460
  2.7 5.9 %copy-start.17 = (bf16[128,128]{1,0:T(8,128)(2,1)S(1)}, bf16[128,128]{1,0:T(8,128)(2,1)}, u32[]{:S(2)}) copy-start(bf16[128,128]{1,0:T(8,128)(2,1)} %param.17) | copy-start | bytes 98308
  2.7 6.0 %copy-start.18 = (bf16[128,128]{1,0:T(8,128)(2,1)S(1)}, bf16[128,128]{1,0:T(8,128)(2,1)}, u32[]{:S(2)}) copy-start(bf16[128,128]{1,0:T(8,128)(2,1)} %param.16) | copy-start | bytes 98308
  4.2 75.3 %collective-permute-start.24 = (bf16[128,1280]{0,1:T(8,128)(2,1)}, bf16[128,1280]{0,1:T(8,128)(2,1)}, u32[]{:S(2)}, u32[]{:S(2)}) collective-permute-start(bf16[128,1280]{0,1:T(8,128)(2,1)} %pad_maximum_fusion.4), channel_id=1, source_target_pairs={{0,3},{1,0},{2,1},{3,2},{4,7},{5,4},{6,5},{7,6},{8,11},{9,8},{10,9... | collective-permute-start | bytes 983048 | tf_op jit(solution)/shard_map/ppermute | solution.py:13
  8.1 74.4 %collective-permute-start.25 = (bf16[128,1280]{0,1:T(8,128)(2,1)}, bf16[128,1280]{0,1:T(8,128)(2,1)}, u32[]{:S(2)}, u32[]{:S(2)}) collective-permute-start(bf16[128,1280]{0,1:T(8,128)(2,1)} %pad_maximum_fusion.4), channel_id=1, source_target_pairs={{0,2},{1,3},{2,0},{3,1},{4,6},{5,7},{6,4},{7,5},{8,10},{9,11},{10,... | collective-permute-start | bytes 983048 | tf_op jit(solution)/shard_map/ppermute | solution.py:13
  8.8 17.1 %collective-permute-start.20 = (bf16[128,256]{0,1:T(8,128)(2,1)S(1)}, bf16[128,256]{0,1:T(8,128)(2,1)S(1)}, u32[]{:S(2)}, u32[]{:S(2)}) collective-permute-start(bf16[128,256]{0,1:T(8,128)(2,1)S(1)} %pad_maximum_fusion.8), channel_id=1, source_target_pairs={{0,8},{8,16},{16,24},{24,0},{1,9},{9,17},{17,25},{25,1},{2,10},{10... | collective-permute-start | bytes 196616 | tf_op jit(solution)/shard_map/ppermute | solution.py:13
  10.4 16.1 %collective-permute-start.19 = (bf16[128,256]{0,1:T(8,128)(2,1)S(1)}, bf16[128,256]{0,1:T(8,128)(2,1)S(1)}, u32[]{:S(2)}, u32[]{:S(2)}) collective-permute-start(bf16[128,256]{0,1:T(8,128)(2,1)S(1)} %pad_maximum_fusion.8), channel_id=1, source_target_pairs={{0,16},{8,24},{16,0},{24,8},{1,17},{9,25},{17,1},{25,9},{2,18},{10... | collective-permute-start | bytes 196616 | tf_op jit(solution)/shard_map/ppermute | solution.py:13
  13.0 15.0 %collective-permute-start.18 = (bf16[128,256]{0,1:T(8,128)(2,1)S(1)}, bf16[128,256]{0,1:T(8,128)(2,1)S(1)}, u32[]{:S(2)}, u32[]{:S(2)}) collective-permute-start(bf16[128,256]{0,1:T(8,128)(2,1)S(1)} %pad_maximum_fusion.8), channel_id=1, source_target_pairs={{0,24},{8,0},{16,8},{24,16},{1,25},{9,1},{17,9},{25,17},{2,26},{10... | collective-permute-start | bytes 196616 | tf_op jit(solution)/shard_map/ppermute | solution.py:13
  22.3 3.6 %copy-start.12 = (f32[512,512]{1,0:T(8,128)S(1)}, f32[512,512]{1,0:T(8,128)}, u32[]{:S(2)}) copy-start(f32[512,512]{1,0:T(8,128)} %fusion.54) | copy-start | bytes 3145732
  26.0 5.4 %collective-permute-start.14 = (bf16[128,512]{1,0:T(8,128)(2,1)S(1)}, bf16[128,512]{1,0:T(8,128)(2,1)S(1)}, u32[]{:S(2)}, u32[]{:S(2)}) collective-permute-start(bf16[128,512]{1,0:T(8,128)(2,1)S(1)} %get-tuple-element.24), channel_id=1, source_target_pairs={{0,3},{1,0},{2,1},{3,2},{4,7},{5,4},{6,5},{7,6},{8,11},{9,8},{10,9... | collective-permute-start | bytes 393224 | tf_op jit(solution)/shard_map/ppermute | solution.py:13
  26.6 5.7 %collective-permute-start.13 = (bf16[128,512]{1,0:T(8,128)(2,1)S(1)}, bf16[128,512]{1,0:T(8,128)(2,1)S(1)}, u32[]{:S(2)}, u32[]{:S(2)}) collective-permute-start(bf16[128,512]{1,0:T(8,128)(2,1)S(1)} %get-tuple-element.25), channel_id=1, source_target_pairs={{0,2},{1,3},{2,0},{3,1},{4,6},{5,7},{6,4},{7,5},{8,10},{9,11},{10,... | collective-permute-start | bytes 393224 | tf_op jit(solution)/shard_map/ppermute | solution.py:13
  28.1 5.9 %collective-permute-start.12 = (bf16[128,512]{1,0:T(8,128)(2,1)S(1)}, bf16[128,512]{1,0:T(8,128)(2,1)S(1)}, u32[]{:S(2)}, u32[]{:S(2)}) collective-permute-start(bf16[128,512]{1,0:T(8,128)(2,1)S(1)} %get-tuple-element.23), channel_id=1, source_target_pairs={{0,1},{1,2},{2,3},{3,0},{4,5},{5,6},{6,7},{7,4},{8,9},{9,10},{10,1... | collective-permute-start | bytes 393224 | tf_op jit(solution)/shard_map/ppermute | solution.py:13
  31.4 11.4 %collective-permute-start.2 = (bf16[128,1024]{1,0:T(8,128)(2,1)}, bf16[128,1024]{1,0:T(8,128)(2,1)}, u32[]{:S(2)}, u32[]{:S(2)}) collective-permute-start(bf16[128,1024]{1,0:T(8,128)(2,1)} %bitcast), channel_id=1, source_target_pairs={{0,8},{8,16},{16,24},{24,0},{1,9},{9,17},{17,25},{25,1},{2,10},{10... | collective-permute-start | bytes 786440 | tf_op jit(solution)/shard_map/ppermute | solution.py:13
  32.2 18.3 %collective-permute-start.1 = (bf16[128,1024]{1,0:T(8,128)(2,1)}, bf16[128,1024]{1,0:T(8,128)(2,1)}, u32[]{:S(2)}, u32[]{:S(2)}) collective-permute-start(bf16[128,1024]{1,0:T(8,128)(2,1)} %bitcast), channel_id=1, source_target_pairs={{0,16},{8,24},{16,0},{24,8},{1,17},{9,25},{17,1},{25,9},{2,18},{10... | collective-permute-start | bytes 786440 | tf_op jit(solution)/shard_map/ppermute | solution.py:13
  33.9 18.0 %collective-permute-start = (bf16[128,1024]{1,0:T(8,128)(2,1)}, bf16[128,1024]{1,0:T(8,128)(2,1)}, u32[]{:S(2)}, u32[]{:S(2)}) collective-permute-start(bf16[128,1024]{1,0:T(8,128)(2,1)} %bitcast), channel_id=1, source_target_pairs={{0,24},{8,0},{16,8},{24,16},{1,25},{9,1},{17,9},{25,17},{2,26},{10... | collective-permute-start | bytes 786440 | tf_op jit(solution)/shard_map/ppermute | solution.py:13
  42.8 41.4 %collective-permute-start.26 = (bf16[128,1280]{0,1:T(8,128)(2,1)}, bf16[128,1280]{0,1:T(8,128)(2,1)}, u32[]{:S(2)}, u32[]{:S(2)}) collective-permute-start(bf16[128,1280]{0,1:T(8,128)(2,1)} %pad_maximum_fusion.4), channel_id=1, source_target_pairs={{0,1},{1,2},{2,3},{3,0},{4,5},{5,6},{6,7},{7,4},{8,9},{9,10},{10,1... | collective-permute-start | bytes 983048 | tf_op jit(solution)/shard_map/ppermute | solution.py:13
  50.6 5.8 %collective-permute-start.15 = (bf16[128,512]{1,0:T(8,128)(2,1)}, bf16[128,512]{1,0:T(8,128)(2,1)S(1)}, u32[]{:S(2)}, u32[]{:S(2)}) collective-permute-start(bf16[128,512]{1,0:T(8,128)(2,1)} %add_convert_fusion.1), channel_id=1, source_target_pairs={{0,3},{1,0},{2,1},{3,2},{4,7},{5,4},{6,5},{7,6},{8,11},{9,8},{10,9... | collective-permute-start | bytes 393224 | tf_op jit(solution)/shard_map/ppermute | solution.py:13
  51.9 8.6 %collective-permute-start.16 = (bf16[128,512]{1,0:T(8,128)(2,1)}, bf16[128,512]{1,0:T(8,128)(2,1)}, u32[]{:S(2)}, u32[]{:S(2)}) collective-permute-start(bf16[128,512]{1,0:T(8,128)(2,1)} %add_convert_fusion.1), channel_id=1, source_target_pairs={{0,2},{1,3},{2,0},{3,1},{4,6},{5,7},{6,4},{7,5},{8,10},{9,11},{10,... | collective-permute-start | bytes 393224 | tf_op jit(solution)/shard_map/ppermute | solution.py:13
  57.0 7.1 %collective-permute-start.17 = (bf16[128,512]{1,0:T(8,128)(2,1)}, bf16[128,512]{1,0:T(8,128)(2,1)}, u32[]{:S(2)}, u32[]{:S(2)}) collective-permute-start(bf16[128,512]{1,0:T(8,128)(2,1)} %add_convert_fusion.1), channel_id=1, source_target_pairs={{0,1},{1,2},{2,3},{3,0},{4,5},{5,6},{6,7},{7,4},{8,9},{9,10},{10,1... | collective-permute-start | bytes 393224 | tf_op jit(solution)/shard_map/ppermute | solution.py:13
  60.5 7.8 %collective-permute-start.21 = (bf16[512,256]{0,1:T(8,128)(2,1)S(1)}, bf16[512,256]{0,1:T(8,128)(2,1)}, u32[]{:S(2)}, u32[]{:S(2)}) collective-permute-start(bf16[512,256]{0,1:T(8,128)(2,1)S(1)} %pad_maximum_fusion.5), channel_id=1, source_target_pairs={{0,3},{1,0},{2,1},{3,2},{4,7},{5,4},{6,5},{7,6},{8,11},{9,8},{10,9... | collective-permute-start | bytes 786440 | tf_op jit(solution)/shard_map/ppermute | solution.py:13
  64.2 12.3 %collective-permute-start.22 = (bf16[512,256]{0,1:T(8,128)(2,1)S(1)}, bf16[512,256]{0,1:T(8,128)(2,1)}, u32[]{:S(2)}, u32[]{:S(2)}) collective-permute-start(bf16[512,256]{0,1:T(8,128)(2,1)S(1)} %pad_maximum_fusion.5), channel_id=1, source_target_pairs={{0,2},{1,3},{2,0},{3,1},{4,6},{5,7},{6,4},{7,5},{8,10},{9,11},{10,... | collective-permute-start | bytes 786440 | tf_op jit(solution)/shard_map/ppermute | solution.py:13
  68.3 9.8 %collective-permute-start.23 = (bf16[512,256]{0,1:T(8,128)(2,1)S(1)}, bf16[512,256]{0,1:T(8,128)(2,1)S(1)}, u32[]{:S(2)}, u32[]{:S(2)}) collective-permute-start(bf16[512,256]{0,1:T(8,128)(2,1)S(1)} %pad_maximum_fusion.5), channel_id=1, source_target_pairs={{0,1},{1,2},{2,3},{3,0},{4,5},{5,6},{6,7},{7,4},{8,9},{9,10},{10,1... | collective-permute-start | bytes 786440 | tf_op jit(solution)/shard_map/ppermute | solution.py:13
  76.4 10.9 %collective-permute-start.5 = (bf16[512,128]{0,1:T(8,128)(2,1)S(1)}, bf16[512,128]{0,1:T(8,128)(2,1)S(1)}, u32[]{:S(2)}, u32[]{:S(2)}) collective-permute-start(bf16[512,128]{0,1:T(8,128)(2,1)S(1)} %get-tuple-element.27), channel_id=1, source_target_pairs={{0,3},{1,0},{2,1},{3,2},{4,7},{5,4},{6,5},{7,6},{8,11},{9,8},{10,9... | collective-permute-start | bytes 393224 | tf_op jit(solution)/shard_map/ppermute | solution.py:13
  78.1 9.2 %collective-permute-start.4 = (bf16[512,128]{0,1:T(8,128)(2,1)S(1)}, bf16[512,128]{0,1:T(8,128)(2,1)S(1)}, u32[]{:S(2)}, u32[]{:S(2)}) collective-permute-start(bf16[512,128]{0,1:T(8,128)(2,1)S(1)} %get-tuple-element.28), channel_id=1, source_target_pairs={{0,2},{1,3},{2,0},{3,1},{4,6},{5,7},{6,4},{7,5},{8,10},{9,11},{10,... | collective-permute-start | bytes 393224 | tf_op jit(solution)/shard_map/ppermute | solution.py:13
  79.4 22.7 %copy-start.3 = (bf16[512,512]{0,1:T(8,128)(2,1)}, bf16[512,512]{0,1:T(8,128)(2,1)S(1)}, u32[]{:S(2)}) copy-start(bf16[512,512]{0,1:T(8,128)(2,1)S(1)} %get-tuple-element.41) | copy-start | bytes 1572868
  79.4 7.9 %collective-permute-start.3 = (bf16[512,128]{0,1:T(8,128)(2,1)S(1)}, bf16[512,128]{0,1:T(8,128)(2,1)S(1)}, u32[]{:S(2)}, u32[]{:S(2)}) collective-permute-start(bf16[512,128]{0,1:T(8,128)(2,1)S(1)} %get-tuple-element.26), channel_id=1, source_target_pairs={{0,1},{1,2},{2,3},{3,0},{4,5},{5,6},{6,7},{7,4},{8,9},{9,10},{10,1... | collective-permute-start | bytes 393224 | tf_op jit(solution)/shard_map/ppermute | solution.py:13
  88.3 10.5 %collective-permute-start.8 = (bf16[512,128]{0,1:T(8,128)(2,1)S(1)}, bf16[512,128]{0,1:T(8,128)(2,1)S(1)}, u32[]{:S(2)}, u32[]{:S(2)}) collective-permute-start(bf16[512,128]{0,1:T(8,128)(2,1)S(1)} %add_convert_fusion.2), channel_id=1, source_target_pairs={{0,8},{8,16},{16,24},{24,0},{1,9},{9,17},{17,25},{25,1},{2,10},{10... | collective-permute-start | bytes 393224 | tf_op jit(solution)/shard_map/ppermute | solution.py:13
  93.1 9.1 %collective-permute-start.7 = (bf16[512,128]{0,1:T(8,128)(2,1)S(1)}, bf16[512,128]{0,1:T(8,128)(2,1)S(1)}, u32[]{:S(2)}, u32[]{:S(2)}) collective-permute-start(bf16[512,128]{0,1:T(8,128)(2,1)S(1)} %add_convert_fusion.2), channel_id=1, source_target_pairs={{0,16},{8,24},{16,0},{24,8},{1,17},{9,25},{17,1},{25,9},{2,18},{10... | collective-permute-start | bytes 393224 | tf_op jit(solution)/shard_map/ppermute | solution.py:13
  94.6 5.5 %collective-permute-start.6 = (bf16[512,128]{0,1:T(8,128)(2,1)S(1)}, bf16[512,128]{0,1:T(8,128)(2,1)S(1)}, u32[]{:S(2)}, u32[]{:S(2)}) collective-permute-start(bf16[512,128]{0,1:T(8,128)(2,1)S(1)} %add_convert_fusion.2), channel_id=1, source_target_pairs={{0,24},{8,0},{16,8},{24,16},{1,25},{9,1},{17,9},{25,17},{2,26},{10... | collective-permute-start | bytes 393224 | tf_op jit(solution)/shard_map/ppermute | solution.py:13
  102.3 5.6 %collective-permute-start.9 = (bf16[512,128]{0,1:T(8,128)(2,1)S(1)}, bf16[512,128]{0,1:T(8,128)(2,1)S(1)}, u32[]{:S(2)}, u32[]{:S(2)}) collective-permute-start(bf16[512,128]{0,1:T(8,128)(2,1)S(1)} %get-tuple-element.14), channel_id=1, source_target_pairs={{0,3},{1,0},{2,1},{3,2},{4,7},{5,4},{6,5},{7,6},{8,11},{9,8},{10,9... | collective-permute-start | bytes 393224 | tf_op jit(solution)/shard_map/ppermute | solution.py:13
  104.3 6.4 %collective-permute-start.10 = (bf16[512,128]{0,1:T(8,128)(2,1)S(1)}, bf16[512,128]{0,1:T(8,128)(2,1)S(1)}, u32[]{:S(2)}, u32[]{:S(2)}) collective-permute-start(bf16[512,128]{0,1:T(8,128)(2,1)S(1)} %get-tuple-element.14), channel_id=1, source_target_pairs={{0,2},{1,3},{2,0},{3,1},{4,6},{5,7},{6,4},{7,5},{8,10},{9,11},{10,... | collective-permute-start | bytes 393224 | tf_op jit(solution)/shard_map/ppermute | solution.py:13
  106.7 5.9 %collective-permute-start.11 = (bf16[512,128]{0,1:T(8,128)(2,1)S(1)}, bf16[512,128]{0,1:T(8,128)(2,1)S(1)}, u32[]{:S(2)}, u32[]{:S(2)}) collective-permute-start(bf16[512,128]{0,1:T(8,128)(2,1)S(1)} %get-tuple-element.14), channel_id=1, source_target_pairs={{0,1},{1,2},{2,3},{3,0},{4,5},{5,6},{6,7},{7,4},{8,9},{9,10},{10,1... | collective-permute-start | bytes 393224 | tf_op jit(solution)/shard_map/ppermute | solution.py:13
  114.2 7.3 %copy-start.1 = (f32[512,512]{0,1:T(8,128)}, f32[512,512]{0,1:T(8,128)S(1)}, u32[]{:S(2)}) copy-start(f32[512,512]{0,1:T(8,128)S(1)} %fusion.62) | copy-start | bytes 3145732
  123.7 3.1 %collective-permute-start.27 = (bf16[512,512]{0,1:T(8,128)(2,1)}, bf16[512,512]{0,1:T(8,128)(2,1)}, u32[]{:S(2)}, u32[]{:S(2)}) collective-permute-start(bf16[512,512]{0,1:T(8,128)(2,1)} %fusion.11), channel_id=1, source_target_pairs={{0,4},{1,5},{2,6},{3,7},{8,12},{9,13},{10,14},{11,15},{16,20},{17,... | collective-permute-start | bytes 1572872 | tf_op jit(solution)/shard_map/ppermute | solution.py:19
  125.8 4.0 %copy-start.2 = (f32[512,512]{0,1:T(8,128)S(1)}, f32[512,512]{0,1:T(8,128)}, u32[]{:S(2)}) copy-start(f32[512,512]{0,1:T(8,128)} %copy-done.1) | copy-start | bytes 3145732
  125.8 4.0 %copy-start.4 = (bf16[512,512]{0,1:T(8,128)(2,1)S(1)}, bf16[512,512]{0,1:T(8,128)(2,1)}, u32[]{:S(2)}) copy-start(bf16[512,512]{0,1:T(8,128)(2,1)} %copy-done.3) | copy-start | bytes 1572868
  130.4 2.2 %copy-start.15 = (bf16[1,128,1024]{2,1,0:T(8,128)(2,1)S(1)}, bf16[1,128,1024]{2,1,0:T(8,128)(2,1)}, u32[]{:S(2)}) copy-start(bf16[1,128,1024]{2,1,0:T(8,128)(2,1)} %param.15) | copy-start | bytes 786436
  130.9 3.9 %collective-permute-start.28 = (bf16[512,512]{0,1:T(8,128)(2,1)S(1)}, bf16[512,512]{0,1:T(8,128)(2,1)S(1)}, u32[]{:S(2)}, u32[]{:S(2)}) collective-permute-start(bf16[512,512]{0,1:T(8,128)(2,1)S(1)} %fusion.12), channel_id=1, source_target_pairs={{4,0},{5,1},{6,2},{7,3},{12,8},{13,9},{14,10},{15,11},{20,16},{21,... | collective-permute-start | bytes 1572872 | tf_op jit(solution)/shard_map/ppermute | solution.py:19
  135.6 11.5 %copy-start.8 = (f32[512,512]{0,1:T(8,128)}, f32[512,512]{0,1:T(8,128)S(1)}, u32[]{:S(2)}) copy-start(f32[512,512]{0,1:T(8,128)S(1)} %fusion.63) | copy-start | bytes 3145732
  147.1 5.3 %copy-start.5 = (f32[512,1024]{1,0:T(8,128)}, f32[512,1024]{1,0:T(8,128)S(1)}, u32[]{:S(2)}) copy-start(f32[512,1024]{1,0:T(8,128)S(1)} %fusion) | copy-start | bytes 6291460
  147.2 8.2 %copy-start.22 = (bf16[1,1024,128]{2,1,0:T(8,128)(2,1)S(1)}, bf16[1,1024,128]{2,1,0:T(8,128)(2,1)}, u32[]{:S(2)}) copy-start(bf16[1,1024,128]{2,1,0:T(8,128)(2,1)} %param.14) | copy-start | bytes 786436
  148.1 20.4 %collective-permute-start.31 = (bf16[128,1024]{1,0:T(8,128)(2,1)}, bf16[128,1024]{1,0:T(8,128)(2,1)}, u32[]{:S(2)}, u32[]{:S(2)}) collective-permute-start(bf16[128,1024]{1,0:T(8,128)(2,1)} %get-tuple-element.21), channel_id=1, source_target_pairs={{0,24},{8,0},{16,8},{24,16},{1,25},{9,1},{17,9},{25,17},{2,26},{10... | collective-permute-start | bytes 786440 | tf_op jit(solution)/shard_map/ppermute | solution.py:13
  152.0 24.0 %collective-permute-start.30 = (bf16[128,1024]{1,0:T(8,128)(2,1)}, bf16[128,1024]{1,0:T(8,128)(2,1)}, u32[]{:S(2)}, u32[]{:S(2)}) collective-permute-start(bf16[128,1024]{1,0:T(8,128)(2,1)} %get-tuple-element.22), channel_id=1, source_target_pairs={{0,16},{8,24},{16,0},{24,8},{1,17},{9,25},{17,1},{25,9},{2,18},{10... | collective-permute-start | bytes 786440 | tf_op jit(solution)/shard_map/ppermute | solution.py:13
  152.6 4.1 %slice-start = ((f32[512,512]{0,1:T(8,128)}), f32[128,512]{0,1:T(8,128)S(1)}, s32[]{:S(2)}) async-start(f32[512,512]{0,1:T(8,128)} %copy-done.8), calls=%async_computation | async-start | bytes 524288 | tf_op jit(solution)/shard_map/slice | solution.py:178
  152.6 9.3 %collective-permute-start.34 = (bf16[128,1024]{1,0:T(8,128)(2,1)S(1)}, bf16[128,1024]{1,0:T(8,128)(2,1)S(1)}, u32[]{:S(2)}, u32[]{:S(2)}) collective-permute-start(bf16[128,1024]{1,0:T(8,128)(2,1)S(1)} %get-tuple-element.18), channel_id=1, source_target_pairs={{0,3},{1,0},{2,1},{3,2},{4,7},{5,4},{6,5},{7,6},{8,11},{9,8},{10,9... | collective-permute-start | bytes 786440 | tf_op jit(solution)/shard_map/ppermute | solution.py:13
  152.7 11.7 %collective-permute-start.33 = (bf16[128,1024]{1,0:T(8,128)(2,1)S(1)}, bf16[128,1024]{1,0:T(8,128)(2,1)}, u32[]{:S(2)}, u32[]{:S(2)}) collective-permute-start(bf16[128,1024]{1,0:T(8,128)(2,1)S(1)} %get-tuple-element.19), channel_id=1, source_target_pairs={{0,2},{1,3},{2,0},{3,1},{4,6},{5,7},{6,4},{7,5},{8,10},{9,11},{10,... | collective-permute-start | bytes 786440 | tf_op jit(solution)/shard_map/ppermute | solution.py:13
  153.4 13.0 %collective-permute-start.32 = (bf16[128,1024]{1,0:T(8,128)(2,1)S(1)}, bf16[128,1024]{1,0:T(8,128)(2,1)}, u32[]{:S(2)}, u32[]{:S(2)}) collective-permute-start(bf16[128,1024]{1,0:T(8,128)(2,1)S(1)} %get-tuple-element.17), channel_id=1, source_target_pairs={{0,1},{1,2},{2,3},{3,0},{4,5},{5,6},{6,7},{7,4},{8,9},{9,10},{10,1... | collective-permute-start | bytes 786440 | tf_op jit(solution)/shard_map/ppermute | solution.py:13
  161.9 14.2 %collective-permute-start.29 = (bf16[128,1024]{1,0:T(8,128)(2,1)}, bf16[128,1024]{1,0:T(8,128)(2,1)S(1)}, u32[]{:S(2)}, u32[]{:S(2)}) collective-permute-start(bf16[128,1024]{1,0:T(8,128)(2,1)} %get-tuple-element.20), channel_id=1, source_target_pairs={{0,8},{8,16},{16,24},{24,0},{1,9},{9,17},{17,25},{25,1},{2,10},{10... | collective-permute-start | bytes 786440 | tf_op jit(solution)/shard_map/ppermute | solution.py:13
  (11 other events, 18.6 us)

commit v4 on v2

v4 whole, which is shorter than its diff:
```python
import functools

import jax
import jax.numpy as jnp
from jax import lax
from jax.experimental import pallas as pl
from jax.experimental.pallas import tpu as pltpu
from jax.sharding import PartitionSpec as P

epsilon = 1e-05
f32 = jnp.float32
bf16 = jnp.bfloat16
NN = ((1,), (0,))
NT = ((1,), (1,))
TN = ((0,), (0,))


def shift(shard, axis, by):
    devices = lax.axis_size(axis)
    return lax.ppermute(shard, axis, [(i, (i + by) % devices) for i in range(devices)])


def move(shard, axis, by):
    devices = lax.axis_size(axis)
    pairs = [(i, i + by) for i in range(devices) if 0 <= i + by < devices]
    return lax.ppermute(shard, axis, pairs)


def gathered(shard, axis):
    return [shard] + [shift(shard, axis, -k) for k in range(1, lax.axis_size(axis))]


def scattered(blocks, axis):
    return [blocks[0]] + [shift(blocks[k], axis, k) for k in range(1, len(blocks))]


def total(blocks):
    result = blocks[0].astype(f32)
    for part in blocks[1:]:
        result = result + part.astype(f32)
    return result


def block(array, axis, dim):
    size = array.shape[dim] // lax.axis_size(axis)
    return lax.dynamic_slice_in_dim(array, lax.axis_index(axis) * size, size, dim)


def dot(left, right, over):
    return lax.dot_general(left, right, (over, ((), ())), preferred_element_type=f32)


def run(kernel, results, where, groups_of_args, scratch=(), flops=0):
    counts = [len(group) for group in groups_of_args]
    flat = [array for group in groups_of_args for array in group]
    out_count = len(results)

    def body(where_ref, *refs):
        ins, at = [], 0
        for count in counts:
            ins.append(refs[at : at + count])
            at += count
        kernel(where_ref, ins, refs[at : at + out_count], refs[at + out_count :])

    size = sum(a.size * a.dtype.itemsize for a in list(flat) + list(results)) if flops else 0
    return pl.pallas_call(
        body,
        out_shape=[jax.ShapeDtypeStruct(r.shape, r.dtype) for r in results],
        in_specs=[pl.BlockSpec(memory_space=pltpu.SMEM)]
        + [pl.BlockSpec(memory_space=pltpu.VMEM)] * len(flat),
        out_specs=[pl.BlockSpec(memory_space=pltpu.VMEM)] * out_count,
        scratch_shapes=list(scratch),
        compiler_params=pltpu.CompilerParams(vmem_limit_bytes=56 << 20),
        cost_estimate=pl.CostEstimate(flops=flops, bytes_accessed=size, transcendentals=0),
    )(where, *flat)


def like(shape, dtype=bf16):
    return jax.ShapeDtypeStruct(shape, dtype)


def by_rows(rows, step):
    chunk = min(rows, 512)
    if rows == chunk:
        step(slice(0, rows))
        return

    @pl.loop(0, rows // chunk)
    def _(index):
        step(pl.ds(pl.multiple_of(index * chunk, chunk), chunk))


def gram_kernel(where, ins, outs, scratch):
    ((dec, recv, send, gain),) = ins
    side, gram = outs
    codes, relay = dec.shape[0], recv.shape[0]
    for ref, rows in ((dec, slice(0, codes)), (recv, slice(codes, codes + relay))):
        values = ref[...]
        gained = (values.astype(f32) * gain[...]).astype(bf16)
        side[rows, :relay] = dot(values, recv[...], NT).astype(bf16)
        side[rows, relay:] = dot(gained, send[...], NN).astype(bf16)
    rows = gram.shape[0]
    mine = dec[pl.ds(pl.multiple_of(where[1] * rows, rows), rows), :]
    gram[...] = dot(mine, dec[...], NT).astype(bf16)


def fold_kernel(where, ins, outs, scratch):
    ((proj, enc),) = ins
    outs[0][...] = dot(proj[...], enc[...], NT).astype(bf16)


def partial_kernel(where, ins, outs, scratch):
    heads, (fold,) = ins
    (whole,) = scratch
    tokens = heads[0].shape[0]
    cols = outs[0].shape[1]
    parts = len(outs)
    together = 4 if len(heads) % 4 == 0 else 1
    for first in range(0, len(heads), together):
        rows = slice(first * tokens, (first + together) * tokens)
        values = jnp.concatenate([h[...] for h in heads[first : first + together]])
        whole[...] = dot(values, fold[...], NN)
        for k in range(parts):
            at = lax.rem(where[0] + k, parts) * cols
            outs[k][rows, :] = whole[:, pl.ds(pl.multiple_of(at, cols), cols)].astype(bf16)


def forward(received, code_mix, code_send, square, products, width):
    relay = products.shape[1] // 2
    count = received.shape[1] // relay
    mixed, unscaled = [], []
    for k in range(count):
        cols = slice(k * relay, (k + 1) * relay)
        both = dot(received[:, cols], products[cols, :], NN)
        mixed.append(code_mix[:, cols] + both[:, :relay])
        unscaled.append(code_send[:, cols] + both[:, relay:])
    mixed = jnp.concatenate(mixed, axis=1)
    unscaled = jnp.concatenate(unscaled, axis=1)
    totals = square + jnp.sum(received.astype(f32) * (code_mix + mixed), axis=1, keepdims=True)
    row_scale = lax.rsqrt(jnp.maximum(totals, 0.0) / width + epsilon)
    return mixed, unscaled, row_scale


def backward(incoming, mixed, unscaled, row_scale, products, width):
    relay = products.shape[1] // 2
    count = incoming.shape[1] // relay
    inner = row_scale * jnp.sum(incoming.astype(f32) * unscaled, axis=1, keepdims=True) / width
    returned = []
    for k in range(count):
        cols = slice(k * relay, (k + 1) * relay)
        back = dot(incoming[:, cols], products[cols, relay:], NT)
        returned.append(row_scale * (back - row_scale * inner * mixed[:, cols]))
    return inner, jnp.concatenate(returned, axis=1).astype(bf16)


def first_kernel(width, where, ins, outs, scratch):
    mix_blocks, sides, grams, end_blocks = ins
    mix, ends, products, weights, mix_gram, mix_recv, mix_send, square, sent = outs
    (gram,) = scratch
    codes = mix.shape[1]
    relay = products.shape[1] // 2
    parts = len(mix_blocks)
    cols = codes // parts
    for k in range(parts):
        at = lax.rem(where[0] + k, parts) * cols
        mix[:, pl.ds(pl.multiple_of(at, cols), cols)] = mix_blocks[k][...]
        here = slice(k * relay, (k + 1) * relay)
        ends[:, here] = end_blocks[k][...]
        products[here, :] = sides[k][codes:, :]
        weights[:, here] = sides[k][:codes, :relay]
        there = slice((parts + k) * relay, (parts + k + 1) * relay)
        weights[:, there] = sides[k][:codes, relay:]
    rows = grams[0].shape[0]
    for k in range(len(grams)):
        at = lax.rem(where[1] + k, len(grams)) * rows
        gram[pl.ds(pl.multiple_of(at, rows), rows), :] = grams[k][...]

    def step(at):
        codes_here = mix[at, :]
        in_gram = dot(codes_here, gram[...], NN)
        sums = jnp.sum(in_gram * codes_here.astype(f32), axis=1, keepdims=True)
        in_relay = dot(codes_here, weights[...], NN)
        in_recv = in_relay[:, : parts * relay]
        in_send = in_relay[:, parts * relay :]
        mix_gram[at, :] = in_gram
        mix_recv[at, :] = in_recv
        mix_send[at, :] = in_send
        square[at, :] = sums
        mixed, unscaled, row_scale = forward(
            ends[at, :], in_recv, in_send, sums, products[...], width
        )
        sent[at, :] = (row_scale * unscaled).astype(bf16)

    by_rows(mix.shape[0], step)


def forward_kernel(width, turn, last, where, ins, outs, scratch):
    ((moved, received, ends, mix_recv, mix_send, square, products),) = ins
    live = where[2] == turn

    def step(at):
        values = jnp.where(live, moved[at, :], received[at, :])
        mixed, unscaled, row_scale = forward(
            values, mix_recv[at, :], mix_send[at, :], square[at, :], products[...], width
        )
        outs[0][at, :] = values
        outs[1][at, :] = (row_scale * unscaled).astype(bf16)
        if last:
            inner, returned = backward(
                ends[at, :], mixed, unscaled, row_scale, products[...], width
            )
            outs[2][at, :] = mixed
            outs[3][at, :] = unscaled
            outs[4][at, :] = row_scale
            outs[5][at, :] = returned

    by_rows(moved.shape[0], step)


def backward_kernel(width, live_section, last, where, ins, outs, scratch):
    (moved, incoming, received, mixed, unscaled, row_scale, mix_gram, products, weights, fold), = ins
    live = where[2] == live_section
    half = weights.shape[1] // 2
    codes = weights.shape[0]
    tokens = outs[4].shape[0] if last else 0

    def step(at):
        values = jnp.where(live, moved[at, :], incoming[at, :])
        scale = row_scale[at, :]
        inner, returned = backward(
            values, mixed[at, :], unscaled[at, :], scale, products[...], width
        )
        outs[0][at, :] = values
        outs[1][at, :] = returned
        if last:
            outs[2][at, :] = inner
            in_mixed = mix_gram[at, :] + dot(received[at, :], weights[:, :half], NT)
            back = dot(values, weights[:, half:], NT)
            outs[3][at, :] = (scale * (back - scale * inner * in_mixed)).astype(bf16)

    by_rows(moved.shape[0], step)
    if last:
        for k, out in enumerate(outs[4:]):
            rows = slice(k * tokens, (k + 1) * tokens)
            out[...] = dot(outs[3][rows, :], fold[...], NT).astype(bf16)


def head_kernel(where, ins, outs, scratch):
    heads, (code_grad, proj) = ins
    head_sum, enc_blocks = outs[0], outs[1:]
    (whole,) = scratch
    tokens = heads[0].shape[0]
    together = 4 if len(heads) % 4 == 0 else 1
    sums = None
    for first in range(0, len(heads), together):
        rows = slice(first * tokens, (first + together) * tokens)
        values = jnp.concatenate([h[...] for h in heads[first : first + together]])
        term = dot(code_grad[rows, :], values, TN)
        sums = term if sums is None else sums + term
    head_sum[...] = sums.astype(bf16)
    whole[...] = dot(head_sum[...], proj[...], NN)
    size = enc_blocks[0].shape[0]
    for k, out in enumerate(enc_blocks):
        at = lax.rem(where[0] + k, len(enc_blocks)) * size
        out[...] = whole[pl.ds(pl.multiple_of(at, size), size), :].astype(bf16)


def on_device(
    heads_out,
    out_proj,
    encoder,
    decoder,
    norm_gain,
    send_encoder,
    recv_decoder,
    input_code,
    code_cotangent,
):
    sections = lax.axis_size("pipe")
    section = lax.axis_index("pipe")
    groups = lax.axis_size("dp")
    parts = lax.axis_size("tensor")
    width = norm_gain.shape[1] * parts
    proj = out_proj[0]
    enc = encoder[0]
    dec = decoder[0]
    gain = norm_gain
    send = send_encoder[0]
    recv = recv_decoder[0]
    tokens, relay = input_code.shape
    codes, features = dec.shape
    cols = codes // parts
    rows = tokens * groups
    head_cols, model_cols = proj.shape
    where = jnp.stack([lax.axis_index("tensor"), lax.axis_index("dp"), section]).astype(jnp.int32)

    heads = gathered(heads_out[0], "dp")
    side, gram = run(
        gram_kernel,
        [like((codes + relay, 2 * relay)), like((codes // groups, codes))],
        where,
        [(dec, recv, send, gain)],
    )
    (fold,) = run(fold_kernel, [like((head_cols, codes))], where, [(proj, enc)])
    fold, side, gram = lax.optimization_barrier((fold, side, gram))
    sides = gathered(side, "tensor")
    grams = gathered(gram, "tensor")

    partials = run(
        partial_kernel,
        [like((rows, cols))] * parts,
        where,
        [heads, (fold,)],
        scratch=[pltpu.VMEM((min(groups, 4) * tokens, codes), f32)],
        flops=2 * rows * head_cols * codes,
    )
    end = jnp.where(section == 0, input_code, code_cotangent)
    end = jnp.concatenate(gathered(end, "dp"))
    gram = total(grams).astype(bf16)
    grams = gathered(gram, "dp")
    code_block = total(scattered(partials, "tensor")).astype(bf16)
    end, code_block = lax.optimization_barrier((end, code_block))
    others = gathered(code_block, "dp")
    end_blocks = gathered(end, "tensor")
    mix_block = code_block.astype(f32)
    for k in range(1, groups):
        other = others[k].astype(f32)
        mix_block = mix_block + jnp.concatenate([other[-k * tokens :], other[: -k * tokens]])
    mix_blocks = gathered(mix_block.astype(bf16), "tensor")

    square_flops = 2 * rows * codes * codes
    wide = parts * relay
    mix, ends, products, weights, mix_gram, mix_recv, mix_send, square, sent = run(
        functools.partial(first_kernel, width),
        [
            like((rows, codes)),
            like((rows, wide)),
            like((wide, 2 * relay)),
            like((codes, 2 * wide)),
            like((rows, codes), f32),
            like((rows, wide), f32),
            like((rows, wide), f32),
            like((rows, 1), f32),
            like((rows, wide)),
        ],
        where,
        [mix_blocks, sides, grams, end_blocks],
        scratch=[pltpu.VMEM((codes, codes), bf16)],
        flops=3 * square_flops,
    )
    received = ends
    for turn in range(1, sections):
        last = turn == sections - 1
        shapes = [like((rows, wide)), like((rows, wide))]
        if last:
            shapes += [like((rows, wide), f32)] * 2 + [like((rows, 1), f32), like((rows, wide))]
        moved = move(sent, "pipe", 1)
        results = run(
            functools.partial(forward_kernel, width, turn, last),
            shapes,
            where,
            [(moved, received, ends, mix_recv, mix_send, square, products)],
            flops=square_flops,
        )
        received, sent = results[:2]
    mixed, unscaled, row_scale, returned = results[2:]
    incoming = ends
    for turn in range(1, sections):
        last = turn == sections - 1
        shapes = [like((rows, wide)), like((rows, wide))]
        if last:
            shapes += [like((rows, 1), f32), like((rows, codes))]
            shapes += [like((tokens, head_cols))] * groups
        moved = move(returned, "pipe", -1)
        results = run(
            functools.partial(backward_kernel, width, sections - 1 - turn, last),
            shapes,
            where,
            [
                (
                    moved,
                    incoming,
                    received,
                    mixed,
                    unscaled,
                    row_scale,
                    mix_gram,
                    products,
                    weights,
                    fold,
                )
            ],
            flops=3 * square_flops,
        )
        incoming, returned = results[:2]
    inner, code_grad, *head_blocks = results[2:]

    heads_grad = total(scattered(head_blocks, "dp")).astype(bf16)
    head_sum, *enc_blocks = run(
        head_kernel,
        [like((codes, head_cols))] + [like((cols, model_cols))] * parts,
        where,
        [heads, (code_grad, proj)],
        scratch=[pltpu.VMEM((codes, model_cols), f32)],
        flops=2 * head_cols * codes * (rows + model_cols),
    )
    head_sum, mix, *enc_blocks = lax.optimization_barrier((head_sum, mix, *enc_blocks))
    enc_grad = total(scattered(enc_blocks, "tensor")).astype(bf16)
    proj_grad = dot(head_sum, enc, TN).astype(bf16)

    received_here = received[:, :relay]
    incoming_here = incoming[:, :relay]
    mixed = dot(mix, dec, NN) + dot(received_here, recv, NN)
    normed = mixed * row_scale
    out_rows = (normed * gain).astype(bf16)
    grad_norm = dot(incoming_here, send, NT)
    grad_mixed = (row_scale * (grad_norm * gain - normed * inner)).astype(bf16)
    dec_grad = dot(block(mix, "dp", 1), grad_mixed, TN).astype(bf16)
    gain_grad = jnp.sum(grad_norm * normed, axis=0)
    send_grad = dot(out_rows, incoming_here, TN).astype(bf16)
    recv_grad = dot(received_here, grad_mixed, TN).astype(bf16)
    return (
        sent[None, :tokens, :relay],
        returned[None, :tokens, :relay],
        heads_grad[None],
        proj_grad[None],
        enc_grad[None],
        dec_grad[None],
        gain_grad[None],
        send_grad[None],
        recv_grad[None],
    )


def solution(mesh):
    return jax.shard_map(
        on_device,
        mesh=mesh,
        in_specs=(
            P("pipe", "dp", "tensor"),
            P("pipe", "tensor", "dp"),
            P("pipe", None, "dp"),
            P("pipe", None, "tensor"),
            P("pipe", "tensor"),
            P("pipe", "tensor", None),
            P("pipe", None, "tensor"),
            P("dp", "tensor"),
            P("dp", "tensor"),
        ),
        out_specs=(
            P("pipe", "dp", "tensor"),
            P("pipe", "dp", "tensor"),
            P("pipe", "dp", "tensor"),
            P("pipe", "tensor", "dp"),
            P("pipe", "tensor", "dp"),
            P("pipe", "dp", "tensor"),
            P("pipe", "tensor"),
            P("pipe", "tensor", None),
            P("pipe", None, "tensor"),
        ),
        check_vma=False,
    )
```

time: 199 us -> 147 us (0.74)
  matrix products: 41.6 us -> 9.48 us
  Pallas kernels: 0 us -> 31.5 us
  waiting for transfers between devices: 47.2 us -> 25.4 us
  blocking collectives: 19.1 us -> 0 us
  between operations: 14.6 us -> 0.95 us
  starting transfers between devices: 55 us -> 64.5 us
  other arithmetic: 10.7 us -> 6.39 us
    ppermute x15 -> x33, starting transfers between devices: 26.4 us -> 61.9 us  [shift(): lax.ppermute(shard, axis, [(i, (i + by) % devices) for i in range(devices)])]
    dot_general x19 -> x7, matrix products: 41.6 us -> 9.48 us  [dot(): lax.dot_general(left, right, (over, ((), ())), preferred_element_type=f32)]
    pallas_call x0 -> x7, Pallas kernels: none -> 31.5 us  [run(): pl.pallas_call(body, out_shape=[jax.ShapeDtypeStruct(r.shape, r.dtype) fo...]
    all_to_all x7 -> x0, waiting for transfers between devices: 27.5 us -> none  [exchanged(): return lax.all_to_all(blocks, axis, 0, 0)]
    all_to_all x7 -> x0, starting transfers between devices: 25.9 us -> none  [exchanged(): return lax.all_to_all(blocks, axis, 0, 0)]
    all_to_all x2 -> x0, blocking collectives: 19.1 us -> none  [exchanged(): return lax.all_to_all(blocks, axis, 0, 0)]
    ppermute x15 -> x33, waiting for transfers between devices: 16.9 us -> 23.5 us  [shift(): lax.ppermute(shard, axis, [(i, (i + by) % devices) for i in range(devices)])]
    reduce_sum x7 -> x0, other arithmetic: 4.17 us -> none  [the longest x3 4.08 us: summed(): jnp.sum(exchanged(jnp.stack(blocks).astype(bf16), axis).astype(f32), axis=0)]
  transfers between devices with their start and end apart: 25 -> 35, of which waited for: 14 -> 13; matrix products, arithmetic and copies ran while one was open for 25% -> 11% of each run, Pallas kernels for 0% -> 11%
where the time goes in v4:
time: 147 us; the launch traced here: 146 us
  starting transfers between devices  64.5 us (44%)
  Pallas kernels  31.5 us (21%)
  waiting for transfers between devices  25.4 us (17%)
  matrix products  9.48 us (6%)
  local copies, waits for them, and re-layouts  7.8 us (5%)
  other arithmetic  6.39 us (4%)
    ppermute x33, starting transfers between devices, shift(): lax.ppermute(shard, axis, [(i, (i + by) % devices) for i in range(devices)])  61.9 us
    pallas_call x7, Pallas kernels, run(): pl.pallas_call(body, out_shape=[jax.ShapeDtypeStruct(r.shape, r.dtype) fo...  31.5 us
    ppermute x33, waiting for transfers between devices, shift(): lax.ppermute(shard, axis, [(i, (i + by) % devices) for i in range(devices)])  23.5 us
    dot_general x7, matrix products, dot(): lax.dot_general(left, right, (over, ((), ())), preferred_element_type=f32)  9.48 us
    unnamed x66, local copies, waits for them, and re-layouts  4.98 us
  transfers between devices with their start and end apart: 35, of which 13 were waited for; matrix products, arithmetic and copies ran while one was open for 11% of the time, Pallas kernels for 11%

profile of v4, /device:TPU:0, one launch (start us, length us, event | category | flops | bytes accessed | tf_op | source)
XLA Modules:
  0.0 146.0 jit_solution(10160872646104526252)
XLA Ops:
  0.6 3.1 %collective-permute-start.5 = (bf16[128,1024]{1,0:T(8,128)(2,1)}, bf16[128,1024]{1,0:T(8,128)(2,1)S(1)}, u32[]{:S(2)}, u32[]{:S(2)}) collective-permute-start(bf16[128,1024]{1,0:T(8,128)(2,1)} %bitcast.46), channel_id=1, source_target_pairs={{0,8},{8,16},{16,24},{24,0},{1,9},{9,17},{17,25},{25,1},{2,10},{10... | collective-permute-start | bytes 786440 | tf_op jit(solution)/shard_map/ppermute | solution.py:20
  3.7 2.6 %collective-permute-start.4 = (bf16[128,1024]{1,0:T(8,128)(2,1)}, bf16[128,1024]{1,0:T(8,128)(2,1)S(1)}, u32[]{:S(2)}, u32[]{:S(2)}) collective-permute-start(bf16[128,1024]{1,0:T(8,128)(2,1)} %bitcast.47), channel_id=1, source_target_pairs={{0,16},{8,24},{16,0},{24,8},{1,17},{9,25},{17,1},{25,9},{2,18},{10... | collective-permute-start | bytes 786440 | tf_op jit(solution)/shard_map/ppermute | solution.py:20
  6.3 1.3 collective-permute-start.3
  10.0 4.1 %shard_map.160.refs_4_.refs_9_ = bf16[1024,512]{1,0:T(8,128)(2,1)} custom-call(s32[3]{0:T(128)} %pad_add_fusion.where_ref, bf16[1024,1024]{1,0:T(8,128)(2,1)} %bitcast.42, bf16[512,1024]{1,0:T(8,128)(2,1)} %bitcast.44), custom_call_target="tpu_custom_call" | custom-call | tf_op jit(solution)/shard_map/pallas_call | solution.py:66
  14.1 3.2 %shard_map.161 = (bf16[640,256]{1,0:T(8,128)(2,1)}, bf16[128,512]{1,0:T(8,128)(2,1)}) custom-call(s32[3]{0:T(128)} %pad_add_fusion.where_ref, bf16[512,1024]{1,0:T(8,128)(2,1)} %bitcast.41, bf16[128,1024]{1,0:T(8,128)(2,1)} %bitcast.45, bf16[1024,128]{1,0:T(8,128)(2,1)} %bitcast.51, f32[1,1024]{1,0:T(1,128)} %refs_3_.1), custom_call_target="tpu_custom_call" | custom-call | tf_op jit(solution)/shard_map/pallas_call | solution.py:66
  17.3 2.9 %collective-permute-start = (bf16[128,128]{1,0:T(8,128)(2,1)S(1)}, bf16[128,128]{1,0:T(8,128)(2,1)S(1)}, u32[]{:S(2)}, u32[]{:S(2)}) collective-permute-start(bf16[128,128]{1,0:T(8,128)(2,1)S(1)} %broadcast_select_fusion), channel_id=1, source_target_pairs={{0,24},{8,0},{16,8},{24,16},{1,25},{9,1},{17,9},{25,17},{2,26},{10... | collective-permute-start | bytes 98312 | tf_op jit(solution)/shard_map/ppermute | solution.py:20
  20.2 4.2 %collective-permute-done.4.refs_2_ = bf16[128,1024]{1,0:T(8,128)(2,1)S(1)} collective-permute-done((bf16[128,1024]{1,0:T(8,128)(2,1)}, bf16[128,1024]{1,0:T(8,128)(2,1)S(1)}, u32[]{:S(2)}, u32[]{:S(2)}) %collective-permute-start.4) | collective-permute-done | bytes 262176 | tf_op jit(solution)/shard_map/ppermute | solution.py:20
  25.8 3.2 %shard_map.162 = (bf16[512,128]{1,0:T(8,128)(2,1)}, bf16[512,128]{1,0:T(8,128)(2,1)}, bf16[512,128]{1,0:T(8,128)(2,1)}, bf16[512,128]{1,0:T(8,128)(2,1)}) custom-call(s32[3]{0:T(128)} %pad_add_fusion.where_ref, bf16[128,1024]{1,0:T(8,128)(2,1)} %bitcast.49, bf16[128,1024]{1,0:T(8,128)(2,1)} %copy-done.9, bf16[128,1024]{1,0:T(8,128)(2,1)} %copy-done.8, ...), custom_call_target="tpu_custom_call" | custom-call | flops 536870912 | bytes 2621440 | tf_op jit(solution)/shard_map/pallas_call | solution.py:66
  29.0 1.5 %collective-permute-start.6 = (bf16[512,128]{1,0:T(8,128)(2,1)}, bf16[512,128]{1,0:T(8,128)(2,1)S(1)}, u32[]{:S(2)}, u32[]{:S(2)}) collective-permute-start(bf16[512,128]{1,0:T(8,128)(2,1)} %get-tuple-element.58), channel_id=1, source_target_pairs={{0,1},{1,2},{2,3},{3,0},{4,5},{5,6},{6,7},{7,4},{8,9},{9,10},{10,1... | collective-permute-start | bytes 393224 | tf_op jit(solution)/shard_map/ppermute | solution.py:20
  30.5 1.5 %collective-permute-start.7 = (bf16[512,128]{1,0:T(8,128)(2,1)}, bf16[512,128]{1,0:T(8,128)(2,1)S(1)}, u32[]{:S(2)}, u32[]{:S(2)}) collective-permute-start(bf16[512,128]{1,0:T(8,128)(2,1)} %get-tuple-element.59), channel_id=1, source_target_pairs={{0,2},{1,3},{2,0},{3,1},{4,6},{5,7},{6,4},{7,5},{8,10},{9,11},{10,... | collective-permute-start | bytes 393224 | tf_op jit(solution)/shard_map/ppermute | solution.py:20
  32.0 1.4 collective-permute-start.8
  34.6 1.9 %collective-permute-done.6 = bf16[512,128]{1,0:T(8,128)(2,1)S(1)} collective-permute-done((bf16[512,128]{1,0:T(8,128)(2,1)}, bf16[512,128]{1,0:T(8,128)(2,1)S(1)}, u32[]{:S(2)}, u32[]{:S(2)}) %collective-permute-start.6) | collective-permute-done | bytes 131104 | tf_op jit(solution)/shard_map/ppermute | solution.py:20
  36.5 1.6 %collective-permute-start.18 = (bf16[128,512]{1,0:T(8,128)(2,1)S(1)}, bf16[128,512]{1,0:T(8,128)(2,1)S(1)}, u32[]{:S(2)}, u32[]{:S(2)}) collective-permute-start(bf16[128,512]{1,0:T(8,128)(2,1)S(1)} %copy-done.14), channel_id=1, source_target_pairs={{0,3},{1,0},{2,1},{3,2},{4,7},{5,4},{6,5},{7,6},{8,11},{9,8},{10,9... | collective-permute-start | bytes 393224 | tf_op jit(solution)/shard_map/ppermute | solution.py:20
  38.0 1.3 collective-permute-done.7
  39.4 1.5 %collective-permute-start.17 = (bf16[640,256]{1,0:T(8,128)(2,1)S(1)}, bf16[640,256]{1,0:T(8,128)(2,1)S(1)}, u32[]{:S(2)}, u32[]{:S(2)}) collective-permute-start(bf16[640,256]{1,0:T(8,128)(2,1)S(1)} %copy-done.19), channel_id=1, source_target_pairs={{0,1},{1,2},{2,3},{3,0},{4,5},{5,6},{6,7},{7,4},{8,9},{9,10},{10,1... | collective-permute-start | bytes 983048 | tf_op jit(solution)/shard_map/ppermute | solution.py:20
  42.1 6.2 %collective-permute-start.11 = (bf16[512,128]{1,0:T(8,128)(2,1)S(1)}, bf16[512,128]{1,0:T(8,128)(2,1)S(1)}, u32[]{:S(2)}, u32[]{:S(2)}) collective-permute-start(bf16[512,128]{1,0:T(8,128)(2,1)S(1)} %add_convert_fusion.3), channel_id=1, source_target_pairs={{0,8},{8,16},{16,24},{24,0},{1,9},{9,17},{17,25},{25,1},{2,10},{10... | collective-permute-start | bytes 393224 | tf_op jit(solution)/shard_map/ppermute | solution.py:20
  48.3 5.7 %collective-permute-start.10 = (bf16[512,128]{1,0:T(8,128)(2,1)S(1)}, bf16[512,128]{1,0:T(8,128)(2,1)S(1)}, u32[]{:S(2)}, u32[]{:S(2)}) collective-permute-start(bf16[512,128]{1,0:T(8,128)(2,1)S(1)} %add_convert_fusion.3), channel_id=1, source_target_pairs={{0,16},{8,24},{16,0},{24,8},{1,17},{9,25},{17,1},{25,9},{2,18},{10... | collective-permute-start | bytes 393224 | tf_op jit(solution)/shard_map/ppermute | solution.py:20
  54.0 4.4 %collective-permute-start.9 = (bf16[512,128]{1,0:T(8,128)(2,1)S(1)}, bf16[512,128]{1,0:T(8,128)(2,1)S(1)}, u32[]{:S(2)}, u32[]{:S(2)}) collective-permute-start(bf16[512,128]{1,0:T(8,128)(2,1)S(1)} %add_convert_fusion.3), channel_id=1, source_target_pairs={{0,24},{8,0},{16,8},{24,16},{1,25},{9,1},{17,9},{25,17},{2,26},{10... | collective-permute-start | bytes 393224 | tf_op jit(solution)/shard_map/ppermute | solution.py:20
  59.3 3.1 %collective-permute-done.10 = bf16[512,128]{1,0:T(8,128)(2,1)S(1)} collective-permute-done((bf16[512,128]{1,0:T(8,128)(2,1)S(1)}, bf16[512,128]{1,0:T(8,128)(2,1)S(1)}, u32[]{:S(2)}, u32[]{:S(2)}) %collective-permute-start.10) | collective-permute-done | bytes 131104 | tf_op jit(solution)/shard_map/ppermute | solution.py:20
  62.5 4.0 %collective-permute-start.23 = (bf16[128,512]{1,0:T(8,128)(2,1)S(1)}, bf16[128,512]{1,0:T(8,128)(2,1)S(1)}, u32[]{:S(2)}, u32[]{:S(2)}) collective-permute-start(bf16[128,512]{1,0:T(8,128)(2,1)S(1)} %add_convert_fusion.2.refs_8_), channel_id=1, source_target_pairs={{0,8},{8,16},{16,24},{24,0},{1,9},{9,17},{17,25},{25,1},{2,10},{10... | collective-permute-start | bytes 393224 | tf_op jit(solution)/shard_map/ppermute | solution.py:20
  66.5 3.4 %collective-permute-start.22 = (bf16[128,512]{1,0:T(8,128)(2,1)S(1)}, bf16[128,512]{1,0:T(8,128)(2,1)S(1)}, u32[]{:S(2)}, u32[]{:S(2)}) collective-permute-start(bf16[128,512]{1,0:T(8,128)(2,1)S(1)} %add_convert_fusion.2.refs_8_), channel_id=1, source_target_pairs={{0,16},{8,24},{16,0},{24,8},{1,17},{9,25},{17,1},{25,9},{2,18},{10... | collective-permute-start | bytes 393224 | tf_op jit(solution)/shard_map/ppermute | solution.py:20
  70.0 2.4 %collective-permute-done.23.refs_11_ = bf16[128,512]{1,0:T(8,128)(2,1)S(1)} collective-permute-done((bf16[128,512]{1,0:T(8,128)(2,1)S(1)}, bf16[128,512]{1,0:T(8,128)(2,1)S(1)}, u32[]{:S(2)}, u32[]{:S(2)}) %collective-permute-start.23) | collective-permute-done | bytes 131104 | tf_op jit(solution)/shard_map/ppermute | solution.py:20
  72.4 3.3 %collective-permute-start.21 = (bf16[128,512]{1,0:T(8,128)(2,1)S(1)}, bf16[128,512]{1,0:T(8,128)(2,1)S(1)}, u32[]{:S(2)}, u32[]{:S(2)}) collective-permute-start(bf16[128,512]{1,0:T(8,128)(2,1)S(1)} %add_convert_fusion.2.refs_8_), channel_id=1, source_target_pairs={{0,24},{8,0},{16,8},{24,16},{1,25},{9,1},{17,9},{25,17},{2,26},{10... | collective-permute-start | bytes 393224 | tf_op jit(solution)/shard_map/ppermute | solution.py:20
  75.8 2.4 %collective-permute-done.21.refs_9_ = bf16[128,512]{1,0:T(8,128)(2,1)S(1)} collective-permute-done((bf16[128,512]{1,0:T(8,128)(2,1)S(1)}, bf16[128,512]{1,0:T(8,128)(2,1)S(1)}, u32[]{:S(2)}, u32[]{:S(2)}) %collective-permute-start.21) | collective-permute-done | bytes 131104 | tf_op jit(solution)/shard_map/ppermute | solution.py:20
  79.1 1.5 %collective-permute-start.14 = (bf16[512,128]{1,0:T(8,128)(2,1)S(1)}, bf16[512,128]{1,0:T(8,128)(2,1)S(1)}, u32[]{:S(2)}, u32[]{:S(2)}) collective-permute-start(bf16[512,128]{1,0:T(8,128)(2,1)S(1)} %fusion.8.refs_0_), channel_id=1, source_target_pairs={{0,1},{1,2},{2,3},{3,0},{4,5},{5,6},{6,7},{7,4},{8,9},{9,10},{10,1... | collective-permute-start | bytes 393224 | tf_op jit(solution)/shard_map/ppermute | solution.py:20
  80.6 1.7 %collective-permute-start.13 = (bf16[512,128]{1,0:T(8,128)(2,1)S(1)}, bf16[512,128]{1,0:T(8,128)(2,1)S(1)}, u32[]{:S(2)}, u32[]{:S(2)}) collective-permute-start(bf16[512,128]{1,0:T(8,128)(2,1)S(1)} %fusion.8.refs_0_), channel_id=1, source_target_pairs={{0,2},{1,3},{2,0},{3,1},{4,6},{5,7},{6,4},{7,5},{8,10},{9,11},{10,... | collective-permute-start | bytes 393224 | tf_op jit(solution)/shard_map/ppermute | solution.py:20
  82.3 1.5 collective-permute-start.12
  83.8 2.4 %collective-permute-done.14.refs_3_ = bf16[512,128]{1,0:T(8,128)(2,1)S(1)} collective-permute-done((bf16[512,128]{1,0:T(8,128)(2,1)S(1)}, bf16[512,128]{1,0:T(8,128)(2,1)S(1)}, u32[]{:S(2)}, u32[]{:S(2)}) %collective-permute-start.14) | collective-permute-done | bytes 131104 | tf_op jit(solution)/shard_map/ppermute | solution.py:20
  88.3 5.2 %shard_map.163 = (bf16[512,512]{1,0:T(8,128)(2,1)}, bf16[512,512]{1,0:T(8,128)(2,1)}, bf16[512,256]{1,0:T(8,128)(2,1)}, bf16[512,1024]{1,0:T(8,128)(2,1)}, f32[5...) custom-call(s32[3]{0:T(128)} %pad_add_fusion.where_ref, ...), custom_call_target="tpu_custom_call" | custom-call | flops 805306368 | bytes 8914944 | tf_op jit(solution)/shard_map/pallas_call | solution.py:66
  93.5 1.3 collective-permute-start.27
  94.8 1.7 %collective-permute-done.27.refs_0_ = bf16[512,512]{1,0:T(8,128)(2,1)S(1)} collective-permute-done((bf16[512,512]{1,0:T(8,128)(2,1)}, bf16[512,512]{1,0:T(8,128)(2,1)S(1)}, u32[]{:S(2)}, u32[]{:S(2)}) %collective-permute-start.27) | collective-permute-done | bytes 524320 | tf_op jit(solution)/shard_map/ppermute | solution.py:26
  97.4 4.6 %shard_map.164 = (bf16[512,512]{1,0:T(8,128)(2,1)}, bf16[512,512]{1,0:T(8,128)(2,1)}, f32[512,512]{1,0:T(8,128)}, f32[512,512]{1,0:T(8,128)}, f32[512,1]{1,0:T(8,128)}, /*index=5*/bf16[512,512]{1,0:T(8,128)(2,1)}) custom-call(s32[3]{0:T(128)} %pad_add_fusion.where_ref, bf16[512,512]{1,0:T(8,128)(2,1)} %copy-done.5, ...), custom_call_target="tpu_custom_call" | custom-call | flops 268435456 | bytes 7606272 | tf_op jit(solution)/shard_map/pallas_call | solution.py:66
  102.0 1.3 collective-permute-start.28
  103.2 1.1 reduce
  104.3 1.4 slice_bitcast_fusion.1
  106.8 6.1 %shard_map.165 = (bf16[512,512]{1,0:T(8,128)(2,1)}, bf16[512,512]{1,0:T(8,128)(2,1)}, f32[512,1]{1,0:T(8,128)}, bf16[512,512]{1,0:T(8,128)(2,1)}, bf16[128,1024]...) custom-call(s32[3]{0:T(128)} %pad_add_fusion.where_ref, ...), custom_call_target="tpu_custom_call" | custom-call | flops 805306368 | bytes 9703424 | tf_op jit(solution)/shard_map/pallas_call | solution.py:66
  112.8 1.4 slice_bitcast_fusion
  114.2 1.1 reduce.1
  115.4 4.8 %collective-permute-start.30 = (bf16[128,1024]{1,0:T(8,128)(2,1)}, bf16[128,1024]{1,0:T(8,128)(2,1)S(1)}, u32[]{:S(2)}, u32[]{:S(2)}) collective-permute-start(bf16[128,1024]{1,0:T(8,128)(2,1)} %get-tuple-element.82), channel_id=1, source_target_pairs={{0,16},{8,24},{16,0},{24,8},{1,17},{9,25},{17,1},{25,9},{2,18},{10... | collective-permute-start | bytes 786440 | tf_op jit(solution)/shard_map/ppermute | solution.py:20
  120.1 5.1 %shard_map.166 = (bf16[512,1024]{1,0:T(8,128)(2,1)}, bf16[128,1024]{1,0:T(8,128)(2,1)}, bf16[128,1024]{1,0:T(8,128)(2,1)}, bf16[128,1024]{1,0:T(8,128)(2,1)}, bf16[128,1024]{1,0:T(8,128)(2,1)}) custom-call(s32[3]{0:T(128)} %pad_add_fusion.where_ref, bf16[128,1024]{1,0:T(8,128)(2,1)} %bitcast.50, bf16[128,1024]{1,0:T(8,128)(2,1)} %copy-done.9, ...), custom_call_target="tpu_custom_call" | custom-call | flops 1610612736 | bytes 5767168 | tf_op jit(solution)/shard_map/pallas_call | solution.py:66
  126.3 1.5 collective-permute-start.33
  127.7 3.8 %convert_bitcast_fusion = bf16[1,1024,1024]{2,1,0:T(8,128)(2,1)} fusion(bf16[512,1024]{1,0:T(8,128)(2,1)} %get-tuple-element.91, bf16[1,512,1024]{2,1,0:T(8,128)(2,1)S(1)} %copy-done.2), kind=kOutput, calls=%fused_computation.4 | convolution fusion | flops 1074790400 | bytes 4194304 | tf_op jit(solution)/shard_map/dot_general | solution.py:50
  133.7 1.2 fusion.1
  134.9 1.2 multiply_reduce_fusion
  136.1 1.0 fusion.2
  137.2 1.6 %collective-permute-start.34 = (bf16[128,1024]{1,0:T(8,128)(2,1)S(1)}, bf16[128,1024]{1,0:T(8,128)(2,1)S(1)}, u32[]{:S(2)}, u32[]{:S(2)}) collective-permute-start(bf16[128,1024]{1,0:T(8,128)(2,1)S(1)} %copy-done.23), channel_id=1, source_target_pairs={{0,3},{1,0},{2,1},{3,2},{4,7},{5,4},{6,5},{7,6},{8,11},{9,8},{10,9... | collective-permute-start | bytes 786440 | tf_op jit(solution)/shard_map/ppermute | solution.py:20
  138.7 1.0 fusion
  140.7 4.5 %collective-permute-done.34 = bf16[128,1024]{1,0:T(8,128)(2,1)S(1)} collective-permute-done((bf16[128,1024]{1,0:T(8,128)(2,1)S(1)}, bf16[128,1024]{1,0:T(8,128)(2,1)S(1)}, u32[]{:S(2)}, u32[]{:S(2)}) %collective-permute-start.34) | collective-permute-done | bytes 262176 | tf_op jit(solution)/shard_map/ppermute | solution.py:20
  (119 shorter events, 16.9 us)
Async XLA Ops:
  0.6 16.7 %collective-permute-start.5 = (bf16[128,1024]{1,0:T(8,128)(2,1)}, bf16[128,1024]{1,0:T(8,128)(2,1)S(1)}, u32[]{:S(2)}, u32[]{:S(2)}) collective-permute-start(bf16[128,1024]{1,0:T(8,128)(2,1)} %bitcast.46), channel_id=1, source_target_pairs={{0,8},{8,16},{16,24},{24,0},{1,9},{9,17},{17,25},{25,1},{2,10},{10... | collective-permute-start | bytes 786440 | tf_op jit(solution)/shard_map/ppermute | solution.py:20
  3.7 20.7 %collective-permute-start.4 = (bf16[128,1024]{1,0:T(8,128)(2,1)}, bf16[128,1024]{1,0:T(8,128)(2,1)S(1)}, u32[]{:S(2)}, u32[]{:S(2)}) collective-permute-start(bf16[128,1024]{1,0:T(8,128)(2,1)} %bitcast.47), channel_id=1, source_target_pairs={{0,16},{8,24},{16,0},{24,8},{1,17},{9,25},{17,1},{25,9},{2,18},{10... | collective-permute-start | bytes 786440 | tf_op jit(solution)/shard_map/ppermute | solution.py:20
  6.3 18.1 %collective-permute-start.3 = (bf16[128,1024]{1,0:T(8,128)(2,1)}, bf16[128,1024]{1,0:T(8,128)(2,1)S(1)}, u32[]{:S(2)}, u32[]{:S(2)}) collective-permute-start(bf16[128,1024]{1,0:T(8,128)(2,1)} %bitcast.48), channel_id=1, source_target_pairs={{0,24},{8,0},{16,8},{24,16},{1,25},{9,1},{17,9},{25,17},{2,26},{10... | collective-permute-start | bytes 786440 | tf_op jit(solution)/shard_map/ppermute | solution.py:20
  8.4 23.6 %collective-permute-start.2 = (bf16[128,128]{1,0:T(8,128)(2,1)S(1)}, bf16[128,128]{1,0:T(8,128)(2,1)S(1)}, u32[]{:S(2)}, u32[]{:S(2)}) collective-permute-start(bf16[128,128]{1,0:T(8,128)(2,1)S(1)} %broadcast_select_fusion), channel_id=1, source_target_pairs={{0,8},{8,16},{16,24},{24,0},{1,9},{9,17},{17,25},{25,1},{2,10},{10... | collective-permute-start | bytes 98312 | tf_op jit(solution)/shard_map/ppermute | solution.py:20
  9.1 24.3 %collective-permute-start.1 = (bf16[128,128]{1,0:T(8,128)(2,1)S(1)}, bf16[128,128]{1,0:T(8,128)(2,1)S(1)}, u32[]{:S(2)}, u32[]{:S(2)}) collective-permute-start(bf16[128,128]{1,0:T(8,128)(2,1)S(1)} %broadcast_select_fusion), channel_id=1, source_target_pairs={{0,16},{8,24},{16,0},{24,8},{1,17},{9,25},{17,1},{25,9},{2,18},{10... | collective-permute-start | bytes 98312 | tf_op jit(solution)/shard_map/ppermute | solution.py:20
  17.3 16.1 %copy-start.14 = (bf16[128,512]{1,0:T(8,128)(2,1)S(1)}, bf16[128,512]{1,0:T(8,128)(2,1)}, u32[]{:S(2)}) copy-start(bf16[128,512]{1,0:T(8,128)(2,1)} %get-tuple-element.63) | copy-start | bytes 393220
  17.3 22.1 %copy-start.19 = (bf16[640,256]{1,0:T(8,128)(2,1)S(1)}, bf16[640,256]{1,0:T(8,128)(2,1)}, u32[]{:S(2)}) copy-start(bf16[640,256]{1,0:T(8,128)(2,1)} %get-tuple-element.62.refs_4_) | copy-start | bytes 983044
  17.3 7.0 %copy-start.7 = (bf16[128,1024]{1,0:T(8,128)(2,1)}, bf16[128,1024]{1,0:T(8,128)(2,1)S(1)}, u32[]{:S(2)}) copy-start(bf16[128,1024]{1,0:T(8,128)(2,1)S(1)} %collective-permute-done.5.refs_3_) | copy-start | bytes 786436
  17.3 16.7 %collective-permute-start = (bf16[128,128]{1,0:T(8,128)(2,1)S(1)}, bf16[128,128]{1,0:T(8,128)(2,1)S(1)}, u32[]{:S(2)}, u32[]{:S(2)}) collective-permute-start(bf16[128,128]{1,0:T(8,128)(2,1)S(1)} %broadcast_select_fusion), channel_id=1, source_target_pairs={{0,24},{8,0},{16,8},{24,16},{1,25},{9,1},{17,9},{25,17},{2,26},{10... | collective-permute-start | bytes 98312 | tf_op jit(solution)/shard_map/ppermute | solution.py:20
  29.0 7.5 %collective-permute-start.6 = (bf16[512,128]{1,0:T(8,128)(2,1)}, bf16[512,128]{1,0:T(8,128)(2,1)S(1)}, u32[]{:S(2)}, u32[]{:S(2)}) collective-permute-start(bf16[512,128]{1,0:T(8,128)(2,1)} %get-tuple-element.58), channel_id=1, source_target_pairs={{0,1},{1,2},{2,3},{3,0},{4,5},{5,6},{6,7},{7,4},{8,9},{9,10},{10,1... | collective-permute-start | bytes 393224 | tf_op jit(solution)/shard_map/ppermute | solution.py:20
  30.5 8.9 %collective-permute-start.7 = (bf16[512,128]{1,0:T(8,128)(2,1)}, bf16[512,128]{1,0:T(8,128)(2,1)S(1)}, u32[]{:S(2)}, u32[]{:S(2)}) collective-permute-start(bf16[512,128]{1,0:T(8,128)(2,1)} %get-tuple-element.59), channel_id=1, source_target_pairs={{0,2},{1,3},{2,0},{3,1},{4,6},{5,7},{6,4},{7,5},{8,10},{9,11},{10,... | collective-permute-start | bytes 393224 | tf_op jit(solution)/shard_map/ppermute | solution.py:20
  32.0 8.9 %collective-permute-start.8 = (bf16[512,128]{1,0:T(8,128)(2,1)}, bf16[512,128]{1,0:T(8,128)(2,1)S(1)}, u32[]{:S(2)}, u32[]{:S(2)}) collective-permute-start(bf16[512,128]{1,0:T(8,128)(2,1)} %get-tuple-element.60), channel_id=1, source_target_pairs={{0,3},{1,0},{2,1},{3,2},{4,7},{5,4},{6,5},{7,6},{8,11},{9,8},{10,9... | collective-permute-start | bytes 393224 | tf_op jit(solution)/shard_map/ppermute | solution.py:20
  33.4 8.6 %collective-permute-start.20 = (bf16[128,512]{1,0:T(8,128)(2,1)S(1)}, bf16[128,512]{1,0:T(8,128)(2,1)S(1)}, u32[]{:S(2)}, u32[]{:S(2)}) collective-permute-start(bf16[128,512]{1,0:T(8,128)(2,1)S(1)} %copy-done.14), channel_id=1, source_target_pairs={{0,1},{1,2},{2,3},{3,0},{4,5},{5,6},{6,7},{7,4},{8,9},{9,10},{10,1... | collective-permute-start | bytes 393224 | tf_op jit(solution)/shard_map/ppermute | solution.py:20
  34.1 14.2 %collective-permute-start.19 = (bf16[128,512]{1,0:T(8,128)(2,1)S(1)}, bf16[128,512]{1,0:T(8,128)(2,1)S(1)}, u32[]{:S(2)}, u32[]{:S(2)}) collective-permute-start(bf16[128,512]{1,0:T(8,128)(2,1)S(1)} %copy-done.14), channel_id=1, source_target_pairs={{0,2},{1,3},{2,0},{3,1},{4,6},{5,7},{6,4},{7,5},{8,10},{9,11},{10,... | collective-permute-start | bytes 393224 | tf_op jit(solution)/shard_map/ppermute | solution.py:20
  34.6 52.7 %copy-start.15 = (bf16[512,128]{1,0:T(8,128)(2,1)}, bf16[512,128]{1,0:T(8,128)(2,1)S(1)}, u32[]{:S(2)}) copy-start(bf16[512,128]{1,0:T(8,128)(2,1)S(1)} %pad_maximum_fusion.refs_12_) | copy-start | bytes 393220
  36.5 17.6 %collective-permute-start.18 = (bf16[128,512]{1,0:T(8,128)(2,1)S(1)}, bf16[128,512]{1,0:T(8,128)(2,1)S(1)}, u32[]{:S(2)}, u32[]{:S(2)}) collective-permute-start(bf16[128,512]{1,0:T(8,128)(2,1)S(1)} %copy-done.14), channel_id=1, source_target_pairs={{0,3},{1,0},{2,1},{3,2},{4,7},{5,4},{6,5},{7,6},{8,11},{9,8},{10,9... | collective-permute-start | bytes 393224 | tf_op jit(solution)/shard_map/ppermute | solution.py:20
  39.4 39.2 %collective-permute-start.17 = (bf16[640,256]{1,0:T(8,128)(2,1)S(1)}, bf16[640,256]{1,0:T(8,128)(2,1)S(1)}, u32[]{:S(2)}, u32[]{:S(2)}) collective-permute-start(bf16[640,256]{1,0:T(8,128)(2,1)S(1)} %copy-done.19), channel_id=1, source_target_pairs={{0,1},{1,2},{2,3},{3,0},{4,5},{5,6},{6,7},{7,4},{8,9},{9,10},{10,1... | collective-permute-start | bytes 983048 | tf_op jit(solution)/shard_map/ppermute | solution.py:20
  40.9 38.2 %collective-permute-start.16 = (bf16[640,256]{1,0:T(8,128)(2,1)S(1)}, bf16[640,256]{1,0:T(8,128)(2,1)S(1)}, u32[]{:S(2)}, u32[]{:S(2)}) collective-permute-start(bf16[640,256]{1,0:T(8,128)(2,1)S(1)} %copy-done.19), channel_id=1, source_target_pairs={{0,2},{1,3},{2,0},{3,1},{4,6},{5,7},{6,4},{7,5},{8,10},{9,11},{10,... | collective-permute-start | bytes 983048 | tf_op jit(solution)/shard_map/ppermute | solution.py:20
  42.1 16.4 %collective-permute-start.11 = (bf16[512,128]{1,0:T(8,128)(2,1)S(1)}, bf16[512,128]{1,0:T(8,128)(2,1)S(1)}, u32[]{:S(2)}, u32[]{:S(2)}) collective-permute-start(bf16[512,128]{1,0:T(8,128)(2,1)S(1)} %add_convert_fusion.3), channel_id=1, source_target_pairs={{0,8},{8,16},{16,24},{24,0},{1,9},{9,17},{17,25},{25,1},{2,10},{10... | collective-permute-start | bytes 393224 | tf_op jit(solution)/shard_map/ppermute | solution.py:20
  48.3 14.2 %collective-permute-start.10 = (bf16[512,128]{1,0:T(8,128)(2,1)S(1)}, bf16[512,128]{1,0:T(8,128)(2,1)S(1)}, u32[]{:S(2)}, u32[]{:S(2)}) collective-permute-start(bf16[512,128]{1,0:T(8,128)(2,1)S(1)} %add_convert_fusion.3), channel_id=1, source_target_pairs={{0,16},{8,24},{16,0},{24,8},{1,17},{9,25},{17,1},{25,9},{2,18},{10... | collective-permute-start | bytes 393224 | tf_op jit(solution)/shard_map/ppermute | solution.py:20
  54.0 12.5 %collective-permute-start.9 = (bf16[512,128]{1,0:T(8,128)(2,1)S(1)}, bf16[512,128]{1,0:T(8,128)(2,1)S(1)}, u32[]{:S(2)}, u32[]{:S(2)}) collective-permute-start(bf16[512,128]{1,0:T(8,128)(2,1)S(1)} %add_convert_fusion.3), channel_id=1, source_target_pairs={{0,24},{8,0},{16,8},{24,16},{1,25},{9,1},{17,9},{25,17},{2,26},{10... | collective-permute-start | bytes 393224 | tf_op jit(solution)/shard_map/ppermute | solution.py:20
  58.5 28.8 %copy-start.13 = (bf16[128,512]{1,0:T(8,128)(2,1)}, bf16[128,512]{1,0:T(8,128)(2,1)S(1)}, u32[]{:S(2)}) copy-start(bf16[128,512]{1,0:T(8,128)(2,1)S(1)} %add_convert_fusion.2.refs_8_) | copy-start | bytes 393220
  58.5 22.1 %collective-permute-start.15 = (bf16[640,256]{1,0:T(8,128)(2,1)S(1)}, bf16[640,256]{1,0:T(8,128)(2,1)S(1)}, u32[]{:S(2)}, u32[]{:S(2)}) collective-permute-start(bf16[640,256]{1,0:T(8,128)(2,1)S(1)} %copy-done.19), channel_id=1, source_target_pairs={{0,3},{1,0},{2,1},{3,2},{4,7},{5,4},{6,5},{7,6},{8,11},{9,8},{10,9... | collective-permute-start | bytes 983048 | tf_op jit(solution)/shard_map/ppermute | solution.py:20
  62.5 9.9 %collective-permute-start.23 = (bf16[128,512]{1,0:T(8,128)(2,1)S(1)}, bf16[128,512]{1,0:T(8,128)(2,1)S(1)}, u32[]{:S(2)}, u32[]{:S(2)}) collective-permute-start(bf16[128,512]{1,0:T(8,128)(2,1)S(1)} %add_convert_fusion.2.refs_8_), channel_id=1, source_target_pairs={{0,8},{8,16},{16,24},{24,0},{1,9},{9,17},{17,25},{25,1},{2,10},{10... | collective-permute-start | bytes 393224 | tf_op jit(solution)/shard_map/ppermute | solution.py:20
  66.5 9.2 %collective-permute-start.22 = (bf16[128,512]{1,0:T(8,128)(2,1)S(1)}, bf16[128,512]{1,0:T(8,128)(2,1)S(1)}, u32[]{:S(2)}, u32[]{:S(2)}) collective-permute-start(bf16[128,512]{1,0:T(8,128)(2,1)S(1)} %add_convert_fusion.2.refs_8_), channel_id=1, source_target_pairs={{0,16},{8,24},{16,0},{24,8},{1,17},{9,25},{17,1},{25,9},{2,18},{10... | collective-permute-start | bytes 393224 | tf_op jit(solution)/shard_map/ppermute | solution.py:20
  72.4 14.9 %copy-start.24 = (bf16[128,512]{1,0:T(8,128)(2,1)}, bf16[128,512]{1,0:T(8,128)(2,1)S(1)}, u32[]{:S(2)}) copy-start(bf16[128,512]{1,0:T(8,128)(2,1)S(1)} %collective-permute-done.23.refs_11_) | copy-start | bytes 393220
  72.4 5.9 %collective-permute-start.21 = (bf16[128,512]{1,0:T(8,128)(2,1)S(1)}, bf16[128,512]{1,0:T(8,128)(2,1)S(1)}, u32[]{:S(2)}, u32[]{:S(2)}) collective-permute-start(bf16[128,512]{1,0:T(8,128)(2,1)S(1)} %add_convert_fusion.2.refs_8_), channel_id=1, source_target_pairs={{0,24},{8,0},{16,8},{24,16},{1,25},{9,1},{17,9},{25,17},{2,26},{10... | collective-permute-start | bytes 393224 | tf_op jit(solution)/shard_map/ppermute | solution.py:20
  75.7 11.6 %copy-start.25 = (bf16[128,512]{1,0:T(8,128)(2,1)}, bf16[128,512]{1,0:T(8,128)(2,1)S(1)}, u32[]{:S(2)}) copy-start(bf16[128,512]{1,0:T(8,128)(2,1)S(1)} %collective-permute-done.22.refs_10_) | copy-start | bytes 393220
  75.7 6.6 %collective-permute-start.26 = (bf16[512,128]{1,0:T(8,128)(2,1)S(1)}, bf16[512,128]{1,0:T(8,128)(2,1)S(1)}, u32[]{:S(2)}, u32[]{:S(2)}) collective-permute-start(bf16[512,128]{1,0:T(8,128)(2,1)S(1)} %pad_maximum_fusion.refs_12_), channel_id=1, source_target_pairs={{0,1},{1,2},{2,3},{3,0},{4,5},{5,6},{6,7},{7,4},{8,9},{9,10},{10,1... | collective-permute-start | bytes 393224 | tf_op jit(solution)/shard_map/ppermute | solution.py:20
  75.8 11.5 %copy-start.16 = (bf16[512,128]{1,0:T(8,128)(2,1)}, bf16[512,128]{1,0:T(8,128)(2,1)S(1)}, u32[]{:S(2)}) copy-start(bf16[512,128]{1,0:T(8,128)(2,1)S(1)} %fusion.8.refs_0_) | copy-start | bytes 393220
  78.2 9.1 %copy-start.26 = (bf16[128,512]{1,0:T(8,128)(2,1)}, bf16[128,512]{1,0:T(8,128)(2,1)S(1)}, u32[]{:S(2)}) copy-start(bf16[128,512]{1,0:T(8,128)(2,1)S(1)} %collective-permute-done.21.refs_9_) | copy-start | bytes 393220
  78.2 5.5 %collective-permute-start.25 = (bf16[512,128]{1,0:T(8,128)(2,1)S(1)}, bf16[512,128]{1,0:T(8,128)(2,1)S(1)}, u32[]{:S(2)}, u32[]{:S(2)}) collective-permute-start(bf16[512,128]{1,0:T(8,128)(2,1)S(1)} %pad_maximum_fusion.refs_12_), channel_id=1, source_target_pairs={{0,2},{1,3},{2,0},{3,1},{4,6},{5,7},{6,4},{7,5},{8,10},{9,11},{10,... | collective-permute-start | bytes 393224 | tf_op jit(solution)/shard_map/ppermute | solution.py:20
  78.6 8.8 %copy-start.20 = (bf16[640,256]{1,0:T(8,128)(2,1)}, bf16[640,256]{1,0:T(8,128)(2,1)S(1)}, u32[]{:S(2)}) copy-start(bf16[640,256]{1,0:T(8,128)(2,1)S(1)} %collective-permute-done.17.refs_7_) | copy-start | bytes 983044
  78.6 5.2 %collective-permute-start.24 = (bf16[512,128]{1,0:T(8,128)(2,1)S(1)}, bf16[512,128]{1,0:T(8,128)(2,1)S(1)}, u32[]{:S(2)}, u32[]{:S(2)}) collective-permute-start(bf16[512,128]{1,0:T(8,128)(2,1)S(1)} %pad_maximum_fusion.refs_12_), channel_id=1, source_target_pairs={{0,3},{1,0},{2,1},{3,2},{4,7},{5,4},{6,5},{7,6},{8,11},{9,8},{10,9... | collective-permute-start | bytes 393224 | tf_op jit(solution)/shard_map/ppermute | solution.py:20
  79.1 8.2 %copy-start.21 = (bf16[640,256]{1,0:T(8,128)(2,1)}, bf16[640,256]{1,0:T(8,128)(2,1)S(1)}, u32[]{:S(2)}) copy-start(bf16[640,256]{1,0:T(8,128)(2,1)S(1)} %collective-permute-done.16.refs_6_) | copy-start | bytes 983044
  79.1 7.1 %collective-permute-start.14 = (bf16[512,128]{1,0:T(8,128)(2,1)S(1)}, bf16[512,128]{1,0:T(8,128)(2,1)S(1)}, u32[]{:S(2)}, u32[]{:S(2)}) collective-permute-start(bf16[512,128]{1,0:T(8,128)(2,1)S(1)} %fusion.8.refs_0_), channel_id=1, source_target_pairs={{0,1},{1,2},{2,3},{3,0},{4,5},{5,6},{6,7},{7,4},{8,9},{9,10},{10,1... | collective-permute-start | bytes 393224 | tf_op jit(solution)/shard_map/ppermute | solution.py:20
  80.6 6.4 %collective-permute-start.13 = (bf16[512,128]{1,0:T(8,128)(2,1)S(1)}, bf16[512,128]{1,0:T(8,128)(2,1)S(1)}, u32[]{:S(2)}, u32[]{:S(2)}) collective-permute-start(bf16[512,128]{1,0:T(8,128)(2,1)S(1)} %fusion.8.refs_0_), channel_id=1, source_target_pairs={{0,2},{1,3},{2,0},{3,1},{4,6},{5,7},{6,4},{7,5},{8,10},{9,11},{10,... | collective-permute-start | bytes 393224 | tf_op jit(solution)/shard_map/ppermute | solution.py:20
  82.3 5.0 %collective-permute-start.12 = (bf16[512,128]{1,0:T(8,128)(2,1)S(1)}, bf16[512,128]{1,0:T(8,128)(2,1)S(1)}, u32[]{:S(2)}, u32[]{:S(2)}) collective-permute-start(bf16[512,128]{1,0:T(8,128)(2,1)S(1)} %fusion.8.refs_0_), channel_id=1, source_target_pairs={{0,3},{1,0},{2,1},{3,2},{4,7},{5,4},{6,5},{7,6},{8,11},{9,8},{10,9... | collective-permute-start | bytes 393224 | tf_op jit(solution)/shard_map/ppermute | solution.py:20
  93.5 3.0 %collective-permute-start.27 = (bf16[512,512]{1,0:T(8,128)(2,1)}, bf16[512,512]{1,0:T(8,128)(2,1)S(1)}, u32[]{:S(2)}, u32[]{:S(2)}) collective-permute-start(bf16[512,512]{1,0:T(8,128)(2,1)} %get-tuple-element.65), channel_id=1, source_target_pairs={{0,4},{1,5},{2,6},{3,7},{8,12},{9,13},{10,14},{11,15},{16,20},{17,... | collective-permute-start | bytes 1572872 | tf_op jit(solution)/shard_map/ppermute | solution.py:26
  102.0 4.0 %collective-permute-start.28 = (bf16[512,512]{1,0:T(8,128)(2,1)}, bf16[512,512]{1,0:T(8,128)(2,1)S(1)}, u32[]{:S(2)}, u32[]{:S(2)}) collective-permute-start(bf16[512,512]{1,0:T(8,128)(2,1)} %get-tuple-element.72), channel_id=1, source_target_pairs={{4,0},{5,1},{6,2},{7,3},{12,8},{13,9},{14,10},{15,11},{20,16},{21,... | collective-permute-start | bytes 1572872 | tf_op jit(solution)/shard_map/ppermute | solution.py:26
  115.3 21.9 %collective-permute-start.29 = (bf16[128,1024]{1,0:T(8,128)(2,1)}, bf16[128,1024]{1,0:T(8,128)(2,1)S(1)}, u32[]{:S(2)}, u32[]{:S(2)}) collective-permute-start(bf16[128,1024]{1,0:T(8,128)(2,1)} %get-tuple-element.81), channel_id=1, source_target_pairs={{0,8},{8,16},{16,24},{24,0},{1,9},{9,17},{17,25},{25,1},{2,10},{10... | collective-permute-start | bytes 786440 | tf_op jit(solution)/shard_map/ppermute | solution.py:20
  115.4 24.4 %collective-permute-start.30 = (bf16[128,1024]{1,0:T(8,128)(2,1)}, bf16[128,1024]{1,0:T(8,128)(2,1)S(1)}, u32[]{:S(2)}, u32[]{:S(2)}) collective-permute-start(bf16[128,1024]{1,0:T(8,128)(2,1)} %get-tuple-element.82), channel_id=1, source_target_pairs={{0,16},{8,24},{16,0},{24,8},{1,17},{9,25},{17,1},{25,9},{2,18},{10... | collective-permute-start | bytes 786440 | tf_op jit(solution)/shard_map/ppermute | solution.py:20
  120.1 19.6 %collective-permute-start.31 = (bf16[128,1024]{1,0:T(8,128)(2,1)}, bf16[128,1024]{1,0:T(8,128)(2,1)S(1)}, u32[]{:S(2)}, u32[]{:S(2)}) collective-permute-start(bf16[128,1024]{1,0:T(8,128)(2,1)} %get-tuple-element.83), channel_id=1, source_target_pairs={{0,24},{8,0},{16,8},{24,16},{1,25},{9,1},{17,9},{25,17},{2,26},{10... | collective-permute-start | bytes 786440 | tf_op jit(solution)/shard_map/ppermute | solution.py:20
  120.1 7.6 %copy-start.2 = (bf16[1,512,1024]{2,1,0:T(8,128)(2,1)S(1)}, bf16[1,512,1024]{2,1,0:T(8,128)(2,1)}, u32[]{:S(2)}) copy-start(bf16[1,512,1024]{2,1,0:T(8,128)(2,1)} %param.11) | copy-start | bytes 3145732
  125.3 15.4 %collective-permute-start.32 = (bf16[128,1024]{1,0:T(8,128)(2,1)}, bf16[128,1024]{1,0:T(8,128)(2,1)S(1)}, u32[]{:S(2)}, u32[]{:S(2)}) collective-permute-start(bf16[128,1024]{1,0:T(8,128)(2,1)} %get-tuple-element.93), channel_id=1, source_target_pairs={{0,1},{1,2},{2,3},{3,0},{4,5},{5,6},{6,7},{7,4},{8,9},{9,10},{10,1... | collective-permute-start | bytes 786440 | tf_op jit(solution)/shard_map/ppermute | solution.py:20
  126.3 14.4 %collective-permute-start.33 = (bf16[128,1024]{1,0:T(8,128)(2,1)}, bf16[128,1024]{1,0:T(8,128)(2,1)S(1)}, u32[]{:S(2)}, u32[]{:S(2)}) collective-permute-start(bf16[128,1024]{1,0:T(8,128)(2,1)} %get-tuple-element.94), channel_id=1, source_target_pairs={{0,2},{1,3},{2,0},{3,1},{4,6},{5,7},{6,4},{7,5},{8,10},{9,11},{10,... | collective-permute-start | bytes 786440 | tf_op jit(solution)/shard_map/ppermute | solution.py:20
  136.1 9.1 %copy-start.11 = (bf16[128,1024]{1,0:T(8,128)(2,1)S(1)}, bf16[128,1024]{1,0:T(8,128)(2,1)}, u32[]{:S(2)}) copy-start(bf16[128,1024]{1,0:T(8,128)(2,1)} %get-tuple-element.92) | copy-start | bytes 786436
  137.2 8.0 %collective-permute-start.34 = (bf16[128,1024]{1,0:T(8,128)(2,1)S(1)}, bf16[128,1024]{1,0:T(8,128)(2,1)S(1)}, u32[]{:S(2)}, u32[]{:S(2)}) collective-permute-start(bf16[128,1024]{1,0:T(8,128)(2,1)S(1)} %copy-done.23), channel_id=1, source_target_pairs={{0,3},{1,0},{2,1},{3,2},{4,7},{5,4},{6,5},{7,6},{8,11},{9,8},{10,9... | collective-permute-start | bytes 786440 | tf_op jit(solution)/shard_map/ppermute | solution.py:20
  (20 other events, 49.1 us)

commit v5 on v4

--- a/solution.py
+++ b/solution.py
@@ -15,9 +15,8 @@
 TN = ((0,), (0,))
 
 
-def shift(shard, axis, by):
-    devices = lax.axis_size(axis)
-    return lax.ppermute(shard, axis, [(i, (i + by) % devices) for i in range(devices)])
+def swap(shard, axis, by):
+    return lax.ppermute(shard, axis, [(i, i ^ by) for i in range(lax.axis_size(axis))])
 
 
 def move(shard, axis, by):
@@ -27,11 +26,34 @@
 
 
 def gathered(shard, axis):
-    return [shard] + [shift(shard, axis, -k) for k in range(1, lax.axis_size(axis))]
+    return [shard] + [swap(shard, axis, k) for k in range(1, lax.axis_size(axis))]
 
 
 def scattered(blocks, axis):
-    return [blocks[0]] + [shift(blocks[k], axis, k) for k in range(1, len(blocks))]
+    return [blocks[0]] + [swap(blocks[k], axis, k) for k in range(1, len(blocks))]
+
+
+def group_sum(rows, axis):
+    groups = lax.axis_size(axis)
+    size = rows.shape[0] // groups
+    step = groups // 2
+    while step:
+        other = swap(rows, axis, step)
+        other = [other[(k ^ step) * size : ((k ^ step) + 1) * size] for k in range(groups)]
+        rows = (rows.astype(f32) + jnp.concatenate(other).astype(f32)).astype(bf16)
+        step //= 2
+    return rows
+
+
+def halved_sum(kept, given, axis, size):
+    step = 1
+    while True:
+        kept = (kept.astype(f32) + swap(given, axis, step).astype(f32)).astype(bf16)
+        step *= 2
+        if step == lax.axis_size(axis):
+            return kept
+        blocks = [kept[at : at + size] for at in range(0, kept.shape[0], size)]
+        kept, given = jnp.concatenate(blocks[::2]), jnp.concatenate(blocks[1::2])
 
 
 def total(blocks):
@@ -92,16 +114,54 @@
 
 def gram_kernel(where, ins, outs, scratch):
     ((dec, recv, send, gain),) = ins
-    side, gram = outs
+    (whole,) = scratch
     codes, relay = dec.shape[0], recv.shape[0]
-    for ref, rows in ((dec, slice(0, codes)), (recv, slice(codes, codes + relay))):
+    cols = codes // len(outs)
+    wide = 2 * relay
+    head = cols * codes // wide
+    whole[...] = dot(dec[...], dec[...], NT)
+    for k, out in enumerate(outs):
+        rows = pl.ds(pl.multiple_of((where[0] ^ k) * cols, cols), cols)
+        for j in range(codes // wide):
+            piece = whole[rows, j * wide : (j + 1) * wide]
+            out[j * cols : (j + 1) * cols, :] = piece.astype(bf16)
+    for ref, rows in ((dec, slice(head, head + codes)), (recv, slice(head + codes, None))):
         values = ref[...]
         gained = (values.astype(f32) * gain[...]).astype(bf16)
-        side[rows, :relay] = dot(values, recv[...], NT).astype(bf16)
-        side[rows, relay:] = dot(gained, send[...], NN).astype(bf16)
-    rows = gram.shape[0]
-    mine = dec[pl.ds(pl.multiple_of(where[1] * rows, rows), rows), :]
-    gram[...] = dot(mine, dec[...], NT).astype(bf16)
+        plain = dot(values, recv[...], NT).astype(bf16)
+        scaled = dot(gained, send[...], NN).astype(bf16)
+        for out in outs:
+            out[rows, :relay] = plain
+            out[rows, relay:] = scaled
+
+
+def setup_kernel(where, ins, outs, scratch):
+    packs, ends = ins
+    payload, products, weights = outs
+    parts = len(packs)
+    wide = products.shape[1]
+    relay = wide // 2
+    codes = weights.shape[0]
+    cols = codes // parts
+    head = cols * codes // wide
+    for j in range(codes // wide):
+        rows = slice(j * cols, (j + 1) * cols)
+        gram = packs[0][rows, :].astype(f32)
+        for pack in packs[1:]:
+            gram = gram + pack[rows, :].astype(f32)
+        gram = gram.astype(bf16)
+        payload[2 * j * cols : (2 * j + 1) * cols, :] = gram[:, :relay]
+        payload[(2 * j + 1) * cols : (2 * j + 2) * cols, :] = gram[:, relay:]
+    start = 2 * head
+    for end in ends:
+        payload[start : start + end.shape[0], :] = end[...]
+        start += end.shape[0]
+    for k, pack in enumerate(packs):
+        here = slice(k * relay, (k + 1) * relay)
+        products[here, :] = pack[head + codes :, :]
+        weights[:, here] = pack[head : head + codes, :relay]
+        there = slice((parts + k) * relay, (parts + k + 1) * relay)
+        weights[:, there] = pack[head : head + codes, relay:]
 
 
 def fold_kernel(where, ins, outs, scratch):
@@ -121,7 +181,7 @@
         values = jnp.concatenate([h[...] for h in heads[first : first + together]])
         whole[...] = dot(values, fold[...], NN)
         for k in range(parts):
-            at = lax.rem(where[0] + k, parts) * cols
+            at = (where[0] ^ k) * cols
             outs[k][rows, :] = whole[:, pl.ds(pl.multiple_of(at, cols), cols)].astype(bf16)
 
 
@@ -154,26 +214,20 @@
 
 
 def first_kernel(width, where, ins, outs, scratch):
-    mix_blocks, sides, grams, end_blocks = ins
-    mix, ends, products, weights, mix_gram, mix_recv, mix_send, square, sent = outs
+    mix_blocks, payloads, (products, weights) = ins
+    mix, ends, mix_gram, mix_recv, mix_send, square, sent = outs
     (gram,) = scratch
     codes = mix.shape[1]
     relay = products.shape[1] // 2
     parts = len(mix_blocks)
     cols = codes // parts
     for k in range(parts):
-        at = lax.rem(where[0] + k, parts) * cols
-        mix[:, pl.ds(pl.multiple_of(at, cols), cols)] = mix_blocks[k][...]
-        here = slice(k * relay, (k + 1) * relay)
-        ends[:, here] = end_blocks[k][...]
-        products[here, :] = sides[k][codes:, :]
-        weights[:, here] = sides[k][:codes, :relay]
-        there = slice((parts + k) * relay, (parts + k + 1) * relay)
-        weights[:, there] = sides[k][:codes, relay:]
-    rows = grams[0].shape[0]
-    for k in range(len(grams)):
-        at = lax.rem(where[1] + k, len(grams)) * rows
-        gram[pl.ds(pl.multiple_of(at, rows), rows), :] = grams[k][...]
+        at = pl.multiple_of((where[0] ^ k) * cols, cols)
+        mix[:, pl.ds(at, cols)] = mix_blocks[k][...]
+        ends[:, k * relay : (k + 1) * relay] = payloads[k][cols * codes // relay :, :]
+        for j in range(codes // relay):
+            piece = payloads[k][j * cols : (j + 1) * cols, :]
+            gram[pl.ds(at, cols), j * relay : (j + 1) * relay] = piece
 
     def step(at):
         codes_here = mix[at, :]
@@ -217,12 +271,10 @@
     by_rows(moved.shape[0], step)
 
 
-def backward_kernel(width, live_section, last, where, ins, outs, scratch):
+def backward_kernel(width, live_section, last, tokens, where, ins, outs, scratch):
     (moved, incoming, received, mixed, unscaled, row_scale, mix_gram, products, weights, fold), = ins
     live = where[2] == live_section
     half = weights.shape[1] // 2
-    codes = weights.shape[0]
-    tokens = outs[4].shape[0] if last else 0
 
     def step(at):
         values = jnp.where(live, moved[at, :], incoming[at, :])
@@ -240,9 +292,13 @@
 
     by_rows(moved.shape[0], step)
     if last:
-        for k, out in enumerate(outs[4:]):
+        kept, given = outs[4:]
+        groups = 2 * kept.shape[0] // tokens
+        for k in range(groups):
             rows = slice(k * tokens, (k + 1) * tokens)
-            out[...] = dot(outs[3][rows, :], fold[...], NT).astype(bf16)
+            there = slice(k // 2 * tokens, (k // 2 + 1) * tokens)
+            term = dot(outs[3][rows, :], fold[...], NT).astype(bf16)
+            (given if k % 2 else kept)[there, :] = term
 
 
 def head_kernel(where, ins, outs, scratch):
@@ -261,8 +317,40 @@
     whole[...] = dot(head_sum[...], proj[...], NN)
     size = enc_blocks[0].shape[0]
     for k, out in enumerate(enc_blocks):
-        at = lax.rem(where[0] + k, len(enc_blocks)) * size
+        at = (where[0] ^ k) * size
         out[...] = whole[pl.ds(pl.multiple_of(at, size), size), :].astype(bf16)
+
+
+def proj_kernel(where, ins, outs, scratch):
+    ((head_sum, enc),) = ins
+    outs[0][...] = dot(head_sum[...], enc[...], TN).astype(bf16)
+
+
+def feature_kernel(where, ins, outs, scratch):
+    (mix, mix_cols, received, incoming, row_scale, inner, dec, recv, send, gain), = ins
+    sums = scratch
+    relay = recv.shape[0]
+    for ref in sums:
+        ref[...] = jnp.zeros_like(ref)
+
+    def step(at):
+        received_here = received[at, :relay]
+        incoming_here = incoming[at, :relay]
+        scale = row_scale[at, :]
+        mixed = dot(mix[at, :], dec[...], NN) + dot(received_here, recv[...], NN)
+        normed = mixed * scale
+        out_rows = (normed * gain[...]).astype(bf16)
+        grad_norm = dot(incoming_here, send[...], NT)
+        grad_mixed = scale * (grad_norm * gain[...] - normed * inner[at, :])
+        grad_mixed = grad_mixed.astype(bf16)
+        sums[0][...] += dot(mix_cols[at, :], grad_mixed, TN)
+        sums[1][...] += jnp.sum(grad_norm * normed, axis=0, keepdims=True)
+        sums[2][...] += dot(out_rows, incoming_here, TN)
+        sums[3][...] += dot(received_here, grad_mixed, TN)
+
+    by_rows(mix.shape[0], step)
+    for out, ref in zip(outs, sums):
+        out[...] = ref[...].astype(out.dtype)
 
 
 def on_device(
@@ -295,16 +383,18 @@
     where = jnp.stack([lax.axis_index("tensor"), lax.axis_index("dp"), section]).astype(jnp.int32)
 
     heads = gathered(heads_out[0], "dp")
-    side, gram = run(
+    end = jnp.where(section == 0, input_code, code_cotangent)
+    ends = gathered(end, "dp")
+    packs = run(
         gram_kernel,
-        [like((codes + relay, 2 * relay)), like((codes // groups, codes))],
+        [like((cols * codes // (2 * relay) + codes + relay, 2 * relay))] * parts,
         where,
         [(dec, recv, send, gain)],
+        scratch=[pltpu.VMEM((codes, codes), f32)],
     )
     (fold,) = run(fold_kernel, [like((head_cols, codes))], where, [(proj, enc)])
-    fold, side, gram = lax.optimization_barrier((fold, side, gram))
-    sides = gathered(side, "tensor")
-    grams = gathered(gram, "tensor")
+    fold, _ = lax.optimization_barrier((fold, packs[0]))
+    packs = scattered(packs, "tensor")
 
     partials = run(
         partial_kernel,
@@ -314,29 +404,28 @@
         scratch=[pltpu.VMEM((min(groups, 4) * tokens, codes), f32)],
         flops=2 * rows * head_cols * codes,
     )
-    end = jnp.where(section == 0, input_code, code_cotangent)
-    end = jnp.concatenate(gathered(end, "dp"))
-    gram = total(grams).astype(bf16)
-    grams = gathered(gram, "dp")
+    wide = parts * relay
+    payload, products, weights = run(
+        setup_kernel,
+        [
+            like((cols * codes // relay + rows, relay)),
+            like((wide, 2 * relay)),
+            like((codes, 2 * wide)),
+        ],
+        where,
+        [packs, ends],
+    )
     code_block = total(scattered(partials, "tensor")).astype(bf16)
-    end, code_block = lax.optimization_barrier((end, code_block))
-    others = gathered(code_block, "dp")
-    end_blocks = gathered(end, "tensor")
-    mix_block = code_block.astype(f32)
-    for k in range(1, groups):
-        other = others[k].astype(f32)
-        mix_block = mix_block + jnp.concatenate([other[-k * tokens :], other[: -k * tokens]])
-    mix_blocks = gathered(mix_block.astype(bf16), "tensor")
+    payload, code_block = lax.optimization_barrier((payload, code_block))
+    payloads = gathered(payload, "tensor")
+    mix_blocks = gathered(group_sum(code_block, "dp"), "tensor")
 
     square_flops = 2 * rows * codes * codes
-    wide = parts * relay
-    mix, ends, products, weights, mix_gram, mix_recv, mix_send, square, sent = run(
+    mix, ends, mix_gram, mix_recv, mix_send, square, sent = run(
         functools.partial(first_kernel, width),
         [
             like((rows, codes)),
             like((rows, wide)),
-            like((wide, 2 * relay)),
-            like((codes, 2 * wide)),
             like((rows, codes), f32),
             like((rows, wide), f32),
             like((rows, wide), f32),
@@ -344,7 +433,7 @@
             like((rows, wide)),
         ],
         where,
-        [mix_blocks, sides, grams, end_blocks],
+        [mix_blocks, payloads, (products, weights)],
         scratch=[pltpu.VMEM((codes, codes), bf16)],
         flops=3 * square_flops,
     )
@@ -370,10 +459,10 @@
         shapes = [like((rows, wide)), like((rows, wide))]
         if last:
             shapes += [like((rows, 1), f32), like((rows, codes))]
-            shapes += [like((tokens, head_cols))] * groups
+            shapes += [like((rows // 2, head_cols))] * 2
         moved = move(returned, "pipe", -1)
         results = run(
-            functools.partial(backward_kernel, width, sections - 1 - turn, last),
+            functools.partial(backward_kernel, width, sections - 1 - turn, last, tokens),
             shapes,
             where,
             [
@@ -393,9 +482,9 @@
             flops=3 * square_flops,
         )
         incoming, returned = results[:2]
-    inner, code_grad, *head_blocks = results[2:]
-
-    heads_grad = total(scattered(head_blocks, "dp")).astype(bf16)
+    inner, code_grad, kept, given = results[2:]
+
+    heads_grad = halved_sum(kept, given, "dp", tokens)
     head_sum, *enc_blocks = run(
         head_kernel,
         [like((codes, head_cols))] + [like((cols, model_cols))] * parts,
@@ -406,19 +495,29 @@
     )
     head_sum, mix, *enc_blocks = lax.optimization_barrier((head_sum, mix, *enc_blocks))
     enc_grad = total(scattered(enc_blocks, "tensor")).astype(bf16)
-    proj_grad = dot(head_sum, enc, TN).astype(bf16)
-
-    received_here = received[:, :relay]
-    incoming_here = incoming[:, :relay]
-    mixed = dot(mix, dec, NN) + dot(received_here, recv, NN)
-    normed = mixed * row_scale
-    out_rows = (normed * gain).astype(bf16)
-    grad_norm = dot(incoming_here, send, NT)
-    grad_mixed = (row_scale * (grad_norm * gain - normed * inner)).astype(bf16)
-    dec_grad = dot(block(mix, "dp", 1), grad_mixed, TN).astype(bf16)
-    gain_grad = jnp.sum(grad_norm * normed, axis=0)
-    send_grad = dot(out_rows, incoming_here, TN).astype(bf16)
-    recv_grad = dot(received_here, grad_mixed, TN).astype(bf16)
+    (proj_grad,) = run(proj_kernel, [like((head_cols, model_cols))], where, [(head_sum, enc)])
+    shapes = [(codes // groups, features), (1, features), (features, relay), (relay, features)]
+    dec_grad, gain_grad, send_grad, recv_grad = run(
+        feature_kernel,
+        [like(shape, f32 if k == 1 else bf16) for k, shape in enumerate(shapes)],
+        where,
+        [
+            (
+                mix,
+                block(mix, "dp", 1),
+                received,
+                incoming,
+                row_scale,
+                inner,
+                dec,
+                recv,
+                send,
+                gain,
+            )
+        ],
+        scratch=[pltpu.VMEM(shape, f32) for shape in shapes],
+    )
+    sent, returned, enc_grad = lax.optimization_barrier((sent, returned, enc_grad))
     return (
         sent[None, :tokens, :relay],
         returned[None, :tokens, :relay],
@@ -426,7 +525,7 @@
         proj_grad[None],
         enc_grad[None],
         dec_grad[None],
-        gain_grad[None],
+        gain_grad,
         send_grad[None],
         recv_grad[None],
     )

time: 147 us -> 140 us (0.952)
  starting transfers between devices: 64.5 us -> 32.8 us
  waiting for transfers between devices: 25.4 us -> 49.7 us
  Pallas kernels: 31.5 us -> 43.8 us
  matrix products: 9.48 us -> 0 us
  other arithmetic: 6.39 us -> 3.48 us
    ppermute x33 -> x25, starting transfers between devices: 61.9 us -> 30.1 us  [swap(): lax.ppermute(shard, axis, [(i, i ^ by) for i in range(lax.axis_size(axis))])]
    ppermute x33 -> x25, waiting for transfers between devices: 23.5 us -> 45.5 us  [swap(): lax.ppermute(shard, axis, [(i, i ^ by) for i in range(lax.axis_size(axis))])]
    pallas_call x7 -> x10, Pallas kernels: 31.5 us -> 43.8 us  [run(): pl.pallas_call(body, out_shape=[jax.ShapeDtypeStruct(r.shape, r.dtype) fo...]
    dot_general x7 -> x0, matrix products: 9.48 us -> none  [dot(): lax.dot_general(left, right, (over, ((), ())), preferred_element_type=f32)]
    ppermute x2, waiting for transfers between devices: 1.93 us -> 4.23 us  [move(): return lax.ppermute(shard, axis, pairs)]
    pallas_call x2 -> x0, other arithmetic: 2.18 us -> none  [run(): pl.pallas_call(body, out_shape=[jax.ShapeDtypeStruct(r.shape, r.dtype) fo...]
    dynamic_slice x0 -> x1, local copies, waits for them, and re-layouts: none -> 1.62 us  [block(): lax.dynamic_slice_in_dim(array, lax.axis_index(axis) * size, size, dim)]
    unnamed x66 -> x48, local copies, waits for them, and re-layouts: 4.98 us -> 5.32 us
  transfers between devices with their start and end apart: 35 -> 27, of which waited for: 13 -> 17; matrix products, arithmetic and copies ran while one was open for 11% -> 4% of each run, Pallas kernels for 11% -> 18%
where the time goes in v5:
time: 140 us; the launch traced here: 139 us
  waiting for transfers between devices  49.7 us (36%)
  Pallas kernels  43.8 us (31%)
  starting transfers between devices  32.8 us (23%)
  local copies, waits for them, and re-layouts  8.38 us (6%)
  other arithmetic  3.48 us (2%)
    ppermute x25, waiting for transfers between devices, swap(): lax.ppermute(shard, axis, [(i, i ^ by) for i in range(lax.axis_size(axis))])  45.5 us
    pallas_call x10, Pallas kernels, run(): pl.pallas_call(body, out_shape=[jax.ShapeDtypeStruct(r.shape, r.dtype) fo...  43.8 us
    ppermute x25, starting transfers between devices, swap(): lax.ppermute(shard, axis, [(i, i ^ by) for i in range(lax.axis_size(axis))])  30.1 us
    unnamed x48, local copies, waits for them, and re-layouts  5.32 us
    ppermute x2, waiting for transfers between devices, move(): return lax.ppermute(shard, axis, pairs)  4.23 us
  transfers between devices with their start and end apart: 27, of which 17 were waited for; matrix products, arithmetic and copies ran while one was open for 4% of the time, Pallas kernels for 18%

profile of v5, /device:TPU:0, one launch (start us, length us, event | category | flops | bytes accessed | tf_op | source)
XLA Modules:
  0.0 139.1 jit_solution(9705208419969974236)
XLA Ops:
  0.6 5.1 %collective-permute-start.8 = (bf16[128,1024]{1,0:T(8,128)(2,1)}, bf16[128,1024]{1,0:T(8,128)(2,1)S(1)}, u32[]{:S(2)}, u32[]{:S(2)}) collective-permute-start(bf16[128,1024]{1,0:T(8,128)(2,1)} %bitcast.31), channel_id=1, source_target_pairs={{0,24},{8,16},{16,8},{24,0},{1,25},{9,17},{17,9},{25,1},{2,26},{10... | collective-permute-start | bytes 786440 | tf_op jit(solution)/shard_map/ppermute | solution.py:19
  7.0 4.0 %shard_map.160 = (bf16[896,256]{1,0:T(8,128)(2,1)}, bf16[896,256]{1,0:T(8,128)(2,1)}, bf16[896,256]{1,0:T(8,128)(2,1)}, bf16[896,256]{1,0:T(8,128)(2,1)}) custom-call(s32[3]{0:T(128)} %pad_add_fusion.where_ref, bf16[512,1024]{1,0:T(8,128)(2,1)} %bitcast.22, bf16[128,1024]{1,0:T(8,128)(2,1)} %bitcast.27, bf16[1024,128]{1,0:T(8,128)(2,1)} %bitcast.29, ...), custom_call_target="tpu_custom_call" | custom-call | tf_op jit(solution)/shard_map/pallas_call | solution.py:88
  11.0 1.6 %collective-permute-start = (bf16[896,256]{1,0:T(8,128)(2,1)}, bf16[896,256]{1,0:T(8,128)(2,1)S(1)}, u32[]{:S(2)}, u32[]{:S(2)}) collective-permute-start(bf16[896,256]{1,0:T(8,128)(2,1)} %get-tuple-element.61), channel_id=1, source_target_pairs={{0,1},{1,0},{2,3},{3,2},{4,5},{5,4},{6,7},{7,6},{8,9},{9,8},{10,11... | collective-permute-start | bytes 1376264 | tf_op jit(solution)/shard_map/ppermute | solution.py:19
  12.7 1.5 %collective-permute-start.1 = (bf16[896,256]{1,0:T(8,128)(2,1)}, bf16[896,256]{1,0:T(8,128)(2,1)S(1)}, u32[]{:S(2)}, u32[]{:S(2)}) collective-permute-start(bf16[896,256]{1,0:T(8,128)(2,1)} %get-tuple-element.62), channel_id=1, source_target_pairs={{0,2},{1,3},{2,0},{3,1},{4,6},{5,7},{6,4},{7,5},{8,10},{9,11},{10,... | collective-permute-start | bytes 1376264 | tf_op jit(solution)/shard_map/ppermute | solution.py:19
  14.2 4.2 %shard_map.162.refs_4_.refs_9_ = bf16[1024,512]{1,0:T(8,128)(2,1)} custom-call(s32[3]{0:T(128)} %pad_add_fusion.where_ref, bf16[1024,1024]{1,0:T(8,128)(2,1)} %bitcast.24, bf16[512,1024]{1,0:T(8,128)(2,1)} %bitcast.20), custom_call_target="tpu_custom_call" | custom-call | tf_op jit(solution)/shard_map/pallas_call | solution.py:88
  18.8 9.5 %collective-permute-done.7.refs_2_ = bf16[128,1024]{1,0:T(8,128)(2,1)S(1)} collective-permute-done((bf16[128,1024]{1,0:T(8,128)(2,1)}, bf16[128,1024]{1,0:T(8,128)(2,1)S(1)}, u32[]{:S(2)}, u32[]{:S(2)}) %collective-permute-start.7) | collective-permute-done | bytes 262176 | tf_op jit(solution)/shard_map/ppermute | solution.py:19
  29.7 3.1 %shard_map.163 = (bf16[512,128]{1,0:T(8,128)(2,1)}, bf16[512,128]{1,0:T(8,128)(2,1)}, bf16[512,128]{1,0:T(8,128)(2,1)}, bf16[512,128]{1,0:T(8,128)(2,1)}) custom-call(s32[3]{0:T(128)} %pad_add_fusion.where_ref, bf16[128,1024]{1,0:T(8,128)(2,1)} %bitcast.34, bf16[128,1024]{1,0:T(8,128)(2,1)} %copy-done.8, bf16[128,1024]{1,0:T(8,128)(2,1)} %copy-done.7, ...), custom_call_target="tpu_custom_call" | custom-call | flops 536870912 | bytes 2621440 | tf_op jit(solution)/shard_map/pallas_call | solution.py:88
  32.8 1.5 %collective-permute-start.9 = (bf16[512,128]{1,0:T(8,128)(2,1)}, bf16[512,128]{1,0:T(8,128)(2,1)S(1)}, u32[]{:S(2)}, u32[]{:S(2)}) collective-permute-start(bf16[512,128]{1,0:T(8,128)(2,1)} %get-tuple-element.67), channel_id=1, source_target_pairs={{0,1},{1,0},{2,3},{3,2},{4,5},{5,4},{6,7},{7,6},{8,9},{9,8},{10,11... | collective-permute-start | bytes 393224 | tf_op jit(solution)/shard_map/ppermute | solution.py:19
  34.3 2.5 %collective-permute-start.5 = (bf16[128,128]{1,0:T(8,128)(2,1)S(1)}, bf16[128,128]{1,0:T(8,128)(2,1)S(1)}, u32[]{:S(2)}, u32[]{:S(2)}) collective-permute-start(bf16[128,128]{1,0:T(8,128)(2,1)S(1)} %broadcast_select_fusion.refs_4_), channel_id=1, source_target_pairs={{0,24},{8,16},{16,8},{24,0},{1,25},{9,17},{17,9},{25,1},{2,26},{10... | collective-permute-start | bytes 98312 | tf_op jit(solution)/shard_map/ppermute | solution.py:19
  36.8 3.2 %collective-permute-done.5.refs_7_ = bf16[128,128]{1,0:T(8,128)(2,1)S(1)} collective-permute-done((bf16[128,128]{1,0:T(8,128)(2,1)S(1)}, bf16[128,128]{1,0:T(8,128)(2,1)S(1)}, u32[]{:S(2)}, u32[]{:S(2)}) %collective-permute-start.5) | collective-permute-done | bytes 32800 | tf_op jit(solution)/shard_map/ppermute | solution.py:19
  40.1 1.5 %collective-permute-start.10 = (bf16[512,128]{1,0:T(8,128)(2,1)}, bf16[512,128]{1,0:T(8,128)(2,1)S(1)}, u32[]{:S(2)}, u32[]{:S(2)}) collective-permute-start(bf16[512,128]{1,0:T(8,128)(2,1)} %get-tuple-element.68), channel_id=1, source_target_pairs={{0,2},{1,3},{2,0},{3,1},{4,6},{5,7},{6,4},{7,5},{8,10},{9,11},{10,... | collective-permute-start | bytes 393224 | tf_op jit(solution)/shard_map/ppermute | solution.py:19
  42.1 3.5 %collective-permute-done.10 = bf16[512,128]{1,0:T(8,128)(2,1)S(1)} collective-permute-done((bf16[512,128]{1,0:T(8,128)(2,1)}, bf16[512,128]{1,0:T(8,128)(2,1)S(1)}, u32[]{:S(2)}, u32[]{:S(2)}) %collective-permute-start.10) | collective-permute-done | bytes 131104 | tf_op jit(solution)/shard_map/ppermute | solution.py:19
  45.6 2.1 %collective-permute-done.11 = bf16[512,128]{1,0:T(8,128)(2,1)S(1)} collective-permute-done((bf16[512,128]{1,0:T(8,128)(2,1)}, bf16[512,128]{1,0:T(8,128)(2,1)S(1)}, u32[]{:S(2)}, u32[]{:S(2)}) %collective-permute-start.11) | collective-permute-done | bytes 131104 | tf_op jit(solution)/shard_map/ppermute | solution.py:19
  48.4 1.0 add_convert_fusion.5
  49.4 1.0 collective-permute-done.4.refs_6_
  50.4 1.2 collective-permute-done.3.refs_5_
  52.5 0.8 copy-done.5
  53.3 2.9 %shard_map.161 = (bf16[1024,128]{1,0:T(8,128)(2,1)}, bf16[512,256]{1,0:T(8,128)(2,1)}, bf16[512,1024]{1,0:T(8,128)(2,1)}) custom-call(s32[3]{0:T(128)} %pad_add_fusion.where_ref, bf16[896,256]{1,0:T(8,128)(2,1)} %get-tuple-element.60.refs_0_, bf16[896,256]{1,0:T(8,128)(2,1)} %copy-done.3, bf16[896,256]{1,0:T(8,128)(2,1)} %copy-done.4, ...), custom_call_target="tpu_custom_call" | custom-call | tf_op jit(solution)/shard_map/pallas_call | solution.py:88
  56.3 1.0 collective-permute-start.12
  57.3 6.3 %collective-permute-done.12 = bf16[512,128]{1,0:T(8,128)(2,1)S(1)} collective-permute-done((bf16[512,128]{1,0:T(8,128)(2,1)S(1)}, bf16[512,128]{1,0:T(8,128)(2,1)S(1)}, u32[]{:S(2)}, u32[]{:S(2)}) %collective-permute-start.12) | collective-permute-done | bytes 131104 | tf_op jit(solution)/shard_map/ppermute | solution.py:19
  64.0 1.5 %collective-permute-start.19 = (bf16[1024,128]{1,0:T(8,128)(2,1)}, bf16[1024,128]{1,0:T(8,128)(2,1)S(1)}, u32[]{:S(2)}, u32[]{:S(2)}) collective-permute-start(bf16[1024,128]{1,0:T(8,128)(2,1)} %get-tuple-element.71.refs_4_), channel_id=1, source_target_pairs={{0,3},{1,2},{2,1},{3,0},{4,7},{5,6},{6,5},{7,4},{8,11},{9,10},{10,... | collective-permute-start | bytes 786440 | tf_op jit(solution)/shard_map/ppermute | solution.py:19
  66.0 1.5 %collective-permute-start.17 = (bf16[1024,128]{1,0:T(8,128)(2,1)}, bf16[1024,128]{1,0:T(8,128)(2,1)S(1)}, u32[]{:S(2)}, u32[]{:S(2)}) collective-permute-start(bf16[1024,128]{1,0:T(8,128)(2,1)} %get-tuple-element.71.refs_4_), channel_id=1, source_target_pairs={{0,1},{1,0},{2,3},{3,2},{4,5},{5,4},{6,7},{7,6},{8,9},{9,8},{10,11... | collective-permute-start | bytes 786440 | tf_op jit(solution)/shard_map/ppermute | solution.py:19
  67.5 1.1 collective-permute-done.13
  69.2 1.6 %collective-permute-start.15 = (bf16[512,128]{1,0:T(8,128)(2,1)S(1)}, bf16[512,128]{1,0:T(8,128)(2,1)S(1)}, u32[]{:S(2)}, u32[]{:S(2)}) collective-permute-start(bf16[512,128]{1,0:T(8,128)(2,1)S(1)} %add_convert_fusion.3.refs_0_), channel_id=1, source_target_pairs={{0,2},{1,3},{2,0},{3,1},{4,6},{5,7},{6,4},{7,5},{8,10},{9,11},{10,... | collective-permute-start | bytes 393224 | tf_op jit(solution)/shard_map/ppermute | solution.py:19
  70.8 2.0 %collective-permute-done.19.refs_7_ = bf16[1024,128]{1,0:T(8,128)(2,1)S(1)} collective-permute-done((bf16[1024,128]{1,0:T(8,128)(2,1)}, bf16[1024,128]{1,0:T(8,128)(2,1)S(1)}, u32[]{:S(2)}, u32[]{:S(2)}) %collective-permute-start.19) | collective-permute-done | bytes 262176 | tf_op jit(solution)/shard_map/ppermute | solution.py:19
  72.8 0.8 collective-permute-start.14
  73.6 1.9 %collective-permute-done.18.refs_6_ = bf16[1024,128]{1,0:T(8,128)(2,1)S(1)} collective-permute-done((bf16[1024,128]{1,0:T(8,128)(2,1)}, bf16[1024,128]{1,0:T(8,128)(2,1)S(1)}, u32[]{:S(2)}, u32[]{:S(2)}) %collective-permute-start.18) | collective-permute-done | bytes 262176 | tf_op jit(solution)/shard_map/ppermute | solution.py:19
  76.1 0.9 collective-permute-done.16.refs_3_
  77.0 1.2 collective-permute-done.15.refs_2_
  79.6 4.9 %shard_map.164 = (bf16[512,512]{1,0:T(8,128)(2,1)}, bf16[512,512]{1,0:T(8,128)(2,1)}, f32[512,512]{1,0:T(8,128)}, f32[512,512]{1,0:T(8,128)}, f32[512,512]{1,0:T...) custom-call(s32[3]{0:T(128)} %pad_add_fusion.where_ref, bf16[512,128]{1,0:T(8,128)(2,1)} %copy-done.11, ...), custom_call_target="tpu_custom_call" | custom-call | flops 805306368 | bytes 7604224 | tf_op jit(solution)/shard_map/pallas_call | solution.py:88
  84.5 1.3 collective-permute-start.20
  85.8 1.7 %collective-permute-done.20.refs_0_ = bf16[512,512]{1,0:T(8,128)(2,1)S(1)} collective-permute-done((bf16[512,512]{1,0:T(8,128)(2,1)}, bf16[512,512]{1,0:T(8,128)(2,1)S(1)}, u32[]{:S(2)}, u32[]{:S(2)}) %collective-permute-start.20) | collective-permute-done | bytes 524320 | tf_op jit(solution)/shard_map/ppermute | solution.py:25
  87.5 0.8 copy-done.1
  88.3 4.5 %shard_map.165 = (bf16[512,512]{1,0:T(8,128)(2,1)}, bf16[512,512]{1,0:T(8,128)(2,1)}, f32[512,512]{1,0:T(8,128)}, f32[512,512]{1,0:T(8,128)}, f32[512,1]{1,0:T(8,128)}, /*index=5*/bf16[512,512]{1,0:T(8,128)(2,1)}) custom-call(s32[3]{0:T(128)} %pad_add_fusion.where_ref, bf16[512,512]{1,0:T(8,128)(2,1)} %copy-done.1, ...), custom_call_target="tpu_custom_call" | custom-call | flops 268435456 | bytes 7606272 | tf_op jit(solution)/shard_map/pallas_call | solution.py:88
  92.8 1.5 %collective-permute-start.21 = (bf16[512,512]{1,0:T(8,128)(2,1)}, bf16[512,512]{1,0:T(8,128)(2,1)S(1)}, u32[]{:S(2)}, u32[]{:S(2)}) collective-permute-start(bf16[512,512]{1,0:T(8,128)(2,1)} %get-tuple-element.80), channel_id=1, source_target_pairs={{4,0},{5,1},{6,2},{7,3},{12,8},{13,9},{14,10},{15,11},{20,16},{21,... | collective-permute-start | bytes 1572872 | tf_op jit(solution)/shard_map/ppermute | solution.py:25
  94.3 2.5 %collective-permute-done.21.refs_0_ = bf16[512,512]{1,0:T(8,128)(2,1)S(1)} collective-permute-done((bf16[512,512]{1,0:T(8,128)(2,1)}, bf16[512,512]{1,0:T(8,128)(2,1)S(1)}, u32[]{:S(2)}, u32[]{:S(2)}) %collective-permute-start.21) | collective-permute-done | bytes 524320 | tf_op jit(solution)/shard_map/ppermute | solution.py:25
  97.6 6.2 %shard_map.166 = (bf16[512,512]{1,0:T(8,128)(2,1)}, bf16[512,512]{1,0:T(8,128)(2,1)}, f32[512,1]{1,0:T(8,128)}, bf16[512,512]{1,0:T(8,128)(2,1)}, bf16[256,1024]{1,0:T(8,128)(2,1)}, /*index=5*/bf16[256,1024]{1,0:T(8,128)(2,1)}) custom-call(s32[3]{0:T(128)} %pad_add_fusion.where_ref, bf16[512,512]{1,0:T(8,128)(2,1)} %copy-done.2, ...), custom_call_target="tpu_custom_call" | custom-call | flops 805306368 | bytes 9703424 | tf_op jit(solution)/shard_map/pallas_call | solution.py:88
  103.8 1.7 %collective-permute-start.25 = (bf16[256,1024]{1,0:T(8,128)(2,1)}, bf16[256,1024]{1,0:T(8,128)(2,1)S(1)}, u32[]{:S(2)}, u32[]{:S(2)}) collective-permute-start(bf16[256,1024]{1,0:T(8,128)(2,1)} %get-tuple-element.101), channel_id=1, source_target_pairs={{0,8},{8,0},{16,24},{24,16},{1,9},{9,1},{17,25},{25,17},{2,10},{10... | collective-permute-start | bytes 1572872 | tf_op jit(solution)/shard_map/ppermute | solution.py:19
  105.4 4.9 %shard_map.167 = (bf16[512,1024]{1,0:T(8,128)(2,1)}, bf16[128,1024]{1,0:T(8,128)(2,1)}, bf16[128,1024]{1,0:T(8,128)(2,1)}, bf16[128,1024]{1,0:T(8,128)(2,1)}, bf16[128,1024]{1,0:T(8,128)(2,1)}) custom-call(s32[3]{0:T(128)} %pad_add_fusion.where_ref, bf16[128,1024]{1,0:T(8,128)(2,1)} %bitcast.35, bf16[128,1024]{1,0:T(8,128)(2,1)} %copy-done.8, ...), custom_call_target="tpu_custom_call" | custom-call | flops 1610612736 | bytes 5767168 | tf_op jit(solution)/shard_map/pallas_call | solution.py:88
  110.9 1.4 collective-permute-start.23
  112.3 1.6 %collective-permute-start.24 = (bf16[128,1024]{1,0:T(8,128)(2,1)}, bf16[128,1024]{1,0:T(8,128)(2,1)S(1)}, u32[]{:S(2)}, u32[]{:S(2)}) collective-permute-start(bf16[128,1024]{1,0:T(8,128)(2,1)} %get-tuple-element.97), channel_id=1, source_target_pairs={{0,3},{1,2},{2,1},{3,0},{4,7},{5,6},{6,5},{7,4},{8,11},{9,10},{10,... | collective-permute-start | bytes 786440 | tf_op jit(solution)/shard_map/ppermute | solution.py:19
  113.8 4.2 %shard_map.168 = bf16[1024,1024]{1,0:T(8,128)(2,1)} custom-call(s32[3]{0:T(128)} %pad_add_fusion.where_ref, bf16[512,1024]{1,0:T(8,128)(2,1)} %get-tuple-element.102.refs_0_, bf16[512,1024]{1,0:T(8,128)(2,1)} %bitcast.21), custom_call_target="tpu_custom_call" | custom-call | tf_op jit(solution)/shard_map/pallas_call | solution.py:88
  118.0 1.6 %constant_dynamic-slice_fusion.refs_1_ = bf16[512,128]{1,0:T(8,128)(2,1)} fusion(bf16[512,512]{1,0:T(8,128)(2,1)} %get-tuple-element.104.refs_0_, s32[]{:T(128)S(6)} %select_n.13), kind=kLoop, calls=%fused_computation.11 | loop fusion | bytes 262148 | tf_op jit(solution)/shard_map/dynamic_slice | solution.py:68
  119.6 4.9 %shard_map.169 = (bf16[128,1024]{1,0:T(8,128)(2,1)}, f32[1,1024]{1,0:T(1,128)}, bf16[1024,128]{1,0:T(8,128)(2,1)}, bf16[128,1024]{1,0:T(8,128)(2,1)}) custom-call(s32[3]{0:T(128)} %pad_add_fusion.where_ref, bf16[512,512]{1,0:T(8,128)(2,1)} %get-tuple-element.104.refs_0_, bf16[512,128]{1,0:T(8,128)(2,1)} %constant_dynamic-slice_fusion.refs_1_, ...), custom_call_target="tpu_custom_call" | custom-call | tf_op jit(solution)/shard_map/pallas_call | solution.py:88
  124.7 1.0 collective-permute-start.26
  125.8 0.9 add_convert_fusion.2
  126.7 1.4 %slice_bitcast_fusion = (bf16[1,128,128]{2,1,0:T(8,128)(2,1)}, bf16[1,128,128]{2,1,0:T(8,128)(2,1)}) fusion(bf16[512,512]{1,0:T(8,128)(2,1)} %get-tuple-element.99, bf16[512,512]{1,0:T(8,128)(2,1)} %get-tuple-element.98), kind=kLoop, calls=%fused_computation.7 | loop fusion | bytes 131072 | tf_op jit(solution)/shard_map/broadcast_in_dim | solution.py:523
  128.1 10.2 %collective-permute-done.26 = bf16[128,1024]{1,0:T(8,128)(2,1)S(1)} collective-permute-done((bf16[128,1024]{1,0:T(8,128)(2,1)S(1)}, bf16[128,1024]{1,0:T(8,128)(2,1)S(1)}, u32[]{:S(2)}, u32[]{:S(2)}) %collective-permute-start.26) | collective-permute-done | bytes 262176 | tf_op jit(solution)/shard_map/ppermute | solution.py:19
  (77 shorter events, 10.9 us)
Async XLA Ops:
  0.6 17.7 %collective-permute-start.8 = (bf16[128,1024]{1,0:T(8,128)(2,1)}, bf16[128,1024]{1,0:T(8,128)(2,1)S(1)}, u32[]{:S(2)}, u32[]{:S(2)}) collective-permute-start(bf16[128,1024]{1,0:T(8,128)(2,1)} %bitcast.31), channel_id=1, source_target_pairs={{0,24},{8,16},{16,8},{24,0},{1,25},{9,17},{17,9},{25,1},{2,26},{10... | collective-permute-start | bytes 786440 | tf_op jit(solution)/shard_map/ppermute | solution.py:19
  5.8 22.5 %collective-permute-start.7 = (bf16[128,1024]{1,0:T(8,128)(2,1)}, bf16[128,1024]{1,0:T(8,128)(2,1)S(1)}, u32[]{:S(2)}, u32[]{:S(2)}) collective-permute-start(bf16[128,1024]{1,0:T(8,128)(2,1)} %bitcast.32), channel_id=1, source_target_pairs={{0,16},{8,24},{16,0},{24,8},{1,17},{9,25},{17,1},{25,9},{2,18},{10... | collective-permute-start | bytes 786440 | tf_op jit(solution)/shard_map/ppermute | solution.py:19
  5.8 22.5 %collective-permute-start.6 = (bf16[128,1024]{1,0:T(8,128)(2,1)}, bf16[128,1024]{1,0:T(8,128)(2,1)S(1)}, u32[]{:S(2)}, u32[]{:S(2)}) collective-permute-start(bf16[128,1024]{1,0:T(8,128)(2,1)} %bitcast.33), channel_id=1, source_target_pairs={{0,8},{8,0},{16,24},{24,16},{1,9},{9,1},{17,25},{25,17},{2,10},{10... | collective-permute-start | bytes 786440 | tf_op jit(solution)/shard_map/ppermute | solution.py:19
  11.0 40.6 %collective-permute-start = (bf16[896,256]{1,0:T(8,128)(2,1)}, bf16[896,256]{1,0:T(8,128)(2,1)S(1)}, u32[]{:S(2)}, u32[]{:S(2)}) collective-permute-start(bf16[896,256]{1,0:T(8,128)(2,1)} %get-tuple-element.61), channel_id=1, source_target_pairs={{0,1},{1,0},{2,3},{3,2},{4,5},{5,4},{6,7},{7,6},{8,9},{9,8},{10,11... | collective-permute-start | bytes 1376264 | tf_op jit(solution)/shard_map/ppermute | solution.py:19
  12.7 38.9 %collective-permute-start.1 = (bf16[896,256]{1,0:T(8,128)(2,1)}, bf16[896,256]{1,0:T(8,128)(2,1)S(1)}, u32[]{:S(2)}, u32[]{:S(2)}) collective-permute-start(bf16[896,256]{1,0:T(8,128)(2,1)} %get-tuple-element.62), channel_id=1, source_target_pairs={{0,2},{1,3},{2,0},{3,1},{4,6},{5,7},{6,4},{7,5},{8,10},{9,11},{10,... | collective-permute-start | bytes 1376264 | tf_op jit(solution)/shard_map/ppermute | solution.py:19
  14.2 4.2 %copy-start.17 = (bf16[896,256]{1,0:T(8,128)(2,1)S(1)}, bf16[896,256]{1,0:T(8,128)(2,1)}, u32[]{:S(2)}) copy-start(bf16[896,256]{1,0:T(8,128)(2,1)} %get-tuple-element.63) | copy-start | bytes 1376260
  18.4 15.9 %copy-start.15 = (bf16[128,128]{1,0:T(8,128)(2,1)S(1)}, bf16[128,128]{1,0:T(8,128)(2,1)}, u32[]{:S(2)}) copy-start(bf16[128,128]{1,0:T(8,128)(2,1)} %param.16) | copy-start | bytes 98308
  18.4 15.9 %copy-start.16 = (bf16[128,128]{1,0:T(8,128)(2,1)S(1)}, bf16[128,128]{1,0:T(8,128)(2,1)}, u32[]{:S(2)}) copy-start(bf16[128,128]{1,0:T(8,128)(2,1)} %param.17) | copy-start | bytes 98308
  18.4 9.9 %copy-start.6 = (bf16[128,1024]{1,0:T(8,128)(2,1)}, bf16[128,1024]{1,0:T(8,128)(2,1)S(1)}, u32[]{:S(2)}) copy-start(bf16[128,1024]{1,0:T(8,128)(2,1)S(1)} %collective-permute-done.8.refs_3_) | copy-start | bytes 786436
  18.4 33.2 %collective-permute-start.2 = (bf16[896,256]{1,0:T(8,128)(2,1)S(1)}, bf16[896,256]{1,0:T(8,128)(2,1)S(1)}, u32[]{:S(2)}, u32[]{:S(2)}) collective-permute-start(bf16[896,256]{1,0:T(8,128)(2,1)S(1)} %copy-done.17), channel_id=1, source_target_pairs={{0,3},{1,2},{2,1},{3,0},{4,7},{5,6},{6,5},{7,4},{8,11},{9,10},{10,... | collective-permute-start | bytes 1376264 | tf_op jit(solution)/shard_map/ppermute | solution.py:19
  28.3 0.7 copy-start.7
  32.8 8.8 %collective-permute-start.9 = (bf16[512,128]{1,0:T(8,128)(2,1)}, bf16[512,128]{1,0:T(8,128)(2,1)S(1)}, u32[]{:S(2)}, u32[]{:S(2)}) collective-permute-start(bf16[512,128]{1,0:T(8,128)(2,1)} %get-tuple-element.67), channel_id=1, source_target_pairs={{0,1},{1,0},{2,3},{3,2},{4,5},{5,4},{6,7},{7,6},{8,9},{9,8},{10,11... | collective-permute-start | bytes 393224 | tf_op jit(solution)/shard_map/ppermute | solution.py:19
  34.3 17.3 %copy-start.10 = (bf16[128,128]{1,0:T(8,128)(2,1)}, bf16[128,128]{1,0:T(8,128)(2,1)S(1)}, u32[]{:S(2)}) copy-start(bf16[128,128]{1,0:T(8,128)(2,1)S(1)} %broadcast_select_fusion.refs_4_) | copy-start | bytes 98308
  34.3 5.8 %collective-permute-start.5 = (bf16[128,128]{1,0:T(8,128)(2,1)S(1)}, bf16[128,128]{1,0:T(8,128)(2,1)S(1)}, u32[]{:S(2)}, u32[]{:S(2)}) collective-permute-start(bf16[128,128]{1,0:T(8,128)(2,1)S(1)} %broadcast_select_fusion.refs_4_), channel_id=1, source_target_pairs={{0,24},{8,16},{16,8},{24,0},{1,25},{9,17},{17,9},{25,1},{2,26},{10... | collective-permute-start | bytes 98312 | tf_op jit(solution)/shard_map/ppermute | solution.py:19
  40.1 11.6 %copy-start.12 = (bf16[128,128]{1,0:T(8,128)(2,1)}, bf16[128,128]{1,0:T(8,128)(2,1)S(1)}, u32[]{:S(2)}) copy-start(bf16[128,128]{1,0:T(8,128)(2,1)S(1)} %collective-permute-done.5.refs_7_) | copy-start | bytes 98308
  40.1 5.5 %collective-permute-start.10 = (bf16[512,128]{1,0:T(8,128)(2,1)}, bf16[512,128]{1,0:T(8,128)(2,1)S(1)}, u32[]{:S(2)}, u32[]{:S(2)}) collective-permute-start(bf16[512,128]{1,0:T(8,128)(2,1)} %get-tuple-element.68), channel_id=1, source_target_pairs={{0,2},{1,3},{2,0},{3,1},{4,6},{5,7},{6,4},{7,5},{8,10},{9,11},{10,... | collective-permute-start | bytes 393224 | tf_op jit(solution)/shard_map/ppermute | solution.py:19
  41.6 6.1 %collective-permute-start.11 = (bf16[512,128]{1,0:T(8,128)(2,1)}, bf16[512,128]{1,0:T(8,128)(2,1)S(1)}, u32[]{:S(2)}, u32[]{:S(2)}) collective-permute-start(bf16[512,128]{1,0:T(8,128)(2,1)} %get-tuple-element.69), channel_id=1, source_target_pairs={{0,3},{1,2},{2,1},{3,0},{4,7},{5,6},{6,5},{7,4},{8,11},{9,10},{10,... | collective-permute-start | bytes 393224 | tf_op jit(solution)/shard_map/ppermute | solution.py:19
  45.5 4.8 %collective-permute-start.4 = (bf16[128,128]{1,0:T(8,128)(2,1)S(1)}, bf16[128,128]{1,0:T(8,128)(2,1)S(1)}, u32[]{:S(2)}, u32[]{:S(2)}) collective-permute-start(bf16[128,128]{1,0:T(8,128)(2,1)S(1)} %broadcast_select_fusion.refs_4_), channel_id=1, source_target_pairs={{0,16},{8,24},{16,0},{24,8},{1,17},{9,25},{17,1},{25,9},{2,18},{10... | collective-permute-start | bytes 98312 | tf_op jit(solution)/shard_map/ppermute | solution.py:19
  47.7 3.9 %collective-permute-start.3 = (bf16[128,128]{1,0:T(8,128)(2,1)S(1)}, bf16[128,128]{1,0:T(8,128)(2,1)S(1)}, u32[]{:S(2)}, u32[]{:S(2)}) collective-permute-start(bf16[128,128]{1,0:T(8,128)(2,1)S(1)} %broadcast_select_fusion.refs_4_), channel_id=1, source_target_pairs={{0,8},{8,0},{16,24},{24,16},{1,9},{9,1},{17,25},{25,17},{2,10},{10... | collective-permute-start | bytes 98312 | tf_op jit(solution)/shard_map/ppermute | solution.py:19
  50.4 1.3 copy-start.13
  51.6 0.8 copy-start.3
  51.6 0.9 copy-start.4
  52.5 0.8 copy-start.5
  56.3 7.3 %collective-permute-start.12 = (bf16[512,128]{1,0:T(8,128)(2,1)S(1)}, bf16[512,128]{1,0:T(8,128)(2,1)S(1)}, u32[]{:S(2)}, u32[]{:S(2)}) collective-permute-start(bf16[512,128]{1,0:T(8,128)(2,1)S(1)} %add_convert_fusion.5), channel_id=1, source_target_pairs={{0,16},{8,24},{16,0},{24,8},{1,17},{9,25},{17,1},{25,9},{2,18},{10... | collective-permute-start | bytes 393224 | tf_op jit(solution)/shard_map/ppermute | solution.py:19
  63.6 5.0 %collective-permute-start.13 = (bf16[512,128]{1,0:T(8,128)(2,1)S(1)}, bf16[512,128]{1,0:T(8,128)(2,1)S(1)}, u32[]{:S(2)}, u32[]{:S(2)}) collective-permute-start(bf16[512,128]{1,0:T(8,128)(2,1)S(1)} %add_convert_fusion.4), channel_id=1, source_target_pairs={{0,8},{8,0},{16,24},{24,16},{1,9},{9,1},{17,25},{25,17},{2,10},{10... | collective-permute-start | bytes 393224 | tf_op jit(solution)/shard_map/ppermute | solution.py:19
  64.0 8.7 %collective-permute-start.19 = (bf16[1024,128]{1,0:T(8,128)(2,1)}, bf16[1024,128]{1,0:T(8,128)(2,1)S(1)}, u32[]{:S(2)}, u32[]{:S(2)}) collective-permute-start(bf16[1024,128]{1,0:T(8,128)(2,1)} %get-tuple-element.71.refs_4_), channel_id=1, source_target_pairs={{0,3},{1,2},{2,1},{3,0},{4,7},{5,6},{6,5},{7,4},{8,11},{9,10},{10,... | collective-permute-start | bytes 786440 | tf_op jit(solution)/shard_map/ppermute | solution.py:19
  65.5 9.9 %collective-permute-start.18 = (bf16[1024,128]{1,0:T(8,128)(2,1)}, bf16[1024,128]{1,0:T(8,128)(2,1)S(1)}, u32[]{:S(2)}, u32[]{:S(2)}) collective-permute-start(bf16[1024,128]{1,0:T(8,128)(2,1)} %get-tuple-element.71.refs_4_), channel_id=1, source_target_pairs={{0,2},{1,3},{2,0},{3,1},{4,6},{5,7},{6,4},{7,5},{8,10},{9,11},{10,... | collective-permute-start | bytes 786440 | tf_op jit(solution)/shard_map/ppermute | solution.py:19
  66.0 10.0 %collective-permute-start.17 = (bf16[1024,128]{1,0:T(8,128)(2,1)}, bf16[1024,128]{1,0:T(8,128)(2,1)S(1)}, u32[]{:S(2)}, u32[]{:S(2)}) collective-permute-start(bf16[1024,128]{1,0:T(8,128)(2,1)} %get-tuple-element.71.refs_4_), channel_id=1, source_target_pairs={{0,1},{1,0},{2,3},{3,2},{4,5},{5,4},{6,7},{7,6},{8,9},{9,8},{10,11... | collective-permute-start | bytes 786440 | tf_op jit(solution)/shard_map/ppermute | solution.py:19
  68.7 10.2 %copy-start.11 = (bf16[512,128]{1,0:T(8,128)(2,1)}, bf16[512,128]{1,0:T(8,128)(2,1)S(1)}, u32[]{:S(2)}) copy-start(bf16[512,128]{1,0:T(8,128)(2,1)S(1)} %add_convert_fusion.3.refs_0_) | copy-start | bytes 393220
  68.7 8.3 %collective-permute-start.16 = (bf16[512,128]{1,0:T(8,128)(2,1)S(1)}, bf16[512,128]{1,0:T(8,128)(2,1)S(1)}, u32[]{:S(2)}, u32[]{:S(2)}) collective-permute-start(bf16[512,128]{1,0:T(8,128)(2,1)S(1)} %add_convert_fusion.3.refs_0_), channel_id=1, source_target_pairs={{0,3},{1,2},{2,1},{3,0},{4,7},{5,6},{6,5},{7,4},{8,11},{9,10},{10,... | collective-permute-start | bytes 393224 | tf_op jit(solution)/shard_map/ppermute | solution.py:19
  69.2 9.1 %collective-permute-start.15 = (bf16[512,128]{1,0:T(8,128)(2,1)S(1)}, bf16[512,128]{1,0:T(8,128)(2,1)S(1)}, u32[]{:S(2)}, u32[]{:S(2)}) collective-permute-start(bf16[512,128]{1,0:T(8,128)(2,1)S(1)} %add_convert_fusion.3.refs_0_), channel_id=1, source_target_pairs={{0,2},{1,3},{2,0},{3,1},{4,6},{5,7},{6,4},{7,5},{8,10},{9,11},{10,... | collective-permute-start | bytes 393224 | tf_op jit(solution)/shard_map/ppermute | solution.py:19
  72.8 6.2 %copy-start.18 = (bf16[1024,128]{1,0:T(8,128)(2,1)}, bf16[1024,128]{1,0:T(8,128)(2,1)S(1)}, u32[]{:S(2)}) copy-start(bf16[1024,128]{1,0:T(8,128)(2,1)S(1)} %collective-permute-done.19.refs_7_) | copy-start | bytes 786436
  72.8 6.2 %collective-permute-start.14 = (bf16[512,128]{1,0:T(8,128)(2,1)S(1)}, bf16[512,128]{1,0:T(8,128)(2,1)S(1)}, u32[]{:S(2)}, u32[]{:S(2)}) collective-permute-start(bf16[512,128]{1,0:T(8,128)(2,1)S(1)} %add_convert_fusion.3.refs_0_), channel_id=1, source_target_pairs={{0,1},{1,0},{2,3},{3,2},{4,5},{5,4},{6,7},{7,6},{8,9},{9,8},{10,11... | collective-permute-start | bytes 393224 | tf_op jit(solution)/shard_map/ppermute | solution.py:19
  75.4 3.5 %copy-start.19 = (bf16[1024,128]{1,0:T(8,128)(2,1)}, bf16[1024,128]{1,0:T(8,128)(2,1)S(1)}, u32[]{:S(2)}) copy-start(bf16[1024,128]{1,0:T(8,128)(2,1)S(1)} %collective-permute-done.18.refs_6_) | copy-start | bytes 786436
  76.1 2.9 %copy-start.20 = (bf16[1024,128]{1,0:T(8,128)(2,1)}, bf16[1024,128]{1,0:T(8,128)(2,1)S(1)}, u32[]{:S(2)}) copy-start(bf16[1024,128]{1,0:T(8,128)(2,1)S(1)} %collective-permute-done.17.refs_5_) | copy-start | bytes 786436
  77.0 1.9 %copy-start.21 = (bf16[512,128]{1,0:T(8,128)(2,1)}, bf16[512,128]{1,0:T(8,128)(2,1)S(1)}, u32[]{:S(2)}) copy-start(bf16[512,128]{1,0:T(8,128)(2,1)S(1)} %collective-permute-done.16.refs_3_) | copy-start | bytes 393220
  78.2 0.7 copy-start.22
  84.5 3.0 %collective-permute-start.20 = (bf16[512,512]{1,0:T(8,128)(2,1)}, bf16[512,512]{1,0:T(8,128)(2,1)S(1)}, u32[]{:S(2)}, u32[]{:S(2)}) collective-permute-start(bf16[512,512]{1,0:T(8,128)(2,1)} %get-tuple-element.74), channel_id=1, source_target_pairs={{0,4},{1,5},{2,6},{3,7},{8,12},{9,13},{10,14},{11,15},{16,20},{17,... | collective-permute-start | bytes 1572872 | tf_op jit(solution)/shard_map/ppermute | solution.py:25
  87.5 0.8 copy-start.1
  92.8 4.0 %collective-permute-start.21 = (bf16[512,512]{1,0:T(8,128)(2,1)}, bf16[512,512]{1,0:T(8,128)(2,1)S(1)}, u32[]{:S(2)}, u32[]{:S(2)}) collective-permute-start(bf16[512,512]{1,0:T(8,128)(2,1)} %get-tuple-element.80), channel_id=1, source_target_pairs={{4,0},{5,1},{6,2},{7,3},{12,8},{13,9},{14,10},{15,11},{20,16},{21,... | collective-permute-start | bytes 1572872 | tf_op jit(solution)/shard_map/ppermute | solution.py:25
  96.8 0.8 copy-start.2
  103.8 20.7 %collective-permute-start.25 = (bf16[256,1024]{1,0:T(8,128)(2,1)}, bf16[256,1024]{1,0:T(8,128)(2,1)S(1)}, u32[]{:S(2)}, u32[]{:S(2)}) collective-permute-start(bf16[256,1024]{1,0:T(8,128)(2,1)} %get-tuple-element.101), channel_id=1, source_target_pairs={{0,8},{8,0},{16,24},{24,16},{1,9},{9,1},{17,25},{25,17},{2,10},{10... | collective-permute-start | bytes 1572872 | tf_op jit(solution)/shard_map/ppermute | solution.py:19
  110.3 15.4 %collective-permute-start.22 = (bf16[128,1024]{1,0:T(8,128)(2,1)}, bf16[128,1024]{1,0:T(8,128)(2,1)S(1)}, u32[]{:S(2)}, u32[]{:S(2)}) collective-permute-start(bf16[128,1024]{1,0:T(8,128)(2,1)} %get-tuple-element.95), channel_id=1, source_target_pairs={{0,1},{1,0},{2,3},{3,2},{4,5},{5,4},{6,7},{7,6},{8,9},{9,8},{10,11... | collective-permute-start | bytes 786440 | tf_op jit(solution)/shard_map/ppermute | solution.py:19
  110.9 14.9 %collective-permute-start.23 = (bf16[128,1024]{1,0:T(8,128)(2,1)}, bf16[128,1024]{1,0:T(8,128)(2,1)S(1)}, u32[]{:S(2)}, u32[]{:S(2)}) collective-permute-start(bf16[128,1024]{1,0:T(8,128)(2,1)} %get-tuple-element.96), channel_id=1, source_target_pairs={{0,2},{1,3},{2,0},{3,1},{4,6},{5,7},{6,4},{7,5},{8,10},{9,11},{10,... | collective-permute-start | bytes 786440 | tf_op jit(solution)/shard_map/ppermute | solution.py:19
  112.3 13.5 %collective-permute-start.24 = (bf16[128,1024]{1,0:T(8,128)(2,1)}, bf16[128,1024]{1,0:T(8,128)(2,1)S(1)}, u32[]{:S(2)}, u32[]{:S(2)}) collective-permute-start(bf16[128,1024]{1,0:T(8,128)(2,1)} %get-tuple-element.97), channel_id=1, source_target_pairs={{0,3},{1,2},{2,1},{3,0},{4,7},{5,6},{6,5},{7,4},{8,11},{9,10},{10,... | collective-permute-start | bytes 786440 | tf_op jit(solution)/shard_map/ppermute | solution.py:19
  118.0 6.5 %copy-start = (bf16[256,1024]{1,0:T(8,128)(2,1)S(1)}, bf16[256,1024]{1,0:T(8,128)(2,1)}, u32[]{:S(2)}) copy-start(bf16[256,1024]{1,0:T(8,128)(2,1)} %get-tuple-element.100) | copy-start | bytes 1572868
  119.6 6.2 %copy-start.9 = (bf16[128,1024]{1,0:T(8,128)(2,1)S(1)}, bf16[128,1024]{1,0:T(8,128)(2,1)}, u32[]{:S(2)}) copy-start(bf16[128,1024]{1,0:T(8,128)(2,1)} %get-tuple-element.94) | copy-start | bytes 786436
  124.7 13.6 %collective-permute-start.26 = (bf16[128,1024]{1,0:T(8,128)(2,1)S(1)}, bf16[128,1024]{1,0:T(8,128)(2,1)S(1)}, u32[]{:S(2)}, u32[]{:S(2)}) collective-permute-start(bf16[128,1024]{1,0:T(8,128)(2,1)S(1)} %slice.51), channel_id=1, source_target_pairs={{0,16},{8,24},{16,0},{24,8},{1,17},{9,25},{17,1},{25,9},{2,18},{10... | collective-permute-start | bytes 786440 | tf_op jit(solution)/shard_map/ppermute | solution.py:19
  (3 other events, 2.0 us)

commit v6 on v5

--- a/solution.py
+++ b/solution.py
@@ -45,13 +45,15 @@
     return rows
 
 
-def halved_sum(kept, given, axis, size):
+def halved_sum(kept, given, after, axis, size):
     step = 1
     while True:
         kept = (kept.astype(f32) + swap(given, axis, step).astype(f32)).astype(bf16)
+        if step == 1:
+            kept, after = lax.optimization_barrier((kept, after))
         step *= 2
         if step == lax.axis_size(axis):
-            return kept
+            return kept, after
         blocks = [kept[at : at + size] for at in range(0, kept.shape[0], size)]
         kept, given = jnp.concatenate(blocks[::2]), jnp.concatenate(blocks[1::2])
 
@@ -84,7 +86,7 @@
             at += count
         kernel(where_ref, ins, refs[at : at + out_count], refs[at + out_count :])
 
-    size = sum(a.size * a.dtype.itemsize for a in list(flat) + list(results)) if flops else 0
+    size = sum(a.size * a.dtype.itemsize for a in list(flat) + list(results))
     return pl.pallas_call(
         body,
         out_shape=[jax.ShapeDtypeStruct(r.shape, r.dtype) for r in results],
@@ -92,8 +94,8 @@
         + [pl.BlockSpec(memory_space=pltpu.VMEM)] * len(flat),
         out_specs=[pl.BlockSpec(memory_space=pltpu.VMEM)] * out_count,
         scratch_shapes=list(scratch),
-        compiler_params=pltpu.CompilerParams(vmem_limit_bytes=56 << 20),
-        cost_estimate=pl.CostEstimate(flops=flops, bytes_accessed=size, transcendentals=0),
+        compiler_params=pltpu.CompilerParams(vmem_limit_bytes=size + (12 << 20)),
+        cost_estimate=pl.CostEstimate(flops=flops, bytes_accessed=size if flops else 0, transcendentals=0),
     )(where, *flat)
 
 
@@ -392,6 +394,7 @@
         [(dec, recv, send, gain)],
         scratch=[pltpu.VMEM((codes, codes), f32)],
     )
+    enc, *_ = lax.optimization_barrier((enc, *ends))
     (fold,) = run(fold_kernel, [like((head_cols, codes))], where, [(proj, enc)])
     fold, _ = lax.optimization_barrier((fold, packs[0]))
     packs = scattered(packs, "tensor")
@@ -415,10 +418,13 @@
         where,
         [packs, ends],
     )
-    code_block = total(scattered(partials, "tensor")).astype(bf16)
-    payload, code_block = lax.optimization_barrier((payload, code_block))
+    arrived = scattered(partials, "tensor")
+    arrived, *_ = lax.optimization_barrier((arrived, *packs))
+    code_block = total(arrived).astype(bf16)
     payloads = gathered(payload, "tensor")
-    mix_blocks = gathered(group_sum(code_block, "dp"), "tensor")
+    mix_block = group_sum(code_block, "dp")
+    mix_block, *_ = lax.optimization_barrier((mix_block, *payloads))
+    mix_blocks = gathered(mix_block, "tensor")
 
     square_flops = 2 * rows * codes * codes
     mix, ends, mix_gram, mix_recv, mix_send, square, sent = run(
@@ -484,7 +490,7 @@
         incoming, returned = results[:2]
     inner, code_grad, kept, given = results[2:]
 
-    heads_grad = halved_sum(kept, given, "dp", tokens)
+    heads_grad, row_scale = halved_sum(kept, given, row_scale, "dp", tokens)
     head_sum, *enc_blocks = run(
         head_kernel,
         [like((codes, head_cols))] + [like((cols, model_cols))] * parts,

time: 140 us -> 143 us (1.021)
  Pallas kernels: 43.8 us -> 22.6 us
  starting transfers between devices: 32.8 us -> 48.8 us
  local copies, waits for them, and re-layouts: 8.38 us -> 17.3 us
    pallas_call x10, Pallas kernels: 43.8 us -> 22.6 us  [run(): pl.pallas_call(body, out_shape=[jax.ShapeDtypeStruct(r.shape, r.dtype) fo...]
    ppermute x25, starting transfers between devices: 30.1 us -> 46 us  [swap(): lax.ppermute(shard, axis, [(i, i ^ by) for i in range(lax.axis_size(axis))])]
    unnamed x48 -> x66, local copies, waits for them, and re-layouts: 5.32 us -> 15.8 us
    dynamic_slice x1, local copies, waits for them, and re-layouts: 1.62 us -> 0.03 us  [block(): lax.dynamic_slice_in_dim(array, lax.axis_index(axis) * size, size, dim)]
  transfers between devices with their start and end apart: 27 -> 27, of which waited for: 17 -> 15; matrix products, arithmetic and copies ran while one was open for 4% -> 3% of each run, Pallas kernels for 18% -> 11%
where the time goes in v6:
time: 143 us; the launch traced here: 142 us
  starting transfers between devices  48.8 us (34%)
  waiting for transfers between devices  48.6 us (34%)
  Pallas kernels  22.6 us (16%)
  local copies, waits for them, and re-layouts  17.3 us (12%)
  other arithmetic  4.02 us (3%)
    ppermute x25, starting transfers between devices, swap(): lax.ppermute(shard, axis, [(i, i ^ by) for i in range(lax.axis_size(axis))])  46 us
    ppermute x25, waiting for transfers between devices, swap(): lax.ppermute(shard, axis, [(i, i ^ by) for i in range(lax.axis_size(axis))])  44.8 us
    pallas_call x10, Pallas kernels, run(): pl.pallas_call(body, out_shape=[jax.ShapeDtypeStruct(r.shape, r.dtype) fo...  22.6 us
    unnamed x66, local copies, waits for them, and re-layouts  15.8 us
    ppermute x2, waiting for transfers between devices, move(): return lax.ppermute(shard, axis, pairs)  3.81 us
  transfers between devices with their start and end apart: 27, of which 15 were waited for; matrix products, arithmetic and copies ran while one was open for 3% of the time, Pallas kernels for 11%

profile of v6, /device:TPU:0, one launch (start us, length us, event | category | flops | bytes accessed | tf_op | source)
XLA Modules:
  0.0 142.3 jit_solution(13014701466241525225)
XLA Ops:
  0.7 5.1 %collective-permute-start.2 = (bf16[128,1024]{1,0:T(8,128)(2,1)}, bf16[128,1024]{1,0:T(8,128)(2,1)S(1)}, u32[]{:S(2)}, u32[]{:S(2)}) collective-permute-start(bf16[128,1024]{1,0:T(8,128)(2,1)} %bitcast.30), channel_id=1, source_target_pairs={{0,24},{8,16},{16,8},{24,0},{1,25},{9,17},{17,9},{25,1},{2,26},{10... | collective-permute-start | bytes 786440 | tf_op jit(solution)/shard_map/ppermute | solution.py:19
  7.5 3.4 %collective-permute-start = (bf16[128,1024]{1,0:T(8,128)(2,1)}, bf16[128,1024]{1,0:T(8,128)(2,1)S(1)}, u32[]{:S(2)}, u32[]{:S(2)}) collective-permute-start(bf16[128,1024]{1,0:T(8,128)(2,1)} %bitcast.32), channel_id=1, source_target_pairs={{0,8},{8,0},{16,24},{24,16},{1,9},{9,1},{17,25},{25,17},{2,10},{10... | collective-permute-start | bytes 786440 | tf_op jit(solution)/shard_map/ppermute | solution.py:19
  10.9 3.0 %collective-permute-done.5.refs_7_ = bf16[128,128]{1,0:T(8,128)(2,1)S(1)} collective-permute-done((bf16[128,128]{1,0:T(8,128)(2,1)S(1)}, bf16[128,128]{1,0:T(8,128)(2,1)S(1)}, u32[]{:S(2)}, u32[]{:S(2)}) %collective-permute-start.5) | collective-permute-done | bytes 32800 | tf_op jit(solution)/shard_map/ppermute | solution.py:19
  13.9 12.4 %collective-permute-start.3 = (bf16[128,128]{1,0:T(8,128)(2,1)S(1)}, bf16[128,128]{1,0:T(8,128)(2,1)S(1)}, u32[]{:S(2)}, u32[]{:S(2)}) collective-permute-start(bf16[128,128]{1,0:T(8,128)(2,1)S(1)} %broadcast_select_fusion.refs_4_), channel_id=1, source_target_pairs={{0,8},{8,0},{16,24},{24,16},{1,9},{9,1},{17,25},{25,17},{2,10},{10... | collective-permute-start | bytes 98312 | tf_op jit(solution)/shard_map/ppermute | solution.py:19
  26.4 1.2 copy-done.1
  27.6 0.9 copy-done.7
  28.6 0.9 copy-done.9
  30.2 2.0 %shard_map.161 = (bf16[896,256]{1,0:T(8,128)(2,1)S(1)}, bf16[896,256]{1,0:T(8,128)(2,1)S(1)}, bf16[896,256]{1,0:T(8,128)(2,1)S(1)}, bf16[896,256]{1,0:T(8,128)(2,1)S(1)}) custom-call(s32[3]{0:T(128)S(1)} %pad_add_fusion.where_ref, bf16[512,1024]{1,0:T(8,128)(2,1)S(1)} %bitcast.22, bf16[128,1024]{1,0:T(8,128)(2,1)S(1)} %bitcast.26, ...), custom_call_target="tpu_custom_call" | custom-call | tf_op jit(solution)/shard_map/pallas_call | solution.py:90
  32.2 1.6 %collective-permute-start.9 = (bf16[896,256]{1,0:T(8,128)(2,1)S(1)}, bf16[896,256]{1,0:T(8,128)(2,1)S(1)}, u32[]{:S(2)}, u32[]{:S(2)}) collective-permute-start(bf16[896,256]{1,0:T(8,128)(2,1)S(1)} %get-tuple-element.73), channel_id=1, source_target_pairs={{0,1},{1,0},{2,3},{3,2},{4,5},{5,4},{6,7},{7,6},{8,9},{9,8},{10,11... | collective-permute-start | bytes 1376264 | tf_op jit(solution)/shard_map/ppermute | solution.py:19
  33.8 1.5 %collective-permute-start.10 = (bf16[896,256]{1,0:T(8,128)(2,1)S(1)}, bf16[896,256]{1,0:T(8,128)(2,1)S(1)}, u32[]{:S(2)}, u32[]{:S(2)}) collective-permute-start(bf16[896,256]{1,0:T(8,128)(2,1)S(1)} %get-tuple-element.74), channel_id=1, source_target_pairs={{0,2},{1,3},{2,0},{3,1},{4,6},{5,7},{6,4},{7,5},{8,10},{9,11},{10,... | collective-permute-start | bytes 1376264 | tf_op jit(solution)/shard_map/ppermute | solution.py:19
  35.8 1.6 %copy-done.3 = bf16[1,1024,1024]{2,1,0:T(8,128)(2,1)S(1)} copy-done((bf16[1,1024,1024]{2,1,0:T(8,128)(2,1)S(1)}, bf16[1,1024,1024]{2,1,0:T(8,128)(2,1)}, u32[]{:S(2)}) %copy-start.3) | copy-done | bytes 2097176
  37.4 1.8 %shard_map.160.refs_4_.refs_9_ = bf16[1024,512]{1,0:T(8,128)(2,1)S(1)} custom-call(s32[3]{0:T(128)S(1)} %pad_add_fusion.where_ref, bf16[1024,1024]{1,0:T(8,128)(2,1)S(1)} %bitcast.24, bf16[512,1024]{1,0:T(8,128)(2,1)S(1)} %bitcast.20), custom_call_target="tpu_custom_call" | custom-call | tf_op jit(solution)/shard_map/pallas_call | solution.py:90
  39.3 1.4 shard_map.162
  40.7 1.6 %collective-permute-start.6 = (bf16[512,128]{1,0:T(8,128)(2,1)S(1)}, bf16[512,128]{1,0:T(8,128)(2,1)S(1)}, u32[]{:S(2)}, u32[]{:S(2)}) collective-permute-start(bf16[512,128]{1,0:T(8,128)(2,1)S(1)} %get-tuple-element.70), channel_id=1, source_target_pairs={{0,1},{1,0},{2,3},{3,2},{4,5},{5,4},{6,7},{7,6},{8,9},{9,8},{10,11... | collective-permute-start | bytes 393224 | tf_op jit(solution)/shard_map/ppermute | solution.py:19
  42.2 1.5 %collective-permute-start.7 = (bf16[512,128]{1,0:T(8,128)(2,1)S(1)}, bf16[512,128]{1,0:T(8,128)(2,1)S(1)}, u32[]{:S(2)}, u32[]{:S(2)}) collective-permute-start(bf16[512,128]{1,0:T(8,128)(2,1)S(1)} %get-tuple-element.71), channel_id=1, source_target_pairs={{0,2},{1,3},{2,0},{3,1},{4,6},{5,7},{6,4},{7,5},{8,10},{9,11},{10,... | collective-permute-start | bytes 393224 | tf_op jit(solution)/shard_map/ppermute | solution.py:19
  43.7 11.7 %collective-permute-done.6 = bf16[512,128]{1,0:T(8,128)(2,1)S(1)} collective-permute-done((bf16[512,128]{1,0:T(8,128)(2,1)S(1)}, bf16[512,128]{1,0:T(8,128)(2,1)S(1)}, u32[]{:S(2)}, u32[]{:S(2)}) %collective-permute-start.6) | collective-permute-done | bytes 131104 | tf_op jit(solution)/shard_map/ppermute | solution.py:19
  55.4 2.7 %collective-permute-start.8 = (bf16[512,128]{1,0:T(8,128)(2,1)S(1)}, bf16[512,128]{1,0:T(8,128)(2,1)S(1)}, u32[]{:S(2)}, u32[]{:S(2)}) collective-permute-start(bf16[512,128]{1,0:T(8,128)(2,1)S(1)} %get-tuple-element.72), channel_id=1, source_target_pairs={{0,3},{1,2},{2,1},{3,0},{4,7},{5,6},{6,5},{7,4},{8,11},{9,10},{10,... | collective-permute-start | bytes 393224 | tf_op jit(solution)/shard_map/ppermute | solution.py:19
  58.1 3.1 %collective-permute-done.8 = bf16[512,128]{1,0:T(8,128)(2,1)S(1)} collective-permute-done((bf16[512,128]{1,0:T(8,128)(2,1)S(1)}, bf16[512,128]{1,0:T(8,128)(2,1)S(1)}, u32[]{:S(2)}, u32[]{:S(2)}) %collective-permute-start.8) | collective-permute-done | bytes 131104 | tf_op jit(solution)/shard_map/ppermute | solution.py:19
  62.1 6.1 %collective-permute-done.12 = bf16[512,128]{1,0:T(8,128)(2,1)S(1)} collective-permute-done((bf16[512,128]{1,0:T(8,128)(2,1)S(1)}, bf16[512,128]{1,0:T(8,128)(2,1)S(1)}, u32[]{:S(2)}, u32[]{:S(2)}) %collective-permute-start.12) | collective-permute-done | bytes 131104 | tf_op jit(solution)/shard_map/ppermute | solution.py:19
  69.2 3.3 %collective-permute-start.16 = (bf16[1024,128]{1,0:T(8,128)(2,1)S(1)}, bf16[1024,128]{1,0:T(8,128)(2,1)S(1)}, u32[]{:S(2)}, u32[]{:S(2)}) collective-permute-start(bf16[1024,128]{1,0:T(8,128)(2,1)S(1)} %get-tuple-element.80.refs_4_), channel_id=1, source_target_pairs={{0,3},{1,2},{2,1},{3,0},{4,7},{5,6},{6,5},{7,4},{8,11},{9,10},{10,... | collective-permute-start | bytes 786440 | tf_op jit(solution)/shard_map/ppermute | solution.py:19
  73.3 3.7 %collective-permute-done.16.refs_7_ = bf16[1024,128]{1,0:T(8,128)(2,1)S(1)} collective-permute-done((bf16[1024,128]{1,0:T(8,128)(2,1)S(1)}, bf16[1024,128]{1,0:T(8,128)(2,1)S(1)}, u32[]{:S(2)}, u32[]{:S(2)}) %collective-permute-start.16) | collective-permute-done | bytes 262176 | tf_op jit(solution)/shard_map/ppermute | solution.py:19
  77.0 5.5 %collective-permute-done.15.refs_6_ = bf16[1024,128]{1,0:T(8,128)(2,1)S(1)} collective-permute-done((bf16[1024,128]{1,0:T(8,128)(2,1)S(1)}, bf16[1024,128]{1,0:T(8,128)(2,1)S(1)}, u32[]{:S(2)}, u32[]{:S(2)}) %collective-permute-start.15) | collective-permute-done | bytes 262176 | tf_op jit(solution)/shard_map/ppermute | solution.py:19
  82.9 1.7 %collective-permute-start.19 = (bf16[512,128]{1,0:T(8,128)(2,1)S(1)}, bf16[512,128]{1,0:T(8,128)(2,1)S(1)}, u32[]{:S(2)}, u32[]{:S(2)}) collective-permute-start(bf16[512,128]{1,0:T(8,128)(2,1)S(1)} %add_convert_fusion.3.refs_0_), channel_id=1, source_target_pairs={{0,3},{1,2},{2,1},{3,0},{4,7},{5,6},{6,5},{7,4},{8,11},{9,10},{10,... | collective-permute-start | bytes 393224 | tf_op jit(solution)/shard_map/ppermute | solution.py:19
  84.6 1.4 %collective-permute-start.18 = (bf16[512,128]{1,0:T(8,128)(2,1)S(1)}, bf16[512,128]{1,0:T(8,128)(2,1)S(1)}, u32[]{:S(2)}, u32[]{:S(2)}) collective-permute-start(bf16[512,128]{1,0:T(8,128)(2,1)S(1)} %add_convert_fusion.3.refs_0_), channel_id=1, source_target_pairs={{0,2},{1,3},{2,0},{3,1},{4,6},{5,7},{6,4},{7,5},{8,10},{9,11},{10,... | collective-permute-start | bytes 393224 | tf_op jit(solution)/shard_map/ppermute | solution.py:19
  86.4 2.4 %collective-permute-done.19.refs_3_ = bf16[512,128]{1,0:T(8,128)(2,1)S(1)} collective-permute-done((bf16[512,128]{1,0:T(8,128)(2,1)S(1)}, bf16[512,128]{1,0:T(8,128)(2,1)S(1)}, u32[]{:S(2)}, u32[]{:S(2)}) %collective-permute-start.19) | collective-permute-done | bytes 131104 | tf_op jit(solution)/shard_map/ppermute | solution.py:19
  88.9 1.3 collective-permute-done.18.refs_2_
  91.0 2.1 %shard_map.164 = (bf16[512,512]{1,0:T(8,128)(2,1)S(1)}, bf16[512,512]{1,0:T(8,128)(2,1)S(1)}, f32[512,512]{1,0:T(8,128)S(1)}, f32[512,512]{1,0:T(8,128)S(1)}, f3...) custom-call(s32[3]{0:T(128)S(1)} %pad_add_fusion.where_ref, ...), custom_call_target="tpu_custom_call" | custom-call | flops 805306368 | bytes 7604224 | tf_op jit(solution)/shard_map/pallas_call | solution.py:90
  93.9 1.3 collective-permute-start.20
  95.2 1.5 %collective-permute-done.20.refs_0_ = bf16[512,512]{1,0:T(8,128)(2,1)S(1)} collective-permute-done((bf16[512,512]{1,0:T(8,128)(2,1)S(1)}, bf16[512,512]{1,0:T(8,128)(2,1)S(1)}, u32[]{:S(2)}, u32[]{:S(2)}) %collective-permute-start.20) | collective-permute-done | bytes 524320 | tf_op jit(solution)/shard_map/ppermute | solution.py:25
  96.7 1.7 %shard_map.165 = (bf16[512,512]{1,0:T(8,128)(2,1)S(1)}, bf16[512,512]{1,0:T(8,128)(2,1)S(1)}, f32[512,512]{1,0:T(8,128)S(1)}, f32[512,512]{1,0:T(8,128)S(1)}, f3...) custom-call(s32[3]{0:T(128)S(1)} %pad_add_fusion.where_ref, bf16[512,512]{1,0:T(8,128)(2,1)S(1)} %collective-permute-done.20.refs_0_, ...), custom_call_target="tpu_custom_call" | custom-call | flops 268435456 | bytes 7606272 | tf_op jit(solution)/shard_map/pallas_call | solution.py:90
  99.2 1.5 %collective-permute-start.21 = (bf16[512,512]{1,0:T(8,128)(2,1)S(1)}, bf16[512,512]{1,0:T(8,128)(2,1)S(1)}, u32[]{:S(2)}, u32[]{:S(2)}) collective-permute-start(bf16[512,512]{1,0:T(8,128)(2,1)S(1)} %get-tuple-element.90), channel_id=1, source_target_pairs={{4,0},{5,1},{6,2},{7,3},{12,8},{13,9},{14,10},{15,11},{20,16},{21,... | collective-permute-start | bytes 1572872 | tf_op jit(solution)/shard_map/ppermute | solution.py:25
  100.7 2.3 %collective-permute-done.21.refs_0_ = bf16[512,512]{1,0:T(8,128)(2,1)S(1)} collective-permute-done((bf16[512,512]{1,0:T(8,128)(2,1)S(1)}, bf16[512,512]{1,0:T(8,128)(2,1)S(1)}, u32[]{:S(2)}, u32[]{:S(2)}) %collective-permute-start.21) | collective-permute-done | bytes 524320 | tf_op jit(solution)/shard_map/ppermute | solution.py:25
  103.0 3.6 %shard_map.166 = (bf16[512,512]{1,0:T(8,128)(2,1)S(1)}, bf16[512,512]{1,0:T(8,128)(2,1)S(1)}, f32[512,1]{1,0:T(8,128)S(1)}, bf16[512,512]{1,0:T(8,128)(2,1)S(1)}...) custom-call(s32[3]{0:T(128)S(1)} %pad_add_fusion.where_ref, ...), custom_call_target="tpu_custom_call" | custom-call | flops 805306368 | bytes 9703424 | tf_op jit(solution)/shard_map/pallas_call | solution.py:90
  110.5 1.8 %collective-permute-start.25 = (bf16[256,1024]{1,0:T(8,128)(2,1)}, bf16[256,1024]{1,0:T(8,128)(2,1)}, u32[]{:S(2)}, u32[]{:S(2)}) collective-permute-start(bf16[256,1024]{1,0:T(8,128)(2,1)} %get-tuple-element.111), channel_id=1, source_target_pairs={{0,8},{8,0},{16,24},{24,16},{1,9},{9,1},{17,25},{25,17},{2,10},{10... | collective-permute-start | bytes 1572872 | tf_op jit(solution)/shard_map/ppermute | solution.py:19
  112.3 0.9 copy-done.18
  114.2 0.9 copy-done.22
  115.2 0.9 copy-done.24
  116.1 1.0 copy-done.32
  117.2 2.5 %shard_map.167 = (bf16[512,1024]{1,0:T(8,128)(2,1)S(1)}, bf16[128,1024]{1,0:T(8,128)(2,1)S(1)}, bf16[128,1024]{1,0:T(8,128)(2,1)S(1)}, bf16[128,1024]{1,0:T(8,128)(2,1)S(1)}, bf16[128,1024]{1,0:T(8,128)(2,1)S(1)}) custom-call(s32[3]{0:T(128)S(1)} %pad_add_fusion.where_ref, bf16[128,1024]{1,0:T(8,128)(2,1)S(1)} %bitcast.34, bf16[128,1024]{1,0:T(8,128)(2,1)S(1)} %copy-done.24, ...), custom_call_target="tpu_custom_call" | custom-call | flops 1610612736 | bytes 5767168 | tf_op jit(solution)/shard_map/pallas_call | solution.py:90
  120.6 1.1 collective-permute-start.23
  121.7 1.5 %collective-permute-start.24 = (bf16[128,1024]{1,0:T(8,128)(2,1)S(1)}, bf16[128,1024]{1,0:T(8,128)(2,1)S(1)}, u32[]{:S(2)}, u32[]{:S(2)}) collective-permute-start(bf16[128,1024]{1,0:T(8,128)(2,1)S(1)} %get-tuple-element.107), channel_id=1, source_target_pairs={{0,3},{1,2},{2,1},{3,0},{4,7},{5,6},{6,5},{7,4},{8,11},{9,10},{10,... | collective-permute-start | bytes 786440 | tf_op jit(solution)/shard_map/ppermute | solution.py:19
  123.2 3.2 %shard_map.168 = bf16[1024,1024]{1,0:T(8,128)(2,1)} custom-call(s32[3]{0:T(128)S(1)} %pad_add_fusion.where_ref, bf16[512,1024]{1,0:T(8,128)(2,1)S(1)} %get-tuple-element.113.refs_0_, bf16[512,1024]{1,0:T(8,128)(2,1)S(1)} %bitcast.21), custom_call_target="tpu_custom_call" | custom-call | tf_op jit(solution)/shard_map/pallas_call | solution.py:90
  126.5 1.4 add_convert_fusion
  127.9 1.2 collective-permute-start.26
  129.1 4.9 %collective-permute-done.23 = bf16[128,1024]{1,0:T(8,128)(2,1)S(1)} collective-permute-done((bf16[128,1024]{1,0:T(8,128)(2,1)S(1)}, bf16[128,1024]{1,0:T(8,128)(2,1)S(1)}, u32[]{:S(2)}, u32[]{:S(2)}) %collective-permute-start.23) | collective-permute-done | bytes 262176 | tf_op jit(solution)/shard_map/ppermute | solution.py:19
  134.9 1.4 slice_bitcast_fusion
  136.3 3.5 %shard_map.169 = (bf16[128,1024]{1,0:T(8,128)(2,1)}, f32[1,1024]{1,0:T(1,128)}, bf16[1024,128]{1,0:T(8,128)(2,1)}, bf16[128,1024]{1,0:T(8,128)(2,1)}) custom-call(s32[3]{0:T(128)S(1)} %pad_add_fusion.where_ref, bf16[512,512]{1,0:T(8,128)(2,1)S(1)} %copy-done.12, bf16[512,128]{1,0:T(8,128)(2,1)S(1)} %constant_dynamic-slice_fusion.refs_1_, ...), custom_call_target="tpu_custom_call" | custom-call | tf_op jit(solution)/shard_map/pallas_call | solution.py:90
  139.8 1.8 %collective-permute-done.26 = bf16[128,1024]{1,0:T(8,128)(2,1)S(1)} collective-permute-done((bf16[128,1024]{1,0:T(8,128)(2,1)S(1)}, bf16[128,1024]{1,0:T(8,128)(2,1)S(1)}, u32[]{:S(2)}, u32[]{:S(2)}) %collective-permute-start.26) | collective-permute-done | bytes 262176 | tf_op jit(solution)/shard_map/ppermute | solution.py:19
  (95 shorter events, 16.4 us)
Async XLA Ops:
  0.6 35.1 %copy-start = (bf16[1,512,1024]{2,1,0:T(8,128)(2,1)S(1)}, bf16[1,512,1024]{2,1,0:T(8,128)(2,1)}, u32[]{:S(2)}) copy-start(bf16[1,512,1024]{2,1,0:T(8,128)(2,1)} %param.11) | copy-start | bytes 3145732
  0.7 34.6 %collective-permute-start.2 = (bf16[128,1024]{1,0:T(8,128)(2,1)}, bf16[128,1024]{1,0:T(8,128)(2,1)S(1)}, u32[]{:S(2)}, u32[]{:S(2)}) collective-permute-start(bf16[128,1024]{1,0:T(8,128)(2,1)} %bitcast.30), channel_id=1, source_target_pairs={{0,24},{8,16},{16,8},{24,0},{1,25},{9,17},{17,9},{25,1},{2,26},{10... | collective-permute-start | bytes 786440 | tf_op jit(solution)/shard_map/ppermute | solution.py:19
  6.5 7.4 %collective-permute-start.5 = (bf16[128,128]{1,0:T(8,128)(2,1)S(1)}, bf16[128,128]{1,0:T(8,128)(2,1)S(1)}, u32[]{:S(2)}, u32[]{:S(2)}) collective-permute-start(bf16[128,128]{1,0:T(8,128)(2,1)S(1)} %broadcast_select_fusion.refs_4_), channel_id=1, source_target_pairs={{0,24},{8,16},{16,8},{24,0},{1,25},{9,17},{17,9},{25,1},{2,26},{10... | collective-permute-start | bytes 98312 | tf_op jit(solution)/shard_map/ppermute | solution.py:19
  6.6 32.6 %collective-permute-start.1 = (bf16[128,1024]{1,0:T(8,128)(2,1)}, bf16[128,1024]{1,0:T(8,128)(2,1)S(1)}, u32[]{:S(2)}, u32[]{:S(2)}) collective-permute-start(bf16[128,1024]{1,0:T(8,128)(2,1)} %bitcast.31), channel_id=1, source_target_pairs={{0,16},{8,24},{16,0},{24,8},{1,17},{9,25},{17,1},{25,9},{2,18},{10... | collective-permute-start | bytes 786440 | tf_op jit(solution)/shard_map/ppermute | solution.py:19
  7.5 31.7 %collective-permute-start = (bf16[128,1024]{1,0:T(8,128)(2,1)}, bf16[128,1024]{1,0:T(8,128)(2,1)S(1)}, u32[]{:S(2)}, u32[]{:S(2)}) collective-permute-start(bf16[128,1024]{1,0:T(8,128)(2,1)} %bitcast.32), channel_id=1, source_target_pairs={{0,8},{8,0},{16,24},{24,16},{1,9},{9,1},{17,25},{25,17},{2,10},{10... | collective-permute-start | bytes 786440 | tf_op jit(solution)/shard_map/ppermute | solution.py:19
  10.9 21.3 %collective-permute-start.4 = (bf16[128,128]{1,0:T(8,128)(2,1)S(1)}, bf16[128,128]{1,0:T(8,128)(2,1)S(1)}, u32[]{:S(2)}, u32[]{:S(2)}) collective-permute-start(bf16[128,128]{1,0:T(8,128)(2,1)S(1)} %broadcast_select_fusion.refs_4_), channel_id=1, source_target_pairs={{0,16},{8,24},{16,0},{24,8},{1,17},{9,25},{17,1},{25,9},{2,18},{10... | collective-permute-start | bytes 98312 | tf_op jit(solution)/shard_map/ppermute | solution.py:19
  13.9 19.8 %collective-permute-start.3 = (bf16[128,128]{1,0:T(8,128)(2,1)S(1)}, bf16[128,128]{1,0:T(8,128)(2,1)S(1)}, u32[]{:S(2)}, u32[]{:S(2)}) collective-permute-start(bf16[128,128]{1,0:T(8,128)(2,1)S(1)} %broadcast_select_fusion.refs_4_), channel_id=1, source_target_pairs={{0,8},{8,0},{16,24},{24,16},{1,9},{9,1},{17,25},{25,17},{2,10},{10... | collective-permute-start | bytes 98312 | tf_op jit(solution)/shard_map/ppermute | solution.py:19
  26.4 1.2 copy-start.1
  27.6 0.9 copy-start.7
  32.2 29.1 %collective-permute-start.9 = (bf16[896,256]{1,0:T(8,128)(2,1)S(1)}, bf16[896,256]{1,0:T(8,128)(2,1)S(1)}, u32[]{:S(2)}, u32[]{:S(2)}) collective-permute-start(bf16[896,256]{1,0:T(8,128)(2,1)S(1)} %get-tuple-element.73), channel_id=1, source_target_pairs={{0,1},{1,0},{2,3},{3,2},{4,5},{5,4},{6,7},{7,6},{8,9},{9,8},{10,11... | collective-permute-start | bytes 1376264 | tf_op jit(solution)/shard_map/ppermute | solution.py:19
  33.8 27.5 %collective-permute-start.10 = (bf16[896,256]{1,0:T(8,128)(2,1)S(1)}, bf16[896,256]{1,0:T(8,128)(2,1)S(1)}, u32[]{:S(2)}, u32[]{:S(2)}) collective-permute-start(bf16[896,256]{1,0:T(8,128)(2,1)S(1)} %get-tuple-element.74), channel_id=1, source_target_pairs={{0,2},{1,3},{2,0},{3,1},{4,6},{5,7},{6,4},{7,5},{8,10},{9,11},{10,... | collective-permute-start | bytes 1376264 | tf_op jit(solution)/shard_map/ppermute | solution.py:19
  35.3 4.0 %copy-start.19 = (bf16[128,1024]{1,0:T(8,128)(2,1)}, bf16[128,1024]{1,0:T(8,128)(2,1)S(1)}, u32[]{:S(2)}) copy-start(bf16[128,1024]{1,0:T(8,128)(2,1)S(1)} %collective-permute-done.2.refs_3_) | copy-start | bytes 786436
  35.3 26.0 %collective-permute-start.11 = (bf16[896,256]{1,0:T(8,128)(2,1)S(1)}, bf16[896,256]{1,0:T(8,128)(2,1)S(1)}, u32[]{:S(2)}, u32[]{:S(2)}) collective-permute-start(bf16[896,256]{1,0:T(8,128)(2,1)S(1)} %get-tuple-element.75), channel_id=1, source_target_pairs={{0,3},{1,2},{2,1},{3,0},{4,7},{5,6},{6,5},{7,4},{8,11},{9,10},{10,... | collective-permute-start | bytes 1376264 | tf_op jit(solution)/shard_map/ppermute | solution.py:19
  35.8 1.6 %copy-start.3 = (bf16[1,1024,1024]{2,1,0:T(8,128)(2,1)S(1)}, bf16[1,1024,1024]{2,1,0:T(8,128)(2,1)}, u32[]{:S(2)}) copy-start(bf16[1,1024,1024]{2,1,0:T(8,128)(2,1)} %param.10) | copy-start | bytes 6291460
  37.4 1.9 %copy-start.17 = (bf16[1,128,1024]{2,1,0:T(8,128)(2,1)S(1)}, bf16[1,128,1024]{2,1,0:T(8,128)(2,1)}, u32[]{:S(2)}) copy-start(bf16[1,128,1024]{2,1,0:T(8,128)(2,1)} %param.9) | copy-start | bytes 786436
  39.2 30.0 %copy-start.21 = (bf16[128,1024]{1,0:T(8,128)(2,1)}, bf16[128,1024]{1,0:T(8,128)(2,1)S(1)}, u32[]{:S(2)}) copy-start(bf16[128,1024]{1,0:T(8,128)(2,1)S(1)} %collective-permute-done.1.refs_2_) | copy-start | bytes 786436
  39.3 30.0 %copy-start.23 = (bf16[128,1024]{1,0:T(8,128)(2,1)}, bf16[128,1024]{1,0:T(8,128)(2,1)S(1)}, u32[]{:S(2)}) copy-start(bf16[128,1024]{1,0:T(8,128)(2,1)S(1)} %collective-permute-done.refs_1_) | copy-start | bytes 786436
  40.7 14.7 %collective-permute-start.6 = (bf16[512,128]{1,0:T(8,128)(2,1)S(1)}, bf16[512,128]{1,0:T(8,128)(2,1)S(1)}, u32[]{:S(2)}, u32[]{:S(2)}) collective-permute-start(bf16[512,128]{1,0:T(8,128)(2,1)S(1)} %get-tuple-element.70), channel_id=1, source_target_pairs={{0,1},{1,0},{2,3},{3,2},{4,5},{5,4},{6,7},{7,6},{8,9},{9,8},{10,11... | collective-permute-start | bytes 393224 | tf_op jit(solution)/shard_map/ppermute | solution.py:19
  42.2 15.9 %collective-permute-start.7 = (bf16[512,128]{1,0:T(8,128)(2,1)S(1)}, bf16[512,128]{1,0:T(8,128)(2,1)S(1)}, u32[]{:S(2)}, u32[]{:S(2)}) collective-permute-start(bf16[512,128]{1,0:T(8,128)(2,1)S(1)} %get-tuple-element.71), channel_id=1, source_target_pairs={{0,2},{1,3},{2,0},{3,1},{4,6},{5,7},{6,4},{7,5},{8,10},{9,11},{10,... | collective-permute-start | bytes 393224 | tf_op jit(solution)/shard_map/ppermute | solution.py:19
  55.4 5.9 %collective-permute-start.8 = (bf16[512,128]{1,0:T(8,128)(2,1)S(1)}, bf16[512,128]{1,0:T(8,128)(2,1)S(1)}, u32[]{:S(2)}, u32[]{:S(2)}) collective-permute-start(bf16[512,128]{1,0:T(8,128)(2,1)S(1)} %get-tuple-element.72), channel_id=1, source_target_pairs={{0,3},{1,2},{2,1},{3,0},{4,7},{5,6},{6,5},{7,4},{8,11},{9,10},{10,... | collective-permute-start | bytes 393224 | tf_op jit(solution)/shard_map/ppermute | solution.py:19
  61.4 6.8 %collective-permute-start.12 = (bf16[512,128]{1,0:T(8,128)(2,1)S(1)}, bf16[512,128]{1,0:T(8,128)(2,1)S(1)}, u32[]{:S(2)}, u32[]{:S(2)}) collective-permute-start(bf16[512,128]{1,0:T(8,128)(2,1)S(1)} %add_convert_fusion.5), channel_id=1, source_target_pairs={{0,16},{8,24},{16,0},{24,8},{1,17},{9,25},{17,1},{25,9},{2,18},{10... | collective-permute-start | bytes 393224 | tf_op jit(solution)/shard_map/ppermute | solution.py:19
  68.2 5.0 %collective-permute-start.13 = (bf16[512,128]{1,0:T(8,128)(2,1)S(1)}, bf16[512,128]{1,0:T(8,128)(2,1)S(1)}, u32[]{:S(2)}, u32[]{:S(2)}) collective-permute-start(bf16[512,128]{1,0:T(8,128)(2,1)S(1)} %add_convert_fusion.4), channel_id=1, source_target_pairs={{0,8},{8,0},{16,24},{24,16},{1,9},{9,1},{17,25},{25,17},{2,10},{10... | collective-permute-start | bytes 393224 | tf_op jit(solution)/shard_map/ppermute | solution.py:19
  69.2 7.8 %collective-permute-start.16 = (bf16[1024,128]{1,0:T(8,128)(2,1)S(1)}, bf16[1024,128]{1,0:T(8,128)(2,1)S(1)}, u32[]{:S(2)}, u32[]{:S(2)}) collective-permute-start(bf16[1024,128]{1,0:T(8,128)(2,1)S(1)} %get-tuple-element.80.refs_4_), channel_id=1, source_target_pairs={{0,3},{1,2},{2,1},{3,0},{4,7},{5,6},{6,5},{7,4},{8,11},{9,10},{10,... | collective-permute-start | bytes 786440 | tf_op jit(solution)/shard_map/ppermute | solution.py:19
  72.5 10.0 %collective-permute-start.15 = (bf16[1024,128]{1,0:T(8,128)(2,1)S(1)}, bf16[1024,128]{1,0:T(8,128)(2,1)S(1)}, u32[]{:S(2)}, u32[]{:S(2)}) collective-permute-start(bf16[1024,128]{1,0:T(8,128)(2,1)S(1)} %get-tuple-element.80.refs_4_), channel_id=1, source_target_pairs={{0,2},{1,3},{2,0},{3,1},{4,6},{5,7},{6,4},{7,5},{8,10},{9,11},{10,... | collective-permute-start | bytes 786440 | tf_op jit(solution)/shard_map/ppermute | solution.py:19
  72.5 10.4 %collective-permute-start.14 = (bf16[1024,128]{1,0:T(8,128)(2,1)S(1)}, bf16[1024,128]{1,0:T(8,128)(2,1)S(1)}, u32[]{:S(2)}, u32[]{:S(2)}) collective-permute-start(bf16[1024,128]{1,0:T(8,128)(2,1)S(1)} %get-tuple-element.80.refs_4_), channel_id=1, source_target_pairs={{0,1},{1,0},{2,3},{3,2},{4,5},{5,4},{6,7},{7,6},{8,9},{9,8},{10,11... | collective-permute-start | bytes 786440 | tf_op jit(solution)/shard_map/ppermute | solution.py:19
  82.9 5.9 %collective-permute-start.19 = (bf16[512,128]{1,0:T(8,128)(2,1)S(1)}, bf16[512,128]{1,0:T(8,128)(2,1)S(1)}, u32[]{:S(2)}, u32[]{:S(2)}) collective-permute-start(bf16[512,128]{1,0:T(8,128)(2,1)S(1)} %add_convert_fusion.3.refs_0_), channel_id=1, source_target_pairs={{0,3},{1,2},{2,1},{3,0},{4,7},{5,6},{6,5},{7,4},{8,11},{9,10},{10,... | collective-permute-start | bytes 393224 | tf_op jit(solution)/shard_map/ppermute | solution.py:19
  84.6 5.6 %collective-permute-start.18 = (bf16[512,128]{1,0:T(8,128)(2,1)S(1)}, bf16[512,128]{1,0:T(8,128)(2,1)S(1)}, u32[]{:S(2)}, u32[]{:S(2)}) collective-permute-start(bf16[512,128]{1,0:T(8,128)(2,1)S(1)} %add_convert_fusion.3.refs_0_), channel_id=1, source_target_pairs={{0,2},{1,3},{2,0},{3,1},{4,6},{5,7},{6,4},{7,5},{8,10},{9,11},{10,... | collective-permute-start | bytes 393224 | tf_op jit(solution)/shard_map/ppermute | solution.py:19
  86.0 5.0 %collective-permute-start.17 = (bf16[512,128]{1,0:T(8,128)(2,1)S(1)}, bf16[512,128]{1,0:T(8,128)(2,1)S(1)}, u32[]{:S(2)}, u32[]{:S(2)}) collective-permute-start(bf16[512,128]{1,0:T(8,128)(2,1)S(1)} %add_convert_fusion.3.refs_0_), channel_id=1, source_target_pairs={{0,1},{1,0},{2,3},{3,2},{4,5},{5,4},{6,7},{7,6},{8,9},{9,8},{10,11... | collective-permute-start | bytes 393224 | tf_op jit(solution)/shard_map/ppermute | solution.py:19
  93.9 2.8 %collective-permute-start.20 = (bf16[512,512]{1,0:T(8,128)(2,1)S(1)}, bf16[512,512]{1,0:T(8,128)(2,1)S(1)}, u32[]{:S(2)}, u32[]{:S(2)}) collective-permute-start(bf16[512,512]{1,0:T(8,128)(2,1)S(1)} %get-tuple-element.84), channel_id=1, source_target_pairs={{0,4},{1,5},{2,6},{3,7},{8,12},{9,13},{10,14},{11,15},{16,20},{17,... | collective-permute-start | bytes 1572872 | tf_op jit(solution)/shard_map/ppermute | solution.py:25
  99.2 7.4 %copy-start.5 = (bf16[512,512]{1,0:T(8,128)(2,1)}, bf16[512,512]{1,0:T(8,128)(2,1)S(1)}, u32[]{:S(2)}) copy-start(bf16[512,512]{1,0:T(8,128)(2,1)S(1)} %get-tuple-element.91.refs_2_) | copy-start | bytes 1572868
  99.2 3.8 %collective-permute-start.21 = (bf16[512,512]{1,0:T(8,128)(2,1)S(1)}, bf16[512,512]{1,0:T(8,128)(2,1)S(1)}, u32[]{:S(2)}, u32[]{:S(2)}) collective-permute-start(bf16[512,512]{1,0:T(8,128)(2,1)S(1)} %get-tuple-element.90), channel_id=1, source_target_pairs={{4,0},{5,1},{6,2},{7,3},{12,8},{13,9},{14,10},{15,11},{20,16},{21,... | collective-permute-start | bytes 1572872 | tf_op jit(solution)/shard_map/ppermute | solution.py:25
  103.0 9.3 %copy-start.4 = (bf16[1,1024,1024]{2,1,0:T(8,128)(2,1)S(1)}, bf16[1,1024,1024]{2,1,0:T(8,128)(2,1)}, u32[]{:S(2)}) copy-start(bf16[1,1024,1024]{2,1,0:T(8,128)(2,1)} %param.10) | copy-start | bytes 6291460
  110.5 15.9 %collective-permute-start.25 = (bf16[256,1024]{1,0:T(8,128)(2,1)}, bf16[256,1024]{1,0:T(8,128)(2,1)}, u32[]{:S(2)}, u32[]{:S(2)}) collective-permute-start(bf16[256,1024]{1,0:T(8,128)(2,1)} %get-tuple-element.111), channel_id=1, source_target_pairs={{0,8},{8,0},{16,24},{24,16},{1,9},{9,1},{17,25},{25,17},{2,10},{10... | collective-permute-start | bytes 1572872 | tf_op jit(solution)/shard_map/ppermute | solution.py:19
  112.3 1.0 copy-start.18
  116.1 1.0 copy-start.32
  119.6 6.7 %copy-start.12 = (bf16[512,512]{1,0:T(8,128)(2,1)S(1)}, bf16[512,512]{1,0:T(8,128)(2,1)}, u32[]{:S(2)}) copy-start(bf16[512,512]{1,0:T(8,128)(2,1)} %copy-done.11) | copy-start | bytes 1572868
  119.7 6.8 %copy-start.16 = (bf16[256,1024]{1,0:T(8,128)(2,1)S(1)}, bf16[256,1024]{1,0:T(8,128)(2,1)}, u32[]{:S(2)}) copy-start(bf16[256,1024]{1,0:T(8,128)(2,1)} %copy-done.15) | copy-start | bytes 1572868
  119.7 9.4 %collective-permute-start.22 = (bf16[128,1024]{1,0:T(8,128)(2,1)S(1)}, bf16[128,1024]{1,0:T(8,128)(2,1)S(1)}, u32[]{:S(2)}, u32[]{:S(2)}) collective-permute-start(bf16[128,1024]{1,0:T(8,128)(2,1)S(1)} %get-tuple-element.105), channel_id=1, source_target_pairs={{0,1},{1,0},{2,3},{3,2},{4,5},{5,4},{6,7},{7,6},{8,9},{9,8},{10,11... | collective-permute-start | bytes 786440 | tf_op jit(solution)/shard_map/ppermute | solution.py:19
  120.6 13.4 %collective-permute-start.23 = (bf16[128,1024]{1,0:T(8,128)(2,1)S(1)}, bf16[128,1024]{1,0:T(8,128)(2,1)S(1)}, u32[]{:S(2)}, u32[]{:S(2)}) collective-permute-start(bf16[128,1024]{1,0:T(8,128)(2,1)S(1)} %get-tuple-element.106), channel_id=1, source_target_pairs={{0,2},{1,3},{2,0},{3,1},{4,6},{5,7},{6,4},{7,5},{8,10},{9,11},{10,... | collective-permute-start | bytes 786440 | tf_op jit(solution)/shard_map/ppermute | solution.py:19
  121.7 12.3 %collective-permute-start.24 = (bf16[128,1024]{1,0:T(8,128)(2,1)S(1)}, bf16[128,1024]{1,0:T(8,128)(2,1)S(1)}, u32[]{:S(2)}, u32[]{:S(2)}) collective-permute-start(bf16[128,1024]{1,0:T(8,128)(2,1)S(1)} %get-tuple-element.107), channel_id=1, source_target_pairs={{0,3},{1,2},{2,1},{3,0},{4,7},{5,6},{6,5},{7,4},{8,11},{9,10},{10,... | collective-permute-start | bytes 786440 | tf_op jit(solution)/shard_map/ppermute | solution.py:19
  126.4 9.9 %copy-start.2 = (bf16[1,512,1024]{2,1,0:T(8,128)(2,1)S(1)}, bf16[1,512,1024]{2,1,0:T(8,128)(2,1)}, u32[]{:S(2)}) copy-start(bf16[1,512,1024]{2,1,0:T(8,128)(2,1)} %param.12) | copy-start | bytes 3145732
  126.4 9.9 %copy-start.6 = (bf16[512,512]{1,0:T(8,128)(2,1)S(1)}, bf16[512,512]{1,0:T(8,128)(2,1)}, u32[]{:S(2)}) copy-start(bf16[512,512]{1,0:T(8,128)(2,1)} %copy-done.5) | copy-start | bytes 1572868
  126.4 9.9 %copy-start.8 = (bf16[1,128,1024]{2,1,0:T(8,128)(2,1)S(1)}, bf16[1,128,1024]{2,1,0:T(8,128)(2,1)}, u32[]{:S(2)}) copy-start(bf16[1,128,1024]{2,1,0:T(8,128)(2,1)} %param.15) | copy-start | bytes 786436
  126.4 9.9 %copy-start.10 = (bf16[1,1024,128]{2,1,0:T(8,128)(2,1)S(1)}, bf16[1,1024,128]{2,1,0:T(8,128)(2,1)}, u32[]{:S(2)}) copy-start(bf16[1,1024,128]{2,1,0:T(8,128)(2,1)} %param.14) | copy-start | bytes 786436
  126.4 9.9 %copy-start.14 = (bf16[512,512]{1,0:T(8,128)(2,1)S(1)}, bf16[512,512]{1,0:T(8,128)(2,1)}, u32[]{:S(2)}) copy-start(bf16[512,512]{1,0:T(8,128)(2,1)} %copy-done.13) | copy-start | bytes 1572868
  126.4 9.9 %copy-start.26 = (f32[512,1]{1,0:T(8,128)S(1)}, f32[512,1]{1,0:T(8,128)}, u32[]{:S(2)}) copy-start(f32[512,1]{1,0:T(8,128)} %copy-done.25) | copy-start | bytes 6148
  126.4 9.9 %copy-start.28 = (f32[1,1024]{1,0:T(1,128)S(1)}, f32[1,1024]{1,0:T(1,128)}, u32[]{:S(2)}) copy-start(f32[1,1024]{1,0:T(1,128)} %refs_9_.1) | copy-start | bytes 12292
  127.9 13.6 %collective-permute-start.26 = (bf16[128,1024]{1,0:T(8,128)(2,1)S(1)}, bf16[128,1024]{1,0:T(8,128)(2,1)S(1)}, u32[]{:S(2)}, u32[]{:S(2)}) collective-permute-start(bf16[128,1024]{1,0:T(8,128)(2,1)S(1)} %slice.43), channel_id=1, source_target_pairs={{0,16},{8,24},{16,0},{24,8},{1,17},{9,25},{17,1},{25,9},{2,18},{10... | collective-permute-start | bytes 786440 | tf_op jit(solution)/shard_map/ppermute | solution.py:19
  (12 other events, 10.0 us)

commit v7 on v6

--- a/solution.py
+++ b/solution.py
@@ -33,36 +33,38 @@
     return [blocks[0]] + [swap(blocks[k], axis, k) for k in range(1, len(blocks))]
 
 
-def group_sum(rows, axis):
+def group_sum(rows, after, axis, where):
     groups = lax.axis_size(axis)
-    size = rows.shape[0] // groups
     step = groups // 2
     while step:
         other = swap(rows, axis, step)
-        other = [other[(k ^ step) * size : ((k ^ step) + 1) * size] for k in range(groups)]
-        rows = (rows.astype(f32) + jnp.concatenate(other).astype(f32)).astype(bf16)
+        if step == 1:
+            other, *_ = lax.optimization_barrier((other, *after))
+        kernel = functools.partial(moved_sum_kernel, groups, step)
+        (rows,) = run(kernel, [like(rows.shape)], where, [(rows, other)])
         step //= 2
     return rows
 
 
-def halved_sum(kept, given, after, axis, size):
+def halved_sum(kept, given, after, axis, size, where):
+    count = kept.shape[0] // size
     step = 1
     while True:
-        kept = (kept.astype(f32) + swap(given, axis, step).astype(f32)).astype(bf16)
+        other = swap(given, axis, step)
         if step == 1:
-            kept, after = lax.optimization_barrier((kept, after))
+            other, after = lax.optimization_barrier((other, after))
+        if count == 1:
+            return total([kept, other], where), after
+        half = like((count // 2 * size, kept.shape[1]))
+        kept, given = run(
+            functools.partial(halved_kernel, size), [half, half], where, [(kept, other)]
+        )
         step *= 2
-        if step == lax.axis_size(axis):
-            return kept, after
-        blocks = [kept[at : at + size] for at in range(0, kept.shape[0], size)]
-        kept, given = jnp.concatenate(blocks[::2]), jnp.concatenate(blocks[1::2])
-
-
-def total(blocks):
-    result = blocks[0].astype(f32)
-    for part in blocks[1:]:
-        result = result + part.astype(f32)
-    return result
+        count //= 2
+
+
+def total(blocks, where):
+    return run(total_kernel, [like(blocks[0].shape)], where, [blocks])[0]
 
 
 def block(array, axis, dim):
@@ -94,7 +96,7 @@
         + [pl.BlockSpec(memory_space=pltpu.VMEM)] * len(flat),
         out_specs=[pl.BlockSpec(memory_space=pltpu.VMEM)] * out_count,
         scratch_shapes=list(scratch),
-        compiler_params=pltpu.CompilerParams(vmem_limit_bytes=size + (12 << 20)),
+        compiler_params=pltpu.CompilerParams(vmem_limit_bytes=(10 << 20) if size < (10 << 20) else size + (12 << 20)),
         cost_estimate=pl.CostEstimate(flops=flops, bytes_accessed=size if flops else 0, transcendentals=0),
     )(where, *flat)
 
@@ -112,6 +114,33 @@
     @pl.loop(0, rows // chunk)
     def _(index):
         step(pl.ds(pl.multiple_of(index * chunk, chunk), chunk))
+
+
+def total_kernel(where, ins, outs, scratch):
+    (blocks,) = ins
+    result = blocks[0][...].astype(f32)
+    for part in blocks[1:]:
+        result = result + part[...].astype(f32)
+    outs[0][...] = result.astype(bf16)
+
+
+def moved_sum_kernel(groups, step, where, ins, outs, scratch):
+    ((mine, other),) = ins
+    size = mine.shape[0] // groups
+    for k in range(groups):
+        here = slice(k * size, (k + 1) * size)
+        there = slice((k ^ step) * size, ((k ^ step) + 1) * size)
+        value = mine[here, :].astype(f32) + other[there, :].astype(f32)
+        outs[0][here, :] = value.astype(bf16)
+
+
+def halved_kernel(size, where, ins, outs, scratch):
+    ((mine, other),) = ins
+    for k in range(mine.shape[0] // size):
+        here = slice(k * size, (k + 1) * size)
+        there = slice(k // 2 * size, (k // 2 + 1) * size)
+        value = mine[here, :].astype(f32) + other[here, :].astype(f32)
+        outs[k % 2][there, :] = value.astype(bf16)
 
 
 def gram_kernel(where, ins, outs, scratch):
@@ -156,7 +185,7 @@
         payload[(2 * j + 1) * cols : (2 * j + 2) * cols, :] = gram[:, relay:]
     start = 2 * head
     for end in ends:
-        payload[start : start + end.shape[0], :] = end[...]
+        payload[start : start + end.shape[0], :] = end[:, end.shape[1] - relay :]
         start += end.shape[0]
     for k, pack in enumerate(packs):
         here = slice(k * relay, (k + 1) * relay)
@@ -174,13 +203,13 @@
 def partial_kernel(where, ins, outs, scratch):
     heads, (fold,) = ins
     (whole,) = scratch
-    tokens = heads[0].shape[0]
+    tokens, width = heads[0].shape[0], fold.shape[0]
     cols = outs[0].shape[1]
     parts = len(outs)
     together = 4 if len(heads) % 4 == 0 else 1
     for first in range(0, len(heads), together):
         rows = slice(first * tokens, (first + together) * tokens)
-        values = jnp.concatenate([h[...] for h in heads[first : first + together]])
+        values = jnp.concatenate([h[:, :width] for h in heads[first : first + together]])
         whole[...] = dot(values, fold[...], NN)
         for k in range(parts):
             at = (where[0] ^ k) * cols
@@ -271,6 +300,8 @@
             outs[5][at, :] = returned
 
     by_rows(moved.shape[0], step)
+    if last:
+        outs[6][...] = outs[1][: outs[6].shape[0], : outs[6].shape[1]]
 
 
 def backward_kernel(width, live_section, last, tokens, where, ins, outs, scratch):
@@ -294,7 +325,8 @@
 
     by_rows(moved.shape[0], step)
     if last:
-        kept, given = outs[4:]
+        outs[6][...] = outs[1][: outs[6].shape[0], : outs[6].shape[1]]
+        kept, given = outs[4:6]
         groups = 2 * kept.shape[0] // tokens
         for k in range(groups):
             rows = slice(k * tokens, (k + 1) * tokens)
@@ -307,12 +339,12 @@
     heads, (code_grad, proj) = ins
     head_sum, enc_blocks = outs[0], outs[1:]
     (whole,) = scratch
-    tokens = heads[0].shape[0]
+    tokens, width = heads[0].shape[0], proj.shape[0]
     together = 4 if len(heads) % 4 == 0 else 1
     sums = None
     for first in range(0, len(heads), together):
         rows = slice(first * tokens, (first + together) * tokens)
-        values = jnp.concatenate([h[...] for h in heads[first : first + together]])
+        values = jnp.concatenate([h[:, :width] for h in heads[first : first + together]])
         term = dot(code_grad[rows, :], values, TN)
         sums = term if sums is None else sums + term
     head_sum[...] = sums.astype(bf16)
@@ -332,6 +364,10 @@
     (mix, mix_cols, received, incoming, row_scale, inner, dec, recv, send, gain), = ins
     sums = scratch
     relay = recv.shape[0]
+    size = sums[0].shape[0]
+    cols = slice(None)
+    if mix_cols.shape[1] > size:
+        cols = pl.ds(pl.multiple_of(where[1] * size, size), size)
     for ref in sums:
         ref[...] = jnp.zeros_like(ref)
 
@@ -345,7 +381,7 @@
         grad_norm = dot(incoming_here, send[...], NT)
         grad_mixed = scale * (grad_norm * gain[...] - normed * inner[at, :])
         grad_mixed = grad_mixed.astype(bf16)
-        sums[0][...] += dot(mix_cols[at, :], grad_mixed, TN)
+        sums[0][...] += dot(mix_cols[at, cols], grad_mixed, TN)
         sums[1][...] += jnp.sum(grad_norm * normed, axis=0, keepdims=True)
         sums[2][...] += dot(out_rows, incoming_here, TN)
         sums[3][...] += dot(received_here, grad_mixed, TN)
@@ -384,9 +420,8 @@
     head_cols, model_cols = proj.shape
     where = jnp.stack([lax.axis_index("tensor"), lax.axis_index("dp"), section]).astype(jnp.int32)
 
-    heads = gathered(heads_out[0], "dp")
     end = jnp.where(section == 0, input_code, code_cotangent)
-    ends = gathered(end, "dp")
+    heads = gathered(jnp.concatenate([heads_out[0], end], axis=1), "dp")
     packs = run(
         gram_kernel,
         [like((cols * codes // (2 * relay) + codes + relay, 2 * relay))] * parts,
@@ -394,7 +429,6 @@
         [(dec, recv, send, gain)],
         scratch=[pltpu.VMEM((codes, codes), f32)],
     )
-    enc, *_ = lax.optimization_barrier((enc, *ends))
     (fold,) = run(fold_kernel, [like((head_cols, codes))], where, [(proj, enc)])
     fold, _ = lax.optimization_barrier((fold, packs[0]))
     packs = scattered(packs, "tensor")
@@ -416,14 +450,13 @@
             like((codes, 2 * wide)),
         ],
         where,
-        [packs, ends],
-    )
-    arrived = scattered(partials, "tensor")
-    arrived, *_ = lax.optimization_barrier((arrived, *packs))
-    code_block = total(arrived).astype(bf16)
+        [packs, heads],
+    )
+    partials = list(partials)
+    partials[3], *_ = lax.optimization_barrier((partials[3], *packs))
+    code_block = total(scattered(partials, "tensor"), where)
     payloads = gathered(payload, "tensor")
-    mix_block = group_sum(code_block, "dp")
-    mix_block, *_ = lax.optimization_barrier((mix_block, *payloads))
+    mix_block = group_sum(code_block, payloads, "dp", where)
     mix_blocks = gathered(mix_block, "tensor")
 
     square_flops = 2 * rows * codes * codes
@@ -449,6 +482,7 @@
         shapes = [like((rows, wide)), like((rows, wide))]
         if last:
             shapes += [like((rows, wide), f32)] * 2 + [like((rows, 1), f32), like((rows, wide))]
+            shapes += [like((tokens, relay))]
         moved = move(sent, "pipe", 1)
         results = run(
             functools.partial(forward_kernel, width, turn, last),
@@ -458,14 +492,14 @@
             flops=square_flops,
         )
         received, sent = results[:2]
-    mixed, unscaled, row_scale, returned = results[2:]
+    mixed, unscaled, row_scale, returned, sent = results[2:]
     incoming = ends
     for turn in range(1, sections):
         last = turn == sections - 1
         shapes = [like((rows, wide)), like((rows, wide))]
         if last:
             shapes += [like((rows, 1), f32), like((rows, codes))]
-            shapes += [like((rows // 2, head_cols))] * 2
+            shapes += [like((rows // 2, head_cols))] * 2 + [like((tokens, relay))]
         moved = move(returned, "pipe", -1)
         results = run(
             functools.partial(backward_kernel, width, sections - 1 - turn, last, tokens),
@@ -488,9 +522,9 @@
             flops=3 * square_flops,
         )
         incoming, returned = results[:2]
-    inner, code_grad, kept, given = results[2:]
-
-    heads_grad, row_scale = halved_sum(kept, given, row_scale, "dp", tokens)
+    inner, code_grad, kept, given, returned = results[2:]
+
+    heads_grad, row_scale = halved_sum(kept, given, row_scale, "dp", tokens, where)
     head_sum, *enc_blocks = run(
         head_kernel,
         [like((codes, head_cols))] + [like((cols, model_cols))] * parts,
@@ -500,7 +534,7 @@
         flops=2 * head_cols * codes * (rows + model_cols),
     )
     head_sum, mix, *enc_blocks = lax.optimization_barrier((head_sum, mix, *enc_blocks))
-    enc_grad = total(scattered(enc_blocks, "tensor")).astype(bf16)
+    enc_grad = total(scattered(enc_blocks, "tensor"), where)
     (proj_grad,) = run(proj_kernel, [like((head_cols, model_cols))], where, [(head_sum, enc)])
     shapes = [(codes // groups, features), (1, features), (features, relay), (relay, features)]
     dec_grad, gain_grad, send_grad, recv_grad = run(
@@ -510,7 +544,7 @@
         [
             (
                 mix,
-                block(mix, "dp", 1),
+                mix if codes // groups % 128 == 0 else block(mix, "dp", 1),
                 received,
                 incoming,
                 row_scale,
@@ -523,10 +557,9 @@
         ],
         scratch=[pltpu.VMEM(shape, f32) for shape in shapes],
     )
-    sent, returned, enc_grad = lax.optimization_barrier((sent, returned, enc_grad))
     return (
-        sent[None, :tokens, :relay],
-        returned[None, :tokens, :relay],
+        sent[None],
+        returned[None],
         heads_grad[None],
         proj_grad[None],
         enc_grad[None],

time: 143 us -> 122 us (0.85)
  local copies, waits for them, and re-layouts: 17.3 us -> 5.43 us
  starting transfers between devices: 48.8 us -> 39.6 us
  Pallas kernels: 22.6 us -> 28.2 us
  waiting for transfers between devices: 48.6 us -> 45.6 us
  other arithmetic: 4.02 us -> 1.91 us
    unnamed x66 -> x20, local copies, waits for them, and re-layouts: 15.8 us -> 5.43 us
    ppermute x25 -> x22, starting transfers between devices: 46 us -> 36.8 us  [swap(): lax.ppermute(shard, axis, [(i, i ^ by) for i in range(lax.axis_size(axis))])]
    pallas_call x10 -> x16, Pallas kernels: 22.6 us -> 28.2 us  [run(): pl.pallas_call(body, out_shape=[jax.ShapeDtypeStruct(r.shape, r.dtype) fo...]
    ppermute x25 -> x22, waiting for transfers between devices: 44.8 us -> 41.8 us  [swap(): lax.ppermute(shard, axis, [(i, i ^ by) for i in range(lax.axis_size(axis))])]
    convert_element_type x5 -> x0, other arithmetic: 2.41 us -> none  [the longest x1 1.39 us: halved_sum(): kept = (kept.astype(f32) + swap(given, axis, step).astype(f32)).astype(bf16)]
  transfers between devices with their start and end apart: 27 -> 24, of which waited for: 15 -> 14; matrix products, arithmetic and copies ran while one was open for 3% -> 0% of each run, Pallas kernels for 11% -> 15%
where the time goes in v7:
time: 122 us
  waiting for transfers between devices  45.6 us (37%)
  starting transfers between devices  39.6 us (32%)
  Pallas kernels  28.2 us (23%)
  local copies, waits for them, and re-layouts  5.43 us (4%)
  other arithmetic  1.91 us (2%)
    ppermute x22, waiting for transfers between devices, swap(): lax.ppermute(shard, axis, [(i, i ^ by) for i in range(lax.axis_size(axis))])  41.8 us
    ppermute x22, starting transfers between devices, swap(): lax.ppermute(shard, axis, [(i, i ^ by) for i in range(lax.axis_size(axis))])  36.8 us
    pallas_call x16, Pallas kernels, run(): pl.pallas_call(body, out_shape=[jax.ShapeDtypeStruct(r.shape, r.dtype) fo...  28.2 us
    unnamed x20, local copies, waits for them, and re-layouts  5.43 us
    ppermute x2, waiting for transfers between devices, move(): return lax.ppermute(shard, axis, pairs)  3.81 us
    ppermute x2, starting transfers between devices, move(): return lax.ppermute(shard, axis, pairs)  2.78 us
  transfers between devices with their start and end apart: 24, of which 14 were waited for; matrix products, arithmetic and copies ran while one was open for 0% of the time, Pallas kernels for 15%

profile of v7, /device:TPU:0, one launch (start us, length us, event | category | flops | bytes accessed | tf_op | source)
XLA Modules:
  0.0 121.5 jit_solution(11126244892446077757)
XLA Ops:
  0.7 0.9 broadcast_select_fusion
  1.5 1.0 pad_maximum_fusion.refs_0_.refs_4_
  2.5 5.1 %collective-permute-start.2 = (bf16[128,1152]{1,0:T(8,128)(2,1)S(1)}, bf16[128,1152]{1,0:T(8,128)(2,1)S(1)}, u32[]{:S(2)}, u32[]{:S(2)}) collective-permute-start(bf16[128,1152]{1,0:T(8,128)(2,1)S(1)} %pad_maximum_fusion.refs_0_.refs_4_), channel_id=1, source_target_pairs={{0,24},{8,16},{16,8},{24,0},{1,25},{9,17},{17,9},{25,1},{2,26},{10... | collective-permute-start | bytes 884744 | tf_op jit(solution)/shard_map/ppermute | solution.py:19
  7.7 1.2 %copy-done.1 = bf16[1,512,1024]{2,1,0:T(8,128)(2,1)S(1)} copy-done((bf16[1,512,1024]{2,1,0:T(8,128)(2,1)S(1)}, bf16[1,512,1024]{2,1,0:T(8,128)(2,1)}, u32[]{:S(2)}) %copy-start.1) | copy-done | bytes 1048600
  8.9 0.9 copy-done.5
  9.9 0.9 copy-done.7
  11.5 2.0 %shard_map.161 = (bf16[896,256]{1,0:T(8,128)(2,1)S(1)}, bf16[896,256]{1,0:T(8,128)(2,1)S(1)}, bf16[896,256]{1,0:T(8,128)(2,1)S(1)}, bf16[896,256]{1,0:T(8,128)(2,1)S(1)}) custom-call(s32[3]{0:T(128)S(1)} %pad_add_fusion.where_ref, bf16[512,1024]{1,0:T(8,128)(2,1)S(1)} %bitcast.19, bf16[128,1024]{1,0:T(8,128)(2,1)S(1)} %bitcast.23, ...), custom_call_target="tpu_custom_call" | custom-call | tf_op jit(solution)/shard_map/pallas_call | solution.py:92
  13.5 1.6 %collective-permute-start.5 = (bf16[896,256]{1,0:T(8,128)(2,1)S(1)}, bf16[896,256]{1,0:T(8,128)(2,1)S(1)}, u32[]{:S(2)}, u32[]{:S(2)}) collective-permute-start(bf16[896,256]{1,0:T(8,128)(2,1)S(1)} %get-tuple-element.67), channel_id=1, source_target_pairs={{0,1},{1,0},{2,3},{3,2},{4,5},{5,4},{6,7},{7,6},{8,9},{9,8},{10,11... | collective-permute-start | bytes 1376264 | tf_op jit(solution)/shard_map/ppermute | solution.py:19
  15.0 1.5 %collective-permute-start.6 = (bf16[896,256]{1,0:T(8,128)(2,1)S(1)}, bf16[896,256]{1,0:T(8,128)(2,1)S(1)}, u32[]{:S(2)}, u32[]{:S(2)}) collective-permute-start(bf16[896,256]{1,0:T(8,128)(2,1)S(1)} %get-tuple-element.68), channel_id=1, source_target_pairs={{0,2},{1,3},{2,0},{3,1},{4,6},{5,7},{6,4},{7,5},{8,10},{9,11},{10,... | collective-permute-start | bytes 1376264 | tf_op jit(solution)/shard_map/ppermute | solution.py:19
  17.0 10.9 %collective-permute-start = (bf16[128,1152]{1,0:T(8,128)(2,1)S(1)}, bf16[128,1152]{1,0:T(8,128)(2,1)S(1)}, u32[]{:S(2)}, u32[]{:S(2)}) collective-permute-start(bf16[128,1152]{1,0:T(8,128)(2,1)S(1)} %pad_maximum_fusion.refs_0_.refs_4_), channel_id=1, source_target_pairs={{0,8},{8,0},{16,24},{24,16},{1,9},{9,1},{17,25},{25,17},{2,10},{10... | collective-permute-start | bytes 884744 | tf_op jit(solution)/shard_map/ppermute | solution.py:19
  27.9 1.6 %copy-done.3 = bf16[1,1024,1024]{2,1,0:T(8,128)(2,1)S(1)} copy-done((bf16[1,1024,1024]{2,1,0:T(8,128)(2,1)S(1)}, bf16[1,1024,1024]{2,1,0:T(8,128)(2,1)}, u32[]{:S(2)}) %copy-start.3) | copy-done | bytes 2097176
  29.5 1.8 %shard_map.160.refs_4_.refs_9_ = bf16[1024,512]{1,0:T(8,128)(2,1)S(1)} custom-call(s32[3]{0:T(128)S(1)} %pad_add_fusion.where_ref, bf16[1024,1024]{1,0:T(8,128)(2,1)S(1)} %bitcast.21, bf16[512,1024]{1,0:T(8,128)(2,1)S(1)} %bitcast.17), custom_call_target="tpu_custom_call" | custom-call | tf_op jit(solution)/shard_map/pallas_call | solution.py:92
  31.4 1.5 %collective-permute-done.1.refs_2_.refs_6_ = bf16[128,1152]{1,0:T(8,128)(2,1)S(1)} collective-permute-done((bf16[128,1152]{1,0:T(8,128)(2,1)S(1)}, bf16[128,1152]{1,0:T(8,128)(2,1)S(1)}, u32[]{:S(2)}, u32[]{:S(2)}) %collective-permute-start.1) | collective-permute-done | bytes 294944 | tf_op jit(solution)/shard_map/ppermute | solution.py:19
  32.8 6.0 %collective-permute-done.refs_1_.refs_5_ = bf16[128,1152]{1,0:T(8,128)(2,1)S(1)} collective-permute-done((bf16[128,1152]{1,0:T(8,128)(2,1)S(1)}, bf16[128,1152]{1,0:T(8,128)(2,1)S(1)}, u32[]{:S(2)}, u32[]{:S(2)}) %collective-permute-start) | collective-permute-done | bytes 294944 | tf_op jit(solution)/shard_map/ppermute | solution.py:19
  38.9 1.4 %shard_map.162 = (bf16[512,128]{1,0:T(8,128)(2,1)S(1)}, bf16[512,128]{1,0:T(8,128)(2,1)S(1)}, bf16[512,128]{1,0:T(8,128)(2,1)S(1)}, bf16[512,128]{1,0:T(8,128)(2,1)S(1)}) custom-call(s32[3]{0:T(128)S(1)} %pad_add_fusion.where_ref, bf16[128,1152]{1,0:T(8,128)(2,1)S(1)} %pad_maximum_fusion.refs_0_.refs_4_, ...), custom_call_target="tpu_custom_call" | custom-call | flops 536870912 | bytes 2752512 | tf_op jit(solution)/shard_map/pallas_call | solution.py:92
  40.2 1.6 %collective-permute-start.3 = (bf16[512,128]{1,0:T(8,128)(2,1)S(1)}, bf16[512,128]{1,0:T(8,128)(2,1)S(1)}, u32[]{:S(2)}, u32[]{:S(2)}) collective-permute-start(bf16[512,128]{1,0:T(8,128)(2,1)S(1)} %get-tuple-element.64), channel_id=1, source_target_pairs={{0,1},{1,0},{2,3},{3,2},{4,5},{5,4},{6,7},{7,6},{8,9},{9,8},{10,11... | collective-permute-start | bytes 393224 | tf_op jit(solution)/shard_map/ppermute | solution.py:19
  41.8 1.5 %collective-permute-start.4 = (bf16[512,128]{1,0:T(8,128)(2,1)S(1)}, bf16[512,128]{1,0:T(8,128)(2,1)S(1)}, u32[]{:S(2)}, u32[]{:S(2)}) collective-permute-start(bf16[512,128]{1,0:T(8,128)(2,1)S(1)} %get-tuple-element.65), channel_id=1, source_target_pairs={{0,2},{1,3},{2,0},{3,1},{4,6},{5,7},{6,4},{7,5},{8,10},{9,11},{10,... | collective-permute-start | bytes 393224 | tf_op jit(solution)/shard_map/ppermute | solution.py:19
  43.9 0.9 shard_map.165
  44.8 2.5 %collective-permute-start.13 = (bf16[1024,128]{1,0:T(8,128)(2,1)S(1)}, bf16[1024,128]{1,0:T(8,128)(2,1)S(1)}, u32[]{:S(2)}, u32[]{:S(2)}) collective-permute-start(bf16[1024,128]{1,0:T(8,128)(2,1)S(1)} %get-tuple-element.71.refs_4_), channel_id=1, source_target_pairs={{0,3},{1,2},{2,1},{3,0},{4,7},{5,6},{6,5},{7,4},{8,11},{9,10},{10,... | collective-permute-start | bytes 786440 | tf_op jit(solution)/shard_map/ppermute | solution.py:19
  47.3 8.1 %collective-permute-done.4.refs_2_ = bf16[512,128]{1,0:T(8,128)(2,1)S(1)} collective-permute-done((bf16[512,128]{1,0:T(8,128)(2,1)S(1)}, bf16[512,128]{1,0:T(8,128)(2,1)S(1)}, u32[]{:S(2)}, u32[]{:S(2)}) %collective-permute-start.4) | collective-permute-done | bytes 131104 | tf_op jit(solution)/shard_map/ppermute | solution.py:19
  56.6 2.0 %collective-permute-start.12 = (bf16[1024,128]{1,0:T(8,128)(2,1)S(1)}, bf16[1024,128]{1,0:T(8,128)(2,1)S(1)}, u32[]{:S(2)}, u32[]{:S(2)}) collective-permute-start(bf16[1024,128]{1,0:T(8,128)(2,1)S(1)} %get-tuple-element.71.refs_4_), channel_id=1, source_target_pairs={{0,2},{1,3},{2,0},{3,1},{4,6},{5,7},{6,4},{7,5},{8,10},{9,11},{10,... | collective-permute-start | bytes 786440 | tf_op jit(solution)/shard_map/ppermute | solution.py:19
  58.6 3.7 %collective-permute-done.9.refs_1_ = bf16[512,128]{1,0:T(8,128)(2,1)S(1)} collective-permute-done((bf16[512,128]{1,0:T(8,128)(2,1)S(1)}, bf16[512,128]{1,0:T(8,128)(2,1)S(1)}, u32[]{:S(2)}, u32[]{:S(2)}) %collective-permute-start.9) | collective-permute-done | bytes 131104 | tf_op jit(solution)/shard_map/ppermute | solution.py:19
  63.1 3.1 %collective-permute-done.11.refs_5_ = bf16[1024,128]{1,0:T(8,128)(2,1)S(1)} collective-permute-done((bf16[1024,128]{1,0:T(8,128)(2,1)S(1)}, bf16[1024,128]{1,0:T(8,128)(2,1)S(1)}, u32[]{:S(2)}, u32[]{:S(2)}) %collective-permute-start.11) | collective-permute-done | bytes 262176 | tf_op jit(solution)/shard_map/ppermute | solution.py:19
  66.2 1.7 %collective-permute-done.10.refs_1_ = bf16[512,128]{1,0:T(8,128)(2,1)S(1)} collective-permute-done((bf16[512,128]{1,0:T(8,128)(2,1)S(1)}, bf16[512,128]{1,0:T(8,128)(2,1)S(1)}, u32[]{:S(2)}, u32[]{:S(2)}) %collective-permute-start.10) | collective-permute-done | bytes 131104 | tf_op jit(solution)/shard_map/ppermute | solution.py:19
  68.5 1.5 %collective-permute-start.16 = (bf16[512,128]{1,0:T(8,128)(2,1)S(1)}, bf16[512,128]{1,0:T(8,128)(2,1)S(1)}, u32[]{:S(2)}, u32[]{:S(2)}) collective-permute-start(bf16[512,128]{1,0:T(8,128)(2,1)S(1)} %shard_map.166.refs_0_), channel_id=1, source_target_pairs={{0,3},{1,2},{2,1},{3,0},{4,7},{5,6},{6,5},{7,4},{8,11},{9,10},{10,... | collective-permute-start | bytes 393224 | tf_op jit(solution)/shard_map/ppermute | solution.py:19
  70.0 1.1 collective-permute-start.15
  71.1 1.4 %collective-permute-start.14 = (bf16[512,128]{1,0:T(8,128)(2,1)S(1)}, bf16[512,128]{1,0:T(8,128)(2,1)S(1)}, u32[]{:S(2)}, u32[]{:S(2)}) collective-permute-start(bf16[512,128]{1,0:T(8,128)(2,1)S(1)} %shard_map.166.refs_0_), channel_id=1, source_target_pairs={{0,1},{1,0},{2,3},{3,2},{4,5},{5,4},{6,7},{7,6},{8,9},{9,8},{10,11... | collective-permute-start | bytes 393224 | tf_op jit(solution)/shard_map/ppermute | solution.py:19
  72.5 2.0 %collective-permute-done.16.refs_3_ = bf16[512,128]{1,0:T(8,128)(2,1)S(1)} collective-permute-done((bf16[512,128]{1,0:T(8,128)(2,1)S(1)}, bf16[512,128]{1,0:T(8,128)(2,1)S(1)}, u32[]{:S(2)}, u32[]{:S(2)}) %collective-permute-start.16) | collective-permute-done | bytes 131104 | tf_op jit(solution)/shard_map/ppermute | solution.py:19
  74.5 1.3 %collective-permute-done.15.refs_2_ = bf16[512,128]{1,0:T(8,128)(2,1)S(1)} collective-permute-done((bf16[512,128]{1,0:T(8,128)(2,1)S(1)}, bf16[512,128]{1,0:T(8,128)(2,1)S(1)}, u32[]{:S(2)}, u32[]{:S(2)}) %collective-permute-start.15) | collective-permute-done | bytes 131104 | tf_op jit(solution)/shard_map/ppermute | solution.py:19
  75.8 1.1 collective-permute-done.14.refs_1_
  76.9 2.1 %shard_map.167 = (bf16[512,512]{1,0:T(8,128)(2,1)S(1)}, bf16[512,512]{1,0:T(8,128)(2,1)S(1)}, f32[512,512]{1,0:T(8,128)S(1)}, f32[512,512]{1,0:T(8,128)S(1)}, f3...) custom-call(s32[3]{0:T(128)S(1)} %pad_add_fusion.where_ref, ...), custom_call_target="tpu_custom_call" | custom-call | flops 805306368 | bytes 7604224 | tf_op jit(solution)/shard_map/pallas_call | solution.py:92
  79.0 1.3 %collective-permute-start.17 = (bf16[512,512]{1,0:T(8,128)(2,1)S(1)}, bf16[512,512]{1,0:T(8,128)(2,1)S(1)}, u32[]{:S(2)}, u32[]{:S(2)}) collective-permute-start(bf16[512,512]{1,0:T(8,128)(2,1)S(1)} %get-tuple-element.75), channel_id=1, source_target_pairs={{0,4},{1,5},{2,6},{3,7},{8,12},{9,13},{10,14},{11,15},{16,20},{17,... | collective-permute-start | bytes 1572872 | tf_op jit(solution)/shard_map/ppermute | solution.py:25
  80.3 1.5 %collective-permute-done.17.refs_0_ = bf16[512,512]{1,0:T(8,128)(2,1)S(1)} collective-permute-done((bf16[512,512]{1,0:T(8,128)(2,1)S(1)}, bf16[512,512]{1,0:T(8,128)(2,1)S(1)}, u32[]{:S(2)}, u32[]{:S(2)}) %collective-permute-start.17) | collective-permute-done | bytes 524320 | tf_op jit(solution)/shard_map/ppermute | solution.py:25
  81.8 2.5 %shard_map.168 = (bf16[512,512]{1,0:T(8,128)(2,1)S(1)}, bf16[512,512]{1,0:T(8,128)(2,1)}, f32[512,512]{1,0:T(8,128)S(1)}, f32[512,512]{1,0:T(8,128)S(1)}, f32[51...) custom-call(s32[3]{0:T(128)S(1)} %pad_add_fusion.where_ref, ...), custom_call_target="tpu_custom_call" | custom-call | flops 268435456 | bytes 7639040 | tf_op jit(solution)/shard_map/pallas_call | solution.py:92
  84.3 1.5 %collective-permute-start.18 = (bf16[512,512]{1,0:T(8,128)(2,1)S(1)}, bf16[512,512]{1,0:T(8,128)(2,1)S(1)}, u32[]{:S(2)}, u32[]{:S(2)}) collective-permute-start(bf16[512,512]{1,0:T(8,128)(2,1)S(1)} %get-tuple-element.81), channel_id=1, source_target_pairs={{4,0},{5,1},{6,2},{7,3},{12,8},{13,9},{14,10},{15,11},{20,16},{21,... | collective-permute-start | bytes 1572872 | tf_op jit(solution)/shard_map/ppermute | solution.py:25
  85.8 2.3 %collective-permute-done.18.refs_0_ = bf16[512,512]{1,0:T(8,128)(2,1)S(1)} collective-permute-done((bf16[512,512]{1,0:T(8,128)(2,1)S(1)}, bf16[512,512]{1,0:T(8,128)(2,1)S(1)}, u32[]{:S(2)}, u32[]{:S(2)}) %collective-permute-start.18) | collective-permute-done | bytes 524320 | tf_op jit(solution)/shard_map/ppermute | solution.py:25
  88.1 3.3 %shard_map.169 = (bf16[512,512]{1,0:T(8,128)(2,1)S(1)}, bf16[512,512]{1,0:T(8,128)(2,1)}, f32[512,1]{1,0:T(8,128)S(1)}, bf16[512,512]{1,0:T(8,128)(2,1)S(1)}, bf...) custom-call(s32[3]{0:T(128)S(1)} %pad_add_fusion.where_ref, ...), custom_call_target="tpu_custom_call" | custom-call | flops 805306368 | bytes 9736192 | tf_op jit(solution)/shard_map/pallas_call | solution.py:92
  91.4 2.5 %shard_map.172 = (bf16[512,1024]{1,0:T(8,128)(2,1)S(1)}, bf16[128,1024]{1,0:T(8,128)(2,1)S(1)}, bf16[128,1024]{1,0:T(8,128)(2,1)S(1)}, bf16[128,1024]{1,0:T(8,128)(2,1)S(1)}, bf16[128,1024]{1,0:T(8,128)(2,1)S(1)}) custom-call(s32[3]{0:T(128)S(1)} %pad_add_fusion.where_ref, bf16[128,1152]{1,0:T(8,128)(2,1)S(1)} %pad_maximum_fusion.refs_0_.refs_4_, ...), custom_call_target="tpu_custom_call" | custom-call | flops 1610612736 | bytes 5898240 | tf_op jit(solution)/shard_map/pallas_call | solution.py:92
  93.9 1.5 %collective-permute-start.21 = (bf16[128,1024]{1,0:T(8,128)(2,1)S(1)}, bf16[128,1024]{1,0:T(8,128)(2,1)S(1)}, u32[]{:S(2)}, u32[]{:S(2)}) collective-permute-start(bf16[128,1024]{1,0:T(8,128)(2,1)S(1)} %get-tuple-element.102), channel_id=1, source_target_pairs={{0,1},{1,0},{2,3},{3,2},{4,5},{5,4},{6,7},{7,6},{8,9},{9,8},{10,11... | collective-permute-start | bytes 786440 | tf_op jit(solution)/shard_map/ppermute | solution.py:19
  95.4 1.2 collective-permute-start.22
  96.6 0.9 collective-permute-start.23
  97.5 7.9 %collective-permute-done.19.refs_1_ = bf16[256,1024]{1,0:T(8,128)(2,1)S(1)} collective-permute-done((bf16[256,1024]{1,0:T(8,128)(2,1)S(1)}, bf16[256,1024]{1,0:T(8,128)(2,1)S(1)}, u32[]{:S(2)}, u32[]{:S(2)}) %collective-permute-start.19) | collective-permute-done | bytes 524320 | tf_op jit(solution)/shard_map/ppermute | solution.py:19
  106.1 0.8 collective-permute-start.20
  106.9 3.2 %shard_map.173 = bf16[1024,1024]{1,0:T(8,128)(2,1)} custom-call(s32[3]{0:T(128)S(1)} %pad_add_fusion.where_ref, bf16[512,1024]{1,0:T(8,128)(2,1)S(1)} %get-tuple-element.100.refs_0_, bf16[512,1024]{1,0:T(8,128)(2,1)S(1)} %bitcast.18), custom_call_target="tpu_custom_call" | custom-call | tf_op jit(solution)/shard_map/pallas_call | solution.py:92
  110.1 1.4 %shard_map.174 = bf16[128,1024]{1,0:T(8,128)(2,1)} custom-call(s32[3]{0:T(128)S(1)} %pad_add_fusion.where_ref, bf16[128,1024]{1,0:T(8,128)(2,1)S(1)} %get-tuple-element.101.refs_0_, bf16[128,1024]{1,0:T(8,128)(2,1)S(1)} %collective-permute-done.21.refs_1_, bf16[128,1024]{1,0:T(8,128)(2,1)S(1)} %collective-permute-done.22.refs_2_, ...), custom_call_target="tpu_custom_call" | custom-call | tf_op jit(solution)/shard_map/pallas_call | solution.py:92
  111.5 3.5 %shard_map.175 = (bf16[128,1024]{1,0:T(8,128)(2,1)}, f32[1,1024]{1,0:T(1,128)}, bf16[1024,128]{1,0:T(8,128)(2,1)}, bf16[128,1024]{1,0:T(8,128)(2,1)}) custom-call(s32[3]{0:T(128)S(1)} %pad_add_fusion.where_ref, bf16[512,512]{1,0:T(8,128)(2,1)S(1)} %get-tuple-element.105.refs_0_.refs_1_, bf16[512,512]{1,0:T(8,128)(2,1)S(1)} %get-tuple-element.105.refs_0_.refs_1_, ...), custom_call_target="tpu_custom_call" | custom-call | tf_op jit(solution)/shard_map/pallas_call | solution.py:92
  114.9 5.3 %collective-permute-done.20.refs_1_ = bf16[128,1024]{1,0:T(8,128)(2,1)S(1)} collective-permute-done((bf16[128,1024]{1,0:T(8,128)(2,1)S(1)}, bf16[128,1024]{1,0:T(8,128)(2,1)S(1)}, u32[]{:S(2)}, u32[]{:S(2)}) %collective-permute-start.20) | collective-permute-done | bytes 262176 | tf_op jit(solution)/shard_map/ppermute | solution.py:19
  120.2 1.3 %shard_map.171 = bf16[128,1024]{1,0:T(8,128)(2,1)} custom-call(s32[3]{0:T(128)S(1)} %pad_add_fusion.where_ref, bf16[128,1024]{1,0:T(8,128)(2,1)S(1)} %get-tuple-element.91.refs_0_, bf16[128,1024]{1,0:T(8,128)(2,1)S(1)} %collective-permute-done.20.refs_1_), custom_call_target="tpu_custom_call" | custom-call | tf_op jit(solution)/shard_map/pallas_call | solution.py:92
  (39 shorter events, 5.1 us)
Async XLA Ops:
  0.6 27.3 %copy-start = (bf16[1,512,1024]{2,1,0:T(8,128)(2,1)S(1)}, bf16[1,512,1024]{2,1,0:T(8,128)(2,1)}, u32[]{:S(2)}) copy-start(bf16[1,512,1024]{2,1,0:T(8,128)(2,1)} %param.11) | copy-start | bytes 3145732
  2.5 14.6 %collective-permute-start.2 = (bf16[128,1152]{1,0:T(8,128)(2,1)S(1)}, bf16[128,1152]{1,0:T(8,128)(2,1)S(1)}, u32[]{:S(2)}, u32[]{:S(2)}) collective-permute-start(bf16[128,1152]{1,0:T(8,128)(2,1)S(1)} %pad_maximum_fusion.refs_0_.refs_4_), channel_id=1, source_target_pairs={{0,24},{8,16},{16,8},{24,0},{1,25},{9,17},{17,9},{25,1},{2,26},{10... | collective-permute-start | bytes 884744 | tf_op jit(solution)/shard_map/ppermute | solution.py:19
  7.7 1.2 %copy-start.1 = (bf16[1,512,1024]{2,1,0:T(8,128)(2,1)S(1)}, bf16[1,512,1024]{2,1,0:T(8,128)(2,1)}, u32[]{:S(2)}) copy-start(bf16[1,512,1024]{2,1,0:T(8,128)(2,1)} %param.12) | copy-start | bytes 3145732
  8.9 0.9 copy-start.5
  9.9 0.9 copy-start.7
  10.8 0.7 copy-start.9
  13.5 29.8 %collective-permute-start.5 = (bf16[896,256]{1,0:T(8,128)(2,1)S(1)}, bf16[896,256]{1,0:T(8,128)(2,1)S(1)}, u32[]{:S(2)}, u32[]{:S(2)}) collective-permute-start(bf16[896,256]{1,0:T(8,128)(2,1)S(1)} %get-tuple-element.67), channel_id=1, source_target_pairs={{0,1},{1,0},{2,3},{3,2},{4,5},{5,4},{6,7},{7,6},{8,9},{9,8},{10,11... | collective-permute-start | bytes 1376264 | tf_op jit(solution)/shard_map/ppermute | solution.py:19
  15.0 28.3 %collective-permute-start.6 = (bf16[896,256]{1,0:T(8,128)(2,1)S(1)}, bf16[896,256]{1,0:T(8,128)(2,1)S(1)}, u32[]{:S(2)}, u32[]{:S(2)}) collective-permute-start(bf16[896,256]{1,0:T(8,128)(2,1)S(1)} %get-tuple-element.68), channel_id=1, source_target_pairs={{0,2},{1,3},{2,0},{3,1},{4,6},{5,7},{6,4},{7,5},{8,10},{9,11},{10,... | collective-permute-start | bytes 1376264 | tf_op jit(solution)/shard_map/ppermute | solution.py:19
  16.6 26.8 %collective-permute-start.7 = (bf16[896,256]{1,0:T(8,128)(2,1)S(1)}, bf16[896,256]{1,0:T(8,128)(2,1)S(1)}, u32[]{:S(2)}, u32[]{:S(2)}) collective-permute-start(bf16[896,256]{1,0:T(8,128)(2,1)S(1)} %get-tuple-element.69), channel_id=1, source_target_pairs={{0,3},{1,2},{2,1},{3,0},{4,7},{5,6},{6,5},{7,4},{8,11},{9,10},{10,... | collective-permute-start | bytes 1376264 | tf_op jit(solution)/shard_map/ppermute | solution.py:19
  17.0 15.8 %collective-permute-start.1 = (bf16[128,1152]{1,0:T(8,128)(2,1)S(1)}, bf16[128,1152]{1,0:T(8,128)(2,1)S(1)}, u32[]{:S(2)}, u32[]{:S(2)}) collective-permute-start(bf16[128,1152]{1,0:T(8,128)(2,1)S(1)} %pad_maximum_fusion.refs_0_.refs_4_), channel_id=1, source_target_pairs={{0,16},{8,24},{16,0},{24,8},{1,17},{9,25},{17,1},{25,9},{2,18},{10... | collective-permute-start | bytes 884744 | tf_op jit(solution)/shard_map/ppermute | solution.py:19
  17.0 21.8 %collective-permute-start = (bf16[128,1152]{1,0:T(8,128)(2,1)S(1)}, bf16[128,1152]{1,0:T(8,128)(2,1)S(1)}, u32[]{:S(2)}, u32[]{:S(2)}) collective-permute-start(bf16[128,1152]{1,0:T(8,128)(2,1)S(1)} %pad_maximum_fusion.refs_0_.refs_4_), channel_id=1, source_target_pairs={{0,8},{8,0},{16,24},{24,16},{1,9},{9,1},{17,25},{25,17},{2,10},{10... | collective-permute-start | bytes 884744 | tf_op jit(solution)/shard_map/ppermute | solution.py:19
  27.9 1.6 %copy-start.3 = (bf16[1,1024,1024]{2,1,0:T(8,128)(2,1)S(1)}, bf16[1,1024,1024]{2,1,0:T(8,128)(2,1)}, u32[]{:S(2)}) copy-start(bf16[1,1024,1024]{2,1,0:T(8,128)(2,1)} %param.10) | copy-start | bytes 6291460
  40.2 7.1 %collective-permute-start.3 = (bf16[512,128]{1,0:T(8,128)(2,1)S(1)}, bf16[512,128]{1,0:T(8,128)(2,1)S(1)}, u32[]{:S(2)}, u32[]{:S(2)}) collective-permute-start(bf16[512,128]{1,0:T(8,128)(2,1)S(1)} %get-tuple-element.64), channel_id=1, source_target_pairs={{0,1},{1,0},{2,3},{3,2},{4,5},{5,4},{6,7},{7,6},{8,9},{9,8},{10,11... | collective-permute-start | bytes 393224 | tf_op jit(solution)/shard_map/ppermute | solution.py:19
  41.8 13.6 %collective-permute-start.4 = (bf16[512,128]{1,0:T(8,128)(2,1)S(1)}, bf16[512,128]{1,0:T(8,128)(2,1)S(1)}, u32[]{:S(2)}, u32[]{:S(2)}) collective-permute-start(bf16[512,128]{1,0:T(8,128)(2,1)S(1)} %get-tuple-element.65), channel_id=1, source_target_pairs={{0,2},{1,3},{2,0},{3,1},{4,6},{5,7},{6,4},{7,5},{8,10},{9,11},{10,... | collective-permute-start | bytes 393224 | tf_op jit(solution)/shard_map/ppermute | solution.py:19
  43.3 12.1 %collective-permute-start.8 = (bf16[512,128]{1,0:T(8,128)(2,1)S(1)}, bf16[512,128]{1,0:T(8,128)(2,1)S(1)}, u32[]{:S(2)}, u32[]{:S(2)}) collective-permute-start(bf16[512,128]{1,0:T(8,128)(2,1)S(1)} %get-tuple-element.70), channel_id=1, source_target_pairs={{0,3},{1,2},{2,1},{3,0},{4,7},{5,6},{6,5},{7,4},{8,11},{9,10},{10,... | collective-permute-start | bytes 393224 | tf_op jit(solution)/shard_map/ppermute | solution.py:19
  44.8 18.2 %collective-permute-start.13 = (bf16[1024,128]{1,0:T(8,128)(2,1)S(1)}, bf16[1024,128]{1,0:T(8,128)(2,1)S(1)}, u32[]{:S(2)}, u32[]{:S(2)}) collective-permute-start(bf16[1024,128]{1,0:T(8,128)(2,1)S(1)} %get-tuple-element.71.refs_4_), channel_id=1, source_target_pairs={{0,3},{1,2},{2,1},{3,0},{4,7},{5,6},{6,5},{7,4},{8,11},{9,10},{10,... | collective-permute-start | bytes 786440 | tf_op jit(solution)/shard_map/ppermute | solution.py:19
  56.0 6.3 %collective-permute-start.9 = (bf16[512,128]{1,0:T(8,128)(2,1)S(1)}, bf16[512,128]{1,0:T(8,128)(2,1)S(1)}, u32[]{:S(2)}, u32[]{:S(2)}) collective-permute-start(bf16[512,128]{1,0:T(8,128)(2,1)S(1)} %shard_map.163.refs_0_), channel_id=1, source_target_pairs={{0,16},{8,24},{16,0},{24,8},{1,17},{9,25},{17,1},{25,9},{2,18},{10... | collective-permute-start | bytes 393224 | tf_op jit(solution)/shard_map/ppermute | solution.py:19
  56.6 6.4 %collective-permute-start.12 = (bf16[1024,128]{1,0:T(8,128)(2,1)S(1)}, bf16[1024,128]{1,0:T(8,128)(2,1)S(1)}, u32[]{:S(2)}, u32[]{:S(2)}) collective-permute-start(bf16[1024,128]{1,0:T(8,128)(2,1)S(1)} %get-tuple-element.71.refs_4_), channel_id=1, source_target_pairs={{0,2},{1,3},{2,0},{3,1},{4,6},{5,7},{6,4},{7,5},{8,10},{9,11},{10,... | collective-permute-start | bytes 786440 | tf_op jit(solution)/shard_map/ppermute | solution.py:19
  58.6 7.6 %collective-permute-start.11 = (bf16[1024,128]{1,0:T(8,128)(2,1)S(1)}, bf16[1024,128]{1,0:T(8,128)(2,1)S(1)}, u32[]{:S(2)}, u32[]{:S(2)}) collective-permute-start(bf16[1024,128]{1,0:T(8,128)(2,1)S(1)} %get-tuple-element.71.refs_4_), channel_id=1, source_target_pairs={{0,1},{1,0},{2,3},{3,2},{4,5},{5,4},{6,7},{7,6},{8,9},{9,8},{10,11... | collective-permute-start | bytes 786440 | tf_op jit(solution)/shard_map/ppermute | solution.py:19
  62.9 5.0 %collective-permute-start.10 = (bf16[512,128]{1,0:T(8,128)(2,1)S(1)}, bf16[512,128]{1,0:T(8,128)(2,1)S(1)}, u32[]{:S(2)}, u32[]{:S(2)}) collective-permute-start(bf16[512,128]{1,0:T(8,128)(2,1)S(1)} %shard_map.164.refs_0_), channel_id=1, source_target_pairs={{0,8},{8,0},{16,24},{24,16},{1,9},{9,1},{17,25},{25,17},{2,10},{10... | collective-permute-start | bytes 393224 | tf_op jit(solution)/shard_map/ppermute | solution.py:19
  68.5 6.0 %collective-permute-start.16 = (bf16[512,128]{1,0:T(8,128)(2,1)S(1)}, bf16[512,128]{1,0:T(8,128)(2,1)S(1)}, u32[]{:S(2)}, u32[]{:S(2)}) collective-permute-start(bf16[512,128]{1,0:T(8,128)(2,1)S(1)} %shard_map.166.refs_0_), channel_id=1, source_target_pairs={{0,3},{1,2},{2,1},{3,0},{4,7},{5,6},{6,5},{7,4},{8,11},{9,10},{10,... | collective-permute-start | bytes 393224 | tf_op jit(solution)/shard_map/ppermute | solution.py:19
  70.0 5.8 %collective-permute-start.15 = (bf16[512,128]{1,0:T(8,128)(2,1)S(1)}, bf16[512,128]{1,0:T(8,128)(2,1)S(1)}, u32[]{:S(2)}, u32[]{:S(2)}) collective-permute-start(bf16[512,128]{1,0:T(8,128)(2,1)S(1)} %shard_map.166.refs_0_), channel_id=1, source_target_pairs={{0,2},{1,3},{2,0},{3,1},{4,6},{5,7},{6,4},{7,5},{8,10},{9,11},{10,... | collective-permute-start | bytes 393224 | tf_op jit(solution)/shard_map/ppermute | solution.py:19
  71.1 5.8 %collective-permute-start.14 = (bf16[512,128]{1,0:T(8,128)(2,1)S(1)}, bf16[512,128]{1,0:T(8,128)(2,1)S(1)}, u32[]{:S(2)}, u32[]{:S(2)}) collective-permute-start(bf16[512,128]{1,0:T(8,128)(2,1)S(1)} %shard_map.166.refs_0_), channel_id=1, source_target_pairs={{0,1},{1,0},{2,3},{3,2},{4,5},{5,4},{6,7},{7,6},{8,9},{9,8},{10,11... | collective-permute-start | bytes 393224 | tf_op jit(solution)/shard_map/ppermute | solution.py:19
  79.0 2.8 %collective-permute-start.17 = (bf16[512,512]{1,0:T(8,128)(2,1)S(1)}, bf16[512,512]{1,0:T(8,128)(2,1)S(1)}, u32[]{:S(2)}, u32[]{:S(2)}) collective-permute-start(bf16[512,512]{1,0:T(8,128)(2,1)S(1)} %get-tuple-element.75), channel_id=1, source_target_pairs={{0,4},{1,5},{2,6},{3,7},{8,12},{9,13},{10,14},{11,15},{16,20},{17,... | collective-permute-start | bytes 1572872 | tf_op jit(solution)/shard_map/ppermute | solution.py:25
  84.3 3.8 %collective-permute-start.18 = (bf16[512,512]{1,0:T(8,128)(2,1)S(1)}, bf16[512,512]{1,0:T(8,128)(2,1)S(1)}, u32[]{:S(2)}, u32[]{:S(2)}) collective-permute-start(bf16[512,512]{1,0:T(8,128)(2,1)S(1)} %get-tuple-element.81), channel_id=1, source_target_pairs={{4,0},{5,1},{6,2},{7,3},{12,8},{13,9},{14,10},{15,11},{20,16},{21,... | collective-permute-start | bytes 1572872 | tf_op jit(solution)/shard_map/ppermute | solution.py:25
  88.1 3.3 %copy-start.4 = (bf16[1,1024,1024]{2,1,0:T(8,128)(2,1)S(1)}, bf16[1,1024,1024]{2,1,0:T(8,128)(2,1)}, u32[]{:S(2)}) copy-start(bf16[1,1024,1024]{2,1,0:T(8,128)(2,1)} %param.10) | copy-start | bytes 6291460
  91.4 14.0 %collective-permute-start.19 = (bf16[256,1024]{1,0:T(8,128)(2,1)S(1)}, bf16[256,1024]{1,0:T(8,128)(2,1)S(1)}, u32[]{:S(2)}, u32[]{:S(2)}) collective-permute-start(bf16[256,1024]{1,0:T(8,128)(2,1)S(1)} %get-tuple-element.89), channel_id=1, source_target_pairs={{0,8},{8,0},{16,24},{24,16},{1,9},{9,1},{17,25},{25,17},{2,10},{10... | collective-permute-start | bytes 1572872 | tf_op jit(solution)/shard_map/ppermute | solution.py:19
  93.9 16.2 %collective-permute-start.21 = (bf16[128,1024]{1,0:T(8,128)(2,1)S(1)}, bf16[128,1024]{1,0:T(8,128)(2,1)S(1)}, u32[]{:S(2)}, u32[]{:S(2)}) collective-permute-start(bf16[128,1024]{1,0:T(8,128)(2,1)S(1)} %get-tuple-element.102), channel_id=1, source_target_pairs={{0,1},{1,0},{2,3},{3,2},{4,5},{5,4},{6,7},{7,6},{8,9},{9,8},{10,11... | collective-permute-start | bytes 786440 | tf_op jit(solution)/shard_map/ppermute | solution.py:19
  95.4 14.7 %collective-permute-start.22 = (bf16[128,1024]{1,0:T(8,128)(2,1)S(1)}, bf16[128,1024]{1,0:T(8,128)(2,1)S(1)}, u32[]{:S(2)}, u32[]{:S(2)}) collective-permute-start(bf16[128,1024]{1,0:T(8,128)(2,1)S(1)} %get-tuple-element.103), channel_id=1, source_target_pairs={{0,2},{1,3},{2,0},{3,1},{4,6},{5,7},{6,4},{7,5},{8,10},{9,11},{10,... | collective-permute-start | bytes 786440 | tf_op jit(solution)/shard_map/ppermute | solution.py:19
  96.6 13.5 %collective-permute-start.23 = (bf16[128,1024]{1,0:T(8,128)(2,1)S(1)}, bf16[128,1024]{1,0:T(8,128)(2,1)S(1)}, u32[]{:S(2)}, u32[]{:S(2)}) collective-permute-start(bf16[128,1024]{1,0:T(8,128)(2,1)S(1)} %get-tuple-element.104), channel_id=1, source_target_pairs={{0,3},{1,2},{2,1},{3,0},{4,7},{5,6},{6,5},{7,4},{8,11},{9,10},{10,... | collective-permute-start | bytes 786440 | tf_op jit(solution)/shard_map/ppermute | solution.py:19
  106.1 5.4 %copy-start.2 = (bf16[1,512,1024]{2,1,0:T(8,128)(2,1)S(1)}, bf16[1,512,1024]{2,1,0:T(8,128)(2,1)}, u32[]{:S(2)}) copy-start(bf16[1,512,1024]{2,1,0:T(8,128)(2,1)} %param.12) | copy-start | bytes 3145732
  106.1 5.4 %copy-start.6 = (bf16[1,128,1024]{2,1,0:T(8,128)(2,1)S(1)}, bf16[1,128,1024]{2,1,0:T(8,128)(2,1)}, u32[]{:S(2)}) copy-start(bf16[1,128,1024]{2,1,0:T(8,128)(2,1)} %param.15) | copy-start | bytes 786436
  106.1 5.4 %copy-start.8 = (bf16[1,1024,128]{2,1,0:T(8,128)(2,1)S(1)}, bf16[1,1024,128]{2,1,0:T(8,128)(2,1)}, u32[]{:S(2)}) copy-start(bf16[1,1024,128]{2,1,0:T(8,128)(2,1)} %param.14) | copy-start | bytes 786436
  106.1 14.1 %collective-permute-start.20 = (bf16[128,1024]{1,0:T(8,128)(2,1)S(1)}, bf16[128,1024]{1,0:T(8,128)(2,1)S(1)}, u32[]{:S(2)}, u32[]{:S(2)}) collective-permute-start(bf16[128,1024]{1,0:T(8,128)(2,1)S(1)} %get-tuple-element.92), channel_id=1, source_target_pairs={{0,16},{8,24},{16,0},{24,8},{1,17},{9,25},{17,1},{25,9},{2,18},{10... | collective-permute-start | bytes 786440 | tf_op jit(solution)/shard_map/ppermute | solution.py:19

commit v8 on v7

--- a/solution.py
+++ b/solution.py
@@ -27,6 +27,16 @@
 
 def gathered(shard, axis):
     return [shard] + [swap(shard, axis, k) for k in range(1, lax.axis_size(axis))]
+
+
+def line_gathered(shard, axis):
+    if lax.axis_size(axis) != 4:
+        return gathered(shard, axis)
+    far, near = swap(shard, axis, 2), swap(shard, axis, 1)
+    shard, far, near = lax.optimization_barrier((shard, far, near))
+    across = lax.ppermute(shard, axis, [(1, 2), (2, 1)])
+    passed = lax.ppermute(far, axis, [(1, 0), (2, 3)])
+    return [shard, near, far, (across, passed)]
 
 
 def scattered(blocks, axis):
@@ -65,6 +75,15 @@
 
 def total(blocks, where):
     return run(total_kernel, [like(blocks[0].shape)], where, [blocks])[0]
+
+
+def ordered(blocks, axis):
+    step = 1
+    while step < len(blocks):
+        odd = (lax.axis_index(axis) & step) > 0
+        blocks = [jnp.where(odd, blocks[k ^ step], part) for k, part in enumerate(blocks)]
+        step *= 2
+    return jnp.concatenate(blocks, axis=1)
 
 
 def block(array, axis, dim):
@@ -195,9 +214,22 @@
         weights[:, there] = pack[head : head + codes, relay:]
 
 
-def fold_kernel(where, ins, outs, scratch):
+def rows_kernel(where, ins, outs, scratch):
+    ((heads, first, last),) = ins
+    width = heads.shape[1]
+    outs[0][:, :width] = heads[...]
+    outs[0][:, width:] = jnp.where(where[2] == 0, first[...], last[...])
+
+
+def fold_kernel(groups, where, ins, outs, scratch):
     ((proj, enc),) = ins
-    outs[0][...] = dot(proj[...], enc[...], NT).astype(bf16)
+    fold = outs[0]
+    size = fold.shape[0] // groups
+    fold[...] = dot(proj[...], enc[...], NT).astype(bf16)
+    for k in range(groups):
+        there = slice(k // 2 * size, (k // 2 + 1) * size)
+        here = pl.ds(pl.multiple_of((where[1] ^ k) * size, size), size)
+        outs[1 + k % 2][there, :] = fold[here, :]
 
 
 def partial_kernel(where, ins, outs, scratch):
@@ -304,8 +336,8 @@
         outs[6][...] = outs[1][: outs[6].shape[0], : outs[6].shape[1]]
 
 
-def backward_kernel(width, live_section, last, tokens, where, ins, outs, scratch):
-    (moved, incoming, received, mixed, unscaled, row_scale, mix_gram, products, weights, fold), = ins
+def backward_kernel(width, live_section, last, where, ins, outs, scratch):
+    (moved, incoming, received, mixed, unscaled, row_scale, mix_gram, products, weights), = ins
     live = where[2] == live_section
     half = weights.shape[1] // 2
 
@@ -325,14 +357,23 @@
 
     by_rows(moved.shape[0], step)
     if last:
-        outs[6][...] = outs[1][: outs[6].shape[0], : outs[6].shape[1]]
-        kept, given = outs[4:6]
-        groups = 2 * kept.shape[0] // tokens
-        for k in range(groups):
-            rows = slice(k * tokens, (k + 1) * tokens)
-            there = slice(k // 2 * tokens, (k // 2 + 1) * tokens)
-            term = dot(outs[3][rows, :], fold[...], NT).astype(bf16)
-            (given if k % 2 else kept)[there, :] = term
+        outs[4][...] = outs[1][: outs[4].shape[0], : outs[4].shape[1]]
+
+
+def heads_kernel(where, ins, outs, scratch):
+    ((code_grad, fold_rows),) = ins
+    tokens = outs[0].shape[0]
+    whole = dot(code_grad[...], fold_rows[...], NT)
+    for k, out in enumerate(outs):
+        out[...] = whole[k * tokens : (k + 1) * tokens, :].astype(bf16)
+
+
+def laid_kernel(where, ins, outs, scratch):
+    (blocks,) = ins
+    size = blocks[0].shape[1]
+    for k, part in enumerate(blocks):
+        at = pl.multiple_of((where[1] ^ k) * size, size)
+        outs[0][:, pl.ds(at, size)] = part[...]
 
 
 def head_kernel(where, ins, outs, scratch):
@@ -420,8 +461,16 @@
     head_cols, model_cols = proj.shape
     where = jnp.stack([lax.axis_index("tensor"), lax.axis_index("dp"), section]).astype(jnp.int32)
 
-    end = jnp.where(section == 0, input_code, code_cotangent)
-    heads = gathered(jnp.concatenate([heads_out[0], end], axis=1), "dp")
+    head_cols, model_cols = proj.shape
+    (rows_here,) = run(
+        rows_kernel,
+        [like((tokens, head_cols + relay))],
+        where,
+        [(heads_out[0], input_code, code_cotangent)],
+    )
+    heads = line_gathered(rows_here, "dp")
+    if isinstance(heads[-1], tuple):
+        heads[-1] = total(heads[-1], where)
     packs = run(
         gram_kernel,
         [like((cols * codes // (2 * relay) + codes + relay, 2 * relay))] * parts,
@@ -429,7 +478,13 @@
         [(dec, recv, send, gain)],
         scratch=[pltpu.VMEM((codes, codes), f32)],
     )
-    (fold,) = run(fold_kernel, [like((head_cols, codes))], where, [(proj, enc)])
+    half = like((head_cols // 2, codes))
+    fold, fold_kept, fold_given = run(
+        functools.partial(fold_kernel, groups),
+        [like((head_cols, codes)), half, half],
+        where,
+        [(proj, enc)],
+    )
     fold, _ = lax.optimization_barrier((fold, packs[0]))
     packs = scattered(packs, "tensor")
 
@@ -441,7 +496,11 @@
         scratch=[pltpu.VMEM((min(groups, 4) * tokens, codes), f32)],
         flops=2 * rows * head_cols * codes,
     )
+    partials = list(partials)
+    partials[3], *_ = lax.optimization_barrier((partials[3], *packs))
+    code_block = total(scattered(partials, "tensor"), where)
     wide = parts * relay
+    packs, _ = lax.optimization_barrier((packs, code_block))
     payload, products, weights = run(
         setup_kernel,
         [
@@ -452,11 +511,9 @@
         where,
         [packs, heads],
     )
-    partials = list(partials)
-    partials[3], *_ = lax.optimization_barrier((partials[3], *packs))
-    code_block = total(scattered(partials, "tensor"), where)
     payloads = gathered(payload, "tensor")
     mix_block = group_sum(code_block, payloads, "dp", where)
+    fold_given, mix_block = lax.optimization_barrier((fold_given, mix_block))
     mix_blocks = gathered(mix_block, "tensor")
 
     square_flops = 2 * rows * codes * codes
@@ -475,6 +532,9 @@
         [mix_blocks, payloads, (products, weights)],
         scratch=[pltpu.VMEM((codes, codes), bf16)],
         flops=3 * square_flops,
+    )
+    fold_rows, sent = halved_sum(
+        fold_kept, fold_given, sent, "dp", head_cols // groups, where
     )
     received = ends
     for turn in range(1, sections):
@@ -499,10 +559,10 @@
         shapes = [like((rows, wide)), like((rows, wide))]
         if last:
             shapes += [like((rows, 1), f32), like((rows, codes))]
-            shapes += [like((rows // 2, head_cols))] * 2 + [like((tokens, relay))]
+            shapes += [like((tokens, relay))]
         moved = move(returned, "pipe", -1)
         results = run(
-            functools.partial(backward_kernel, width, sections - 1 - turn, last, tokens),
+            functools.partial(backward_kernel, width, sections - 1 - turn, last),
             shapes,
             where,
             [
@@ -516,15 +576,13 @@
                     mix_gram,
                     products,
                     weights,
-                    fold,
                 )
             ],
             flops=3 * square_flops,
         )
         incoming, returned = results[:2]
-    inner, code_grad, kept, given, returned = results[2:]
-
-    heads_grad, row_scale = halved_sum(kept, given, row_scale, "dp", tokens, where)
+    inner, code_grad, returned = results[2:]
+
     head_sum, *enc_blocks = run(
         head_kernel,
         [like((codes, head_cols))] + [like((cols, model_cols))] * parts,
@@ -535,6 +593,17 @@
     )
     head_sum, mix, *enc_blocks = lax.optimization_barrier((head_sum, mix, *enc_blocks))
     enc_grad = total(scattered(enc_blocks, "tensor"), where)
+    head_blocks = run(
+        heads_kernel,
+        [like((tokens, head_cols // groups))] * groups,
+        where,
+        [(code_grad, fold_rows)],
+    )
+    head_blocks = scattered(head_blocks, "dp")
+    if head_cols // groups % 128 == 0:
+        (heads_grad,) = run(laid_kernel, [like((tokens, head_cols))], where, [head_blocks])
+    else:
+        heads_grad = ordered(head_blocks, "dp")
     (proj_grad,) = run(proj_kernel, [like((head_cols, model_cols))], where, [(head_sum, enc)])
     shapes = [(codes // groups, features), (1, features), (features, relay), (relay, features)]
     dec_grad, gain_grad, send_grad, recv_grad = run(

time: 122 us -> 113 us (0.926)
  waiting for transfers between devices: 45.6 us -> 37.5 us
  starting transfers between devices: 39.6 us -> 37 us
  local copies, waits for them, and re-layouts: 5.43 us -> 7.96 us
  other arithmetic: 1.91 us -> 0.08 us
    ppermute x22 -> x24, waiting for transfers between devices: 41.8 us -> 31.7 us  [swap(): lax.ppermute(shard, axis, [(i, i ^ by) for i in range(lax.axis_size(axis))])]
    ppermute x22 -> x24, starting transfers between devices: 36.8 us -> 32.3 us  [swap(): lax.ppermute(shard, axis, [(i, i ^ by) for i in range(lax.axis_size(axis))])]
    ppermute x0 -> x2, waiting for transfers between devices: none -> 4.37 us  [the longest x1 4.37 us: line_gathered(): passed = lax.ppermute(far, axis, [(1, 0), (2, 3)])]
    unnamed x20 -> x28, local copies, waits for them, and re-layouts: 5.43 us -> 7.96 us
    ppermute x2, waiting for transfers between devices: 3.81 us -> 1.49 us  [move(): return lax.ppermute(shard, axis, pairs)]
    ppermute x0 -> x2, starting transfers between devices: none -> 1.96 us  [the longest x1 1.29 us: line_gathered(): passed = lax.ppermute(far, axis, [(1, 0), (2, 3)])]
    pallas_call x16 -> x20, Pallas kernels: 28.2 us -> 29.4 us  [run(): pl.pallas_call(body, out_shape=[jax.ShapeDtypeStruct(r.shape, r.dtype) fo...]
  transfers between devices with their start and end apart: 24 -> 28, of which waited for: 14 -> 16; matrix products, arithmetic and copies ran while one was open for 0% -> 0% of each run, Pallas kernels for 15% -> 21%
where the time goes in v8:
time: 113 us
  waiting for transfers between devices  37.5 us (33%)
  starting transfers between devices  37 us (33%)
  Pallas kernels  29.4 us (26%)
  local copies, waits for them, and re-layouts  7.96 us (7%)
    ppermute x24, starting transfers between devices, swap(): lax.ppermute(shard, axis, [(i, i ^ by) for i in range(lax.axis_size(axis))])  32.3 us
    ppermute x24, waiting for transfers between devices, swap(): lax.ppermute(shard, axis, [(i, i ^ by) for i in range(lax.axis_size(axis))])  31.7 us
    pallas_call x20, Pallas kernels, run(): pl.pallas_call(body, out_shape=[jax.ShapeDtypeStruct(r.shape, r.dtype) fo...  29.4 us
    unnamed x28, local copies, waits for them, and re-layouts  7.96 us
    ppermute x1, waiting for transfers between devices, line_gathered(): passed = lax.ppermute(far, axis, [(1, 0), (2, 3)])  4.37 us
    ppermute x2, starting transfers between devices, move(): return lax.ppermute(shard, axis, pairs)  2.77 us
  transfers between devices with their start and end apart: 28, of which 16 were waited for; matrix products, arithmetic and copies ran while one was open for 0% of the time, Pallas kernels for 21%

profile of v8, /device:TPU:0, one launch (start us, length us, event | category | flops | bytes accessed | tf_op | source)
XLA Modules:
  0.0 112.9 jit_solution(12404540334416159583)
XLA Ops:
  0.7 1.0 copy-done.9
  3.8 3.1 %collective-permute-start.1 = (bf16[128,1152]{1,0:T(8,128)(2,1)S(1)}, bf16[128,1152]{1,0:T(8,128)(2,1)S(1)}, u32[]{:S(2)}, u32[]{:S(2)}) collective-permute-start(bf16[128,1152]{1,0:T(8,128)(2,1)S(1)} %shard_map.161.refs_0_.refs_4_), channel_id=1, source_target_pairs={{0,8},{8,0},{16,24},{24,16},{1,9},{9,1},{17,25},{25,17},{2,10},{10... | collective-permute-start | bytes 884744 | tf_op jit(solution)/shard_map/ppermute | solution.py:19
  6.9 2.6 %collective-permute-start = (bf16[128,1152]{1,0:T(8,128)(2,1)S(1)}, bf16[128,1152]{1,0:T(8,128)(2,1)S(1)}, u32[]{:S(2)}, u32[]{:S(2)}) collective-permute-start(bf16[128,1152]{1,0:T(8,128)(2,1)S(1)} %shard_map.161.refs_0_.refs_4_), channel_id=1, source_target_pairs={{0,16},{8,24},{16,0},{24,8},{1,17},{9,25},{17,1},{25,9},{2,18},{10... | collective-permute-start | bytes 884744 | tf_op jit(solution)/shard_map/ppermute | solution.py:19
  9.5 1.2 %copy-done.1 = bf16[1,512,1024]{2,1,0:T(8,128)(2,1)S(1)} copy-done((bf16[1,512,1024]{2,1,0:T(8,128)(2,1)S(1)}, bf16[1,512,1024]{2,1,0:T(8,128)(2,1)}, u32[]{:S(2)}) %copy-start.1) | copy-done | bytes 1048600
  10.8 0.9 copy-done.5
  11.7 0.9 copy-done.7
  13.3 2.0 %shard_map.163 = (bf16[896,256]{1,0:T(8,128)(2,1)S(1)}, bf16[896,256]{1,0:T(8,128)(2,1)S(1)}, bf16[896,256]{1,0:T(8,128)(2,1)S(1)}, bf16[896,256]{1,0:T(8,128)(2,1)S(1)}) custom-call(s32[3]{0:T(128)S(1)} %pad_add_fusion.where_ref, bf16[512,1024]{1,0:T(8,128)(2,1)S(1)} %bitcast.19, bf16[128,1024]{1,0:T(8,128)(2,1)S(1)} %bitcast.23, ...), custom_call_target="tpu_custom_call" | custom-call | tf_op jit(solution)/shard_map/pallas_call | solution.py:111
  15.3 1.6 %collective-permute-start.6 = (bf16[896,256]{1,0:T(8,128)(2,1)S(1)}, bf16[896,256]{1,0:T(8,128)(2,1)S(1)}, u32[]{:S(2)}, u32[]{:S(2)}) collective-permute-start(bf16[896,256]{1,0:T(8,128)(2,1)S(1)} %get-tuple-element.86), channel_id=1, source_target_pairs={{0,1},{1,0},{2,3},{3,2},{4,5},{5,4},{6,7},{7,6},{8,9},{9,8},{10,11... | collective-permute-start | bytes 1376264 | tf_op jit(solution)/shard_map/ppermute | solution.py:19
  16.9 1.5 %collective-permute-start.7 = (bf16[896,256]{1,0:T(8,128)(2,1)S(1)}, bf16[896,256]{1,0:T(8,128)(2,1)S(1)}, u32[]{:S(2)}, u32[]{:S(2)}) collective-permute-start(bf16[896,256]{1,0:T(8,128)(2,1)S(1)} %get-tuple-element.87), channel_id=1, source_target_pairs={{0,2},{1,3},{2,0},{3,1},{4,6},{5,7},{6,4},{7,5},{8,10},{9,11},{10,... | collective-permute-start | bytes 1376264 | tf_op jit(solution)/shard_map/ppermute | solution.py:19
  18.9 1.3 %collective-permute-done.1.refs_1_.refs_5_ = bf16[128,1152]{1,0:T(8,128)(2,1)S(1)} collective-permute-done((bf16[128,1152]{1,0:T(8,128)(2,1)S(1)}, bf16[128,1152]{1,0:T(8,128)(2,1)S(1)}, u32[]{:S(2)}, u32[]{:S(2)}) %collective-permute-start.1) | collective-permute-done | bytes 294944 | tf_op jit(solution)/shard_map/ppermute | solution.py:19
  20.1 2.5 %collective-permute-done.refs_2_.refs_6_ = bf16[128,1152]{1,0:T(8,128)(2,1)S(1)} collective-permute-done((bf16[128,1152]{1,0:T(8,128)(2,1)S(1)}, bf16[128,1152]{1,0:T(8,128)(2,1)S(1)}, u32[]{:S(2)}, u32[]{:S(2)}) %collective-permute-start) | collective-permute-done | bytes 294944 | tf_op jit(solution)/shard_map/ppermute | solution.py:19
  23.3 1.3 %collective-permute-start.3 = (bf16[128,1152]{1,0:T(8,128)(2,1)S(1)}, bf16[128,1152]{1,0:T(8,128)(2,1)S(1)}, u32[]{:S(2)}, u32[]{:S(2)}) collective-permute-start(bf16[128,1152]{1,0:T(8,128)(2,1)S(1)} %collective-permute-done.refs_2_.refs_6_), channel_id=1, source_target_pairs={{8,0},{16,24},{9,1},{17,25},{10,2},{18,26},{11,3},{19,27},{12,4},{... | collective-permute-start | bytes 884744 | tf_op jit(solution)/shard_map/ppermute | solution.py:38
  24.7 1.6 %copy-done.3 = bf16[1,1024,1024]{2,1,0:T(8,128)(2,1)S(1)} copy-done((bf16[1,1024,1024]{2,1,0:T(8,128)(2,1)S(1)}, bf16[1,1024,1024]{2,1,0:T(8,128)(2,1)}, u32[]{:S(2)}) %copy-start.3) | copy-done | bytes 2097176
  26.3 1.9 %shard_map.160 = (bf16[1024,512]{1,0:T(8,128)(2,1)S(1)}, bf16[512,512]{1,0:T(8,128)(2,1)S(1)}, bf16[512,512]{1,0:T(8,128)(2,1)S(1)}) custom-call(s32[3]{0:T(128)S(1)} %pad_add_fusion.where_ref, bf16[1024,1024]{1,0:T(8,128)(2,1)S(1)} %bitcast.21, bf16[512,1024]{1,0:T(8,128)(2,1)S(1)} %bitcast.17), custom_call_target="tpu_custom_call" | custom-call | tf_op jit(solution)/shard_map/pallas_call | solution.py:111
  28.2 4.4 %collective-permute-done.3.refs_1_ = bf16[128,1152]{1,0:T(8,128)(2,1)S(1)} collective-permute-done((bf16[128,1152]{1,0:T(8,128)(2,1)S(1)}, bf16[128,1152]{1,0:T(8,128)(2,1)S(1)}, u32[]{:S(2)}, u32[]{:S(2)}) %collective-permute-start.3) | collective-permute-done | bytes 294944 | tf_op jit(solution)/shard_map/ppermute | solution.py:38
  33.2 1.4 %shard_map.164 = (bf16[512,128]{1,0:T(8,128)(2,1)S(1)}, bf16[512,128]{1,0:T(8,128)(2,1)S(1)}, bf16[512,128]{1,0:T(8,128)(2,1)S(1)}, bf16[512,128]{1,0:T(8,128)(2,1)S(1)}) custom-call(s32[3]{0:T(128)S(1)} %pad_add_fusion.where_ref, bf16[128,1152]{1,0:T(8,128)(2,1)S(1)} %shard_map.161.refs_0_.refs_4_, ...), custom_call_target="tpu_custom_call" | custom-call | flops 536870912 | bytes 2752512 | tf_op jit(solution)/shard_map/pallas_call | solution.py:111
  34.6 3.6 %collective-permute-done.7.refs_2_ = bf16[896,256]{1,0:T(8,128)(2,1)S(1)} collective-permute-done((bf16[896,256]{1,0:T(8,128)(2,1)S(1)}, bf16[896,256]{1,0:T(8,128)(2,1)S(1)}, u32[]{:S(2)}, u32[]{:S(2)}) %collective-permute-start.7) | collective-permute-done | bytes 458784 | tf_op jit(solution)/shard_map/ppermute | solution.py:19
  38.1 1.5 %collective-permute-start.9 = (bf16[512,128]{1,0:T(8,128)(2,1)S(1)}, bf16[512,128]{1,0:T(8,128)(2,1)S(1)}, u32[]{:S(2)}, u32[]{:S(2)}) collective-permute-start(bf16[512,128]{1,0:T(8,128)(2,1)S(1)} %get-tuple-element.89), channel_id=1, source_target_pairs={{0,3},{1,2},{2,1},{3,0},{4,7},{5,6},{6,5},{7,4},{8,11},{9,10},{10,... | collective-permute-start | bytes 393224 | tf_op jit(solution)/shard_map/ppermute | solution.py:19
  39.6 1.5 %collective-permute-start.4 = (bf16[512,128]{1,0:T(8,128)(2,1)S(1)}, bf16[512,128]{1,0:T(8,128)(2,1)S(1)}, u32[]{:S(2)}, u32[]{:S(2)}) collective-permute-start(bf16[512,128]{1,0:T(8,128)(2,1)S(1)} %get-tuple-element.83), channel_id=1, source_target_pairs={{0,1},{1,0},{2,3},{3,2},{4,5},{5,4},{6,7},{7,6},{8,9},{9,8},{10,11... | collective-permute-start | bytes 393224 | tf_op jit(solution)/shard_map/ppermute | solution.py:19
  41.6 2.4 %collective-permute-done.9.refs_3_ = bf16[512,128]{1,0:T(8,128)(2,1)S(1)} collective-permute-done((bf16[512,128]{1,0:T(8,128)(2,1)S(1)}, bf16[512,128]{1,0:T(8,128)(2,1)S(1)}, u32[]{:S(2)}, u32[]{:S(2)}) %collective-permute-start.9) | collective-permute-done | bytes 131104 | tf_op jit(solution)/shard_map/ppermute | solution.py:19
  44.0 1.5 %collective-permute-done.4.refs_1_ = bf16[512,128]{1,0:T(8,128)(2,1)S(1)} collective-permute-done((bf16[512,128]{1,0:T(8,128)(2,1)S(1)}, bf16[512,128]{1,0:T(8,128)(2,1)S(1)}, u32[]{:S(2)}, u32[]{:S(2)}) %collective-permute-start.4) | collective-permute-done | bytes 131104 | tf_op jit(solution)/shard_map/ppermute | solution.py:19
  47.1 0.9 shard_map.167
  48.0 1.2 %collective-permute-start.14 = (bf16[1024,128]{1,0:T(8,128)(2,1)S(1)}, bf16[1024,128]{1,0:T(8,128)(2,1)S(1)}, u32[]{:S(2)}, u32[]{:S(2)}) collective-permute-start(bf16[1024,128]{1,0:T(8,128)(2,1)S(1)} %get-tuple-element.94.refs_4_), channel_id=1, source_target_pairs={{0,3},{1,2},{2,1},{3,0},{4,7},{5,6},{6,5},{7,4},{8,11},{9,10},{10,... | collective-permute-start | bytes 786440 | tf_op jit(solution)/shard_map/ppermute | solution.py:19
  49.3 1.0 collective-permute-start.13
  50.3 1.3 %collective-permute-start.12 = (bf16[1024,128]{1,0:T(8,128)(2,1)S(1)}, bf16[1024,128]{1,0:T(8,128)(2,1)S(1)}, u32[]{:S(2)}, u32[]{:S(2)}) collective-permute-start(bf16[1024,128]{1,0:T(8,128)(2,1)S(1)} %get-tuple-element.94.refs_4_), channel_id=1, source_target_pairs={{0,1},{1,0},{2,3},{3,2},{4,5},{5,4},{6,7},{7,6},{8,9},{9,8},{10,11... | collective-permute-start | bytes 786440 | tf_op jit(solution)/shard_map/ppermute | solution.py:19
  51.6 2.5 %collective-permute-done.10.refs_1_ = bf16[512,128]{1,0:T(8,128)(2,1)S(1)} collective-permute-done((bf16[512,128]{1,0:T(8,128)(2,1)S(1)}, bf16[512,128]{1,0:T(8,128)(2,1)S(1)}, u32[]{:S(2)}, u32[]{:S(2)}) %collective-permute-start.10) | collective-permute-done | bytes 131104 | tf_op jit(solution)/shard_map/ppermute | solution.py:19
  54.7 5.0 %collective-permute-done.11.refs_1_ = bf16[512,128]{1,0:T(8,128)(2,1)S(1)} collective-permute-done((bf16[512,128]{1,0:T(8,128)(2,1)S(1)}, bf16[512,128]{1,0:T(8,128)(2,1)S(1)}, u32[]{:S(2)}, u32[]{:S(2)}) %collective-permute-start.11) | collective-permute-done | bytes 131104 | tf_op jit(solution)/shard_map/ppermute | solution.py:19
  60.3 1.6 %collective-permute-start.18 = (bf16[512,128]{1,0:T(8,128)(2,1)S(1)}, bf16[512,128]{1,0:T(8,128)(2,1)S(1)}, u32[]{:S(2)}, u32[]{:S(2)}) collective-permute-start(bf16[512,128]{1,0:T(8,128)(2,1)S(1)} %shard_map.168.refs_0_), channel_id=1, source_target_pairs={{0,3},{1,2},{2,1},{3,0},{4,7},{5,6},{6,5},{7,4},{8,11},{9,10},{10,... | collective-permute-start | bytes 393224 | tf_op jit(solution)/shard_map/ppermute | solution.py:19
  61.9 1.2 %collective-permute-start.17 = (bf16[512,128]{1,0:T(8,128)(2,1)S(1)}, bf16[512,128]{1,0:T(8,128)(2,1)S(1)}, u32[]{:S(2)}, u32[]{:S(2)}) collective-permute-start(bf16[512,128]{1,0:T(8,128)(2,1)S(1)} %shard_map.168.refs_0_), channel_id=1, source_target_pairs={{0,2},{1,3},{2,0},{3,1},{4,6},{5,7},{6,4},{7,5},{8,10},{9,11},{10,... | collective-permute-start | bytes 393224 | tf_op jit(solution)/shard_map/ppermute | solution.py:19
  63.9 2.5 %collective-permute-done.18.refs_3_ = bf16[512,128]{1,0:T(8,128)(2,1)S(1)} collective-permute-done((bf16[512,128]{1,0:T(8,128)(2,1)S(1)}, bf16[512,128]{1,0:T(8,128)(2,1)S(1)}, u32[]{:S(2)}, u32[]{:S(2)}) %collective-permute-start.18) | collective-permute-done | bytes 131104 | tf_op jit(solution)/shard_map/ppermute | solution.py:19
  66.3 1.3 %collective-permute-done.17.refs_2_ = bf16[512,128]{1,0:T(8,128)(2,1)S(1)} collective-permute-done((bf16[512,128]{1,0:T(8,128)(2,1)S(1)}, bf16[512,128]{1,0:T(8,128)(2,1)S(1)}, u32[]{:S(2)}, u32[]{:S(2)}) %collective-permute-start.17) | collective-permute-done | bytes 131104 | tf_op jit(solution)/shard_map/ppermute | solution.py:19
  68.1 2.1 %shard_map.169 = (bf16[512,512]{1,0:T(8,128)(2,1)S(1)}, bf16[512,512]{1,0:T(8,128)(2,1)S(1)}, f32[512,512]{1,0:T(8,128)S(1)}, f32[512,512]{1,0:T(8,128)S(1)}, f3...) custom-call(s32[3]{0:T(128)S(1)} %pad_add_fusion.where_ref, ...), custom_call_target="tpu_custom_call" | custom-call | flops 805306368 | bytes 7604224 | tf_op jit(solution)/shard_map/pallas_call | solution.py:111
  71.1 1.3 %collective-permute-start.19 = (bf16[512,512]{1,0:T(8,128)(2,1)S(1)}, bf16[512,512]{1,0:T(8,128)(2,1)S(1)}, u32[]{:S(2)}, u32[]{:S(2)}) collective-permute-start(bf16[512,512]{1,0:T(8,128)(2,1)S(1)} %get-tuple-element.101), channel_id=1, source_target_pairs={{0,4},{1,5},{2,6},{3,7},{8,12},{9,13},{10,14},{11,15},{16,20},{17,... | collective-permute-start | bytes 1572872 | tf_op jit(solution)/shard_map/ppermute | solution.py:25
  72.4 1.5 %collective-permute-done.19.refs_0_ = bf16[512,512]{1,0:T(8,128)(2,1)S(1)} collective-permute-done((bf16[512,512]{1,0:T(8,128)(2,1)S(1)}, bf16[512,512]{1,0:T(8,128)(2,1)S(1)}, u32[]{:S(2)}, u32[]{:S(2)}) %collective-permute-start.19) | collective-permute-done | bytes 524320 | tf_op jit(solution)/shard_map/ppermute | solution.py:25
  73.9 2.5 %shard_map.170 = (bf16[512,512]{1,0:T(8,128)(2,1)S(1)}, bf16[512,512]{1,0:T(8,128)(2,1)}, f32[512,512]{1,0:T(8,128)S(1)}, f32[512,512]{1,0:T(8,128)S(1)}, f32[51...) custom-call(s32[3]{0:T(128)S(1)} %pad_add_fusion.where_ref, ...), custom_call_target="tpu_custom_call" | custom-call | flops 268435456 | bytes 7639040 | tf_op jit(solution)/shard_map/pallas_call | solution.py:111
  76.3 1.5 %collective-permute-start.20 = (bf16[512,512]{1,0:T(8,128)(2,1)S(1)}, bf16[512,512]{1,0:T(8,128)(2,1)S(1)}, u32[]{:S(2)}, u32[]{:S(2)}) collective-permute-start(bf16[512,512]{1,0:T(8,128)(2,1)S(1)} %get-tuple-element.107), channel_id=1, source_target_pairs={{4,0},{5,1},{6,2},{7,3},{12,8},{13,9},{14,10},{15,11},{20,16},{21,... | collective-permute-start | bytes 1572872 | tf_op jit(solution)/shard_map/ppermute | solution.py:25
  78.5 2.7 %collective-permute-start.21 = (bf16[256,512]{1,0:T(8,128)(2,1)S(1)}, bf16[256,512]{1,0:T(8,128)(2,1)S(1)}, u32[]{:S(2)}, u32[]{:S(2)}) collective-permute-start(bf16[256,512]{1,0:T(8,128)(2,1)S(1)} %get-tuple-element.118), channel_id=1, source_target_pairs={{0,16},{8,24},{16,0},{24,8},{1,17},{9,25},{17,1},{25,9},{2,18},{10... | collective-permute-start | bytes 786440 | tf_op jit(solution)/shard_map/ppermute | solution.py:19
  81.2 1.9 %shard_map.171 = (bf16[512,512]{1,0:T(8,128)(2,1)S(1)}, bf16[512,512]{1,0:T(8,128)(2,1)}, f32[512,1]{1,0:T(8,128)S(1)}, bf16[512,512]{1,0:T(8,128)(2,1)S(1)}, bf16[128,128]{1,0:T(8,128)(2,1)}) custom-call(s32[3]{0:T(128)S(1)} %pad_add_fusion.where_ref, bf16[512,512]{1,0:T(8,128)(2,1)S(1)} %collective-permute-done.20.refs_0_, ...), custom_call_target="tpu_custom_call" | custom-call | flops 805306368 | bytes 7639040 | tf_op jit(solution)/shard_map/pallas_call | solution.py:111
  83.0 2.5 %shard_map.176 = (bf16[512,1024]{1,0:T(8,128)(2,1)S(1)}, bf16[128,1024]{1,0:T(8,128)(2,1)S(1)}, bf16[128,1024]{1,0:T(8,128)(2,1)S(1)}, bf16[128,1024]{1,0:T(8,128)(2,1)S(1)}, bf16[128,1024]{1,0:T(8,128)(2,1)S(1)}) custom-call(s32[3]{0:T(128)S(1)} %pad_add_fusion.where_ref, bf16[128,1152]{1,0:T(8,128)(2,1)S(1)} %shard_map.161.refs_0_.refs_4_, ...), custom_call_target="tpu_custom_call" | custom-call | flops 1610612736 | bytes 5898240 | tf_op jit(solution)/shard_map/pallas_call | solution.py:111
  85.6 2.6 %collective-permute-start.26 = (bf16[128,1024]{1,0:T(8,128)(2,1)S(1)}, bf16[128,1024]{1,0:T(8,128)(2,1)S(1)}, u32[]{:S(2)}, u32[]{:S(2)}) collective-permute-start(bf16[128,1024]{1,0:T(8,128)(2,1)S(1)} %get-tuple-element.132), channel_id=1, source_target_pairs={{0,2},{1,3},{2,0},{3,1},{4,6},{5,7},{6,4},{7,5},{8,10},{9,11},{10,... | collective-permute-start | bytes 786440 | tf_op jit(solution)/shard_map/ppermute | solution.py:19
  89.1 5.0 %collective-permute-done.21.refs_1_ = bf16[256,512]{1,0:T(8,128)(2,1)S(1)} collective-permute-done((bf16[256,512]{1,0:T(8,128)(2,1)S(1)}, bf16[256,512]{1,0:T(8,128)(2,1)S(1)}, u32[]{:S(2)}, u32[]{:S(2)}) %collective-permute-start.21) | collective-permute-done | bytes 262176 | tf_op jit(solution)/shard_map/ppermute | solution.py:19
  95.6 3.0 %collective-permute-start.23 = (bf16[128,256]{1,0:T(8,128)(2,1)S(1)}, bf16[128,256]{1,0:T(8,128)(2,1)S(1)}, u32[]{:S(2)}, u32[]{:S(2)}) collective-permute-start(bf16[128,256]{1,0:T(8,128)(2,1)S(1)} %get-tuple-element.121), channel_id=1, source_target_pairs={{0,16},{8,24},{16,0},{24,8},{1,17},{9,25},{17,1},{25,9},{2,18},{10... | collective-permute-start | bytes 196616 | tf_op jit(solution)/shard_map/ppermute | solution.py:19
  98.7 2.3 %collective-permute-done.22.refs_1_ = bf16[128,256]{1,0:T(8,128)(2,1)S(1)} collective-permute-done((bf16[128,256]{1,0:T(8,128)(2,1)S(1)}, bf16[128,256]{1,0:T(8,128)(2,1)S(1)}, u32[]{:S(2)}, u32[]{:S(2)}) %collective-permute-start.22) | collective-permute-done | bytes 65568 | tf_op jit(solution)/shard_map/ppermute | solution.py:19
  101.0 2.6 %collective-permute-start.24 = (bf16[128,256]{1,0:T(8,128)(2,1)S(1)}, bf16[128,256]{1,0:T(8,128)(2,1)S(1)}, u32[]{:S(2)}, u32[]{:S(2)}) collective-permute-start(bf16[128,256]{1,0:T(8,128)(2,1)S(1)} %get-tuple-element.122), channel_id=1, source_target_pairs={{0,24},{8,16},{16,8},{24,0},{1,25},{9,17},{17,9},{25,1},{2,26},{10... | collective-permute-start | bytes 196616 | tf_op jit(solution)/shard_map/ppermute | solution.py:19
  103.6 3.2 %shard_map.177 = bf16[1024,1024]{1,0:T(8,128)(2,1)} custom-call(s32[3]{0:T(128)S(1)} %pad_add_fusion.where_ref, bf16[512,1024]{1,0:T(8,128)(2,1)S(1)} %get-tuple-element.129.refs_0_, bf16[512,1024]{1,0:T(8,128)(2,1)S(1)} %bitcast.18), custom_call_target="tpu_custom_call" | custom-call | tf_op jit(solution)/shard_map/pallas_call | solution.py:111
  106.8 3.5 %shard_map.179 = (bf16[128,1024]{1,0:T(8,128)(2,1)}, f32[1,1024]{1,0:T(1,128)}, bf16[1024,128]{1,0:T(8,128)(2,1)}, bf16[128,1024]{1,0:T(8,128)(2,1)}) custom-call(s32[3]{0:T(128)S(1)} %pad_add_fusion.where_ref, bf16[512,512]{1,0:T(8,128)(2,1)S(1)} %get-tuple-element.134.refs_0_.refs_1_, bf16[512,512]{1,0:T(8,128)(2,1)S(1)} %get-tuple-element.134.refs_0_.refs_1_, ...), custom_call_target="tpu_custom_call" | custom-call | tf_op jit(solution)/shard_map/pallas_call | solution.py:111
  110.3 1.3 %shard_map.175 = bf16[128,1024]{1,0:T(8,128)(2,1)} custom-call(s32[3]{0:T(128)S(1)} %pad_add_fusion.where_ref, bf16[128,256]{1,0:T(8,128)(2,1)S(1)} %get-tuple-element.119.refs_0_, bf16[128,256]{1,0:T(8,128)(2,1)S(1)} %collective-permute-done.22.refs_1_, bf16[128,256]{1,0:T(8,128)(2,1)S(1)} %collective-permute-done.23.refs_2_, ...), custom_call_target="tpu_custom_call" | custom-call | tf_op jit(solution)/shard_map/pallas_call | solution.py:111
  111.5 1.4 %shard_map.178 = bf16[128,1024]{1,0:T(8,128)(2,1)} custom-call(s32[3]{0:T(128)S(1)} %pad_add_fusion.where_ref, bf16[128,1024]{1,0:T(8,128)(2,1)S(1)} %get-tuple-element.130.refs_0_, bf16[128,1024]{1,0:T(8,128)(2,1)S(1)} %collective-permute-done.25.refs_1_, bf16[128,1024]{1,0:T(8,128)(2,1)S(1)} %collective-permute-done.26.refs_2_, ...), custom_call_target="tpu_custom_call" | custom-call | tf_op jit(solution)/shard_map/pallas_call | solution.py:111
  (57 shorter events, 13.3 us)
Async XLA Ops:
  0.6 24.0 %copy-start = (bf16[1,512,1024]{2,1,0:T(8,128)(2,1)S(1)}, bf16[1,512,1024]{2,1,0:T(8,128)(2,1)}, u32[]{:S(2)}) copy-start(bf16[1,512,1024]{2,1,0:T(8,128)(2,1)} %param.11) | copy-start | bytes 3145732
  0.7 1.0 copy-start.9
  1.8 0.8 copy-start.10
  2.5 0.8 copy-start.11
  3.8 16.3 %collective-permute-start.1 = (bf16[128,1152]{1,0:T(8,128)(2,1)S(1)}, bf16[128,1152]{1,0:T(8,128)(2,1)S(1)}, u32[]{:S(2)}, u32[]{:S(2)}) collective-permute-start(bf16[128,1152]{1,0:T(8,128)(2,1)S(1)} %shard_map.161.refs_0_.refs_4_), channel_id=1, source_target_pairs={{0,8},{8,0},{16,24},{24,16},{1,9},{9,1},{17,25},{25,17},{2,10},{10... | collective-permute-start | bytes 884744 | tf_op jit(solution)/shard_map/ppermute | solution.py:19
  6.9 15.7 %collective-permute-start = (bf16[128,1152]{1,0:T(8,128)(2,1)S(1)}, bf16[128,1152]{1,0:T(8,128)(2,1)S(1)}, u32[]{:S(2)}, u32[]{:S(2)}) collective-permute-start(bf16[128,1152]{1,0:T(8,128)(2,1)S(1)} %shard_map.161.refs_0_.refs_4_), channel_id=1, source_target_pairs={{0,16},{8,24},{16,0},{24,8},{1,17},{9,25},{17,1},{25,9},{2,18},{10... | collective-permute-start | bytes 884744 | tf_op jit(solution)/shard_map/ppermute | solution.py:19
  9.5 1.2 %copy-start.1 = (bf16[1,512,1024]{2,1,0:T(8,128)(2,1)S(1)}, bf16[1,512,1024]{2,1,0:T(8,128)(2,1)}, u32[]{:S(2)}) copy-start(bf16[1,512,1024]{2,1,0:T(8,128)(2,1)} %param.12) | copy-start | bytes 3145732
  10.8 0.9 copy-start.5
  11.7 0.9 copy-start.7
  12.7 0.7 copy-start.12
  15.3 19.2 %collective-permute-start.6 = (bf16[896,256]{1,0:T(8,128)(2,1)S(1)}, bf16[896,256]{1,0:T(8,128)(2,1)S(1)}, u32[]{:S(2)}, u32[]{:S(2)}) collective-permute-start(bf16[896,256]{1,0:T(8,128)(2,1)S(1)} %get-tuple-element.86), channel_id=1, source_target_pairs={{0,1},{1,0},{2,3},{3,2},{4,5},{5,4},{6,7},{7,6},{8,9},{9,8},{10,11... | collective-permute-start | bytes 1376264 | tf_op jit(solution)/shard_map/ppermute | solution.py:19
  16.9 21.2 %collective-permute-start.7 = (bf16[896,256]{1,0:T(8,128)(2,1)S(1)}, bf16[896,256]{1,0:T(8,128)(2,1)S(1)}, u32[]{:S(2)}, u32[]{:S(2)}) collective-permute-start(bf16[896,256]{1,0:T(8,128)(2,1)S(1)} %get-tuple-element.87), channel_id=1, source_target_pairs={{0,2},{1,3},{2,0},{3,1},{4,6},{5,7},{6,4},{7,5},{8,10},{9,11},{10,... | collective-permute-start | bytes 1376264 | tf_op jit(solution)/shard_map/ppermute | solution.py:19
  18.4 19.7 %collective-permute-start.8 = (bf16[896,256]{1,0:T(8,128)(2,1)S(1)}, bf16[896,256]{1,0:T(8,128)(2,1)S(1)}, u32[]{:S(2)}, u32[]{:S(2)}) collective-permute-start(bf16[896,256]{1,0:T(8,128)(2,1)S(1)} %get-tuple-element.88), channel_id=1, source_target_pairs={{0,3},{1,2},{2,1},{3,0},{4,7},{5,6},{6,5},{7,4},{8,11},{9,10},{10,... | collective-permute-start | bytes 1376264 | tf_op jit(solution)/shard_map/ppermute | solution.py:19
  22.7 5.5 %collective-permute-start.2 = (bf16[128,1152]{1,0:T(8,128)(2,1)S(1)}, bf16[128,1152]{1,0:T(8,128)(2,1)S(1)}, u32[]{:S(2)}, u32[]{:S(2)}) collective-permute-start(bf16[128,1152]{1,0:T(8,128)(2,1)S(1)} %shard_map.161.refs_0_.refs_4_), channel_id=1, source_target_pairs={{8,16},{16,8},{9,17},{17,9},{10,18},{18,10},{11,19},{19,11},{12,20... | collective-permute-start | bytes 884744 | tf_op jit(solution)/shard_map/ppermute | solution.py:37
  23.3 9.2 %collective-permute-start.3 = (bf16[128,1152]{1,0:T(8,128)(2,1)S(1)}, bf16[128,1152]{1,0:T(8,128)(2,1)S(1)}, u32[]{:S(2)}, u32[]{:S(2)}) collective-permute-start(bf16[128,1152]{1,0:T(8,128)(2,1)S(1)} %collective-permute-done.refs_2_.refs_6_), channel_id=1, source_target_pairs={{8,0},{16,24},{9,1},{17,25},{10,2},{18,26},{11,3},{19,27},{12,4},{... | collective-permute-start | bytes 884744 | tf_op jit(solution)/shard_map/ppermute | solution.py:38
  24.7 1.6 %copy-start.3 = (bf16[1,1024,1024]{2,1,0:T(8,128)(2,1)S(1)}, bf16[1,1024,1024]{2,1,0:T(8,128)(2,1)}, u32[]{:S(2)}) copy-start(bf16[1,1024,1024]{2,1,0:T(8,128)(2,1)} %param.10) | copy-start | bytes 6291460
  38.1 5.9 %collective-permute-start.9 = (bf16[512,128]{1,0:T(8,128)(2,1)S(1)}, bf16[512,128]{1,0:T(8,128)(2,1)S(1)}, u32[]{:S(2)}, u32[]{:S(2)}) collective-permute-start(bf16[512,128]{1,0:T(8,128)(2,1)S(1)} %get-tuple-element.89), channel_id=1, source_target_pairs={{0,3},{1,2},{2,1},{3,0},{4,7},{5,6},{6,5},{7,4},{8,11},{9,10},{10,... | collective-permute-start | bytes 393224 | tf_op jit(solution)/shard_map/ppermute | solution.py:19
  39.6 5.8 %collective-permute-start.4 = (bf16[512,128]{1,0:T(8,128)(2,1)S(1)}, bf16[512,128]{1,0:T(8,128)(2,1)S(1)}, u32[]{:S(2)}, u32[]{:S(2)}) collective-permute-start(bf16[512,128]{1,0:T(8,128)(2,1)S(1)} %get-tuple-element.83), channel_id=1, source_target_pairs={{0,1},{1,0},{2,3},{3,2},{4,5},{5,4},{6,7},{7,6},{8,9},{9,8},{10,11... | collective-permute-start | bytes 393224 | tf_op jit(solution)/shard_map/ppermute | solution.py:19
  41.1 5.0 %collective-permute-start.5 = (bf16[512,128]{1,0:T(8,128)(2,1)S(1)}, bf16[512,128]{1,0:T(8,128)(2,1)S(1)}, u32[]{:S(2)}, u32[]{:S(2)}) collective-permute-start(bf16[512,128]{1,0:T(8,128)(2,1)S(1)} %get-tuple-element.84), channel_id=1, source_target_pairs={{0,2},{1,3},{2,0},{3,1},{4,6},{5,7},{6,4},{7,5},{8,10},{9,11},{10,... | collective-permute-start | bytes 393224 | tf_op jit(solution)/shard_map/ppermute | solution.py:19
  46.7 7.3 %collective-permute-start.10 = (bf16[512,128]{1,0:T(8,128)(2,1)S(1)}, bf16[512,128]{1,0:T(8,128)(2,1)S(1)}, u32[]{:S(2)}, u32[]{:S(2)}) collective-permute-start(bf16[512,128]{1,0:T(8,128)(2,1)S(1)} %shard_map.165.refs_0_), channel_id=1, source_target_pairs={{0,16},{8,24},{16,0},{24,8},{1,17},{9,25},{17,1},{25,9},{2,18},{10... | collective-permute-start | bytes 393224 | tf_op jit(solution)/shard_map/ppermute | solution.py:19
  48.0 11.6 %collective-permute-start.14 = (bf16[1024,128]{1,0:T(8,128)(2,1)S(1)}, bf16[1024,128]{1,0:T(8,128)(2,1)S(1)}, u32[]{:S(2)}, u32[]{:S(2)}) collective-permute-start(bf16[1024,128]{1,0:T(8,128)(2,1)S(1)} %get-tuple-element.94.refs_4_), channel_id=1, source_target_pairs={{0,3},{1,2},{2,1},{3,0},{4,7},{5,6},{6,5},{7,4},{8,11},{9,10},{10,... | collective-permute-start | bytes 786440 | tf_op jit(solution)/shard_map/ppermute | solution.py:19
  49.3 10.4 %collective-permute-start.13 = (bf16[1024,128]{1,0:T(8,128)(2,1)S(1)}, bf16[1024,128]{1,0:T(8,128)(2,1)S(1)}, u32[]{:S(2)}, u32[]{:S(2)}) collective-permute-start(bf16[1024,128]{1,0:T(8,128)(2,1)S(1)} %get-tuple-element.94.refs_4_), channel_id=1, source_target_pairs={{0,2},{1,3},{2,0},{3,1},{4,6},{5,7},{6,4},{7,5},{8,10},{9,11},{10,... | collective-permute-start | bytes 786440 | tf_op jit(solution)/shard_map/ppermute | solution.py:19
  50.3 9.4 %collective-permute-start.12 = (bf16[1024,128]{1,0:T(8,128)(2,1)S(1)}, bf16[1024,128]{1,0:T(8,128)(2,1)S(1)}, u32[]{:S(2)}, u32[]{:S(2)}) collective-permute-start(bf16[1024,128]{1,0:T(8,128)(2,1)S(1)} %get-tuple-element.94.refs_4_), channel_id=1, source_target_pairs={{0,1},{1,0},{2,3},{3,2},{4,5},{5,4},{6,7},{7,6},{8,9},{9,8},{10,11... | collective-permute-start | bytes 786440 | tf_op jit(solution)/shard_map/ppermute | solution.py:19
  54.6 5.0 %collective-permute-start.11 = (bf16[512,128]{1,0:T(8,128)(2,1)S(1)}, bf16[512,128]{1,0:T(8,128)(2,1)S(1)}, u32[]{:S(2)}, u32[]{:S(2)}) collective-permute-start(bf16[512,128]{1,0:T(8,128)(2,1)S(1)} %shard_map.166.refs_0_), channel_id=1, source_target_pairs={{0,8},{8,0},{16,24},{24,16},{1,9},{9,1},{17,25},{25,17},{2,10},{10... | collective-permute-start | bytes 393224 | tf_op jit(solution)/shard_map/ppermute | solution.py:19
  60.2 10.8 %collective-permute-start.15 = (bf16[512,512]{1,0:T(8,128)(2,1)S(1)}, bf16[512,512]{1,0:T(8,128)(2,1)S(1)}, u32[]{:S(2)}, u32[]{:S(2)}) collective-permute-start(bf16[512,512]{1,0:T(8,128)(2,1)S(1)} %get-tuple-element.96), channel_id=1, source_target_pairs={{0,8},{8,0},{16,24},{24,16},{1,9},{9,1},{17,25},{25,17},{2,10},{10... | collective-permute-start | bytes 1572872 | tf_op jit(solution)/shard_map/ppermute | solution.py:19
  60.3 6.0 %collective-permute-start.18 = (bf16[512,128]{1,0:T(8,128)(2,1)S(1)}, bf16[512,128]{1,0:T(8,128)(2,1)S(1)}, u32[]{:S(2)}, u32[]{:S(2)}) collective-permute-start(bf16[512,128]{1,0:T(8,128)(2,1)S(1)} %shard_map.168.refs_0_), channel_id=1, source_target_pairs={{0,3},{1,2},{2,1},{3,0},{4,7},{5,6},{6,5},{7,4},{8,11},{9,10},{10,... | collective-permute-start | bytes 393224 | tf_op jit(solution)/shard_map/ppermute | solution.py:19
  61.9 5.7 %collective-permute-start.17 = (bf16[512,128]{1,0:T(8,128)(2,1)S(1)}, bf16[512,128]{1,0:T(8,128)(2,1)S(1)}, u32[]{:S(2)}, u32[]{:S(2)}) collective-permute-start(bf16[512,128]{1,0:T(8,128)(2,1)S(1)} %shard_map.168.refs_0_), channel_id=1, source_target_pairs={{0,2},{1,3},{2,0},{3,1},{4,6},{5,7},{6,4},{7,5},{8,10},{9,11},{10,... | collective-permute-start | bytes 393224 | tf_op jit(solution)/shard_map/ppermute | solution.py:19
  63.1 5.0 %collective-permute-start.16 = (bf16[512,128]{1,0:T(8,128)(2,1)S(1)}, bf16[512,128]{1,0:T(8,128)(2,1)S(1)}, u32[]{:S(2)}, u32[]{:S(2)}) collective-permute-start(bf16[512,128]{1,0:T(8,128)(2,1)S(1)} %shard_map.168.refs_0_), channel_id=1, source_target_pairs={{0,1},{1,0},{2,3},{3,2},{4,5},{5,4},{6,7},{7,6},{8,9},{9,8},{10,11... | collective-permute-start | bytes 393224 | tf_op jit(solution)/shard_map/ppermute | solution.py:19
  71.1 2.8 %collective-permute-start.19 = (bf16[512,512]{1,0:T(8,128)(2,1)S(1)}, bf16[512,512]{1,0:T(8,128)(2,1)S(1)}, u32[]{:S(2)}, u32[]{:S(2)}) collective-permute-start(bf16[512,512]{1,0:T(8,128)(2,1)S(1)} %get-tuple-element.101), channel_id=1, source_target_pairs={{0,4},{1,5},{2,6},{3,7},{8,12},{9,13},{10,14},{11,15},{16,20},{17,... | collective-permute-start | bytes 1572872 | tf_op jit(solution)/shard_map/ppermute | solution.py:25
  76.3 4.8 %collective-permute-start.20 = (bf16[512,512]{1,0:T(8,128)(2,1)S(1)}, bf16[512,512]{1,0:T(8,128)(2,1)S(1)}, u32[]{:S(2)}, u32[]{:S(2)}) collective-permute-start(bf16[512,512]{1,0:T(8,128)(2,1)S(1)} %get-tuple-element.107), channel_id=1, source_target_pairs={{4,0},{5,1},{6,2},{7,3},{12,8},{13,9},{14,10},{15,11},{20,16},{21,... | collective-permute-start | bytes 1572872 | tf_op jit(solution)/shard_map/ppermute | solution.py:25
  78.5 15.6 %collective-permute-start.21 = (bf16[256,512]{1,0:T(8,128)(2,1)S(1)}, bf16[256,512]{1,0:T(8,128)(2,1)S(1)}, u32[]{:S(2)}, u32[]{:S(2)}) collective-permute-start(bf16[256,512]{1,0:T(8,128)(2,1)S(1)} %get-tuple-element.118), channel_id=1, source_target_pairs={{0,16},{8,24},{16,0},{24,8},{1,17},{9,25},{17,1},{25,9},{2,18},{10... | collective-permute-start | bytes 786440 | tf_op jit(solution)/shard_map/ppermute | solution.py:19
  81.2 1.9 %copy-start.4 = (bf16[1,1024,1024]{2,1,0:T(8,128)(2,1)S(1)}, bf16[1,1024,1024]{2,1,0:T(8,128)(2,1)}, u32[]{:S(2)}) copy-start(bf16[1,1024,1024]{2,1,0:T(8,128)(2,1)} %param.10) | copy-start | bytes 6291460
  85.5 26.0 %collective-permute-start.25 = (bf16[128,1024]{1,0:T(8,128)(2,1)S(1)}, bf16[128,1024]{1,0:T(8,128)(2,1)S(1)}, u32[]{:S(2)}, u32[]{:S(2)}) collective-permute-start(bf16[128,1024]{1,0:T(8,128)(2,1)S(1)} %get-tuple-element.131), channel_id=1, source_target_pairs={{0,1},{1,0},{2,3},{3,2},{4,5},{5,4},{6,7},{7,6},{8,9},{9,8},{10,11... | collective-permute-start | bytes 786440 | tf_op jit(solution)/shard_map/ppermute | solution.py:19
  85.6 26.0 %collective-permute-start.26 = (bf16[128,1024]{1,0:T(8,128)(2,1)S(1)}, bf16[128,1024]{1,0:T(8,128)(2,1)S(1)}, u32[]{:S(2)}, u32[]{:S(2)}) collective-permute-start(bf16[128,1024]{1,0:T(8,128)(2,1)S(1)} %get-tuple-element.132), channel_id=1, source_target_pairs={{0,2},{1,3},{2,0},{3,1},{4,6},{5,7},{6,4},{7,5},{8,10},{9,11},{10,... | collective-permute-start | bytes 786440 | tf_op jit(solution)/shard_map/ppermute | solution.py:19
  88.2 23.4 %collective-permute-start.27 = (bf16[128,1024]{1,0:T(8,128)(2,1)S(1)}, bf16[128,1024]{1,0:T(8,128)(2,1)S(1)}, u32[]{:S(2)}, u32[]{:S(2)}) collective-permute-start(bf16[128,1024]{1,0:T(8,128)(2,1)S(1)} %get-tuple-element.133), channel_id=1, source_target_pairs={{0,3},{1,2},{2,1},{3,0},{4,7},{5,6},{6,5},{7,4},{8,11},{9,10},{10,... | collective-permute-start | bytes 786440 | tf_op jit(solution)/shard_map/ppermute | solution.py:19
  95.5 5.5 %collective-permute-start.22 = (bf16[128,256]{1,0:T(8,128)(2,1)S(1)}, bf16[128,256]{1,0:T(8,128)(2,1)S(1)}, u32[]{:S(2)}, u32[]{:S(2)}) collective-permute-start(bf16[128,256]{1,0:T(8,128)(2,1)S(1)} %get-tuple-element.120), channel_id=1, source_target_pairs={{0,8},{8,0},{16,24},{24,16},{1,9},{9,1},{17,25},{25,17},{2,10},{10... | collective-permute-start | bytes 196616 | tf_op jit(solution)/shard_map/ppermute | solution.py:19
  95.6 14.6 %collective-permute-start.23 = (bf16[128,256]{1,0:T(8,128)(2,1)S(1)}, bf16[128,256]{1,0:T(8,128)(2,1)S(1)}, u32[]{:S(2)}, u32[]{:S(2)}) collective-permute-start(bf16[128,256]{1,0:T(8,128)(2,1)S(1)} %get-tuple-element.121), channel_id=1, source_target_pairs={{0,16},{8,24},{16,0},{24,8},{1,17},{9,25},{17,1},{25,9},{2,18},{10... | collective-permute-start | bytes 196616 | tf_op jit(solution)/shard_map/ppermute | solution.py:19
  101.0 5.8 %copy-start.2 = (bf16[1,512,1024]{2,1,0:T(8,128)(2,1)S(1)}, bf16[1,512,1024]{2,1,0:T(8,128)(2,1)}, u32[]{:S(2)}) copy-start(bf16[1,512,1024]{2,1,0:T(8,128)(2,1)} %param.12) | copy-start | bytes 3145732
  101.0 5.8 %copy-start.6 = (bf16[1,128,1024]{2,1,0:T(8,128)(2,1)S(1)}, bf16[1,128,1024]{2,1,0:T(8,128)(2,1)}, u32[]{:S(2)}) copy-start(bf16[1,128,1024]{2,1,0:T(8,128)(2,1)} %param.15) | copy-start | bytes 786436
  101.0 5.8 %copy-start.8 = (bf16[1,1024,128]{2,1,0:T(8,128)(2,1)S(1)}, bf16[1,1024,128]{2,1,0:T(8,128)(2,1)}, u32[]{:S(2)}) copy-start(bf16[1,1024,128]{2,1,0:T(8,128)(2,1)} %param.14) | copy-start | bytes 786436
  101.0 5.8 %copy-start.13 = (f32[1,1024]{1,0:T(1,128)S(1)}, f32[1,1024]{1,0:T(1,128)}, u32[]{:S(2)}) copy-start(f32[1,1024]{1,0:T(1,128)} %refs_9_.1) | copy-start | bytes 12292
  101.0 9.2 %collective-permute-start.24 = (bf16[128,256]{1,0:T(8,128)(2,1)S(1)}, bf16[128,256]{1,0:T(8,128)(2,1)S(1)}, u32[]{:S(2)}, u32[]{:S(2)}) collective-permute-start(bf16[128,256]{1,0:T(8,128)(2,1)S(1)} %get-tuple-element.122), channel_id=1, source_target_pairs={{0,24},{8,16},{16,8},{24,0},{1,25},{9,17},{17,9},{25,1},{2,26},{10... | collective-permute-start | bytes 196616 | tf_op jit(solution)/shard_map/ppermute | solution.py:19

commit v9 on v8

--- a/solution.py
+++ b/solution.py
@@ -31,12 +31,12 @@
 
 def line_gathered(shard, axis):
     if lax.axis_size(axis) != 4:
-        return gathered(shard, axis)
+        return gathered(shard, axis), []
     far, near = swap(shard, axis, 2), swap(shard, axis, 1)
     shard, far, near = lax.optimization_barrier((shard, far, near))
     across = lax.ppermute(shard, axis, [(1, 2), (2, 1)])
     passed = lax.ppermute(far, axis, [(1, 0), (2, 3)])
-    return [shard, near, far, (across, passed)]
+    return [shard, near, far], [across, passed]
 
 
 def scattered(blocks, axis):
@@ -64,7 +64,7 @@
         if step == 1:
             other, after = lax.optimization_barrier((other, after))
         if count == 1:
-            return total([kept, other], where), after
+            return [kept, other], after
         half = like((count // 2 * size, kept.shape[1]))
         kept, given = run(
             functools.partial(halved_kernel, size), [half, half], where, [(kept, other)]
@@ -95,28 +95,50 @@
     return lax.dot_general(left, right, (over, ((), ())), preferred_element_type=f32)
 
 
-def run(kernel, results, where, groups_of_args, scratch=(), flops=0):
+def run(kernel, results, where, groups_of_args, scratch=(), flops=0, fetch=False):
     counts = [len(group) for group in groups_of_args]
     flat = [array for group in groups_of_args for array in group]
     out_count = len(results)
+    scratch = list(scratch)
+    own = len(scratch)
+    space = pltpu.HBM if fetch else pltpu.VMEM
+    if fetch:
+        scratch += [pltpu.VMEM(array.shape, array.dtype) for array in flat]
+        scratch.append(pltpu.SemaphoreType.DMA((len(flat),)))
 
     def body(where_ref, *refs):
+        args, refs = refs[: len(flat)], refs[len(flat) :]
+        outs, refs = refs[:out_count], refs[out_count:]
+        if fetch:
+            held, arrived = refs[own:-1], refs[-1]
+            copies = [
+                pltpu.make_async_copy(arg, here, arrived.at[k])
+                for k, (arg, here) in enumerate(zip(args, held))
+            ]
+            for copy in copies:
+                copy.start()
+            for copy in copies:
+                copy.wait()
+            args = held
         ins, at = [], 0
         for count in counts:
-            ins.append(refs[at : at + count])
+            ins.append(args[at : at + count])
             at += count
-        kernel(where_ref, ins, refs[at : at + out_count], refs[at + out_count :])
+        kernel(where_ref, ins, outs, refs[:own])
 
     size = sum(a.size * a.dtype.itemsize for a in list(flat) + list(results))
+    limit = (10 << 20) if size < (10 << 20) else size + (12 << 20)
     return pl.pallas_call(
         body,
         out_shape=[jax.ShapeDtypeStruct(r.shape, r.dtype) for r in results],
         in_specs=[pl.BlockSpec(memory_space=pltpu.SMEM)]
-        + [pl.BlockSpec(memory_space=pltpu.VMEM)] * len(flat),
+        + [pl.BlockSpec(memory_space=space)] * len(flat),
         out_specs=[pl.BlockSpec(memory_space=pltpu.VMEM)] * out_count,
-        scratch_shapes=list(scratch),
-        compiler_params=pltpu.CompilerParams(vmem_limit_bytes=(10 << 20) if size < (10 << 20) else size + (12 << 20)),
-        cost_estimate=pl.CostEstimate(flops=flops, bytes_accessed=size if flops else 0, transcendentals=0),
+        scratch_shapes=scratch,
+        compiler_params=pltpu.CompilerParams(vmem_limit_bytes=limit),
+        cost_estimate=pl.CostEstimate(
+            flops=flops, bytes_accessed=size if flops else 0, transcendentals=0
+        ),
     )(where, *flat)
 
 
@@ -204,7 +226,7 @@
         payload[(2 * j + 1) * cols : (2 * j + 2) * cols, :] = gram[:, relay:]
     start = 2 * head
     for end in ends:
-        payload[start : start + end.shape[0], :] = end[:, end.shape[1] - relay :]
+        payload[start : start + end.shape[0], :] = end[...]
         start += end.shape[0]
     for k, pack in enumerate(packs):
         here = slice(k * relay, (k + 1) * relay)
@@ -212,13 +234,6 @@
         weights[:, here] = pack[head : head + codes, :relay]
         there = slice((parts + k) * relay, (parts + k + 1) * relay)
         weights[:, there] = pack[head : head + codes, relay:]
-
-
-def rows_kernel(where, ins, outs, scratch):
-    ((heads, first, last),) = ins
-    width = heads.shape[1]
-    outs[0][:, :width] = heads[...]
-    outs[0][:, width:] = jnp.where(where[2] == 0, first[...], last[...])
 
 
 def fold_kernel(groups, where, ins, outs, scratch):
@@ -233,15 +248,19 @@
 
 
 def partial_kernel(where, ins, outs, scratch):
-    heads, (fold,) = ins
+    heads, pair, (fold,) = ins
     (whole,) = scratch
-    tokens, width = heads[0].shape[0], fold.shape[0]
+    if pair:
+        outs, last = outs[:-1], outs[-1]
+        last[...] = pair[0][...] + pair[1][...]
+        heads = [*heads, last]
+    tokens = heads[0].shape[0]
     cols = outs[0].shape[1]
     parts = len(outs)
     together = 4 if len(heads) % 4 == 0 else 1
     for first in range(0, len(heads), together):
         rows = slice(first * tokens, (first + together) * tokens)
-        values = jnp.concatenate([h[:, :width] for h in heads[first : first + together]])
+        values = jnp.concatenate([h[...] for h in heads[first : first + together]])
         whole[...] = dot(values, fold[...], NN)
         for k in range(parts):
             at = (where[0] ^ k) * cols
@@ -361,9 +380,12 @@
 
 
 def heads_kernel(where, ins, outs, scratch):
-    ((code_grad, fold_rows),) = ins
+    (code_grad,), terms = ins
     tokens = outs[0].shape[0]
-    whole = dot(code_grad[...], fold_rows[...], NT)
+    fold_rows = terms[0][...].astype(f32)
+    for term in terms[1:]:
+        fold_rows = fold_rows + term[...].astype(f32)
+    whole = dot(code_grad[...], fold_rows.astype(bf16), NT)
     for k, out in enumerate(outs):
         out[...] = whole[k * tokens : (k + 1) * tokens, :].astype(bf16)
 
@@ -380,12 +402,12 @@
     heads, (code_grad, proj) = ins
     head_sum, enc_blocks = outs[0], outs[1:]
     (whole,) = scratch
-    tokens, width = heads[0].shape[0], proj.shape[0]
+    tokens = heads[0].shape[0]
     together = 4 if len(heads) % 4 == 0 else 1
     sums = None
     for first in range(0, len(heads), together):
         rows = slice(first * tokens, (first + together) * tokens)
-        values = jnp.concatenate([h[:, :width] for h in heads[first : first + together]])
+        values = jnp.concatenate([h[...] for h in heads[first : first + together]])
         term = dot(code_grad[rows, :], values, TN)
         sums = term if sums is None else sums + term
     head_sum[...] = sums.astype(bf16)
@@ -461,22 +483,16 @@
     head_cols, model_cols = proj.shape
     where = jnp.stack([lax.axis_index("tensor"), lax.axis_index("dp"), section]).astype(jnp.int32)
 
-    head_cols, model_cols = proj.shape
-    (rows_here,) = run(
-        rows_kernel,
-        [like((tokens, head_cols + relay))],
-        where,
-        [(heads_out[0], input_code, code_cotangent)],
-    )
-    heads = line_gathered(rows_here, "dp")
-    if isinstance(heads[-1], tuple):
-        heads[-1] = total(heads[-1], where)
+    heads, pair = line_gathered(heads_out[0], "dp")
+    end = jnp.where(section == 0, input_code, code_cotangent)
+    ends = gathered(end, "dp")
     packs = run(
         gram_kernel,
         [like((cols * codes // (2 * relay) + codes + relay, 2 * relay))] * parts,
         where,
         [(dec, recv, send, gain)],
         scratch=[pltpu.VMEM((codes, codes), f32)],
+        fetch=True,
     )
     half = like((head_cols // 2, codes))
     fold, fold_kept, fold_given = run(
@@ -484,20 +500,21 @@
         [like((head_cols, codes)), half, half],
         where,
         [(proj, enc)],
+        fetch=True,
     )
     fold, _ = lax.optimization_barrier((fold, packs[0]))
     packs = scattered(packs, "tensor")
 
     partials = run(
         partial_kernel,
-        [like((rows, cols))] * parts,
-        where,
-        [heads, (fold,)],
+        [like((rows, cols))] * parts + [like((tokens, head_cols))] * (len(pair) // 2),
+        where,
+        [heads, pair, (fold,)],
         scratch=[pltpu.VMEM((min(groups, 4) * tokens, codes), f32)],
         flops=2 * rows * head_cols * codes,
     )
-    partials = list(partials)
-    partials[3], *_ = lax.optimization_barrier((partials[3], *packs))
+    partials, heads = list(partials[:parts]), [*heads, *partials[parts:]]
+    partials[-1], *_ = lax.optimization_barrier((partials[-1], *packs, *ends))
     code_block = total(scattered(partials, "tensor"), where)
     wide = parts * relay
     packs, _ = lax.optimization_barrier((packs, code_block))
@@ -509,7 +526,7 @@
             like((codes, 2 * wide)),
         ],
         where,
-        [packs, heads],
+        [packs, ends],
     )
     payloads = gathered(payload, "tensor")
     mix_block = group_sum(code_block, payloads, "dp", where)
@@ -533,7 +550,7 @@
         scratch=[pltpu.VMEM((codes, codes), bf16)],
         flops=3 * square_flops,
     )
-    fold_rows, sent = halved_sum(
+    fold_terms, sent = halved_sum(
         fold_kept, fold_given, sent, "dp", head_cols // groups, where
     )
     received = ends
@@ -593,17 +610,6 @@
     )
     head_sum, mix, *enc_blocks = lax.optimization_barrier((head_sum, mix, *enc_blocks))
     enc_grad = total(scattered(enc_blocks, "tensor"), where)
-    head_blocks = run(
-        heads_kernel,
-        [like((tokens, head_cols // groups))] * groups,
-        where,
-        [(code_grad, fold_rows)],
-    )
-    head_blocks = scattered(head_blocks, "dp")
-    if head_cols // groups % 128 == 0:
-        (heads_grad,) = run(laid_kernel, [like((tokens, head_cols))], where, [head_blocks])
-    else:
-        heads_grad = ordered(head_blocks, "dp")
     (proj_grad,) = run(proj_kernel, [like((head_cols, model_cols))], where, [(head_sum, enc)])
     shapes = [(codes // groups, features), (1, features), (features, relay), (relay, features)]
     dec_grad, gain_grad, send_grad, recv_grad = run(
@@ -626,6 +632,18 @@
         ],
         scratch=[pltpu.VMEM(shape, f32) for shape in shapes],
     )
+    fold_terms, _, _ = lax.optimization_barrier((fold_terms, proj_grad, dec_grad))
+    head_blocks = run(
+        heads_kernel,
+        [like((tokens, head_cols // groups))] * groups,
+        where,
+        [(code_grad,), fold_terms],
+    )
+    head_blocks = scattered(head_blocks, "dp")
+    if head_cols // groups % 128 == 0:
+        (heads_grad,) = run(laid_kernel, [like((tokens, head_cols))], where, [head_blocks])
+    else:
+        heads_grad = ordered(head_blocks, "dp")
     return (
         sent[None],
         returned[None],

time: 113 us -> 109 us (0.965)
  waiting for transfers between devices: 37.5 us -> 32.4 us
  local copies, waits for them, and re-layouts: 7.96 us -> 5.43 us
  starting transfers between devices: 37 us -> 38.9 us
    ppermute x24 -> x27, waiting for transfers between devices: 31.7 us -> 28.6 us  [swap(): lax.ppermute(shard, axis, [(i, i ^ by) for i in range(lax.axis_size(axis))])]
    unnamed x28 -> x24, local copies, waits for them, and re-layouts: 7.96 us -> 5.43 us
    ppermute x1, waiting for transfers between devices: 4.37 us -> 2.32 us  [line_gathered(): passed = lax.ppermute(far, axis, [(1, 0), (2, 3)])]
    ppermute x24 -> x27, starting transfers between devices: 32.3 us -> 34.2 us  [swap(): lax.ppermute(shard, axis, [(i, i ^ by) for i in range(lax.axis_size(axis))])]
    pallas_call x20 -> x17, Pallas kernels: 29.4 us -> 30 us  [run(): pl.pallas_call(body, out_shape=[jax.ShapeDtypeStruct(r.shape, r.dtype) fo...]
  transfers between devices with their start and end apart: 28 -> 31, of which waited for: 16 -> 15; matrix products, arithmetic and copies ran while one was open for 0% -> 1% of each run, Pallas kernels for 21% -> 23%
where the time goes in v9:
time: 109 us; the launch traced here: 108 us
  starting transfers between devices  38.9 us (36%)
  waiting for transfers between devices  32.4 us (30%)
  Pallas kernels  30 us (28%)
  local copies, waits for them, and re-layouts  5.43 us (5%)
    ppermute x27, starting transfers between devices, swap(): lax.ppermute(shard, axis, [(i, i ^ by) for i in range(lax.axis_size(axis))])  34.2 us
    pallas_call x17, Pallas kernels, run(): pl.pallas_call(body, out_shape=[jax.ShapeDtypeStruct(r.shape, r.dtype) fo...  30 us
    ppermute x27, waiting for transfers between devices, swap(): lax.ppermute(shard, axis, [(i, i ^ by) for i in range(lax.axis_size(axis))])  28.6 us
    unnamed x24, local copies, waits for them, and re-layouts  5.43 us
    ppermute x2, starting transfers between devices, move(): return lax.ppermute(shard, axis, pairs)  2.78 us
    ppermute x1, waiting for transfers between devices, line_gathered(): passed = lax.ppermute(far, axis, [(1, 0), (2, 3)])  2.32 us
  transfers between devices with their start and end apart: 31, of which 15 were waited for; matrix products, arithmetic and copies ran while one was open for 1% of the time, Pallas kernels for 23%

profile of v9, /device:TPU:0, one launch (start us, length us, event | category | flops | bytes accessed | tf_op | source)
XLA Modules:
  0.0 108.5 jit_solution(17512703246476005248)
XLA Ops:
  0.7 3.1 %collective-permute-start.1 = (bf16[128,1024]{1,0:T(8,128)(2,1)}, bf16[128,1024]{1,0:T(8,128)(2,1)S(1)}, u32[]{:S(2)}, u32[]{:S(2)}) collective-permute-start(bf16[128,1024]{1,0:T(8,128)(2,1)} %bitcast.27), channel_id=1, source_target_pairs={{0,8},{8,0},{16,24},{24,16},{1,9},{9,1},{17,25},{25,17},{2,10},{10... | collective-permute-start | bytes 786440 | tf_op jit(solution)/shard_map/ppermute | solution.py:19
  3.7 2.6 %collective-permute-start = (bf16[128,1024]{1,0:T(8,128)(2,1)}, bf16[128,1024]{1,0:T(8,128)(2,1)}, u32[]{:S(2)}, u32[]{:S(2)}) collective-permute-start(bf16[128,1024]{1,0:T(8,128)(2,1)} %bitcast.28), channel_id=1, source_target_pairs={{0,16},{8,24},{16,0},{24,8},{1,17},{9,25},{17,1},{25,9},{2,18},{10... | collective-permute-start | bytes 786440 | tf_op jit(solution)/shard_map/ppermute | solution.py:19
  6.4 1.2 %copy-done.1 = bf16[1,512,1024]{2,1,0:T(8,128)(2,1)S(1)} copy-done((bf16[1,512,1024]{2,1,0:T(8,128)(2,1)S(1)}, bf16[1,512,1024]{2,1,0:T(8,128)(2,1)}, u32[]{:S(2)}) %copy-start.1) | copy-done | bytes 1048600
  7.6 0.9 copy-done.5
  8.6 0.9 copy-done.7
  10.2 3.2 %shard_map.161 = (bf16[896,256]{1,0:T(8,128)(2,1)S(1)}, bf16[896,256]{1,0:T(8,128)(2,1)}, bf16[896,256]{1,0:T(8,128)(2,1)}, bf16[896,256]{1,0:T(8,128)(2,1)}) custom-call(s32[3]{0:T(128)S(1)} %pad_add_fusion.where_ref, bf16[512,1024]{1,0:T(8,128)(2,1)S(1)} %bitcast.19, bf16[128,1024]{1,0:T(8,128)(2,1)S(1)} %bitcast.23, bf16[1024,128]{1,0:T(8,128)(2,1)S(1)} %bitcast.25, ...), custom_call_target="tpu_custom_call" | custom-call | tf_op jit(solution)/shard_map/pallas_call | solution.py:131
  13.5 1.6 %collective-permute-start.6 = (bf16[896,256]{1,0:T(8,128)(2,1)}, bf16[896,256]{1,0:T(8,128)(2,1)S(1)}, u32[]{:S(2)}, u32[]{:S(2)}) collective-permute-start(bf16[896,256]{1,0:T(8,128)(2,1)} %get-tuple-element.89), channel_id=1, source_target_pairs={{0,1},{1,0},{2,3},{3,2},{4,5},{5,4},{6,7},{7,6},{8,9},{9,8},{10,11... | collective-permute-start | bytes 1376264 | tf_op jit(solution)/shard_map/ppermute | solution.py:19
  15.0 1.5 %collective-permute-start.7 = (bf16[896,256]{1,0:T(8,128)(2,1)}, bf16[896,256]{1,0:T(8,128)(2,1)S(1)}, u32[]{:S(2)}, u32[]{:S(2)}) collective-permute-start(bf16[896,256]{1,0:T(8,128)(2,1)} %get-tuple-element.90), channel_id=1, source_target_pairs={{0,2},{1,3},{2,0},{3,1},{4,6},{5,7},{6,4},{7,5},{8,10},{9,11},{10,... | collective-permute-start | bytes 1376264 | tf_op jit(solution)/shard_map/ppermute | solution.py:19
  19.1 4.6 %collective-permute-done.11.refs_7_ = bf16[128,128]{1,0:T(8,128)(2,1)S(1)} collective-permute-done((bf16[128,128]{1,0:T(8,128)(2,1)S(1)}, bf16[128,128]{1,0:T(8,128)(2,1)S(1)}, u32[]{:S(2)}, u32[]{:S(2)}) %collective-permute-start.11) | collective-permute-done | bytes 32800 | tf_op jit(solution)/shard_map/ppermute | solution.py:19
  23.7 1.3 %collective-permute-start.3 = (bf16[128,1024]{1,0:T(8,128)(2,1)}, bf16[128,1024]{1,0:T(8,128)(2,1)S(1)}, u32[]{:S(2)}, u32[]{:S(2)}) collective-permute-start(bf16[128,1024]{1,0:T(8,128)(2,1)} %collective-permute-done.refs_2_), channel_id=1, source_target_pairs={{8,0},{16,24},{9,1},{17,25},{10,2},{18,26},{11,3},{19,27},{12,4},{... | collective-permute-start | bytes 786440 | tf_op jit(solution)/shard_map/ppermute | solution.py:38
  25.0 1.6 %copy-done.3 = bf16[1,1024,1024]{2,1,0:T(8,128)(2,1)S(1)} copy-done((bf16[1,1024,1024]{2,1,0:T(8,128)(2,1)S(1)}, bf16[1,1024,1024]{2,1,0:T(8,128)(2,1)}, u32[]{:S(2)}) %copy-start.3) | copy-done | bytes 2097176
  26.6 2.1 %shard_map.160 = (bf16[1024,512]{1,0:T(8,128)(2,1)S(1)}, bf16[512,512]{1,0:T(8,128)(2,1)S(1)}, bf16[512,512]{1,0:T(8,128)(2,1)S(1)}) custom-call(s32[3]{0:T(128)S(1)} %pad_add_fusion.where_ref, bf16[1024,1024]{1,0:T(8,128)(2,1)S(1)} %bitcast.21, bf16[512,1024]{1,0:T(8,128)(2,1)S(1)} %bitcast.17), custom_call_target="tpu_custom_call" | custom-call | tf_op jit(solution)/shard_map/pallas_call | solution.py:131
  28.7 1.8 %collective-permute-start.10 = (bf16[128,128]{1,0:T(8,128)(2,1)S(1)}, bf16[128,128]{1,0:T(8,128)(2,1)S(1)}, u32[]{:S(2)}, u32[]{:S(2)}) collective-permute-start(bf16[128,128]{1,0:T(8,128)(2,1)S(1)} %broadcast_select_fusion.refs_4_), channel_id=1, source_target_pairs={{0,16},{8,24},{16,0},{24,8},{1,17},{9,25},{17,1},{25,9},{2,18},{10... | collective-permute-start | bytes 98312 | tf_op jit(solution)/shard_map/ppermute | solution.py:19
  30.5 2.3 %collective-permute-done.3.refs_4_ = bf16[128,1024]{1,0:T(8,128)(2,1)S(1)} collective-permute-done((bf16[128,1024]{1,0:T(8,128)(2,1)}, bf16[128,1024]{1,0:T(8,128)(2,1)S(1)}, u32[]{:S(2)}, u32[]{:S(2)}) %collective-permute-start.3) | collective-permute-done | bytes 262176 | tf_op jit(solution)/shard_map/ppermute | solution.py:38
  32.8 1.8 %shard_map.162 = (bf16[512,128]{1,0:T(8,128)(2,1)S(1)}, bf16[512,128]{1,0:T(8,128)(2,1)S(1)}, bf16[512,128]{1,0:T(8,128)(2,1)S(1)}, bf16[512,128]{1,0:T(8,128)(2,1)S(1)}, bf16[128,1024]{1,0:T(8,128)(2,1)S(1)}) custom-call(s32[3]{0:T(128)S(1)} %pad_add_fusion.where_ref, bf16[128,1024]{1,0:T(8,128)(2,1)S(1)} %bitcast.30, ...), custom_call_target="tpu_custom_call" | custom-call | flops 536870912 | bytes 3145728 | tf_op jit(solution)/shard_map/pallas_call | solution.py:131
  34.7 2.1 %collective-permute-done.9.refs_5_ = bf16[128,128]{1,0:T(8,128)(2,1)S(1)} collective-permute-done((bf16[128,128]{1,0:T(8,128)(2,1)S(1)}, bf16[128,128]{1,0:T(8,128)(2,1)S(1)}, u32[]{:S(2)}, u32[]{:S(2)}) %collective-permute-start.9) | collective-permute-done | bytes 32800 | tf_op jit(solution)/shard_map/ppermute | solution.py:19
  36.8 2.5 %collective-permute-start.12 = (bf16[512,128]{1,0:T(8,128)(2,1)S(1)}, bf16[512,128]{1,0:T(8,128)(2,1)S(1)}, u32[]{:S(2)}, u32[]{:S(2)}) collective-permute-start(bf16[512,128]{1,0:T(8,128)(2,1)S(1)} %get-tuple-element.92), channel_id=1, source_target_pairs={{0,3},{1,2},{2,1},{3,0},{4,7},{5,6},{6,5},{7,4},{8,11},{9,10},{10,... | collective-permute-start | bytes 393224 | tf_op jit(solution)/shard_map/ppermute | solution.py:19
  40.3 2.4 %collective-permute-done.12.refs_3_ = bf16[512,128]{1,0:T(8,128)(2,1)S(1)} collective-permute-done((bf16[512,128]{1,0:T(8,128)(2,1)S(1)}, bf16[512,128]{1,0:T(8,128)(2,1)S(1)}, u32[]{:S(2)}, u32[]{:S(2)}) %collective-permute-start.12) | collective-permute-done | bytes 131104 | tf_op jit(solution)/shard_map/ppermute | solution.py:19
  42.7 1.6 %collective-permute-done.4.refs_1_ = bf16[512,128]{1,0:T(8,128)(2,1)S(1)} collective-permute-done((bf16[512,128]{1,0:T(8,128)(2,1)S(1)}, bf16[512,128]{1,0:T(8,128)(2,1)S(1)}, u32[]{:S(2)}, u32[]{:S(2)}) %collective-permute-start.4) | collective-permute-done | bytes 131104 | tf_op jit(solution)/shard_map/ppermute | solution.py:19
  45.5 0.9 shard_map.165
  46.4 1.8 %collective-permute-start.17 = (bf16[1024,128]{1,0:T(8,128)(2,1)S(1)}, bf16[1024,128]{1,0:T(8,128)(2,1)S(1)}, u32[]{:S(2)}, u32[]{:S(2)}) collective-permute-start(bf16[1024,128]{1,0:T(8,128)(2,1)S(1)} %get-tuple-element.97.refs_4_), channel_id=1, source_target_pairs={{0,3},{1,2},{2,1},{3,0},{4,7},{5,6},{6,5},{7,4},{8,11},{9,10},{10,... | collective-permute-start | bytes 786440 | tf_op jit(solution)/shard_map/ppermute | solution.py:19
  48.2 1.2 %collective-permute-start.16 = (bf16[1024,128]{1,0:T(8,128)(2,1)S(1)}, bf16[1024,128]{1,0:T(8,128)(2,1)S(1)}, u32[]{:S(2)}, u32[]{:S(2)}) collective-permute-start(bf16[1024,128]{1,0:T(8,128)(2,1)S(1)} %get-tuple-element.97.refs_4_), channel_id=1, source_target_pairs={{0,2},{1,3},{2,0},{3,1},{4,6},{5,7},{6,4},{7,5},{8,10},{9,11},{10,... | collective-permute-start | bytes 786440 | tf_op jit(solution)/shard_map/ppermute | solution.py:19
  49.9 2.4 %collective-permute-done.13.refs_1_ = bf16[512,128]{1,0:T(8,128)(2,1)S(1)} collective-permute-done((bf16[512,128]{1,0:T(8,128)(2,1)S(1)}, bf16[512,128]{1,0:T(8,128)(2,1)S(1)}, u32[]{:S(2)}, u32[]{:S(2)}) %collective-permute-start.13) | collective-permute-done | bytes 131104 | tf_op jit(solution)/shard_map/ppermute | solution.py:19
  53.0 6.3 %collective-permute-done.14.refs_1_ = bf16[512,128]{1,0:T(8,128)(2,1)S(1)} collective-permute-done((bf16[512,128]{1,0:T(8,128)(2,1)S(1)}, bf16[512,128]{1,0:T(8,128)(2,1)S(1)}, u32[]{:S(2)}, u32[]{:S(2)}) %collective-permute-start.14) | collective-permute-done | bytes 131104 | tf_op jit(solution)/shard_map/ppermute | solution.py:19
  60.7 2.2 %collective-permute-start.20 = (bf16[512,128]{1,0:T(8,128)(2,1)S(1)}, bf16[512,128]{1,0:T(8,128)(2,1)S(1)}, u32[]{:S(2)}, u32[]{:S(2)}) collective-permute-start(bf16[512,128]{1,0:T(8,128)(2,1)S(1)} %shard_map.166.refs_0_), channel_id=1, source_target_pairs={{0,2},{1,3},{2,0},{3,1},{4,6},{5,7},{6,4},{7,5},{8,10},{9,11},{10,... | collective-permute-start | bytes 393224 | tf_op jit(solution)/shard_map/ppermute | solution.py:19
  63.5 2.5 %collective-permute-done.21.refs_3_ = bf16[512,128]{1,0:T(8,128)(2,1)S(1)} collective-permute-done((bf16[512,128]{1,0:T(8,128)(2,1)S(1)}, bf16[512,128]{1,0:T(8,128)(2,1)S(1)}, u32[]{:S(2)}, u32[]{:S(2)}) %collective-permute-start.21) | collective-permute-done | bytes 131104 | tf_op jit(solution)/shard_map/ppermute | solution.py:19
  66.0 1.2 %collective-permute-done.20.refs_2_ = bf16[512,128]{1,0:T(8,128)(2,1)S(1)} collective-permute-done((bf16[512,128]{1,0:T(8,128)(2,1)S(1)}, bf16[512,128]{1,0:T(8,128)(2,1)S(1)}, u32[]{:S(2)}, u32[]{:S(2)}) %collective-permute-start.20) | collective-permute-done | bytes 131104 | tf_op jit(solution)/shard_map/ppermute | solution.py:19
  67.8 2.1 %shard_map.167 = (bf16[512,512]{1,0:T(8,128)(2,1)S(1)}, bf16[512,512]{1,0:T(8,128)(2,1)S(1)}, f32[512,512]{1,0:T(8,128)S(1)}, f32[512,512]{1,0:T(8,128)S(1)}, f3...) custom-call(s32[3]{0:T(128)S(1)} %pad_add_fusion.where_ref, ...), custom_call_target="tpu_custom_call" | custom-call | flops 805306368 | bytes 7604224 | tf_op jit(solution)/shard_map/pallas_call | solution.py:131
  69.9 1.3 %collective-permute-start.22 = (bf16[512,512]{1,0:T(8,128)(2,1)S(1)}, bf16[512,512]{1,0:T(8,128)(2,1)S(1)}, u32[]{:S(2)}, u32[]{:S(2)}) collective-permute-start(bf16[512,512]{1,0:T(8,128)(2,1)S(1)} %get-tuple-element.104), channel_id=1, source_target_pairs={{0,4},{1,5},{2,6},{3,7},{8,12},{9,13},{10,14},{11,15},{16,20},{17,... | collective-permute-start | bytes 1572872 | tf_op jit(solution)/shard_map/ppermute | solution.py:25
  71.3 1.5 %collective-permute-done.22.refs_0_ = bf16[512,512]{1,0:T(8,128)(2,1)S(1)} collective-permute-done((bf16[512,512]{1,0:T(8,128)(2,1)S(1)}, bf16[512,512]{1,0:T(8,128)(2,1)S(1)}, u32[]{:S(2)}, u32[]{:S(2)}) %collective-permute-start.22) | collective-permute-done | bytes 524320 | tf_op jit(solution)/shard_map/ppermute | solution.py:25
  72.7 2.5 %shard_map.168 = (bf16[512,512]{1,0:T(8,128)(2,1)S(1)}, bf16[512,512]{1,0:T(8,128)(2,1)}, f32[512,512]{1,0:T(8,128)S(1)}, f32[512,512]{1,0:T(8,128)S(1)}, f32[51...) custom-call(s32[3]{0:T(128)S(1)} %pad_add_fusion.where_ref, ...), custom_call_target="tpu_custom_call" | custom-call | flops 268435456 | bytes 7639040 | tf_op jit(solution)/shard_map/pallas_call | solution.py:131
  75.2 1.5 %collective-permute-start.23 = (bf16[512,512]{1,0:T(8,128)(2,1)S(1)}, bf16[512,512]{1,0:T(8,128)(2,1)S(1)}, u32[]{:S(2)}, u32[]{:S(2)}) collective-permute-start(bf16[512,512]{1,0:T(8,128)(2,1)S(1)} %get-tuple-element.110), channel_id=1, source_target_pairs={{4,0},{5,1},{6,2},{7,3},{12,8},{13,9},{14,10},{15,11},{20,16},{21,... | collective-permute-start | bytes 1572872 | tf_op jit(solution)/shard_map/ppermute | solution.py:25
  77.4 2.0 %collective-permute-start.24 = (bf16[256,512]{1,0:T(8,128)(2,1)S(1)}, bf16[256,512]{1,0:T(8,128)(2,1)S(1)}, u32[]{:S(2)}, u32[]{:S(2)}) collective-permute-start(bf16[256,512]{1,0:T(8,128)(2,1)S(1)} %get-tuple-element.121), channel_id=1, source_target_pairs={{0,16},{8,24},{16,0},{24,8},{1,17},{9,25},{17,1},{25,9},{2,18},{10... | collective-permute-start | bytes 786440 | tf_op jit(solution)/shard_map/ppermute | solution.py:19
  79.4 1.9 %shard_map.169 = (bf16[512,512]{1,0:T(8,128)(2,1)S(1)}, bf16[512,512]{1,0:T(8,128)(2,1)}, f32[512,1]{1,0:T(8,128)S(1)}, bf16[512,512]{1,0:T(8,128)(2,1)S(1)}, bf16[128,128]{1,0:T(8,128)(2,1)}) custom-call(s32[3]{0:T(128)S(1)} %pad_add_fusion.where_ref, bf16[512,512]{1,0:T(8,128)(2,1)S(1)} %collective-permute-done.23.refs_0_, ...), custom_call_target="tpu_custom_call" | custom-call | flops 805306368 | bytes 7639040 | tf_op jit(solution)/shard_map/pallas_call | solution.py:131
  81.3 2.9 %shard_map.171 = (bf16[512,1024]{1,0:T(8,128)(2,1)S(1)}, bf16[128,1024]{1,0:T(8,128)(2,1)S(1)}, bf16[128,1024]{1,0:T(8,128)(2,1)S(1)}, bf16[128,1024]{1,0:T(8,128)(2,1)S(1)}, bf16[128,1024]{1,0:T(8,128)(2,1)S(1)}) custom-call(s32[3]{0:T(128)S(1)} %pad_add_fusion.where_ref, bf16[128,1024]{1,0:T(8,128)(2,1)S(1)} %bitcast.31, ...), custom_call_target="tpu_custom_call" | custom-call | flops 1610612736 | bytes 5767168 | tf_op jit(solution)/shard_map/pallas_call | solution.py:131
  84.2 0.9 collective-permute-start.28
  85.8 2.0 %collective-permute-start.30 = (bf16[128,1024]{1,0:T(8,128)(2,1)S(1)}, bf16[128,1024]{1,0:T(8,128)(2,1)S(1)}, u32[]{:S(2)}, u32[]{:S(2)}) collective-permute-start(bf16[128,1024]{1,0:T(8,128)(2,1)S(1)} %get-tuple-element.143), channel_id=1, source_target_pairs={{0,3},{1,2},{2,1},{3,0},{4,7},{5,6},{6,5},{7,4},{8,11},{9,10},{10,... | collective-permute-start | bytes 786440 | tf_op jit(solution)/shard_map/ppermute | solution.py:19
  87.8 3.2 %shard_map.172 = bf16[1024,1024]{1,0:T(8,128)(2,1)} custom-call(s32[3]{0:T(128)S(1)} %pad_add_fusion.where_ref, bf16[512,1024]{1,0:T(8,128)(2,1)S(1)} %get-tuple-element.129.refs_0_, bf16[512,1024]{1,0:T(8,128)(2,1)S(1)} %bitcast.18), custom_call_target="tpu_custom_call" | custom-call | tf_op jit(solution)/shard_map/pallas_call | solution.py:131
  90.9 3.5 %shard_map.173 = (bf16[128,1024]{1,0:T(8,128)(2,1)}, f32[1,1024]{1,0:T(1,128)}, bf16[1024,128]{1,0:T(8,128)(2,1)}, bf16[128,1024]{1,0:T(8,128)(2,1)}) custom-call(s32[3]{0:T(128)S(1)} %pad_add_fusion.where_ref, bf16[512,512]{1,0:T(8,128)(2,1)S(1)} %get-tuple-element.130.refs_0_.refs_1_, bf16[512,512]{1,0:T(8,128)(2,1)S(1)} %get-tuple-element.130.refs_0_.refs_1_, ...), custom_call_target="tpu_custom_call" | custom-call | tf_op jit(solution)/shard_map/pallas_call | solution.py:131
  94.4 0.9 shard_map.174
  95.3 1.7 %collective-permute-start.25 = (bf16[128,256]{1,0:T(8,128)(2,1)S(1)}, bf16[128,256]{1,0:T(8,128)(2,1)S(1)}, u32[]{:S(2)}, u32[]{:S(2)}) collective-permute-start(bf16[128,256]{1,0:T(8,128)(2,1)S(1)} %get-tuple-element.137), channel_id=1, source_target_pairs={{0,8},{8,0},{16,24},{24,16},{1,9},{9,1},{17,25},{25,17},{2,10},{10... | collective-permute-start | bytes 196616 | tf_op jit(solution)/shard_map/ppermute | solution.py:19
  96.9 1.3 %collective-permute-start.26 = (bf16[128,256]{1,0:T(8,128)(2,1)S(1)}, bf16[128,256]{1,0:T(8,128)(2,1)S(1)}, u32[]{:S(2)}, u32[]{:S(2)}) collective-permute-start(bf16[128,256]{1,0:T(8,128)(2,1)S(1)} %get-tuple-element.138), channel_id=1, source_target_pairs={{0,16},{8,24},{16,0},{24,8},{1,17},{9,25},{17,1},{25,9},{2,18},{10... | collective-permute-start | bytes 196616 | tf_op jit(solution)/shard_map/ppermute | solution.py:19
  98.3 1.3 %collective-permute-done.25.refs_1_ = bf16[128,256]{1,0:T(8,128)(2,1)S(1)} collective-permute-done((bf16[128,256]{1,0:T(8,128)(2,1)S(1)}, bf16[128,256]{1,0:T(8,128)(2,1)S(1)}, u32[]{:S(2)}, u32[]{:S(2)}) %collective-permute-start.25) | collective-permute-done | bytes 65568 | tf_op jit(solution)/shard_map/ppermute | solution.py:19
  99.6 3.1 %collective-permute-start.27 = (bf16[128,256]{1,0:T(8,128)(2,1)S(1)}, bf16[128,256]{1,0:T(8,128)(2,1)S(1)}, u32[]{:S(2)}, u32[]{:S(2)}) collective-permute-start(bf16[128,256]{1,0:T(8,128)(2,1)S(1)} %get-tuple-element.139), channel_id=1, source_target_pairs={{0,24},{8,16},{16,8},{24,0},{1,25},{9,17},{17,9},{25,1},{2,26},{10... | collective-permute-start | bytes 196616 | tf_op jit(solution)/shard_map/ppermute | solution.py:19
  102.7 1.4 %collective-permute-done.26.refs_2_ = bf16[128,256]{1,0:T(8,128)(2,1)S(1)} collective-permute-done((bf16[128,256]{1,0:T(8,128)(2,1)S(1)}, bf16[128,256]{1,0:T(8,128)(2,1)S(1)}, u32[]{:S(2)}, u32[]{:S(2)}) %collective-permute-start.26) | collective-permute-done | bytes 65568 | tf_op jit(solution)/shard_map/ppermute | solution.py:19
  104.1 1.7 %collective-permute-done.27.refs_3_ = bf16[128,256]{1,0:T(8,128)(2,1)S(1)} collective-permute-done((bf16[128,256]{1,0:T(8,128)(2,1)S(1)}, bf16[128,256]{1,0:T(8,128)(2,1)S(1)}, u32[]{:S(2)}, u32[]{:S(2)}) %collective-permute-start.27) | collective-permute-done | bytes 65568 | tf_op jit(solution)/shard_map/ppermute | solution.py:19
  105.8 1.3 %shard_map.175 = bf16[128,1024]{1,0:T(8,128)(2,1)} custom-call(s32[3]{0:T(128)S(1)} %pad_add_fusion.where_ref, bf16[128,256]{1,0:T(8,128)(2,1)S(1)} %get-tuple-element.136.refs_0_, bf16[128,256]{1,0:T(8,128)(2,1)S(1)} %collective-permute-done.25.refs_1_, bf16[128,256]{1,0:T(8,128)(2,1)S(1)} %collective-permute-done.26.refs_2_, ...), custom_call_target="tpu_custom_call" | custom-call | tf_op jit(solution)/shard_map/pallas_call | solution.py:131
  107.1 1.4 %shard_map.176 = bf16[128,1024]{1,0:T(8,128)(2,1)} custom-call(s32[3]{0:T(128)S(1)} %pad_add_fusion.where_ref, bf16[128,1024]{1,0:T(8,128)(2,1)S(1)} %get-tuple-element.140.refs_0_, bf16[128,1024]{1,0:T(8,128)(2,1)S(1)} %collective-permute-done.28.refs_1_, bf16[128,1024]{1,0:T(8,128)(2,1)S(1)} %collective-permute-done.29.refs_2_, ...), custom_call_target="tpu_custom_call" | custom-call | tf_op jit(solution)/shard_map/pallas_call | solution.py:131
  (57 shorter events, 10.8 us)
Async XLA Ops:
  0.6 24.3 %copy-start = (bf16[1,512,1024]{2,1,0:T(8,128)(2,1)S(1)}, bf16[1,512,1024]{2,1,0:T(8,128)(2,1)}, u32[]{:S(2)}) copy-start(bf16[1,512,1024]{2,1,0:T(8,128)(2,1)} %param.11) | copy-start | bytes 3145732
  0.7 17.1 %collective-permute-start.1 = (bf16[128,1024]{1,0:T(8,128)(2,1)}, bf16[128,1024]{1,0:T(8,128)(2,1)S(1)}, u32[]{:S(2)}, u32[]{:S(2)}) collective-permute-start(bf16[128,1024]{1,0:T(8,128)(2,1)} %bitcast.27), channel_id=1, source_target_pairs={{0,8},{8,0},{16,24},{24,16},{1,9},{9,1},{17,25},{25,17},{2,10},{10... | collective-permute-start | bytes 786440 | tf_op jit(solution)/shard_map/ppermute | solution.py:19
  3.7 14.7 %collective-permute-start = (bf16[128,1024]{1,0:T(8,128)(2,1)}, bf16[128,1024]{1,0:T(8,128)(2,1)}, u32[]{:S(2)}, u32[]{:S(2)}) collective-permute-start(bf16[128,1024]{1,0:T(8,128)(2,1)} %bitcast.28), channel_id=1, source_target_pairs={{0,16},{8,24},{16,0},{24,8},{1,17},{9,25},{17,1},{25,9},{2,18},{10... | collective-permute-start | bytes 786440 | tf_op jit(solution)/shard_map/ppermute | solution.py:19
  6.4 1.2 %copy-start.1 = (bf16[1,512,1024]{2,1,0:T(8,128)(2,1)S(1)}, bf16[1,512,1024]{2,1,0:T(8,128)(2,1)}, u32[]{:S(2)}) copy-start(bf16[1,512,1024]{2,1,0:T(8,128)(2,1)} %param.12) | copy-start | bytes 3145732
  7.6 0.9 copy-start.5
  8.6 0.9 copy-start.7
  9.5 0.7 copy-start.10
  10.2 22.6 %copy-start.9 = (bf16[1,128,1024]{2,1,0:T(8,128)(2,1)S(1)}, bf16[1,128,1024]{2,1,0:T(8,128)(2,1)}, u32[]{:S(2)}) copy-start(bf16[1,128,1024]{2,1,0:T(8,128)(2,1)} %param.9) | copy-start | bytes 786436
  13.5 23.3 %collective-permute-start.6 = (bf16[896,256]{1,0:T(8,128)(2,1)}, bf16[896,256]{1,0:T(8,128)(2,1)S(1)}, u32[]{:S(2)}, u32[]{:S(2)}) collective-permute-start(bf16[896,256]{1,0:T(8,128)(2,1)} %get-tuple-element.89), channel_id=1, source_target_pairs={{0,1},{1,0},{2,3},{3,2},{4,5},{5,4},{6,7},{7,6},{8,9},{9,8},{10,11... | collective-permute-start | bytes 1376264 | tf_op jit(solution)/shard_map/ppermute | solution.py:19
  15.0 21.7 %collective-permute-start.7 = (bf16[896,256]{1,0:T(8,128)(2,1)}, bf16[896,256]{1,0:T(8,128)(2,1)S(1)}, u32[]{:S(2)}, u32[]{:S(2)}) collective-permute-start(bf16[896,256]{1,0:T(8,128)(2,1)} %get-tuple-element.90), channel_id=1, source_target_pairs={{0,2},{1,3},{2,0},{3,1},{4,6},{5,7},{6,4},{7,5},{8,10},{9,11},{10,... | collective-permute-start | bytes 1376264 | tf_op jit(solution)/shard_map/ppermute | solution.py:19
  16.5 20.2 %collective-permute-start.8 = (bf16[896,256]{1,0:T(8,128)(2,1)}, bf16[896,256]{1,0:T(8,128)(2,1)S(1)}, u32[]{:S(2)}, u32[]{:S(2)}) collective-permute-start(bf16[896,256]{1,0:T(8,128)(2,1)} %get-tuple-element.91), channel_id=1, source_target_pairs={{0,3},{1,2},{2,1},{3,0},{4,7},{5,6},{6,5},{7,4},{8,11},{9,10},{10,... | collective-permute-start | bytes 1376264 | tf_op jit(solution)/shard_map/ppermute | solution.py:19
  17.8 5.9 %collective-permute-start.11 = (bf16[128,128]{1,0:T(8,128)(2,1)S(1)}, bf16[128,128]{1,0:T(8,128)(2,1)S(1)}, u32[]{:S(2)}, u32[]{:S(2)}) collective-permute-start(bf16[128,128]{1,0:T(8,128)(2,1)S(1)} %broadcast_select_fusion.refs_4_), channel_id=1, source_target_pairs={{0,24},{8,16},{16,8},{24,0},{1,25},{9,17},{17,9},{25,1},{2,26},{10... | collective-permute-start | bytes 98312 | tf_op jit(solution)/shard_map/ppermute | solution.py:19
  18.4 10.3 %collective-permute-start.2 = (bf16[128,1024]{1,0:T(8,128)(2,1)}, bf16[128,1024]{1,0:T(8,128)(2,1)S(1)}, u32[]{:S(2)}, u32[]{:S(2)}) collective-permute-start(bf16[128,1024]{1,0:T(8,128)(2,1)} %bitcast.29), channel_id=1, source_target_pairs={{8,16},{16,8},{9,17},{17,9},{10,18},{18,10},{11,19},{19,11},{12,20... | collective-permute-start | bytes 786440 | tf_op jit(solution)/shard_map/ppermute | solution.py:37
  23.7 9.2 %collective-permute-start.3 = (bf16[128,1024]{1,0:T(8,128)(2,1)}, bf16[128,1024]{1,0:T(8,128)(2,1)S(1)}, u32[]{:S(2)}, u32[]{:S(2)}) collective-permute-start(bf16[128,1024]{1,0:T(8,128)(2,1)} %collective-permute-done.refs_2_), channel_id=1, source_target_pairs={{8,0},{16,24},{9,1},{17,25},{10,2},{18,26},{11,3},{19,27},{12,4},{... | collective-permute-start | bytes 786440 | tf_op jit(solution)/shard_map/ppermute | solution.py:38
  25.0 1.6 %copy-start.3 = (bf16[1,1024,1024]{2,1,0:T(8,128)(2,1)S(1)}, bf16[1,1024,1024]{2,1,0:T(8,128)(2,1)}, u32[]{:S(2)}) copy-start(bf16[1,1024,1024]{2,1,0:T(8,128)(2,1)} %param.10) | copy-start | bytes 6291460
  28.7 6.0 %collective-permute-start.10 = (bf16[128,128]{1,0:T(8,128)(2,1)S(1)}, bf16[128,128]{1,0:T(8,128)(2,1)S(1)}, u32[]{:S(2)}, u32[]{:S(2)}) collective-permute-start(bf16[128,128]{1,0:T(8,128)(2,1)S(1)} %broadcast_select_fusion.refs_4_), channel_id=1, source_target_pairs={{0,16},{8,24},{16,0},{24,8},{1,17},{9,25},{17,1},{25,9},{2,18},{10... | collective-permute-start | bytes 98312 | tf_op jit(solution)/shard_map/ppermute | solution.py:19
  32.8 3.9 %collective-permute-start.9 = (bf16[128,128]{1,0:T(8,128)(2,1)S(1)}, bf16[128,128]{1,0:T(8,128)(2,1)S(1)}, u32[]{:S(2)}, u32[]{:S(2)}) collective-permute-start(bf16[128,128]{1,0:T(8,128)(2,1)S(1)} %broadcast_select_fusion.refs_4_), channel_id=1, source_target_pairs={{0,8},{8,0},{16,24},{24,16},{1,9},{9,1},{17,25},{25,17},{2,10},{10... | collective-permute-start | bytes 98312 | tf_op jit(solution)/shard_map/ppermute | solution.py:19
  36.8 5.9 %collective-permute-start.12 = (bf16[512,128]{1,0:T(8,128)(2,1)S(1)}, bf16[512,128]{1,0:T(8,128)(2,1)S(1)}, u32[]{:S(2)}, u32[]{:S(2)}) collective-permute-start(bf16[512,128]{1,0:T(8,128)(2,1)S(1)} %get-tuple-element.92), channel_id=1, source_target_pairs={{0,3},{1,2},{2,1},{3,0},{4,7},{5,6},{6,5},{7,4},{8,11},{9,10},{10,... | collective-permute-start | bytes 393224 | tf_op jit(solution)/shard_map/ppermute | solution.py:19
  39.3 5.0 %collective-permute-start.4 = (bf16[512,128]{1,0:T(8,128)(2,1)S(1)}, bf16[512,128]{1,0:T(8,128)(2,1)S(1)}, u32[]{:S(2)}, u32[]{:S(2)}) collective-permute-start(bf16[512,128]{1,0:T(8,128)(2,1)S(1)} %get-tuple-element.86), channel_id=1, source_target_pairs={{0,1},{1,0},{2,3},{3,2},{4,5},{5,4},{6,7},{7,6},{8,9},{9,8},{10,11... | collective-permute-start | bytes 393224 | tf_op jit(solution)/shard_map/ppermute | solution.py:19
  39.8 5.0 %collective-permute-start.5 = (bf16[512,128]{1,0:T(8,128)(2,1)S(1)}, bf16[512,128]{1,0:T(8,128)(2,1)S(1)}, u32[]{:S(2)}, u32[]{:S(2)}) collective-permute-start(bf16[512,128]{1,0:T(8,128)(2,1)S(1)} %get-tuple-element.87), channel_id=1, source_target_pairs={{0,2},{1,3},{2,0},{3,1},{4,6},{5,7},{6,4},{7,5},{8,10},{9,11},{10,... | collective-permute-start | bytes 393224 | tf_op jit(solution)/shard_map/ppermute | solution.py:19
  45.4 7.0 %collective-permute-start.13 = (bf16[512,128]{1,0:T(8,128)(2,1)S(1)}, bf16[512,128]{1,0:T(8,128)(2,1)S(1)}, u32[]{:S(2)}, u32[]{:S(2)}) collective-permute-start(bf16[512,128]{1,0:T(8,128)(2,1)S(1)} %shard_map.163.refs_0_), channel_id=1, source_target_pairs={{0,16},{8,24},{16,0},{24,8},{1,17},{9,25},{17,1},{25,9},{2,18},{10... | collective-permute-start | bytes 393224 | tf_op jit(solution)/shard_map/ppermute | solution.py:19
  46.4 12.9 %collective-permute-start.17 = (bf16[1024,128]{1,0:T(8,128)(2,1)S(1)}, bf16[1024,128]{1,0:T(8,128)(2,1)S(1)}, u32[]{:S(2)}, u32[]{:S(2)}) collective-permute-start(bf16[1024,128]{1,0:T(8,128)(2,1)S(1)} %get-tuple-element.97.refs_4_), channel_id=1, source_target_pairs={{0,3},{1,2},{2,1},{3,0},{4,7},{5,6},{6,5},{7,4},{8,11},{9,10},{10,... | collective-permute-start | bytes 786440 | tf_op jit(solution)/shard_map/ppermute | solution.py:19
  48.2 11.1 %collective-permute-start.16 = (bf16[1024,128]{1,0:T(8,128)(2,1)S(1)}, bf16[1024,128]{1,0:T(8,128)(2,1)S(1)}, u32[]{:S(2)}, u32[]{:S(2)}) collective-permute-start(bf16[1024,128]{1,0:T(8,128)(2,1)S(1)} %get-tuple-element.97.refs_4_), channel_id=1, source_target_pairs={{0,2},{1,3},{2,0},{3,1},{4,6},{5,7},{6,4},{7,5},{8,10},{9,11},{10,... | collective-permute-start | bytes 786440 | tf_op jit(solution)/shard_map/ppermute | solution.py:19
  49.4 9.9 %collective-permute-start.15 = (bf16[1024,128]{1,0:T(8,128)(2,1)S(1)}, bf16[1024,128]{1,0:T(8,128)(2,1)S(1)}, u32[]{:S(2)}, u32[]{:S(2)}) collective-permute-start(bf16[1024,128]{1,0:T(8,128)(2,1)S(1)} %get-tuple-element.97.refs_4_), channel_id=1, source_target_pairs={{0,1},{1,0},{2,3},{3,2},{4,5},{5,4},{6,7},{7,6},{8,9},{9,8},{10,11... | collective-permute-start | bytes 786440 | tf_op jit(solution)/shard_map/ppermute | solution.py:19
  53.0 6.3 %collective-permute-start.14 = (bf16[512,128]{1,0:T(8,128)(2,1)S(1)}, bf16[512,128]{1,0:T(8,128)(2,1)S(1)}, u32[]{:S(2)}, u32[]{:S(2)}) collective-permute-start(bf16[512,128]{1,0:T(8,128)(2,1)S(1)} %shard_map.164.refs_0_), channel_id=1, source_target_pairs={{0,8},{8,0},{16,24},{24,16},{1,9},{9,1},{17,25},{25,17},{2,10},{10... | collective-permute-start | bytes 393224 | tf_op jit(solution)/shard_map/ppermute | solution.py:19
  59.9 10.0 %collective-permute-start.18 = (bf16[512,512]{1,0:T(8,128)(2,1)S(1)}, bf16[512,512]{1,0:T(8,128)(2,1)S(1)}, u32[]{:S(2)}, u32[]{:S(2)}) collective-permute-start(bf16[512,512]{1,0:T(8,128)(2,1)S(1)} %get-tuple-element.99), channel_id=1, source_target_pairs={{0,8},{8,0},{16,24},{24,16},{1,9},{9,1},{17,25},{25,17},{2,10},{10... | collective-permute-start | bytes 1572872 | tf_op jit(solution)/shard_map/ppermute | solution.py:19
  60.0 6.0 %collective-permute-start.21 = (bf16[512,128]{1,0:T(8,128)(2,1)S(1)}, bf16[512,128]{1,0:T(8,128)(2,1)S(1)}, u32[]{:S(2)}, u32[]{:S(2)}) collective-permute-start(bf16[512,128]{1,0:T(8,128)(2,1)S(1)} %shard_map.166.refs_0_), channel_id=1, source_target_pairs={{0,3},{1,2},{2,1},{3,0},{4,7},{5,6},{6,5},{7,4},{8,11},{9,10},{10,... | collective-permute-start | bytes 393224 | tf_op jit(solution)/shard_map/ppermute | solution.py:19
  60.7 6.5 %collective-permute-start.20 = (bf16[512,128]{1,0:T(8,128)(2,1)S(1)}, bf16[512,128]{1,0:T(8,128)(2,1)S(1)}, u32[]{:S(2)}, u32[]{:S(2)}) collective-permute-start(bf16[512,128]{1,0:T(8,128)(2,1)S(1)} %shard_map.166.refs_0_), channel_id=1, source_target_pairs={{0,2},{1,3},{2,0},{3,1},{4,6},{5,7},{6,4},{7,5},{8,10},{9,11},{10,... | collective-permute-start | bytes 393224 | tf_op jit(solution)/shard_map/ppermute | solution.py:19
  62.8 5.0 %collective-permute-start.19 = (bf16[512,128]{1,0:T(8,128)(2,1)S(1)}, bf16[512,128]{1,0:T(8,128)(2,1)S(1)}, u32[]{:S(2)}, u32[]{:S(2)}) collective-permute-start(bf16[512,128]{1,0:T(8,128)(2,1)S(1)} %shard_map.166.refs_0_), channel_id=1, source_target_pairs={{0,1},{1,0},{2,3},{3,2},{4,5},{5,4},{6,7},{7,6},{8,9},{9,8},{10,11... | collective-permute-start | bytes 393224 | tf_op jit(solution)/shard_map/ppermute | solution.py:19
  69.9 2.8 %collective-permute-start.22 = (bf16[512,512]{1,0:T(8,128)(2,1)S(1)}, bf16[512,512]{1,0:T(8,128)(2,1)S(1)}, u32[]{:S(2)}, u32[]{:S(2)}) collective-permute-start(bf16[512,512]{1,0:T(8,128)(2,1)S(1)} %get-tuple-element.104), channel_id=1, source_target_pairs={{0,4},{1,5},{2,6},{3,7},{8,12},{9,13},{10,14},{11,15},{16,20},{17,... | collective-permute-start | bytes 1572872 | tf_op jit(solution)/shard_map/ppermute | solution.py:25
  75.2 4.2 %collective-permute-start.23 = (bf16[512,512]{1,0:T(8,128)(2,1)S(1)}, bf16[512,512]{1,0:T(8,128)(2,1)S(1)}, u32[]{:S(2)}, u32[]{:S(2)}) collective-permute-start(bf16[512,512]{1,0:T(8,128)(2,1)S(1)} %get-tuple-element.110), channel_id=1, source_target_pairs={{4,0},{5,1},{6,2},{7,3},{12,8},{13,9},{14,10},{15,11},{20,16},{21,... | collective-permute-start | bytes 1572872 | tf_op jit(solution)/shard_map/ppermute | solution.py:25
  77.4 17.0 %collective-permute-start.24 = (bf16[256,512]{1,0:T(8,128)(2,1)S(1)}, bf16[256,512]{1,0:T(8,128)(2,1)S(1)}, u32[]{:S(2)}, u32[]{:S(2)}) collective-permute-start(bf16[256,512]{1,0:T(8,128)(2,1)S(1)} %get-tuple-element.121), channel_id=1, source_target_pairs={{0,16},{8,24},{16,0},{24,8},{1,17},{9,25},{17,1},{25,9},{2,18},{10... | collective-permute-start | bytes 786440 | tf_op jit(solution)/shard_map/ppermute | solution.py:19
  79.4 1.9 %copy-start.4 = (bf16[1,1024,1024]{2,1,0:T(8,128)(2,1)S(1)}, bf16[1,1024,1024]{2,1,0:T(8,128)(2,1)}, u32[]{:S(2)}) copy-start(bf16[1,1024,1024]{2,1,0:T(8,128)(2,1)} %param.10) | copy-start | bytes 6291460
  84.2 6.8 %copy-start.2 = (bf16[1,512,1024]{2,1,0:T(8,128)(2,1)S(1)}, bf16[1,512,1024]{2,1,0:T(8,128)(2,1)}, u32[]{:S(2)}) copy-start(bf16[1,512,1024]{2,1,0:T(8,128)(2,1)} %param.12) | copy-start | bytes 3145732
  84.2 6.8 %copy-start.6 = (bf16[1,128,1024]{2,1,0:T(8,128)(2,1)S(1)}, bf16[1,128,1024]{2,1,0:T(8,128)(2,1)}, u32[]{:S(2)}) copy-start(bf16[1,128,1024]{2,1,0:T(8,128)(2,1)} %param.15) | copy-start | bytes 786436
  84.2 6.7 %copy-start.8 = (bf16[1,1024,128]{2,1,0:T(8,128)(2,1)S(1)}, bf16[1,1024,128]{2,1,0:T(8,128)(2,1)}, u32[]{:S(2)}) copy-start(bf16[1,1024,128]{2,1,0:T(8,128)(2,1)} %param.14) | copy-start | bytes 786436
  84.2 6.7 %copy-start.11 = (f32[1,1024]{1,0:T(1,128)S(1)}, f32[1,1024]{1,0:T(1,128)}, u32[]{:S(2)}) copy-start(f32[1,1024]{1,0:T(1,128)} %refs_9_.1) | copy-start | bytes 12292
  84.2 22.9 %collective-permute-start.28 = (bf16[128,1024]{1,0:T(8,128)(2,1)S(1)}, bf16[128,1024]{1,0:T(8,128)(2,1)S(1)}, u32[]{:S(2)}, u32[]{:S(2)}) collective-permute-start(bf16[128,1024]{1,0:T(8,128)(2,1)S(1)} %get-tuple-element.141), channel_id=1, source_target_pairs={{0,1},{1,0},{2,3},{3,2},{4,5},{5,4},{6,7},{7,6},{8,9},{9,8},{10,11... | collective-permute-start | bytes 786440 | tf_op jit(solution)/shard_map/ppermute | solution.py:19
  85.1 21.9 %collective-permute-start.29 = (bf16[128,1024]{1,0:T(8,128)(2,1)S(1)}, bf16[128,1024]{1,0:T(8,128)(2,1)S(1)}, u32[]{:S(2)}, u32[]{:S(2)}) collective-permute-start(bf16[128,1024]{1,0:T(8,128)(2,1)S(1)} %get-tuple-element.142), channel_id=1, source_target_pairs={{0,2},{1,3},{2,0},{3,1},{4,6},{5,7},{6,4},{7,5},{8,10},{9,11},{10,... | collective-permute-start | bytes 786440 | tf_op jit(solution)/shard_map/ppermute | solution.py:19
  85.8 21.3 %collective-permute-start.30 = (bf16[128,1024]{1,0:T(8,128)(2,1)S(1)}, bf16[128,1024]{1,0:T(8,128)(2,1)S(1)}, u32[]{:S(2)}, u32[]{:S(2)}) collective-permute-start(bf16[128,1024]{1,0:T(8,128)(2,1)S(1)} %get-tuple-element.143), channel_id=1, source_target_pairs={{0,3},{1,2},{2,1},{3,0},{4,7},{5,6},{6,5},{7,4},{8,11},{9,10},{10,... | collective-permute-start | bytes 786440 | tf_op jit(solution)/shard_map/ppermute | solution.py:19
  95.3 4.3 %collective-permute-start.25 = (bf16[128,256]{1,0:T(8,128)(2,1)S(1)}, bf16[128,256]{1,0:T(8,128)(2,1)S(1)}, u32[]{:S(2)}, u32[]{:S(2)}) collective-permute-start(bf16[128,256]{1,0:T(8,128)(2,1)S(1)} %get-tuple-element.137), channel_id=1, source_target_pairs={{0,8},{8,0},{16,24},{24,16},{1,9},{9,1},{17,25},{25,17},{2,10},{10... | collective-permute-start | bytes 196616 | tf_op jit(solution)/shard_map/ppermute | solution.py:19
  96.9 7.2 %collective-permute-start.26 = (bf16[128,256]{1,0:T(8,128)(2,1)S(1)}, bf16[128,256]{1,0:T(8,128)(2,1)S(1)}, u32[]{:S(2)}, u32[]{:S(2)}) collective-permute-start(bf16[128,256]{1,0:T(8,128)(2,1)S(1)} %get-tuple-element.138), channel_id=1, source_target_pairs={{0,16},{8,24},{16,0},{24,8},{1,17},{9,25},{17,1},{25,9},{2,18},{10... | collective-permute-start | bytes 196616 | tf_op jit(solution)/shard_map/ppermute | solution.py:19
  99.6 6.2 %collective-permute-start.27 = (bf16[128,256]{1,0:T(8,128)(2,1)S(1)}, bf16[128,256]{1,0:T(8,128)(2,1)S(1)}, u32[]{:S(2)}, u32[]{:S(2)}) collective-permute-start(bf16[128,256]{1,0:T(8,128)(2,1)S(1)} %get-tuple-element.139), channel_id=1, source_target_pairs={{0,24},{8,16},{16,8},{24,0},{1,25},{9,17},{17,9},{25,1},{2,26},{10... | collective-permute-start | bytes 196616 | tf_op jit(solution)/shard_map/ppermute | solution.py:19

commit v10 on v9

--- a/solution.py
+++ b/solution.py
@@ -29,14 +29,16 @@
     return [shard] + [swap(shard, axis, k) for k in range(1, lax.axis_size(axis))]
 
 
-def line_gathered(shard, axis):
+def line_gathered(shard, small, axis):
     if lax.axis_size(axis) != 4:
-        return gathered(shard, axis), []
+        return gathered(shard, axis), [], gathered(small, axis)
     far, near = swap(shard, axis, 2), swap(shard, axis, 1)
-    shard, far, near = lax.optimization_barrier((shard, far, near))
+    beside = swap(small, axis, 1)
+    shard, far, near, beside = lax.optimization_barrier((shard, far, near, beside))
     across = lax.ppermute(shard, axis, [(1, 2), (2, 1)])
     passed = lax.ppermute(far, axis, [(1, 0), (2, 3)])
-    return [shard, near, far], [across, passed]
+    others = swap(jnp.concatenate([small, beside]), axis, 2)
+    return [shard, near, far], [across, passed], [small, beside, others]
 
 
 def scattered(blocks, axis):
@@ -56,25 +58,13 @@
     return rows
 
 
-def halved_sum(kept, given, after, axis, size, where):
-    count = kept.shape[0] // size
-    step = 1
-    while True:
-        other = swap(given, axis, step)
-        if step == 1:
-            other, after = lax.optimization_barrier((other, after))
-        if count == 1:
-            return [kept, other], after
-        half = like((count // 2 * size, kept.shape[1]))
-        kept, given = run(
-            functools.partial(halved_kernel, size), [half, half], where, [(kept, other)]
-        )
-        step *= 2
-        count //= 2
-
-
-def total(blocks, where):
-    return run(total_kernel, [like(blocks[0].shape)], where, [blocks])[0]
+def halved(mine, other, size, where):
+    half = like((mine.shape[0] // 2, mine.shape[1]))
+    return run(functools.partial(halved_kernel, size), [half, half], where, [(mine, other)])
+
+
+def total(blocks, where, flops=0):
+    return run(total_kernel, [like(blocks[0].shape)], where, [blocks], flops=flops)[0]
 
 
 def ordered(blocks, axis):
@@ -126,6 +116,8 @@
             at += count
         kernel(where_ref, ins, outs, refs[:own])
 
+    if fetch:
+        flat = [pltpu.with_memory_space_constraint(array, pltpu.HBM) for array in flat]
     size = sum(a.size * a.dtype.itemsize for a in list(flat) + list(results))
     limit = (10 << 20) if size < (10 << 20) else size + (12 << 20)
     return pl.pallas_call(
@@ -380,12 +372,9 @@
 
 
 def heads_kernel(where, ins, outs, scratch):
-    (code_grad,), terms = ins
+    ((code_grad, fold_rows),) = ins
     tokens = outs[0].shape[0]
-    fold_rows = terms[0][...].astype(f32)
-    for term in terms[1:]:
-        fold_rows = fold_rows + term[...].astype(f32)
-    whole = dot(code_grad[...], fold_rows.astype(bf16), NT)
+    whole = dot(code_grad[...], fold_rows[...], NT)
     for k, out in enumerate(outs):
         out[...] = whole[k * tokens : (k + 1) * tokens, :].astype(bf16)
 
@@ -400,7 +389,7 @@
 
 def head_kernel(where, ins, outs, scratch):
     heads, (code_grad, proj) = ins
-    head_sum, enc_blocks = outs[0], outs[1:]
+    enc_blocks = outs
     (whole,) = scratch
     tokens = heads[0].shape[0]
     together = 4 if len(heads) % 4 == 0 else 1
@@ -410,17 +399,24 @@
         values = jnp.concatenate([h[...] for h in heads[first : first + together]])
         term = dot(code_grad[rows, :], values, TN)
         sums = term if sums is None else sums + term
-    head_sum[...] = sums.astype(bf16)
-    whole[...] = dot(head_sum[...], proj[...], NN)
+    whole[...] = dot(sums.astype(bf16), proj[...], NN)
     size = enc_blocks[0].shape[0]
     for k, out in enumerate(enc_blocks):
         at = (where[0] ^ k) * size
         out[...] = whole[pl.ds(pl.multiple_of(at, size), size), :].astype(bf16)
 
 
+def turn_kernel(where, ins, outs, scratch):
+    (heads,) = ins
+    tokens = heads[0].shape[0]
+    for k, part in enumerate(heads):
+        outs[0][:, k * tokens : (k + 1) * tokens] = part[...].T
+
+
 def proj_kernel(where, ins, outs, scratch):
-    ((head_sum, enc),) = ins
-    outs[0][...] = dot(head_sum[...], enc[...], TN).astype(bf16)
+    ((turned, code_grad, enc),) = ins
+    head_sum = dot(turned[...], code_grad[...], NN).astype(bf16)
+    outs[0][...] = dot(head_sum, enc[...], NN).astype(bf16)
 
 
 def feature_kernel(where, ins, outs, scratch):
@@ -483,9 +479,8 @@
     head_cols, model_cols = proj.shape
     where = jnp.stack([lax.axis_index("tensor"), lax.axis_index("dp"), section]).astype(jnp.int32)
 
-    heads, pair = line_gathered(heads_out[0], "dp")
     end = jnp.where(section == 0, input_code, code_cotangent)
-    ends = gathered(end, "dp")
+    heads, pair, ends = line_gathered(heads_out[0], end, "dp")
     packs = run(
         gram_kernel,
         [like((cols * codes // (2 * relay) + codes + relay, 2 * relay))] * parts,
@@ -515,7 +510,11 @@
     )
     partials, heads = list(partials[:parts]), [*heads, *partials[parts:]]
     partials[-1], *_ = lax.optimization_barrier((partials[-1], *packs, *ends))
+    fold_given, partials = lax.optimization_barrier((fold_given, partials))
+    fold_other = swap(fold_given, "dp", 1)
     code_block = total(scattered(partials, "tensor"), where)
+    code_block, fold_other = lax.optimization_barrier((code_block, fold_other))
+    fold_terms = halved(fold_kept, fold_other, head_cols // groups, where)
     wide = parts * relay
     packs, _ = lax.optimization_barrier((packs, code_block))
     payload, products, weights = run(
@@ -529,8 +528,9 @@
         [packs, ends],
     )
     payloads = gathered(payload, "tensor")
-    mix_block = group_sum(code_block, payloads, "dp", where)
-    fold_given, mix_block = lax.optimization_barrier((fold_given, mix_block))
+    (turned,) = run(turn_kernel, [like((head_cols, rows))], where, [heads])
+    mix_block = group_sum(code_block, [*payloads, *fold_terms, turned], "dp", where)
+    mix_block, fold_terms = lax.optimization_barrier((mix_block, fold_terms))
     mix_blocks = gathered(mix_block, "tensor")
 
     square_flops = 2 * rows * codes * codes
@@ -550,9 +550,15 @@
         scratch=[pltpu.VMEM((codes, codes), bf16)],
         flops=3 * square_flops,
     )
-    fold_terms, sent = halved_sum(
-        fold_kept, fold_given, sent, "dp", head_cols // groups, where
-    )
+    step = 2
+    while step < groups:
+        kept, given = fold_terms
+        other = swap(given, "dp", step)
+        step *= 2
+        if step < groups:
+            fold_terms = halved(kept, other, head_cols // groups, where)
+        else:
+            fold_rows = total([kept, other], where, flops=1 << 33)
     received = ends
     for turn in range(1, sections):
         last = turn == sections - 1
@@ -561,6 +567,8 @@
             shapes += [like((rows, wide), f32)] * 2 + [like((rows, 1), f32), like((rows, wide))]
             shapes += [like((tokens, relay))]
         moved = move(sent, "pipe", 1)
+        if turn == 1:
+            moved, fold_rows = lax.optimization_barrier((moved, fold_rows))
         results = run(
             functools.partial(forward_kernel, width, turn, last),
             shapes,
@@ -600,17 +608,29 @@
         incoming, returned = results[:2]
     inner, code_grad, returned = results[2:]
 
-    head_sum, *enc_blocks = run(
+    enc_blocks = run(
         head_kernel,
-        [like((codes, head_cols))] + [like((cols, model_cols))] * parts,
+        [like((cols, model_cols))] * parts,
         where,
         [heads, (code_grad, proj)],
         scratch=[pltpu.VMEM((codes, model_cols), f32)],
         flops=2 * head_cols * codes * (rows + model_cols),
     )
-    head_sum, mix, *enc_blocks = lax.optimization_barrier((head_sum, mix, *enc_blocks))
-    enc_grad = total(scattered(enc_blocks, "tensor"), where)
-    (proj_grad,) = run(proj_kernel, [like((head_cols, model_cols))], where, [(head_sum, enc)])
+    code_grad, mix, turned, enc_blocks = lax.optimization_barrier(
+        (code_grad, mix, turned, enc_blocks)
+    )
+    enc_blocks = scattered(enc_blocks, "tensor")
+    head_blocks = run(
+        heads_kernel,
+        [like((tokens, head_cols // groups))] * groups,
+        where,
+        [(code_grad, fold_rows)],
+    )
+    *head_blocks, mix, turned = lax.optimization_barrier((*head_blocks, mix, turned))
+    head_blocks = scattered(head_blocks, "dp")
+    (proj_grad,) = run(
+        proj_kernel, [like((head_cols, model_cols))], where, [(turned, code_grad, enc)]
+    )
     shapes = [(codes // groups, features), (1, features), (features, relay), (relay, features)]
     dec_grad, gain_grad, send_grad, recv_grad = run(
         feature_kernel,
@@ -632,14 +652,7 @@
         ],
         scratch=[pltpu.VMEM(shape, f32) for shape in shapes],
     )
-    fold_terms, _, _ = lax.optimization_barrier((fold_terms, proj_grad, dec_grad))
-    head_blocks = run(
-        heads_kernel,
-        [like((tokens, head_cols // groups))] * groups,
-        where,
-        [(code_grad,), fold_terms],
-    )
-    head_blocks = scattered(head_blocks, "dp")
+    enc_grad = total(enc_blocks, where)
     if head_cols // groups % 128 == 0:
         (heads_grad,) = run(laid_kernel, [like((tokens, head_cols))], where, [head_blocks])
     else:

time: 109 us -> 108 us (level)
  starting transfers between devices: 38.9 us -> 48.1 us
  waiting for transfers between devices: 32.4 us -> 24.6 us
  local copies, waits for them, and re-layouts: 5.43 us -> 0.04 us
  Pallas kernels: 30 us -> 32.9 us
    ppermute x27 -> x26, starting transfers between devices: 34.2 us -> 43.3 us  [swap(): lax.ppermute(shard, axis, [(i, i ^ by) for i in range(lax.axis_size(axis))])]
    ppermute x27 -> x26, waiting for transfers between devices: 28.6 us -> 21.4 us  [swap(): lax.ppermute(shard, axis, [(i, i ^ by) for i in range(lax.axis_size(axis))])]
    unnamed x24 -> x14, local copies, waits for them, and re-layouts: 5.43 us -> 0.04 us
    pallas_call x17 -> x19, Pallas kernels: 30 us -> 32.9 us  [run(): pl.pallas_call(body, out_shape=[jax.ShapeDtypeStruct(r.shape, r.dtype) fo...]
    ppermute x1, waiting for transfers between devices: 2.32 us -> 0.01 us  [line_gathered(): passed = lax.ppermute(far, axis, [(1, 0), (2, 3)])]
    ppermute x2, waiting for transfers between devices: 1.49 us -> 3.19 us  [move(): return lax.ppermute(shard, axis, pairs)]
  transfers between devices with their start and end apart: 31 -> 30, of which waited for: 15 -> 13; matrix products, arithmetic and copies ran while one was open for 1% -> 1% of each run, Pallas kernels for 23% -> 22%
where the time goes in v10:
time: 108 us; the launch traced here: 107 us
  starting transfers between devices  48.1 us (45%)
  Pallas kernels  32.9 us (30%)
  waiting for transfers between devices  24.6 us (23%)
    ppermute x26, starting transfers between devices, swap(): lax.ppermute(shard, axis, [(i, i ^ by) for i in range(lax.axis_size(axis))])  43.3 us
    pallas_call x19, Pallas kernels, run(): pl.pallas_call(body, out_shape=[jax.ShapeDtypeStruct(r.shape, r.dtype) fo...  32.9 us
    ppermute x26, waiting for transfers between devices, swap(): lax.ppermute(shard, axis, [(i, i ^ by) for i in range(lax.axis_size(axis))])  21.4 us
    ppermute x2, waiting for transfers between devices, move(): return lax.ppermute(shard, axis, pairs)  3.19 us
    ppermute x2, starting transfers between devices, move(): return lax.ppermute(shard, axis, pairs)  2.78 us
  transfers between devices with their start and end apart: 30, of which 13 were waited for; matrix products, arithmetic and copies ran while one was open for 1% of the time, Pallas kernels for 22%

profile of v10, /device:TPU:0, one launch (start us, length us, event | category | flops | bytes accessed | tf_op | source)
XLA Modules:
  0.0 107.3 jit_solution(11739704139782849933)
XLA Ops:
  0.6 3.1 %collective-permute-start.1 = (bf16[128,1024]{1,0:T(8,128)(2,1)}, bf16[128,1024]{1,0:T(8,128)(2,1)S(1)}, u32[]{:S(2)}, u32[]{:S(2)}) collective-permute-start(bf16[128,1024]{1,0:T(8,128)(2,1)} %bitcast.23), channel_id=1, source_target_pairs={{0,8},{8,0},{16,24},{24,16},{1,9},{9,1},{17,25},{25,17},{2,10},{10... | collective-permute-start | bytes 786440 | tf_op jit(solution)/shard_map/ppermute | solution.py:19
  3.7 2.6 %collective-permute-start = (bf16[128,1024]{1,0:T(8,128)(2,1)}, bf16[128,1024]{1,0:T(8,128)(2,1)S(1)}, u32[]{:S(2)}, u32[]{:S(2)}) collective-permute-start(bf16[128,1024]{1,0:T(8,128)(2,1)} %bitcast.24), channel_id=1, source_target_pairs={{0,16},{8,24},{16,0},{24,8},{1,17},{9,25},{17,1},{25,9},{2,18},{10... | collective-permute-start | bytes 786440 | tf_op jit(solution)/shard_map/ppermute | solution.py:19
  6.3 0.8 broadcast_select_fusion.refs_4_
  7.6 3.4 %shard_map.161 = (bf16[896,256]{1,0:T(8,128)(2,1)S(1)}, bf16[896,256]{1,0:T(8,128)(2,1)S(1)}, bf16[896,256]{1,0:T(8,128)(2,1)S(1)}, bf16[896,256]{1,0:T(8,128)(2,1)S(1)}) custom-call(s32[3]{0:T(128)S(1)} %pad_add_fusion.where_ref, bf16[512,1024]{1,0:T(8,128)(2,1)} %bitcast.19, bf16[128,1024]{1,0:T(8,128)(2,1)} %bitcast.29, bf16[1024,128]{1,0:T(8,128)(2,1)} %bitcast.31, ...), custom_call_target="tpu_custom_call" | custom-call | tf_op jit(solution)/shard_map/pallas_call | solution.py:123
  11.0 1.6 %collective-permute-start.5 = (bf16[896,256]{1,0:T(8,128)(2,1)S(1)}, bf16[896,256]{1,0:T(8,128)(2,1)S(1)}, u32[]{:S(2)}, u32[]{:S(2)}) collective-permute-start(bf16[896,256]{1,0:T(8,128)(2,1)S(1)} %get-tuple-element.102), channel_id=1, source_target_pairs={{0,1},{1,0},{2,3},{3,2},{4,5},{5,4},{6,7},{7,6},{8,9},{9,8},{10,11... | collective-permute-start | bytes 1376264 | tf_op jit(solution)/shard_map/ppermute | solution.py:19
  12.5 1.5 %collective-permute-start.6 = (bf16[896,256]{1,0:T(8,128)(2,1)S(1)}, bf16[896,256]{1,0:T(8,128)(2,1)S(1)}, u32[]{:S(2)}, u32[]{:S(2)}) collective-permute-start(bf16[896,256]{1,0:T(8,128)(2,1)S(1)} %get-tuple-element.103), channel_id=1, source_target_pairs={{0,2},{1,3},{2,0},{3,1},{4,6},{5,7},{6,4},{7,5},{8,10},{9,11},{10,... | collective-permute-start | bytes 1376264 | tf_op jit(solution)/shard_map/ppermute | solution.py:19
  14.1 2.4 %collective-permute-done.2.refs_5_ = bf16[128,128]{1,0:T(8,128)(2,1)S(1)} collective-permute-done((bf16[128,128]{1,0:T(8,128)(2,1)S(1)}, bf16[128,128]{1,0:T(8,128)(2,1)S(1)}, u32[]{:S(2)}, u32[]{:S(2)}) %collective-permute-start.2) | collective-permute-done | bytes 32800 | tf_op jit(solution)/shard_map/ppermute | solution.py:19
  16.4 2.6 %collective-permute-start.7 = (bf16[896,256]{1,0:T(8,128)(2,1)S(1)}, bf16[896,256]{1,0:T(8,128)(2,1)S(1)}, u32[]{:S(2)}, u32[]{:S(2)}) collective-permute-start(bf16[896,256]{1,0:T(8,128)(2,1)S(1)} %get-tuple-element.104), channel_id=1, source_target_pairs={{0,3},{1,2},{2,1},{3,0},{4,7},{5,6},{6,5},{7,4},{8,11},{9,10},{10,... | collective-permute-start | bytes 1376264 | tf_op jit(solution)/shard_map/ppermute | solution.py:19
  19.1 0.7 collective-permute-start.3
  19.7 1.3 %collective-permute-start.4 = (bf16[128,1024]{1,0:T(8,128)(2,1)S(1)}, bf16[128,1024]{1,0:T(8,128)(2,1)S(1)}, u32[]{:S(2)}, u32[]{:S(2)}) collective-permute-start(bf16[128,1024]{1,0:T(8,128)(2,1)S(1)} %collective-permute-done.refs_2_), channel_id=1, source_target_pairs={{8,0},{16,24},{9,1},{17,25},{10,2},{18,26},{11,3},{19,27},{12,4},{... | collective-permute-start | bytes 786440 | tf_op jit(solution)/shard_map/ppermute | solution.py:39
  21.1 10.5 %collective-permute-start.8 = (bf16[256,128]{1,0:T(8,128)(2,1)S(1)}, bf16[256,128]{1,0:T(8,128)(2,1)S(1)}, u32[]{:S(2)}, u32[]{:S(2)}) collective-permute-start(bf16[256,128]{1,0:T(8,128)(2,1)S(1)} %pad_maximum_fusion), channel_id=1, source_target_pairs={{0,16},{8,24},{16,0},{24,8},{1,17},{9,25},{17,1},{25,9},{2,18},{10... | collective-permute-start | bytes 196616 | tf_op jit(solution)/shard_map/ppermute | solution.py:19
  31.5 3.8 %shard_map.160 = (bf16[1024,512]{1,0:T(8,128)(2,1)S(1)}, bf16[512,512]{1,0:T(8,128)(2,1)S(1)}, bf16[512,512]{1,0:T(8,128)(2,1)S(1)}) custom-call(s32[3]{0:T(128)S(1)} %pad_add_fusion.where_ref, bf16[1024,1024]{1,0:T(8,128)(2,1)} %bitcast.21, bf16[512,1024]{1,0:T(8,128)(2,1)} %bitcast.17), custom_call_target="tpu_custom_call" | custom-call | tf_op jit(solution)/shard_map/pallas_call | solution.py:123
  35.3 1.4 %shard_map.162 = (bf16[512,128]{1,0:T(8,128)(2,1)S(1)}, bf16[512,128]{1,0:T(8,128)(2,1)S(1)}, bf16[512,128]{1,0:T(8,128)(2,1)S(1)}, bf16[512,128]{1,0:T(8,128)(2,1)S(1)}, bf16[128,1024]{1,0:T(8,128)(2,1)S(1)}) custom-call(s32[3]{0:T(128)S(1)} %pad_add_fusion.where_ref, bf16[128,1024]{1,0:T(8,128)(2,1)S(1)} %bitcast.26, ...), custom_call_target="tpu_custom_call" | custom-call | flops 536870912 | bytes 3145728 | tf_op jit(solution)/shard_map/pallas_call | solution.py:123
  37.9 2.4 %collective-permute-start.11 = (bf16[512,128]{1,0:T(8,128)(2,1)S(1)}, bf16[512,128]{1,0:T(8,128)(2,1)S(1)}, u32[]{:S(2)}, u32[]{:S(2)}) collective-permute-start(bf16[512,128]{1,0:T(8,128)(2,1)S(1)} %get-tuple-element.110), channel_id=1, source_target_pairs={{0,3},{1,2},{2,1},{3,0},{4,7},{5,6},{6,5},{7,4},{8,11},{9,10},{10,... | collective-permute-start | bytes 393224 | tf_op jit(solution)/shard_map/ppermute | solution.py:19
  40.4 1.5 %collective-permute-done.9.refs_1_ = bf16[512,128]{1,0:T(8,128)(2,1)S(1)} collective-permute-done((bf16[512,128]{1,0:T(8,128)(2,1)S(1)}, bf16[512,128]{1,0:T(8,128)(2,1)S(1)}, u32[]{:S(2)}, u32[]{:S(2)}) %collective-permute-start.9) | collective-permute-done | bytes 131104 | tf_op jit(solution)/shard_map/ppermute | solution.py:19
  42.4 1.4 %collective-permute-done.11.refs_3_ = bf16[512,128]{1,0:T(8,128)(2,1)S(1)} collective-permute-done((bf16[512,128]{1,0:T(8,128)(2,1)S(1)}, bf16[512,128]{1,0:T(8,128)(2,1)S(1)}, u32[]{:S(2)}, u32[]{:S(2)}) %collective-permute-start.11) | collective-permute-done | bytes 131104 | tf_op jit(solution)/shard_map/ppermute | solution.py:19
  44.4 3.5 %collective-permute-done.12.refs_1_ = bf16[512,512]{1,0:T(8,128)(2,1)S(1)} collective-permute-done((bf16[512,512]{1,0:T(8,128)(2,1)S(1)}, bf16[512,512]{1,0:T(8,128)(2,1)S(1)}, u32[]{:S(2)}, u32[]{:S(2)}) %collective-permute-start.12) | collective-permute-done | bytes 524320 | tf_op jit(solution)/shard_map/ppermute | solution.py:19
  48.0 0.9 shard_map.165
  49.4 1.6 %collective-permute-start.16 = (bf16[1024,128]{1,0:T(8,128)(2,1)S(1)}, bf16[1024,128]{1,0:T(8,128)(2,1)S(1)}, u32[]{:S(2)}, u32[]{:S(2)}) collective-permute-start(bf16[1024,128]{1,0:T(8,128)(2,1)S(1)} %get-tuple-element.117.refs_4_), channel_id=1, source_target_pairs={{0,2},{1,3},{2,0},{3,1},{4,6},{5,7},{6,4},{7,5},{8,10},{9,11},{10,... | collective-permute-start | bytes 786440 | tf_op jit(solution)/shard_map/ppermute | solution.py:19
  51.0 1.5 %collective-permute-start.15 = (bf16[1024,128]{1,0:T(8,128)(2,1)S(1)}, bf16[1024,128]{1,0:T(8,128)(2,1)S(1)}, u32[]{:S(2)}, u32[]{:S(2)}) collective-permute-start(bf16[1024,128]{1,0:T(8,128)(2,1)S(1)} %get-tuple-element.117.refs_4_), channel_id=1, source_target_pairs={{0,1},{1,0},{2,3},{3,2},{4,5},{5,4},{6,7},{7,6},{8,9},{9,8},{10,11... | collective-permute-start | bytes 786440 | tf_op jit(solution)/shard_map/ppermute | solution.py:19
  52.5 2.2 %collective-permute-done.13.refs_1_ = bf16[512,128]{1,0:T(8,128)(2,1)S(1)} collective-permute-done((bf16[512,128]{1,0:T(8,128)(2,1)S(1)}, bf16[512,128]{1,0:T(8,128)(2,1)S(1)}, u32[]{:S(2)}, u32[]{:S(2)}) %collective-permute-start.13) | collective-permute-done | bytes 131104 | tf_op jit(solution)/shard_map/ppermute | solution.py:19
  55.3 1.4 %collective-permute-start.14 = (bf16[512,128]{1,0:T(8,128)(2,1)S(1)}, bf16[512,128]{1,0:T(8,128)(2,1)S(1)}, u32[]{:S(2)}, u32[]{:S(2)}) collective-permute-start(bf16[512,128]{1,0:T(8,128)(2,1)S(1)} %shard_map.164.refs_0_), channel_id=1, source_target_pairs={{0,8},{8,0},{16,24},{24,16},{1,9},{9,1},{17,25},{25,17},{2,10},{10... | collective-permute-start | bytes 393224 | tf_op jit(solution)/shard_map/ppermute | solution.py:19
  56.7 0.9 shard_map.167.refs_0_
  58.2 3.3 %collective-permute-done.14.refs_1_ = bf16[512,128]{1,0:T(8,128)(2,1)S(1)} collective-permute-done((bf16[512,128]{1,0:T(8,128)(2,1)S(1)}, bf16[512,128]{1,0:T(8,128)(2,1)S(1)}, u32[]{:S(2)}, u32[]{:S(2)}) %collective-permute-start.14) | collective-permute-done | bytes 131104 | tf_op jit(solution)/shard_map/ppermute | solution.py:19
  62.2 1.6 %collective-permute-start.20 = (bf16[512,128]{1,0:T(8,128)(2,1)S(1)}, bf16[512,128]{1,0:T(8,128)(2,1)S(1)}, u32[]{:S(2)}, u32[]{:S(2)}) collective-permute-start(bf16[512,128]{1,0:T(8,128)(2,1)S(1)} %shard_map.168.refs_0_), channel_id=1, source_target_pairs={{0,3},{1,2},{2,1},{3,0},{4,7},{5,6},{6,5},{7,4},{8,11},{9,10},{10,... | collective-permute-start | bytes 393224 | tf_op jit(solution)/shard_map/ppermute | solution.py:19
  63.8 2.1 %collective-permute-start.19 = (bf16[512,128]{1,0:T(8,128)(2,1)S(1)}, bf16[512,128]{1,0:T(8,128)(2,1)S(1)}, u32[]{:S(2)}, u32[]{:S(2)}) collective-permute-start(bf16[512,128]{1,0:T(8,128)(2,1)S(1)} %shard_map.168.refs_0_), channel_id=1, source_target_pairs={{0,2},{1,3},{2,0},{3,1},{4,6},{5,7},{6,4},{7,5},{8,10},{9,11},{10,... | collective-permute-start | bytes 393224 | tf_op jit(solution)/shard_map/ppermute | solution.py:19
  65.9 2.3 %collective-permute-done.20.refs_3_ = bf16[512,128]{1,0:T(8,128)(2,1)S(1)} collective-permute-done((bf16[512,128]{1,0:T(8,128)(2,1)S(1)}, bf16[512,128]{1,0:T(8,128)(2,1)S(1)}, u32[]{:S(2)}, u32[]{:S(2)}) %collective-permute-start.20) | collective-permute-done | bytes 131104 | tf_op jit(solution)/shard_map/ppermute | solution.py:19
  68.2 1.3 %collective-permute-done.19.refs_2_ = bf16[512,128]{1,0:T(8,128)(2,1)S(1)} collective-permute-done((bf16[512,128]{1,0:T(8,128)(2,1)S(1)}, bf16[512,128]{1,0:T(8,128)(2,1)S(1)}, u32[]{:S(2)}, u32[]{:S(2)}) %collective-permute-start.19) | collective-permute-done | bytes 131104 | tf_op jit(solution)/shard_map/ppermute | solution.py:19
  69.5 1.3 %collective-permute-done.18.refs_1_ = bf16[512,128]{1,0:T(8,128)(2,1)S(1)} collective-permute-done((bf16[512,128]{1,0:T(8,128)(2,1)S(1)}, bf16[512,128]{1,0:T(8,128)(2,1)S(1)}, u32[]{:S(2)}, u32[]{:S(2)}) %collective-permute-start.18) | collective-permute-done | bytes 131104 | tf_op jit(solution)/shard_map/ppermute | solution.py:19
  70.8 2.1 %shard_map.169 = (bf16[512,512]{1,0:T(8,128)(2,1)S(1)}, bf16[512,512]{1,0:T(8,128)(2,1)S(1)}, f32[512,512]{1,0:T(8,128)S(1)}, f32[512,512]{1,0:T(8,128)S(1)}, f3...) custom-call(s32[3]{0:T(128)S(1)} %pad_add_fusion.where_ref, ...), custom_call_target="tpu_custom_call" | custom-call | flops 805306368 | bytes 7604224 | tf_op jit(solution)/shard_map/pallas_call | solution.py:123
  73.0 1.3 %collective-permute-start.21 = (bf16[512,512]{1,0:T(8,128)(2,1)S(1)}, bf16[512,512]{1,0:T(8,128)(2,1)S(1)}, u32[]{:S(2)}, u32[]{:S(2)}) collective-permute-start(bf16[512,512]{1,0:T(8,128)(2,1)S(1)} %get-tuple-element.127), channel_id=1, source_target_pairs={{0,4},{1,5},{2,6},{3,7},{8,12},{9,13},{10,14},{11,15},{16,20},{17,... | collective-permute-start | bytes 1572872 | tf_op jit(solution)/shard_map/ppermute | solution.py:25
  74.9 0.9 collective-permute-done.21.refs_0_
  75.8 2.5 %shard_map.171 = (bf16[512,512]{1,0:T(8,128)(2,1)S(1)}, bf16[512,512]{1,0:T(8,128)(2,1)}, f32[512,512]{1,0:T(8,128)S(1)}, f32[512,512]{1,0:T(8,128)S(1)}, f32[51...) custom-call(s32[3]{0:T(128)S(1)} %pad_add_fusion.where_ref, ...), custom_call_target="tpu_custom_call" | custom-call | flops 268435456 | bytes 7639040 | tf_op jit(solution)/shard_map/pallas_call | solution.py:123
  78.3 1.5 %collective-permute-start.23 = (bf16[512,512]{1,0:T(8,128)(2,1)S(1)}, bf16[512,512]{1,0:T(8,128)(2,1)S(1)}, u32[]{:S(2)}, u32[]{:S(2)}) collective-permute-start(bf16[512,512]{1,0:T(8,128)(2,1)S(1)} %get-tuple-element.136), channel_id=1, source_target_pairs={{4,0},{5,1},{6,2},{7,3},{12,8},{13,9},{14,10},{15,11},{20,16},{21,... | collective-permute-start | bytes 1572872 | tf_op jit(solution)/shard_map/ppermute | solution.py:25
  79.7 2.3 %collective-permute-done.23.refs_0_ = bf16[512,512]{1,0:T(8,128)(2,1)S(1)} collective-permute-done((bf16[512,512]{1,0:T(8,128)(2,1)S(1)}, bf16[512,512]{1,0:T(8,128)(2,1)S(1)}, u32[]{:S(2)}, u32[]{:S(2)}) %collective-permute-start.23) | collective-permute-done | bytes 524320 | tf_op jit(solution)/shard_map/ppermute | solution.py:25
  82.1 1.9 %shard_map.172 = (bf16[512,512]{1,0:T(8,128)(2,1)S(1)}, bf16[512,512]{1,0:T(8,128)(2,1)}, f32[512,1]{1,0:T(8,128)S(1)}, bf16[512,512]{1,0:T(8,128)(2,1)S(1)}, bf16[128,128]{1,0:T(8,128)(2,1)}) custom-call(s32[3]{0:T(128)S(1)} %pad_add_fusion.where_ref, bf16[512,512]{1,0:T(8,128)(2,1)S(1)} %collective-permute-done.23.refs_0_, ...), custom_call_target="tpu_custom_call" | custom-call | flops 805306368 | bytes 7639040 | tf_op jit(solution)/shard_map/pallas_call | solution.py:123
  83.9 2.5 %shard_map.173 = (bf16[128,1024]{1,0:T(8,128)(2,1)S(1)}, bf16[128,1024]{1,0:T(8,128)(2,1)S(1)}, bf16[128,1024]{1,0:T(8,128)(2,1)S(1)}, bf16[128,1024]{1,0:T(8,128)(2,1)S(1)}) custom-call(s32[3]{0:T(128)S(1)} %pad_add_fusion.where_ref, bf16[128,1024]{1,0:T(8,128)(2,1)S(1)} %bitcast.28, bf16[128,1024]{1,0:T(8,128)(2,1)S(1)} %collective-permute-done.1.refs_1_, ...), custom_call_target="tpu_custom_call" | custom-call | flops 1610612736 | bytes 4718592 | tf_op jit(solution)/shard_map/pallas_call | solution.py:123
  86.4 0.9 collective-permute-start.27
  87.3 1.1 %collective-permute-start.28 = (bf16[128,1024]{1,0:T(8,128)(2,1)S(1)}, bf16[128,1024]{1,0:T(8,128)(2,1)S(1)}, u32[]{:S(2)}, u32[]{:S(2)}) collective-permute-start(bf16[128,1024]{1,0:T(8,128)(2,1)S(1)} %get-tuple-element.164), channel_id=1, source_target_pairs={{0,2},{1,3},{2,0},{3,1},{4,6},{5,7},{6,4},{7,5},{8,10},{9,11},{10,... | collective-permute-start | bytes 786440 | tf_op jit(solution)/shard_map/ppermute | solution.py:19
  88.5 1.5 %collective-permute-start.29 = (bf16[128,1024]{1,0:T(8,128)(2,1)S(1)}, bf16[128,1024]{1,0:T(8,128)(2,1)S(1)}, u32[]{:S(2)}, u32[]{:S(2)}) collective-permute-start(bf16[128,1024]{1,0:T(8,128)(2,1)S(1)} %get-tuple-element.165), channel_id=1, source_target_pairs={{0,3},{1,2},{2,1},{3,0},{4,7},{5,6},{6,5},{7,4},{8,11},{9,10},{10,... | collective-permute-start | bytes 786440 | tf_op jit(solution)/shard_map/ppermute | solution.py:19
  90.0 0.9 shard_map.174
  91.0 2.9 %collective-permute-start.25 = (bf16[128,256]{1,0:T(8,128)(2,1)S(1)}, bf16[128,256]{1,0:T(8,128)(2,1)S(1)}, u32[]{:S(2)}, u32[]{:S(2)}) collective-permute-start(bf16[128,256]{1,0:T(8,128)(2,1)S(1)} %get-tuple-element.159), channel_id=1, source_target_pairs={{0,16},{8,24},{16,0},{24,8},{1,17},{9,25},{17,1},{25,9},{2,18},{10... | collective-permute-start | bytes 196616 | tf_op jit(solution)/shard_map/ppermute | solution.py:19
  93.9 1.6 %collective-permute-done.24.refs_1_ = bf16[128,256]{1,0:T(8,128)(2,1)S(1)} collective-permute-done((bf16[128,256]{1,0:T(8,128)(2,1)S(1)}, bf16[128,256]{1,0:T(8,128)(2,1)S(1)}, u32[]{:S(2)}, u32[]{:S(2)}) %collective-permute-start.24) | collective-permute-done | bytes 65568 | tf_op jit(solution)/shard_map/ppermute | solution.py:19
  95.4 2.1 %collective-permute-start.26 = (bf16[128,256]{1,0:T(8,128)(2,1)S(1)}, bf16[128,256]{1,0:T(8,128)(2,1)S(1)}, u32[]{:S(2)}, u32[]{:S(2)}) collective-permute-start(bf16[128,256]{1,0:T(8,128)(2,1)S(1)} %get-tuple-element.160), channel_id=1, source_target_pairs={{0,24},{8,16},{16,8},{24,0},{1,25},{9,17},{17,9},{25,1},{2,26},{10... | collective-permute-start | bytes 196616 | tf_op jit(solution)/shard_map/ppermute | solution.py:19
  97.5 3.7 %shard_map.176 = bf16[1024,1024]{1,0:T(8,128)(2,1)} custom-call(s32[3]{0:T(128)S(1)} %pad_add_fusion.where_ref, bf16[1024,512]{1,0:T(8,128)(2,1)S(1)} %shard_map.167.refs_0_, bf16[512,512]{1,0:T(8,128)(2,1)S(1)} %get-tuple-element.149.refs_4_.refs_0_.refs_1_, bf16[512,1024]{1,0:T(8,128)(2,1)S(1)} %bitcast.18), custom_call_target="tpu_custom_call" | custom-call | tf_op jit(solution)/shard_map/pallas_call | solution.py:123
  101.2 3.5 %shard_map.178 = (bf16[128,1024]{1,0:T(8,128)(2,1)}, f32[1,1024]{1,0:T(1,128)}, bf16[1024,128]{1,0:T(8,128)(2,1)}, bf16[128,1024]{1,0:T(8,128)(2,1)}) custom-call(s32[3]{0:T(128)S(1)} %pad_add_fusion.where_ref, bf16[512,512]{1,0:T(8,128)(2,1)S(1)} %get-tuple-element.166.refs_0_.refs_1_, bf16[512,512]{1,0:T(8,128)(2,1)S(1)} %get-tuple-element.166.refs_0_.refs_1_, ...), custom_call_target="tpu_custom_call" | custom-call | tf_op jit(solution)/shard_map/pallas_call | solution.py:123
  104.7 1.3 %shard_map.175 = bf16[128,1024]{1,0:T(8,128)(2,1)} custom-call(s32[3]{0:T(128)S(1)} %pad_add_fusion.where_ref, bf16[128,256]{1,0:T(8,128)(2,1)S(1)} %get-tuple-element.157.refs_0_, bf16[128,256]{1,0:T(8,128)(2,1)S(1)} %collective-permute-done.24.refs_1_, bf16[128,256]{1,0:T(8,128)(2,1)S(1)} %collective-permute-done.25.refs_2_, ...), custom_call_target="tpu_custom_call" | custom-call | tf_op jit(solution)/shard_map/pallas_call | solution.py:123
  105.9 1.4 %shard_map.177 = bf16[128,1024]{1,0:T(8,128)(2,1)} custom-call(s32[3]{0:T(128)S(1)} %pad_add_fusion.where_ref, bf16[128,1024]{1,0:T(8,128)(2,1)S(1)} %get-tuple-element.162.refs_0_, bf16[128,1024]{1,0:T(8,128)(2,1)S(1)} %collective-permute-done.27.refs_1_, bf16[128,1024]{1,0:T(8,128)(2,1)S(1)} %collective-permute-done.28.refs_2_, ...), custom_call_target="tpu_custom_call" | custom-call | tf_op jit(solution)/shard_map/pallas_call | solution.py:123
  (48 shorter events, 6.1 us)
Async XLA Ops:
  0.6 18.4 %collective-permute-start.1 = (bf16[128,1024]{1,0:T(8,128)(2,1)}, bf16[128,1024]{1,0:T(8,128)(2,1)S(1)}, u32[]{:S(2)}, u32[]{:S(2)}) collective-permute-start(bf16[128,1024]{1,0:T(8,128)(2,1)} %bitcast.23), channel_id=1, source_target_pairs={{0,8},{8,0},{16,24},{24,16},{1,9},{9,1},{17,25},{25,17},{2,10},{10... | collective-permute-start | bytes 786440 | tf_op jit(solution)/shard_map/ppermute | solution.py:19
  3.7 15.3 %collective-permute-start = (bf16[128,1024]{1,0:T(8,128)(2,1)}, bf16[128,1024]{1,0:T(8,128)(2,1)S(1)}, u32[]{:S(2)}, u32[]{:S(2)}) collective-permute-start(bf16[128,1024]{1,0:T(8,128)(2,1)} %bitcast.24), channel_id=1, source_target_pairs={{0,16},{8,24},{16,0},{24,8},{1,17},{9,25},{17,1},{25,9},{2,18},{10... | collective-permute-start | bytes 786440 | tf_op jit(solution)/shard_map/ppermute | solution.py:19
  7.1 9.3 %collective-permute-start.2 = (bf16[128,128]{1,0:T(8,128)(2,1)S(1)}, bf16[128,128]{1,0:T(8,128)(2,1)S(1)}, u32[]{:S(2)}, u32[]{:S(2)}) collective-permute-start(bf16[128,128]{1,0:T(8,128)(2,1)S(1)} %broadcast_select_fusion.refs_4_), channel_id=1, source_target_pairs={{0,8},{8,0},{16,24},{24,16},{1,9},{9,1},{17,25},{25,17},{2,10},{10... | collective-permute-start | bytes 98312 | tf_op jit(solution)/shard_map/ppermute | solution.py:19
  7.6 27.7 %copy-start.3 = (bf16[1,128,1024]{2,1,0:T(8,128)(2,1)S(1)}, bf16[1,128,1024]{2,1,0:T(8,128)(2,1)}, u32[]{:S(2)}) copy-start(bf16[1,128,1024]{2,1,0:T(8,128)(2,1)} %param.9) | copy-start | bytes 786436
  11.0 25.7 %collective-permute-start.5 = (bf16[896,256]{1,0:T(8,128)(2,1)S(1)}, bf16[896,256]{1,0:T(8,128)(2,1)S(1)}, u32[]{:S(2)}, u32[]{:S(2)}) collective-permute-start(bf16[896,256]{1,0:T(8,128)(2,1)S(1)} %get-tuple-element.102), channel_id=1, source_target_pairs={{0,1},{1,0},{2,3},{3,2},{4,5},{5,4},{6,7},{7,6},{8,9},{9,8},{10,11... | collective-permute-start | bytes 1376264 | tf_op jit(solution)/shard_map/ppermute | solution.py:19
  12.5 24.2 %collective-permute-start.6 = (bf16[896,256]{1,0:T(8,128)(2,1)S(1)}, bf16[896,256]{1,0:T(8,128)(2,1)S(1)}, u32[]{:S(2)}, u32[]{:S(2)}) collective-permute-start(bf16[896,256]{1,0:T(8,128)(2,1)S(1)} %get-tuple-element.103), channel_id=1, source_target_pairs={{0,2},{1,3},{2,0},{3,1},{4,6},{5,7},{6,4},{7,5},{8,10},{9,11},{10,... | collective-permute-start | bytes 1376264 | tf_op jit(solution)/shard_map/ppermute | solution.py:19
  16.4 20.3 %collective-permute-start.7 = (bf16[896,256]{1,0:T(8,128)(2,1)S(1)}, bf16[896,256]{1,0:T(8,128)(2,1)S(1)}, u32[]{:S(2)}, u32[]{:S(2)}) collective-permute-start(bf16[896,256]{1,0:T(8,128)(2,1)S(1)} %get-tuple-element.104), channel_id=1, source_target_pairs={{0,3},{1,2},{2,1},{3,0},{4,7},{5,6},{6,5},{7,4},{8,11},{9,10},{10,... | collective-permute-start | bytes 1376264 | tf_op jit(solution)/shard_map/ppermute | solution.py:19
  19.1 2.0 %collective-permute-start.3 = (bf16[128,1024]{1,0:T(8,128)(2,1)}, bf16[128,1024]{1,0:T(8,128)(2,1)S(1)}, u32[]{:S(2)}, u32[]{:S(2)}) collective-permute-start(bf16[128,1024]{1,0:T(8,128)(2,1)} %bitcast.25), channel_id=1, source_target_pairs={{8,16},{16,8},{9,17},{17,9},{10,18},{18,10},{11,19},{19,11},{12,20... | collective-permute-start | bytes 786440 | tf_op jit(solution)/shard_map/ppermute | solution.py:38
  19.7 15.6 %collective-permute-start.4 = (bf16[128,1024]{1,0:T(8,128)(2,1)S(1)}, bf16[128,1024]{1,0:T(8,128)(2,1)S(1)}, u32[]{:S(2)}, u32[]{:S(2)}) collective-permute-start(bf16[128,1024]{1,0:T(8,128)(2,1)S(1)} %collective-permute-done.refs_2_), channel_id=1, source_target_pairs={{8,0},{16,24},{9,1},{17,25},{10,2},{18,26},{11,3},{19,27},{12,4},{... | collective-permute-start | bytes 786440 | tf_op jit(solution)/shard_map/ppermute | solution.py:39
  21.1 15.7 %collective-permute-start.8 = (bf16[256,128]{1,0:T(8,128)(2,1)S(1)}, bf16[256,128]{1,0:T(8,128)(2,1)S(1)}, u32[]{:S(2)}, u32[]{:S(2)}) collective-permute-start(bf16[256,128]{1,0:T(8,128)(2,1)S(1)} %pad_maximum_fusion), channel_id=1, source_target_pairs={{0,16},{8,24},{16,0},{24,8},{1,17},{9,25},{17,1},{25,9},{2,18},{10... | collective-permute-start | bytes 196616 | tf_op jit(solution)/shard_map/ppermute | solution.py:19
  36.7 11.1 %collective-permute-start.12 = (bf16[512,512]{1,0:T(8,128)(2,1)S(1)}, bf16[512,512]{1,0:T(8,128)(2,1)S(1)}, u32[]{:S(2)}, u32[]{:S(2)}) collective-permute-start(bf16[512,512]{1,0:T(8,128)(2,1)S(1)} %get-tuple-element.111), channel_id=1, source_target_pairs={{0,8},{8,0},{16,24},{24,16},{1,9},{9,1},{17,25},{25,17},{2,10},{10... | collective-permute-start | bytes 1572872 | tf_op jit(solution)/shard_map/ppermute | solution.py:19
  36.8 5.0 %collective-permute-start.9 = (bf16[512,128]{1,0:T(8,128)(2,1)S(1)}, bf16[512,128]{1,0:T(8,128)(2,1)S(1)}, u32[]{:S(2)}, u32[]{:S(2)}) collective-permute-start(bf16[512,128]{1,0:T(8,128)(2,1)S(1)} %get-tuple-element.108), channel_id=1, source_target_pairs={{0,1},{1,0},{2,3},{3,2},{4,5},{5,4},{6,7},{7,6},{8,9},{9,8},{10,11... | collective-permute-start | bytes 393224 | tf_op jit(solution)/shard_map/ppermute | solution.py:19
  37.4 5.0 %collective-permute-start.10 = (bf16[512,128]{1,0:T(8,128)(2,1)S(1)}, bf16[512,128]{1,0:T(8,128)(2,1)S(1)}, u32[]{:S(2)}, u32[]{:S(2)}) collective-permute-start(bf16[512,128]{1,0:T(8,128)(2,1)S(1)} %get-tuple-element.109), channel_id=1, source_target_pairs={{0,2},{1,3},{2,0},{3,1},{4,6},{5,7},{6,4},{7,5},{8,10},{9,11},{10,... | collective-permute-start | bytes 393224 | tf_op jit(solution)/shard_map/ppermute | solution.py:19
  37.9 5.9 %collective-permute-start.11 = (bf16[512,128]{1,0:T(8,128)(2,1)S(1)}, bf16[512,128]{1,0:T(8,128)(2,1)S(1)}, u32[]{:S(2)}, u32[]{:S(2)}) collective-permute-start(bf16[512,128]{1,0:T(8,128)(2,1)S(1)} %get-tuple-element.110), channel_id=1, source_target_pairs={{0,3},{1,2},{2,1},{3,0},{4,7},{5,6},{6,5},{7,4},{8,11},{9,10},{10,... | collective-permute-start | bytes 393224 | tf_op jit(solution)/shard_map/ppermute | solution.py:19
  47.9 6.8 %collective-permute-start.13 = (bf16[512,128]{1,0:T(8,128)(2,1)S(1)}, bf16[512,128]{1,0:T(8,128)(2,1)S(1)}, u32[]{:S(2)}, u32[]{:S(2)}) collective-permute-start(bf16[512,128]{1,0:T(8,128)(2,1)S(1)} %shard_map.163.refs_0_), channel_id=1, source_target_pairs={{0,16},{8,24},{16,0},{24,8},{1,17},{9,25},{17,1},{25,9},{2,18},{10... | collective-permute-start | bytes 393224 | tf_op jit(solution)/shard_map/ppermute | solution.py:19
  48.9 12.6 %collective-permute-start.17 = (bf16[1024,128]{1,0:T(8,128)(2,1)S(1)}, bf16[1024,128]{1,0:T(8,128)(2,1)S(1)}, u32[]{:S(2)}, u32[]{:S(2)}) collective-permute-start(bf16[1024,128]{1,0:T(8,128)(2,1)S(1)} %get-tuple-element.117.refs_4_), channel_id=1, source_target_pairs={{0,3},{1,2},{2,1},{3,0},{4,7},{5,6},{6,5},{7,4},{8,11},{9,10},{10,... | collective-permute-start | bytes 786440 | tf_op jit(solution)/shard_map/ppermute | solution.py:19
  49.4 12.1 %collective-permute-start.16 = (bf16[1024,128]{1,0:T(8,128)(2,1)S(1)}, bf16[1024,128]{1,0:T(8,128)(2,1)S(1)}, u32[]{:S(2)}, u32[]{:S(2)}) collective-permute-start(bf16[1024,128]{1,0:T(8,128)(2,1)S(1)} %get-tuple-element.117.refs_4_), channel_id=1, source_target_pairs={{0,2},{1,3},{2,0},{3,1},{4,6},{5,7},{6,4},{7,5},{8,10},{9,11},{10,... | collective-permute-start | bytes 786440 | tf_op jit(solution)/shard_map/ppermute | solution.py:19
  51.0 10.6 %collective-permute-start.15 = (bf16[1024,128]{1,0:T(8,128)(2,1)S(1)}, bf16[1024,128]{1,0:T(8,128)(2,1)S(1)}, u32[]{:S(2)}, u32[]{:S(2)}) collective-permute-start(bf16[1024,128]{1,0:T(8,128)(2,1)S(1)} %get-tuple-element.117.refs_4_), channel_id=1, source_target_pairs={{0,1},{1,0},{2,3},{3,2},{4,5},{5,4},{6,7},{7,6},{8,9},{9,8},{10,11... | collective-permute-start | bytes 786440 | tf_op jit(solution)/shard_map/ppermute | solution.py:19
  55.3 6.3 %collective-permute-start.14 = (bf16[512,128]{1,0:T(8,128)(2,1)S(1)}, bf16[512,128]{1,0:T(8,128)(2,1)S(1)}, u32[]{:S(2)}, u32[]{:S(2)}) collective-permute-start(bf16[512,128]{1,0:T(8,128)(2,1)S(1)} %shard_map.164.refs_0_), channel_id=1, source_target_pairs={{0,8},{8,0},{16,24},{24,16},{1,9},{9,1},{17,25},{25,17},{2,10},{10... | collective-permute-start | bytes 393224 | tf_op jit(solution)/shard_map/ppermute | solution.py:19
  62.1 12.2 %collective-permute-start.22 = (bf16[256,512]{1,0:T(8,128)(2,1)S(1)}, bf16[256,512]{1,0:T(8,128)(2,1)S(1)}, u32[]{:S(2)}, u32[]{:S(2)}) collective-permute-start(bf16[256,512]{1,0:T(8,128)(2,1)S(1)} %get-tuple-element.129), channel_id=1, source_target_pairs={{0,16},{8,24},{16,0},{24,8},{1,17},{9,25},{17,1},{25,9},{2,18},{10... | collective-permute-start | bytes 786440 | tf_op jit(solution)/shard_map/ppermute | solution.py:19
  62.2 6.0 %collective-permute-start.20 = (bf16[512,128]{1,0:T(8,128)(2,1)S(1)}, bf16[512,128]{1,0:T(8,128)(2,1)S(1)}, u32[]{:S(2)}, u32[]{:S(2)}) collective-permute-start(bf16[512,128]{1,0:T(8,128)(2,1)S(1)} %shard_map.168.refs_0_), channel_id=1, source_target_pairs={{0,3},{1,2},{2,1},{3,0},{4,7},{5,6},{6,5},{7,4},{8,11},{9,10},{10,... | collective-permute-start | bytes 393224 | tf_op jit(solution)/shard_map/ppermute | solution.py:19
  63.8 5.8 %collective-permute-start.19 = (bf16[512,128]{1,0:T(8,128)(2,1)S(1)}, bf16[512,128]{1,0:T(8,128)(2,1)S(1)}, u32[]{:S(2)}, u32[]{:S(2)}) collective-permute-start(bf16[512,128]{1,0:T(8,128)(2,1)S(1)} %shard_map.168.refs_0_), channel_id=1, source_target_pairs={{0,2},{1,3},{2,0},{3,1},{4,6},{5,7},{6,4},{7,5},{8,10},{9,11},{10,... | collective-permute-start | bytes 393224 | tf_op jit(solution)/shard_map/ppermute | solution.py:19
  65.9 5.0 %collective-permute-start.18 = (bf16[512,128]{1,0:T(8,128)(2,1)S(1)}, bf16[512,128]{1,0:T(8,128)(2,1)S(1)}, u32[]{:S(2)}, u32[]{:S(2)}) collective-permute-start(bf16[512,128]{1,0:T(8,128)(2,1)S(1)} %shard_map.168.refs_0_), channel_id=1, source_target_pairs={{0,1},{1,0},{2,3},{3,2},{4,5},{5,4},{6,7},{7,6},{8,9},{9,8},{10,11... | collective-permute-start | bytes 393224 | tf_op jit(solution)/shard_map/ppermute | solution.py:19
  73.0 2.8 %collective-permute-start.21 = (bf16[512,512]{1,0:T(8,128)(2,1)S(1)}, bf16[512,512]{1,0:T(8,128)(2,1)S(1)}, u32[]{:S(2)}, u32[]{:S(2)}) collective-permute-start(bf16[512,512]{1,0:T(8,128)(2,1)S(1)} %get-tuple-element.127), channel_id=1, source_target_pairs={{0,4},{1,5},{2,6},{3,7},{8,12},{9,13},{10,14},{11,15},{16,20},{17,... | collective-permute-start | bytes 1572872 | tf_op jit(solution)/shard_map/ppermute | solution.py:25
  78.3 3.8 %collective-permute-start.23 = (bf16[512,512]{1,0:T(8,128)(2,1)S(1)}, bf16[512,512]{1,0:T(8,128)(2,1)S(1)}, u32[]{:S(2)}, u32[]{:S(2)}) collective-permute-start(bf16[512,512]{1,0:T(8,128)(2,1)S(1)} %get-tuple-element.136), channel_id=1, source_target_pairs={{4,0},{5,1},{6,2},{7,3},{12,8},{13,9},{14,10},{15,11},{20,16},{21,... | collective-permute-start | bytes 1572872 | tf_op jit(solution)/shard_map/ppermute | solution.py:25
  82.1 1.9 %copy-start.2 = (bf16[1,1024,1024]{2,1,0:T(8,128)(2,1)S(1)}, bf16[1,1024,1024]{2,1,0:T(8,128)(2,1)}, u32[]{:S(2)}) copy-start(bf16[1,1024,1024]{2,1,0:T(8,128)(2,1)} %param.10) | copy-start | bytes 6291460
  83.9 13.6 %copy-start = (bf16[1,512,1024]{2,1,0:T(8,128)(2,1)S(1)}, bf16[1,512,1024]{2,1,0:T(8,128)(2,1)}, u32[]{:S(2)}) copy-start(bf16[1,512,1024]{2,1,0:T(8,128)(2,1)} %param.11) | copy-start | bytes 3145732
  86.4 19.5 %collective-permute-start.27 = (bf16[128,1024]{1,0:T(8,128)(2,1)S(1)}, bf16[128,1024]{1,0:T(8,128)(2,1)S(1)}, u32[]{:S(2)}, u32[]{:S(2)}) collective-permute-start(bf16[128,1024]{1,0:T(8,128)(2,1)S(1)} %get-tuple-element.163), channel_id=1, source_target_pairs={{0,1},{1,0},{2,3},{3,2},{4,5},{5,4},{6,7},{7,6},{8,9},{9,8},{10,11... | collective-permute-start | bytes 786440 | tf_op jit(solution)/shard_map/ppermute | solution.py:19
  87.3 18.6 %collective-permute-start.28 = (bf16[128,1024]{1,0:T(8,128)(2,1)S(1)}, bf16[128,1024]{1,0:T(8,128)(2,1)S(1)}, u32[]{:S(2)}, u32[]{:S(2)}) collective-permute-start(bf16[128,1024]{1,0:T(8,128)(2,1)S(1)} %get-tuple-element.164), channel_id=1, source_target_pairs={{0,2},{1,3},{2,0},{3,1},{4,6},{5,7},{6,4},{7,5},{8,10},{9,11},{10,... | collective-permute-start | bytes 786440 | tf_op jit(solution)/shard_map/ppermute | solution.py:19
  88.5 17.5 %collective-permute-start.29 = (bf16[128,1024]{1,0:T(8,128)(2,1)S(1)}, bf16[128,1024]{1,0:T(8,128)(2,1)S(1)}, u32[]{:S(2)}, u32[]{:S(2)}) collective-permute-start(bf16[128,1024]{1,0:T(8,128)(2,1)S(1)} %get-tuple-element.165), channel_id=1, source_target_pairs={{0,3},{1,2},{2,1},{3,0},{4,7},{5,6},{6,5},{7,4},{8,11},{9,10},{10,... | collective-permute-start | bytes 786440 | tf_op jit(solution)/shard_map/ppermute | solution.py:19
  90.8 10.3 %copy-start.1 = (bf16[1,512,1024]{2,1,0:T(8,128)(2,1)S(1)}, bf16[1,512,1024]{2,1,0:T(8,128)(2,1)}, u32[]{:S(2)}) copy-start(bf16[1,512,1024]{2,1,0:T(8,128)(2,1)} %param.12) | copy-start | bytes 3145732
  90.9 10.3 %copy-start.4 = (bf16[1,128,1024]{2,1,0:T(8,128)(2,1)S(1)}, bf16[1,128,1024]{2,1,0:T(8,128)(2,1)}, u32[]{:S(2)}) copy-start(bf16[1,128,1024]{2,1,0:T(8,128)(2,1)} %param.15) | copy-start | bytes 786436
  90.9 10.3 %copy-start.5 = (bf16[1,1024,128]{2,1,0:T(8,128)(2,1)S(1)}, bf16[1,1024,128]{2,1,0:T(8,128)(2,1)}, u32[]{:S(2)}) copy-start(bf16[1,1024,128]{2,1,0:T(8,128)(2,1)} %param.14) | copy-start | bytes 786436
  90.9 10.3 %copy-start.6 = (f32[1,1024]{1,0:T(1,128)S(1)}, f32[1,1024]{1,0:T(1,128)}, u32[]{:S(2)}) copy-start(f32[1,1024]{1,0:T(1,128)} %refs_9_.1) | copy-start | bytes 12292
  90.9 4.5 %collective-permute-start.24 = (bf16[128,256]{1,0:T(8,128)(2,1)S(1)}, bf16[128,256]{1,0:T(8,128)(2,1)S(1)}, u32[]{:S(2)}, u32[]{:S(2)}) collective-permute-start(bf16[128,256]{1,0:T(8,128)(2,1)S(1)} %get-tuple-element.158), channel_id=1, source_target_pairs={{0,8},{8,0},{16,24},{24,16},{1,9},{9,1},{17,25},{25,17},{2,10},{10... | collective-permute-start | bytes 196616 | tf_op jit(solution)/shard_map/ppermute | solution.py:19
  91.0 13.7 %collective-permute-start.25 = (bf16[128,256]{1,0:T(8,128)(2,1)S(1)}, bf16[128,256]{1,0:T(8,128)(2,1)S(1)}, u32[]{:S(2)}, u32[]{:S(2)}) collective-permute-start(bf16[128,256]{1,0:T(8,128)(2,1)S(1)} %get-tuple-element.159), channel_id=1, source_target_pairs={{0,16},{8,24},{16,0},{24,8},{1,17},{9,25},{17,1},{25,9},{2,18},{10... | collective-permute-start | bytes 196616 | tf_op jit(solution)/shard_map/ppermute | solution.py:19
  95.4 9.2 %collective-permute-start.26 = (bf16[128,256]{1,0:T(8,128)(2,1)S(1)}, bf16[128,256]{1,0:T(8,128)(2,1)S(1)}, u32[]{:S(2)}, u32[]{:S(2)}) collective-permute-start(bf16[128,256]{1,0:T(8,128)(2,1)S(1)} %get-tuple-element.160), channel_id=1, source_target_pairs={{0,24},{8,16},{16,8},{24,0},{1,25},{9,17},{17,9},{25,1},{2,26},{10... | collective-permute-start | bytes 196616 | tf_op jit(solution)/shard_map/ppermute | solution.py:19

commit v11 on v10

--- a/solution.py
+++ b/solution.py
@@ -37,8 +37,9 @@
     shard, far, near, beside = lax.optimization_barrier((shard, far, near, beside))
     across = lax.ppermute(shard, axis, [(1, 2), (2, 1)])
     passed = lax.ppermute(far, axis, [(1, 0), (2, 3)])
-    others = swap(jnp.concatenate([small, beside]), axis, 2)
-    return [shard, near, far], [across, passed], [small, beside, others]
+    both = jnp.concatenate([small, beside])
+    both, across, passed = lax.optimization_barrier((both, across, passed))
+    return [shard, near, far], [across, passed], [small, beside, swap(both, axis, 2)]
 
 
 def scattered(blocks, axis):
@@ -58,6 +59,24 @@
     return rows
 
 
+def exchanged(kept, given, size, axis):
+    count = lax.axis_size(axis)
+    parts = [[(part, 0) for part in kept]]
+    step = 1
+    while True:
+        arrived = swap(given, axis, step)
+        left = count // (2 * step)
+        parts += [
+            [(arrived, (j * left + k) * size) for k in range(left)] for j in range(len(parts))
+        ]
+        step *= 2
+        if step == count:
+            return [part[0] for part in parts]
+        given = [array[row : row + size] for part in parts for array, row in part[1::2]]
+        given = jnp.concatenate(given)
+        parts = [part[::2] for part in parts]
+
+
 def halved(mine, other, size, where):
     half = like((mine.shape[0] // 2, mine.shape[1]))
     return run(functools.partial(halved_kernel, size), [half, half], where, [(mine, other)])
@@ -85,7 +104,7 @@
     return lax.dot_general(left, right, (over, ((), ())), preferred_element_type=f32)
 
 
-def run(kernel, results, where, groups_of_args, scratch=(), flops=0, fetch=False):
+def run(kernel, results, where, groups_of_args, scratch=(), flops=0, fetch=False, store=False):
     counts = [len(group) for group in groups_of_args]
     flat = [array for group in groups_of_args for array in group]
     out_count = len(results)
@@ -125,7 +144,7 @@
         out_shape=[jax.ShapeDtypeStruct(r.shape, r.dtype) for r in results],
         in_specs=[pl.BlockSpec(memory_space=pltpu.SMEM)]
         + [pl.BlockSpec(memory_space=space)] * len(flat),
-        out_specs=[pl.BlockSpec(memory_space=pltpu.VMEM)] * out_count,
+        out_specs=[pl.BlockSpec(memory_space=pltpu.HBM if store else pltpu.VMEM)] * out_count,
         scratch_shapes=scratch,
         compiler_params=pltpu.CompilerParams(vmem_limit_bytes=limit),
         cost_estimate=pl.CostEstimate(
@@ -374,17 +393,25 @@
 def heads_kernel(where, ins, outs, scratch):
     ((code_grad, fold_rows),) = ins
     tokens = outs[0].shape[0]
-    whole = dot(code_grad[...], fold_rows[...], NT)
-    for k, out in enumerate(outs):
-        out[...] = whole[k * tokens : (k + 1) * tokens, :].astype(bf16)
-
-
-def laid_kernel(where, ins, outs, scratch):
-    (blocks,) = ins
-    size = blocks[0].shape[1]
-    for k, part in enumerate(blocks):
+    whole = dot(code_grad[...], fold_rows[...], NT).astype(bf16)
+    for k in range(whole.shape[0] // tokens):
+        value = whole[k * tokens : (k + 1) * tokens, :]
+        if k % 2:
+            outs[-1][k // 2 * tokens : (k // 2 + 1) * tokens, :] = value
+        else:
+            outs[k // 2][...] = value
+
+
+def last_kernel(places, where, ins, outs, scratch):
+    terms, blocks = ins
+    result = terms[0][...].astype(f32)
+    for term in terms[1:]:
+        result = result + term[...].astype(f32)
+    outs[0][...] = result.astype(bf16)
+    for k, (index, row) in enumerate(places):
+        size = blocks[index].shape[1]
         at = pl.multiple_of((where[1] ^ k) * size, size)
-        outs[0][:, pl.ds(at, size)] = part[...]
+        outs[1][:, pl.ds(at, size)] = blocks[index][row : row + outs[1].shape[0], :]
 
 
 def head_kernel(where, ins, outs, scratch):
@@ -415,8 +442,17 @@
 
 def proj_kernel(where, ins, outs, scratch):
     ((turned, code_grad, enc),) = ins
-    head_sum = dot(turned[...], code_grad[...], NN).astype(bf16)
-    outs[0][...] = dot(head_sum, enc[...], NN).astype(bf16)
+    held, sent = scratch
+    size = held.shape[1]
+    copies = []
+    for k in range(held.shape[0]):
+        rows = slice(k * size, (k + 1) * size)
+        head_sum = dot(turned[rows, :], code_grad[...], NN).astype(bf16)
+        held[k, :, :] = dot(head_sum, enc[...], NN).astype(bf16)
+        copies.append(pltpu.make_async_copy(held.at[k], outs[0].at[rows, :], sent.at[k]))
+        copies[-1].start()
+    for copy in copies:
+        copy.wait()
 
 
 def feature_kernel(where, ins, outs, scratch):
@@ -509,11 +545,12 @@
         flops=2 * rows * head_cols * codes,
     )
     partials, heads = list(partials[:parts]), [*heads, *partials[parts:]]
-    partials[-1], *_ = lax.optimization_barrier((partials[-1], *packs, *ends))
+    partials[-1], *_ = lax.optimization_barrier((partials[-1], *packs))
     fold_given, partials = lax.optimization_barrier((fold_given, partials))
     fold_other = swap(fold_given, "dp", 1)
-    code_block = total(scattered(partials, "tensor"), where)
-    code_block, fold_other = lax.optimization_barrier((code_block, fold_other))
+    arrived = scattered(partials, "tensor")
+    arrived, ends = lax.optimization_barrier((arrived, ends))
+    code_block = total(arrived, where)
     fold_terms = halved(fold_kept, fold_other, head_cols // groups, where)
     wide = parts * relay
     packs, _ = lax.optimization_barrier((packs, code_block))
@@ -620,16 +657,25 @@
         (code_grad, mix, turned, enc_blocks)
     )
     enc_blocks = scattered(enc_blocks, "tensor")
-    head_blocks = run(
+    size = head_cols // groups
+    *kept, given = run(
         heads_kernel,
-        [like((tokens, head_cols // groups))] * groups,
+        [like((tokens, size))] * (groups // 2) + [like((rows // 2, size))],
         where,
         [(code_grad, fold_rows)],
     )
-    *head_blocks, mix, turned = lax.optimization_barrier((*head_blocks, mix, turned))
-    head_blocks = scattered(head_blocks, "dp")
+    given, mix, turned = lax.optimization_barrier((given, mix, turned))
+    head_blocks = exchanged(kept, given, tokens, "dp")
     (proj_grad,) = run(
-        proj_kernel, [like((head_cols, model_cols))], where, [(turned, code_grad, enc)]
+        proj_kernel,
+        [like((head_cols, model_cols))],
+        where,
+        [(turned, code_grad, enc)],
+        scratch=[
+            pltpu.VMEM((4, head_cols // 4, model_cols), bf16),
+            pltpu.SemaphoreType.DMA((4,)),
+        ],
+        store=True,
     )
     shapes = [(codes // groups, features), (1, features), (features, relay), (relay, features)]
     dec_grad, gain_grad, send_grad, recv_grad = run(
@@ -652,11 +698,25 @@
         ],
         scratch=[pltpu.VMEM(shape, f32) for shape in shapes],
     )
-    enc_grad = total(enc_blocks, where)
-    if head_cols // groups % 128 == 0:
-        (heads_grad,) = run(laid_kernel, [like((tokens, head_cols))], where, [head_blocks])
+    if size % 128 == 0:
+        arrays = []
+        for array, _ in head_blocks:
+            if not any(array is other for other in arrays):
+                arrays.append(array)
+        places = [
+            (next(k for k, other in enumerate(arrays) if other is array), row)
+            for array, row in head_blocks
+        ]
+        enc_grad, heads_grad = run(
+            functools.partial(last_kernel, places),
+            [like((cols, model_cols)), like((tokens, head_cols))],
+            where,
+            [enc_blocks, arrays],
+        )
     else:
-        heads_grad = ordered(head_blocks, "dp")
+        enc_grad = total(enc_blocks, where)
+        blocks = [array[row : row + tokens] for array, row in head_blocks]
+        heads_grad = ordered(blocks, "dp")
     return (
         sent[None],
         returned[None],

time: 108 us -> 104 us (0.963)
  starting transfers between devices: 48.1 us -> 39.2 us
  waiting for transfers between devices: 24.6 us -> 31.2 us
  Pallas kernels: 32.9 us -> 31.4 us
    ppermute x26 -> x25, starting transfers between devices: 43.3 us -> 34.4 us  [swap(): lax.ppermute(shard, axis, [(i, i ^ by) for i in range(lax.axis_size(axis))])]
    ppermute x1, waiting for transfers between devices: 0.01 us -> 5.61 us  [line_gathered(): passed = lax.ppermute(far, axis, [(1, 0), (2, 3)])]
    pallas_call x19 -> x18, Pallas kernels: 32.9 us -> 31.4 us  [run(): pl.pallas_call(body, out_shape=[jax.ShapeDtypeStruct(r.shape, r.dtype) fo...]
    ppermute x26 -> x25, waiting for transfers between devices: 21.4 us -> 22.4 us  [swap(): lax.ppermute(shard, axis, [(i, i ^ by) for i in range(lax.axis_size(axis))])]
  transfers between devices with their start and end apart: 30 -> 29, of which waited for: 13 -> 13; matrix products, arithmetic and copies ran while one was open for 1% -> 1% of each run, Pallas kernels for 22% -> 21%
where the time goes in v11:
time: 104 us
  starting transfers between devices  39.2 us (38%)
  Pallas kernels  31.4 us (30%)
  waiting for transfers between devices  31.2 us (30%)
    ppermute x25, starting transfers between devices, swap(): lax.ppermute(shard, axis, [(i, i ^ by) for i in range(lax.axis_size(axis))])  34.4 us
    pallas_call x18, Pallas kernels, run(): pl.pallas_call(body, out_shape=[jax.ShapeDtypeStruct(r.shape, r.dtype) fo...  31.4 us
    ppermute x25, waiting for transfers between devices, swap(): lax.ppermute(shard, axis, [(i, i ^ by) for i in range(lax.axis_size(axis))])  22.4 us
    ppermute x1, waiting for transfers between devices, line_gathered(): passed = lax.ppermute(far, axis, [(1, 0), (2, 3)])  5.61 us
    ppermute x2, waiting for transfers between devices, move(): return lax.ppermute(shard, axis, pairs)  3.19 us
    ppermute x2, starting transfers between devices, move(): return lax.ppermute(shard, axis, pairs)  2.78 us
  transfers between devices with their start and end apart: 29, of which 13 were waited for; matrix products, arithmetic and copies ran while one was open for 1% of the time, Pallas kernels for 21%

profile of v11, /device:TPU:0, one launch (start us, length us, event | category | flops | bytes accessed | tf_op | source)
XLA Modules:
  0.0 103.6 jit_solution(12428167745346678715)
XLA Ops:
  0.6 3.1 %collective-permute-start.1 = (bf16[128,1024]{1,0:T(8,128)(2,1)}, bf16[128,1024]{1,0:T(8,128)(2,1)S(1)}, u32[]{:S(2)}, u32[]{:S(2)}) collective-permute-start(bf16[128,1024]{1,0:T(8,128)(2,1)} %bitcast.23), channel_id=1, source_target_pairs={{0,8},{8,0},{16,24},{24,16},{1,9},{9,1},{17,25},{25,17},{2,10},{10... | collective-permute-start | bytes 786440 | tf_op jit(solution)/shard_map/ppermute | solution.py:19
  3.7 2.6 %collective-permute-start = (bf16[128,1024]{1,0:T(8,128)(2,1)}, bf16[128,1024]{1,0:T(8,128)(2,1)S(1)}, u32[]{:S(2)}, u32[]{:S(2)}) collective-permute-start(bf16[128,1024]{1,0:T(8,128)(2,1)} %bitcast.24), channel_id=1, source_target_pairs={{0,16},{8,24},{16,0},{24,8},{1,17},{9,25},{17,1},{25,9},{2,18},{10... | collective-permute-start | bytes 786440 | tf_op jit(solution)/shard_map/ppermute | solution.py:19
  6.3 0.8 broadcast_select_fusion.refs_4_
  7.6 3.4 %shard_map.161 = (bf16[896,256]{1,0:T(8,128)(2,1)S(1)}, bf16[896,256]{1,0:T(8,128)(2,1)S(1)}, bf16[896,256]{1,0:T(8,128)(2,1)S(1)}, bf16[896,256]{1,0:T(8,128)(2,1)S(1)}) custom-call(s32[3]{0:T(128)S(1)} %pad_add_fusion.where_ref, bf16[512,1024]{1,0:T(8,128)(2,1)} %bitcast.19, bf16[128,1024]{1,0:T(8,128)(2,1)} %bitcast.29, bf16[1024,128]{1,0:T(8,128)(2,1)} %bitcast.31, ...), custom_call_target="tpu_custom_call" | custom-call | tf_op jit(solution)/shard_map/pallas_call | solution.py:142
  11.0 1.6 %collective-permute-start.5 = (bf16[896,256]{1,0:T(8,128)(2,1)S(1)}, bf16[896,256]{1,0:T(8,128)(2,1)S(1)}, u32[]{:S(2)}, u32[]{:S(2)}) collective-permute-start(bf16[896,256]{1,0:T(8,128)(2,1)S(1)} %get-tuple-element.111), channel_id=1, source_target_pairs={{0,1},{1,0},{2,3},{3,2},{4,5},{5,4},{6,7},{7,6},{8,9},{9,8},{10,11... | collective-permute-start | bytes 1376264 | tf_op jit(solution)/shard_map/ppermute | solution.py:19
  12.5 1.5 %collective-permute-start.6 = (bf16[896,256]{1,0:T(8,128)(2,1)S(1)}, bf16[896,256]{1,0:T(8,128)(2,1)S(1)}, u32[]{:S(2)}, u32[]{:S(2)}) collective-permute-start(bf16[896,256]{1,0:T(8,128)(2,1)S(1)} %get-tuple-element.112), channel_id=1, source_target_pairs={{0,2},{1,3},{2,0},{3,1},{4,6},{5,7},{6,4},{7,5},{8,10},{9,11},{10,... | collective-permute-start | bytes 1376264 | tf_op jit(solution)/shard_map/ppermute | solution.py:19
  14.1 2.4 %collective-permute-done.2.refs_5_ = bf16[128,128]{1,0:T(8,128)(2,1)S(1)} collective-permute-done((bf16[128,128]{1,0:T(8,128)(2,1)S(1)}, bf16[128,128]{1,0:T(8,128)(2,1)S(1)}, u32[]{:S(2)}, u32[]{:S(2)}) %collective-permute-start.2) | collective-permute-done | bytes 32800 | tf_op jit(solution)/shard_map/ppermute | solution.py:19
  16.4 2.6 %collective-permute-start.7 = (bf16[896,256]{1,0:T(8,128)(2,1)S(1)}, bf16[896,256]{1,0:T(8,128)(2,1)S(1)}, u32[]{:S(2)}, u32[]{:S(2)}) collective-permute-start(bf16[896,256]{1,0:T(8,128)(2,1)S(1)} %get-tuple-element.113), channel_id=1, source_target_pairs={{0,3},{1,2},{2,1},{3,0},{4,7},{5,6},{6,5},{7,4},{8,11},{9,10},{10,... | collective-permute-start | bytes 1376264 | tf_op jit(solution)/shard_map/ppermute | solution.py:19
  19.7 1.3 %collective-permute-start.4 = (bf16[128,1024]{1,0:T(8,128)(2,1)S(1)}, bf16[128,1024]{1,0:T(8,128)(2,1)S(1)}, u32[]{:S(2)}, u32[]{:S(2)}) collective-permute-start(bf16[128,1024]{1,0:T(8,128)(2,1)S(1)} %collective-permute-done.refs_2_), channel_id=1, source_target_pairs={{8,0},{16,24},{9,1},{17,25},{10,2},{18,26},{11,3},{19,27},{12,4},{... | collective-permute-start | bytes 786440 | tf_op jit(solution)/shard_map/ppermute | solution.py:39
  21.0 3.8 %shard_map.160 = (bf16[1024,512]{1,0:T(8,128)(2,1)S(1)}, bf16[512,512]{1,0:T(8,128)(2,1)S(1)}, bf16[512,512]{1,0:T(8,128)(2,1)S(1)}) custom-call(s32[3]{0:T(128)S(1)} %pad_add_fusion.where_ref, bf16[1024,1024]{1,0:T(8,128)(2,1)} %bitcast.21, bf16[512,1024]{1,0:T(8,128)(2,1)} %bitcast.17), custom_call_target="tpu_custom_call" | custom-call | tf_op jit(solution)/shard_map/pallas_call | solution.py:142
  24.8 5.6 %collective-permute-done.4.refs_4_ = bf16[128,1024]{1,0:T(8,128)(2,1)S(1)} collective-permute-done((bf16[128,1024]{1,0:T(8,128)(2,1)S(1)}, bf16[128,1024]{1,0:T(8,128)(2,1)S(1)}, u32[]{:S(2)}, u32[]{:S(2)}) %collective-permute-start.4) | collective-permute-done | bytes 262176 | tf_op jit(solution)/shard_map/ppermute | solution.py:39
  30.4 1.4 %shard_map.162 = (bf16[512,128]{1,0:T(8,128)(2,1)S(1)}, bf16[512,128]{1,0:T(8,128)(2,1)S(1)}, bf16[512,128]{1,0:T(8,128)(2,1)S(1)}, bf16[512,128]{1,0:T(8,128)(2,1)S(1)}, bf16[128,1024]{1,0:T(8,128)(2,1)S(1)}) custom-call(s32[3]{0:T(128)S(1)} %pad_add_fusion.where_ref, bf16[128,1024]{1,0:T(8,128)(2,1)S(1)} %bitcast.26, ...), custom_call_target="tpu_custom_call" | custom-call | flops 536870912 | bytes 3145728 | tf_op jit(solution)/shard_map/pallas_call | solution.py:142
  31.8 1.7 %collective-permute-done.6.refs_2_ = bf16[896,256]{1,0:T(8,128)(2,1)S(1)} collective-permute-done((bf16[896,256]{1,0:T(8,128)(2,1)S(1)}, bf16[896,256]{1,0:T(8,128)(2,1)S(1)}, u32[]{:S(2)}, u32[]{:S(2)}) %collective-permute-start.6) | collective-permute-done | bytes 458784 | tf_op jit(solution)/shard_map/ppermute | solution.py:19
  33.5 1.6 %collective-permute-start.17 = (bf16[512,512]{1,0:T(8,128)(2,1)S(1)}, bf16[512,512]{1,0:T(8,128)(2,1)S(1)}, u32[]{:S(2)}, u32[]{:S(2)}) collective-permute-start(bf16[512,512]{1,0:T(8,128)(2,1)S(1)} %get-tuple-element.133), channel_id=1, source_target_pairs={{0,8},{8,0},{16,24},{24,16},{1,9},{9,1},{17,25},{25,17},{2,10},{10... | collective-permute-start | bytes 1572872 | tf_op jit(solution)/shard_map/ppermute | solution.py:19
  35.1 1.2 %collective-permute-start.8 = (bf16[512,128]{1,0:T(8,128)(2,1)S(1)}, bf16[512,128]{1,0:T(8,128)(2,1)S(1)}, u32[]{:S(2)}, u32[]{:S(2)}) collective-permute-start(bf16[512,128]{1,0:T(8,128)(2,1)S(1)} %get-tuple-element.116), channel_id=1, source_target_pairs={{0,1},{1,0},{2,3},{3,2},{4,5},{5,4},{6,7},{7,6},{8,9},{9,8},{10,11... | collective-permute-start | bytes 393224 | tf_op jit(solution)/shard_map/ppermute | solution.py:19
  36.3 0.8 collective-permute-start.9
  37.1 1.4 %collective-permute-start.10 = (bf16[512,128]{1,0:T(8,128)(2,1)S(1)}, bf16[512,128]{1,0:T(8,128)(2,1)S(1)}, u32[]{:S(2)}, u32[]{:S(2)}) collective-permute-start(bf16[512,128]{1,0:T(8,128)(2,1)S(1)} %get-tuple-element.118), channel_id=1, source_target_pairs={{0,3},{1,2},{2,1},{3,0},{4,7},{5,6},{6,5},{7,4},{8,11},{9,10},{10,... | collective-permute-start | bytes 393224 | tf_op jit(solution)/shard_map/ppermute | solution.py:19
  38.9 6.8 %collective-permute-done.11.refs_6_ = bf16[256,128]{1,0:T(8,128)(2,1)S(1)} collective-permute-done((bf16[256,128]{1,0:T(8,128)(2,1)S(1)}, bf16[256,128]{1,0:T(8,128)(2,1)S(1)}, u32[]{:S(2)}, u32[]{:S(2)}) %collective-permute-start.11) | collective-permute-done | bytes 65568 | tf_op jit(solution)/shard_map/ppermute | solution.py:19
  46.3 3.5 %collective-permute-start.12 = (bf16[512,128]{1,0:T(8,128)(2,1)S(1)}, bf16[512,128]{1,0:T(8,128)(2,1)S(1)}, u32[]{:S(2)}, u32[]{:S(2)}) collective-permute-start(bf16[512,128]{1,0:T(8,128)(2,1)S(1)} %shard_map.163.refs_0_), channel_id=1, source_target_pairs={{0,16},{8,24},{16,0},{24,8},{1,17},{9,25},{17,1},{25,9},{2,18},{10... | collective-permute-start | bytes 393224 | tf_op jit(solution)/shard_map/ppermute | solution.py:19
  49.8 0.9 shard_map.165
  50.7 1.6 %collective-permute-start.16 = (bf16[1024,128]{1,0:T(8,128)(2,1)S(1)}, bf16[1024,128]{1,0:T(8,128)(2,1)S(1)}, u32[]{:S(2)}, u32[]{:S(2)}) collective-permute-start(bf16[1024,128]{1,0:T(8,128)(2,1)S(1)} %get-tuple-element.131.refs_4_), channel_id=1, source_target_pairs={{0,3},{1,2},{2,1},{3,0},{4,7},{5,6},{6,5},{7,4},{8,11},{9,10},{10,... | collective-permute-start | bytes 786440 | tf_op jit(solution)/shard_map/ppermute | solution.py:19
  52.3 1.5 %collective-permute-start.15 = (bf16[1024,128]{1,0:T(8,128)(2,1)S(1)}, bf16[1024,128]{1,0:T(8,128)(2,1)S(1)}, u32[]{:S(2)}, u32[]{:S(2)}) collective-permute-start(bf16[1024,128]{1,0:T(8,128)(2,1)S(1)} %get-tuple-element.131.refs_4_), channel_id=1, source_target_pairs={{0,2},{1,3},{2,0},{3,1},{4,6},{5,7},{6,4},{7,5},{8,10},{9,11},{10,... | collective-permute-start | bytes 786440 | tf_op jit(solution)/shard_map/ppermute | solution.py:19
  54.9 0.9 shard_map.167.refs_0_
  56.5 3.4 %collective-permute-done.13.refs_1_ = bf16[512,128]{1,0:T(8,128)(2,1)S(1)} collective-permute-done((bf16[512,128]{1,0:T(8,128)(2,1)S(1)}, bf16[512,128]{1,0:T(8,128)(2,1)S(1)}, u32[]{:S(2)}, u32[]{:S(2)}) %collective-permute-start.13) | collective-permute-done | bytes 131104 | tf_op jit(solution)/shard_map/ppermute | solution.py:19
  59.9 2.0 %collective-permute-done.15.refs_6_ = bf16[1024,128]{1,0:T(8,128)(2,1)S(1)} collective-permute-done((bf16[1024,128]{1,0:T(8,128)(2,1)S(1)}, bf16[1024,128]{1,0:T(8,128)(2,1)S(1)}, u32[]{:S(2)}, u32[]{:S(2)}) %collective-permute-start.15) | collective-permute-done | bytes 262176 | tf_op jit(solution)/shard_map/ppermute | solution.py:19
  62.4 0.8 collective-permute-start.22
  63.3 1.3 %collective-permute-start.20 = (bf16[512,128]{1,0:T(8,128)(2,1)S(1)}, bf16[512,128]{1,0:T(8,128)(2,1)S(1)}, u32[]{:S(2)}, u32[]{:S(2)}) collective-permute-start(bf16[512,128]{1,0:T(8,128)(2,1)S(1)} %shard_map.168.refs_0_), channel_id=1, source_target_pairs={{0,3},{1,2},{2,1},{3,0},{4,7},{5,6},{6,5},{7,4},{8,11},{9,10},{10,... | collective-permute-start | bytes 393224 | tf_op jit(solution)/shard_map/ppermute | solution.py:19
  64.5 1.8 %collective-permute-start.19 = (bf16[512,128]{1,0:T(8,128)(2,1)S(1)}, bf16[512,128]{1,0:T(8,128)(2,1)S(1)}, u32[]{:S(2)}, u32[]{:S(2)}) collective-permute-start(bf16[512,128]{1,0:T(8,128)(2,1)S(1)} %shard_map.168.refs_0_), channel_id=1, source_target_pairs={{0,2},{1,3},{2,0},{3,1},{4,6},{5,7},{6,4},{7,5},{8,10},{9,11},{10,... | collective-permute-start | bytes 393224 | tf_op jit(solution)/shard_map/ppermute | solution.py:19
  66.7 2.5 %collective-permute-done.20.refs_3_ = bf16[512,128]{1,0:T(8,128)(2,1)S(1)} collective-permute-done((bf16[512,128]{1,0:T(8,128)(2,1)S(1)}, bf16[512,128]{1,0:T(8,128)(2,1)S(1)}, u32[]{:S(2)}, u32[]{:S(2)}) %collective-permute-start.20) | collective-permute-done | bytes 131104 | tf_op jit(solution)/shard_map/ppermute | solution.py:19
  69.2 1.3 %collective-permute-done.19.refs_2_ = bf16[512,128]{1,0:T(8,128)(2,1)S(1)} collective-permute-done((bf16[512,128]{1,0:T(8,128)(2,1)S(1)}, bf16[512,128]{1,0:T(8,128)(2,1)S(1)}, u32[]{:S(2)}, u32[]{:S(2)}) %collective-permute-start.19) | collective-permute-done | bytes 131104 | tf_op jit(solution)/shard_map/ppermute | solution.py:19
  70.5 0.7 collective-permute-done.18.refs_1_
  71.3 2.1 %shard_map.169 = (bf16[512,512]{1,0:T(8,128)(2,1)S(1)}, bf16[512,512]{1,0:T(8,128)(2,1)S(1)}, f32[512,512]{1,0:T(8,128)S(1)}, f32[512,512]{1,0:T(8,128)S(1)}, f3...) custom-call(s32[3]{0:T(128)S(1)} %pad_add_fusion.where_ref, ...), custom_call_target="tpu_custom_call" | custom-call | flops 805306368 | bytes 7604224 | tf_op jit(solution)/shard_map/pallas_call | solution.py:142
  73.4 1.3 %collective-permute-start.21 = (bf16[512,512]{1,0:T(8,128)(2,1)S(1)}, bf16[512,512]{1,0:T(8,128)(2,1)S(1)}, u32[]{:S(2)}, u32[]{:S(2)}) collective-permute-start(bf16[512,512]{1,0:T(8,128)(2,1)S(1)} %get-tuple-element.141), channel_id=1, source_target_pairs={{0,4},{1,5},{2,6},{3,7},{8,12},{9,13},{10,14},{11,15},{16,20},{17,... | collective-permute-start | bytes 1572872 | tf_op jit(solution)/shard_map/ppermute | solution.py:25
  75.3 0.9 collective-permute-done.21.refs_0_
  76.2 2.5 %shard_map.171 = (bf16[512,512]{1,0:T(8,128)(2,1)S(1)}, bf16[512,512]{1,0:T(8,128)(2,1)}, f32[512,512]{1,0:T(8,128)S(1)}, f32[512,512]{1,0:T(8,128)S(1)}, f32[51...) custom-call(s32[3]{0:T(128)S(1)} %pad_add_fusion.where_ref, ...), custom_call_target="tpu_custom_call" | custom-call | flops 268435456 | bytes 7639040 | tf_op jit(solution)/shard_map/pallas_call | solution.py:142
  78.7 1.5 %collective-permute-start.23 = (bf16[512,512]{1,0:T(8,128)(2,1)S(1)}, bf16[512,512]{1,0:T(8,128)(2,1)S(1)}, u32[]{:S(2)}, u32[]{:S(2)}) collective-permute-start(bf16[512,512]{1,0:T(8,128)(2,1)S(1)} %get-tuple-element.150), channel_id=1, source_target_pairs={{4,0},{5,1},{6,2},{7,3},{12,8},{13,9},{14,10},{15,11},{20,16},{21,... | collective-permute-start | bytes 1572872 | tf_op jit(solution)/shard_map/ppermute | solution.py:25
  80.1 2.3 %collective-permute-done.23.refs_0_ = bf16[512,512]{1,0:T(8,128)(2,1)S(1)} collective-permute-done((bf16[512,512]{1,0:T(8,128)(2,1)S(1)}, bf16[512,512]{1,0:T(8,128)(2,1)S(1)}, u32[]{:S(2)}, u32[]{:S(2)}) %collective-permute-start.23) | collective-permute-done | bytes 524320 | tf_op jit(solution)/shard_map/ppermute | solution.py:25
  82.5 1.9 %shard_map.172 = (bf16[512,512]{1,0:T(8,128)(2,1)S(1)}, bf16[512,512]{1,0:T(8,128)(2,1)}, f32[512,1]{1,0:T(8,128)S(1)}, bf16[512,512]{1,0:T(8,128)(2,1)S(1)}, bf16[128,128]{1,0:T(8,128)(2,1)}) custom-call(s32[3]{0:T(128)S(1)} %pad_add_fusion.where_ref, bf16[512,512]{1,0:T(8,128)(2,1)S(1)} %collective-permute-done.23.refs_0_, ...), custom_call_target="tpu_custom_call" | custom-call | flops 805306368 | bytes 7639040 | tf_op jit(solution)/shard_map/pallas_call | solution.py:142
  84.3 2.5 %shard_map.173 = (bf16[128,1024]{1,0:T(8,128)(2,1)S(1)}, bf16[128,1024]{1,0:T(8,128)(2,1)S(1)}, bf16[128,1024]{1,0:T(8,128)(2,1)S(1)}, bf16[128,1024]{1,0:T(8,128)(2,1)S(1)}) custom-call(s32[3]{0:T(128)S(1)} %pad_add_fusion.where_ref, bf16[128,1024]{1,0:T(8,128)(2,1)S(1)} %bitcast.28, bf16[128,1024]{1,0:T(8,128)(2,1)S(1)} %collective-permute-done.1.refs_1_, ...), custom_call_target="tpu_custom_call" | custom-call | flops 1610612736 | bytes 4718592 | tf_op jit(solution)/shard_map/pallas_call | solution.py:142
  86.8 0.9 shard_map.174
  87.7 0.8 collective-permute-start.27
  88.8 1.2 %collective-permute-start.25 = (bf16[128,1024]{1,0:T(8,128)(2,1)S(1)}, bf16[128,1024]{1,0:T(8,128)(2,1)S(1)}, u32[]{:S(2)}, u32[]{:S(2)}) collective-permute-start(bf16[128,1024]{1,0:T(8,128)(2,1)S(1)} %get-tuple-element.165), channel_id=1, source_target_pairs={{0,2},{1,3},{2,0},{3,1},{4,6},{5,7},{6,4},{7,5},{8,10},{9,11},{10,... | collective-permute-start | bytes 786440 | tf_op jit(solution)/shard_map/ppermute | solution.py:19
  90.0 2.0 %collective-permute-start.26 = (bf16[128,1024]{1,0:T(8,128)(2,1)S(1)}, bf16[128,1024]{1,0:T(8,128)(2,1)S(1)}, u32[]{:S(2)}, u32[]{:S(2)}) collective-permute-start(bf16[128,1024]{1,0:T(8,128)(2,1)S(1)} %get-tuple-element.166), channel_id=1, source_target_pairs={{0,3},{1,2},{2,1},{3,0},{4,7},{5,6},{6,5},{7,4},{8,11},{9,10},{10,... | collective-permute-start | bytes 786440 | tf_op jit(solution)/shard_map/ppermute | solution.py:19
  92.0 1.3 %collective-permute-done.27.refs_5_ = bf16[256,256]{1,0:T(8,128)(2,1)S(1)} collective-permute-done((bf16[256,256]{1,0:T(8,128)(2,1)S(1)}, bf16[256,256]{1,0:T(8,128)(2,1)S(1)}, u32[]{:S(2)}, u32[]{:S(2)}) %collective-permute-start.27) | collective-permute-done | bytes 131104 | tf_op jit(solution)/shard_map/ppermute | solution.py:19
  93.4 1.5 %collective-permute-start.28 = (bf16[256,256]{1,0:T(8,128)(2,1)S(1)}, bf16[256,256]{1,0:T(8,128)(2,1)S(1)}, u32[]{:S(2)}, u32[]{:S(2)}) collective-permute-start(bf16[256,256]{1,0:T(8,128)(2,1)S(1)} %pad_maximum_fusion), channel_id=1, source_target_pairs={{0,16},{8,24},{16,0},{24,8},{1,17},{9,25},{17,1},{25,9},{2,18},{10... | collective-permute-start | bytes 393224 | tf_op jit(solution)/shard_map/ppermute | solution.py:19
  94.9 3.5 %shard_map.176 = bf16[1024,1024]{1,0:T(8,128)(2,1)} custom-call(s32[3]{0:T(128)S(1)} %pad_add_fusion.where_ref, bf16[1024,512]{1,0:T(8,128)(2,1)S(1)} %shard_map.167.refs_0_, bf16[512,512]{1,0:T(8,128)(2,1)S(1)} %get-tuple-element.167.refs_4_.refs_0_.refs_1_, bf16[512,1024]{1,0:T(8,128)(2,1)S(1)} %bitcast.18), custom_call_target="tpu_custom_call" | custom-call | tf_op jit(solution)/shard_map/pallas_call | solution.py:142
  98.4 3.5 %shard_map.177 = (bf16[128,1024]{1,0:T(8,128)(2,1)}, f32[1,1024]{1,0:T(1,128)}, bf16[1024,128]{1,0:T(8,128)(2,1)}, bf16[128,1024]{1,0:T(8,128)(2,1)}) custom-call(s32[3]{0:T(128)S(1)} %pad_add_fusion.where_ref, bf16[512,512]{1,0:T(8,128)(2,1)S(1)} %get-tuple-element.178.refs_0_.refs_1_, bf16[512,512]{1,0:T(8,128)(2,1)S(1)} %get-tuple-element.178.refs_0_.refs_1_, ...), custom_call_target="tpu_custom_call" | custom-call | tf_op jit(solution)/shard_map/pallas_call | solution.py:142
  102.2 1.4 %shard_map.175 = (bf16[128,1024]{1,0:T(8,128)(2,1)}, bf16[128,1024]{1,0:T(8,128)(2,1)}) custom-call(s32[3]{0:T(128)S(1)} %pad_add_fusion.where_ref, bf16[128,1024]{1,0:T(8,128)(2,1)S(1)} %get-tuple-element.163.refs_0_, bf16[128,1024]{1,0:T(8,128)(2,1)S(1)} %collective-permute-done.24.refs_1_, bf16[128,1024]{1,0:T(8,128)(2,1)S(1)} %collective-permute-done.25.refs_2_, ...), custom_call_target="tpu_custom_call" | custom-call | tf_op jit(solution)/shard_map/pallas_call | solution.py:142
  (47 shorter events, 6.3 us)
Async XLA Ops:
  0.6 18.4 %collective-permute-start.1 = (bf16[128,1024]{1,0:T(8,128)(2,1)}, bf16[128,1024]{1,0:T(8,128)(2,1)S(1)}, u32[]{:S(2)}, u32[]{:S(2)}) collective-permute-start(bf16[128,1024]{1,0:T(8,128)(2,1)} %bitcast.23), channel_id=1, source_target_pairs={{0,8},{8,0},{16,24},{24,16},{1,9},{9,1},{17,25},{25,17},{2,10},{10... | collective-permute-start | bytes 786440 | tf_op jit(solution)/shard_map/ppermute | solution.py:19
  3.7 15.3 %collective-permute-start = (bf16[128,1024]{1,0:T(8,128)(2,1)}, bf16[128,1024]{1,0:T(8,128)(2,1)S(1)}, u32[]{:S(2)}, u32[]{:S(2)}) collective-permute-start(bf16[128,1024]{1,0:T(8,128)(2,1)} %bitcast.24), channel_id=1, source_target_pairs={{0,16},{8,24},{16,0},{24,8},{1,17},{9,25},{17,1},{25,9},{2,18},{10... | collective-permute-start | bytes 786440 | tf_op jit(solution)/shard_map/ppermute | solution.py:19
  7.1 9.3 %collective-permute-start.2 = (bf16[128,128]{1,0:T(8,128)(2,1)S(1)}, bf16[128,128]{1,0:T(8,128)(2,1)S(1)}, u32[]{:S(2)}, u32[]{:S(2)}) collective-permute-start(bf16[128,128]{1,0:T(8,128)(2,1)S(1)} %broadcast_select_fusion.refs_4_), channel_id=1, source_target_pairs={{0,8},{8,0},{16,24},{24,16},{1,9},{9,1},{17,25},{25,17},{2,10},{10... | collective-permute-start | bytes 98312 | tf_op jit(solution)/shard_map/ppermute | solution.py:19
  7.6 22.8 %copy-start.3 = (bf16[1,128,1024]{2,1,0:T(8,128)(2,1)S(1)}, bf16[1,128,1024]{2,1,0:T(8,128)(2,1)}, u32[]{:S(2)}) copy-start(bf16[1,128,1024]{2,1,0:T(8,128)(2,1)} %param.9) | copy-start | bytes 786436
  11.0 20.9 %collective-permute-start.5 = (bf16[896,256]{1,0:T(8,128)(2,1)S(1)}, bf16[896,256]{1,0:T(8,128)(2,1)S(1)}, u32[]{:S(2)}, u32[]{:S(2)}) collective-permute-start(bf16[896,256]{1,0:T(8,128)(2,1)S(1)} %get-tuple-element.111), channel_id=1, source_target_pairs={{0,1},{1,0},{2,3},{3,2},{4,5},{5,4},{6,7},{7,6},{8,9},{9,8},{10,11... | collective-permute-start | bytes 1376264 | tf_op jit(solution)/shard_map/ppermute | solution.py:19
  12.5 21.0 %collective-permute-start.6 = (bf16[896,256]{1,0:T(8,128)(2,1)S(1)}, bf16[896,256]{1,0:T(8,128)(2,1)S(1)}, u32[]{:S(2)}, u32[]{:S(2)}) collective-permute-start(bf16[896,256]{1,0:T(8,128)(2,1)S(1)} %get-tuple-element.112), channel_id=1, source_target_pairs={{0,2},{1,3},{2,0},{3,1},{4,6},{5,7},{6,4},{7,5},{8,10},{9,11},{10,... | collective-permute-start | bytes 1376264 | tf_op jit(solution)/shard_map/ppermute | solution.py:19
  16.4 17.1 %collective-permute-start.7 = (bf16[896,256]{1,0:T(8,128)(2,1)S(1)}, bf16[896,256]{1,0:T(8,128)(2,1)S(1)}, u32[]{:S(2)}, u32[]{:S(2)}) collective-permute-start(bf16[896,256]{1,0:T(8,128)(2,1)S(1)} %get-tuple-element.113), channel_id=1, source_target_pairs={{0,3},{1,2},{2,1},{3,0},{4,7},{5,6},{6,5},{7,4},{8,11},{9,10},{10,... | collective-permute-start | bytes 1376264 | tf_op jit(solution)/shard_map/ppermute | solution.py:19
  19.1 5.8 %collective-permute-start.3 = (bf16[128,1024]{1,0:T(8,128)(2,1)}, bf16[128,1024]{1,0:T(8,128)(2,1)S(1)}, u32[]{:S(2)}, u32[]{:S(2)}) collective-permute-start(bf16[128,1024]{1,0:T(8,128)(2,1)} %bitcast.25), channel_id=1, source_target_pairs={{8,16},{16,8},{9,17},{17,9},{10,18},{18,10},{11,19},{19,11},{12,20... | collective-permute-start | bytes 786440 | tf_op jit(solution)/shard_map/ppermute | solution.py:38
  19.7 10.7 %collective-permute-start.4 = (bf16[128,1024]{1,0:T(8,128)(2,1)S(1)}, bf16[128,1024]{1,0:T(8,128)(2,1)S(1)}, u32[]{:S(2)}, u32[]{:S(2)}) collective-permute-start(bf16[128,1024]{1,0:T(8,128)(2,1)S(1)} %collective-permute-done.refs_2_), channel_id=1, source_target_pairs={{8,0},{16,24},{9,1},{17,25},{10,2},{18,26},{11,3},{19,27},{12,4},{... | collective-permute-start | bytes 786440 | tf_op jit(solution)/shard_map/ppermute | solution.py:39
  33.5 22.3 %collective-permute-start.17 = (bf16[512,512]{1,0:T(8,128)(2,1)S(1)}, bf16[512,512]{1,0:T(8,128)(2,1)S(1)}, u32[]{:S(2)}, u32[]{:S(2)}) collective-permute-start(bf16[512,512]{1,0:T(8,128)(2,1)S(1)} %get-tuple-element.133), channel_id=1, source_target_pairs={{0,8},{8,0},{16,24},{24,16},{1,9},{9,1},{17,25},{25,17},{2,10},{10... | collective-permute-start | bytes 1572872 | tf_op jit(solution)/shard_map/ppermute | solution.py:19
  35.1 10.6 %collective-permute-start.8 = (bf16[512,128]{1,0:T(8,128)(2,1)S(1)}, bf16[512,128]{1,0:T(8,128)(2,1)S(1)}, u32[]{:S(2)}, u32[]{:S(2)}) collective-permute-start(bf16[512,128]{1,0:T(8,128)(2,1)S(1)} %get-tuple-element.116), channel_id=1, source_target_pairs={{0,1},{1,0},{2,3},{3,2},{4,5},{5,4},{6,7},{7,6},{8,9},{9,8},{10,11... | collective-permute-start | bytes 393224 | tf_op jit(solution)/shard_map/ppermute | solution.py:19
  36.3 9.4 %collective-permute-start.9 = (bf16[512,128]{1,0:T(8,128)(2,1)S(1)}, bf16[512,128]{1,0:T(8,128)(2,1)S(1)}, u32[]{:S(2)}, u32[]{:S(2)}) collective-permute-start(bf16[512,128]{1,0:T(8,128)(2,1)S(1)} %get-tuple-element.117), channel_id=1, source_target_pairs={{0,2},{1,3},{2,0},{3,1},{4,6},{5,7},{6,4},{7,5},{8,10},{9,11},{10,... | collective-permute-start | bytes 393224 | tf_op jit(solution)/shard_map/ppermute | solution.py:19
  37.1 8.6 %collective-permute-start.10 = (bf16[512,128]{1,0:T(8,128)(2,1)S(1)}, bf16[512,128]{1,0:T(8,128)(2,1)S(1)}, u32[]{:S(2)}, u32[]{:S(2)}) collective-permute-start(bf16[512,128]{1,0:T(8,128)(2,1)S(1)} %get-tuple-element.118), channel_id=1, source_target_pairs={{0,3},{1,2},{2,1},{3,0},{4,7},{5,6},{6,5},{7,4},{8,11},{9,10},{10,... | collective-permute-start | bytes 393224 | tf_op jit(solution)/shard_map/ppermute | solution.py:19
  38.6 7.1 %collective-permute-start.11 = (bf16[256,128]{1,0:T(8,128)(2,1)S(1)}, bf16[256,128]{1,0:T(8,128)(2,1)S(1)}, u32[]{:S(2)}, u32[]{:S(2)}) collective-permute-start(bf16[256,128]{1,0:T(8,128)(2,1)S(1)} %pad_maximum_fusion.1), channel_id=1, source_target_pairs={{0,16},{8,24},{16,0},{24,8},{1,17},{9,25},{17,1},{25,9},{2,18},{10... | collective-permute-start | bytes 196616 | tf_op jit(solution)/shard_map/ppermute | solution.py:19
  46.3 7.9 %collective-permute-start.12 = (bf16[512,128]{1,0:T(8,128)(2,1)S(1)}, bf16[512,128]{1,0:T(8,128)(2,1)S(1)}, u32[]{:S(2)}, u32[]{:S(2)}) collective-permute-start(bf16[512,128]{1,0:T(8,128)(2,1)S(1)} %shard_map.163.refs_0_), channel_id=1, source_target_pairs={{0,16},{8,24},{16,0},{24,8},{1,17},{9,25},{17,1},{25,9},{2,18},{10... | collective-permute-start | bytes 393224 | tf_op jit(solution)/shard_map/ppermute | solution.py:19
  50.7 9.2 %collective-permute-start.16 = (bf16[1024,128]{1,0:T(8,128)(2,1)S(1)}, bf16[1024,128]{1,0:T(8,128)(2,1)S(1)}, u32[]{:S(2)}, u32[]{:S(2)}) collective-permute-start(bf16[1024,128]{1,0:T(8,128)(2,1)S(1)} %get-tuple-element.131.refs_4_), channel_id=1, source_target_pairs={{0,3},{1,2},{2,1},{3,0},{4,7},{5,6},{6,5},{7,4},{8,11},{9,10},{10,... | collective-permute-start | bytes 786440 | tf_op jit(solution)/shard_map/ppermute | solution.py:19
  52.3 9.6 %collective-permute-start.15 = (bf16[1024,128]{1,0:T(8,128)(2,1)S(1)}, bf16[1024,128]{1,0:T(8,128)(2,1)S(1)}, u32[]{:S(2)}, u32[]{:S(2)}) collective-permute-start(bf16[1024,128]{1,0:T(8,128)(2,1)S(1)} %get-tuple-element.131.refs_4_), channel_id=1, source_target_pairs={{0,2},{1,3},{2,0},{3,1},{4,6},{5,7},{6,4},{7,5},{8,10},{9,11},{10,... | collective-permute-start | bytes 786440 | tf_op jit(solution)/shard_map/ppermute | solution.py:19
  53.7 8.1 %collective-permute-start.14 = (bf16[1024,128]{1,0:T(8,128)(2,1)S(1)}, bf16[1024,128]{1,0:T(8,128)(2,1)S(1)}, u32[]{:S(2)}, u32[]{:S(2)}) collective-permute-start(bf16[1024,128]{1,0:T(8,128)(2,1)S(1)} %get-tuple-element.131.refs_4_), channel_id=1, source_target_pairs={{0,1},{1,0},{2,3},{3,2},{4,5},{5,4},{6,7},{7,6},{8,9},{9,8},{10,11... | collective-permute-start | bytes 786440 | tf_op jit(solution)/shard_map/ppermute | solution.py:19
  54.8 5.0 %collective-permute-start.13 = (bf16[512,128]{1,0:T(8,128)(2,1)S(1)}, bf16[512,128]{1,0:T(8,128)(2,1)S(1)}, u32[]{:S(2)}, u32[]{:S(2)}) collective-permute-start(bf16[512,128]{1,0:T(8,128)(2,1)S(1)} %shard_map.164.refs_0_), channel_id=1, source_target_pairs={{0,8},{8,0},{16,24},{24,16},{1,9},{9,1},{17,25},{25,17},{2,10},{10... | collective-permute-start | bytes 393224 | tf_op jit(solution)/shard_map/ppermute | solution.py:19
  62.4 12.3 %collective-permute-start.22 = (bf16[256,512]{1,0:T(8,128)(2,1)S(1)}, bf16[256,512]{1,0:T(8,128)(2,1)S(1)}, u32[]{:S(2)}, u32[]{:S(2)}) collective-permute-start(bf16[256,512]{1,0:T(8,128)(2,1)S(1)} %get-tuple-element.143), channel_id=1, source_target_pairs={{0,16},{8,24},{16,0},{24,8},{1,17},{9,25},{17,1},{25,9},{2,18},{10... | collective-permute-start | bytes 786440 | tf_op jit(solution)/shard_map/ppermute | solution.py:19
  63.3 6.0 %collective-permute-start.20 = (bf16[512,128]{1,0:T(8,128)(2,1)S(1)}, bf16[512,128]{1,0:T(8,128)(2,1)S(1)}, u32[]{:S(2)}, u32[]{:S(2)}) collective-permute-start(bf16[512,128]{1,0:T(8,128)(2,1)S(1)} %shard_map.168.refs_0_), channel_id=1, source_target_pairs={{0,3},{1,2},{2,1},{3,0},{4,7},{5,6},{6,5},{7,4},{8,11},{9,10},{10,... | collective-permute-start | bytes 393224 | tf_op jit(solution)/shard_map/ppermute | solution.py:19
  64.5 6.0 %collective-permute-start.19 = (bf16[512,128]{1,0:T(8,128)(2,1)S(1)}, bf16[512,128]{1,0:T(8,128)(2,1)S(1)}, u32[]{:S(2)}, u32[]{:S(2)}) collective-permute-start(bf16[512,128]{1,0:T(8,128)(2,1)S(1)} %shard_map.168.refs_0_), channel_id=1, source_target_pairs={{0,2},{1,3},{2,0},{3,1},{4,6},{5,7},{6,4},{7,5},{8,10},{9,11},{10,... | collective-permute-start | bytes 393224 | tf_op jit(solution)/shard_map/ppermute | solution.py:19
  66.3 5.0 %collective-permute-start.18 = (bf16[512,128]{1,0:T(8,128)(2,1)S(1)}, bf16[512,128]{1,0:T(8,128)(2,1)S(1)}, u32[]{:S(2)}, u32[]{:S(2)}) collective-permute-start(bf16[512,128]{1,0:T(8,128)(2,1)S(1)} %shard_map.168.refs_0_), channel_id=1, source_target_pairs={{0,1},{1,0},{2,3},{3,2},{4,5},{5,4},{6,7},{7,6},{8,9},{9,8},{10,11... | collective-permute-start | bytes 393224 | tf_op jit(solution)/shard_map/ppermute | solution.py:19
  73.4 2.8 %collective-permute-start.21 = (bf16[512,512]{1,0:T(8,128)(2,1)S(1)}, bf16[512,512]{1,0:T(8,128)(2,1)S(1)}, u32[]{:S(2)}, u32[]{:S(2)}) collective-permute-start(bf16[512,512]{1,0:T(8,128)(2,1)S(1)} %get-tuple-element.141), channel_id=1, source_target_pairs={{0,4},{1,5},{2,6},{3,7},{8,12},{9,13},{10,14},{11,15},{16,20},{17,... | collective-permute-start | bytes 1572872 | tf_op jit(solution)/shard_map/ppermute | solution.py:25
  78.7 3.8 %collective-permute-start.23 = (bf16[512,512]{1,0:T(8,128)(2,1)S(1)}, bf16[512,512]{1,0:T(8,128)(2,1)S(1)}, u32[]{:S(2)}, u32[]{:S(2)}) collective-permute-start(bf16[512,512]{1,0:T(8,128)(2,1)S(1)} %get-tuple-element.150), channel_id=1, source_target_pairs={{4,0},{5,1},{6,2},{7,3},{12,8},{13,9},{14,10},{15,11},{20,16},{21,... | collective-permute-start | bytes 1572872 | tf_op jit(solution)/shard_map/ppermute | solution.py:25
  82.5 1.9 %copy-start.2 = (bf16[1,1024,1024]{2,1,0:T(8,128)(2,1)S(1)}, bf16[1,1024,1024]{2,1,0:T(8,128)(2,1)}, u32[]{:S(2)}) copy-start(bf16[1,1024,1024]{2,1,0:T(8,128)(2,1)} %param.10) | copy-start | bytes 6291460
  84.3 10.5 %copy-start = (bf16[1,512,1024]{2,1,0:T(8,128)(2,1)S(1)}, bf16[1,512,1024]{2,1,0:T(8,128)(2,1)}, u32[]{:S(2)}) copy-start(bf16[1,512,1024]{2,1,0:T(8,128)(2,1)} %param.11) | copy-start | bytes 3145732
  87.7 5.6 %collective-permute-start.27 = (bf16[256,256]{1,0:T(8,128)(2,1)S(1)}, bf16[256,256]{1,0:T(8,128)(2,1)S(1)}, u32[]{:S(2)}, u32[]{:S(2)}) collective-permute-start(bf16[256,256]{1,0:T(8,128)(2,1)S(1)} %get-tuple-element.173), channel_id=1, source_target_pairs={{0,8},{8,0},{16,24},{24,16},{1,9},{9,1},{17,25},{25,17},{2,10},{10... | collective-permute-start | bytes 393224 | tf_op jit(solution)/shard_map/ppermute | solution.py:19
  88.5 13.3 %collective-permute-start.24 = (bf16[128,1024]{1,0:T(8,128)(2,1)S(1)}, bf16[128,1024]{1,0:T(8,128)(2,1)S(1)}, u32[]{:S(2)}, u32[]{:S(2)}) collective-permute-start(bf16[128,1024]{1,0:T(8,128)(2,1)S(1)} %get-tuple-element.164), channel_id=1, source_target_pairs={{0,1},{1,0},{2,3},{3,2},{4,5},{5,4},{6,7},{7,6},{8,9},{9,8},{10,11... | collective-permute-start | bytes 786440 | tf_op jit(solution)/shard_map/ppermute | solution.py:19
  88.8 13.1 %collective-permute-start.25 = (bf16[128,1024]{1,0:T(8,128)(2,1)S(1)}, bf16[128,1024]{1,0:T(8,128)(2,1)S(1)}, u32[]{:S(2)}, u32[]{:S(2)}) collective-permute-start(bf16[128,1024]{1,0:T(8,128)(2,1)S(1)} %get-tuple-element.165), channel_id=1, source_target_pairs={{0,2},{1,3},{2,0},{3,1},{4,6},{5,7},{6,4},{7,5},{8,10},{9,11},{10,... | collective-permute-start | bytes 786440 | tf_op jit(solution)/shard_map/ppermute | solution.py:19
  90.0 12.2 %collective-permute-start.26 = (bf16[128,1024]{1,0:T(8,128)(2,1)S(1)}, bf16[128,1024]{1,0:T(8,128)(2,1)S(1)}, u32[]{:S(2)}, u32[]{:S(2)}) collective-permute-start(bf16[128,1024]{1,0:T(8,128)(2,1)S(1)} %get-tuple-element.166), channel_id=1, source_target_pairs={{0,3},{1,2},{2,1},{3,0},{4,7},{5,6},{6,5},{7,4},{8,11},{9,10},{10,... | collective-permute-start | bytes 786440 | tf_op jit(solution)/shard_map/ppermute | solution.py:19
  93.3 5.0 %copy-start.1 = (bf16[1,512,1024]{2,1,0:T(8,128)(2,1)S(1)}, bf16[1,512,1024]{2,1,0:T(8,128)(2,1)}, u32[]{:S(2)}) copy-start(bf16[1,512,1024]{2,1,0:T(8,128)(2,1)} %param.12) | copy-start | bytes 3145732
  93.3 5.0 %copy-start.4 = (bf16[1,128,1024]{2,1,0:T(8,128)(2,1)S(1)}, bf16[1,128,1024]{2,1,0:T(8,128)(2,1)}, u32[]{:S(2)}) copy-start(bf16[1,128,1024]{2,1,0:T(8,128)(2,1)} %param.15) | copy-start | bytes 786436
  93.3 5.0 %copy-start.5 = (bf16[1,1024,128]{2,1,0:T(8,128)(2,1)S(1)}, bf16[1,1024,128]{2,1,0:T(8,128)(2,1)}, u32[]{:S(2)}) copy-start(bf16[1,1024,128]{2,1,0:T(8,128)(2,1)} %param.14) | copy-start | bytes 786436
  93.4 5.0 %copy-start.6 = (f32[1,1024]{1,0:T(1,128)S(1)}, f32[1,1024]{1,0:T(1,128)}, u32[]{:S(2)}) copy-start(f32[1,1024]{1,0:T(1,128)} %refs_9_.1) | copy-start | bytes 12292
  93.4 8.9 %collective-permute-start.28 = (bf16[256,256]{1,0:T(8,128)(2,1)S(1)}, bf16[256,256]{1,0:T(8,128)(2,1)S(1)}, u32[]{:S(2)}, u32[]{:S(2)}) collective-permute-start(bf16[256,256]{1,0:T(8,128)(2,1)S(1)} %pad_maximum_fusion), channel_id=1, source_target_pairs={{0,16},{8,24},{16,0},{24,8},{1,17},{9,25},{17,1},{25,9},{2,18},{10... | collective-permute-start | bytes 393224 | tf_op jit(solution)/shard_map/ppermute | solution.py:19

commit v12 on v11

--- a/solution.py
+++ b/solution.py
@@ -29,7 +29,7 @@
     return [shard] + [swap(shard, axis, k) for k in range(1, lax.axis_size(axis))]
 
 
-def line_gathered(shard, small, axis):
+def line_gathered(shard, small, after, axis):
     if lax.axis_size(axis) != 4:
         return gathered(shard, axis), [], gathered(small, axis)
     far, near = swap(shard, axis, 2), swap(shard, axis, 1)
@@ -38,7 +38,7 @@
     across = lax.ppermute(shard, axis, [(1, 2), (2, 1)])
     passed = lax.ppermute(far, axis, [(1, 0), (2, 3)])
     both = jnp.concatenate([small, beside])
-    both, across, passed = lax.optimization_barrier((both, across, passed))
+    both, across, passed, _ = lax.optimization_barrier((both, across, passed, after))
     return [shard, near, far], [across, passed], [small, beside, swap(both, axis, 2)]
 
 
@@ -455,10 +455,21 @@
         copy.wait()
 
 
+def normed_kernel(where, ins, outs, scratch):
+    ((mix, received, row_scale, dec, recv),) = ins
+    relay = recv.shape[0]
+
+    def step(at):
+        mixed = dot(mix[at, :], dec[...], NN) + dot(received[at, :relay], recv[...], NN)
+        outs[0][at, :] = mixed * row_scale[at, :]
+
+    by_rows(mix.shape[0], step)
+
+
 def feature_kernel(where, ins, outs, scratch):
-    (mix, mix_cols, received, incoming, row_scale, inner, dec, recv, send, gain), = ins
+    ((normed_rows, mix_cols, received, incoming, row_scale, inner, send, gain),) = ins
     sums = scratch
-    relay = recv.shape[0]
+    relay = send.shape[1]
     size = sums[0].shape[0]
     cols = slice(None)
     if mix_cols.shape[1] > size:
@@ -469,19 +480,17 @@
     def step(at):
         received_here = received[at, :relay]
         incoming_here = incoming[at, :relay]
-        scale = row_scale[at, :]
-        mixed = dot(mix[at, :], dec[...], NN) + dot(received_here, recv[...], NN)
-        normed = mixed * scale
+        normed = normed_rows[at, :]
         out_rows = (normed * gain[...]).astype(bf16)
         grad_norm = dot(incoming_here, send[...], NT)
-        grad_mixed = scale * (grad_norm * gain[...] - normed * inner[at, :])
+        grad_mixed = row_scale[at, :] * (grad_norm * gain[...] - normed * inner[at, :])
         grad_mixed = grad_mixed.astype(bf16)
         sums[0][...] += dot(mix_cols[at, cols], grad_mixed, TN)
         sums[1][...] += jnp.sum(grad_norm * normed, axis=0, keepdims=True)
         sums[2][...] += dot(out_rows, incoming_here, TN)
         sums[3][...] += dot(received_here, grad_mixed, TN)
 
-    by_rows(mix.shape[0], step)
+    by_rows(normed_rows.shape[0], step)
     for out, ref in zip(outs, sums):
         out[...] = ref[...].astype(out.dtype)
 
@@ -515,8 +524,6 @@
     head_cols, model_cols = proj.shape
     where = jnp.stack([lax.axis_index("tensor"), lax.axis_index("dp"), section]).astype(jnp.int32)
 
-    end = jnp.where(section == 0, input_code, code_cotangent)
-    heads, pair, ends = line_gathered(heads_out[0], end, "dp")
     packs = run(
         gram_kernel,
         [like((cols * codes // (2 * relay) + codes + relay, 2 * relay))] * parts,
@@ -534,6 +541,8 @@
         fetch=True,
     )
     fold, _ = lax.optimization_barrier((fold, packs[0]))
+    end = jnp.where(section == 0, input_code, code_cotangent)
+    heads, pair, ends = line_gathered(heads_out[0], end, fold, "dp")
     packs = scattered(packs, "tensor")
 
     partials = run(
@@ -546,7 +555,7 @@
     )
     partials, heads = list(partials[:parts]), [*heads, *partials[parts:]]
     partials[-1], *_ = lax.optimization_barrier((partials[-1], *packs))
-    fold_given, partials = lax.optimization_barrier((fold_given, partials))
+    fold_given, partials, ends = lax.optimization_barrier((fold_given, partials, ends))
     fold_other = swap(fold_given, "dp", 1)
     arrived = scattered(partials, "tensor")
     arrived, ends = lax.optimization_barrier((arrived, ends))
@@ -615,6 +624,12 @@
         )
         received, sent = results[:2]
     mixed, unscaled, row_scale, returned, sent = results[2:]
+    (normed,) = run(
+        normed_kernel,
+        [like((rows, features), f32)],
+        where,
+        [(mix, received, row_scale, dec, recv)],
+    )
     incoming = ends
     for turn in range(1, sections):
         last = turn == sections - 1
@@ -623,6 +638,8 @@
             shapes += [like((rows, 1), f32), like((rows, codes))]
             shapes += [like((tokens, relay))]
         moved = move(returned, "pipe", -1)
+        if turn == 1:
+            moved, normed = lax.optimization_barrier((moved, normed))
         results = run(
             functools.partial(backward_kernel, width, sections - 1 - turn, last),
             shapes,
@@ -684,14 +701,12 @@
         where,
         [
             (
-                mix,
+                normed,
                 mix if codes // groups % 128 == 0 else block(mix, "dp", 1),
                 received,
                 incoming,
                 row_scale,
                 inner,
-                dec,
-                recv,
                 send,
                 gain,
             )

time: 104 us -> 102 us (0.981)
  waiting for transfers between devices: 31.2 us -> 29.8 us
    ppermute x2, waiting for transfers between devices: 3.19 us -> 1.66 us  [move(): return lax.ppermute(shard, axis, pairs)]
    pallas_call x18 -> x19, Pallas kernels: 31.4 us -> 32.2 us  [run(): pl.pallas_call(body, out_shape=[jax.ShapeDtypeStruct(r.shape, r.dtype) fo...]
  transfers between devices with their start and end apart: 29 -> 29, of which waited for: 13 -> 16; matrix products, arithmetic and copies ran while one was open for 1% -> 1% of each run, Pallas kernels for 21% -> 22%
where the time goes in v12:
time: 102 us
  starting transfers between devices  38.2 us (37%)
  Pallas kernels  32.2 us (32%)
  waiting for transfers between devices  29.8 us (29%)
    ppermute x25, starting transfers between devices, swap(): lax.ppermute(shard, axis, [(i, i ^ by) for i in range(lax.axis_size(axis))])  33.4 us
    pallas_call x19, Pallas kernels, run(): pl.pallas_call(body, out_shape=[jax.ShapeDtypeStruct(r.shape, r.dtype) fo...  32.2 us
    ppermute x25, waiting for transfers between devices, swap(): lax.ppermute(shard, axis, [(i, i ^ by) for i in range(lax.axis_size(axis))])  22.6 us
    ppermute x1, waiting for transfers between devices, line_gathered(): passed = lax.ppermute(far, axis, [(1, 0), (2, 3)])  5.61 us
    ppermute x2, starting transfers between devices, move(): return lax.ppermute(shard, axis, pairs)  2.78 us
  transfers between devices with their start and end apart: 29, of which 16 were waited for; matrix products, arithmetic and copies ran while one was open for 1% of the time, Pallas kernels for 22%

profile of v12, /device:TPU:0, one launch (start us, length us, event | category | flops | bytes accessed | tf_op | source)
XLA Modules:
  0.0 102.1 jit_solution(2098186959711846434)
XLA Ops:
  0.6 3.1 %collective-permute-start.1 = (bf16[128,1024]{1,0:T(8,128)(2,1)}, bf16[128,1024]{1,0:T(8,128)(2,1)S(1)}, u32[]{:S(2)}, u32[]{:S(2)}) collective-permute-start(bf16[128,1024]{1,0:T(8,128)(2,1)} %bitcast.23), channel_id=1, source_target_pairs={{0,8},{8,0},{16,24},{24,16},{1,9},{9,1},{17,25},{25,17},{2,10},{10... | collective-permute-start | bytes 786440 | tf_op jit(solution)/shard_map/ppermute | solution.py:19
  3.7 2.6 %collective-permute-start = (bf16[128,1024]{1,0:T(8,128)(2,1)}, bf16[128,1024]{1,0:T(8,128)(2,1)S(1)}, u32[]{:S(2)}, u32[]{:S(2)}) collective-permute-start(bf16[128,1024]{1,0:T(8,128)(2,1)} %bitcast.24), channel_id=1, source_target_pairs={{0,16},{8,24},{16,0},{24,8},{1,17},{9,25},{17,1},{25,9},{2,18},{10... | collective-permute-start | bytes 786440 | tf_op jit(solution)/shard_map/ppermute | solution.py:19
  6.3 0.8 broadcast_select_fusion.refs_4_
  7.6 3.4 %shard_map.161 = (bf16[896,256]{1,0:T(8,128)(2,1)S(1)}, bf16[896,256]{1,0:T(8,128)(2,1)S(1)}, bf16[896,256]{1,0:T(8,128)(2,1)S(1)}, bf16[896,256]{1,0:T(8,128)(2,1)S(1)}) custom-call(s32[3]{0:T(128)S(1)} %pad_add_fusion.where_ref, bf16[512,1024]{1,0:T(8,128)(2,1)} %bitcast.17, bf16[128,1024]{1,0:T(8,128)(2,1)} %bitcast.29, bf16[1024,128]{1,0:T(8,128)(2,1)} %bitcast.31, ...), custom_call_target="tpu_custom_call" | custom-call | tf_op jit(solution)/shard_map/pallas_call | solution.py:142
  11.0 1.6 %collective-permute-start.5 = (bf16[896,256]{1,0:T(8,128)(2,1)S(1)}, bf16[896,256]{1,0:T(8,128)(2,1)S(1)}, u32[]{:S(2)}, u32[]{:S(2)}) collective-permute-start(bf16[896,256]{1,0:T(8,128)(2,1)S(1)} %get-tuple-element.116), channel_id=1, source_target_pairs={{0,1},{1,0},{2,3},{3,2},{4,5},{5,4},{6,7},{7,6},{8,9},{9,8},{10,11... | collective-permute-start | bytes 1376264 | tf_op jit(solution)/shard_map/ppermute | solution.py:19
  12.5 1.5 %collective-permute-start.6 = (bf16[896,256]{1,0:T(8,128)(2,1)S(1)}, bf16[896,256]{1,0:T(8,128)(2,1)S(1)}, u32[]{:S(2)}, u32[]{:S(2)}) collective-permute-start(bf16[896,256]{1,0:T(8,128)(2,1)S(1)} %get-tuple-element.117), channel_id=1, source_target_pairs={{0,2},{1,3},{2,0},{3,1},{4,6},{5,7},{6,4},{7,5},{8,10},{9,11},{10,... | collective-permute-start | bytes 1376264 | tf_op jit(solution)/shard_map/ppermute | solution.py:19
  14.1 2.4 %collective-permute-done.2.refs_5_ = bf16[128,128]{1,0:T(8,128)(2,1)S(1)} collective-permute-done((bf16[128,128]{1,0:T(8,128)(2,1)S(1)}, bf16[128,128]{1,0:T(8,128)(2,1)S(1)}, u32[]{:S(2)}, u32[]{:S(2)}) %collective-permute-start.2) | collective-permute-done | bytes 32800 | tf_op jit(solution)/shard_map/ppermute | solution.py:19
  16.4 2.6 %collective-permute-start.7 = (bf16[896,256]{1,0:T(8,128)(2,1)S(1)}, bf16[896,256]{1,0:T(8,128)(2,1)S(1)}, u32[]{:S(2)}, u32[]{:S(2)}) collective-permute-start(bf16[896,256]{1,0:T(8,128)(2,1)S(1)} %get-tuple-element.118), channel_id=1, source_target_pairs={{0,3},{1,2},{2,1},{3,0},{4,7},{5,6},{6,5},{7,4},{8,11},{9,10},{10,... | collective-permute-start | bytes 1376264 | tf_op jit(solution)/shard_map/ppermute | solution.py:19
  19.7 1.3 %collective-permute-start.4 = (bf16[128,1024]{1,0:T(8,128)(2,1)S(1)}, bf16[128,1024]{1,0:T(8,128)(2,1)S(1)}, u32[]{:S(2)}, u32[]{:S(2)}) collective-permute-start(bf16[128,1024]{1,0:T(8,128)(2,1)S(1)} %collective-permute-done.refs_2_), channel_id=1, source_target_pairs={{8,0},{16,24},{9,1},{17,25},{10,2},{18,26},{11,3},{19,27},{12,4},{... | collective-permute-start | bytes 786440 | tf_op jit(solution)/shard_map/ppermute | solution.py:39
  21.0 3.8 %shard_map.160 = (bf16[1024,512]{1,0:T(8,128)(2,1)S(1)}, bf16[512,512]{1,0:T(8,128)(2,1)S(1)}, bf16[512,512]{1,0:T(8,128)(2,1)S(1)}) custom-call(s32[3]{0:T(128)S(1)} %pad_add_fusion.where_ref, bf16[1024,1024]{1,0:T(8,128)(2,1)} %bitcast.21, bf16[512,1024]{1,0:T(8,128)(2,1)} %bitcast.19), custom_call_target="tpu_custom_call" | custom-call | tf_op jit(solution)/shard_map/pallas_call | solution.py:142
  24.8 5.6 %collective-permute-done.4.refs_4_ = bf16[128,1024]{1,0:T(8,128)(2,1)S(1)} collective-permute-done((bf16[128,1024]{1,0:T(8,128)(2,1)S(1)}, bf16[128,1024]{1,0:T(8,128)(2,1)S(1)}, u32[]{:S(2)}, u32[]{:S(2)}) %collective-permute-start.4) | collective-permute-done | bytes 262176 | tf_op jit(solution)/shard_map/ppermute | solution.py:39
  30.8 1.4 %shard_map.162 = (bf16[512,128]{1,0:T(8,128)(2,1)S(1)}, bf16[512,128]{1,0:T(8,128)(2,1)S(1)}, bf16[512,128]{1,0:T(8,128)(2,1)S(1)}, bf16[512,128]{1,0:T(8,128)(2,1)S(1)}, bf16[128,1024]{1,0:T(8,128)(2,1)S(1)}) custom-call(s32[3]{0:T(128)S(1)} %pad_add_fusion.where_ref, bf16[128,1024]{1,0:T(8,128)(2,1)S(1)} %bitcast.26, ...), custom_call_target="tpu_custom_call" | custom-call | flops 536870912 | bytes 3145728 | tf_op jit(solution)/shard_map/pallas_call | solution.py:142
  32.2 1.3 %collective-permute-done.6.refs_2_ = bf16[896,256]{1,0:T(8,128)(2,1)S(1)} collective-permute-done((bf16[896,256]{1,0:T(8,128)(2,1)S(1)}, bf16[896,256]{1,0:T(8,128)(2,1)S(1)}, u32[]{:S(2)}, u32[]{:S(2)}) %collective-permute-start.6) | collective-permute-done | bytes 458784 | tf_op jit(solution)/shard_map/ppermute | solution.py:19
  33.5 2.1 %collective-permute-done.8.refs_6_ = bf16[256,128]{1,0:T(8,128)(2,1)S(1)} collective-permute-done((bf16[256,128]{1,0:T(8,128)(2,1)S(1)}, bf16[256,128]{1,0:T(8,128)(2,1)S(1)}, u32[]{:S(2)}, u32[]{:S(2)}) %collective-permute-start.8) | collective-permute-done | bytes 65568 | tf_op jit(solution)/shard_map/ppermute | solution.py:19
  36.3 0.8 collective-permute-start.10
  37.1 2.0 %collective-permute-start.11 = (bf16[512,128]{1,0:T(8,128)(2,1)S(1)}, bf16[512,128]{1,0:T(8,128)(2,1)S(1)}, u32[]{:S(2)}, u32[]{:S(2)}) collective-permute-start(bf16[512,128]{1,0:T(8,128)(2,1)S(1)} %get-tuple-element.124), channel_id=1, source_target_pairs={{0,3},{1,2},{2,1},{3,0},{4,7},{5,6},{6,5},{7,4},{8,11},{9,10},{10,... | collective-permute-start | bytes 393224 | tf_op jit(solution)/shard_map/ppermute | solution.py:19
  39.1 1.5 %collective-permute-done.9.refs_1_ = bf16[512,128]{1,0:T(8,128)(2,1)S(1)} collective-permute-done((bf16[512,128]{1,0:T(8,128)(2,1)S(1)}, bf16[512,128]{1,0:T(8,128)(2,1)S(1)}, u32[]{:S(2)}, u32[]{:S(2)}) %collective-permute-start.9) | collective-permute-done | bytes 131104 | tf_op jit(solution)/shard_map/ppermute | solution.py:19
  41.3 1.7 %collective-permute-done.11.refs_3_ = bf16[512,128]{1,0:T(8,128)(2,1)S(1)} collective-permute-done((bf16[512,128]{1,0:T(8,128)(2,1)S(1)}, bf16[512,128]{1,0:T(8,128)(2,1)S(1)}, u32[]{:S(2)}, u32[]{:S(2)}) %collective-permute-start.11) | collective-permute-done | bytes 131104 | tf_op jit(solution)/shard_map/ppermute | solution.py:19
  43.6 2.2 %collective-permute-start.12 = (bf16[512,128]{1,0:T(8,128)(2,1)S(1)}, bf16[512,128]{1,0:T(8,128)(2,1)S(1)}, u32[]{:S(2)}, u32[]{:S(2)}) collective-permute-start(bf16[512,128]{1,0:T(8,128)(2,1)S(1)} %shard_map.163.refs_0_), channel_id=1, source_target_pairs={{0,16},{8,24},{16,0},{24,8},{1,17},{9,25},{17,1},{25,9},{2,18},{10... | collective-permute-start | bytes 393224 | tf_op jit(solution)/shard_map/ppermute | solution.py:19
  45.8 0.9 shard_map.165
  46.7 2.5 %collective-permute-start.16 = (bf16[1024,128]{1,0:T(8,128)(2,1)S(1)}, bf16[1024,128]{1,0:T(8,128)(2,1)S(1)}, u32[]{:S(2)}, u32[]{:S(2)}) collective-permute-start(bf16[1024,128]{1,0:T(8,128)(2,1)S(1)} %get-tuple-element.139.refs_4_), channel_id=1, source_target_pairs={{0,3},{1,2},{2,1},{3,0},{4,7},{5,6},{6,5},{7,4},{8,11},{9,10},{10,... | collective-permute-start | bytes 786440 | tf_op jit(solution)/shard_map/ppermute | solution.py:19
  51.5 0.8 collective-permute-start.13
  52.3 0.9 shard_map.167.refs_0_
  53.8 4.6 %collective-permute-done.13.refs_1_ = bf16[512,128]{1,0:T(8,128)(2,1)S(1)} collective-permute-done((bf16[512,128]{1,0:T(8,128)(2,1)S(1)}, bf16[512,128]{1,0:T(8,128)(2,1)S(1)}, u32[]{:S(2)}, u32[]{:S(2)}) %collective-permute-start.13) | collective-permute-done | bytes 131104 | tf_op jit(solution)/shard_map/ppermute | solution.py:19
  59.1 0.9 collective-permute-start.22
  60.0 2.9 %collective-permute-start.20 = (bf16[512,128]{1,0:T(8,128)(2,1)S(1)}, bf16[512,128]{1,0:T(8,128)(2,1)S(1)}, u32[]{:S(2)}, u32[]{:S(2)}) collective-permute-start(bf16[512,128]{1,0:T(8,128)(2,1)S(1)} %shard_map.168.refs_0_), channel_id=1, source_target_pairs={{0,3},{1,2},{2,1},{3,0},{4,7},{5,6},{6,5},{7,4},{8,11},{9,10},{10,... | collective-permute-start | bytes 393224 | tf_op jit(solution)/shard_map/ppermute | solution.py:19
  63.5 2.4 %collective-permute-done.20.refs_3_ = bf16[512,128]{1,0:T(8,128)(2,1)S(1)} collective-permute-done((bf16[512,128]{1,0:T(8,128)(2,1)S(1)}, bf16[512,128]{1,0:T(8,128)(2,1)S(1)}, u32[]{:S(2)}, u32[]{:S(2)}) %collective-permute-start.20) | collective-permute-done | bytes 131104 | tf_op jit(solution)/shard_map/ppermute | solution.py:19
  65.9 2.0 %collective-permute-done.19.refs_2_ = bf16[512,128]{1,0:T(8,128)(2,1)S(1)} collective-permute-done((bf16[512,128]{1,0:T(8,128)(2,1)S(1)}, bf16[512,128]{1,0:T(8,128)(2,1)S(1)}, u32[]{:S(2)}, u32[]{:S(2)}) %collective-permute-start.19) | collective-permute-done | bytes 131104 | tf_op jit(solution)/shard_map/ppermute | solution.py:19
  67.9 2.1 %shard_map.169 = (bf16[512,512]{1,0:T(8,128)(2,1)S(1)}, bf16[512,512]{1,0:T(8,128)(2,1)S(1)}, f32[512,512]{1,0:T(8,128)S(1)}, f32[512,512]{1,0:T(8,128)S(1)}, f3...) custom-call(s32[3]{0:T(128)S(1)} %pad_add_fusion.where_ref, ...), custom_call_target="tpu_custom_call" | custom-call | flops 805306368 | bytes 7604224 | tf_op jit(solution)/shard_map/pallas_call | solution.py:142
  70.0 1.3 %collective-permute-start.21 = (bf16[512,512]{1,0:T(8,128)(2,1)S(1)}, bf16[512,512]{1,0:T(8,128)(2,1)S(1)}, u32[]{:S(2)}, u32[]{:S(2)}) collective-permute-start(bf16[512,512]{1,0:T(8,128)(2,1)S(1)} %get-tuple-element.149), channel_id=1, source_target_pairs={{0,4},{1,5},{2,6},{3,7},{8,12},{9,13},{10,14},{11,15},{16,20},{17,... | collective-permute-start | bytes 1572872 | tf_op jit(solution)/shard_map/ppermute | solution.py:25
  72.0 0.9 collective-permute-done.21.refs_0_
  72.8 2.5 %shard_map.171 = (bf16[512,512]{1,0:T(8,128)(2,1)S(1)}, bf16[512,512]{1,0:T(8,128)(2,1)}, f32[512,512]{1,0:T(8,128)S(1)}, f32[512,512]{1,0:T(8,128)S(1)}, f32[51...) custom-call(s32[3]{0:T(128)S(1)} %pad_add_fusion.where_ref, ...), custom_call_target="tpu_custom_call" | custom-call | flops 268435456 | bytes 7639040 | tf_op jit(solution)/shard_map/pallas_call | solution.py:142
  75.3 1.5 %collective-permute-start.23 = (bf16[512,512]{1,0:T(8,128)(2,1)S(1)}, bf16[512,512]{1,0:T(8,128)(2,1)S(1)}, u32[]{:S(2)}, u32[]{:S(2)}) collective-permute-start(bf16[512,512]{1,0:T(8,128)(2,1)S(1)} %get-tuple-element.158), channel_id=1, source_target_pairs={{4,0},{5,1},{6,2},{7,3},{12,8},{13,9},{14,10},{15,11},{20,16},{21,... | collective-permute-start | bytes 1572872 | tf_op jit(solution)/shard_map/ppermute | solution.py:25
  76.8 1.5 %shard_map.172.refs_0_ = f32[512,1024]{1,0:T(8,128)S(1)} custom-call(s32[3]{0:T(128)S(1)} %pad_add_fusion.where_ref, bf16[512,512]{1,0:T(8,128)(2,1)S(1)} %get-tuple-element.188.refs_0_.refs_1_, bf16[512,512]{1,0:T(8,128)(2,1)S(1)} %get-tuple-element.160.refs_1_.refs_2_, f32[512,1]{1,0:T(8,128)S(1)} %get-tuple-element.161.refs_2_.refs_5_.refs_4_, ...), custom_call_target="tpu_custom_call" | custom-call | tf_op jit(solution)/shard_map/pallas_call | solution.py:142
  78.3 0.8 collective-permute-done.23.refs_0_
  79.1 1.9 %shard_map.173 = (bf16[512,512]{1,0:T(8,128)(2,1)S(1)}, bf16[512,512]{1,0:T(8,128)(2,1)}, f32[512,1]{1,0:T(8,128)S(1)}, bf16[512,512]{1,0:T(8,128)(2,1)S(1)}, bf16[128,128]{1,0:T(8,128)(2,1)}) custom-call(s32[3]{0:T(128)S(1)} %pad_add_fusion.where_ref, bf16[512,512]{1,0:T(8,128)(2,1)S(1)} %collective-permute-done.23.refs_0_, ...), custom_call_target="tpu_custom_call" | custom-call | flops 805306368 | bytes 7639040 | tf_op jit(solution)/shard_map/pallas_call | solution.py:142
  81.0 2.5 %shard_map.174 = (bf16[128,1024]{1,0:T(8,128)(2,1)S(1)}, bf16[128,1024]{1,0:T(8,128)(2,1)S(1)}, bf16[128,1024]{1,0:T(8,128)(2,1)S(1)}, bf16[128,1024]{1,0:T(8,128)(2,1)S(1)}) custom-call(s32[3]{0:T(128)S(1)} %pad_add_fusion.where_ref, bf16[128,1024]{1,0:T(8,128)(2,1)S(1)} %bitcast.28, bf16[128,1024]{1,0:T(8,128)(2,1)S(1)} %collective-permute-done.1.refs_1_, ...), custom_call_target="tpu_custom_call" | custom-call | flops 1610612736 | bytes 4718592 | tf_op jit(solution)/shard_map/pallas_call | solution.py:142
  83.5 0.9 shard_map.175
  84.3 1.2 %collective-permute-start.27 = (bf16[256,256]{1,0:T(8,128)(2,1)S(1)}, bf16[256,256]{1,0:T(8,128)(2,1)S(1)}, u32[]{:S(2)}, u32[]{:S(2)}) collective-permute-start(bf16[256,256]{1,0:T(8,128)(2,1)S(1)} %get-tuple-element.182), channel_id=1, source_target_pairs={{0,8},{8,0},{16,24},{24,16},{1,9},{9,1},{17,25},{25,17},{2,10},{10... | collective-permute-start | bytes 393224 | tf_op jit(solution)/shard_map/ppermute | solution.py:19
  85.6 1.2 %collective-permute-start.24 = (bf16[128,1024]{1,0:T(8,128)(2,1)S(1)}, bf16[128,1024]{1,0:T(8,128)(2,1)S(1)}, u32[]{:S(2)}, u32[]{:S(2)}) collective-permute-start(bf16[128,1024]{1,0:T(8,128)(2,1)S(1)} %get-tuple-element.173), channel_id=1, source_target_pairs={{0,1},{1,0},{2,3},{3,2},{4,5},{5,4},{6,7},{7,6},{8,9},{9,8},{10,11... | collective-permute-start | bytes 786440 | tf_op jit(solution)/shard_map/ppermute | solution.py:19
  86.7 1.1 %collective-permute-start.25 = (bf16[128,1024]{1,0:T(8,128)(2,1)S(1)}, bf16[128,1024]{1,0:T(8,128)(2,1)S(1)}, u32[]{:S(2)}, u32[]{:S(2)}) collective-permute-start(bf16[128,1024]{1,0:T(8,128)(2,1)S(1)} %get-tuple-element.174), channel_id=1, source_target_pairs={{0,2},{1,3},{2,0},{3,1},{4,6},{5,7},{6,4},{7,5},{8,10},{9,11},{10,... | collective-permute-start | bytes 786440 | tf_op jit(solution)/shard_map/ppermute | solution.py:19
  87.8 1.2 %collective-permute-start.26 = (bf16[128,1024]{1,0:T(8,128)(2,1)S(1)}, bf16[128,1024]{1,0:T(8,128)(2,1)S(1)}, u32[]{:S(2)}, u32[]{:S(2)}) collective-permute-start(bf16[128,1024]{1,0:T(8,128)(2,1)S(1)} %get-tuple-element.175), channel_id=1, source_target_pairs={{0,3},{1,2},{2,1},{3,0},{4,7},{5,6},{6,5},{7,4},{8,11},{9,10},{10,... | collective-permute-start | bytes 786440 | tf_op jit(solution)/shard_map/ppermute | solution.py:19
  89.1 1.1 %collective-permute-done.27.refs_5_ = bf16[256,256]{1,0:T(8,128)(2,1)S(1)} collective-permute-done((bf16[256,256]{1,0:T(8,128)(2,1)S(1)}, bf16[256,256]{1,0:T(8,128)(2,1)S(1)}, u32[]{:S(2)}, u32[]{:S(2)}) %collective-permute-start.27) | collective-permute-done | bytes 131104 | tf_op jit(solution)/shard_map/ppermute | solution.py:19
  90.2 2.2 %collective-permute-start.28 = (bf16[256,256]{1,0:T(8,128)(2,1)S(1)}, bf16[256,256]{1,0:T(8,128)(2,1)S(1)}, u32[]{:S(2)}, u32[]{:S(2)}) collective-permute-start(bf16[256,256]{1,0:T(8,128)(2,1)S(1)} %pad_maximum_fusion), channel_id=1, source_target_pairs={{0,16},{8,24},{16,0},{24,8},{1,17},{9,25},{17,1},{25,9},{2,18},{10... | collective-permute-start | bytes 393224 | tf_op jit(solution)/shard_map/ppermute | solution.py:19
  92.4 3.5 %shard_map.177 = bf16[1024,1024]{1,0:T(8,128)(2,1)} custom-call(s32[3]{0:T(128)S(1)} %pad_add_fusion.where_ref, bf16[1024,512]{1,0:T(8,128)(2,1)S(1)} %shard_map.167.refs_0_, bf16[512,512]{1,0:T(8,128)(2,1)S(1)} %get-tuple-element.176.refs_4_.refs_0_.refs_1_, bf16[512,1024]{1,0:T(8,128)(2,1)S(1)} %bitcast.20), custom_call_target="tpu_custom_call" | custom-call | tf_op jit(solution)/shard_map/pallas_call | solution.py:142
  95.9 2.7 %shard_map.178 = (bf16[128,1024]{1,0:T(8,128)(2,1)}, f32[1,1024]{1,0:T(1,128)}, bf16[1024,128]{1,0:T(8,128)(2,1)}, bf16[128,1024]{1,0:T(8,128)(2,1)}) custom-call(s32[3]{0:T(128)S(1)} %pad_add_fusion.where_ref, f32[512,1024]{1,0:T(8,128)S(1)} %shard_map.172.refs_0_, bf16[512,512]{1,0:T(8,128)(2,1)S(1)} %get-tuple-element.188.refs_0_.refs_1_, ...), custom_call_target="tpu_custom_call" | custom-call | tf_op jit(solution)/shard_map/pallas_call | solution.py:142
  99.0 1.6 %collective-permute-done.26.refs_3_ = bf16[128,1024]{1,0:T(8,128)(2,1)S(1)} collective-permute-done((bf16[128,1024]{1,0:T(8,128)(2,1)S(1)}, bf16[128,1024]{1,0:T(8,128)(2,1)S(1)}, u32[]{:S(2)}, u32[]{:S(2)}) %collective-permute-start.26) | collective-permute-done | bytes 262176 | tf_op jit(solution)/shard_map/ppermute | solution.py:19
  100.6 1.4 %shard_map.176 = (bf16[128,1024]{1,0:T(8,128)(2,1)}, bf16[128,1024]{1,0:T(8,128)(2,1)}) custom-call(s32[3]{0:T(128)S(1)} %pad_add_fusion.where_ref, bf16[128,1024]{1,0:T(8,128)(2,1)S(1)} %get-tuple-element.172.refs_0_, bf16[128,1024]{1,0:T(8,128)(2,1)S(1)} %collective-permute-done.24.refs_1_, bf16[128,1024]{1,0:T(8,128)(2,1)S(1)} %collective-permute-done.25.refs_2_, ...), custom_call_target="tpu_custom_call" | custom-call | tf_op jit(solution)/shard_map/pallas_call | solution.py:142
  (48 shorter events, 8.7 us)
Async XLA Ops:
  0.6 18.4 %collective-permute-start.1 = (bf16[128,1024]{1,0:T(8,128)(2,1)}, bf16[128,1024]{1,0:T(8,128)(2,1)S(1)}, u32[]{:S(2)}, u32[]{:S(2)}) collective-permute-start(bf16[128,1024]{1,0:T(8,128)(2,1)} %bitcast.23), channel_id=1, source_target_pairs={{0,8},{8,0},{16,24},{24,16},{1,9},{9,1},{17,25},{25,17},{2,10},{10... | collective-permute-start | bytes 786440 | tf_op jit(solution)/shard_map/ppermute | solution.py:19
  3.7 15.3 %collective-permute-start = (bf16[128,1024]{1,0:T(8,128)(2,1)}, bf16[128,1024]{1,0:T(8,128)(2,1)S(1)}, u32[]{:S(2)}, u32[]{:S(2)}) collective-permute-start(bf16[128,1024]{1,0:T(8,128)(2,1)} %bitcast.24), channel_id=1, source_target_pairs={{0,16},{8,24},{16,0},{24,8},{1,17},{9,25},{17,1},{25,9},{2,18},{10... | collective-permute-start | bytes 786440 | tf_op jit(solution)/shard_map/ppermute | solution.py:19
  7.1 9.3 %collective-permute-start.2 = (bf16[128,128]{1,0:T(8,128)(2,1)S(1)}, bf16[128,128]{1,0:T(8,128)(2,1)S(1)}, u32[]{:S(2)}, u32[]{:S(2)}) collective-permute-start(bf16[128,128]{1,0:T(8,128)(2,1)S(1)} %broadcast_select_fusion.refs_4_), channel_id=1, source_target_pairs={{0,8},{8,0},{16,24},{24,16},{1,9},{9,1},{17,25},{25,17},{2,10},{10... | collective-permute-start | bytes 98312 | tf_op jit(solution)/shard_map/ppermute | solution.py:19
  7.6 23.2 %copy-start.3 = (bf16[1,128,1024]{2,1,0:T(8,128)(2,1)S(1)}, bf16[1,128,1024]{2,1,0:T(8,128)(2,1)}, u32[]{:S(2)}) copy-start(bf16[1,128,1024]{2,1,0:T(8,128)(2,1)} %param.9) | copy-start | bytes 786436
  11.0 21.2 %collective-permute-start.5 = (bf16[896,256]{1,0:T(8,128)(2,1)S(1)}, bf16[896,256]{1,0:T(8,128)(2,1)S(1)}, u32[]{:S(2)}, u32[]{:S(2)}) collective-permute-start(bf16[896,256]{1,0:T(8,128)(2,1)S(1)} %get-tuple-element.116), channel_id=1, source_target_pairs={{0,1},{1,0},{2,3},{3,2},{4,5},{5,4},{6,7},{7,6},{8,9},{9,8},{10,11... | collective-permute-start | bytes 1376264 | tf_op jit(solution)/shard_map/ppermute | solution.py:19
  12.5 21.0 %collective-permute-start.6 = (bf16[896,256]{1,0:T(8,128)(2,1)S(1)}, bf16[896,256]{1,0:T(8,128)(2,1)S(1)}, u32[]{:S(2)}, u32[]{:S(2)}) collective-permute-start(bf16[896,256]{1,0:T(8,128)(2,1)S(1)} %get-tuple-element.117), channel_id=1, source_target_pairs={{0,2},{1,3},{2,0},{3,1},{4,6},{5,7},{6,4},{7,5},{8,10},{9,11},{10,... | collective-permute-start | bytes 1376264 | tf_op jit(solution)/shard_map/ppermute | solution.py:19
  16.4 17.1 %collective-permute-start.7 = (bf16[896,256]{1,0:T(8,128)(2,1)S(1)}, bf16[896,256]{1,0:T(8,128)(2,1)S(1)}, u32[]{:S(2)}, u32[]{:S(2)}) collective-permute-start(bf16[896,256]{1,0:T(8,128)(2,1)S(1)} %get-tuple-element.118), channel_id=1, source_target_pairs={{0,3},{1,2},{2,1},{3,0},{4,7},{5,6},{6,5},{7,4},{8,11},{9,10},{10,... | collective-permute-start | bytes 1376264 | tf_op jit(solution)/shard_map/ppermute | solution.py:19
  19.1 5.8 %collective-permute-start.3 = (bf16[128,1024]{1,0:T(8,128)(2,1)}, bf16[128,1024]{1,0:T(8,128)(2,1)S(1)}, u32[]{:S(2)}, u32[]{:S(2)}) collective-permute-start(bf16[128,1024]{1,0:T(8,128)(2,1)} %bitcast.25), channel_id=1, source_target_pairs={{8,16},{16,8},{9,17},{17,9},{10,18},{18,10},{11,19},{19,11},{12,20... | collective-permute-start | bytes 786440 | tf_op jit(solution)/shard_map/ppermute | solution.py:38
  19.7 10.7 %collective-permute-start.4 = (bf16[128,1024]{1,0:T(8,128)(2,1)S(1)}, bf16[128,1024]{1,0:T(8,128)(2,1)S(1)}, u32[]{:S(2)}, u32[]{:S(2)}) collective-permute-start(bf16[128,1024]{1,0:T(8,128)(2,1)S(1)} %collective-permute-done.refs_2_), channel_id=1, source_target_pairs={{8,0},{16,24},{9,1},{17,25},{10,2},{18,26},{11,3},{19,27},{12,4},{... | collective-permute-start | bytes 786440 | tf_op jit(solution)/shard_map/ppermute | solution.py:39
  30.4 5.2 %collective-permute-start.8 = (bf16[256,128]{1,0:T(8,128)(2,1)S(1)}, bf16[256,128]{1,0:T(8,128)(2,1)S(1)}, u32[]{:S(2)}, u32[]{:S(2)}) collective-permute-start(bf16[256,128]{1,0:T(8,128)(2,1)S(1)} %pad_maximum_fusion.1), channel_id=1, source_target_pairs={{0,16},{8,24},{16,0},{24,8},{1,17},{9,25},{17,1},{25,9},{2,18},{10... | collective-permute-start | bytes 196616 | tf_op jit(solution)/shard_map/ppermute | solution.py:19
  35.7 17.5 %collective-permute-start.17 = (bf16[512,512]{1,0:T(8,128)(2,1)S(1)}, bf16[512,512]{1,0:T(8,128)(2,1)S(1)}, u32[]{:S(2)}, u32[]{:S(2)}) collective-permute-start(bf16[512,512]{1,0:T(8,128)(2,1)S(1)} %get-tuple-element.141), channel_id=1, source_target_pairs={{0,8},{8,0},{16,24},{24,16},{1,9},{9,1},{17,25},{25,17},{2,10},{10... | collective-permute-start | bytes 1572872 | tf_op jit(solution)/shard_map/ppermute | solution.py:19
  35.7 5.0 %collective-permute-start.9 = (bf16[512,128]{1,0:T(8,128)(2,1)S(1)}, bf16[512,128]{1,0:T(8,128)(2,1)S(1)}, u32[]{:S(2)}, u32[]{:S(2)}) collective-permute-start(bf16[512,128]{1,0:T(8,128)(2,1)S(1)} %get-tuple-element.122), channel_id=1, source_target_pairs={{0,1},{1,0},{2,3},{3,2},{4,5},{5,4},{6,7},{7,6},{8,9},{9,8},{10,11... | collective-permute-start | bytes 393224 | tf_op jit(solution)/shard_map/ppermute | solution.py:19
  36.3 5.0 %collective-permute-start.10 = (bf16[512,128]{1,0:T(8,128)(2,1)S(1)}, bf16[512,128]{1,0:T(8,128)(2,1)S(1)}, u32[]{:S(2)}, u32[]{:S(2)}) collective-permute-start(bf16[512,128]{1,0:T(8,128)(2,1)S(1)} %get-tuple-element.123), channel_id=1, source_target_pairs={{0,2},{1,3},{2,0},{3,1},{4,6},{5,7},{6,4},{7,5},{8,10},{9,11},{10,... | collective-permute-start | bytes 393224 | tf_op jit(solution)/shard_map/ppermute | solution.py:19
  37.1 5.9 %collective-permute-start.11 = (bf16[512,128]{1,0:T(8,128)(2,1)S(1)}, bf16[512,128]{1,0:T(8,128)(2,1)S(1)}, u32[]{:S(2)}, u32[]{:S(2)}) collective-permute-start(bf16[512,128]{1,0:T(8,128)(2,1)S(1)} %get-tuple-element.124), channel_id=1, source_target_pairs={{0,3},{1,2},{2,1},{3,0},{4,7},{5,6},{6,5},{7,4},{8,11},{9,10},{10,... | collective-permute-start | bytes 393224 | tf_op jit(solution)/shard_map/ppermute | solution.py:19
  43.6 7.3 %collective-permute-start.12 = (bf16[512,128]{1,0:T(8,128)(2,1)S(1)}, bf16[512,128]{1,0:T(8,128)(2,1)S(1)}, u32[]{:S(2)}, u32[]{:S(2)}) collective-permute-start(bf16[512,128]{1,0:T(8,128)(2,1)S(1)} %shard_map.163.refs_0_), channel_id=1, source_target_pairs={{0,16},{8,24},{16,0},{24,8},{1,17},{9,25},{17,1},{25,9},{2,18},{10... | collective-permute-start | bytes 393224 | tf_op jit(solution)/shard_map/ppermute | solution.py:19
  46.7 11.8 %collective-permute-start.16 = (bf16[1024,128]{1,0:T(8,128)(2,1)S(1)}, bf16[1024,128]{1,0:T(8,128)(2,1)S(1)}, u32[]{:S(2)}, u32[]{:S(2)}) collective-permute-start(bf16[1024,128]{1,0:T(8,128)(2,1)S(1)} %get-tuple-element.139.refs_4_), channel_id=1, source_target_pairs={{0,3},{1,2},{2,1},{3,0},{4,7},{5,6},{6,5},{7,4},{8,11},{9,10},{10,... | collective-permute-start | bytes 786440 | tf_op jit(solution)/shard_map/ppermute | solution.py:19
  49.2 9.3 %collective-permute-start.15 = (bf16[1024,128]{1,0:T(8,128)(2,1)S(1)}, bf16[1024,128]{1,0:T(8,128)(2,1)S(1)}, u32[]{:S(2)}, u32[]{:S(2)}) collective-permute-start(bf16[1024,128]{1,0:T(8,128)(2,1)S(1)} %get-tuple-element.139.refs_4_), channel_id=1, source_target_pairs={{0,2},{1,3},{2,0},{3,1},{4,6},{5,7},{6,4},{7,5},{8,10},{9,11},{10,... | collective-permute-start | bytes 786440 | tf_op jit(solution)/shard_map/ppermute | solution.py:19
  49.7 8.8 %collective-permute-start.14 = (bf16[1024,128]{1,0:T(8,128)(2,1)S(1)}, bf16[1024,128]{1,0:T(8,128)(2,1)S(1)}, u32[]{:S(2)}, u32[]{:S(2)}) collective-permute-start(bf16[1024,128]{1,0:T(8,128)(2,1)S(1)} %get-tuple-element.139.refs_4_), channel_id=1, source_target_pairs={{0,1},{1,0},{2,3},{3,2},{4,5},{5,4},{6,7},{7,6},{8,9},{9,8},{10,11... | collective-permute-start | bytes 786440 | tf_op jit(solution)/shard_map/ppermute | solution.py:19
  51.5 7.0 %collective-permute-start.13 = (bf16[512,128]{1,0:T(8,128)(2,1)S(1)}, bf16[512,128]{1,0:T(8,128)(2,1)S(1)}, u32[]{:S(2)}, u32[]{:S(2)}) collective-permute-start(bf16[512,128]{1,0:T(8,128)(2,1)S(1)} %shard_map.164.refs_0_), channel_id=1, source_target_pairs={{0,8},{8,0},{16,24},{24,16},{1,9},{9,1},{17,25},{25,17},{2,10},{10... | collective-permute-start | bytes 393224 | tf_op jit(solution)/shard_map/ppermute | solution.py:19
  59.1 12.3 %collective-permute-start.22 = (bf16[256,512]{1,0:T(8,128)(2,1)S(1)}, bf16[256,512]{1,0:T(8,128)(2,1)S(1)}, u32[]{:S(2)}, u32[]{:S(2)}) collective-permute-start(bf16[256,512]{1,0:T(8,128)(2,1)S(1)} %get-tuple-element.151), channel_id=1, source_target_pairs={{0,16},{8,24},{16,0},{24,8},{1,17},{9,25},{17,1},{25,9},{2,18},{10... | collective-permute-start | bytes 786440 | tf_op jit(solution)/shard_map/ppermute | solution.py:19
  60.0 5.9 %collective-permute-start.20 = (bf16[512,128]{1,0:T(8,128)(2,1)S(1)}, bf16[512,128]{1,0:T(8,128)(2,1)S(1)}, u32[]{:S(2)}, u32[]{:S(2)}) collective-permute-start(bf16[512,128]{1,0:T(8,128)(2,1)S(1)} %shard_map.168.refs_0_), channel_id=1, source_target_pairs={{0,3},{1,2},{2,1},{3,0},{4,7},{5,6},{6,5},{7,4},{8,11},{9,10},{10,... | collective-permute-start | bytes 393224 | tf_op jit(solution)/shard_map/ppermute | solution.py:19
  62.9 5.0 %collective-permute-start.19 = (bf16[512,128]{1,0:T(8,128)(2,1)S(1)}, bf16[512,128]{1,0:T(8,128)(2,1)S(1)}, u32[]{:S(2)}, u32[]{:S(2)}) collective-permute-start(bf16[512,128]{1,0:T(8,128)(2,1)S(1)} %shard_map.168.refs_0_), channel_id=1, source_target_pairs={{0,2},{1,3},{2,0},{3,1},{4,6},{5,7},{6,4},{7,5},{8,10},{9,11},{10,... | collective-permute-start | bytes 393224 | tf_op jit(solution)/shard_map/ppermute | solution.py:19
  62.9 5.0 %collective-permute-start.18 = (bf16[512,128]{1,0:T(8,128)(2,1)S(1)}, bf16[512,128]{1,0:T(8,128)(2,1)S(1)}, u32[]{:S(2)}, u32[]{:S(2)}) collective-permute-start(bf16[512,128]{1,0:T(8,128)(2,1)S(1)} %shard_map.168.refs_0_), channel_id=1, source_target_pairs={{0,1},{1,0},{2,3},{3,2},{4,5},{5,4},{6,7},{7,6},{8,9},{9,8},{10,11... | collective-permute-start | bytes 393224 | tf_op jit(solution)/shard_map/ppermute | solution.py:19
  70.0 2.8 %collective-permute-start.21 = (bf16[512,512]{1,0:T(8,128)(2,1)S(1)}, bf16[512,512]{1,0:T(8,128)(2,1)S(1)}, u32[]{:S(2)}, u32[]{:S(2)}) collective-permute-start(bf16[512,512]{1,0:T(8,128)(2,1)S(1)} %get-tuple-element.149), channel_id=1, source_target_pairs={{0,4},{1,5},{2,6},{3,7},{8,12},{9,13},{10,14},{11,15},{16,20},{17,... | collective-permute-start | bytes 1572872 | tf_op jit(solution)/shard_map/ppermute | solution.py:25
  72.8 4.0 %copy-start = (bf16[1,512,1024]{2,1,0:T(8,128)(2,1)S(1)}, bf16[1,512,1024]{2,1,0:T(8,128)(2,1)}, u32[]{:S(2)}) copy-start(bf16[1,512,1024]{2,1,0:T(8,128)(2,1)} %param.12) | copy-start | bytes 3145732
  72.8 4.0 %copy-start.4 = (bf16[1,128,1024]{2,1,0:T(8,128)(2,1)S(1)}, bf16[1,128,1024]{2,1,0:T(8,128)(2,1)}, u32[]{:S(2)}) copy-start(bf16[1,128,1024]{2,1,0:T(8,128)(2,1)} %param.15) | copy-start | bytes 786436
  75.3 3.8 %collective-permute-start.23 = (bf16[512,512]{1,0:T(8,128)(2,1)S(1)}, bf16[512,512]{1,0:T(8,128)(2,1)S(1)}, u32[]{:S(2)}, u32[]{:S(2)}) collective-permute-start(bf16[512,512]{1,0:T(8,128)(2,1)S(1)} %get-tuple-element.158), channel_id=1, source_target_pairs={{4,0},{5,1},{6,2},{7,3},{12,8},{13,9},{14,10},{15,11},{20,16},{21,... | collective-permute-start | bytes 1572872 | tf_op jit(solution)/shard_map/ppermute | solution.py:25
  79.1 1.9 %copy-start.2 = (bf16[1,1024,1024]{2,1,0:T(8,128)(2,1)S(1)}, bf16[1,1024,1024]{2,1,0:T(8,128)(2,1)}, u32[]{:S(2)}) copy-start(bf16[1,1024,1024]{2,1,0:T(8,128)(2,1)} %param.10) | copy-start | bytes 6291460
  81.0 11.4 %copy-start.1 = (bf16[1,512,1024]{2,1,0:T(8,128)(2,1)S(1)}, bf16[1,512,1024]{2,1,0:T(8,128)(2,1)}, u32[]{:S(2)}) copy-start(bf16[1,512,1024]{2,1,0:T(8,128)(2,1)} %param.11) | copy-start | bytes 3145732
  84.3 5.9 %collective-permute-start.27 = (bf16[256,256]{1,0:T(8,128)(2,1)S(1)}, bf16[256,256]{1,0:T(8,128)(2,1)S(1)}, u32[]{:S(2)}, u32[]{:S(2)}) collective-permute-start(bf16[256,256]{1,0:T(8,128)(2,1)S(1)} %get-tuple-element.182), channel_id=1, source_target_pairs={{0,8},{8,0},{16,24},{24,16},{1,9},{9,1},{17,25},{25,17},{2,10},{10... | collective-permute-start | bytes 393224 | tf_op jit(solution)/shard_map/ppermute | solution.py:19
  85.6 13.1 %collective-permute-start.24 = (bf16[128,1024]{1,0:T(8,128)(2,1)S(1)}, bf16[128,1024]{1,0:T(8,128)(2,1)S(1)}, u32[]{:S(2)}, u32[]{:S(2)}) collective-permute-start(bf16[128,1024]{1,0:T(8,128)(2,1)S(1)} %get-tuple-element.173), channel_id=1, source_target_pairs={{0,1},{1,0},{2,3},{3,2},{4,5},{5,4},{6,7},{7,6},{8,9},{9,8},{10,11... | collective-permute-start | bytes 786440 | tf_op jit(solution)/shard_map/ppermute | solution.py:19
  86.7 12.3 %collective-permute-start.25 = (bf16[128,1024]{1,0:T(8,128)(2,1)S(1)}, bf16[128,1024]{1,0:T(8,128)(2,1)S(1)}, u32[]{:S(2)}, u32[]{:S(2)}) collective-permute-start(bf16[128,1024]{1,0:T(8,128)(2,1)S(1)} %get-tuple-element.174), channel_id=1, source_target_pairs={{0,2},{1,3},{2,0},{3,1},{4,6},{5,7},{6,4},{7,5},{8,10},{9,11},{10,... | collective-permute-start | bytes 786440 | tf_op jit(solution)/shard_map/ppermute | solution.py:19
  87.8 12.8 %collective-permute-start.26 = (bf16[128,1024]{1,0:T(8,128)(2,1)S(1)}, bf16[128,1024]{1,0:T(8,128)(2,1)S(1)}, u32[]{:S(2)}, u32[]{:S(2)}) collective-permute-start(bf16[128,1024]{1,0:T(8,128)(2,1)S(1)} %get-tuple-element.175), channel_id=1, source_target_pairs={{0,3},{1,2},{2,1},{3,0},{4,7},{5,6},{6,5},{7,4},{8,11},{9,10},{10,... | collective-permute-start | bytes 786440 | tf_op jit(solution)/shard_map/ppermute | solution.py:19
  90.2 5.7 %copy-start.5 = (bf16[1,1024,128]{2,1,0:T(8,128)(2,1)S(1)}, bf16[1,1024,128]{2,1,0:T(8,128)(2,1)}, u32[]{:S(2)}) copy-start(bf16[1,1024,128]{2,1,0:T(8,128)(2,1)} %param.14) | copy-start | bytes 786436
  90.2 5.7 %copy-start.6 = (f32[1,1024]{1,0:T(1,128)S(1)}, f32[1,1024]{1,0:T(1,128)}, u32[]{:S(2)}) copy-start(f32[1,1024]{1,0:T(1,128)} %refs_7_.1) | copy-start | bytes 12292
  90.2 10.4 %collective-permute-start.28 = (bf16[256,256]{1,0:T(8,128)(2,1)S(1)}, bf16[256,256]{1,0:T(8,128)(2,1)S(1)}, u32[]{:S(2)}, u32[]{:S(2)}) collective-permute-start(bf16[256,256]{1,0:T(8,128)(2,1)S(1)} %pad_maximum_fusion), channel_id=1, source_target_pairs={{0,16},{8,24},{16,0},{24,8},{1,17},{9,25},{17,1},{25,9},{2,18},{10... | collective-permute-start | bytes 393224 | tf_op jit(solution)/shard_map/ppermute | solution.py:19

commit v13 on v12

--- a/solution.py
+++ b/solution.py
@@ -306,7 +306,31 @@
     return inner, jnp.concatenate(returned, axis=1).astype(bf16)
 
 
-def first_kernel(width, where, ins, outs, scratch):
+def early_kernel(where, ins, outs, scratch):
+    payloads, (products,) = ins
+    relay = products.shape[1] // 2
+    rows = outs[0].shape[0] - relay
+    for k, payload in enumerate(payloads):
+        cols = slice(k * relay, (k + 1) * relay)
+        end = payload[payload.shape[0] - rows :, :]
+        outs[0][:rows, cols] = dot(end, products[cols, relay:], NT).astype(bf16)
+        outs[0][rows:, cols] = products[cols, :relay]
+
+
+def split(column, lane, first):
+    high = column.astype(bf16).astype(f32)
+    middle = (column - high).astype(bf16).astype(f32)
+    low = column - high - middle
+    result = jnp.where(lane == first, high, 0.0)
+    result = jnp.where(lane == first + 1, middle, result)
+    return jnp.where(lane == first + 2, low, result)
+
+
+def joined(lanes, first):
+    return jnp.sum(lanes[:, first : first + 3].astype(f32), axis=1, keepdims=True)
+
+
+def first_kernel(width, swapped, where, ins, outs, scratch):
     mix_blocks, payloads, (products, weights) = ins
     mix, ends, mix_gram, mix_recv, mix_send, square, sent = outs
     (gram,) = scratch
@@ -336,9 +360,72 @@
         mixed, unscaled, row_scale = forward(
             ends[at, :], in_recv, in_send, sums, products[...], width
         )
-        sent[at, :] = (row_scale * unscaled).astype(bf16)
+        offer = (row_scale * unscaled).astype(bf16)
+        if not swapped:
+            sent[at, :] = offer
+            return
+        wide = parts * relay
+        sent[at, :wide] = jnp.where(where[2] == 0, offer, in_recv.astype(bf16))
+        dots = jnp.sum(ends[at, :].astype(f32) * in_send, axis=1, keepdims=True)
+        lane = lax.broadcasted_iota(jnp.int32, (sums.shape[0], relay), 1)
+        sent[at, wide:] = (split(sums, lane, 0) + split(dots, lane, 3)).astype(bf16)
 
     by_rows(mix.shape[0], step)
+
+
+def meet_kernel(width, where, ins, outs, scratch):
+    ((got, early, ends, mix_recv, mix_send, mix_gram, square, products, weights),) = ins
+    received_out, incoming_out, scale_out, inner_out, code_grad, sent_out, returned_out = outs
+    relay = products.shape[1] // 2
+    wide = ends.shape[1]
+    rows = ends.shape[0]
+    first = where[2] == 0
+
+    def step(at):
+        here = ends[at, :]
+        given = got[at, :wide]
+        received = jnp.where(first, here, given)
+        mixed, unscaled, row_scale = forward(
+            received, mix_recv[at, :], mix_send[at, :], square[at, :], products[...], width
+        )
+        sent = (row_scale * unscaled).astype(bf16)
+        sent_rows = sent.astype(f32)
+        other_recv = given.astype(f32)
+        back = early[at, :].astype(f32)
+        other_mixed = []
+        for k in range(wide // relay):
+            cols = slice(k * relay, (k + 1) * relay)
+            other_mixed.append(other_recv[:, cols] + dot(sent[:, cols], early[rows:, cols], NN))
+        other_mixed = jnp.concatenate(other_mixed, axis=1)
+        lanes = got[at, wide:]
+        totals = joined(lanes, 0) + jnp.sum(
+            sent_rows * (other_recv + other_mixed), axis=1, keepdims=True
+        )
+        scale = lax.rsqrt(jnp.maximum(totals, 0.0) / width + epsilon)
+        dots = joined(lanes, 3) + jnp.sum(sent_rows * back, axis=1, keepdims=True)
+        inner = scale * dots / width
+        returned = (scale * (back - scale * inner * other_mixed)).astype(bf16)
+        incoming = jnp.where(first, returned, here)
+        inner, returned = backward(incoming, mixed, unscaled, row_scale, products[...], width)
+        in_mixed = mix_gram[at, :] + dot(received, weights[:, :wide], NT)
+        back = dot(incoming, weights[:, wide:], NT)
+        code_grad[at, :] = (row_scale * (back - row_scale * inner * in_mixed)).astype(bf16)
+        received_out[at, :] = received[:, :relay]
+        incoming_out[at, :] = incoming[:, :relay]
+        scale_out[at, :] = row_scale
+        inner_out[at, :] = inner
+        tokens = min(sent_out.shape[0], sent.shape[0])
+        if isinstance(at, slice):
+            sent_out[...] = sent[:tokens, :relay]
+            returned_out[...] = returned[:tokens, :relay]
+        else:
+
+            @pl.when(at.start == 0)
+            def _():
+                sent_out[...] = sent[:tokens, :relay]
+                returned_out[...] = returned[:tokens, :relay]
+
+    by_rows(rows, step)
 
 
 def forward_kernel(width, turn, last, where, ins, outs, scratch):
@@ -455,19 +542,17 @@
         copy.wait()
 
 
-def normed_kernel(where, ins, outs, scratch):
-    ((mix, received, row_scale, dec, recv),) = ins
-    relay = recv.shape[0]
+def attention_kernel(where, ins, outs, scratch):
+    ((mix, dec),) = ins
 
     def step(at):
-        mixed = dot(mix[at, :], dec[...], NN) + dot(received[at, :relay], recv[...], NN)
-        outs[0][at, :] = mixed * row_scale[at, :]
+        outs[0][at, :] = dot(mix[at, :], dec[...], NN)
 
     by_rows(mix.shape[0], step)
 
 
 def feature_kernel(where, ins, outs, scratch):
-    ((normed_rows, mix_cols, received, incoming, row_scale, inner, send, gain),) = ins
+    ((attention, mix_cols, received, incoming, row_scale, inner, recv, send, gain),) = ins
     sums = scratch
     relay = send.shape[1]
     size = sums[0].shape[0]
@@ -480,7 +565,8 @@
     def step(at):
         received_here = received[at, :relay]
         incoming_here = incoming[at, :relay]
-        normed = normed_rows[at, :]
+        normed = attention[at, :] + dot(received_here, recv[...], NN)
+        normed = normed * row_scale[at, :]
         out_rows = (normed * gain[...]).astype(bf16)
         grad_norm = dot(incoming_here, send[...], NT)
         grad_mixed = row_scale[at, :] * (grad_norm * gain[...] - normed * inner[at, :])
@@ -490,7 +576,7 @@
         sums[2][...] += dot(out_rows, incoming_here, TN)
         sums[3][...] += dot(received_here, grad_mixed, TN)
 
-    by_rows(normed_rows.shape[0], step)
+    by_rows(attention.shape[0], step)
     for out, ref in zip(outs, sums):
         out[...] = ref[...].astype(out.dtype)
 
@@ -578,10 +664,13 @@
     mix_block = group_sum(code_block, [*payloads, *fold_terms, turned], "dp", where)
     mix_block, fold_terms = lax.optimization_barrier((mix_block, fold_terms))
     mix_blocks = gathered(mix_block, "tensor")
+    if sections == 2:
+        (early,) = run(early_kernel, [like((rows + relay, wide))], where, [payloads, (products,)])
+        early = move(early, "pipe", -1)
 
     square_flops = 2 * rows * codes * codes
     mix, ends, mix_gram, mix_recv, mix_send, square, sent = run(
-        functools.partial(first_kernel, width),
+        functools.partial(first_kernel, width, sections == 2),
         [
             like((rows, codes)),
             like((rows, wide)),
@@ -589,7 +678,7 @@
             like((rows, wide), f32),
             like((rows, wide), f32),
             like((rows, 1), f32),
-            like((rows, wide)),
+            like((rows, wide + relay if sections == 2 else wide)),
         ],
         where,
         [mix_blocks, payloads, (products, weights)],
@@ -605,62 +694,74 @@
             fold_terms = halved(kept, other, head_cols // groups, where)
         else:
             fold_rows = total([kept, other], where, flops=1 << 33)
-    received = ends
-    for turn in range(1, sections):
-        last = turn == sections - 1
-        shapes = [like((rows, wide)), like((rows, wide))]
-        if last:
-            shapes += [like((rows, wide), f32)] * 2 + [like((rows, 1), f32), like((rows, wide))]
-            shapes += [like((tokens, relay))]
-        moved = move(sent, "pipe", 1)
-        if turn == 1:
-            moved, fold_rows = lax.optimization_barrier((moved, fold_rows))
-        results = run(
-            functools.partial(forward_kernel, width, turn, last),
-            shapes,
+    (attention,) = run(
+        attention_kernel, [like((rows, features), f32)], where, [(mix, dec)]
+    )
+    if sections == 2:
+        got = lax.ppermute(sent, "pipe", [(0, 1), (1, 0)])
+        got, fold_rows, attention = lax.optimization_barrier((got, fold_rows, attention))
+        received, incoming, row_scale, inner, code_grad, sent, returned = run(
+            functools.partial(meet_kernel, width),
+            [
+                like((rows, relay)),
+                like((rows, relay)),
+                like((rows, 1), f32),
+                like((rows, 1), f32),
+                like((rows, codes)),
+                like((tokens, relay)),
+                like((tokens, relay)),
+            ],
             where,
-            [(moved, received, ends, mix_recv, mix_send, square, products)],
-            flops=square_flops,
+            [(got, early, ends, mix_recv, mix_send, mix_gram, square, products, weights)],
+            flops=4 * square_flops,
         )
-        received, sent = results[:2]
-    mixed, unscaled, row_scale, returned, sent = results[2:]
-    (normed,) = run(
-        normed_kernel,
-        [like((rows, features), f32)],
-        where,
-        [(mix, received, row_scale, dec, recv)],
-    )
-    incoming = ends
-    for turn in range(1, sections):
-        last = turn == sections - 1
-        shapes = [like((rows, wide)), like((rows, wide))]
-        if last:
-            shapes += [like((rows, 1), f32), like((rows, codes))]
-            shapes += [like((tokens, relay))]
-        moved = move(returned, "pipe", -1)
-        if turn == 1:
-            moved, normed = lax.optimization_barrier((moved, normed))
-        results = run(
-            functools.partial(backward_kernel, width, sections - 1 - turn, last),
-            shapes,
-            where,
-            [
-                (
-                    moved,
-                    incoming,
-                    received,
-                    mixed,
-                    unscaled,
-                    row_scale,
-                    mix_gram,
-                    products,
-                    weights,
-                )
-            ],
-            flops=3 * square_flops,
-        )
-        incoming, returned = results[:2]
-    inner, code_grad, returned = results[2:]
+    else:
+        received = ends
+        for turn in range(1, sections):
+            last = turn == sections - 1
+            shapes = [like((rows, wide)), like((rows, wide))]
+            if last:
+                shapes += [like((rows, wide), f32)] * 2 + [like((rows, 1), f32), like((rows, wide))]
+                shapes += [like((tokens, relay))]
+            moved = move(sent, "pipe", 1)
+            results = run(
+                functools.partial(forward_kernel, width, turn, last),
+                shapes,
+                where,
+                [(moved, received, ends, mix_recv, mix_send, square, products)],
+                flops=square_flops,
+            )
+            received, sent = results[:2]
+        mixed, unscaled, row_scale, returned, sent = results[2:]
+        incoming = ends
+        for turn in range(1, sections):
+            last = turn == sections - 1
+            shapes = [like((rows, wide)), like((rows, wide))]
+            if last:
+                shapes += [like((rows, 1), f32), like((rows, codes))]
+                shapes += [like((tokens, relay))]
+            moved = move(returned, "pipe", -1)
+            results = run(
+                functools.partial(backward_kernel, width, sections - 1 - turn, last),
+                shapes,
+                where,
+                [
+                    (
+                        moved,
+                        incoming,
+                        received,
+                        mixed,
+                        unscaled,
+                        row_scale,
+                        mix_gram,
+                        products,
+                        weights,
+                    )
+                ],
+                flops=3 * square_flops,
+            )
+            incoming, returned = results[:2]
+        inner, code_grad, returned = results[2:]
 
     enc_blocks = run(
         head_kernel,
@@ -701,12 +802,13 @@
         where,
         [
             (
-                normed,
+                attention,
                 mix if codes // groups % 128 == 0 else block(mix, "dp", 1),
                 received,
                 incoming,
                 row_scale,
                 inner,
+                recv,
                 send,
                 gain,
             )

time: 102 us -> 96.7 us (0.948)
  waiting for transfers between devices: 29.8 us -> 25.7 us
  starting transfers between devices: 38.2 us -> 36.9 us
    ppermute x25, waiting for transfers between devices: 22.6 us -> 19.9 us  [swap(): lax.ppermute(shard, axis, [(i, i ^ by) for i in range(lax.axis_size(axis))])]
    ppermute x2 -> x1, waiting for transfers between devices: 1.66 us -> 0.01 us  [move(): return lax.ppermute(shard, axis, pairs)]
    ppermute x2 -> x1, starting transfers between devices: 2.78 us -> 1.47 us  [move(): return lax.ppermute(shard, axis, pairs)]
  transfers between devices with their start and end apart: 29 -> 29, of which waited for: 16 -> 14; matrix products, arithmetic and copies ran while one was open for 1% -> 1% of each run, Pallas kernels for 22% -> 24%
where the time goes in v13:
time: 96.7 us; the launch traced here: 96.4 us
  starting transfers between devices  36.9 us (38%)
  Pallas kernels  32 us (33%)
  waiting for transfers between devices  25.7 us (27%)
    ppermute x25, starting transfers between devices, swap(): lax.ppermute(shard, axis, [(i, i ^ by) for i in range(lax.axis_size(axis))])  33.4 us
    pallas_call x19, Pallas kernels, run(): pl.pallas_call(body, out_shape=[jax.ShapeDtypeStruct(r.shape, r.dtype) fo...  32 us
    ppermute x25, waiting for transfers between devices, swap(): lax.ppermute(shard, axis, [(i, i ^ by) for i in range(lax.axis_size(axis))])  19.9 us
    ppermute x1, waiting for transfers between devices, line_gathered(): passed = lax.ppermute(far, axis, [(1, 0), (2, 3)])  5.61 us
  transfers between devices with their start and end apart: 29, of which 14 were waited for; matrix products, arithmetic and copies ran while one was open for 1% of the time, Pallas kernels for 24%

profile of v13, /device:TPU:0, one launch (start us, length us, event | category | flops | bytes accessed | tf_op | source)
XLA Modules:
  0.0 96.4 jit_solution(14470519384600513637)
XLA Ops:
  0.6 3.1 %collective-permute-start.1 = (bf16[128,1024]{1,0:T(8,128)(2,1)}, bf16[128,1024]{1,0:T(8,128)(2,1)S(1)}, u32[]{:S(2)}, u32[]{:S(2)}) collective-permute-start(bf16[128,1024]{1,0:T(8,128)(2,1)} %bitcast.23), channel_id=1, source_target_pairs={{0,8},{8,0},{16,24},{24,16},{1,9},{9,1},{17,25},{25,17},{2,10},{10... | collective-permute-start | bytes 786440 | tf_op jit(solution)/shard_map/ppermute | solution.py:19
  3.7 2.6 %collective-permute-start = (bf16[128,1024]{1,0:T(8,128)(2,1)}, bf16[128,1024]{1,0:T(8,128)(2,1)S(1)}, u32[]{:S(2)}, u32[]{:S(2)}) collective-permute-start(bf16[128,1024]{1,0:T(8,128)(2,1)} %bitcast.24), channel_id=1, source_target_pairs={{0,16},{8,24},{16,0},{24,8},{1,17},{9,25},{17,1},{25,9},{2,18},{10... | collective-permute-start | bytes 786440 | tf_op jit(solution)/shard_map/ppermute | solution.py:19
  6.3 0.8 broadcast_select_fusion.refs_4_
  7.6 3.4 %shard_map.161 = (bf16[896,256]{1,0:T(8,128)(2,1)S(1)}, bf16[896,256]{1,0:T(8,128)(2,1)S(1)}, bf16[896,256]{1,0:T(8,128)(2,1)S(1)}, bf16[896,256]{1,0:T(8,128)(2,1)S(1)}) custom-call(s32[3]{0:T(128)S(1)} %pad_add_fusion.where_ref, bf16[512,1024]{1,0:T(8,128)(2,1)} %bitcast.19, bf16[128,1024]{1,0:T(8,128)(2,1)} %bitcast.29, bf16[1024,128]{1,0:T(8,128)(2,1)} %bitcast.31, ...), custom_call_target="tpu_custom_call" | custom-call | tf_op jit(solution)/shard_map/pallas_call | solution.py:142
  11.0 1.6 %collective-permute-start.5 = (bf16[896,256]{1,0:T(8,128)(2,1)S(1)}, bf16[896,256]{1,0:T(8,128)(2,1)S(1)}, u32[]{:S(2)}, u32[]{:S(2)}) collective-permute-start(bf16[896,256]{1,0:T(8,128)(2,1)S(1)} %get-tuple-element.112), channel_id=1, source_target_pairs={{0,1},{1,0},{2,3},{3,2},{4,5},{5,4},{6,7},{7,6},{8,9},{9,8},{10,11... | collective-permute-start | bytes 1376264 | tf_op jit(solution)/shard_map/ppermute | solution.py:19
  12.5 1.5 %collective-permute-start.6 = (bf16[896,256]{1,0:T(8,128)(2,1)S(1)}, bf16[896,256]{1,0:T(8,128)(2,1)S(1)}, u32[]{:S(2)}, u32[]{:S(2)}) collective-permute-start(bf16[896,256]{1,0:T(8,128)(2,1)S(1)} %get-tuple-element.113), channel_id=1, source_target_pairs={{0,2},{1,3},{2,0},{3,1},{4,6},{5,7},{6,4},{7,5},{8,10},{9,11},{10,... | collective-permute-start | bytes 1376264 | tf_op jit(solution)/shard_map/ppermute | solution.py:19
  14.1 2.4 %collective-permute-done.2.refs_5_ = bf16[128,128]{1,0:T(8,128)(2,1)S(1)} collective-permute-done((bf16[128,128]{1,0:T(8,128)(2,1)S(1)}, bf16[128,128]{1,0:T(8,128)(2,1)S(1)}, u32[]{:S(2)}, u32[]{:S(2)}) %collective-permute-start.2) | collective-permute-done | bytes 32800 | tf_op jit(solution)/shard_map/ppermute | solution.py:19
  16.4 2.6 %collective-permute-start.7 = (bf16[896,256]{1,0:T(8,128)(2,1)S(1)}, bf16[896,256]{1,0:T(8,128)(2,1)S(1)}, u32[]{:S(2)}, u32[]{:S(2)}) collective-permute-start(bf16[896,256]{1,0:T(8,128)(2,1)S(1)} %get-tuple-element.114), channel_id=1, source_target_pairs={{0,3},{1,2},{2,1},{3,0},{4,7},{5,6},{6,5},{7,4},{8,11},{9,10},{10,... | collective-permute-start | bytes 1376264 | tf_op jit(solution)/shard_map/ppermute | solution.py:19
  19.1 0.7 collective-permute-start.3
  19.7 1.3 %collective-permute-start.4 = (bf16[128,1024]{1,0:T(8,128)(2,1)S(1)}, bf16[128,1024]{1,0:T(8,128)(2,1)S(1)}, u32[]{:S(2)}, u32[]{:S(2)}) collective-permute-start(bf16[128,1024]{1,0:T(8,128)(2,1)S(1)} %collective-permute-done.refs_2_), channel_id=1, source_target_pairs={{8,0},{16,24},{9,1},{17,25},{10,2},{18,26},{11,3},{19,27},{12,4},{... | collective-permute-start | bytes 786440 | tf_op jit(solution)/shard_map/ppermute | solution.py:39
  21.0 3.8 %shard_map.160 = (bf16[1024,512]{1,0:T(8,128)(2,1)S(1)}, bf16[512,512]{1,0:T(8,128)(2,1)S(1)}, bf16[512,512]{1,0:T(8,128)(2,1)S(1)}) custom-call(s32[3]{0:T(128)S(1)} %pad_add_fusion.where_ref, bf16[1024,1024]{1,0:T(8,128)(2,1)} %bitcast.21, bf16[512,1024]{1,0:T(8,128)(2,1)} %bitcast.17), custom_call_target="tpu_custom_call" | custom-call | tf_op jit(solution)/shard_map/pallas_call | solution.py:142
  24.8 5.6 %collective-permute-done.4.refs_4_ = bf16[128,1024]{1,0:T(8,128)(2,1)S(1)} collective-permute-done((bf16[128,1024]{1,0:T(8,128)(2,1)S(1)}, bf16[128,1024]{1,0:T(8,128)(2,1)S(1)}, u32[]{:S(2)}, u32[]{:S(2)}) %collective-permute-start.4) | collective-permute-done | bytes 262176 | tf_op jit(solution)/shard_map/ppermute | solution.py:39
  30.8 1.4 %shard_map.162 = (bf16[512,128]{1,0:T(8,128)(2,1)S(1)}, bf16[512,128]{1,0:T(8,128)(2,1)S(1)}, bf16[512,128]{1,0:T(8,128)(2,1)S(1)}, bf16[512,128]{1,0:T(8,128)(2,1)S(1)}, bf16[128,1024]{1,0:T(8,128)(2,1)S(1)}) custom-call(s32[3]{0:T(128)S(1)} %pad_add_fusion.where_ref, bf16[128,1024]{1,0:T(8,128)(2,1)S(1)} %bitcast.26, ...), custom_call_target="tpu_custom_call" | custom-call | flops 536870912 | bytes 3145728 | tf_op jit(solution)/shard_map/pallas_call | solution.py:142
  32.2 1.3 %collective-permute-done.6.refs_2_ = bf16[896,256]{1,0:T(8,128)(2,1)S(1)} collective-permute-done((bf16[896,256]{1,0:T(8,128)(2,1)S(1)}, bf16[896,256]{1,0:T(8,128)(2,1)S(1)}, u32[]{:S(2)}, u32[]{:S(2)}) %collective-permute-start.6) | collective-permute-done | bytes 458784 | tf_op jit(solution)/shard_map/ppermute | solution.py:19
  33.5 2.1 %collective-permute-done.8.refs_6_ = bf16[256,128]{1,0:T(8,128)(2,1)S(1)} collective-permute-done((bf16[256,128]{1,0:T(8,128)(2,1)S(1)}, bf16[256,128]{1,0:T(8,128)(2,1)S(1)}, u32[]{:S(2)}, u32[]{:S(2)}) %collective-permute-start.8) | collective-permute-done | bytes 65568 | tf_op jit(solution)/shard_map/ppermute | solution.py:19
  35.7 0.7 collective-permute-start.9
  36.3 0.8 collective-permute-start.10
  37.1 2.0 %collective-permute-start.11 = (bf16[512,128]{1,0:T(8,128)(2,1)S(1)}, bf16[512,128]{1,0:T(8,128)(2,1)S(1)}, u32[]{:S(2)}, u32[]{:S(2)}) collective-permute-start(bf16[512,128]{1,0:T(8,128)(2,1)S(1)} %get-tuple-element.120), channel_id=1, source_target_pairs={{0,3},{1,2},{2,1},{3,0},{4,7},{5,6},{6,5},{7,4},{8,11},{9,10},{10,... | collective-permute-start | bytes 393224 | tf_op jit(solution)/shard_map/ppermute | solution.py:19
  39.1 1.5 %collective-permute-done.9.refs_1_ = bf16[512,128]{1,0:T(8,128)(2,1)S(1)} collective-permute-done((bf16[512,128]{1,0:T(8,128)(2,1)S(1)}, bf16[512,128]{1,0:T(8,128)(2,1)S(1)}, u32[]{:S(2)}, u32[]{:S(2)}) %collective-permute-start.9) | collective-permute-done | bytes 131104 | tf_op jit(solution)/shard_map/ppermute | solution.py:19
  41.3 1.7 %collective-permute-done.11.refs_3_ = bf16[512,128]{1,0:T(8,128)(2,1)S(1)} collective-permute-done((bf16[512,128]{1,0:T(8,128)(2,1)S(1)}, bf16[512,128]{1,0:T(8,128)(2,1)S(1)}, u32[]{:S(2)}, u32[]{:S(2)}) %collective-permute-start.11) | collective-permute-done | bytes 131104 | tf_op jit(solution)/shard_map/ppermute | solution.py:19
  43.6 2.2 %collective-permute-start.12 = (bf16[512,128]{1,0:T(8,128)(2,1)S(1)}, bf16[512,128]{1,0:T(8,128)(2,1)S(1)}, u32[]{:S(2)}, u32[]{:S(2)}) collective-permute-start(bf16[512,128]{1,0:T(8,128)(2,1)S(1)} %shard_map.163.refs_0_), channel_id=1, source_target_pairs={{0,16},{8,24},{16,0},{24,8},{1,17},{9,25},{17,1},{25,9},{2,18},{10... | collective-permute-start | bytes 393224 | tf_op jit(solution)/shard_map/ppermute | solution.py:19
  45.8 0.9 shard_map.165
  46.7 2.5 %collective-permute-start.16 = (bf16[1024,128]{1,0:T(8,128)(2,1)S(1)}, bf16[1024,128]{1,0:T(8,128)(2,1)S(1)}, u32[]{:S(2)}, u32[]{:S(2)}) collective-permute-start(bf16[1024,128]{1,0:T(8,128)(2,1)S(1)} %get-tuple-element.135.refs_4_.refs_0_), channel_id=1, source_target_pairs={{0,3},{1,2},{2,1},{3,0},{4,7},{5,6},{6,5},{7,4},{8,11},{9,10},{10,... | collective-permute-start | bytes 786440 | tf_op jit(solution)/shard_map/ppermute | solution.py:19
  50.3 0.7 collective-permute-done.12.refs_1_
  51.5 0.8 collective-permute-start.13
  52.3 0.9 shard_map.167.refs_0_
  53.1 0.7 shard_map.166
  53.8 4.6 %collective-permute-done.13.refs_1_ = bf16[512,128]{1,0:T(8,128)(2,1)S(1)} collective-permute-done((bf16[512,128]{1,0:T(8,128)(2,1)S(1)}, bf16[512,128]{1,0:T(8,128)(2,1)S(1)}, u32[]{:S(2)}, u32[]{:S(2)}) %collective-permute-start.13) | collective-permute-done | bytes 131104 | tf_op jit(solution)/shard_map/ppermute | solution.py:19
  59.1 0.9 collective-permute-start.22
  60.0 2.9 %collective-permute-start.20 = (bf16[512,128]{1,0:T(8,128)(2,1)S(1)}, bf16[512,128]{1,0:T(8,128)(2,1)S(1)}, u32[]{:S(2)}, u32[]{:S(2)}) collective-permute-start(bf16[512,128]{1,0:T(8,128)(2,1)S(1)} %shard_map.168.refs_0_), channel_id=1, source_target_pairs={{0,3},{1,2},{2,1},{3,0},{4,7},{5,6},{6,5},{7,4},{8,11},{9,10},{10,... | collective-permute-start | bytes 393224 | tf_op jit(solution)/shard_map/ppermute | solution.py:19
  63.5 0.8 shard_map.172
  64.3 1.5 %collective-permute-start.23 = (bf16[640,512]{1,0:T(8,128)(2,1)S(1)}, bf16[640,512]{1,0:T(8,128)(2,1)S(1)}, u32[]{:S(2)}, u32[]{:S(2)}) collective-permute-start(bf16[640,512]{1,0:T(8,128)(2,1)S(1)} %shard_map.172), channel_id=1, source_target_pairs={{4,0},{5,1},{6,2},{7,3},{12,8},{13,9},{14,10},{15,11},{20,16},{21,... | collective-permute-start | bytes 1966088 | tf_op jit(solution)/shard_map/ppermute | solution.py:25
  65.9 2.0 %collective-permute-done.19.refs_2_ = bf16[512,128]{1,0:T(8,128)(2,1)S(1)} collective-permute-done((bf16[512,128]{1,0:T(8,128)(2,1)S(1)}, bf16[512,128]{1,0:T(8,128)(2,1)S(1)}, u32[]{:S(2)}, u32[]{:S(2)}) %collective-permute-start.19) | collective-permute-done | bytes 131104 | tf_op jit(solution)/shard_map/ppermute | solution.py:19
  67.9 2.2 %shard_map.169 = (bf16[512,512]{1,0:T(8,128)(2,1)S(1)}, bf16[512,512]{1,0:T(8,128)(2,1)S(1)}, f32[512,512]{1,0:T(8,128)S(1)}, f32[512,512]{1,0:T(8,128)S(1)}, f3...) custom-call(s32[3]{0:T(128)S(1)} %pad_add_fusion.where_ref, ...), custom_call_target="tpu_custom_call" | custom-call | flops 805306368 | bytes 7735296 | tf_op jit(solution)/shard_map/pallas_call | solution.py:142
  70.2 1.2 %shard_map.171.refs_0_ = f32[512,1024]{1,0:T(8,128)S(1)} custom-call(s32[3]{0:T(128)S(1)} %pad_add_fusion.where_ref, bf16[512,512]{1,0:T(8,128)(2,1)S(1)} %get-tuple-element.178.refs_0_.refs_1_, bf16[512,1024]{1,0:T(8,128)(2,1)S(1)} %bitcast.20), custom_call_target="tpu_custom_call" | custom-call | tf_op jit(solution)/shard_map/pallas_call | solution.py:142
  72.3 3.1 %shard_map.173 = (bf16[512,128]{1,0:T(8,128)(2,1)S(1)}, bf16[512,128]{1,0:T(8,128)(2,1)S(1)}, f32[512,1]{1,0:T(8,128)S(1)}, f32[512,1]{1,0:T(8,128)S(1)}, bf16[5...) custom-call(s32[3]{0:T(128)S(1)} %pad_add_fusion.where_ref, ...), custom_call_target="tpu_custom_call" | custom-call | flops 1073741824 | bytes 7149568 | tf_op jit(solution)/shard_map/pallas_call | solution.py:142
  75.4 2.5 %shard_map.174 = (bf16[128,1024]{1,0:T(8,128)(2,1)S(1)}, bf16[128,1024]{1,0:T(8,128)(2,1)S(1)}, bf16[128,1024]{1,0:T(8,128)(2,1)S(1)}, bf16[128,1024]{1,0:T(8,128)(2,1)S(1)}) custom-call(s32[3]{0:T(128)S(1)} %pad_add_fusion.where_ref, bf16[128,1024]{1,0:T(8,128)(2,1)S(1)} %bitcast.28, bf16[128,1024]{1,0:T(8,128)(2,1)S(1)} %collective-permute-done.1.refs_1_, ...), custom_call_target="tpu_custom_call" | custom-call | flops 1610612736 | bytes 4718592 | tf_op jit(solution)/shard_map/pallas_call | solution.py:142
  77.9 0.9 shard_map.175
  78.8 1.2 %collective-permute-start.27 = (bf16[256,256]{1,0:T(8,128)(2,1)S(1)}, bf16[256,256]{1,0:T(8,128)(2,1)S(1)}, u32[]{:S(2)}, u32[]{:S(2)}) collective-permute-start(bf16[256,256]{1,0:T(8,128)(2,1)S(1)} %get-tuple-element.172), channel_id=1, source_target_pairs={{0,8},{8,0},{16,24},{24,16},{1,9},{9,1},{17,25},{25,17},{2,10},{10... | collective-permute-start | bytes 393224 | tf_op jit(solution)/shard_map/ppermute | solution.py:19
  80.0 1.1 %collective-permute-start.24 = (bf16[128,1024]{1,0:T(8,128)(2,1)S(1)}, bf16[128,1024]{1,0:T(8,128)(2,1)S(1)}, u32[]{:S(2)}, u32[]{:S(2)}) collective-permute-start(bf16[128,1024]{1,0:T(8,128)(2,1)S(1)} %get-tuple-element.163), channel_id=1, source_target_pairs={{0,1},{1,0},{2,3},{3,2},{4,5},{5,4},{6,7},{7,6},{8,9},{9,8},{10,11... | collective-permute-start | bytes 786440 | tf_op jit(solution)/shard_map/ppermute | solution.py:19
  81.1 1.1 %collective-permute-start.25 = (bf16[128,1024]{1,0:T(8,128)(2,1)S(1)}, bf16[128,1024]{1,0:T(8,128)(2,1)S(1)}, u32[]{:S(2)}, u32[]{:S(2)}) collective-permute-start(bf16[128,1024]{1,0:T(8,128)(2,1)S(1)} %get-tuple-element.164), channel_id=1, source_target_pairs={{0,2},{1,3},{2,0},{3,1},{4,6},{5,7},{6,4},{7,5},{8,10},{9,11},{10,... | collective-permute-start | bytes 786440 | tf_op jit(solution)/shard_map/ppermute | solution.py:19
  82.2 1.2 %collective-permute-start.26 = (bf16[128,1024]{1,0:T(8,128)(2,1)S(1)}, bf16[128,1024]{1,0:T(8,128)(2,1)S(1)}, u32[]{:S(2)}, u32[]{:S(2)}) collective-permute-start(bf16[128,1024]{1,0:T(8,128)(2,1)S(1)} %get-tuple-element.165), channel_id=1, source_target_pairs={{0,3},{1,2},{2,1},{3,0},{4,7},{5,6},{6,5},{7,4},{8,11},{9,10},{10,... | collective-permute-start | bytes 786440 | tf_op jit(solution)/shard_map/ppermute | solution.py:19
  83.5 1.1 %collective-permute-done.27.refs_5_ = bf16[256,256]{1,0:T(8,128)(2,1)S(1)} collective-permute-done((bf16[256,256]{1,0:T(8,128)(2,1)S(1)}, bf16[256,256]{1,0:T(8,128)(2,1)S(1)}, u32[]{:S(2)}, u32[]{:S(2)}) %collective-permute-start.27) | collective-permute-done | bytes 131104 | tf_op jit(solution)/shard_map/ppermute | solution.py:19
  84.6 2.2 %collective-permute-start.28 = (bf16[256,256]{1,0:T(8,128)(2,1)S(1)}, bf16[256,256]{1,0:T(8,128)(2,1)S(1)}, u32[]{:S(2)}, u32[]{:S(2)}) collective-permute-start(bf16[256,256]{1,0:T(8,128)(2,1)S(1)} %pad_maximum_fusion), channel_id=1, source_target_pairs={{0,16},{8,24},{16,0},{24,8},{1,17},{9,25},{17,1},{25,9},{2,18},{10... | collective-permute-start | bytes 393224 | tf_op jit(solution)/shard_map/ppermute | solution.py:19
  86.8 3.5 %shard_map.177 = bf16[1024,1024]{1,0:T(8,128)(2,1)} custom-call(s32[3]{0:T(128)S(1)} %pad_add_fusion.where_ref, bf16[1024,512]{1,0:T(8,128)(2,1)S(1)} %shard_map.167.refs_0_, bf16[512,512]{1,0:T(8,128)(2,1)S(1)} %get-tuple-element.166.refs_4_.refs_0_.refs_1_, bf16[512,1024]{1,0:T(8,128)(2,1)S(1)} %bitcast.18), custom_call_target="tpu_custom_call" | custom-call | tf_op jit(solution)/shard_map/pallas_call | solution.py:142
  90.3 3.0 %shard_map.178 = (bf16[128,1024]{1,0:T(8,128)(2,1)}, f32[1,1024]{1,0:T(1,128)}, bf16[1024,128]{1,0:T(8,128)(2,1)}, bf16[128,1024]{1,0:T(8,128)(2,1)}) custom-call(s32[3]{0:T(128)S(1)} %pad_add_fusion.where_ref, f32[512,1024]{1,0:T(8,128)S(1)} %shard_map.171.refs_0_, bf16[512,512]{1,0:T(8,128)(2,1)S(1)} %get-tuple-element.178.refs_0_.refs_1_, ...), custom_call_target="tpu_custom_call" | custom-call | tf_op jit(solution)/shard_map/pallas_call | solution.py:142
  93.4 1.6 %collective-permute-done.26.refs_3_ = bf16[128,1024]{1,0:T(8,128)(2,1)S(1)} collective-permute-done((bf16[128,1024]{1,0:T(8,128)(2,1)S(1)}, bf16[128,1024]{1,0:T(8,128)(2,1)S(1)}, u32[]{:S(2)}, u32[]{:S(2)}) %collective-permute-start.26) | collective-permute-done | bytes 262176 | tf_op jit(solution)/shard_map/ppermute | solution.py:19
  95.0 1.4 %shard_map.176 = (bf16[128,1024]{1,0:T(8,128)(2,1)}, bf16[128,1024]{1,0:T(8,128)(2,1)}) custom-call(s32[3]{0:T(128)S(1)} %pad_add_fusion.where_ref, bf16[128,1024]{1,0:T(8,128)(2,1)S(1)} %get-tuple-element.162.refs_0_, bf16[128,1024]{1,0:T(8,128)(2,1)S(1)} %collective-permute-done.24.refs_1_, bf16[128,1024]{1,0:T(8,128)(2,1)S(1)} %collective-permute-done.25.refs_2_, ...), custom_call_target="tpu_custom_call" | custom-call | tf_op jit(solution)/shard_map/pallas_call | solution.py:142
  (48 shorter events, 6.1 us)
Async XLA Ops:
  0.6 18.4 %collective-permute-start.1 = (bf16[128,1024]{1,0:T(8,128)(2,1)}, bf16[128,1024]{1,0:T(8,128)(2,1)S(1)}, u32[]{:S(2)}, u32[]{:S(2)}) collective-permute-start(bf16[128,1024]{1,0:T(8,128)(2,1)} %bitcast.23), channel_id=1, source_target_pairs={{0,8},{8,0},{16,24},{24,16},{1,9},{9,1},{17,25},{25,17},{2,10},{10... | collective-permute-start | bytes 786440 | tf_op jit(solution)/shard_map/ppermute | solution.py:19
  3.7 15.3 %collective-permute-start = (bf16[128,1024]{1,0:T(8,128)(2,1)}, bf16[128,1024]{1,0:T(8,128)(2,1)S(1)}, u32[]{:S(2)}, u32[]{:S(2)}) collective-permute-start(bf16[128,1024]{1,0:T(8,128)(2,1)} %bitcast.24), channel_id=1, source_target_pairs={{0,16},{8,24},{16,0},{24,8},{1,17},{9,25},{17,1},{25,9},{2,18},{10... | collective-permute-start | bytes 786440 | tf_op jit(solution)/shard_map/ppermute | solution.py:19
  7.1 9.3 %collective-permute-start.2 = (bf16[128,128]{1,0:T(8,128)(2,1)S(1)}, bf16[128,128]{1,0:T(8,128)(2,1)S(1)}, u32[]{:S(2)}, u32[]{:S(2)}) collective-permute-start(bf16[128,128]{1,0:T(8,128)(2,1)S(1)} %broadcast_select_fusion.refs_4_), channel_id=1, source_target_pairs={{0,8},{8,0},{16,24},{24,16},{1,9},{9,1},{17,25},{25,17},{2,10},{10... | collective-permute-start | bytes 98312 | tf_op jit(solution)/shard_map/ppermute | solution.py:19
  7.6 23.2 %copy-start.3 = (bf16[1,128,1024]{2,1,0:T(8,128)(2,1)S(1)}, bf16[1,128,1024]{2,1,0:T(8,128)(2,1)}, u32[]{:S(2)}) copy-start(bf16[1,128,1024]{2,1,0:T(8,128)(2,1)} %param.9) | copy-start | bytes 786436
  11.0 21.2 %collective-permute-start.5 = (bf16[896,256]{1,0:T(8,128)(2,1)S(1)}, bf16[896,256]{1,0:T(8,128)(2,1)S(1)}, u32[]{:S(2)}, u32[]{:S(2)}) collective-permute-start(bf16[896,256]{1,0:T(8,128)(2,1)S(1)} %get-tuple-element.112), channel_id=1, source_target_pairs={{0,1},{1,0},{2,3},{3,2},{4,5},{5,4},{6,7},{7,6},{8,9},{9,8},{10,11... | collective-permute-start | bytes 1376264 | tf_op jit(solution)/shard_map/ppermute | solution.py:19
  12.5 21.0 %collective-permute-start.6 = (bf16[896,256]{1,0:T(8,128)(2,1)S(1)}, bf16[896,256]{1,0:T(8,128)(2,1)S(1)}, u32[]{:S(2)}, u32[]{:S(2)}) collective-permute-start(bf16[896,256]{1,0:T(8,128)(2,1)S(1)} %get-tuple-element.113), channel_id=1, source_target_pairs={{0,2},{1,3},{2,0},{3,1},{4,6},{5,7},{6,4},{7,5},{8,10},{9,11},{10,... | collective-permute-start | bytes 1376264 | tf_op jit(solution)/shard_map/ppermute | solution.py:19
  16.4 17.1 %collective-permute-start.7 = (bf16[896,256]{1,0:T(8,128)(2,1)S(1)}, bf16[896,256]{1,0:T(8,128)(2,1)S(1)}, u32[]{:S(2)}, u32[]{:S(2)}) collective-permute-start(bf16[896,256]{1,0:T(8,128)(2,1)S(1)} %get-tuple-element.114), channel_id=1, source_target_pairs={{0,3},{1,2},{2,1},{3,0},{4,7},{5,6},{6,5},{7,4},{8,11},{9,10},{10,... | collective-permute-start | bytes 1376264 | tf_op jit(solution)/shard_map/ppermute | solution.py:19
  19.1 5.8 %collective-permute-start.3 = (bf16[128,1024]{1,0:T(8,128)(2,1)}, bf16[128,1024]{1,0:T(8,128)(2,1)S(1)}, u32[]{:S(2)}, u32[]{:S(2)}) collective-permute-start(bf16[128,1024]{1,0:T(8,128)(2,1)} %bitcast.25), channel_id=1, source_target_pairs={{8,16},{16,8},{9,17},{17,9},{10,18},{18,10},{11,19},{19,11},{12,20... | collective-permute-start | bytes 786440 | tf_op jit(solution)/shard_map/ppermute | solution.py:38
  19.7 10.7 %collective-permute-start.4 = (bf16[128,1024]{1,0:T(8,128)(2,1)S(1)}, bf16[128,1024]{1,0:T(8,128)(2,1)S(1)}, u32[]{:S(2)}, u32[]{:S(2)}) collective-permute-start(bf16[128,1024]{1,0:T(8,128)(2,1)S(1)} %collective-permute-done.refs_2_), channel_id=1, source_target_pairs={{8,0},{16,24},{9,1},{17,25},{10,2},{18,26},{11,3},{19,27},{12,4},{... | collective-permute-start | bytes 786440 | tf_op jit(solution)/shard_map/ppermute | solution.py:39
  30.4 5.2 %collective-permute-start.8 = (bf16[256,128]{1,0:T(8,128)(2,1)S(1)}, bf16[256,128]{1,0:T(8,128)(2,1)S(1)}, u32[]{:S(2)}, u32[]{:S(2)}) collective-permute-start(bf16[256,128]{1,0:T(8,128)(2,1)S(1)} %pad_maximum_fusion.1), channel_id=1, source_target_pairs={{0,16},{8,24},{16,0},{24,8},{1,17},{9,25},{17,1},{25,9},{2,18},{10... | collective-permute-start | bytes 196616 | tf_op jit(solution)/shard_map/ppermute | solution.py:19
  35.7 17.5 %collective-permute-start.17 = (bf16[512,512]{1,0:T(8,128)(2,1)S(1)}, bf16[512,512]{1,0:T(8,128)(2,1)S(1)}, u32[]{:S(2)}, u32[]{:S(2)}) collective-permute-start(bf16[512,512]{1,0:T(8,128)(2,1)S(1)} %get-tuple-element.137), channel_id=1, source_target_pairs={{0,8},{8,0},{16,24},{24,16},{1,9},{9,1},{17,25},{25,17},{2,10},{10... | collective-permute-start | bytes 1572872 | tf_op jit(solution)/shard_map/ppermute | solution.py:19
  35.7 5.0 %collective-permute-start.9 = (bf16[512,128]{1,0:T(8,128)(2,1)S(1)}, bf16[512,128]{1,0:T(8,128)(2,1)S(1)}, u32[]{:S(2)}, u32[]{:S(2)}) collective-permute-start(bf16[512,128]{1,0:T(8,128)(2,1)S(1)} %get-tuple-element.118), channel_id=1, source_target_pairs={{0,1},{1,0},{2,3},{3,2},{4,5},{5,4},{6,7},{7,6},{8,9},{9,8},{10,11... | collective-permute-start | bytes 393224 | tf_op jit(solution)/shard_map/ppermute | solution.py:19
  36.3 5.0 %collective-permute-start.10 = (bf16[512,128]{1,0:T(8,128)(2,1)S(1)}, bf16[512,128]{1,0:T(8,128)(2,1)S(1)}, u32[]{:S(2)}, u32[]{:S(2)}) collective-permute-start(bf16[512,128]{1,0:T(8,128)(2,1)S(1)} %get-tuple-element.119), channel_id=1, source_target_pairs={{0,2},{1,3},{2,0},{3,1},{4,6},{5,7},{6,4},{7,5},{8,10},{9,11},{10,... | collective-permute-start | bytes 393224 | tf_op jit(solution)/shard_map/ppermute | solution.py:19
  37.1 5.9 %collective-permute-start.11 = (bf16[512,128]{1,0:T(8,128)(2,1)S(1)}, bf16[512,128]{1,0:T(8,128)(2,1)S(1)}, u32[]{:S(2)}, u32[]{:S(2)}) collective-permute-start(bf16[512,128]{1,0:T(8,128)(2,1)S(1)} %get-tuple-element.120), channel_id=1, source_target_pairs={{0,3},{1,2},{2,1},{3,0},{4,7},{5,6},{6,5},{7,4},{8,11},{9,10},{10,... | collective-permute-start | bytes 393224 | tf_op jit(solution)/shard_map/ppermute | solution.py:19
  43.6 7.3 %collective-permute-start.12 = (bf16[512,128]{1,0:T(8,128)(2,1)S(1)}, bf16[512,128]{1,0:T(8,128)(2,1)S(1)}, u32[]{:S(2)}, u32[]{:S(2)}) collective-permute-start(bf16[512,128]{1,0:T(8,128)(2,1)S(1)} %shard_map.163.refs_0_), channel_id=1, source_target_pairs={{0,16},{8,24},{16,0},{24,8},{1,17},{9,25},{17,1},{25,9},{2,18},{10... | collective-permute-start | bytes 393224 | tf_op jit(solution)/shard_map/ppermute | solution.py:19
  46.7 11.8 %collective-permute-start.16 = (bf16[1024,128]{1,0:T(8,128)(2,1)S(1)}, bf16[1024,128]{1,0:T(8,128)(2,1)S(1)}, u32[]{:S(2)}, u32[]{:S(2)}) collective-permute-start(bf16[1024,128]{1,0:T(8,128)(2,1)S(1)} %get-tuple-element.135.refs_4_.refs_0_), channel_id=1, source_target_pairs={{0,3},{1,2},{2,1},{3,0},{4,7},{5,6},{6,5},{7,4},{8,11},{9,10},{10,... | collective-permute-start | bytes 786440 | tf_op jit(solution)/shard_map/ppermute | solution.py:19
  49.2 9.3 %collective-permute-start.15 = (bf16[1024,128]{1,0:T(8,128)(2,1)S(1)}, bf16[1024,128]{1,0:T(8,128)(2,1)S(1)}, u32[]{:S(2)}, u32[]{:S(2)}) collective-permute-start(bf16[1024,128]{1,0:T(8,128)(2,1)S(1)} %get-tuple-element.135.refs_4_.refs_0_), channel_id=1, source_target_pairs={{0,2},{1,3},{2,0},{3,1},{4,6},{5,7},{6,4},{7,5},{8,10},{9,11},{10,... | collective-permute-start | bytes 786440 | tf_op jit(solution)/shard_map/ppermute | solution.py:19
  49.7 8.8 %collective-permute-start.14 = (bf16[1024,128]{1,0:T(8,128)(2,1)S(1)}, bf16[1024,128]{1,0:T(8,128)(2,1)S(1)}, u32[]{:S(2)}, u32[]{:S(2)}) collective-permute-start(bf16[1024,128]{1,0:T(8,128)(2,1)S(1)} %get-tuple-element.135.refs_4_.refs_0_), channel_id=1, source_target_pairs={{0,1},{1,0},{2,3},{3,2},{4,5},{5,4},{6,7},{7,6},{8,9},{9,8},{10,11... | collective-permute-start | bytes 786440 | tf_op jit(solution)/shard_map/ppermute | solution.py:19
  51.5 7.0 %collective-permute-start.13 = (bf16[512,128]{1,0:T(8,128)(2,1)S(1)}, bf16[512,128]{1,0:T(8,128)(2,1)S(1)}, u32[]{:S(2)}, u32[]{:S(2)}) collective-permute-start(bf16[512,128]{1,0:T(8,128)(2,1)S(1)} %shard_map.164.refs_0_), channel_id=1, source_target_pairs={{0,8},{8,0},{16,24},{24,16},{1,9},{9,1},{17,25},{25,17},{2,10},{10... | collective-permute-start | bytes 393224 | tf_op jit(solution)/shard_map/ppermute | solution.py:19
  59.1 12.4 %collective-permute-start.22 = (bf16[256,512]{1,0:T(8,128)(2,1)S(1)}, bf16[256,512]{1,0:T(8,128)(2,1)S(1)}, u32[]{:S(2)}, u32[]{:S(2)}) collective-permute-start(bf16[256,512]{1,0:T(8,128)(2,1)S(1)} %get-tuple-element.147), channel_id=1, source_target_pairs={{0,16},{8,24},{16,0},{24,8},{1,17},{9,25},{17,1},{25,9},{2,18},{10... | collective-permute-start | bytes 786440 | tf_op jit(solution)/shard_map/ppermute | solution.py:19
  60.0 5.9 %collective-permute-start.20 = (bf16[512,128]{1,0:T(8,128)(2,1)S(1)}, bf16[512,128]{1,0:T(8,128)(2,1)S(1)}, u32[]{:S(2)}, u32[]{:S(2)}) collective-permute-start(bf16[512,128]{1,0:T(8,128)(2,1)S(1)} %shard_map.168.refs_0_), channel_id=1, source_target_pairs={{0,3},{1,2},{2,1},{3,0},{4,7},{5,6},{6,5},{7,4},{8,11},{9,10},{10,... | collective-permute-start | bytes 393224 | tf_op jit(solution)/shard_map/ppermute | solution.py:19
  62.9 5.0 %collective-permute-start.19 = (bf16[512,128]{1,0:T(8,128)(2,1)S(1)}, bf16[512,128]{1,0:T(8,128)(2,1)S(1)}, u32[]{:S(2)}, u32[]{:S(2)}) collective-permute-start(bf16[512,128]{1,0:T(8,128)(2,1)S(1)} %shard_map.168.refs_0_), channel_id=1, source_target_pairs={{0,2},{1,3},{2,0},{3,1},{4,6},{5,7},{6,4},{7,5},{8,10},{9,11},{10,... | collective-permute-start | bytes 393224 | tf_op jit(solution)/shard_map/ppermute | solution.py:19
  62.9 5.0 %collective-permute-start.18 = (bf16[512,128]{1,0:T(8,128)(2,1)S(1)}, bf16[512,128]{1,0:T(8,128)(2,1)S(1)}, u32[]{:S(2)}, u32[]{:S(2)}) collective-permute-start(bf16[512,128]{1,0:T(8,128)(2,1)S(1)} %shard_map.168.refs_0_), channel_id=1, source_target_pairs={{0,1},{1,0},{2,3},{3,2},{4,5},{5,4},{6,7},{7,6},{8,9},{9,8},{10,11... | collective-permute-start | bytes 393224 | tf_op jit(solution)/shard_map/ppermute | solution.py:19
  63.5 6.7 %copy-start.1 = (bf16[1,512,1024]{2,1,0:T(8,128)(2,1)S(1)}, bf16[1,512,1024]{2,1,0:T(8,128)(2,1)}, u32[]{:S(2)}) copy-start(bf16[1,512,1024]{2,1,0:T(8,128)(2,1)} %param.12) | copy-start | bytes 3145732
  64.3 8.0 %collective-permute-start.23 = (bf16[640,512]{1,0:T(8,128)(2,1)S(1)}, bf16[640,512]{1,0:T(8,128)(2,1)S(1)}, u32[]{:S(2)}, u32[]{:S(2)}) collective-permute-start(bf16[640,512]{1,0:T(8,128)(2,1)S(1)} %shard_map.172), channel_id=1, source_target_pairs={{4,0},{5,1},{6,2},{7,3},{12,8},{13,9},{14,10},{15,11},{20,16},{21,... | collective-permute-start | bytes 1966088 | tf_op jit(solution)/shard_map/ppermute | solution.py:25
  70.1 2.2 %collective-permute-start.21 = (bf16[512,640]{1,0:T(8,128)(2,1)S(1)}, bf16[512,640]{1,0:T(8,128)(2,1)S(1)}, u32[]{:S(2)}, u32[]{:S(2)}) collective-permute-start(bf16[512,640]{1,0:T(8,128)(2,1)S(1)} %get-tuple-element.145), channel_id=1, source_target_pairs={{0,4},{4,0},{1,5},{5,1},{2,6},{6,2},{3,7},{7,3},{8,12},{12,8},{9,1... | collective-permute-start | bytes 1966088 | tf_op jit(solution)/shard_map/ppermute | solution.py:701
  72.3 3.1 %copy-start.2 = (bf16[1,1024,1024]{2,1,0:T(8,128)(2,1)S(1)}, bf16[1,1024,1024]{2,1,0:T(8,128)(2,1)}, u32[]{:S(2)}) copy-start(bf16[1,1024,1024]{2,1,0:T(8,128)(2,1)} %param.10) | copy-start | bytes 6291460
  75.4 11.4 %copy-start = (bf16[1,512,1024]{2,1,0:T(8,128)(2,1)S(1)}, bf16[1,512,1024]{2,1,0:T(8,128)(2,1)}, u32[]{:S(2)}) copy-start(bf16[1,512,1024]{2,1,0:T(8,128)(2,1)} %param.11) | copy-start | bytes 3145732
  78.8 5.8 %collective-permute-start.27 = (bf16[256,256]{1,0:T(8,128)(2,1)S(1)}, bf16[256,256]{1,0:T(8,128)(2,1)S(1)}, u32[]{:S(2)}, u32[]{:S(2)}) collective-permute-start(bf16[256,256]{1,0:T(8,128)(2,1)S(1)} %get-tuple-element.172), channel_id=1, source_target_pairs={{0,8},{8,0},{16,24},{24,16},{1,9},{9,1},{17,25},{25,17},{2,10},{10... | collective-permute-start | bytes 393224 | tf_op jit(solution)/shard_map/ppermute | solution.py:19
  80.0 13.3 %collective-permute-start.24 = (bf16[128,1024]{1,0:T(8,128)(2,1)S(1)}, bf16[128,1024]{1,0:T(8,128)(2,1)S(1)}, u32[]{:S(2)}, u32[]{:S(2)}) collective-permute-start(bf16[128,1024]{1,0:T(8,128)(2,1)S(1)} %get-tuple-element.163), channel_id=1, source_target_pairs={{0,1},{1,0},{2,3},{3,2},{4,5},{5,4},{6,7},{7,6},{8,9},{9,8},{10,11... | collective-permute-start | bytes 786440 | tf_op jit(solution)/shard_map/ppermute | solution.py:19
  81.1 12.3 %collective-permute-start.25 = (bf16[128,1024]{1,0:T(8,128)(2,1)S(1)}, bf16[128,1024]{1,0:T(8,128)(2,1)S(1)}, u32[]{:S(2)}, u32[]{:S(2)}) collective-permute-start(bf16[128,1024]{1,0:T(8,128)(2,1)S(1)} %get-tuple-element.164), channel_id=1, source_target_pairs={{0,2},{1,3},{2,0},{3,1},{4,6},{5,7},{6,4},{7,5},{8,10},{9,11},{10,... | collective-permute-start | bytes 786440 | tf_op jit(solution)/shard_map/ppermute | solution.py:19
  82.2 12.8 %collective-permute-start.26 = (bf16[128,1024]{1,0:T(8,128)(2,1)S(1)}, bf16[128,1024]{1,0:T(8,128)(2,1)S(1)}, u32[]{:S(2)}, u32[]{:S(2)}) collective-permute-start(bf16[128,1024]{1,0:T(8,128)(2,1)S(1)} %get-tuple-element.165), channel_id=1, source_target_pairs={{0,3},{1,2},{2,1},{3,0},{4,7},{5,6},{6,5},{7,4},{8,11},{9,10},{10,... | collective-permute-start | bytes 786440 | tf_op jit(solution)/shard_map/ppermute | solution.py:19
  84.6 5.7 %copy-start.4 = (bf16[1,128,1024]{2,1,0:T(8,128)(2,1)S(1)}, bf16[1,128,1024]{2,1,0:T(8,128)(2,1)}, u32[]{:S(2)}) copy-start(bf16[1,128,1024]{2,1,0:T(8,128)(2,1)} %param.15) | copy-start | bytes 786436
  84.6 5.7 %copy-start.5 = (bf16[1,1024,128]{2,1,0:T(8,128)(2,1)S(1)}, bf16[1,1024,128]{2,1,0:T(8,128)(2,1)}, u32[]{:S(2)}) copy-start(bf16[1,1024,128]{2,1,0:T(8,128)(2,1)} %param.14) | copy-start | bytes 786436
  84.6 5.7 %copy-start.6 = (f32[1,1024]{1,0:T(1,128)S(1)}, f32[1,1024]{1,0:T(1,128)}, u32[]{:S(2)}) copy-start(f32[1,1024]{1,0:T(1,128)} %refs_8_.1) | copy-start | bytes 12292
  84.6 10.4 %collective-permute-start.28 = (bf16[256,256]{1,0:T(8,128)(2,1)S(1)}, bf16[256,256]{1,0:T(8,128)(2,1)S(1)}, u32[]{:S(2)}, u32[]{:S(2)}) collective-permute-start(bf16[256,256]{1,0:T(8,128)(2,1)S(1)} %pad_maximum_fusion), channel_id=1, source_target_pairs={{0,16},{8,24},{16,0},{24,8},{1,17},{9,25},{17,1},{25,9},{2,18},{10... | collective-permute-start | bytes 393224 | tf_op jit(solution)/shard_map/ppermute | solution.py:19

commit v14 on v13

--- a/solution.py
+++ b/solution.py
@@ -693,7 +693,7 @@
         if step < groups:
             fold_terms = halved(kept, other, head_cols // groups, where)
         else:
-            fold_rows = total([kept, other], where, flops=1 << 33)
+            fold_rows = total([kept, other], where, flops=1 << 32)
     (attention,) = run(
         attention_kernel, [like((rows, features), f32)], where, [(mix, dec)]
     )
@@ -790,8 +790,8 @@
         where,
         [(turned, code_grad, enc)],
         scratch=[
-            pltpu.VMEM((4, head_cols // 4, model_cols), bf16),
-            pltpu.SemaphoreType.DMA((4,)),
+            pltpu.VMEM((2, head_cols // 2, model_cols), bf16),
+            pltpu.SemaphoreType.DMA((2,)),
         ],
         store=True,
     )

time: 96.7 us -> 98.7 us (1.021)
  waiting for transfers between devices: 25.7 us -> 30.6 us
  starting transfers between devices: 36.9 us -> 34.2 us
    ppermute x25, waiting for transfers between devices: 19.9 us -> 24.3 us  [swap(): lax.ppermute(shard, axis, [(i, i ^ by) for i in range(lax.axis_size(axis))])]
    ppermute x25, starting transfers between devices: 33.4 us -> 30.7 us  [swap(): lax.ppermute(shard, axis, [(i, i ^ by) for i in range(lax.axis_size(axis))])]
  transfers between devices with their start and end apart: 29 -> 29, of which waited for: 14 -> 17; matrix products, arithmetic and copies ran while one was open for 1% -> 1% of each run, Pallas kernels for 24% -> 24%
where the time goes in v14:
time: 98.7 us; the launch traced here: 98.4 us
  starting transfers between devices  34.2 us (35%)
  Pallas kernels  31.8 us (32%)
  waiting for transfers between devices  30.6 us (31%)
    pallas_call x19, Pallas kernels, run(): pl.pallas_call(body, out_shape=[jax.ShapeDtypeStruct(r.shape, r.dtype) fo...  31.8 us
    ppermute x25, starting transfers between devices, swap(): lax.ppermute(shard, axis, [(i, i ^ by) for i in range(lax.axis_size(axis))])  30.7 us
    ppermute x25, waiting for transfers between devices, swap(): lax.ppermute(shard, axis, [(i, i ^ by) for i in range(lax.axis_size(axis))])  24.3 us
    ppermute x1, waiting for transfers between devices, line_gathered(): passed = lax.ppermute(far, axis, [(1, 0), (2, 3)])  5.61 us
  transfers between devices with their start and end apart: 29, of which 17 were waited for; matrix products, arithmetic and copies ran while one was open for 1% of the time, Pallas kernels for 24%

profile of v14, /device:TPU:0, one launch (start us, length us, event | category | flops | bytes accessed | tf_op | source)
XLA Modules:
  0.0 98.4 jit_solution(4974507346580216048)
XLA Ops:
  0.6 3.1 %collective-permute-start.1 = (bf16[128,1024]{1,0:T(8,128)(2,1)}, bf16[128,1024]{1,0:T(8,128)(2,1)S(1)}, u32[]{:S(2)}, u32[]{:S(2)}) collective-permute-start(bf16[128,1024]{1,0:T(8,128)(2,1)} %bitcast.23), channel_id=1, source_target_pairs={{0,8},{8,0},{16,24},{24,16},{1,9},{9,1},{17,25},{25,17},{2,10},{10... | collective-permute-start | bytes 786440 | tf_op jit(solution)/shard_map/ppermute | solution.py:19
  3.7 2.6 %collective-permute-start = (bf16[128,1024]{1,0:T(8,128)(2,1)}, bf16[128,1024]{1,0:T(8,128)(2,1)S(1)}, u32[]{:S(2)}, u32[]{:S(2)}) collective-permute-start(bf16[128,1024]{1,0:T(8,128)(2,1)} %bitcast.24), channel_id=1, source_target_pairs={{0,16},{8,24},{16,0},{24,8},{1,17},{9,25},{17,1},{25,9},{2,18},{10... | collective-permute-start | bytes 786440 | tf_op jit(solution)/shard_map/ppermute | solution.py:19
  6.3 0.8 broadcast_select_fusion.refs_4_
  7.6 3.4 %shard_map.161 = (bf16[896,256]{1,0:T(8,128)(2,1)S(1)}, bf16[896,256]{1,0:T(8,128)(2,1)S(1)}, bf16[896,256]{1,0:T(8,128)(2,1)S(1)}, bf16[896,256]{1,0:T(8,128)(2,1)S(1)}) custom-call(s32[3]{0:T(128)S(1)} %pad_add_fusion.where_ref, bf16[512,1024]{1,0:T(8,128)(2,1)} %bitcast.19, bf16[128,1024]{1,0:T(8,128)(2,1)} %bitcast.29, bf16[1024,128]{1,0:T(8,128)(2,1)} %bitcast.31, ...), custom_call_target="tpu_custom_call" | custom-call | tf_op jit(solution)/shard_map/pallas_call | solution.py:142
  11.0 1.6 %collective-permute-start.5 = (bf16[896,256]{1,0:T(8,128)(2,1)S(1)}, bf16[896,256]{1,0:T(8,128)(2,1)S(1)}, u32[]{:S(2)}, u32[]{:S(2)}) collective-permute-start(bf16[896,256]{1,0:T(8,128)(2,1)S(1)} %get-tuple-element.112), channel_id=1, source_target_pairs={{0,1},{1,0},{2,3},{3,2},{4,5},{5,4},{6,7},{7,6},{8,9},{9,8},{10,11... | collective-permute-start | bytes 1376264 | tf_op jit(solution)/shard_map/ppermute | solution.py:19
  12.5 1.5 %collective-permute-start.6 = (bf16[896,256]{1,0:T(8,128)(2,1)S(1)}, bf16[896,256]{1,0:T(8,128)(2,1)S(1)}, u32[]{:S(2)}, u32[]{:S(2)}) collective-permute-start(bf16[896,256]{1,0:T(8,128)(2,1)S(1)} %get-tuple-element.113), channel_id=1, source_target_pairs={{0,2},{1,3},{2,0},{3,1},{4,6},{5,7},{6,4},{7,5},{8,10},{9,11},{10,... | collective-permute-start | bytes 1376264 | tf_op jit(solution)/shard_map/ppermute | solution.py:19
  14.1 2.4 %collective-permute-done.2.refs_5_ = bf16[128,128]{1,0:T(8,128)(2,1)S(1)} collective-permute-done((bf16[128,128]{1,0:T(8,128)(2,1)S(1)}, bf16[128,128]{1,0:T(8,128)(2,1)S(1)}, u32[]{:S(2)}, u32[]{:S(2)}) %collective-permute-start.2) | collective-permute-done | bytes 32800 | tf_op jit(solution)/shard_map/ppermute | solution.py:19
  16.4 2.6 %collective-permute-start.7 = (bf16[896,256]{1,0:T(8,128)(2,1)S(1)}, bf16[896,256]{1,0:T(8,128)(2,1)S(1)}, u32[]{:S(2)}, u32[]{:S(2)}) collective-permute-start(bf16[896,256]{1,0:T(8,128)(2,1)S(1)} %get-tuple-element.114), channel_id=1, source_target_pairs={{0,3},{1,2},{2,1},{3,0},{4,7},{5,6},{6,5},{7,4},{8,11},{9,10},{10,... | collective-permute-start | bytes 1376264 | tf_op jit(solution)/shard_map/ppermute | solution.py:19
  19.1 0.7 collective-permute-start.3
  19.7 1.3 %collective-permute-start.4 = (bf16[128,1024]{1,0:T(8,128)(2,1)S(1)}, bf16[128,1024]{1,0:T(8,128)(2,1)S(1)}, u32[]{:S(2)}, u32[]{:S(2)}) collective-permute-start(bf16[128,1024]{1,0:T(8,128)(2,1)S(1)} %collective-permute-done.refs_2_), channel_id=1, source_target_pairs={{8,0},{16,24},{9,1},{17,25},{10,2},{18,26},{11,3},{19,27},{12,4},{... | collective-permute-start | bytes 786440 | tf_op jit(solution)/shard_map/ppermute | solution.py:39
  21.0 3.8 %shard_map.160 = (bf16[1024,512]{1,0:T(8,128)(2,1)S(1)}, bf16[512,512]{1,0:T(8,128)(2,1)S(1)}, bf16[512,512]{1,0:T(8,128)(2,1)S(1)}) custom-call(s32[3]{0:T(128)S(1)} %pad_add_fusion.where_ref, bf16[1024,1024]{1,0:T(8,128)(2,1)} %bitcast.21, bf16[512,1024]{1,0:T(8,128)(2,1)} %bitcast.17), custom_call_target="tpu_custom_call" | custom-call | tf_op jit(solution)/shard_map/pallas_call | solution.py:142
  24.8 5.6 %collective-permute-done.4.refs_4_ = bf16[128,1024]{1,0:T(8,128)(2,1)S(1)} collective-permute-done((bf16[128,1024]{1,0:T(8,128)(2,1)S(1)}, bf16[128,1024]{1,0:T(8,128)(2,1)S(1)}, u32[]{:S(2)}, u32[]{:S(2)}) %collective-permute-start.4) | collective-permute-done | bytes 262176 | tf_op jit(solution)/shard_map/ppermute | solution.py:39
  30.8 1.4 %shard_map.162 = (bf16[512,128]{1,0:T(8,128)(2,1)S(1)}, bf16[512,128]{1,0:T(8,128)(2,1)S(1)}, bf16[512,128]{1,0:T(8,128)(2,1)S(1)}, bf16[512,128]{1,0:T(8,128)(2,1)S(1)}, bf16[128,1024]{1,0:T(8,128)(2,1)S(1)}) custom-call(s32[3]{0:T(128)S(1)} %pad_add_fusion.where_ref, bf16[128,1024]{1,0:T(8,128)(2,1)S(1)} %bitcast.26, ...), custom_call_target="tpu_custom_call" | custom-call | flops 536870912 | bytes 3145728 | tf_op jit(solution)/shard_map/pallas_call | solution.py:142
  32.2 1.3 %collective-permute-done.6.refs_2_ = bf16[896,256]{1,0:T(8,128)(2,1)S(1)} collective-permute-done((bf16[896,256]{1,0:T(8,128)(2,1)S(1)}, bf16[896,256]{1,0:T(8,128)(2,1)S(1)}, u32[]{:S(2)}, u32[]{:S(2)}) %collective-permute-start.6) | collective-permute-done | bytes 458784 | tf_op jit(solution)/shard_map/ppermute | solution.py:19
  33.5 2.1 %collective-permute-done.8.refs_6_ = bf16[256,128]{1,0:T(8,128)(2,1)S(1)} collective-permute-done((bf16[256,128]{1,0:T(8,128)(2,1)S(1)}, bf16[256,128]{1,0:T(8,128)(2,1)S(1)}, u32[]{:S(2)}, u32[]{:S(2)}) %collective-permute-start.8) | collective-permute-done | bytes 65568 | tf_op jit(solution)/shard_map/ppermute | solution.py:19
  36.3 0.8 collective-permute-start.10
  37.1 2.0 %collective-permute-start.11 = (bf16[512,128]{1,0:T(8,128)(2,1)S(1)}, bf16[512,128]{1,0:T(8,128)(2,1)S(1)}, u32[]{:S(2)}, u32[]{:S(2)}) collective-permute-start(bf16[512,128]{1,0:T(8,128)(2,1)S(1)} %get-tuple-element.120), channel_id=1, source_target_pairs={{0,3},{1,2},{2,1},{3,0},{4,7},{5,6},{6,5},{7,4},{8,11},{9,10},{10,... | collective-permute-start | bytes 393224 | tf_op jit(solution)/shard_map/ppermute | solution.py:19
  39.1 1.5 %collective-permute-done.9.refs_1_ = bf16[512,128]{1,0:T(8,128)(2,1)S(1)} collective-permute-done((bf16[512,128]{1,0:T(8,128)(2,1)S(1)}, bf16[512,128]{1,0:T(8,128)(2,1)S(1)}, u32[]{:S(2)}, u32[]{:S(2)}) %collective-permute-start.9) | collective-permute-done | bytes 131104 | tf_op jit(solution)/shard_map/ppermute | solution.py:19
  41.3 1.7 %collective-permute-done.11.refs_3_ = bf16[512,128]{1,0:T(8,128)(2,1)S(1)} collective-permute-done((bf16[512,128]{1,0:T(8,128)(2,1)S(1)}, bf16[512,128]{1,0:T(8,128)(2,1)S(1)}, u32[]{:S(2)}, u32[]{:S(2)}) %collective-permute-start.11) | collective-permute-done | bytes 131104 | tf_op jit(solution)/shard_map/ppermute | solution.py:19
  43.6 2.2 %collective-permute-start.12 = (bf16[512,128]{1,0:T(8,128)(2,1)S(1)}, bf16[512,128]{1,0:T(8,128)(2,1)S(1)}, u32[]{:S(2)}, u32[]{:S(2)}) collective-permute-start(bf16[512,128]{1,0:T(8,128)(2,1)S(1)} %shard_map.163.refs_0_), channel_id=1, source_target_pairs={{0,16},{8,24},{16,0},{24,8},{1,17},{9,25},{17,1},{25,9},{2,18},{10... | collective-permute-start | bytes 393224 | tf_op jit(solution)/shard_map/ppermute | solution.py:19
  45.8 0.9 shard_map.165
  46.7 2.5 %collective-permute-start.16 = (bf16[1024,128]{1,0:T(8,128)(2,1)S(1)}, bf16[1024,128]{1,0:T(8,128)(2,1)S(1)}, u32[]{:S(2)}, u32[]{:S(2)}) collective-permute-start(bf16[1024,128]{1,0:T(8,128)(2,1)S(1)} %get-tuple-element.135.refs_4_.refs_0_), channel_id=1, source_target_pairs={{0,3},{1,2},{2,1},{3,0},{4,7},{5,6},{6,5},{7,4},{8,11},{9,10},{10,... | collective-permute-start | bytes 786440 | tf_op jit(solution)/shard_map/ppermute | solution.py:19
  50.3 0.7 collective-permute-done.12.refs_1_
  51.5 0.8 collective-permute-start.13
  52.3 0.9 shard_map.167.refs_0_
  53.8 2.7 %collective-permute-done.13.refs_1_ = bf16[512,128]{1,0:T(8,128)(2,1)S(1)} collective-permute-done((bf16[512,128]{1,0:T(8,128)(2,1)S(1)}, bf16[512,128]{1,0:T(8,128)(2,1)S(1)}, u32[]{:S(2)}, u32[]{:S(2)}) %collective-permute-start.13) | collective-permute-done | bytes 131104 | tf_op jit(solution)/shard_map/ppermute | solution.py:19
  56.5 3.0 %collective-permute-done.15.refs_6_.refs_2_ = bf16[1024,128]{1,0:T(8,128)(2,1)S(1)} collective-permute-done((bf16[1024,128]{1,0:T(8,128)(2,1)S(1)}, bf16[1024,128]{1,0:T(8,128)(2,1)S(1)}, u32[]{:S(2)}, u32[]{:S(2)}) %collective-permute-start.15) | collective-permute-done | bytes 262176 | tf_op jit(solution)/shard_map/ppermute | solution.py:19
  60.1 2.2 %collective-permute-start.20 = (bf16[512,128]{1,0:T(8,128)(2,1)S(1)}, bf16[512,128]{1,0:T(8,128)(2,1)S(1)}, u32[]{:S(2)}, u32[]{:S(2)}) collective-permute-start(bf16[512,128]{1,0:T(8,128)(2,1)S(1)} %shard_map.168.refs_0_), channel_id=1, source_target_pairs={{0,3},{1,2},{2,1},{3,0},{4,7},{5,6},{6,5},{7,4},{8,11},{9,10},{10,... | collective-permute-start | bytes 393224 | tf_op jit(solution)/shard_map/ppermute | solution.py:19
  62.3 0.9 collective-permute-start.19
  64.3 1.8 %collective-permute-done.20.refs_3_ = bf16[512,128]{1,0:T(8,128)(2,1)S(1)} collective-permute-done((bf16[512,128]{1,0:T(8,128)(2,1)S(1)}, bf16[512,128]{1,0:T(8,128)(2,1)S(1)}, u32[]{:S(2)}, u32[]{:S(2)}) %collective-permute-start.20) | collective-permute-done | bytes 131104 | tf_op jit(solution)/shard_map/ppermute | solution.py:19
  66.1 1.4 %collective-permute-done.19.refs_2_ = bf16[512,128]{1,0:T(8,128)(2,1)S(1)} collective-permute-done((bf16[512,128]{1,0:T(8,128)(2,1)S(1)}, bf16[512,128]{1,0:T(8,128)(2,1)S(1)}, u32[]{:S(2)}, u32[]{:S(2)}) %collective-permute-start.19) | collective-permute-done | bytes 131104 | tf_op jit(solution)/shard_map/ppermute | solution.py:19
  67.5 0.7 collective-permute-done.18.refs_1_
  68.2 2.2 %shard_map.169 = (bf16[512,512]{1,0:T(8,128)(2,1)S(1)}, bf16[512,512]{1,0:T(8,128)(2,1)S(1)}, f32[512,512]{1,0:T(8,128)S(1)}, f32[512,512]{1,0:T(8,128)S(1)}, f3...) custom-call(s32[3]{0:T(128)S(1)} %pad_add_fusion.where_ref, ...), custom_call_target="tpu_custom_call" | custom-call | flops 805306368 | bytes 7735296 | tf_op jit(solution)/shard_map/pallas_call | solution.py:142
  70.5 0.8 shard_map.172
  71.4 1.5 %collective-permute-start.23 = (bf16[640,512]{1,0:T(8,128)(2,1)S(1)}, bf16[640,512]{1,0:T(8,128)(2,1)S(1)}, u32[]{:S(2)}, u32[]{:S(2)}) collective-permute-start(bf16[640,512]{1,0:T(8,128)(2,1)S(1)} %shard_map.172), channel_id=1, source_target_pairs={{4,0},{5,1},{6,2},{7,3},{12,8},{13,9},{14,10},{15,11},{20,16},{21,... | collective-permute-start | bytes 1966088 | tf_op jit(solution)/shard_map/ppermute | solution.py:25
  72.9 1.2 %shard_map.171.refs_0_ = f32[512,1024]{1,0:T(8,128)S(1)} custom-call(s32[3]{0:T(128)S(1)} %pad_add_fusion.where_ref, bf16[512,512]{1,0:T(8,128)(2,1)S(1)} %get-tuple-element.178.refs_0_.refs_1_, bf16[512,1024]{1,0:T(8,128)(2,1)S(1)} %bitcast.20), custom_call_target="tpu_custom_call" | custom-call | tf_op jit(solution)/shard_map/pallas_call | solution.py:142
  75.4 3.1 %shard_map.173 = (bf16[512,128]{1,0:T(8,128)(2,1)S(1)}, bf16[512,128]{1,0:T(8,128)(2,1)S(1)}, f32[512,1]{1,0:T(8,128)S(1)}, f32[512,1]{1,0:T(8,128)S(1)}, bf16[5...) custom-call(s32[3]{0:T(128)S(1)} %pad_add_fusion.where_ref, ...), custom_call_target="tpu_custom_call" | custom-call | flops 1073741824 | bytes 7149568 | tf_op jit(solution)/shard_map/pallas_call | solution.py:142
  78.5 2.5 %shard_map.174 = (bf16[128,1024]{1,0:T(8,128)(2,1)S(1)}, bf16[128,1024]{1,0:T(8,128)(2,1)S(1)}, bf16[128,1024]{1,0:T(8,128)(2,1)S(1)}, bf16[128,1024]{1,0:T(8,128)(2,1)S(1)}) custom-call(s32[3]{0:T(128)S(1)} %pad_add_fusion.where_ref, bf16[128,1024]{1,0:T(8,128)(2,1)S(1)} %bitcast.28, bf16[128,1024]{1,0:T(8,128)(2,1)S(1)} %collective-permute-done.1.refs_1_, ...), custom_call_target="tpu_custom_call" | custom-call | flops 1610612736 | bytes 4718592 | tf_op jit(solution)/shard_map/pallas_call | solution.py:142
  81.0 0.9 shard_map.175
  81.9 0.9 collective-permute-start.24
  82.8 1.2 %collective-permute-start.25 = (bf16[128,1024]{1,0:T(8,128)(2,1)S(1)}, bf16[128,1024]{1,0:T(8,128)(2,1)S(1)}, u32[]{:S(2)}, u32[]{:S(2)}) collective-permute-start(bf16[128,1024]{1,0:T(8,128)(2,1)S(1)} %get-tuple-element.164), channel_id=1, source_target_pairs={{0,2},{1,3},{2,0},{3,1},{4,6},{5,7},{6,4},{7,5},{8,10},{9,11},{10,... | collective-permute-start | bytes 786440 | tf_op jit(solution)/shard_map/ppermute | solution.py:19
  84.1 1.4 %collective-permute-start.26 = (bf16[128,1024]{1,0:T(8,128)(2,1)S(1)}, bf16[128,1024]{1,0:T(8,128)(2,1)S(1)}, u32[]{:S(2)}, u32[]{:S(2)}) collective-permute-start(bf16[128,1024]{1,0:T(8,128)(2,1)S(1)} %get-tuple-element.165), channel_id=1, source_target_pairs={{0,3},{1,2},{2,1},{3,0},{4,7},{5,6},{6,5},{7,4},{8,11},{9,10},{10,... | collective-permute-start | bytes 786440 | tf_op jit(solution)/shard_map/ppermute | solution.py:19
  85.5 2.4 %collective-permute-done.27.refs_5_ = bf16[256,256]{1,0:T(8,128)(2,1)S(1)} collective-permute-done((bf16[256,256]{1,0:T(8,128)(2,1)S(1)}, bf16[256,256]{1,0:T(8,128)(2,1)S(1)}, u32[]{:S(2)}, u32[]{:S(2)}) %collective-permute-start.27) | collective-permute-done | bytes 131104 | tf_op jit(solution)/shard_map/ppermute | solution.py:19
  88.0 0.7 collective-permute-start.28
  88.7 3.3 %shard_map.177 = bf16[1024,1024]{1,0:T(8,128)(2,1)} custom-call(s32[3]{0:T(128)S(1)} %pad_add_fusion.where_ref, bf16[1024,512]{1,0:T(8,128)(2,1)S(1)} %shard_map.167.refs_0_, bf16[512,512]{1,0:T(8,128)(2,1)S(1)} %get-tuple-element.166.refs_4_.refs_0_.refs_1_, bf16[512,1024]{1,0:T(8,128)(2,1)S(1)} %bitcast.18), custom_call_target="tpu_custom_call" | custom-call | tf_op jit(solution)/shard_map/pallas_call | solution.py:142
  92.1 3.0 %shard_map.178 = (bf16[128,1024]{1,0:T(8,128)(2,1)}, f32[1,1024]{1,0:T(1,128)}, bf16[1024,128]{1,0:T(8,128)(2,1)}, bf16[128,1024]{1,0:T(8,128)(2,1)}) custom-call(s32[3]{0:T(128)S(1)} %pad_add_fusion.where_ref, f32[512,1024]{1,0:T(8,128)S(1)} %shard_map.171.refs_0_, bf16[512,512]{1,0:T(8,128)(2,1)S(1)} %get-tuple-element.178.refs_0_.refs_1_, ...), custom_call_target="tpu_custom_call" | custom-call | tf_op jit(solution)/shard_map/pallas_call | solution.py:142
  95.7 1.2 %collective-permute-done.26.refs_3_ = bf16[128,1024]{1,0:T(8,128)(2,1)S(1)} collective-permute-done((bf16[128,1024]{1,0:T(8,128)(2,1)S(1)}, bf16[128,1024]{1,0:T(8,128)(2,1)S(1)}, u32[]{:S(2)}, u32[]{:S(2)}) %collective-permute-start.26) | collective-permute-done | bytes 262176 | tf_op jit(solution)/shard_map/ppermute | solution.py:19
  97.0 1.4 %shard_map.176 = (bf16[128,1024]{1,0:T(8,128)(2,1)}, bf16[128,1024]{1,0:T(8,128)(2,1)}) custom-call(s32[3]{0:T(128)S(1)} %pad_add_fusion.where_ref, bf16[128,1024]{1,0:T(8,128)(2,1)S(1)} %get-tuple-element.162.refs_0_, bf16[128,1024]{1,0:T(8,128)(2,1)S(1)} %collective-permute-done.24.refs_1_, bf16[128,1024]{1,0:T(8,128)(2,1)S(1)} %collective-permute-done.25.refs_2_, ...), custom_call_target="tpu_custom_call" | custom-call | tf_op jit(solution)/shard_map/pallas_call | solution.py:142
  (48 shorter events, 8.9 us)
Async XLA Ops:
  0.6 18.4 %collective-permute-start.1 = (bf16[128,1024]{1,0:T(8,128)(2,1)}, bf16[128,1024]{1,0:T(8,128)(2,1)S(1)}, u32[]{:S(2)}, u32[]{:S(2)}) collective-permute-start(bf16[128,1024]{1,0:T(8,128)(2,1)} %bitcast.23), channel_id=1, source_target_pairs={{0,8},{8,0},{16,24},{24,16},{1,9},{9,1},{17,25},{25,17},{2,10},{10... | collective-permute-start | bytes 786440 | tf_op jit(solution)/shard_map/ppermute | solution.py:19
  3.7 15.3 %collective-permute-start = (bf16[128,1024]{1,0:T(8,128)(2,1)}, bf16[128,1024]{1,0:T(8,128)(2,1)S(1)}, u32[]{:S(2)}, u32[]{:S(2)}) collective-permute-start(bf16[128,1024]{1,0:T(8,128)(2,1)} %bitcast.24), channel_id=1, source_target_pairs={{0,16},{8,24},{16,0},{24,8},{1,17},{9,25},{17,1},{25,9},{2,18},{10... | collective-permute-start | bytes 786440 | tf_op jit(solution)/shard_map/ppermute | solution.py:19
  7.1 9.3 %collective-permute-start.2 = (bf16[128,128]{1,0:T(8,128)(2,1)S(1)}, bf16[128,128]{1,0:T(8,128)(2,1)S(1)}, u32[]{:S(2)}, u32[]{:S(2)}) collective-permute-start(bf16[128,128]{1,0:T(8,128)(2,1)S(1)} %broadcast_select_fusion.refs_4_), channel_id=1, source_target_pairs={{0,8},{8,0},{16,24},{24,16},{1,9},{9,1},{17,25},{25,17},{2,10},{10... | collective-permute-start | bytes 98312 | tf_op jit(solution)/shard_map/ppermute | solution.py:19
  7.6 23.2 %copy-start.3 = (bf16[1,128,1024]{2,1,0:T(8,128)(2,1)S(1)}, bf16[1,128,1024]{2,1,0:T(8,128)(2,1)}, u32[]{:S(2)}) copy-start(bf16[1,128,1024]{2,1,0:T(8,128)(2,1)} %param.9) | copy-start | bytes 786436
  11.0 21.2 %collective-permute-start.5 = (bf16[896,256]{1,0:T(8,128)(2,1)S(1)}, bf16[896,256]{1,0:T(8,128)(2,1)S(1)}, u32[]{:S(2)}, u32[]{:S(2)}) collective-permute-start(bf16[896,256]{1,0:T(8,128)(2,1)S(1)} %get-tuple-element.112), channel_id=1, source_target_pairs={{0,1},{1,0},{2,3},{3,2},{4,5},{5,4},{6,7},{7,6},{8,9},{9,8},{10,11... | collective-permute-start | bytes 1376264 | tf_op jit(solution)/shard_map/ppermute | solution.py:19
  12.5 21.0 %collective-permute-start.6 = (bf16[896,256]{1,0:T(8,128)(2,1)S(1)}, bf16[896,256]{1,0:T(8,128)(2,1)S(1)}, u32[]{:S(2)}, u32[]{:S(2)}) collective-permute-start(bf16[896,256]{1,0:T(8,128)(2,1)S(1)} %get-tuple-element.113), channel_id=1, source_target_pairs={{0,2},{1,3},{2,0},{3,1},{4,6},{5,7},{6,4},{7,5},{8,10},{9,11},{10,... | collective-permute-start | bytes 1376264 | tf_op jit(solution)/shard_map/ppermute | solution.py:19
  16.4 17.1 %collective-permute-start.7 = (bf16[896,256]{1,0:T(8,128)(2,1)S(1)}, bf16[896,256]{1,0:T(8,128)(2,1)S(1)}, u32[]{:S(2)}, u32[]{:S(2)}) collective-permute-start(bf16[896,256]{1,0:T(8,128)(2,1)S(1)} %get-tuple-element.114), channel_id=1, source_target_pairs={{0,3},{1,2},{2,1},{3,0},{4,7},{5,6},{6,5},{7,4},{8,11},{9,10},{10,... | collective-permute-start | bytes 1376264 | tf_op jit(solution)/shard_map/ppermute | solution.py:19
  19.1 5.8 %collective-permute-start.3 = (bf16[128,1024]{1,0:T(8,128)(2,1)}, bf16[128,1024]{1,0:T(8,128)(2,1)S(1)}, u32[]{:S(2)}, u32[]{:S(2)}) collective-permute-start(bf16[128,1024]{1,0:T(8,128)(2,1)} %bitcast.25), channel_id=1, source_target_pairs={{8,16},{16,8},{9,17},{17,9},{10,18},{18,10},{11,19},{19,11},{12,20... | collective-permute-start | bytes 786440 | tf_op jit(solution)/shard_map/ppermute | solution.py:38
  19.7 10.7 %collective-permute-start.4 = (bf16[128,1024]{1,0:T(8,128)(2,1)S(1)}, bf16[128,1024]{1,0:T(8,128)(2,1)S(1)}, u32[]{:S(2)}, u32[]{:S(2)}) collective-permute-start(bf16[128,1024]{1,0:T(8,128)(2,1)S(1)} %collective-permute-done.refs_2_), channel_id=1, source_target_pairs={{8,0},{16,24},{9,1},{17,25},{10,2},{18,26},{11,3},{19,27},{12,4},{... | collective-permute-start | bytes 786440 | tf_op jit(solution)/shard_map/ppermute | solution.py:39
  30.4 5.2 %collective-permute-start.8 = (bf16[256,128]{1,0:T(8,128)(2,1)S(1)}, bf16[256,128]{1,0:T(8,128)(2,1)S(1)}, u32[]{:S(2)}, u32[]{:S(2)}) collective-permute-start(bf16[256,128]{1,0:T(8,128)(2,1)S(1)} %pad_maximum_fusion.1), channel_id=1, source_target_pairs={{0,16},{8,24},{16,0},{24,8},{1,17},{9,25},{17,1},{25,9},{2,18},{10... | collective-permute-start | bytes 196616 | tf_op jit(solution)/shard_map/ppermute | solution.py:19
  35.7 17.5 %collective-permute-start.17 = (bf16[512,512]{1,0:T(8,128)(2,1)S(1)}, bf16[512,512]{1,0:T(8,128)(2,1)S(1)}, u32[]{:S(2)}, u32[]{:S(2)}) collective-permute-start(bf16[512,512]{1,0:T(8,128)(2,1)S(1)} %get-tuple-element.137), channel_id=1, source_target_pairs={{0,8},{8,0},{16,24},{24,16},{1,9},{9,1},{17,25},{25,17},{2,10},{10... | collective-permute-start | bytes 1572872 | tf_op jit(solution)/shard_map/ppermute | solution.py:19
  35.7 5.0 %collective-permute-start.9 = (bf16[512,128]{1,0:T(8,128)(2,1)S(1)}, bf16[512,128]{1,0:T(8,128)(2,1)S(1)}, u32[]{:S(2)}, u32[]{:S(2)}) collective-permute-start(bf16[512,128]{1,0:T(8,128)(2,1)S(1)} %get-tuple-element.118), channel_id=1, source_target_pairs={{0,1},{1,0},{2,3},{3,2},{4,5},{5,4},{6,7},{7,6},{8,9},{9,8},{10,11... | collective-permute-start | bytes 393224 | tf_op jit(solution)/shard_map/ppermute | solution.py:19
  36.3 5.0 %collective-permute-start.10 = (bf16[512,128]{1,0:T(8,128)(2,1)S(1)}, bf16[512,128]{1,0:T(8,128)(2,1)S(1)}, u32[]{:S(2)}, u32[]{:S(2)}) collective-permute-start(bf16[512,128]{1,0:T(8,128)(2,1)S(1)} %get-tuple-element.119), channel_id=1, source_target_pairs={{0,2},{1,3},{2,0},{3,1},{4,6},{5,7},{6,4},{7,5},{8,10},{9,11},{10,... | collective-permute-start | bytes 393224 | tf_op jit(solution)/shard_map/ppermute | solution.py:19
  37.1 5.9 %collective-permute-start.11 = (bf16[512,128]{1,0:T(8,128)(2,1)S(1)}, bf16[512,128]{1,0:T(8,128)(2,1)S(1)}, u32[]{:S(2)}, u32[]{:S(2)}) collective-permute-start(bf16[512,128]{1,0:T(8,128)(2,1)S(1)} %get-tuple-element.120), channel_id=1, source_target_pairs={{0,3},{1,2},{2,1},{3,0},{4,7},{5,6},{6,5},{7,4},{8,11},{9,10},{10,... | collective-permute-start | bytes 393224 | tf_op jit(solution)/shard_map/ppermute | solution.py:19
  43.6 7.3 %collective-permute-start.12 = (bf16[512,128]{1,0:T(8,128)(2,1)S(1)}, bf16[512,128]{1,0:T(8,128)(2,1)S(1)}, u32[]{:S(2)}, u32[]{:S(2)}) collective-permute-start(bf16[512,128]{1,0:T(8,128)(2,1)S(1)} %shard_map.163.refs_0_), channel_id=1, source_target_pairs={{0,16},{8,24},{16,0},{24,8},{1,17},{9,25},{17,1},{25,9},{2,18},{10... | collective-permute-start | bytes 393224 | tf_op jit(solution)/shard_map/ppermute | solution.py:19
  46.7 9.8 %collective-permute-start.16 = (bf16[1024,128]{1,0:T(8,128)(2,1)S(1)}, bf16[1024,128]{1,0:T(8,128)(2,1)S(1)}, u32[]{:S(2)}, u32[]{:S(2)}) collective-permute-start(bf16[1024,128]{1,0:T(8,128)(2,1)S(1)} %get-tuple-element.135.refs_4_.refs_0_), channel_id=1, source_target_pairs={{0,3},{1,2},{2,1},{3,0},{4,7},{5,6},{6,5},{7,4},{8,11},{9,10},{10,... | collective-permute-start | bytes 786440 | tf_op jit(solution)/shard_map/ppermute | solution.py:19
  49.2 10.3 %collective-permute-start.15 = (bf16[1024,128]{1,0:T(8,128)(2,1)S(1)}, bf16[1024,128]{1,0:T(8,128)(2,1)S(1)}, u32[]{:S(2)}, u32[]{:S(2)}) collective-permute-start(bf16[1024,128]{1,0:T(8,128)(2,1)S(1)} %get-tuple-element.135.refs_4_.refs_0_), channel_id=1, source_target_pairs={{0,2},{1,3},{2,0},{3,1},{4,6},{5,7},{6,4},{7,5},{8,10},{9,11},{10,... | collective-permute-start | bytes 786440 | tf_op jit(solution)/shard_map/ppermute | solution.py:19
  49.7 9.8 %collective-permute-start.14 = (bf16[1024,128]{1,0:T(8,128)(2,1)S(1)}, bf16[1024,128]{1,0:T(8,128)(2,1)S(1)}, u32[]{:S(2)}, u32[]{:S(2)}) collective-permute-start(bf16[1024,128]{1,0:T(8,128)(2,1)S(1)} %get-tuple-element.135.refs_4_.refs_0_), channel_id=1, source_target_pairs={{0,1},{1,0},{2,3},{3,2},{4,5},{5,4},{6,7},{7,6},{8,9},{9,8},{10,11... | collective-permute-start | bytes 786440 | tf_op jit(solution)/shard_map/ppermute | solution.py:19
  51.5 5.0 %collective-permute-start.13 = (bf16[512,128]{1,0:T(8,128)(2,1)S(1)}, bf16[512,128]{1,0:T(8,128)(2,1)S(1)}, u32[]{:S(2)}, u32[]{:S(2)}) collective-permute-start(bf16[512,128]{1,0:T(8,128)(2,1)S(1)} %shard_map.164.refs_0_), channel_id=1, source_target_pairs={{0,8},{8,0},{16,24},{24,16},{1,9},{9,1},{17,25},{25,17},{2,10},{10... | collective-permute-start | bytes 393224 | tf_op jit(solution)/shard_map/ppermute | solution.py:19
  60.1 5.9 %collective-permute-start.20 = (bf16[512,128]{1,0:T(8,128)(2,1)S(1)}, bf16[512,128]{1,0:T(8,128)(2,1)S(1)}, u32[]{:S(2)}, u32[]{:S(2)}) collective-permute-start(bf16[512,128]{1,0:T(8,128)(2,1)S(1)} %shard_map.168.refs_0_), channel_id=1, source_target_pairs={{0,3},{1,2},{2,1},{3,0},{4,7},{5,6},{6,5},{7,4},{8,11},{9,10},{10,... | collective-permute-start | bytes 393224 | tf_op jit(solution)/shard_map/ppermute | solution.py:19
  62.3 5.1 %collective-permute-start.19 = (bf16[512,128]{1,0:T(8,128)(2,1)S(1)}, bf16[512,128]{1,0:T(8,128)(2,1)S(1)}, u32[]{:S(2)}, u32[]{:S(2)}) collective-permute-start(bf16[512,128]{1,0:T(8,128)(2,1)S(1)} %shard_map.168.refs_0_), channel_id=1, source_target_pairs={{0,2},{1,3},{2,0},{3,1},{4,6},{5,7},{6,4},{7,5},{8,10},{9,11},{10,... | collective-permute-start | bytes 393224 | tf_op jit(solution)/shard_map/ppermute | solution.py:19
  63.2 5.0 %collective-permute-start.18 = (bf16[512,128]{1,0:T(8,128)(2,1)S(1)}, bf16[512,128]{1,0:T(8,128)(2,1)S(1)}, u32[]{:S(2)}, u32[]{:S(2)}) collective-permute-start(bf16[512,128]{1,0:T(8,128)(2,1)S(1)} %shard_map.168.refs_0_), channel_id=1, source_target_pairs={{0,1},{1,0},{2,3},{3,2},{4,5},{5,4},{6,7},{7,6},{8,9},{9,8},{10,11... | collective-permute-start | bytes 393224 | tf_op jit(solution)/shard_map/ppermute | solution.py:19
  63.7 10.4 %collective-permute-start.22 = (bf16[256,512]{1,0:T(8,128)(2,1)S(1)}, bf16[256,512]{1,0:T(8,128)(2,1)S(1)}, u32[]{:S(2)}, u32[]{:S(2)}) collective-permute-start(bf16[256,512]{1,0:T(8,128)(2,1)S(1)} %get-tuple-element.147), channel_id=1, source_target_pairs={{0,16},{8,24},{16,0},{24,8},{1,17},{9,25},{17,1},{25,9},{2,18},{10... | collective-permute-start | bytes 786440 | tf_op jit(solution)/shard_map/ppermute | solution.py:19
  68.2 4.6 %copy-start.1 = (bf16[1,512,1024]{2,1,0:T(8,128)(2,1)S(1)}, bf16[1,512,1024]{2,1,0:T(8,128)(2,1)}, u32[]{:S(2)}) copy-start(bf16[1,512,1024]{2,1,0:T(8,128)(2,1)} %param.12) | copy-start | bytes 3145732
  70.5 4.3 %collective-permute-start.21 = (bf16[512,640]{1,0:T(8,128)(2,1)S(1)}, bf16[512,640]{1,0:T(8,128)(2,1)S(1)}, u32[]{:S(2)}, u32[]{:S(2)}) collective-permute-start(bf16[512,640]{1,0:T(8,128)(2,1)S(1)} %get-tuple-element.145), channel_id=1, source_target_pairs={{0,4},{4,0},{1,5},{5,1},{2,6},{6,2},{3,7},{7,3},{8,12},{12,8},{9,1... | collective-permute-start | bytes 1966088 | tf_op jit(solution)/shard_map/ppermute | solution.py:701
  71.4 4.0 %collective-permute-start.23 = (bf16[640,512]{1,0:T(8,128)(2,1)S(1)}, bf16[640,512]{1,0:T(8,128)(2,1)S(1)}, u32[]{:S(2)}, u32[]{:S(2)}) collective-permute-start(bf16[640,512]{1,0:T(8,128)(2,1)S(1)} %shard_map.172), channel_id=1, source_target_pairs={{4,0},{5,1},{6,2},{7,3},{12,8},{13,9},{14,10},{15,11},{20,16},{21,... | collective-permute-start | bytes 1966088 | tf_op jit(solution)/shard_map/ppermute | solution.py:25
  75.4 3.1 %copy-start.2 = (bf16[1,1024,1024]{2,1,0:T(8,128)(2,1)S(1)}, bf16[1,1024,1024]{2,1,0:T(8,128)(2,1)}, u32[]{:S(2)}) copy-start(bf16[1,1024,1024]{2,1,0:T(8,128)(2,1)} %param.10) | copy-start | bytes 6291460
  78.5 10.2 %copy-start = (bf16[1,512,1024]{2,1,0:T(8,128)(2,1)S(1)}, bf16[1,512,1024]{2,1,0:T(8,128)(2,1)}, u32[]{:S(2)}) copy-start(bf16[1,512,1024]{2,1,0:T(8,128)(2,1)} %param.11) | copy-start | bytes 3145732
  81.9 6.0 %collective-permute-start.27 = (bf16[256,256]{1,0:T(8,128)(2,1)S(1)}, bf16[256,256]{1,0:T(8,128)(2,1)S(1)}, u32[]{:S(2)}, u32[]{:S(2)}) collective-permute-start(bf16[256,256]{1,0:T(8,128)(2,1)S(1)} %get-tuple-element.172), channel_id=1, source_target_pairs={{0,8},{8,0},{16,24},{24,16},{1,9},{9,1},{17,25},{25,17},{2,10},{10... | collective-permute-start | bytes 393224 | tf_op jit(solution)/shard_map/ppermute | solution.py:19
  81.9 13.1 %collective-permute-start.24 = (bf16[128,1024]{1,0:T(8,128)(2,1)S(1)}, bf16[128,1024]{1,0:T(8,128)(2,1)S(1)}, u32[]{:S(2)}, u32[]{:S(2)}) collective-permute-start(bf16[128,1024]{1,0:T(8,128)(2,1)S(1)} %get-tuple-element.163), channel_id=1, source_target_pairs={{0,1},{1,0},{2,3},{3,2},{4,5},{5,4},{6,7},{7,6},{8,9},{9,8},{10,11... | collective-permute-start | bytes 786440 | tf_op jit(solution)/shard_map/ppermute | solution.py:19
  82.8 12.9 %collective-permute-start.25 = (bf16[128,1024]{1,0:T(8,128)(2,1)S(1)}, bf16[128,1024]{1,0:T(8,128)(2,1)S(1)}, u32[]{:S(2)}, u32[]{:S(2)}) collective-permute-start(bf16[128,1024]{1,0:T(8,128)(2,1)S(1)} %get-tuple-element.164), channel_id=1, source_target_pairs={{0,2},{1,3},{2,0},{3,1},{4,6},{5,7},{6,4},{7,5},{8,10},{9,11},{10,... | collective-permute-start | bytes 786440 | tf_op jit(solution)/shard_map/ppermute | solution.py:19
  84.1 12.9 %collective-permute-start.26 = (bf16[128,1024]{1,0:T(8,128)(2,1)S(1)}, bf16[128,1024]{1,0:T(8,128)(2,1)S(1)}, u32[]{:S(2)}, u32[]{:S(2)}) collective-permute-start(bf16[128,1024]{1,0:T(8,128)(2,1)S(1)} %get-tuple-element.165), channel_id=1, source_target_pairs={{0,3},{1,2},{2,1},{3,0},{4,7},{5,6},{6,5},{7,4},{8,11},{9,10},{10,... | collective-permute-start | bytes 786440 | tf_op jit(solution)/shard_map/ppermute | solution.py:19
  87.9 4.1 %copy-start.4 = (bf16[1,128,1024]{2,1,0:T(8,128)(2,1)S(1)}, bf16[1,128,1024]{2,1,0:T(8,128)(2,1)}, u32[]{:S(2)}) copy-start(bf16[1,128,1024]{2,1,0:T(8,128)(2,1)} %param.15) | copy-start | bytes 786436
  87.9 4.1 %copy-start.5 = (bf16[1,1024,128]{2,1,0:T(8,128)(2,1)S(1)}, bf16[1,1024,128]{2,1,0:T(8,128)(2,1)}, u32[]{:S(2)}) copy-start(bf16[1,1024,128]{2,1,0:T(8,128)(2,1)} %param.14) | copy-start | bytes 786436
  87.9 4.1 %copy-start.6 = (f32[1,1024]{1,0:T(1,128)S(1)}, f32[1,1024]{1,0:T(1,128)}, u32[]{:S(2)}) copy-start(f32[1,1024]{1,0:T(1,128)} %refs_8_.1) | copy-start | bytes 12292
  88.0 9.0 %collective-permute-start.28 = (bf16[256,256]{1,0:T(8,128)(2,1)S(1)}, bf16[256,256]{1,0:T(8,128)(2,1)S(1)}, u32[]{:S(2)}, u32[]{:S(2)}) collective-permute-start(bf16[256,256]{1,0:T(8,128)(2,1)S(1)} %pad_maximum_fusion), channel_id=1, source_target_pairs={{0,16},{8,24},{16,0},{24,8},{1,17},{9,25},{17,1},{25,9},{2,18},{10... | collective-permute-start | bytes 393224 | tf_op jit(solution)/shard_map/ppermute | solution.py:19

commit v15 on v14

--- a/solution.py
+++ b/solution.py
@@ -59,7 +59,7 @@
     return rows
 
 
-def exchanged(kept, given, size, axis):
+def exchanged(kept, given, after, size, axis):
     count = lax.axis_size(axis)
     parts = [[(part, 0) for part in kept]]
     step = 1
@@ -71,9 +71,9 @@
         ]
         step *= 2
         if step == count:
-            return [part[0] for part in parts]
+            return [part[0] for part in parts], after
         given = [array[row : row + size] for part in parts for array, row in part[1::2]]
-        given = jnp.concatenate(given)
+        given, after = lax.optimization_barrier((jnp.concatenate(given), after))
         parts = [part[::2] for part in parts]
 
 
@@ -490,15 +490,11 @@
 
 
 def last_kernel(places, where, ins, outs, scratch):
-    terms, blocks = ins
-    result = terms[0][...].astype(f32)
-    for term in terms[1:]:
-        result = result + term[...].astype(f32)
-    outs[0][...] = result.astype(bf16)
+    (blocks,) = ins
     for k, (index, row) in enumerate(places):
         size = blocks[index].shape[1]
         at = pl.multiple_of((where[1] ^ k) * size, size)
-        outs[1][:, pl.ds(at, size)] = blocks[index][row : row + outs[1].shape[0], :]
+        outs[0][:, pl.ds(at, size)] = blocks[index][row : row + outs[0].shape[0], :]
 
 
 def head_kernel(where, ins, outs, scratch):
@@ -693,7 +689,7 @@
         if step < groups:
             fold_terms = halved(kept, other, head_cols // groups, where)
         else:
-            fold_rows = total([kept, other], where, flops=1 << 32)
+            fold_rows = total([kept, other], where, flops=1 << 33)
     (attention,) = run(
         attention_kernel, [like((rows, features), f32)], where, [(mix, dec)]
     )
@@ -783,7 +779,7 @@
         [(code_grad, fold_rows)],
     )
     given, mix, turned = lax.optimization_barrier((given, mix, turned))
-    head_blocks = exchanged(kept, given, tokens, "dp")
+    head_blocks, attention = exchanged(kept, given, attention, tokens, "dp")
     (proj_grad,) = run(
         proj_kernel,
         [like((head_cols, model_cols))],
@@ -824,16 +820,16 @@
             (next(k for k, other in enumerate(arrays) if other is array), row)
             for array, row in head_blocks
         ]
-        enc_grad, heads_grad = run(
+        (heads_grad,) = run(
             functools.partial(last_kernel, places),
-            [like((cols, model_cols)), like((tokens, head_cols))],
+            [like((tokens, head_cols))],
             where,
-            [enc_blocks, arrays],
+            [arrays],
         )
     else:
-        enc_grad = total(enc_blocks, where)
         blocks = [array[row : row + tokens] for array, row in head_blocks]
         heads_grad = ordered(blocks, "dp")
+    enc_grad = total(enc_blocks, where, flops=1 << 33)
     return (
         sent[None],
         returned[None],

time: 98.7 us -> 97.2 us (0.985)
  waiting for transfers between devices: 30.6 us -> 25.3 us
  starting transfers between devices: 34.2 us -> 36.8 us
  Pallas kernels: 31.8 us -> 33 us
    ppermute x25, waiting for transfers between devices: 24.3 us -> 19.5 us  [swap(): lax.ppermute(shard, axis, [(i, i ^ by) for i in range(lax.axis_size(axis))])]
    ppermute x25, starting transfers between devices: 30.7 us -> 33.3 us  [swap(): lax.ppermute(shard, axis, [(i, i ^ by) for i in range(lax.axis_size(axis))])]
    pallas_call x19 -> x20, Pallas kernels: 31.8 us -> 33 us  [run(): pl.pallas_call(body, out_shape=[jax.ShapeDtypeStruct(r.shape, r.dtype) fo...]
  transfers between devices with their start and end apart: 29 -> 29, of which waited for: 17 -> 14; matrix products, arithmetic and copies ran while one was open for 1% -> 1% of each run, Pallas kernels for 24% -> 26%
where the time goes in v15:
time: 97.2 us; the launch traced here: 97 us
  starting transfers between devices  36.8 us (38%)
  Pallas kernels  33 us (34%)
  waiting for transfers between devices  25.3 us (26%)
    ppermute x25, starting transfers between devices, swap(): lax.ppermute(shard, axis, [(i, i ^ by) for i in range(lax.axis_size(axis))])  33.3 us
    pallas_call x20, Pallas kernels, run(): pl.pallas_call(body, out_shape=[jax.ShapeDtypeStruct(r.shape, r.dtype) fo...  33 us
    ppermute x25, waiting for transfers between devices, swap(): lax.ppermute(shard, axis, [(i, i ^ by) for i in range(lax.axis_size(axis))])  19.5 us
    ppermute x1, waiting for transfers between devices, line_gathered(): passed = lax.ppermute(far, axis, [(1, 0), (2, 3)])  5.61 us
  transfers between devices with their start and end apart: 29, of which 14 were waited for; matrix products, arithmetic and copies ran while one was open for 1% of the time, Pallas kernels for 26%

profile of v15, /device:TPU:0, one launch (start us, length us, event | category | flops | bytes accessed | tf_op | source)
XLA Modules:
  0.0 97.0 jit_solution(3767055449872014313)
XLA Ops:
  0.6 3.1 %collective-permute-start.1 = (bf16[128,1024]{1,0:T(8,128)(2,1)}, bf16[128,1024]{1,0:T(8,128)(2,1)S(1)}, u32[]{:S(2)}, u32[]{:S(2)}) collective-permute-start(bf16[128,1024]{1,0:T(8,128)(2,1)} %bitcast.23), channel_id=1, source_target_pairs={{0,8},{8,0},{16,24},{24,16},{1,9},{9,1},{17,25},{25,17},{2,10},{10... | collective-permute-start | bytes 786440 | tf_op jit(solution)/shard_map/ppermute | solution.py:19
  3.7 2.6 %collective-permute-start = (bf16[128,1024]{1,0:T(8,128)(2,1)}, bf16[128,1024]{1,0:T(8,128)(2,1)S(1)}, u32[]{:S(2)}, u32[]{:S(2)}) collective-permute-start(bf16[128,1024]{1,0:T(8,128)(2,1)} %bitcast.24), channel_id=1, source_target_pairs={{0,16},{8,24},{16,0},{24,8},{1,17},{9,25},{17,1},{25,9},{2,18},{10... | collective-permute-start | bytes 786440 | tf_op jit(solution)/shard_map/ppermute | solution.py:19
  6.3 0.8 broadcast_select_fusion.refs_4_
  7.6 3.4 %shard_map.161 = (bf16[896,256]{1,0:T(8,128)(2,1)S(1)}, bf16[896,256]{1,0:T(8,128)(2,1)S(1)}, bf16[896,256]{1,0:T(8,128)(2,1)S(1)}, bf16[896,256]{1,0:T(8,128)(2,1)S(1)}) custom-call(s32[3]{0:T(128)S(1)} %pad_add_fusion.where_ref, bf16[512,1024]{1,0:T(8,128)(2,1)} %bitcast.19, bf16[128,1024]{1,0:T(8,128)(2,1)} %bitcast.29, bf16[1024,128]{1,0:T(8,128)(2,1)} %bitcast.31, ...), custom_call_target="tpu_custom_call" | custom-call | tf_op jit(solution)/shard_map/pallas_call | solution.py:142
  11.0 1.6 %collective-permute-start.5 = (bf16[896,256]{1,0:T(8,128)(2,1)S(1)}, bf16[896,256]{1,0:T(8,128)(2,1)S(1)}, u32[]{:S(2)}, u32[]{:S(2)}) collective-permute-start(bf16[896,256]{1,0:T(8,128)(2,1)S(1)} %get-tuple-element.112), channel_id=1, source_target_pairs={{0,1},{1,0},{2,3},{3,2},{4,5},{5,4},{6,7},{7,6},{8,9},{9,8},{10,11... | collective-permute-start | bytes 1376264 | tf_op jit(solution)/shard_map/ppermute | solution.py:19
  12.5 1.5 %collective-permute-start.6 = (bf16[896,256]{1,0:T(8,128)(2,1)S(1)}, bf16[896,256]{1,0:T(8,128)(2,1)S(1)}, u32[]{:S(2)}, u32[]{:S(2)}) collective-permute-start(bf16[896,256]{1,0:T(8,128)(2,1)S(1)} %get-tuple-element.113), channel_id=1, source_target_pairs={{0,2},{1,3},{2,0},{3,1},{4,6},{5,7},{6,4},{7,5},{8,10},{9,11},{10,... | collective-permute-start | bytes 1376264 | tf_op jit(solution)/shard_map/ppermute | solution.py:19
  14.1 2.4 %collective-permute-done.2.refs_5_ = bf16[128,128]{1,0:T(8,128)(2,1)S(1)} collective-permute-done((bf16[128,128]{1,0:T(8,128)(2,1)S(1)}, bf16[128,128]{1,0:T(8,128)(2,1)S(1)}, u32[]{:S(2)}, u32[]{:S(2)}) %collective-permute-start.2) | collective-permute-done | bytes 32800 | tf_op jit(solution)/shard_map/ppermute | solution.py:19
  16.4 2.6 %collective-permute-start.7 = (bf16[896,256]{1,0:T(8,128)(2,1)S(1)}, bf16[896,256]{1,0:T(8,128)(2,1)S(1)}, u32[]{:S(2)}, u32[]{:S(2)}) collective-permute-start(bf16[896,256]{1,0:T(8,128)(2,1)S(1)} %get-tuple-element.114), channel_id=1, source_target_pairs={{0,3},{1,2},{2,1},{3,0},{4,7},{5,6},{6,5},{7,4},{8,11},{9,10},{10,... | collective-permute-start | bytes 1376264 | tf_op jit(solution)/shard_map/ppermute | solution.py:19
  19.1 0.7 collective-permute-start.3
  19.7 1.3 %collective-permute-start.4 = (bf16[128,1024]{1,0:T(8,128)(2,1)S(1)}, bf16[128,1024]{1,0:T(8,128)(2,1)S(1)}, u32[]{:S(2)}, u32[]{:S(2)}) collective-permute-start(bf16[128,1024]{1,0:T(8,128)(2,1)S(1)} %collective-permute-done.refs_2_), channel_id=1, source_target_pairs={{8,0},{16,24},{9,1},{17,25},{10,2},{18,26},{11,3},{19,27},{12,4},{... | collective-permute-start | bytes 786440 | tf_op jit(solution)/shard_map/ppermute | solution.py:39
  21.0 3.8 %shard_map.160 = (bf16[1024,512]{1,0:T(8,128)(2,1)S(1)}, bf16[512,512]{1,0:T(8,128)(2,1)S(1)}, bf16[512,512]{1,0:T(8,128)(2,1)S(1)}) custom-call(s32[3]{0:T(128)S(1)} %pad_add_fusion.where_ref, bf16[1024,1024]{1,0:T(8,128)(2,1)} %bitcast.21, bf16[512,1024]{1,0:T(8,128)(2,1)} %bitcast.17), custom_call_target="tpu_custom_call" | custom-call | tf_op jit(solution)/shard_map/pallas_call | solution.py:142
  24.8 5.6 %collective-permute-done.4.refs_4_ = bf16[128,1024]{1,0:T(8,128)(2,1)S(1)} collective-permute-done((bf16[128,1024]{1,0:T(8,128)(2,1)S(1)}, bf16[128,1024]{1,0:T(8,128)(2,1)S(1)}, u32[]{:S(2)}, u32[]{:S(2)}) %collective-permute-start.4) | collective-permute-done | bytes 262176 | tf_op jit(solution)/shard_map/ppermute | solution.py:39
  30.8 1.4 %shard_map.162 = (bf16[512,128]{1,0:T(8,128)(2,1)S(1)}, bf16[512,128]{1,0:T(8,128)(2,1)S(1)}, bf16[512,128]{1,0:T(8,128)(2,1)S(1)}, bf16[512,128]{1,0:T(8,128)(2,1)S(1)}, bf16[128,1024]{1,0:T(8,128)(2,1)S(1)}) custom-call(s32[3]{0:T(128)S(1)} %pad_add_fusion.where_ref, bf16[128,1024]{1,0:T(8,128)(2,1)S(1)} %bitcast.26, ...), custom_call_target="tpu_custom_call" | custom-call | flops 536870912 | bytes 3145728 | tf_op jit(solution)/shard_map/pallas_call | solution.py:142
  32.2 1.3 %collective-permute-done.6.refs_2_ = bf16[896,256]{1,0:T(8,128)(2,1)S(1)} collective-permute-done((bf16[896,256]{1,0:T(8,128)(2,1)S(1)}, bf16[896,256]{1,0:T(8,128)(2,1)S(1)}, u32[]{:S(2)}, u32[]{:S(2)}) %collective-permute-start.6) | collective-permute-done | bytes 458784 | tf_op jit(solution)/shard_map/ppermute | solution.py:19
  33.5 2.1 %collective-permute-done.8.refs_6_ = bf16[256,128]{1,0:T(8,128)(2,1)S(1)} collective-permute-done((bf16[256,128]{1,0:T(8,128)(2,1)S(1)}, bf16[256,128]{1,0:T(8,128)(2,1)S(1)}, u32[]{:S(2)}, u32[]{:S(2)}) %collective-permute-start.8) | collective-permute-done | bytes 65568 | tf_op jit(solution)/shard_map/ppermute | solution.py:19
  36.3 0.8 collective-permute-start.10
  37.1 2.0 %collective-permute-start.11 = (bf16[512,128]{1,0:T(8,128)(2,1)S(1)}, bf16[512,128]{1,0:T(8,128)(2,1)S(1)}, u32[]{:S(2)}, u32[]{:S(2)}) collective-permute-start(bf16[512,128]{1,0:T(8,128)(2,1)S(1)} %get-tuple-element.120), channel_id=1, source_target_pairs={{0,3},{1,2},{2,1},{3,0},{4,7},{5,6},{6,5},{7,4},{8,11},{9,10},{10,... | collective-permute-start | bytes 393224 | tf_op jit(solution)/shard_map/ppermute | solution.py:19
  39.1 1.5 %collective-permute-done.9.refs_1_ = bf16[512,128]{1,0:T(8,128)(2,1)S(1)} collective-permute-done((bf16[512,128]{1,0:T(8,128)(2,1)S(1)}, bf16[512,128]{1,0:T(8,128)(2,1)S(1)}, u32[]{:S(2)}, u32[]{:S(2)}) %collective-permute-start.9) | collective-permute-done | bytes 131104 | tf_op jit(solution)/shard_map/ppermute | solution.py:19
  41.3 1.7 %collective-permute-done.11.refs_3_ = bf16[512,128]{1,0:T(8,128)(2,1)S(1)} collective-permute-done((bf16[512,128]{1,0:T(8,128)(2,1)S(1)}, bf16[512,128]{1,0:T(8,128)(2,1)S(1)}, u32[]{:S(2)}, u32[]{:S(2)}) %collective-permute-start.11) | collective-permute-done | bytes 131104 | tf_op jit(solution)/shard_map/ppermute | solution.py:19
  43.6 2.2 %collective-permute-start.12 = (bf16[512,128]{1,0:T(8,128)(2,1)S(1)}, bf16[512,128]{1,0:T(8,128)(2,1)S(1)}, u32[]{:S(2)}, u32[]{:S(2)}) collective-permute-start(bf16[512,128]{1,0:T(8,128)(2,1)S(1)} %shard_map.163.refs_0_), channel_id=1, source_target_pairs={{0,16},{8,24},{16,0},{24,8},{1,17},{9,25},{17,1},{25,9},{2,18},{10... | collective-permute-start | bytes 393224 | tf_op jit(solution)/shard_map/ppermute | solution.py:19
  45.8 0.9 shard_map.165
  46.7 2.5 %collective-permute-start.16 = (bf16[1024,128]{1,0:T(8,128)(2,1)S(1)}, bf16[1024,128]{1,0:T(8,128)(2,1)S(1)}, u32[]{:S(2)}, u32[]{:S(2)}) collective-permute-start(bf16[1024,128]{1,0:T(8,128)(2,1)S(1)} %get-tuple-element.135.refs_4_.refs_0_), channel_id=1, source_target_pairs={{0,3},{1,2},{2,1},{3,0},{4,7},{5,6},{6,5},{7,4},{8,11},{9,10},{10,... | collective-permute-start | bytes 786440 | tf_op jit(solution)/shard_map/ppermute | solution.py:19
  50.3 0.7 collective-permute-done.12.refs_1_
  51.5 0.8 collective-permute-start.13
  52.3 0.9 shard_map.167.refs_0_
  53.8 4.6 %collective-permute-done.13.refs_1_ = bf16[512,128]{1,0:T(8,128)(2,1)S(1)} collective-permute-done((bf16[512,128]{1,0:T(8,128)(2,1)S(1)}, bf16[512,128]{1,0:T(8,128)(2,1)S(1)}, u32[]{:S(2)}, u32[]{:S(2)}) %collective-permute-start.13) | collective-permute-done | bytes 131104 | tf_op jit(solution)/shard_map/ppermute | solution.py:19
  59.1 0.9 collective-permute-start.22
  60.0 2.9 %collective-permute-start.20 = (bf16[512,128]{1,0:T(8,128)(2,1)S(1)}, bf16[512,128]{1,0:T(8,128)(2,1)S(1)}, u32[]{:S(2)}, u32[]{:S(2)}) collective-permute-start(bf16[512,128]{1,0:T(8,128)(2,1)S(1)} %shard_map.168.refs_0_), channel_id=1, source_target_pairs={{0,3},{1,2},{2,1},{3,0},{4,7},{5,6},{6,5},{7,4},{8,11},{9,10},{10,... | collective-permute-start | bytes 393224 | tf_op jit(solution)/shard_map/ppermute | solution.py:19
  63.5 0.8 shard_map.172
  64.3 1.5 %collective-permute-start.23 = (bf16[640,512]{1,0:T(8,128)(2,1)S(1)}, bf16[640,512]{1,0:T(8,128)(2,1)S(1)}, u32[]{:S(2)}, u32[]{:S(2)}) collective-permute-start(bf16[640,512]{1,0:T(8,128)(2,1)S(1)} %shard_map.172), channel_id=1, source_target_pairs={{4,0},{5,1},{6,2},{7,3},{12,8},{13,9},{14,10},{15,11},{20,16},{21,... | collective-permute-start | bytes 1966088 | tf_op jit(solution)/shard_map/ppermute | solution.py:25
  65.9 2.0 %collective-permute-done.19.refs_2_ = bf16[512,128]{1,0:T(8,128)(2,1)S(1)} collective-permute-done((bf16[512,128]{1,0:T(8,128)(2,1)S(1)}, bf16[512,128]{1,0:T(8,128)(2,1)S(1)}, u32[]{:S(2)}, u32[]{:S(2)}) %collective-permute-start.19) | collective-permute-done | bytes 131104 | tf_op jit(solution)/shard_map/ppermute | solution.py:19
  67.9 2.2 %shard_map.169 = (bf16[512,512]{1,0:T(8,128)(2,1)S(1)}, bf16[512,512]{1,0:T(8,128)(2,1)S(1)}, f32[512,512]{1,0:T(8,128)S(1)}, f32[512,512]{1,0:T(8,128)S(1)}, f3...) custom-call(s32[3]{0:T(128)S(1)} %pad_add_fusion.where_ref, ...), custom_call_target="tpu_custom_call" | custom-call | flops 805306368 | bytes 7735296 | tf_op jit(solution)/shard_map/pallas_call | solution.py:142
  70.2 1.2 %shard_map.171.refs_0_ = f32[512,1024]{1,0:T(8,128)S(1)} custom-call(s32[3]{0:T(128)S(1)} %pad_add_fusion.where_ref, bf16[512,512]{1,0:T(8,128)(2,1)S(1)} %get-tuple-element.178.refs_0_.refs_1_, bf16[512,1024]{1,0:T(8,128)(2,1)S(1)} %bitcast.20), custom_call_target="tpu_custom_call" | custom-call | tf_op jit(solution)/shard_map/pallas_call | solution.py:142
  72.3 3.1 %shard_map.173 = (bf16[512,128]{1,0:T(8,128)(2,1)S(1)}, bf16[512,128]{1,0:T(8,128)(2,1)S(1)}, f32[512,1]{1,0:T(8,128)S(1)}, f32[512,1]{1,0:T(8,128)S(1)}, bf16[5...) custom-call(s32[3]{0:T(128)S(1)} %pad_add_fusion.where_ref, ...), custom_call_target="tpu_custom_call" | custom-call | flops 1073741824 | bytes 7149568 | tf_op jit(solution)/shard_map/pallas_call | solution.py:142
  75.4 2.5 %shard_map.174 = (bf16[128,1024]{1,0:T(8,128)(2,1)S(1)}, bf16[128,1024]{1,0:T(8,128)(2,1)S(1)}, bf16[128,1024]{1,0:T(8,128)(2,1)S(1)}, bf16[128,1024]{1,0:T(8,128)(2,1)S(1)}) custom-call(s32[3]{0:T(128)S(1)} %pad_add_fusion.where_ref, bf16[128,1024]{1,0:T(8,128)(2,1)S(1)} %bitcast.28, bf16[128,1024]{1,0:T(8,128)(2,1)S(1)} %collective-permute-done.1.refs_1_, ...), custom_call_target="tpu_custom_call" | custom-call | flops 1610612736 | bytes 4718592 | tf_op jit(solution)/shard_map/pallas_call | solution.py:142
  77.9 1.5 %collective-permute-start.26 = (bf16[128,1024]{1,0:T(8,128)(2,1)S(1)}, bf16[128,1024]{1,0:T(8,128)(2,1)S(1)}, u32[]{:S(2)}, u32[]{:S(2)}) collective-permute-start(bf16[128,1024]{1,0:T(8,128)(2,1)S(1)} %get-tuple-element.174), channel_id=1, source_target_pairs={{0,1},{1,0},{2,3},{3,2},{4,5},{5,4},{6,7},{7,6},{8,9},{9,8},{10,11... | collective-permute-start | bytes 786440 | tf_op jit(solution)/shard_map/ppermute | solution.py:19
  79.4 1.1 %collective-permute-start.27 = (bf16[128,1024]{1,0:T(8,128)(2,1)S(1)}, bf16[128,1024]{1,0:T(8,128)(2,1)S(1)}, u32[]{:S(2)}, u32[]{:S(2)}) collective-permute-start(bf16[128,1024]{1,0:T(8,128)(2,1)S(1)} %get-tuple-element.175), channel_id=1, source_target_pairs={{0,2},{1,3},{2,0},{3,1},{4,6},{5,7},{6,4},{7,5},{8,10},{9,11},{10,... | collective-permute-start | bytes 786440 | tf_op jit(solution)/shard_map/ppermute | solution.py:19
  80.5 0.9 collective-permute-start.28
  81.5 0.9 shard_map.175
  82.4 1.2 %collective-permute-start.24 = (bf16[256,256]{1,0:T(8,128)(2,1)S(1)}, bf16[256,256]{1,0:T(8,128)(2,1)S(1)}, u32[]{:S(2)}, u32[]{:S(2)}) collective-permute-start(bf16[256,256]{1,0:T(8,128)(2,1)S(1)} %get-tuple-element.168), channel_id=1, source_target_pairs={{0,8},{8,0},{16,24},{24,16},{1,9},{9,1},{17,25},{25,17},{2,10},{10... | collective-permute-start | bytes 393224 | tf_op jit(solution)/shard_map/ppermute | solution.py:19
  83.6 3.3 %shard_map.177 = bf16[1024,1024]{1,0:T(8,128)(2,1)} custom-call(s32[3]{0:T(128)S(1)} %pad_add_fusion.where_ref, bf16[1024,512]{1,0:T(8,128)(2,1)S(1)} %shard_map.167.refs_0_, bf16[512,512]{1,0:T(8,128)(2,1)S(1)} %get-tuple-element.162.refs_4_.refs_0_.refs_1_, bf16[512,1024]{1,0:T(8,128)(2,1)S(1)} %bitcast.18), custom_call_target="tpu_custom_call" | custom-call | tf_op jit(solution)/shard_map/pallas_call | solution.py:142
  86.9 0.7 collective-permute-done.24.refs_1_
  87.6 1.9 %collective-permute-start.25 = (bf16[256,256]{1,0:T(8,128)(2,1)S(1)}, bf16[256,256]{1,0:T(8,128)(2,1)S(1)}, u32[]{:S(2)}, u32[]{:S(2)}) collective-permute-start(bf16[256,256]{1,0:T(8,128)(2,1)S(1)} %pad_maximum_fusion), channel_id=1, source_target_pairs={{0,16},{8,24},{16,0},{24,8},{1,17},{9,25},{17,1},{25,9},{2,18},{10... | collective-permute-start | bytes 393224 | tf_op jit(solution)/shard_map/ppermute | solution.py:19
  89.6 3.0 %shard_map.179 = (bf16[128,1024]{1,0:T(8,128)(2,1)}, f32[1,1024]{1,0:T(1,128)}, bf16[1024,128]{1,0:T(8,128)(2,1)}, bf16[128,1024]{1,0:T(8,128)(2,1)}) custom-call(s32[3]{0:T(128)S(1)} %pad_add_fusion.where_ref, f32[512,1024]{1,0:T(8,128)S(1)} %shard_map.171.refs_0_, bf16[512,512]{1,0:T(8,128)(2,1)S(1)} %get-tuple-element.178.refs_0_.refs_1_, ...), custom_call_target="tpu_custom_call" | custom-call | tf_op jit(solution)/shard_map/pallas_call | solution.py:142
  92.6 1.0 %collective-permute-done.28.refs_3_ = bf16[128,1024]{1,0:T(8,128)(2,1)S(1)} collective-permute-done((bf16[128,1024]{1,0:T(8,128)(2,1)S(1)}, bf16[128,1024]{1,0:T(8,128)(2,1)S(1)}, u32[]{:S(2)}, u32[]{:S(2)}) %collective-permute-start.28) | collective-permute-done | bytes 262176 | tf_op jit(solution)/shard_map/ppermute | solution.py:19
  93.6 1.4 %shard_map.178 = bf16[128,1024]{1,0:T(8,128)(2,1)} custom-call(s32[3]{0:T(128)S(1)} %pad_add_fusion.where_ref, bf16[128,1024]{1,0:T(8,128)(2,1)S(1)} %get-tuple-element.173.refs_0_, bf16[128,1024]{1,0:T(8,128)(2,1)S(1)} %collective-permute-done.26.refs_1_, bf16[128,1024]{1,0:T(8,128)(2,1)S(1)} %collective-permute-done.27.refs_2_, ...), custom_call_target="tpu_custom_call" | custom-call | flops 8589934592 | bytes 1310720 | tf_op jit(solution)/shard_map/pallas_call | solution.py:142
  95.0 0.7 collective-permute-done.25.refs_2_
  95.7 1.3 %shard_map.176 = bf16[128,1024]{1,0:T(8,128)(2,1)} custom-call(s32[3]{0:T(128)S(1)} %pad_add_fusion.where_ref, bf16[128,256]{1,0:T(8,128)(2,1)S(1)} %get-tuple-element.164.refs_0_, bf16[256,256]{1,0:T(8,128)(2,1)S(1)} %collective-permute-done.24.refs_1_, bf16[256,256]{1,0:T(8,128)(2,1)S(1)} %collective-permute-done.25.refs_2_), custom_call_target="tpu_custom_call" | custom-call | tf_op jit(solution)/shard_map/pallas_call | solution.py:142
  (49 shorter events, 7.3 us)
Async XLA Ops:
  0.6 18.4 %collective-permute-start.1 = (bf16[128,1024]{1,0:T(8,128)(2,1)}, bf16[128,1024]{1,0:T(8,128)(2,1)S(1)}, u32[]{:S(2)}, u32[]{:S(2)}) collective-permute-start(bf16[128,1024]{1,0:T(8,128)(2,1)} %bitcast.23), channel_id=1, source_target_pairs={{0,8},{8,0},{16,24},{24,16},{1,9},{9,1},{17,25},{25,17},{2,10},{10... | collective-permute-start | bytes 786440 | tf_op jit(solution)/shard_map/ppermute | solution.py:19
  3.7 15.3 %collective-permute-start = (bf16[128,1024]{1,0:T(8,128)(2,1)}, bf16[128,1024]{1,0:T(8,128)(2,1)S(1)}, u32[]{:S(2)}, u32[]{:S(2)}) collective-permute-start(bf16[128,1024]{1,0:T(8,128)(2,1)} %bitcast.24), channel_id=1, source_target_pairs={{0,16},{8,24},{16,0},{24,8},{1,17},{9,25},{17,1},{25,9},{2,18},{10... | collective-permute-start | bytes 786440 | tf_op jit(solution)/shard_map/ppermute | solution.py:19
  7.1 9.3 %collective-permute-start.2 = (bf16[128,128]{1,0:T(8,128)(2,1)S(1)}, bf16[128,128]{1,0:T(8,128)(2,1)S(1)}, u32[]{:S(2)}, u32[]{:S(2)}) collective-permute-start(bf16[128,128]{1,0:T(8,128)(2,1)S(1)} %broadcast_select_fusion.refs_4_), channel_id=1, source_target_pairs={{0,8},{8,0},{16,24},{24,16},{1,9},{9,1},{17,25},{25,17},{2,10},{10... | collective-permute-start | bytes 98312 | tf_op jit(solution)/shard_map/ppermute | solution.py:19
  7.6 23.2 %copy-start.3 = (bf16[1,128,1024]{2,1,0:T(8,128)(2,1)S(1)}, bf16[1,128,1024]{2,1,0:T(8,128)(2,1)}, u32[]{:S(2)}) copy-start(bf16[1,128,1024]{2,1,0:T(8,128)(2,1)} %param.9) | copy-start | bytes 786436
  11.0 21.2 %collective-permute-start.5 = (bf16[896,256]{1,0:T(8,128)(2,1)S(1)}, bf16[896,256]{1,0:T(8,128)(2,1)S(1)}, u32[]{:S(2)}, u32[]{:S(2)}) collective-permute-start(bf16[896,256]{1,0:T(8,128)(2,1)S(1)} %get-tuple-element.112), channel_id=1, source_target_pairs={{0,1},{1,0},{2,3},{3,2},{4,5},{5,4},{6,7},{7,6},{8,9},{9,8},{10,11... | collective-permute-start | bytes 1376264 | tf_op jit(solution)/shard_map/ppermute | solution.py:19
  12.5 21.0 %collective-permute-start.6 = (bf16[896,256]{1,0:T(8,128)(2,1)S(1)}, bf16[896,256]{1,0:T(8,128)(2,1)S(1)}, u32[]{:S(2)}, u32[]{:S(2)}) collective-permute-start(bf16[896,256]{1,0:T(8,128)(2,1)S(1)} %get-tuple-element.113), channel_id=1, source_target_pairs={{0,2},{1,3},{2,0},{3,1},{4,6},{5,7},{6,4},{7,5},{8,10},{9,11},{10,... | collective-permute-start | bytes 1376264 | tf_op jit(solution)/shard_map/ppermute | solution.py:19
  16.4 17.1 %collective-permute-start.7 = (bf16[896,256]{1,0:T(8,128)(2,1)S(1)}, bf16[896,256]{1,0:T(8,128)(2,1)S(1)}, u32[]{:S(2)}, u32[]{:S(2)}) collective-permute-start(bf16[896,256]{1,0:T(8,128)(2,1)S(1)} %get-tuple-element.114), channel_id=1, source_target_pairs={{0,3},{1,2},{2,1},{3,0},{4,7},{5,6},{6,5},{7,4},{8,11},{9,10},{10,... | collective-permute-start | bytes 1376264 | tf_op jit(solution)/shard_map/ppermute | solution.py:19
  19.1 5.8 %collective-permute-start.3 = (bf16[128,1024]{1,0:T(8,128)(2,1)}, bf16[128,1024]{1,0:T(8,128)(2,1)S(1)}, u32[]{:S(2)}, u32[]{:S(2)}) collective-permute-start(bf16[128,1024]{1,0:T(8,128)(2,1)} %bitcast.25), channel_id=1, source_target_pairs={{8,16},{16,8},{9,17},{17,9},{10,18},{18,10},{11,19},{19,11},{12,20... | collective-permute-start | bytes 786440 | tf_op jit(solution)/shard_map/ppermute | solution.py:38
  19.7 10.7 %collective-permute-start.4 = (bf16[128,1024]{1,0:T(8,128)(2,1)S(1)}, bf16[128,1024]{1,0:T(8,128)(2,1)S(1)}, u32[]{:S(2)}, u32[]{:S(2)}) collective-permute-start(bf16[128,1024]{1,0:T(8,128)(2,1)S(1)} %collective-permute-done.refs_2_), channel_id=1, source_target_pairs={{8,0},{16,24},{9,1},{17,25},{10,2},{18,26},{11,3},{19,27},{12,4},{... | collective-permute-start | bytes 786440 | tf_op jit(solution)/shard_map/ppermute | solution.py:39
  30.4 5.2 %collective-permute-start.8 = (bf16[256,128]{1,0:T(8,128)(2,1)S(1)}, bf16[256,128]{1,0:T(8,128)(2,1)S(1)}, u32[]{:S(2)}, u32[]{:S(2)}) collective-permute-start(bf16[256,128]{1,0:T(8,128)(2,1)S(1)} %pad_maximum_fusion.1), channel_id=1, source_target_pairs={{0,16},{8,24},{16,0},{24,8},{1,17},{9,25},{17,1},{25,9},{2,18},{10... | collective-permute-start | bytes 196616 | tf_op jit(solution)/shard_map/ppermute | solution.py:19
  35.7 17.5 %collective-permute-start.17 = (bf16[512,512]{1,0:T(8,128)(2,1)S(1)}, bf16[512,512]{1,0:T(8,128)(2,1)S(1)}, u32[]{:S(2)}, u32[]{:S(2)}) collective-permute-start(bf16[512,512]{1,0:T(8,128)(2,1)S(1)} %get-tuple-element.137), channel_id=1, source_target_pairs={{0,8},{8,0},{16,24},{24,16},{1,9},{9,1},{17,25},{25,17},{2,10},{10... | collective-permute-start | bytes 1572872 | tf_op jit(solution)/shard_map/ppermute | solution.py:19
  35.7 5.0 %collective-permute-start.9 = (bf16[512,128]{1,0:T(8,128)(2,1)S(1)}, bf16[512,128]{1,0:T(8,128)(2,1)S(1)}, u32[]{:S(2)}, u32[]{:S(2)}) collective-permute-start(bf16[512,128]{1,0:T(8,128)(2,1)S(1)} %get-tuple-element.118), channel_id=1, source_target_pairs={{0,1},{1,0},{2,3},{3,2},{4,5},{5,4},{6,7},{7,6},{8,9},{9,8},{10,11... | collective-permute-start | bytes 393224 | tf_op jit(solution)/shard_map/ppermute | solution.py:19
  36.3 5.0 %collective-permute-start.10 = (bf16[512,128]{1,0:T(8,128)(2,1)S(1)}, bf16[512,128]{1,0:T(8,128)(2,1)S(1)}, u32[]{:S(2)}, u32[]{:S(2)}) collective-permute-start(bf16[512,128]{1,0:T(8,128)(2,1)S(1)} %get-tuple-element.119), channel_id=1, source_target_pairs={{0,2},{1,3},{2,0},{3,1},{4,6},{5,7},{6,4},{7,5},{8,10},{9,11},{10,... | collective-permute-start | bytes 393224 | tf_op jit(solution)/shard_map/ppermute | solution.py:19
  37.1 5.9 %collective-permute-start.11 = (bf16[512,128]{1,0:T(8,128)(2,1)S(1)}, bf16[512,128]{1,0:T(8,128)(2,1)S(1)}, u32[]{:S(2)}, u32[]{:S(2)}) collective-permute-start(bf16[512,128]{1,0:T(8,128)(2,1)S(1)} %get-tuple-element.120), channel_id=1, source_target_pairs={{0,3},{1,2},{2,1},{3,0},{4,7},{5,6},{6,5},{7,4},{8,11},{9,10},{10,... | collective-permute-start | bytes 393224 | tf_op jit(solution)/shard_map/ppermute | solution.py:19
  43.6 7.3 %collective-permute-start.12 = (bf16[512,128]{1,0:T(8,128)(2,1)S(1)}, bf16[512,128]{1,0:T(8,128)(2,1)S(1)}, u32[]{:S(2)}, u32[]{:S(2)}) collective-permute-start(bf16[512,128]{1,0:T(8,128)(2,1)S(1)} %shard_map.163.refs_0_), channel_id=1, source_target_pairs={{0,16},{8,24},{16,0},{24,8},{1,17},{9,25},{17,1},{25,9},{2,18},{10... | collective-permute-start | bytes 393224 | tf_op jit(solution)/shard_map/ppermute | solution.py:19
  46.7 11.8 %collective-permute-start.16 = (bf16[1024,128]{1,0:T(8,128)(2,1)S(1)}, bf16[1024,128]{1,0:T(8,128)(2,1)S(1)}, u32[]{:S(2)}, u32[]{:S(2)}) collective-permute-start(bf16[1024,128]{1,0:T(8,128)(2,1)S(1)} %get-tuple-element.135.refs_4_.refs_0_), channel_id=1, source_target_pairs={{0,3},{1,2},{2,1},{3,0},{4,7},{5,6},{6,5},{7,4},{8,11},{9,10},{10,... | collective-permute-start | bytes 786440 | tf_op jit(solution)/shard_map/ppermute | solution.py:19
  49.2 9.3 %collective-permute-start.15 = (bf16[1024,128]{1,0:T(8,128)(2,1)S(1)}, bf16[1024,128]{1,0:T(8,128)(2,1)S(1)}, u32[]{:S(2)}, u32[]{:S(2)}) collective-permute-start(bf16[1024,128]{1,0:T(8,128)(2,1)S(1)} %get-tuple-element.135.refs_4_.refs_0_), channel_id=1, source_target_pairs={{0,2},{1,3},{2,0},{3,1},{4,6},{5,7},{6,4},{7,5},{8,10},{9,11},{10,... | collective-permute-start | bytes 786440 | tf_op jit(solution)/shard_map/ppermute | solution.py:19
  49.7 8.8 %collective-permute-start.14 = (bf16[1024,128]{1,0:T(8,128)(2,1)S(1)}, bf16[1024,128]{1,0:T(8,128)(2,1)S(1)}, u32[]{:S(2)}, u32[]{:S(2)}) collective-permute-start(bf16[1024,128]{1,0:T(8,128)(2,1)S(1)} %get-tuple-element.135.refs_4_.refs_0_), channel_id=1, source_target_pairs={{0,1},{1,0},{2,3},{3,2},{4,5},{5,4},{6,7},{7,6},{8,9},{9,8},{10,11... | collective-permute-start | bytes 786440 | tf_op jit(solution)/shard_map/ppermute | solution.py:19
  51.5 7.0 %collective-permute-start.13 = (bf16[512,128]{1,0:T(8,128)(2,1)S(1)}, bf16[512,128]{1,0:T(8,128)(2,1)S(1)}, u32[]{:S(2)}, u32[]{:S(2)}) collective-permute-start(bf16[512,128]{1,0:T(8,128)(2,1)S(1)} %shard_map.164.refs_0_), channel_id=1, source_target_pairs={{0,8},{8,0},{16,24},{24,16},{1,9},{9,1},{17,25},{25,17},{2,10},{10... | collective-permute-start | bytes 393224 | tf_op jit(solution)/shard_map/ppermute | solution.py:19
  59.1 12.4 %collective-permute-start.22 = (bf16[256,512]{1,0:T(8,128)(2,1)S(1)}, bf16[256,512]{1,0:T(8,128)(2,1)S(1)}, u32[]{:S(2)}, u32[]{:S(2)}) collective-permute-start(bf16[256,512]{1,0:T(8,128)(2,1)S(1)} %get-tuple-element.147), channel_id=1, source_target_pairs={{0,16},{8,24},{16,0},{24,8},{1,17},{9,25},{17,1},{25,9},{2,18},{10... | collective-permute-start | bytes 786440 | tf_op jit(solution)/shard_map/ppermute | solution.py:19
  60.0 5.9 %collective-permute-start.20 = (bf16[512,128]{1,0:T(8,128)(2,1)S(1)}, bf16[512,128]{1,0:T(8,128)(2,1)S(1)}, u32[]{:S(2)}, u32[]{:S(2)}) collective-permute-start(bf16[512,128]{1,0:T(8,128)(2,1)S(1)} %shard_map.168.refs_0_), channel_id=1, source_target_pairs={{0,3},{1,2},{2,1},{3,0},{4,7},{5,6},{6,5},{7,4},{8,11},{9,10},{10,... | collective-permute-start | bytes 393224 | tf_op jit(solution)/shard_map/ppermute | solution.py:19
  62.9 5.0 %collective-permute-start.19 = (bf16[512,128]{1,0:T(8,128)(2,1)S(1)}, bf16[512,128]{1,0:T(8,128)(2,1)S(1)}, u32[]{:S(2)}, u32[]{:S(2)}) collective-permute-start(bf16[512,128]{1,0:T(8,128)(2,1)S(1)} %shard_map.168.refs_0_), channel_id=1, source_target_pairs={{0,2},{1,3},{2,0},{3,1},{4,6},{5,7},{6,4},{7,5},{8,10},{9,11},{10,... | collective-permute-start | bytes 393224 | tf_op jit(solution)/shard_map/ppermute | solution.py:19
  62.9 5.0 %collective-permute-start.18 = (bf16[512,128]{1,0:T(8,128)(2,1)S(1)}, bf16[512,128]{1,0:T(8,128)(2,1)S(1)}, u32[]{:S(2)}, u32[]{:S(2)}) collective-permute-start(bf16[512,128]{1,0:T(8,128)(2,1)S(1)} %shard_map.168.refs_0_), channel_id=1, source_target_pairs={{0,1},{1,0},{2,3},{3,2},{4,5},{5,4},{6,7},{7,6},{8,9},{9,8},{10,11... | collective-permute-start | bytes 393224 | tf_op jit(solution)/shard_map/ppermute | solution.py:19
  63.5 6.7 %copy-start.1 = (bf16[1,512,1024]{2,1,0:T(8,128)(2,1)S(1)}, bf16[1,512,1024]{2,1,0:T(8,128)(2,1)}, u32[]{:S(2)}) copy-start(bf16[1,512,1024]{2,1,0:T(8,128)(2,1)} %param.12) | copy-start | bytes 3145732
  64.3 8.0 %collective-permute-start.23 = (bf16[640,512]{1,0:T(8,128)(2,1)S(1)}, bf16[640,512]{1,0:T(8,128)(2,1)S(1)}, u32[]{:S(2)}, u32[]{:S(2)}) collective-permute-start(bf16[640,512]{1,0:T(8,128)(2,1)S(1)} %shard_map.172), channel_id=1, source_target_pairs={{4,0},{5,1},{6,2},{7,3},{12,8},{13,9},{14,10},{15,11},{20,16},{21,... | collective-permute-start | bytes 1966088 | tf_op jit(solution)/shard_map/ppermute | solution.py:25
  70.1 2.2 %collective-permute-start.21 = (bf16[512,640]{1,0:T(8,128)(2,1)S(1)}, bf16[512,640]{1,0:T(8,128)(2,1)S(1)}, u32[]{:S(2)}, u32[]{:S(2)}) collective-permute-start(bf16[512,640]{1,0:T(8,128)(2,1)S(1)} %get-tuple-element.145), channel_id=1, source_target_pairs={{0,4},{4,0},{1,5},{5,1},{2,6},{6,2},{3,7},{7,3},{8,12},{12,8},{9,1... | collective-permute-start | bytes 1966088 | tf_op jit(solution)/shard_map/ppermute | solution.py:697
  72.3 3.1 %copy-start.2 = (bf16[1,1024,1024]{2,1,0:T(8,128)(2,1)S(1)}, bf16[1,1024,1024]{2,1,0:T(8,128)(2,1)}, u32[]{:S(2)}) copy-start(bf16[1,1024,1024]{2,1,0:T(8,128)(2,1)} %param.10) | copy-start | bytes 6291460
  75.4 8.2 %copy-start = (bf16[1,512,1024]{2,1,0:T(8,128)(2,1)S(1)}, bf16[1,512,1024]{2,1,0:T(8,128)(2,1)}, u32[]{:S(2)}) copy-start(bf16[1,512,1024]{2,1,0:T(8,128)(2,1)} %param.11) | copy-start | bytes 3145732
  77.9 14.7 %collective-permute-start.26 = (bf16[128,1024]{1,0:T(8,128)(2,1)S(1)}, bf16[128,1024]{1,0:T(8,128)(2,1)S(1)}, u32[]{:S(2)}, u32[]{:S(2)}) collective-permute-start(bf16[128,1024]{1,0:T(8,128)(2,1)S(1)} %get-tuple-element.174), channel_id=1, source_target_pairs={{0,1},{1,0},{2,3},{3,2},{4,5},{5,4},{6,7},{7,6},{8,9},{9,8},{10,11... | collective-permute-start | bytes 786440 | tf_op jit(solution)/shard_map/ppermute | solution.py:19
  79.4 13.2 %collective-permute-start.27 = (bf16[128,1024]{1,0:T(8,128)(2,1)S(1)}, bf16[128,1024]{1,0:T(8,128)(2,1)S(1)}, u32[]{:S(2)}, u32[]{:S(2)}) collective-permute-start(bf16[128,1024]{1,0:T(8,128)(2,1)S(1)} %get-tuple-element.175), channel_id=1, source_target_pairs={{0,2},{1,3},{2,0},{3,1},{4,6},{5,7},{6,4},{7,5},{8,10},{9,11},{10,... | collective-permute-start | bytes 786440 | tf_op jit(solution)/shard_map/ppermute | solution.py:19
  80.5 13.1 %collective-permute-start.28 = (bf16[128,1024]{1,0:T(8,128)(2,1)S(1)}, bf16[128,1024]{1,0:T(8,128)(2,1)S(1)}, u32[]{:S(2)}, u32[]{:S(2)}) collective-permute-start(bf16[128,1024]{1,0:T(8,128)(2,1)S(1)} %get-tuple-element.176), channel_id=1, source_target_pairs={{0,3},{1,2},{2,1},{3,0},{4,7},{5,6},{6,5},{7,4},{8,11},{9,10},{10,... | collective-permute-start | bytes 786440 | tf_op jit(solution)/shard_map/ppermute | solution.py:19
  82.3 7.2 %copy-start.4 = (bf16[1,128,1024]{2,1,0:T(8,128)(2,1)S(1)}, bf16[1,128,1024]{2,1,0:T(8,128)(2,1)}, u32[]{:S(2)}) copy-start(bf16[1,128,1024]{2,1,0:T(8,128)(2,1)} %param.15) | copy-start | bytes 786436
  82.3 7.2 %copy-start.5 = (bf16[1,1024,128]{2,1,0:T(8,128)(2,1)S(1)}, bf16[1,1024,128]{2,1,0:T(8,128)(2,1)}, u32[]{:S(2)}) copy-start(bf16[1,1024,128]{2,1,0:T(8,128)(2,1)} %param.14) | copy-start | bytes 786436
  82.4 7.2 %copy-start.6 = (f32[1,1024]{1,0:T(1,128)S(1)}, f32[1,1024]{1,0:T(1,128)}, u32[]{:S(2)}) copy-start(f32[1,1024]{1,0:T(1,128)} %refs_8_.1) | copy-start | bytes 12292
  82.4 5.2 %collective-permute-start.24 = (bf16[256,256]{1,0:T(8,128)(2,1)S(1)}, bf16[256,256]{1,0:T(8,128)(2,1)S(1)}, u32[]{:S(2)}, u32[]{:S(2)}) collective-permute-start(bf16[256,256]{1,0:T(8,128)(2,1)S(1)} %get-tuple-element.168), channel_id=1, source_target_pairs={{0,8},{8,0},{16,24},{24,16},{1,9},{9,1},{17,25},{25,17},{2,10},{10... | collective-permute-start | bytes 393224 | tf_op jit(solution)/shard_map/ppermute | solution.py:19
  87.6 8.1 %collective-permute-start.25 = (bf16[256,256]{1,0:T(8,128)(2,1)S(1)}, bf16[256,256]{1,0:T(8,128)(2,1)S(1)}, u32[]{:S(2)}, u32[]{:S(2)}) collective-permute-start(bf16[256,256]{1,0:T(8,128)(2,1)S(1)} %pad_maximum_fusion), channel_id=1, source_target_pairs={{0,16},{8,24},{16,0},{24,8},{1,17},{9,25},{17,1},{25,9},{2,18},{10... | collective-permute-start | bytes 393224 | tf_op jit(solution)/shard_map/ppermute | solution.py:19
